TPU v7x, 32 devices: a whole 2x2x4 slice. The times are simulated.
32 devices in a mesh: groups: 2 (over x), dp: 16 (over z, y, core).
Axes of the slice: x: 2, y: 2, z: 4, core: 2. Of those that a mesh axis runs over, the one named last changes fastest.
Arguments:
- activations: bfloat16 [12288, 8192], P(('groups', 'dp')), parts along dimension 0, may hold values from -6 to 6
- out_grads: bfloat16 [12288, 4096], P(('groups', 'dp')), parts along dimension 0, may hold values from -0.109375 to 0.109375
- projector: bfloat16 [16384, 512], P(('groups', 'dp')), parts along dimension 0, may hold values from -0.0625 to 0.0625
- first_moment: float32 [8192, 512], P(('groups', 'dp')), parts along dimension 0, may hold values from -6 to 6
- second_moment: float32 [8192, 512], P(('groups', 'dp')), parts along dimension 0, may hold values from 0.02 to 0.5
Outputs:
- update: bfloat16 [8192, 8192], P('groups', 'dp'), parts along dimension 0
- new_first: float32 [8192, 512], P(('groups', 'dp')), parts along dimension 0
- new_second: float32 [8192, 512], P(('groups', 'dp')), parts along dimension 0
There are 2 independent parts, one for each index of `groups`. A program takes and returns all parts, laid end to end along the dimension named above; each array names one. Nothing has to cross between parts.
All inputs are finite; a program needn't handle non-finite values.
Results may differ from a plain program's by a relative error of at most 0.005.
Values may be sent and summed in bfloat16 or wider, within the bound.
No kernel may reach another device: no remote copies, remote signals or barrier semaphores. Data moves between devices by JAX's collectives and lax.ppermute only.
A program may use at most 128 MiB of HBM per device.

v0:
```python
import jax
import jax.numpy as jnp
from jax import lax
from jax.sharding import PartitionSpec as P

STEP = 100


decay_first = 0.9
decay_second = 0.999
epsilon = 1e-08


def body(activations, out_grads, projector, first_moment, second_moment):
    projected = jnp.dot(
        activations,
        lax.all_gather(projector, "dp", axis=0, tiled=True),
        preferred_element_type=jnp.float32,
    ).astype(jnp.bfloat16)
    reduced = lax.psum_scatter(
        lax.dot_general(
            out_grads, projected, (((0,), (0,)), ((), ())), preferred_element_type=jnp.float32
        ),
        "dp",
        scatter_dimension=0,
        tiled=True,
    )
    new_first = decay_first * first_moment + (1.0 - decay_first) * reduced
    new_second = decay_second * second_moment + (1.0 - decay_second) * reduced * reduced
    first_fix = 1.0 - decay_first**STEP
    second_fix = 1.0 - decay_second**STEP
    direction = (new_first / first_fix / (jnp.sqrt(new_second / second_fix) + epsilon)).astype(
        jnp.bfloat16
    )
    update = lax.dot_general(
        lax.all_gather(direction, "dp", axis=0, tiled=True),
        projector,
        (((1,), (1,)), ((), ())),
        preferred_element_type=jnp.float32,
    ).astype(jnp.bfloat16)
    return (update, new_first, new_second)


def solution(mesh):
    placed = (
        P(("groups", "dp"), None),
        P(("groups", "dp"), None),
        P(("groups", "dp"), None),
        P(("groups", "dp"), None),
        P(("groups", "dp"), None),
    )
    return jax.shard_map(
        body,
        mesh=mesh,
        in_specs=placed,
        out_specs=(P("groups", "dp"), P(("groups", "dp"), None), P(("groups", "dp"), None)),
        check_vma=False,
    )
```

profile of v0, /device:TPU:0, one launch (start us, length us, event | category | flops | bytes accessed | tf_op | source)
XLA Modules:
  0.0 274.3 jit_solution(12362935569705012927)
XLA Ops:
  7.2 0.0 copy-start
  7.2 0.0 all-gather.3.cloned.1.call-start
  7.2 0.7 all-gather.3.cloned.1.call-update
  7.9 0.0 reduce-scatter.2.cloned.1.call-start
  8.0 79.8 %all-gather.3.cloned.1.call-done = bf16[8192,512]{1,0:T(8,128)(2,1)} async-done(((bf16[512,512]{1,0:T(8,128)(2,1)}), bf16[8192,512]{1,0:T(8,128)(2,1)}) %all-gather.3.cloned.1.call-update) | async-done | bytes 8388624 | tf_op jit(solution)/shard_map/all_gather | solution.py:17
  87.8 0.0 copy-done
  87.8 14.2 %convolution_bitcast_fusion = f32[4096,512]{0,1:T(8,128)} fusion(bf16[384,4096]{1,0:T(8,128)(2,1)S(1)} %copy-done, bf16[384,8192]{1,0:T(8,128)(2,1)} %param.5, bf16[8192,512]{1,0:T(8,128)(2,1)} %all-gather.3.cloned.1.call-done), kind=kOutput, calls=%fused_computation | convolution fusion | flops 4832034816 | bytes 26214400 | tf_op jit(solution)/shard_map/dot_general | solution.py:21
  102.0 0.0 reduce-scatter.2.cloned.1.call-update
  102.0 0.0 all-gather.5.cloned.1.call-start
  102.0 2.0 copy.8
  104.1 2.0 copy.9
  106.1 99.1 %reduce-scatter.2.cloned.1.call-done = f32[256,512]{0,1:T(8,128)} async-done(((f32[4096,512]{0,1:T(8,128)}), f32[256,512]{0,1:T(8,128)}) %reduce-scatter.2.cloned.1.call-update) | async-done | bytes 524304 | tf_op jit(solution)/shard_map/reduce_scatter | solution.py:20
  205.3 2.6 divide_convert_fusion
  207.9 0.0 all-gather.5.cloned.1.call-update
  207.9 2.0 copy.10
  209.9 2.0 copy.11
  212.0 49.0 %all-gather.5.cloned.1.call-done = bf16[4096,512]{0,1:T(8,128)(2,1)} async-done(((bf16[256,512]{0,1:T(8,128)(2,1)}), bf16[4096,512]{0,1:T(8,128)(2,1)}) %all-gather.5.cloned.1.call-update) | async-done | bytes 4194320 | tf_op jit(solution)/shard_map/all_gather | solution.py:36
  261.0 6.7 %convolution_convert_fusion = bf16[4096,512]{1,0:T(8,128)(2,1)} fusion(bf16[4096,512]{0,1:T(8,128)(2,1)} %all-gather.5.cloned.1.call-done, bf16[512,512]{1,0:T(8,128)(2,1)} %param.7), kind=kOutput, calls=%fused_computation.1 | convolution fusion | flops 2149580800 | bytes 8912896 | tf_op jit(solution)/shard_map/dot_general | solution.py:35
Async XLA Ops:
  7.2 80.6 %copy-start = (bf16[384,4096]{1,0:T(8,128)(2,1)S(1)}, bf16[384,4096]{1,0:T(8,128)(2,1)}, u32[]{:S(2)}) copy-start(bf16[384,4096]{1,0:T(8,128)(2,1)} %param.6) | copy-start | bytes 9437188
  7.2 80.6 %all-gather.3.cloned.1.call-start = ((), (), s32[]{:S(2)}) async-start(), calls=%async_computation.1 | async-start | bytes 8912896 | tf_op jit(solution)/shard_map/all_gather | solution.py:17
  7.9 197.3 %reduce-scatter.2.cloned.1.call-start = ((), (), s32[]{:S(2)}) async-start(), calls=%async_computation.2 | async-start | bytes 8912896 | tf_op jit(solution)/shard_map/reduce_scatter | solution.py:20
  102.0 159.0 %all-gather.5.cloned.1.call-start = ((), (), s32[]{:S(2)}) async-start(), calls=%async_computation.3 | async-start | bytes 4456448 | tf_op jit(solution)/shard_map/all_gather | solution.py:36
Sparse Core Ops, SparseCore 0:
  10.2 77.5 all-gather.2
  102.1 103.0 reduce-scatter.1
  208.0 52.9 all-gather.4
where the time goes:
time: 275 us; the launch traced here: 274 us
  waiting for transfers between devices  229 us (83%)
  matrix products  20.9 us (8%)
  between operations  13.8 us (5%)
  local copies, waits for them, and re-layouts  8.16 us (3%)
    reduce_scatter x1, waiting for transfers between devices, body(): lax.psum_scatter(lax.dot_general(out_grads, projected, (((0,), (0,)), (()...  99.1 us
    all_gather x1, waiting for transfers between devices, body(): lax.all_gather(projector, 'dp', axis=0, tiled=True)  79.8 us
    all_gather x1, waiting for transfers between devices, body(): lax.all_gather(direction, 'dp', axis=0, tiled=True)  49 us
    dot_general x1, matrix products, body(): lax.dot_general(out_grads, projected, (((0,), (0,)), ((), ())), preferred...  14.2 us
    unnamed x6, local copies, waits for them, and re-layouts  8.16 us
    dot_general x1, matrix products, body(): lax.dot_general(lax.all_gather(direction, 'dp', axis=0, tiled=True), proj...  6.72 us
  transfers between devices with their start and end apart: 3, of which 3 were waited for; matrix products, arithmetic and copies ran while one was open for 3% of the time, Pallas kernels for 0%

commit v1 on v0

v1 whole, which is shorter than its diff:
```python
import functools
import jax
import jax.numpy as jnp
from jax import lax
from jax.experimental import pallas as pl
from jax.experimental.pallas import tpu as pltpu
from jax.sharding import PartitionSpec as P

STEP = 100

decay_first = 0.9
decay_second = 0.999
epsilon = 1e-08

CHUNKS = 2
F32, BF16 = jnp.float32, jnp.bfloat16
VMEM_LIMIT = 40 * 1024 * 1024


def adam(reduced, first_moment, second_moment):
    new_first = decay_first * first_moment + (1.0 - decay_first) * reduced
    new_second = decay_second * second_moment + (1.0 - decay_second) * reduced * reduced
    first_fix = 1.0 - decay_first**STEP
    second_fix = 1.0 - decay_second**STEP
    direction = (new_first / first_fix / (jnp.sqrt(new_second / second_fix) + epsilon)).astype(BF16)
    return new_first, new_second, direction


def plain(activations, out_grads, projector, first_moment, second_moment):
    projected = jnp.dot(
        activations,
        lax.all_gather(projector, "dp", axis=0, tiled=True),
        preferred_element_type=F32,
    ).astype(BF16)
    reduced = lax.psum_scatter(
        lax.dot_general(out_grads, projected, (((0,), (0,)), ((), ())), preferred_element_type=F32),
        "dp",
        scatter_dimension=0,
        tiled=True,
    )
    new_first, new_second, direction = adam(reduced, first_moment, second_moment)
    update = lax.dot_general(
        lax.all_gather(direction, "dp", axis=0, tiled=True),
        projector,
        (((1,), (1,)), ((), ())),
        preferred_element_type=F32,
    ).astype(BF16)
    return update, new_first, new_second


def params():
    return pltpu.CompilerParams(vmem_limit_bytes=VMEM_LIMIT)


def cost(flops, moved):
    return pl.CostEstimate(flops=flops, bytes_accessed=moved, transcendentals=0)


def pick(array, at, width):
    rows, many = array.shape[0], at.shape[0]

    def kernel(at_ref, in_ref, out_ref):
        out_ref[...] = in_ref[...]

    return pl.pallas_call(
        kernel,
        grid_spec=pltpu.PrefetchScalarGridSpec(
            num_scalar_prefetch=1,
            grid=(many,),
            in_specs=[pl.BlockSpec((rows, width), lambda j, at_ref: (0, at_ref[j]))],
            out_specs=pl.BlockSpec((rows, width), lambda j, at_ref: (0, j)),
        ),
        out_shape=jax.ShapeDtypeStruct((rows, many * width), array.dtype),
        compiler_params=params(),
        cost_estimate=cost(0, 4 * rows * many * width),
        name="pick",
    )(at, array)


def project(activations, sibling, at, blocks):
    many, (depth, cols), rows = len(blocks), blocks[0].shape, activations.shape[0]

    def kernel(at_ref, own_ref, sib_ref, *refs):
        out_ref = refs[-1]
        for j in range(many):

            @pl.when(pl.program_id(0) == j)
            def _(j=j):
                block = refs[j][...]
                own = jnp.dot(own_ref[...], block, preferred_element_type=F32)
                sib = jnp.dot(sib_ref[...], block, preferred_element_type=F32)
                if j == 0:
                    out_ref[:rows, :] = own
                    out_ref[rows:, :] = sib
                else:
                    out_ref[:rows, :] += own
                    out_ref[rows:, :] += sib

    whole = pl.BlockSpec((depth, cols), lambda j, at_ref: (0, 0))
    return pl.pallas_call(
        kernel,
        grid_spec=pltpu.PrefetchScalarGridSpec(
            num_scalar_prefetch=1,
            grid=(many,),
            in_specs=[
                pl.BlockSpec((rows, depth), lambda j, at_ref: (0, at_ref[j])),
                pl.BlockSpec((rows, depth), lambda j, at_ref: (0, j)),
            ]
            + [whole] * many,
            out_specs=pl.BlockSpec((2 * rows, cols), lambda j, at_ref: (0, 0)),
        ),
        out_shape=jax.ShapeDtypeStruct((2 * rows, cols), F32),
        compiler_params=params(),
        cost_estimate=cost(4 * rows * depth * many * cols, 4 * rows * depth * many + 2 * depth * many * cols),
        name="project",
    )(at, activations, sibling, *blocks)


def outer(out_grads, sibling, at, mine, theirs, width):
    many, rows, cols = at.shape[0], out_grads.shape[0], mine.shape[1]
    half = many // 2
    dims = (((0,), (0,)), ((), ()))

    def kernel(at_ref, own_ref, sib_ref, mine_ref, theirs_ref, send_ref, keep_ref, held):
        j = pl.program_id(0)

        @pl.when(j == 0)
        def _():
            held[:rows, :] = (mine_ref[:rows, :] + theirs_ref[rows:, :]).astype(BF16)
            held[rows:, :] = (mine_ref[rows:, :] + theirs_ref[:rows, :]).astype(BF16)

        term = lax.dot_general(own_ref[...], held[:rows, :], dims, preferred_element_type=F32)
        term += lax.dot_general(sib_ref[...], held[rows:, :], dims, preferred_element_type=F32)

        @pl.when(j < half)
        def _():
            send_ref[0] = term.astype(BF16)

        @pl.when(j >= half)
        def _():
            keep_ref[0] = term

    whole = pl.BlockSpec((2 * rows, cols), lambda j, at_ref: (0, 0))
    return pl.pallas_call(
        kernel,
        grid_spec=pltpu.PrefetchScalarGridSpec(
            num_scalar_prefetch=1,
            grid=(many,),
            in_specs=[
                pl.BlockSpec((rows, width), lambda j, at_ref: (0, at_ref[j])),
                pl.BlockSpec((rows, width), lambda j, at_ref: (0, j)),
                whole,
                whole,
            ],
            out_specs=[
                pl.BlockSpec((1, width, cols), lambda j, at_ref: (jnp.minimum(j, half - 1), 0, 0)),
                pl.BlockSpec((1, width, cols), lambda j, at_ref: (jnp.maximum(j - half, 0), 0, 0)),
            ],
            scratch_shapes=[pltpu.VMEM((2 * rows, cols), BF16)],
        ),
        out_shape=[
            jax.ShapeDtypeStruct((half, width, cols), BF16),
            jax.ShapeDtypeStruct((half, width, cols), F32),
        ],
        compiler_params=params(),
        cost_estimate=cost(4 * rows * width * many * cols, 4 * rows * width * many + 6 * half * width * cols),
        name="outer",
    )(at, out_grads, sibling, mine, theirs)


def back(blocks, projector, at):
    many, chunks = len(blocks), len(blocks[0])
    (rows, cols), width = blocks[0][0].shape, projector.shape[0]
    flat = [part for block in blocks for part in block]

    def kernel(at_ref, projector_ref, *refs):
        out_ref = refs[-1]
        for j in range(many):

            @pl.when(pl.program_id(0) == j)
            def _(j=j):
                total = None
                for i in range(chunks):
                    term = lax.dot_general(
                        refs[j * chunks + i][...],
                        projector_ref[:, i * cols : (i + 1) * cols],
                        (((1,), (1,)), ((), ())),
                        preferred_element_type=F32,
                    )
                    total = term if total is None else total + term
                out_ref[...] = total.astype(BF16)

    return pl.pallas_call(
        kernel,
        grid_spec=pltpu.PrefetchScalarGridSpec(
            num_scalar_prefetch=1,
            grid=(many,),
            in_specs=[pl.BlockSpec(projector.shape, lambda j, at_ref: (0, 0))]
            + [pl.BlockSpec((rows, cols), lambda j, at_ref: (0, 0))] * len(flat),
            out_specs=pl.BlockSpec((rows, width), lambda j, at_ref: (at_ref[j], 0)),
        ),
        out_shape=jax.ShapeDtypeStruct((many * rows, width), BF16),
        compiler_params=params(),
        cost_estimate=cost(2 * many * rows * width * cols * chunks, 2 * many * rows * (width + cols * chunks)),
        name="back",
    )(at, projector, *flat)


def levels(activations, out_grads, projector, first_moment, second_moment, *, nz):
    me = lax.axis_index("dp")
    z, y, core = me // 4, me // 2 % 2, me % 2
    grid = [(a, b, c) for a in range(nz) for b in range(2) for c in range(2)]

    def pairs(to):
        return [((a * 2 + b) * 2 + c, (to(a, b, c)[0] * 2 + to(a, b, c)[1]) * 2 + to(a, b, c)[2]) for a, b, c in grid]

    def swap_core(x):
        return lax.ppermute(x, "dp", pairs(lambda a, b, c: (a, b, 1 - c)))

    def swap_y(x):
        return lax.ppermute(x, "dp", pairs(lambda a, b, c: (a, 1 - b, c)))

    def shift_z(x, k):
        return lax.ppermute(x, "dp", pairs(lambda a, b, c: ((a + k) % nz, b, c)))

    def index(k, dy, dc):
        return (lax.rem(z + nz + k, nz) * 2 + (1 - y if dy else y)) * 2 + (1 - core if dc else core)

    def named(*order):
        return jnp.stack([index(*o) for o in order]).astype(jnp.int32)

    ks = sorted(range(1, nz), key=lambda k: min(k, nz - k))
    depth, rank = projector.shape
    width = first_moment.shape[0]
    cols = rank // CHUNKS

    gathered = []
    for i in range(CHUNKS):
        own = projector[:, i * cols : (i + 1) * cols]
        line = [own] + [shift_z(own, k) for k in ks]
        gathered.append(line + [swap_y(x) for x in line])
    order_in = [(-k, dy) for dy in (0, 1) for k in [0] + ks]
    order_out = [(k, dy) for dy in (1, 0) for k in [0] + ks]
    a_sibling = swap_core(pick(activations, named(*[(k, dy, 1) for k, dy in order_in]), depth))
    g_sibling = swap_core(pick(out_grads, named(*[(k, dy, 1) for k, dy in order_out]), width))
    at_in = named(*[(k, dy, 0) for k, dy in order_in])
    at_out = named(*[(k, dy, 0) for k, dy in order_out])

    firsts, seconds, directions = [], [], []
    for i in range(CHUNKS):
        mine = project(activations, a_sibling, at_in, gathered[i])
        send, keep = outer(out_grads, g_sibling, at_out, mine, swap_core(mine), width)
        line = keep + swap_y(send).astype(F32)
        reduced = line[0]
        for at, k in enumerate(ks):
            reduced = reduced + shift_z(line[1 + at].astype(BF16), k).astype(F32)
        part = slice(i * cols, (i + 1) * cols)
        new_first, new_second, direction = adam(reduced, first_moment[:, part], second_moment[:, part])
        firsts.append(new_first)
        seconds.append(new_second)
        line = [direction] + [shift_z(direction, k) for k in ks]
        line = line + [swap_y(x) for x in line]
        directions.append(line + [swap_core(x) for x in line])
    order = [(-k, dy, dc) for dc in (0, 1) for dy in (0, 1) for k in [0] + ks]
    update = back(list(zip(*directions)), projector, named(*order))
    return update, jnp.concatenate(firsts, axis=1), jnp.concatenate(seconds, axis=1)


def solution(mesh):
    devices = mesh.shape["dp"]

    def body(activations, out_grads, projector, first_moment, second_moment):
        aligned = projector.shape[0] % 128 == 0 and first_moment.shape[0] % 128 == 0
        if devices % 4 or devices < 8 or not aligned:
            return plain(activations, out_grads, projector, first_moment, second_moment)
        return levels(activations, out_grads, projector, first_moment, second_moment, nz=devices // 4)

    placed = P(("groups", "dp"), None)
    return jax.shard_map(
        body,
        mesh=mesh,
        in_specs=(placed,) * 5,
        out_specs=(P("groups", "dp"), placed, placed),
        check_vma=False,
    )
```

time: 275 us -> 207 us (0.75)
  waiting for transfers between devices: 229 us -> 98.7 us
  Pallas kernels: 0 us -> 48.7 us
  starting transfers between devices: 0.12 us -> 44.1 us
  matrix products: 20.9 us -> 0 us
  between operations: 13.8 us -> 0.94 us
    all_gather x2 -> x0, waiting for transfers between devices: 129 us -> none  [the longest x1 79.8 us: body(): lax.all_gather(projector, 'dp', axis=0, tiled=True)]
    reduce_scatter x1 -> x0, waiting for transfers between devices: 99.1 us -> none  [body(): lax.psum_scatter(lax.dot_general(out_grads, projected, (((0,), (0,)), (()...]
    ppermute x0 -> x56, waiting for transfers between devices: none -> 98.7 us  [the longest x18 53.5 us: swap_y(): return lax.ppermute(x, 'dp', pairs(lambda a, b, c: (a, 1 - b, c)))]
    pallas_call x0 -> x7, Pallas kernels: none -> 48.7 us  [the longest x2 16.4 us: project(): pl.pallas_call(kernel, grid_spec=pltpu.PrefetchScalarGridSpec(num_scalar_...]
    ppermute x0 -> x56, starting transfers between devices: none -> 44.1 us  [the longest x18 22.7 us: shift_z(): return lax.ppermute(x, 'dp', pairs(lambda a, b, c: ((a + k) % nz, b, c)))]
    dot_general x2 -> x0, matrix products: 20.9 us -> none  [the longest x1 14.2 us: body(): lax.dot_general(out_grads, projected, (((0,), (0,)), ((), ())), preferred...]
    unnamed x6 -> x22, local copies, waits for them, and re-layouts: 8.16 us -> 8.89 us
  transfers between devices with their start and end apart: 3 -> 56, of which waited for: 3 -> 26; matrix products, arithmetic and copies ran while one was open for 3% -> 2% of each run, Pallas kernels for 0% -> 16%
where the time goes in v1:
time: 207 us; the launch traced here: 206 us
  waiting for transfers between devices  98.7 us (48%)
  Pallas kernels  48.7 us (24%)
  starting transfers between devices  44.1 us (21%)
  local copies, waits for them, and re-layouts  10.1 us (5%)
  other arithmetic  3.93 us (2%)
    ppermute x18, waiting for transfers between devices, swap_y(): return lax.ppermute(x, 'dp', pairs(lambda a, b, c: (a, 1 - b, c)))  53.5 us
    ppermute x18, waiting for transfers between devices, shift_z(): return lax.ppermute(x, 'dp', pairs(lambda a, b, c: ((a + k) % nz, b, c)))  44.8 us
    ppermute x18, starting transfers between devices, shift_z(): return lax.ppermute(x, 'dp', pairs(lambda a, b, c: ((a + k) % nz, b, c)))  22.7 us
    ppermute x18, starting transfers between devices, swap_y(): return lax.ppermute(x, 'dp', pairs(lambda a, b, c: (a, 1 - b, c)))  18.3 us
    pallas_call x2, Pallas kernels, project(): pl.pallas_call(kernel, grid_spec=pltpu.PrefetchScalarGridSpec(num_scalar_...  16.4 us
    pallas_call x2, Pallas kernels, outer(): pl.pallas_call(kernel, grid_spec=pltpu.PrefetchScalarGridSpec(num_scalar_...  13.9 us
    pallas_call x1, Pallas kernels, back(): pl.pallas_call(kernel, grid_spec=pltpu.PrefetchScalarGridSpec(num_scalar_...  10.8 us
    unnamed x22, local copies, waits for them, and re-layouts  8.89 us
  transfers between devices with their start and end apart: 56, of which 26 were waited for; matrix products, arithmetic and copies ran while one was open for 2% of the time, Pallas kernels for 16%

profile of v1, /device:TPU:0, one launch (start us, length us, event | category | flops | bytes accessed | tf_op | source)
XLA Modules:
  0.0 206.4 jit_solution(3896503521854541630)
XLA Ops:
  0.8 2.8 %copy-done = bf16[384,8192]{1,0:T(8,128)(2,1)S(1)} copy-done((bf16[384,8192]{1,0:T(8,128)(2,1)S(1)}, bf16[384,8192]{1,0:T(8,128)(2,1)}, u32[]{:S(2)}) %copy-start) | copy-done | bytes 6291480
  3.6 3.9 %pick.3 = bf16[384,4096]{1,0:T(8,128)(2,1)} custom-call(s32[8]{0:T(128)S(1)} %stack.151.at_ref, bf16[384,8192]{1,0:T(8,128)(2,1)S(1)} %copy-done), custom_call_target="tpu_custom_call" | custom-call | bytes 6291456 | tf_op jit(solution)/shard_map/pick/pallas_call | solution.py:65
  8.7 2.6 %collective-permute-start.2 = (bf16[512,256]{1,0:T(8,128)(2,1)}, bf16[512,256]{1,0:T(8,128)(2,1)}, u32[]{:S(2)}, u32[]{:S(2)}) collective-permute-start(bf16[512,256]{1,0:T(8,128)(2,1)} %get-tuple-element.28.refs_0_), channel_id=1, source_target_pairs={{0,4},{1,5},{2,6},{3,7},{4,8},{5,9},{6,10},{7,11},{8,12},{9,13},{1... | collective-permute-start | bytes 786440 | tf_op jit(solution)/shard_map/ppermute | solution.py:224
  11.3 2.0 collective-permute-start.3
  13.4 3.7 %pick.2 = bf16[384,2048]{1,0:T(8,128)(2,1)} custom-call(s32[8]{0:T(128)S(1)} %stack.149.at_ref, bf16[384,4096]{1,0:T(8,128)(2,1)S(1)} %copy-done.2), custom_call_target="tpu_custom_call" | custom-call | bytes 3145728 | tf_op jit(solution)/shard_map/pick/pallas_call | solution.py:65
  18.2 2.7 %collective-permute-done.2.refs_1_ = bf16[512,256]{1,0:T(8,128)(2,1)} collective-permute-done((bf16[512,256]{1,0:T(8,128)(2,1)}, bf16[512,256]{1,0:T(8,128)(2,1)}, u32[]{:S(2)}, u32[]{:S(2)}) %collective-permute-start.2) | collective-permute-done | bytes 262176 | tf_op jit(solution)/shard_map/ppermute | solution.py:224
  20.9 1.7 collective-permute-start.5
  22.5 3.2 %collective-permute-done.3.refs_2_ = bf16[512,256]{1,0:T(8,128)(2,1)} collective-permute-done((bf16[512,256]{1,0:T(8,128)(2,1)}, bf16[512,256]{1,0:T(8,128)(2,1)}, u32[]{:S(2)}, u32[]{:S(2)}) %collective-permute-start.3) | collective-permute-done | bytes 262176 | tf_op jit(solution)/shard_map/ppermute | solution.py:224
  25.7 1.5 collective-permute-start.6
  27.2 10.3 %collective-permute-done.4.refs_3_ = bf16[512,256]{1,0:T(8,128)(2,1)} collective-permute-done((bf16[512,256]{1,0:T(8,128)(2,1)}, bf16[512,256]{1,0:T(8,128)(2,1)}, u32[]{:S(2)}, u32[]{:S(2)}) %collective-permute-start.4) | collective-permute-done | bytes 262176 | tf_op jit(solution)/shard_map/ppermute | solution.py:224
  37.5 1.5 collective-permute-start.7
  40.9 6.1 %collective-permute-done.7.refs_6_ = bf16[512,256]{1,0:T(8,128)(2,1)} collective-permute-done((bf16[512,256]{1,0:T(8,128)(2,1)}, bf16[512,256]{1,0:T(8,128)(2,1)}, u32[]{:S(2)}, u32[]{:S(2)}) %collective-permute-start.7) | collective-permute-done | bytes 262176 | tf_op jit(solution)/shard_map/ppermute | solution.py:221
  47.0 1.6 collective-permute-start.15
  48.5 3.1 %collective-permute-done.8.refs_7_ = bf16[512,256]{1,0:T(8,128)(2,1)} collective-permute-done((bf16[512,256]{1,0:T(8,128)(2,1)}, bf16[512,256]{1,0:T(8,128)(2,1)}, u32[]{:S(2)}, u32[]{:S(2)}) %collective-permute-start.8) | collective-permute-done | bytes 262176 | tf_op jit(solution)/shard_map/ppermute | solution.py:221
  51.7 1.7 collective-permute-start.16
  53.3 1.5 collective-permute-start.17
  54.9 2.8 %copy-done.1 = bf16[384,8192]{1,0:T(8,128)(2,1)S(1)} copy-done((bf16[384,8192]{1,0:T(8,128)(2,1)S(1)}, bf16[384,8192]{1,0:T(8,128)(2,1)}, u32[]{:S(2)}) %copy-start.1) | copy-done | bytes 6291480
  59.6 8.3 %project.2.mine_ref = f32[768,256]{1,0:T(8,128)} custom-call(s32[8]{0:T(128)S(1)} %stack.150.at_ref, bf16[384,8192]{1,0:T(8,128)(2,1)S(1)} %copy-done.1, bf16[384,4096]{1,0:T(8,128)(2,1)} %collective-permute-done.1.sib_ref, bf16[512,256]{1,0:T(8,128)(2,1)} %get-tuple-element.28.refs_0_, bf16[512,256]{1,0:T(8,128)(2,1)} %collective-permute-done.2.refs_1_, ...), custom_call_target="tpu_custom_call" | custom-call | flops 1610612736 | bytes 8388608 | tf_op jit(solution)/shard_map/project/pallas_call | solution.py:100
  68.5 1.6 collective-permute-start.19
  70.6 6.8 %collective-permute-done.18.refs_5_ = bf16[512,256]{1,0:T(8,128)(2,1)S(1)} collective-permute-done((bf16[512,256]{1,0:T(8,128)(2,1)}, bf16[512,256]{1,0:T(8,128)(2,1)S(1)}, u32[]{:S(2)}, u32[]{:S(2)}) %collective-permute-start.18) | collective-permute-done | bytes 262176 | tf_op jit(solution)/shard_map/ppermute | solution.py:221
  77.3 5.6 %collective-permute-done.19.refs_6_ = bf16[512,256]{1,0:T(8,128)(2,1)S(1)} collective-permute-done((bf16[512,256]{1,0:T(8,128)(2,1)}, bf16[512,256]{1,0:T(8,128)(2,1)S(1)}, u32[]{:S(2)}, u32[]{:S(2)}) %collective-permute-start.19) | collective-permute-done | bytes 262176 | tf_op jit(solution)/shard_map/ppermute | solution.py:221
  83.0 5.2 %collective-permute-done.20.refs_7_ = bf16[512,256]{1,0:T(8,128)(2,1)S(1)} collective-permute-done((bf16[512,256]{1,0:T(8,128)(2,1)}, bf16[512,256]{1,0:T(8,128)(2,1)S(1)}, u32[]{:S(2)}, u32[]{:S(2)}) %collective-permute-start.20) | collective-permute-done | bytes 262176 | tf_op jit(solution)/shard_map/ppermute | solution.py:221
  88.1 8.1 %project.3.mine_ref = f32[768,256]{1,0:T(8,128)} custom-call(s32[8]{0:T(128)S(1)} %stack.150.at_ref, bf16[384,8192]{1,0:T(8,128)(2,1)S(1)} %copy-done.1, bf16[384,4096]{1,0:T(8,128)(2,1)} %collective-permute-done.1.sib_ref, bf16[512,256]{1,0:T(8,128)(2,1)S(1)} %get-tuple-element.27.refs_0_, bf16[512,256]{1,0:T(8,128)(2,1)} %collective-permute-done.14.refs_1_, ...), custom_call_target="tpu_custom_call" | custom-call | flops 1610612736 | bytes 8388608 | tf_op jit(solution)/shard_map/project/pallas_call | solution.py:100
  96.3 6.9 %outer.2 = (bf16[4,256,256]{2,1,0:T(8,128)(2,1)S(1)}, f32[4,256,256]{2,1,0:T(8,128)S(1)}) custom-call(s32[8]{0:T(128)S(1)} %stack.142.at_ref, bf16[384,4096]{1,0:T(8,128)(2,1)S(1)} %copy-done.2, bf16[384,2048]{1,0:T(8,128)(2,1)} %collective-permute-done.sib_ref, f32[768,256]{1,0:T(8,128)} %project.2.mine_ref, f32[768,256]{1,0:T(8,128)} %collective-permute-done.9.theirs_ref), custom_call_target="tpu_custom_call" | custom-call | flops 805306368 | bytes 4718592 | tf_op jit(solution)/shard_map/outer/pallas_call | solution.py:144
  103.8 6.9 %outer.3 = (bf16[4,256,256]{2,1,0:T(8,128)(2,1)S(1)}, f32[4,256,256]{2,1,0:T(8,128)S(1)}) custom-call(s32[8]{0:T(128)S(1)} %stack.142.at_ref, bf16[384,4096]{1,0:T(8,128)(2,1)S(1)} %copy-done.2, bf16[384,2048]{1,0:T(8,128)(2,1)} %collective-permute-done.sib_ref, f32[768,256]{1,0:T(8,128)} %project.3.mine_ref, f32[768,256]{1,0:T(8,128)} %collective-permute-done.21.theirs_ref), custom_call_target="tpu_custom_call" | custom-call | flops 805306368 | bytes 4718592 | tf_op jit(solution)/shard_map/outer/pallas_call | solution.py:144
  110.8 1.6 collective-permute-start.22
  112.4 5.7 %collective-permute-done.10 = bf16[4,256,256]{2,1,0:T(8,128)(2,1)S(1)} collective-permute-done((bf16[4,256,256]{2,1,0:T(8,128)(2,1)S(1)}, bf16[4,256,256]{2,1,0:T(8,128)(2,1)S(1)}, u32[]{:S(2)}, u32[]{:S(2)}) %collective-permute-start.10) | collective-permute-done | bytes 524320 | tf_op jit(solution)/shard_map/ppermute | solution.py:221
  118.9 3.3 %collective-permute-start.12 = (bf16[256,256]{1,0:T(8,128)(2,1)S(1)}, bf16[256,256]{1,0:T(8,128)(2,1)S(1)}, u32[]{:S(2)}, u32[]{:S(2)}) collective-permute-start(bf16[256,256]{1,0:T(8,128)(2,1)S(1)} %get-tuple-element.31), channel_id=1, source_target_pairs={{0,12},{1,13},{2,14},{3,15},{4,0},{5,1},{6,2},{7,3},{8,4},{9,5},{1... | collective-permute-start | bytes 393224 | tf_op jit(solution)/shard_map/ppermute | solution.py:224
  122.2 6.7 %collective-permute-done.22 = bf16[4,256,256]{2,1,0:T(8,128)(2,1)S(1)} collective-permute-done((bf16[4,256,256]{2,1,0:T(8,128)(2,1)S(1)}, bf16[4,256,256]{2,1,0:T(8,128)(2,1)S(1)}, u32[]{:S(2)}, u32[]{:S(2)}) %collective-permute-start.22) | collective-permute-done | bytes 524320 | tf_op jit(solution)/shard_map/ppermute | solution.py:221
  129.7 3.3 %collective-permute-start.24 = (bf16[256,256]{1,0:T(8,128)(2,1)S(1)}, bf16[256,256]{1,0:T(8,128)(2,1)S(1)}, u32[]{:S(2)}, u32[]{:S(2)}) collective-permute-start(bf16[256,256]{1,0:T(8,128)(2,1)S(1)} %get-tuple-element.26), channel_id=1, source_target_pairs={{0,12},{1,13},{2,14},{3,15},{4,0},{5,1},{6,2},{7,3},{8,4},{9,5},{1... | collective-permute-start | bytes 393224 | tf_op jit(solution)/shard_map/ppermute | solution.py:224
  133.0 4.4 %collective-permute-done.23 = bf16[256,256]{1,0:T(8,128)(2,1)S(1)} collective-permute-done((bf16[256,256]{1,0:T(8,128)(2,1)S(1)}, bf16[256,256]{1,0:T(8,128)(2,1)S(1)}, u32[]{:S(2)}, u32[]{:S(2)}) %collective-permute-start.23) | collective-permute-done | bytes 131104 | tf_op jit(solution)/shard_map/ppermute | solution.py:224
  138.6 5.1 %collective-permute-done.25 = bf16[256,256]{1,0:T(8,128)(2,1)S(1)} collective-permute-done((bf16[256,256]{1,0:T(8,128)(2,1)S(1)}, bf16[256,256]{1,0:T(8,128)(2,1)S(1)}, u32[]{:S(2)}, u32[]{:S(2)}) %collective-permute-start.25) | collective-permute-done | bytes 131104 | tf_op jit(solution)/shard_map/ppermute | solution.py:224
  145.2 3.7 %collective-permute-start.28 = (bf16[256,256]{1,0:T(8,128)(2,1)S(1)}, bf16[256,256]{1,0:T(8,128)(2,1)S(1)}, u32[]{:S(2)}, u32[]{:S(2)}) collective-permute-start(bf16[256,256]{1,0:T(8,128)(2,1)S(1)} %get-tuple-element.21.refs_0_), channel_id=1, source_target_pairs={{0,12},{1,13},{2,14},{3,15},{4,0},{5,1},{6,2},{7,3},{8,4},{9,5},{1... | collective-permute-start | bytes 393224 | tf_op jit(solution)/shard_map/ppermute | solution.py:224
  148.9 2.0 collective-permute-start.29
  150.9 2.4 %collective-permute-done.26.refs_2_ = bf16[256,256]{1,0:T(8,128)(2,1)S(1)} collective-permute-done((bf16[256,256]{1,0:T(8,128)(2,1)S(1)}, bf16[256,256]{1,0:T(8,128)(2,1)S(1)}, u32[]{:S(2)}, u32[]{:S(2)}) %collective-permute-start.26) | collective-permute-done | bytes 131104 | tf_op jit(solution)/shard_map/ppermute | solution.py:224
  153.9 2.3 %collective-permute-done.27.refs_3_ = bf16[256,256]{1,0:T(8,128)(2,1)S(1)} collective-permute-done((bf16[256,256]{1,0:T(8,128)(2,1)S(1)}, bf16[256,256]{1,0:T(8,128)(2,1)S(1)}, u32[]{:S(2)}, u32[]{:S(2)}) %collective-permute-start.27) | collective-permute-done | bytes 131104 | tf_op jit(solution)/shard_map/ppermute | solution.py:224
  158.5 9.9 %collective-permute-done.30.refs_6_ = bf16[256,256]{1,0:T(8,128)(2,1)S(1)} collective-permute-done((bf16[256,256]{1,0:T(8,128)(2,1)S(1)}, bf16[256,256]{1,0:T(8,128)(2,1)S(1)}, u32[]{:S(2)}, u32[]{:S(2)}) %collective-permute-start.30) | collective-permute-done | bytes 131104 | tf_op jit(solution)/shard_map/ppermute | solution.py:224
  168.4 2.7 %collective-permute-done.31.refs_7_ = bf16[256,256]{1,0:T(8,128)(2,1)S(1)} collective-permute-done((bf16[256,256]{1,0:T(8,128)(2,1)S(1)}, bf16[256,256]{1,0:T(8,128)(2,1)S(1)}, u32[]{:S(2)}, u32[]{:S(2)}) %collective-permute-start.31) | collective-permute-done | bytes 131104 | tf_op jit(solution)/shard_map/ppermute | solution.py:224
  171.6 1.5 collective-permute-start.35
  173.6 1.5 collective-permute-start.37
  175.7 1.8 collective-permute-done.34.refs_10_
  178.0 2.3 %collective-permute-done.35.refs_11_ = bf16[256,256]{1,0:T(8,128)(2,1)S(1)} collective-permute-done((bf16[256,256]{1,0:T(8,128)(2,1)S(1)}, bf16[256,256]{1,0:T(8,128)(2,1)S(1)}, u32[]{:S(2)}, u32[]{:S(2)}) %collective-permute-start.35) | collective-permute-done | bytes 131104 | tf_op jit(solution)/shard_map/ppermute | solution.py:221
  180.3 2.8 %collective-permute-done.36.refs_12_ = bf16[256,256]{1,0:T(8,128)(2,1)S(1)} collective-permute-done((bf16[256,256]{1,0:T(8,128)(2,1)S(1)}, bf16[256,256]{1,0:T(8,128)(2,1)S(1)}, u32[]{:S(2)}, u32[]{:S(2)}) %collective-permute-start.36) | collective-permute-done | bytes 131104 | tf_op jit(solution)/shard_map/ppermute | solution.py:221
  183.1 2.8 %collective-permute-done.37.refs_13_ = bf16[256,256]{1,0:T(8,128)(2,1)S(1)} collective-permute-done((bf16[256,256]{1,0:T(8,128)(2,1)S(1)}, bf16[256,256]{1,0:T(8,128)(2,1)S(1)}, u32[]{:S(2)}, u32[]{:S(2)}) %collective-permute-start.37) | collective-permute-done | bytes 131104 | tf_op jit(solution)/shard_map/ppermute | solution.py:221
  185.9 2.8 %collective-permute-done.38.refs_14_ = bf16[256,256]{1,0:T(8,128)(2,1)S(1)} collective-permute-done((bf16[256,256]{1,0:T(8,128)(2,1)S(1)}, bf16[256,256]{1,0:T(8,128)(2,1)S(1)}, u32[]{:S(2)}, u32[]{:S(2)}) %collective-permute-start.38) | collective-permute-done | bytes 131104 | tf_op jit(solution)/shard_map/ppermute | solution.py:221
  188.7 1.9 collective-permute-done.39.refs_15_
  193.3 2.3 %pad_maximum_fusion = (f32[256,512]{1,0:T(8,128)}, f32[256,512]{1,0:T(8,128)}) fusion(f32[256,256]{1,0:T(8,128)} %get-tuple-element.12, f32[256,256]{1,0:T(8,128)} %get-tuple-element.23, f32[256,256]{1,0:T(8,128)} %get-tuple-element.13, f32[256,256]{1,0:T(8,128)} %get-tuple-element.22), kind=kLoop, calls=%fused_computation.2 | loop fusion | flops 262144 | bytes 2097152 | tf_op jit(solution)/shard_map/concatenate | solution.py:266
  195.6 10.8 %back.1 = bf16[4096,512]{1,0:T(8,128)(2,1)} custom-call(s32[16]{0:T(128)S(1)} %stack.135.at_ref, bf16[512,512]{1,0:T(8,128)(2,1)S(1)} %copy-done.4, bf16[256,256]{1,0:T(8,128)(2,1)S(1)} %get-tuple-element.21.refs_0_, bf16[256,256]{1,0:T(8,128)(2,1)S(1)} %get-tuple-element.11.refs_1_, bf16[256,256]{1,0:T(8,128)(2,1)S(1)} %collective-permute-done.26.refs_2_, ...), custom_call_target="tpu_custom_call" | custom-call | flops 2147483648 | bytes 8388608 | tf_op jit(solution)/shard_map/back/pallas_call | solution.py:193
  (105 shorter events, 20.0 us)
Async XLA Ops:
  7.6 45.8 %collective-permute-start.1 = (bf16[384,4096]{1,0:T(8,128)(2,1)}, bf16[384,4096]{1,0:T(8,128)(2,1)}, u32[]{:S(2)}, u32[]{:S(2)}) collective-permute-start(bf16[384,4096]{1,0:T(8,128)(2,1)} %pick.3), channel_id=1, source_target_pairs={{0,1},{1,0},{2,3},{3,2},{4,5},{5,4},{6,7},{7,6},{8,9},{9,8},{10,11... | collective-permute-start | bytes 9437192 | tf_op jit(solution)/shard_map/ppermute | solution.py:218
  8.7 12.1 %collective-permute-start.2 = (bf16[512,256]{1,0:T(8,128)(2,1)}, bf16[512,256]{1,0:T(8,128)(2,1)}, u32[]{:S(2)}, u32[]{:S(2)}) collective-permute-start(bf16[512,256]{1,0:T(8,128)(2,1)} %get-tuple-element.28.refs_0_), channel_id=1, source_target_pairs={{0,4},{1,5},{2,6},{3,7},{4,8},{5,9},{6,10},{7,11},{8,12},{9,13},{1... | collective-permute-start | bytes 786440 | tf_op jit(solution)/shard_map/ppermute | solution.py:224
  11.3 14.4 %collective-permute-start.3 = (bf16[512,256]{1,0:T(8,128)(2,1)}, bf16[512,256]{1,0:T(8,128)(2,1)}, u32[]{:S(2)}, u32[]{:S(2)}) collective-permute-start(bf16[512,256]{1,0:T(8,128)(2,1)} %get-tuple-element.28.refs_0_), channel_id=1, source_target_pairs={{0,12},{1,13},{2,14},{3,15},{4,0},{5,1},{6,2},{7,3},{8,4},{9,5},{1... | collective-permute-start | bytes 786440 | tf_op jit(solution)/shard_map/ppermute | solution.py:224
  17.1 79.2 %collective-permute-start = (bf16[384,2048]{1,0:T(8,128)(2,1)}, bf16[384,2048]{1,0:T(8,128)(2,1)}, u32[]{:S(2)}, u32[]{:S(2)}) collective-permute-start(bf16[384,2048]{1,0:T(8,128)(2,1)} %pick.2), channel_id=1, source_target_pairs={{0,1},{1,0},{2,3},{3,2},{4,5},{5,4},{6,7},{7,6},{8,9},{9,8},{10,11... | collective-permute-start | bytes 4718600 | tf_op jit(solution)/shard_map/ppermute | solution.py:218
  17.4 20.1 %collective-permute-start.4 = (bf16[512,256]{1,0:T(8,128)(2,1)}, bf16[512,256]{1,0:T(8,128)(2,1)}, u32[]{:S(2)}, u32[]{:S(2)}) collective-permute-start(bf16[512,256]{1,0:T(8,128)(2,1)} %get-tuple-element.28.refs_0_), channel_id=1, source_target_pairs={{0,8},{1,9},{2,10},{3,11},{4,12},{5,13},{6,14},{7,15},{8,0},{9,1},... | collective-permute-start | bytes 786440 | tf_op jit(solution)/shard_map/ppermute | solution.py:224
  20.9 18.1 %collective-permute-start.5 = (bf16[512,256]{1,0:T(8,128)(2,1)}, bf16[512,256]{1,0:T(8,128)(2,1)S(1)}, u32[]{:S(2)}, u32[]{:S(2)}) collective-permute-start(bf16[512,256]{1,0:T(8,128)(2,1)} %get-tuple-element.28.refs_0_), channel_id=1, source_target_pairs={{0,2},{1,3},{2,0},{3,1},{4,6},{5,7},{6,4},{7,5},{8,10},{9,11},{10,... | collective-permute-start | bytes 786440 | tf_op jit(solution)/shard_map/ppermute | solution.py:221
  25.7 14.5 %collective-permute-start.6 = (bf16[512,256]{1,0:T(8,128)(2,1)}, bf16[512,256]{1,0:T(8,128)(2,1)S(1)}, u32[]{:S(2)}, u32[]{:S(2)}) collective-permute-start(bf16[512,256]{1,0:T(8,128)(2,1)} %collective-permute-done.2.refs_1_), channel_id=1, source_target_pairs={{0,2},{1,3},{2,0},{3,1},{4,6},{5,7},{6,4},{7,5},{8,10},{9,11},{10,... | collective-permute-start | bytes 786440 | tf_op jit(solution)/shard_map/ppermute | solution.py:221
  37.5 9.5 %collective-permute-start.7 = (bf16[512,256]{1,0:T(8,128)(2,1)}, bf16[512,256]{1,0:T(8,128)(2,1)}, u32[]{:S(2)}, u32[]{:S(2)}) collective-permute-start(bf16[512,256]{1,0:T(8,128)(2,1)} %collective-permute-done.3.refs_2_), channel_id=1, source_target_pairs={{0,2},{1,3},{2,0},{3,1},{4,6},{5,7},{6,4},{7,5},{8,10},{9,11},{10,... | collective-permute-start | bytes 786440 | tf_op jit(solution)/shard_map/ppermute | solution.py:221
  39.7 12.0 %collective-permute-start.8 = (bf16[512,256]{1,0:T(8,128)(2,1)}, bf16[512,256]{1,0:T(8,128)(2,1)}, u32[]{:S(2)}, u32[]{:S(2)}) collective-permute-start(bf16[512,256]{1,0:T(8,128)(2,1)} %collective-permute-done.4.refs_3_), channel_id=1, source_target_pairs={{0,2},{1,3},{2,0},{3,1},{4,6},{5,7},{6,4},{7,5},{8,10},{9,11},{10,... | collective-permute-start | bytes 786440 | tf_op jit(solution)/shard_map/ppermute | solution.py:221
  40.9 27.0 %collective-permute-start.14 = (bf16[512,256]{1,0:T(8,128)(2,1)S(1)}, bf16[512,256]{1,0:T(8,128)(2,1)}, u32[]{:S(2)}, u32[]{:S(2)}) collective-permute-start(bf16[512,256]{1,0:T(8,128)(2,1)S(1)} %get-tuple-element.27.refs_0_), channel_id=1, source_target_pairs={{0,4},{1,5},{2,6},{3,7},{4,8},{5,9},{6,10},{7,11},{8,12},{9,13},{1... | collective-permute-start | bytes 786440 | tf_op jit(solution)/shard_map/ppermute | solution.py:224
  47.0 21.0 %collective-permute-start.15 = (bf16[512,256]{1,0:T(8,128)(2,1)S(1)}, bf16[512,256]{1,0:T(8,128)(2,1)}, u32[]{:S(2)}, u32[]{:S(2)}) collective-permute-start(bf16[512,256]{1,0:T(8,128)(2,1)S(1)} %get-tuple-element.27.refs_0_), channel_id=1, source_target_pairs={{0,12},{1,13},{2,14},{3,15},{4,0},{5,1},{6,2},{7,3},{8,4},{9,5},{1... | collective-permute-start | bytes 786440 | tf_op jit(solution)/shard_map/ppermute | solution.py:224
  51.7 16.9 %collective-permute-start.16 = (bf16[512,256]{1,0:T(8,128)(2,1)S(1)}, bf16[512,256]{1,0:T(8,128)(2,1)}, u32[]{:S(2)}, u32[]{:S(2)}) collective-permute-start(bf16[512,256]{1,0:T(8,128)(2,1)S(1)} %get-tuple-element.27.refs_0_), channel_id=1, source_target_pairs={{0,8},{1,9},{2,10},{3,11},{4,12},{5,13},{6,14},{7,15},{8,0},{9,1},... | collective-permute-start | bytes 786440 | tf_op jit(solution)/shard_map/ppermute | solution.py:224
  53.3 16.8 %collective-permute-start.17 = (bf16[512,256]{1,0:T(8,128)(2,1)S(1)}, bf16[512,256]{1,0:T(8,128)(2,1)}, u32[]{:S(2)}, u32[]{:S(2)}) collective-permute-start(bf16[512,256]{1,0:T(8,128)(2,1)S(1)} %get-tuple-element.27.refs_0_), channel_id=1, source_target_pairs={{0,2},{1,3},{2,0},{3,1},{4,6},{5,7},{6,4},{7,5},{8,10},{9,11},{10,... | collective-permute-start | bytes 786440 | tf_op jit(solution)/shard_map/ppermute | solution.py:221
  67.9 28.4 %collective-permute-start.9 = (f32[768,256]{1,0:T(8,128)}, f32[768,256]{1,0:T(8,128)}, u32[]{:S(2)}, u32[]{:S(2)}) collective-permute-start(f32[768,256]{1,0:T(8,128)} %project.2.mine_ref), channel_id=1, source_target_pairs={{0,1},{1,0},{2,3},{3,2},{4,5},{5,4},{6,7},{7,6},{8,9},{9,8},{10,11... | collective-permute-start | bytes 2359304 | tf_op jit(solution)/shard_map/ppermute | solution.py:218
  68.0 9.4 %collective-permute-start.18 = (bf16[512,256]{1,0:T(8,128)(2,1)}, bf16[512,256]{1,0:T(8,128)(2,1)S(1)}, u32[]{:S(2)}, u32[]{:S(2)}) collective-permute-start(bf16[512,256]{1,0:T(8,128)(2,1)} %collective-permute-done.14.refs_1_), channel_id=1, source_target_pairs={{0,2},{1,3},{2,0},{3,1},{4,6},{5,7},{6,4},{7,5},{8,10},{9,11},{10,... | collective-permute-start | bytes 786440 | tf_op jit(solution)/shard_map/ppermute | solution.py:221
  68.5 14.4 %collective-permute-start.19 = (bf16[512,256]{1,0:T(8,128)(2,1)}, bf16[512,256]{1,0:T(8,128)(2,1)S(1)}, u32[]{:S(2)}, u32[]{:S(2)}) collective-permute-start(bf16[512,256]{1,0:T(8,128)(2,1)} %collective-permute-done.15.refs_2_), channel_id=1, source_target_pairs={{0,2},{1,3},{2,0},{3,1},{4,6},{5,7},{6,4},{7,5},{8,10},{9,11},{10,... | collective-permute-start | bytes 786440 | tf_op jit(solution)/shard_map/ppermute | solution.py:221
  70.1 18.0 %collective-permute-start.20 = (bf16[512,256]{1,0:T(8,128)(2,1)}, bf16[512,256]{1,0:T(8,128)(2,1)S(1)}, u32[]{:S(2)}, u32[]{:S(2)}) collective-permute-start(bf16[512,256]{1,0:T(8,128)(2,1)} %collective-permute-done.16.refs_3_), channel_id=1, source_target_pairs={{0,2},{1,3},{2,0},{3,1},{4,6},{5,7},{6,4},{7,5},{8,10},{9,11},{10,... | collective-permute-start | bytes 786440 | tf_op jit(solution)/shard_map/ppermute | solution.py:221
  96.2 7.6 %collective-permute-start.21 = (f32[768,256]{1,0:T(8,128)}, f32[768,256]{1,0:T(8,128)}, u32[]{:S(2)}, u32[]{:S(2)}) collective-permute-start(f32[768,256]{1,0:T(8,128)} %project.3.mine_ref), channel_id=1, source_target_pairs={{0,1},{1,0},{2,3},{3,2},{4,5},{5,4},{6,7},{7,6},{8,9},{9,8},{10,11... | collective-permute-start | bytes 2359304 | tf_op jit(solution)/shard_map/ppermute | solution.py:218
  103.3 14.8 %collective-permute-start.10 = (bf16[4,256,256]{2,1,0:T(8,128)(2,1)S(1)}, bf16[4,256,256]{2,1,0:T(8,128)(2,1)S(1)}, u32[]{:S(2)}, u32[]{:S(2)}) collective-permute-start(bf16[4,256,256]{2,1,0:T(8,128)(2,1)S(1)} %get-tuple-element.8), channel_id=1, source_target_pairs={{0,2},{1,3},{2,0},{3,1},{4,6},{5,7},{6,4},{7,5},{8,10},{9,11},{10,... | collective-permute-start | bytes 1572872 | tf_op jit(solution)/shard_map/ppermute | solution.py:221
  110.8 18.1 %collective-permute-start.22 = (bf16[4,256,256]{2,1,0:T(8,128)(2,1)S(1)}, bf16[4,256,256]{2,1,0:T(8,128)(2,1)S(1)}, u32[]{:S(2)}, u32[]{:S(2)}) collective-permute-start(bf16[4,256,256]{2,1,0:T(8,128)(2,1)S(1)} %get-tuple-element.10), channel_id=1, source_target_pairs={{0,2},{1,3},{2,0},{3,1},{4,6},{5,7},{6,4},{7,5},{8,10},{9,11},{10,... | collective-permute-start | bytes 1572872 | tf_op jit(solution)/shard_map/ppermute | solution.py:221
  118.3 14.7 %collective-permute-start.11 = (bf16[256,256]{1,0:T(8,128)(2,1)S(1)}, bf16[256,256]{1,0:T(8,128)(2,1)S(1)}, u32[]{:S(2)}, u32[]{:S(2)}) collective-permute-start(bf16[256,256]{1,0:T(8,128)(2,1)S(1)} %get-tuple-element.29), channel_id=1, source_target_pairs={{0,4},{1,5},{2,6},{3,7},{4,8},{5,9},{6,10},{7,11},{8,12},{9,13},{1... | collective-permute-start | bytes 393224 | tf_op jit(solution)/shard_map/ppermute | solution.py:224
  118.9 14.1 %collective-permute-start.12 = (bf16[256,256]{1,0:T(8,128)(2,1)S(1)}, bf16[256,256]{1,0:T(8,128)(2,1)S(1)}, u32[]{:S(2)}, u32[]{:S(2)}) collective-permute-start(bf16[256,256]{1,0:T(8,128)(2,1)S(1)} %get-tuple-element.31), channel_id=1, source_target_pairs={{0,12},{1,13},{2,14},{3,15},{4,0},{5,1},{6,2},{7,3},{8,4},{9,5},{1... | collective-permute-start | bytes 393224 | tf_op jit(solution)/shard_map/ppermute | solution.py:224
  122.2 10.9 %collective-permute-start.13 = (bf16[256,256]{1,0:T(8,128)(2,1)S(1)}, bf16[256,256]{1,0:T(8,128)(2,1)S(1)}, u32[]{:S(2)}, u32[]{:S(2)}) collective-permute-start(bf16[256,256]{1,0:T(8,128)(2,1)S(1)} %get-tuple-element.30), channel_id=1, source_target_pairs={{0,8},{1,9},{2,10},{3,11},{4,12},{5,13},{6,14},{7,15},{8,0},{9,1},... | collective-permute-start | bytes 393224 | tf_op jit(solution)/shard_map/ppermute | solution.py:224
  129.1 8.3 %collective-permute-start.23 = (bf16[256,256]{1,0:T(8,128)(2,1)S(1)}, bf16[256,256]{1,0:T(8,128)(2,1)S(1)}, u32[]{:S(2)}, u32[]{:S(2)}) collective-permute-start(bf16[256,256]{1,0:T(8,128)(2,1)S(1)} %get-tuple-element.24), channel_id=1, source_target_pairs={{0,4},{1,5},{2,6},{3,7},{4,8},{5,9},{6,10},{7,11},{8,12},{9,13},{1... | collective-permute-start | bytes 393224 | tf_op jit(solution)/shard_map/ppermute | solution.py:224
  129.7 8.9 %collective-permute-start.24 = (bf16[256,256]{1,0:T(8,128)(2,1)S(1)}, bf16[256,256]{1,0:T(8,128)(2,1)S(1)}, u32[]{:S(2)}, u32[]{:S(2)}) collective-permute-start(bf16[256,256]{1,0:T(8,128)(2,1)S(1)} %get-tuple-element.26), channel_id=1, source_target_pairs={{0,12},{1,13},{2,14},{3,15},{4,0},{5,1},{6,2},{7,3},{8,4},{9,5},{1... | collective-permute-start | bytes 393224 | tf_op jit(solution)/shard_map/ppermute | solution.py:224
  133.0 10.7 %collective-permute-start.25 = (bf16[256,256]{1,0:T(8,128)(2,1)S(1)}, bf16[256,256]{1,0:T(8,128)(2,1)S(1)}, u32[]{:S(2)}, u32[]{:S(2)}) collective-permute-start(bf16[256,256]{1,0:T(8,128)(2,1)S(1)} %get-tuple-element.25), channel_id=1, source_target_pairs={{0,8},{1,9},{2,10},{3,11},{4,12},{5,13},{6,14},{7,15},{8,0},{9,1},... | collective-permute-start | bytes 393224 | tf_op jit(solution)/shard_map/ppermute | solution.py:224
  145.1 8.3 %collective-permute-start.26 = (bf16[256,256]{1,0:T(8,128)(2,1)S(1)}, bf16[256,256]{1,0:T(8,128)(2,1)S(1)}, u32[]{:S(2)}, u32[]{:S(2)}) collective-permute-start(bf16[256,256]{1,0:T(8,128)(2,1)S(1)} %get-tuple-element.21.refs_0_), channel_id=1, source_target_pairs={{0,4},{1,5},{2,6},{3,7},{4,8},{5,9},{6,10},{7,11},{8,12},{9,13},{1... | collective-permute-start | bytes 393224 | tf_op jit(solution)/shard_map/ppermute | solution.py:224
  145.1 11.1 %collective-permute-start.27 = (bf16[256,256]{1,0:T(8,128)(2,1)S(1)}, bf16[256,256]{1,0:T(8,128)(2,1)S(1)}, u32[]{:S(2)}, u32[]{:S(2)}) collective-permute-start(bf16[256,256]{1,0:T(8,128)(2,1)S(1)} %get-tuple-element.11.refs_1_), channel_id=1, source_target_pairs={{0,4},{1,5},{2,6},{3,7},{4,8},{5,9},{6,10},{7,11},{8,12},{9,13},{1... | collective-permute-start | bytes 393224 | tf_op jit(solution)/shard_map/ppermute | solution.py:224
  145.2 11.8 %collective-permute-start.28 = (bf16[256,256]{1,0:T(8,128)(2,1)S(1)}, bf16[256,256]{1,0:T(8,128)(2,1)S(1)}, u32[]{:S(2)}, u32[]{:S(2)}) collective-permute-start(bf16[256,256]{1,0:T(8,128)(2,1)S(1)} %get-tuple-element.21.refs_0_), channel_id=1, source_target_pairs={{0,12},{1,13},{2,14},{3,15},{4,0},{5,1},{6,2},{7,3},{8,4},{9,5},{1... | collective-permute-start | bytes 393224 | tf_op jit(solution)/shard_map/ppermute | solution.py:224
  148.9 9.6 %collective-permute-start.29 = (bf16[256,256]{1,0:T(8,128)(2,1)S(1)}, bf16[256,256]{1,0:T(8,128)(2,1)S(1)}, u32[]{:S(2)}, u32[]{:S(2)}) collective-permute-start(bf16[256,256]{1,0:T(8,128)(2,1)S(1)} %get-tuple-element.11.refs_1_), channel_id=1, source_target_pairs={{0,12},{1,13},{2,14},{3,15},{4,0},{5,1},{6,2},{7,3},{8,4},{9,5},{1... | collective-permute-start | bytes 393224 | tf_op jit(solution)/shard_map/ppermute | solution.py:224
  150.9 17.4 %collective-permute-start.30 = (bf16[256,256]{1,0:T(8,128)(2,1)S(1)}, bf16[256,256]{1,0:T(8,128)(2,1)S(1)}, u32[]{:S(2)}, u32[]{:S(2)}) collective-permute-start(bf16[256,256]{1,0:T(8,128)(2,1)S(1)} %get-tuple-element.21.refs_0_), channel_id=1, source_target_pairs={{0,8},{1,9},{2,10},{3,11},{4,12},{5,13},{6,14},{7,15},{8,0},{9,1},... | collective-permute-start | bytes 393224 | tf_op jit(solution)/shard_map/ppermute | solution.py:224
  153.3 17.7 %collective-permute-start.31 = (bf16[256,256]{1,0:T(8,128)(2,1)S(1)}, bf16[256,256]{1,0:T(8,128)(2,1)S(1)}, u32[]{:S(2)}, u32[]{:S(2)}) collective-permute-start(bf16[256,256]{1,0:T(8,128)(2,1)S(1)} %get-tuple-element.11.refs_1_), channel_id=1, source_target_pairs={{0,8},{1,9},{2,10},{3,11},{4,12},{5,13},{6,14},{7,15},{8,0},{9,1},... | collective-permute-start | bytes 393224 | tf_op jit(solution)/shard_map/ppermute | solution.py:224
  156.2 15.4 %collective-permute-start.32 = (bf16[256,256]{1,0:T(8,128)(2,1)S(1)}, bf16[256,256]{1,0:T(8,128)(2,1)S(1)}, u32[]{:S(2)}, u32[]{:S(2)}) collective-permute-start(bf16[256,256]{1,0:T(8,128)(2,1)S(1)} %get-tuple-element.21.refs_0_), channel_id=1, source_target_pairs={{0,2},{1,3},{2,0},{3,1},{4,6},{5,7},{6,4},{7,5},{8,10},{9,11},{10,... | collective-permute-start | bytes 393224 | tf_op jit(solution)/shard_map/ppermute | solution.py:221
  157.0 16.1 %collective-permute-start.33 = (bf16[256,256]{1,0:T(8,128)(2,1)S(1)}, bf16[256,256]{1,0:T(8,128)(2,1)S(1)}, u32[]{:S(2)}, u32[]{:S(2)}) collective-permute-start(bf16[256,256]{1,0:T(8,128)(2,1)S(1)} %get-tuple-element.11.refs_1_), channel_id=1, source_target_pairs={{0,2},{1,3},{2,0},{3,1},{4,6},{5,7},{6,4},{7,5},{8,10},{9,11},{10,... | collective-permute-start | bytes 393224 | tf_op jit(solution)/shard_map/ppermute | solution.py:221
  158.5 15.2 %collective-permute-start.40 = (bf16[256,256]{1,0:T(8,128)(2,1)S(1)}, bf16[256,256]{1,0:T(8,128)(2,1)S(1)}, u32[]{:S(2)}, u32[]{:S(2)}) collective-permute-start(bf16[256,256]{1,0:T(8,128)(2,1)S(1)} %get-tuple-element.21.refs_0_), channel_id=1, source_target_pairs={{0,1},{1,0},{2,3},{3,2},{4,5},{5,4},{6,7},{7,6},{8,9},{9,8},{10,11... | collective-permute-start | bytes 393224 | tf_op jit(solution)/shard_map/ppermute | solution.py:218
  168.4 6.8 %collective-permute-start.41 = (bf16[256,256]{1,0:T(8,128)(2,1)S(1)}, bf16[256,256]{1,0:T(8,128)(2,1)S(1)}, u32[]{:S(2)}, u32[]{:S(2)}) collective-permute-start(bf16[256,256]{1,0:T(8,128)(2,1)S(1)} %get-tuple-element.11.refs_1_), channel_id=1, source_target_pairs={{0,1},{1,0},{2,3},{3,2},{4,5},{5,4},{6,7},{7,6},{8,9},{9,8},{10,11... | collective-permute-start | bytes 393224 | tf_op jit(solution)/shard_map/ppermute | solution.py:218
  171.1 6.4 %collective-permute-start.34 = (bf16[256,256]{1,0:T(8,128)(2,1)S(1)}, bf16[256,256]{1,0:T(8,128)(2,1)S(1)}, u32[]{:S(2)}, u32[]{:S(2)}) collective-permute-start(bf16[256,256]{1,0:T(8,128)(2,1)S(1)} %collective-permute-done.26.refs_2_), channel_id=1, source_target_pairs={{0,2},{1,3},{2,0},{3,1},{4,6},{5,7},{6,4},{7,5},{8,10},{9,11},{10,... | collective-permute-start | bytes 393224 | tf_op jit(solution)/shard_map/ppermute | solution.py:221
  171.6 8.6 %collective-permute-start.35 = (bf16[256,256]{1,0:T(8,128)(2,1)S(1)}, bf16[256,256]{1,0:T(8,128)(2,1)S(1)}, u32[]{:S(2)}, u32[]{:S(2)}) collective-permute-start(bf16[256,256]{1,0:T(8,128)(2,1)S(1)} %collective-permute-done.27.refs_3_), channel_id=1, source_target_pairs={{0,2},{1,3},{2,0},{3,1},{4,6},{5,7},{6,4},{7,5},{8,10},{9,11},{10,... | collective-permute-start | bytes 393224 | tf_op jit(solution)/shard_map/ppermute | solution.py:221
  173.1 9.9 %collective-permute-start.36 = (bf16[256,256]{1,0:T(8,128)(2,1)S(1)}, bf16[256,256]{1,0:T(8,128)(2,1)S(1)}, u32[]{:S(2)}, u32[]{:S(2)}) collective-permute-start(bf16[256,256]{1,0:T(8,128)(2,1)S(1)} %collective-permute-done.28.refs_4_), channel_id=1, source_target_pairs={{0,2},{1,3},{2,0},{3,1},{4,6},{5,7},{6,4},{7,5},{8,10},{9,11},{10,... | collective-permute-start | bytes 393224 | tf_op jit(solution)/shard_map/ppermute | solution.py:221
  173.6 12.2 %collective-permute-start.37 = (bf16[256,256]{1,0:T(8,128)(2,1)S(1)}, bf16[256,256]{1,0:T(8,128)(2,1)S(1)}, u32[]{:S(2)}, u32[]{:S(2)}) collective-permute-start(bf16[256,256]{1,0:T(8,128)(2,1)S(1)} %collective-permute-done.29.refs_5_), channel_id=1, source_target_pairs={{0,2},{1,3},{2,0},{3,1},{4,6},{5,7},{6,4},{7,5},{8,10},{9,11},{10,... | collective-permute-start | bytes 393224 | tf_op jit(solution)/shard_map/ppermute | solution.py:221
  175.2 13.5 %collective-permute-start.38 = (bf16[256,256]{1,0:T(8,128)(2,1)S(1)}, bf16[256,256]{1,0:T(8,128)(2,1)S(1)}, u32[]{:S(2)}, u32[]{:S(2)}) collective-permute-start(bf16[256,256]{1,0:T(8,128)(2,1)S(1)} %collective-permute-done.30.refs_6_), channel_id=1, source_target_pairs={{0,2},{1,3},{2,0},{3,1},{4,6},{5,7},{6,4},{7,5},{8,10},{9,11},{10,... | collective-permute-start | bytes 393224 | tf_op jit(solution)/shard_map/ppermute | solution.py:221
  177.4 13.1 %collective-permute-start.39 = (bf16[256,256]{1,0:T(8,128)(2,1)S(1)}, bf16[256,256]{1,0:T(8,128)(2,1)S(1)}, u32[]{:S(2)}, u32[]{:S(2)}) collective-permute-start(bf16[256,256]{1,0:T(8,128)(2,1)S(1)} %collective-permute-done.31.refs_7_), channel_id=1, source_target_pairs={{0,2},{1,3},{2,0},{3,1},{4,6},{5,7},{6,4},{7,5},{8,10},{9,11},{10,... | collective-permute-start | bytes 393224 | tf_op jit(solution)/shard_map/ppermute | solution.py:221
  180.3 10.3 %collective-permute-start.42 = (bf16[256,256]{1,0:T(8,128)(2,1)S(1)}, bf16[256,256]{1,0:T(8,128)(2,1)S(1)}, u32[]{:S(2)}, u32[]{:S(2)}) collective-permute-start(bf16[256,256]{1,0:T(8,128)(2,1)S(1)} %collective-permute-done.26.refs_2_), channel_id=1, source_target_pairs={{0,1},{1,0},{2,3},{3,2},{4,5},{5,4},{6,7},{7,6},{8,9},{9,8},{10,11... | collective-permute-start | bytes 393224 | tf_op jit(solution)/shard_map/ppermute | solution.py:218
  183.1 8.0 %collective-permute-start.43 = (bf16[256,256]{1,0:T(8,128)(2,1)S(1)}, bf16[256,256]{1,0:T(8,128)(2,1)S(1)}, u32[]{:S(2)}, u32[]{:S(2)}) collective-permute-start(bf16[256,256]{1,0:T(8,128)(2,1)S(1)} %collective-permute-done.27.refs_3_), channel_id=1, source_target_pairs={{0,1},{1,0},{2,3},{3,2},{4,5},{5,4},{6,7},{7,6},{8,9},{9,8},{10,11... | collective-permute-start | bytes 393224 | tf_op jit(solution)/shard_map/ppermute | solution.py:218
  185.9 5.3 %collective-permute-start.44 = (bf16[256,256]{1,0:T(8,128)(2,1)S(1)}, bf16[256,256]{1,0:T(8,128)(2,1)S(1)}, u32[]{:S(2)}, u32[]{:S(2)}) collective-permute-start(bf16[256,256]{1,0:T(8,128)(2,1)S(1)} %collective-permute-done.28.refs_4_), channel_id=1, source_target_pairs={{0,1},{1,0},{2,3},{3,2},{4,5},{5,4},{6,7},{7,6},{8,9},{9,8},{10,11... | collective-permute-start | bytes 393224 | tf_op jit(solution)/shard_map/ppermute | solution.py:218
  192.0 3.6 %collective-permute-start.51 = (bf16[256,256]{1,0:T(8,128)(2,1)S(1)}, bf16[256,256]{1,0:T(8,128)(2,1)S(1)}, u32[]{:S(2)}, u32[]{:S(2)}) collective-permute-start(bf16[256,256]{1,0:T(8,128)(2,1)S(1)} %collective-permute-done.35.refs_11_), channel_id=1, source_target_pairs={{0,1},{1,0},{2,3},{3,2},{4,5},{5,4},{6,7},{7,6},{8,9},{9,8},{10,11... | collective-permute-start | bytes 393224 | tf_op jit(solution)/shard_map/ppermute | solution.py:218
  192.3 3.3 %collective-permute-start.52 = (bf16[256,256]{1,0:T(8,128)(2,1)S(1)}, bf16[256,256]{1,0:T(8,128)(2,1)S(1)}, u32[]{:S(2)}, u32[]{:S(2)}) collective-permute-start(bf16[256,256]{1,0:T(8,128)(2,1)S(1)} %collective-permute-done.36.refs_12_), channel_id=1, source_target_pairs={{0,1},{1,0},{2,3},{3,2},{4,5},{5,4},{6,7},{7,6},{8,9},{9,8},{10,11... | collective-permute-start | bytes 393224 | tf_op jit(solution)/shard_map/ppermute | solution.py:218
  192.5 3.0 %collective-permute-start.53 = (bf16[256,256]{1,0:T(8,128)(2,1)S(1)}, bf16[256,256]{1,0:T(8,128)(2,1)S(1)}, u32[]{:S(2)}, u32[]{:S(2)}) collective-permute-start(bf16[256,256]{1,0:T(8,128)(2,1)S(1)} %collective-permute-done.37.refs_13_), channel_id=1, source_target_pairs={{0,1},{1,0},{2,3},{3,2},{4,5},{5,4},{6,7},{7,6},{8,9},{9,8},{10,11... | collective-permute-start | bytes 393224 | tf_op jit(solution)/shard_map/ppermute | solution.py:218
  (19 other events, 156.6 us)

commit v2 on v0

v2 whole, which is shorter than its diff:
```python
import functools
import jax
import jax.numpy as jnp
from jax import lax
from jax.experimental import pallas as pl
from jax.experimental.pallas import tpu as pltpu
from jax.sharding import PartitionSpec as P

STEP = 100

decay_first = 0.9
decay_second = 0.999
epsilon = 1e-08

CHUNKS = 2
F32, BF16 = jnp.float32, jnp.bfloat16
VMEM_LIMIT = 40 * 1024 * 1024


def adam(reduced, first_moment, second_moment):
    new_first = decay_first * first_moment + (1.0 - decay_first) * reduced
    new_second = decay_second * second_moment + (1.0 - decay_second) * reduced * reduced
    first_fix = 1.0 - decay_first**STEP
    second_fix = 1.0 - decay_second**STEP
    direction = (new_first / first_fix / (jnp.sqrt(new_second / second_fix) + epsilon)).astype(BF16)
    return new_first, new_second, direction


def plain(activations, out_grads, projector, first_moment, second_moment):
    projected = jnp.dot(
        activations,
        lax.all_gather(projector, "dp", axis=0, tiled=True),
        preferred_element_type=F32,
    ).astype(BF16)
    reduced = lax.psum_scatter(
        lax.dot_general(out_grads, projected, (((0,), (0,)), ((), ())), preferred_element_type=F32),
        "dp",
        scatter_dimension=0,
        tiled=True,
    )
    new_first, new_second, direction = adam(reduced, first_moment, second_moment)
    update = lax.dot_general(
        lax.all_gather(direction, "dp", axis=0, tiled=True),
        projector,
        (((1,), (1,)), ((), ())),
        preferred_element_type=F32,
    ).astype(BF16)
    return update, new_first, new_second


def params():
    return pltpu.CompilerParams(vmem_limit_bytes=VMEM_LIMIT)


def cost(flops, moved):
    return pl.CostEstimate(flops=flops, bytes_accessed=moved, transcendentals=0)


def pick(array, at, width, transposed):
    rows, many = array.shape[0], at.shape[0]

    def kernel(at_ref, in_ref, out_ref):
        out_ref[...] = in_ref[...].T if transposed else in_ref[...]

    if transposed:
        out_spec = pl.BlockSpec((width, rows), lambda j, at_ref: (j, 0))
        out_shape = jax.ShapeDtypeStruct((many * width, rows), array.dtype)
    else:
        out_spec = pl.BlockSpec((rows, width), lambda j, at_ref: (0, j))
        out_shape = jax.ShapeDtypeStruct((rows, many * width), array.dtype)
    return pl.pallas_call(
        kernel,
        grid_spec=pltpu.PrefetchScalarGridSpec(
            num_scalar_prefetch=1,
            grid=(many,),
            in_specs=[pl.BlockSpec((rows, width), lambda j, at_ref: (0, at_ref[j]))],
            out_specs=out_spec,
        ),
        out_shape=out_shape,
        compiler_params=params(),
        cost_estimate=cost(0, 4 * rows * many * width),
        name="pick",
    )(at, array)


def call(kernel, scalars, arrays, outs, scratch, *, flops, moved, name, aliases=None):
    anywhere = pl.BlockSpec(memory_space=pl.ANY)
    return pl.pallas_call(
        kernel,
        grid_spec=pltpu.PrefetchScalarGridSpec(
            num_scalar_prefetch=1,
            grid=(),
            in_specs=[anywhere] * len(arrays),
            out_specs=[anywhere] * len(outs),
            scratch_shapes=scratch,
        ),
        out_shape=outs,
        input_output_aliases=aliases or {},
        compiler_params=params(),
        cost_estimate=cost(flops, moved),
        name=name,
    )(scalars, *arrays)


def project(activations, sibling, first, at, blocks, before):
    chunks, many = len(blocks), len(blocks[0])
    (depth, cols), rows = blocks[0][0].shape, activations.shape[0]
    copies = many * (2 + chunks)
    flat = [block for chunk in blocks for block in chunk]
    held = [] if before is None else [before]

    def kernel(at_ref, own_ref, sib_ref, *refs):
        block_refs, out_ref = refs[: chunks * many], refs[chunks * many + len(held)]
        a, b, total, sems = refs[chunks * many + len(held) + 1 :]
        started = []
        for j in range(many):
            start = pl.multiple_of(at_ref[j] * depth, depth)
            moves = [
                (own_ref.at[:, pl.ds(start, depth)], a.at[pl.ds(0, rows), pl.ds(j * depth, depth)]),
                (sib_ref.at[:, pl.ds((first + j) * depth, depth)], a.at[pl.ds(rows, rows), pl.ds(j * depth, depth)]),
            ]
            for i in range(chunks):
                moves.append((block_refs[i * many + j], b.at[pl.ds(j * depth, depth), pl.ds(i * cols, cols)]))
            for source, target in moves:
                started.append(pltpu.make_async_copy(source, target, sems.at[len(started)]))
                started[-1].start()
        if held:
            started.append(pltpu.make_async_copy(refs[chunks * many], total, sems.at[len(started)]))
            started[-1].start()
        for copy in started:
            copy.wait()
        for i in range(chunks):
            part = slice(i * cols, (i + 1) * cols)
            term = jnp.dot(a[...], b[:, part], preferred_element_type=F32)
            total[:, part] = total[:, part] + term if held else term
        back_copy = pltpu.make_async_copy(total, out_ref, sems.at[len(started)])
        back_copy.start()
        back_copy.wait()

    wide = chunks * cols
    return call(
        kernel,
        at,
        [activations, sibling, *flat, *held],
        [jax.ShapeDtypeStruct((2 * rows, wide), F32)],
        [
            pltpu.VMEM((2 * rows, many * depth), BF16),
            pltpu.VMEM((many * depth, wide), BF16),
            pltpu.VMEM((2 * rows, wide), F32),
            pltpu.SemaphoreType.DMA((copies + 2,)),
        ],
        flops=4 * rows * depth * many * wide,
        moved=4 * rows * depth * many + 2 * depth * many * wide + 8 * rows * wide,
        name="project",
    )[0]


def outer_first(own, sibling, mine, theirs, width):
    rows, cols = own.shape[1], mine.shape[1]

    def kernel(own_ref, sib_ref, mine_ref, theirs_ref, held_ref, out_ref):
        held_ref[:rows, :] = (mine_ref[:rows, :] + theirs_ref[rows:, :]).astype(BF16)
        held_ref[rows:, :] = (mine_ref[rows:, :] + theirs_ref[:rows, :]).astype(BF16)
        term = jnp.dot(own_ref[...], held_ref[:rows, :], preferred_element_type=F32)
        term += jnp.dot(sib_ref[...], held_ref[rows:, :], preferred_element_type=F32)
        out_ref[...] = term.astype(BF16)

    whole = lambda *shape: pl.BlockSpec(shape, lambda j: (0, 0))
    return pl.pallas_call(
        kernel,
        grid=(1,),
        in_specs=[whole(width, rows), whole(width, rows), whole(2 * rows, cols), whole(2 * rows, cols)],
        out_specs=[whole(2 * rows, cols), whole(width, cols)],
        out_shape=[jax.ShapeDtypeStruct((2 * rows, cols), BF16), jax.ShapeDtypeStruct((width, cols), BF16)],
        compiler_params=params(),
        cost_estimate=cost(4 * rows * width * cols, 4 * rows * width + 20 * rows * cols),
        name="outer_first",
    )(own, sibling, mine, theirs)


def outer(own, sibling, held, width, start, many, dtype):
    rows, cols = own.shape[1], held.shape[1]

    def kernel(own_ref, sib_ref, held_ref, *out_refs):
        for j, out_ref in enumerate(out_refs):

            @pl.when(pl.program_id(0) == j)
            def _(out_ref=out_ref):
                term = jnp.dot(own_ref[...], held_ref[:rows, :], preferred_element_type=F32)
                term += jnp.dot(sib_ref[...], held_ref[rows:, :], preferred_element_type=F32)
                out_ref[...] = term.astype(dtype)

    return pl.pallas_call(
        kernel,
        grid=(many,),
        in_specs=[
            pl.BlockSpec((width, rows), lambda j: (start + j, 0)),
            pl.BlockSpec((width, rows), lambda j: (start + j, 0)),
            pl.BlockSpec((2 * rows, cols), lambda j: (0, 0)),
        ],
        out_specs=[pl.BlockSpec((width, cols), lambda j: (0, 0))] * many,
        out_shape=[jax.ShapeDtypeStruct((width, cols), dtype)] * many,
        compiler_params=params(),
        cost_estimate=cost(4 * rows * width * many * cols, many * (4 * rows * width + 4 * width * cols)),
        name="outer",
    )(own, sibling, held)


def back(blocks, projector_t, at, rows_in_all, before):
    many, chunks = len(blocks), len(blocks[0])
    (rows, cols), (rank, width) = blocks[0][0].shape, projector_t.shape
    flat = [part for block in blocks for part in block]
    held = [] if before is None else [before]
    slots = min(4, many)

    def kernel(at_ref, projector_ref, *refs):
        block_refs, out_ref = refs[: many * chunks], refs[many * chunks + len(held)]
        p, d, o, in_sems, out_sems = refs[many * chunks + len(held) + 1 :]
        p_copy = pltpu.make_async_copy(projector_ref, p, in_sems.at[many * chunks])
        p_copy.start()
        loads, stores = [], []
        for j in range(many):
            for i in range(chunks):
                n = j * chunks + i
                loads.append(pltpu.make_async_copy(block_refs[n], d.at[j, :, pl.ds(i * cols, cols)], in_sems.at[n]))
                loads[-1].start()
        p_copy.wait()
        for j in range(many):
            for i in range(chunks):
                loads[j * chunks + i].wait()
            if j >= slots:
                stores[j - slots].wait()
            o[j % slots] = jnp.dot(d[j], p[...], preferred_element_type=F32).astype(BF16)
            target = out_ref.at[pl.ds(pl.multiple_of(at_ref[j] * rows, rows), rows), :]
            stores.append(pltpu.make_async_copy(o.at[j % slots], target, out_sems.at[j % slots]))
            stores[-1].start()
        for j in range(many - slots, many):
            stores[j].wait()

    return call(
        kernel,
        at,
        [projector_t, *flat, *held],
        [jax.ShapeDtypeStruct((rows_in_all, width), BF16)],
        [
            pltpu.VMEM((rank, width), BF16),
            pltpu.VMEM((many, rows, rank), BF16),
            pltpu.VMEM((slots, rows, width), BF16),
            pltpu.SemaphoreType.DMA((many * chunks + 1,)),
            pltpu.SemaphoreType.DMA((slots,)),
        ],
        flops=2 * many * rows * width * rank,
        moved=2 * many * rows * (width + rank),
        name="back",
        aliases={2 + len(flat): 0} if held else None,
    )[0]


def levels(activations, out_grads, projector, first_moment, second_moment, *, nz):
    me = lax.axis_index("dp")
    z, y, core = me // 4, me // 2 % 2, me % 2
    grid = [(a, b, c) for a in range(nz) for b in range(2) for c in range(2)]

    def pairs(to):
        return [((a * 2 + b) * 2 + c, (to(a, b, c)[0] * 2 + to(a, b, c)[1]) * 2 + to(a, b, c)[2]) for a, b, c in grid]

    def swap_core(x):
        return lax.ppermute(x, "dp", pairs(lambda a, b, c: (a, b, 1 - c)))

    def swap_y(x):
        return lax.ppermute(x, "dp", pairs(lambda a, b, c: (a, 1 - b, c)))

    def shift_z(x, k):
        return lax.ppermute(x, "dp", pairs(lambda a, b, c: ((a + k) % nz, b, c)))

    def index(k, dy, dc):
        return (lax.rem(z + nz + k, nz) * 2 + (1 - y if dy else y)) * 2 + (1 - core if dc else core)

    def named(order):
        return jnp.stack([index(*o) for o in order]).astype(jnp.int32)

    def gather(chunks):
        line = [[own] for own in chunks]
        across = [[] for _ in chunks]
        for step in range(nz):
            for i in range(len(chunks)):
                if step:
                    line[i][step], across[i][step - 1] = lax.optimization_barrier((line[i][step], across[i][step - 1]))
                if step < nz - 1:
                    line[i].append(shift_z(line[i][step], 1))
                if step < nz - 1 or i < len(chunks) - 1:
                    across[i].append(swap_y(line[i][step]))
                else:
                    across[i].append(shift_z(across[i][0], nz - 1))
        return [{(-k, dy): (line, across)[dy][i][k] for k in range(nz) for dy in (0, 1)} for i in range(len(chunks))]

    ks = sorted(range(1, nz), key=lambda k: -min(k, nz - k))
    depth, rank = projector.shape
    width = first_moment.shape[0]
    cols = rank // CHUNKS
    parts = [slice(i * cols, (i + 1) * cols) for i in range(CHUNKS)]

    late = [(2 - nz, 1), (1 - nz, 0), (1 - nz, 1)]
    early = [(-k, dy) for k in range(nz) for dy in (0, 1) if (-k, dy) not in late]
    order_out = [(k, dy) for dy in (1, 0) for k in ks + [0]]

    gathered = gather([projector[:, part] for part in parts])
    a_sibling = swap_core(pick(activations, named([(k, dy, 1) for k, dy in early + late]), depth, False))
    g_sibling = swap_core(pick(out_grads, named([(k, dy, 1) for k, dy in order_out]), width, True))
    g_own = pick(out_grads, named([(k, dy, 0) for k, dy in order_out]), width, True)
    projector_t = projector.T

    mine, first = None, 0
    for order in (early, late):
        at = named([(k, dy, 0) for k, dy in order])
        mine = project(activations, a_sibling, first, at, [[chunk[o] for o in order] for chunk in gathered], mine)
        first += len(order)

    held, send = outer_first(g_own, g_sibling, mine, swap_core(mine), width)
    sends = [send] + list(outer(g_own, g_sibling, held, width, 1, nz - 1, BF16))
    keeps = list(outer(g_own, g_sibling, held, width, nz, nz, F32))
    reduced = None
    for at, k in enumerate(ks + [0]):
        term = keeps[at] + swap_y(sends[at]).astype(F32)
        if k:
            term = shift_z(term.astype(BF16), k).astype(F32)
        reduced = term if reduced is None else reduced + term
    new_first, new_second, direction = adam(reduced, first_moment, second_moment)

    gathered = gather([direction[:, part] for part in parts])
    update = None
    for order in (early, late):
        blocks = [[chunk[o] for chunk in gathered] for o in order]
        blocks = blocks + [[swap_core(x) for x in block] for block in blocks]
        at = named([(k, dy, dc) for dc in (0, 1) for k, dy in order])
        update = back(blocks, projector_t, at, 4 * nz * width, update)
    return update, new_first, new_second


def solution(mesh):
    devices = mesh.shape["dp"]

    def body(activations, out_grads, projector, first_moment, second_moment):
        aligned = projector.shape[0] % 128 == 0 and first_moment.shape[0] % 128 == 0
        if devices % 4 or devices < 8 or not aligned:
            return plain(activations, out_grads, projector, first_moment, second_moment)
        return levels(activations, out_grads, projector, first_moment, second_moment, nz=devices // 4)

    placed = P(("groups", "dp"), None)
    return jax.shard_map(
        body,
        mesh=mesh,
        in_specs=(placed,) * 5,
        out_specs=(P("groups", "dp"), placed, placed),
        check_vma=False,
    )
```

time: 275 us -> 168 us (0.61)
  waiting for transfers between devices: 229 us -> 47.2 us
  starting transfers between devices: 0.12 us -> 52.8 us
  Pallas kernels: 0 us -> 29.1 us
  local copies, waits for them, and re-layouts: 8.16 us -> 35.4 us
  matrix products: 20.9 us -> 0 us
  between operations: 13.8 us -> 1.18 us
    all_gather x2 -> x0, waiting for transfers between devices: 129 us -> none  [the longest x1 79.8 us: body(): lax.all_gather(projector, 'dp', axis=0, tiled=True)]
    reduce_scatter x1 -> x0, waiting for transfers between devices: 99.1 us -> none  [body(): lax.psum_scatter(lax.dot_general(out_grads, projected, (((0,), (0,)), (()...]
    ppermute x0 -> x54, starting transfers between devices: none -> 52.8 us  [the longest x17 30.4 us: shift_z(): return lax.ppermute(x, 'dp', pairs(lambda a, b, c: ((a + k) % nz, b, c)))]
    ppermute x0 -> x54, waiting for transfers between devices: none -> 47.2 us  [the longest x17 36.1 us: shift_z(): return lax.ppermute(x, 'dp', pairs(lambda a, b, c: ((a + k) % nz, b, c)))]
    pallas_call x0 -> x10, Pallas kernels: none -> 29.1 us  [the longest x4 16.7 us: call(): pl.pallas_call(kernel, grid_spec=pltpu.PrefetchScalarGridSpec(num_scalar_...]
    unnamed x6 -> x81, local copies, waits for them, and re-layouts: 8.16 us -> 34.8 us
    dot_general x2 -> x0, matrix products: 20.9 us -> none  [the longest x1 14.2 us: body(): lax.dot_general(out_grads, projected, (((0,), (0,)), ((), ())), preferred...]
  transfers between devices with their start and end apart: 3 -> 54, of which waited for: 3 -> 18; matrix products, arithmetic and copies ran while one was open for 3% -> 1% of each run, Pallas kernels for 0% -> 12%
where the time goes in v2:
time: 168 us; the launch traced here: 167 us
  starting transfers between devices  52.8 us (31%)
  waiting for transfers between devices  47.2 us (28%)
  local copies, waits for them, and re-layouts  35.4 us (21%)
  Pallas kernels  29.1 us (17%)
  other arithmetic  1.71 us (1%)
    ppermute x17, waiting for transfers between devices, shift_z(): return lax.ppermute(x, 'dp', pairs(lambda a, b, c: ((a + k) % nz, b, c)))  36.1 us
    unnamed x81, local copies, waits for them, and re-layouts  34.8 us
    ppermute x17, starting transfers between devices, shift_z(): return lax.ppermute(x, 'dp', pairs(lambda a, b, c: ((a + k) % nz, b, c)))  30.4 us
    ppermute x18, starting transfers between devices, swap_y(): return lax.ppermute(x, 'dp', pairs(lambda a, b, c: (a, 1 - b, c)))  19.3 us
    pallas_call x4, Pallas kernels, call(): pl.pallas_call(kernel, grid_spec=pltpu.PrefetchScalarGridSpec(num_scalar_...  16.7 us
    ppermute x18, waiting for transfers between devices, swap_y(): return lax.ppermute(x, 'dp', pairs(lambda a, b, c: (a, 1 - b, c)))  11.1 us
    pallas_call x3, Pallas kernels, pick(): pl.pallas_call(kernel, grid_spec=pltpu.PrefetchScalarGridSpec(num_scalar_...  7.38 us
  transfers between devices with their start and end apart: 54, of which 18 were waited for; matrix products, arithmetic and copies ran while one was open for 1% of the time, Pallas kernels for 12%

profile of v2, /device:TPU:0, one launch (start us, length us, event | category | flops | bytes accessed | tf_op | source)
XLA Modules:
  0.0 167.4 jit_solution(13269562656096735751)
XLA Ops:
  0.8 2.8 %copy-done = bf16[384,8192]{1,0:T(8,128)(2,1)S(1)} copy-done((bf16[384,8192]{1,0:T(8,128)(2,1)S(1)}, bf16[384,8192]{1,0:T(8,128)(2,1)}, u32[]{:S(2)}) %copy-start) | copy-done | bytes 6291480
  3.6 3.9 %pick.5 = bf16[384,4096]{1,0:T(8,128)(2,1)} custom-call(s32[8]{0:T(128)S(1)} %stack.154.at_ref, bf16[384,8192]{1,0:T(8,128)(2,1)S(1)} %copy-done), custom_call_target="tpu_custom_call" | custom-call | bytes 6291456 | tf_op jit(solution)/shard_map/pick/pallas_call | solution.py:71
  8.0 2.6 %collective-permute-start.2 = (bf16[512,256]{1,0:T(8,128)(2,1)S(1)}, bf16[512,256]{1,0:T(8,128)(2,1)S(1)}, u32[]{:S(2)}, u32[]{:S(2)}) collective-permute-start(bf16[512,256]{1,0:T(8,128)(2,1)S(1)} %get-tuple-element.73.refs_0_), channel_id=1, source_target_pairs={{0,4},{1,5},{2,6},{3,7},{4,8},{5,9},{6,10},{7,11},{8,12},{9,13},{1... | collective-permute-start | bytes 786440 | tf_op jit(solution)/shard_map/ppermute | solution.py:274
  10.7 1.5 collective-permute-start.3
  13.4 1.6 collective-permute-start.9
  15.0 4.9 %collective-permute-done.2.refs_2_ = bf16[512,256]{1,0:T(8,128)(2,1)S(1)} collective-permute-done((bf16[512,256]{1,0:T(8,128)(2,1)S(1)}, bf16[512,256]{1,0:T(8,128)(2,1)S(1)}, u32[]{:S(2)}, u32[]{:S(2)}) %collective-permute-start.2) | collective-permute-done | bytes 262176 | tf_op jit(solution)/shard_map/ppermute | solution.py:274
  20.6 1.5 collective-permute-start.4
  22.1 1.5 collective-permute-start.5
  25.5 1.5 collective-permute-start.11
  27.0 1.5 collective-permute-start.12
  29.2 2.5 %collective-permute-done.4.refs_4_ = bf16[512,256]{1,0:T(8,128)(2,1)} collective-permute-done((bf16[512,256]{1,0:T(8,128)(2,1)S(1)}, bf16[512,256]{1,0:T(8,128)(2,1)}, u32[]{:S(2)}, u32[]{:S(2)}) %collective-permute-start.4) | collective-permute-done | bytes 262176 | tf_op jit(solution)/shard_map/ppermute | solution.py:274
  33.6 1.5 collective-permute-start.7
  35.2 2.2 %collective-permute-done.11.refs_9_ = bf16[512,256]{1,0:T(8,128)(2,1)} collective-permute-done((bf16[512,256]{1,0:T(8,128)(2,1)S(1)}, bf16[512,256]{1,0:T(8,128)(2,1)}, u32[]{:S(2)}, u32[]{:S(2)}) %collective-permute-start.11) | collective-permute-done | bytes 262176 | tf_op jit(solution)/shard_map/ppermute | solution.py:274
  39.3 1.5 collective-permute-start.14
  40.9 1.7 %pick.4 = bf16[2048,384]{1,0:T(8,128)(2,1)S(1)} custom-call(s32[8]{0:T(128)S(1)} %stack.149.at_ref, bf16[384,4096]{1,0:T(8,128)(2,1)S(1)} %copy-done.2), custom_call_target="tpu_custom_call" | custom-call | bytes 3145728 | tf_op jit(solution)/shard_map/pick/pallas_call | solution.py:71
  43.8 2.8 %collective-permute-start.15 = (bf16[512,256]{1,0:T(8,128)(2,1)}, bf16[512,256]{1,0:T(8,128)(2,1)S(1)}, u32[]{:S(2)}, u32[]{:S(2)}) collective-permute-start(bf16[512,256]{1,0:T(8,128)(2,1)} %copy-done.9), channel_id=1, source_target_pairs={{0,12},{1,13},{2,14},{3,15},{4,0},{5,1},{6,2},{7,3},{8,4},{9,5},{1... | collective-permute-start | bytes 786440 | tf_op jit(solution)/shard_map/ppermute | solution.py:274
  47.1 2.4 %collective-permute-done.13.refs_4_ = bf16[512,256]{1,0:T(8,128)(2,1)} collective-permute-done((bf16[512,256]{1,0:T(8,128)(2,1)}, bf16[512,256]{1,0:T(8,128)(2,1)}, u32[]{:S(2)}, u32[]{:S(2)}) %collective-permute-start.13) | collective-permute-done | bytes 262176 | tf_op jit(solution)/shard_map/ppermute | solution.py:274
  49.4 2.8 %copy-done.1 = bf16[384,8192]{1,0:T(8,128)(2,1)S(1)} copy-done((bf16[384,8192]{1,0:T(8,128)(2,1)S(1)}, bf16[384,8192]{1,0:T(8,128)(2,1)}, u32[]{:S(2)}) %copy-start.1) | copy-done | bytes 6291480
  58.9 4.8 %project.2.refs_6_ = f32[768,512]{1,0:T(8,128)S(1)} custom-call(s32[5]{0:T(128)S(1)} %stack.158.at_ref, bf16[384,8192]{1,0:T(8,128)(2,1)S(1)} %copy-done.1, bf16[384,4096]{1,0:T(8,128)(2,1)} %collective-permute-done.1.sib_ref, bf16[512,256]{1,0:T(8,128)(2,1)S(1)} %copy-done.6, bf16[512,256]{1,0:T(8,128)(2,1)S(1)} %copy-done.12, ...), custom_call_target="tpu_custom_call" | custom-call | flops 2013265920 | bytes 8126464 | tf_op jit(solution)/shard_map/project/pallas_call | solution.py:88
  63.7 3.8 %project.3.mine_ref = f32[768,512]{1,0:T(8,128)S(1)} custom-call(s32[3]{0:T(128)S(1)} %pad_add_fusion.at_ref, bf16[384,8192]{1,0:T(8,128)(2,1)S(1)} %copy-done.1, bf16[384,4096]{1,0:T(8,128)(2,1)} %collective-permute-done.1.sib_ref, bf16[512,256]{1,0:T(8,128)(2,1)} %collective-permute-done.7.refs_0_, bf16[512,256]{1,0:T(8,128)(2,1)} %collective-permute-done.6.refs_1_, ...), custom_call_target="tpu_custom_call" | custom-call | flops 1207959552 | bytes 5505024 | tf_op jit(solution)/shard_map/project/pallas_call | solution.py:88
  68.1 1.9 %copy-done.3 = bf16[384,4096]{1,0:T(8,128)(2,1)S(1)} copy-done((bf16[384,4096]{1,0:T(8,128)(2,1)S(1)}, bf16[384,4096]{1,0:T(8,128)(2,1)}, u32[]{:S(2)}) %copy-start.3) | copy-done | bytes 3145752
  70.0 1.7 %pick.3.own_ref = bf16[2048,384]{1,0:T(8,128)(2,1)S(1)} custom-call(s32[8]{0:T(128)S(1)} %stack.140.at_ref, bf16[384,4096]{1,0:T(8,128)(2,1)S(1)} %copy-done.3), custom_call_target="tpu_custom_call" | custom-call | bytes 3145728 | tf_op jit(solution)/shard_map/pick/pallas_call | solution.py:71
  71.8 1.9 %outer_first.1 = (bf16[768,512]{1,0:T(8,128)(2,1)S(1)}, bf16[256,512]{1,0:T(8,128)(2,1)S(1)}) custom-call(bf16[2048,384]{1,0:T(8,128)(2,1)S(1)} %pick.3.own_ref, bf16[2048,384]{1,0:T(8,128)(2,1)S(1)} %collective-permute-done.sib_ref, f32[768,512]{1,0:T(8,128)S(1)} %project.3.mine_ref, f32[768,512]{1,0:T(8,128)} %collective-permute-done.16.theirs_ref), custom_call_target="tpu_custom_call" | custom-call | flops 201326592 | bytes 4325376 | tf_op jit(solution)/shard_map/outer_first/pallas_call | solution.py:169
  73.6 1.7 %collective-permute-start.17 = (bf16[256,512]{1,0:T(8,128)(2,1)S(1)}, bf16[256,512]{1,0:T(8,128)(2,1)S(1)}, u32[]{:S(2)}, u32[]{:S(2)}) collective-permute-start(bf16[256,512]{1,0:T(8,128)(2,1)S(1)} %get-tuple-element.50), channel_id=1, source_target_pairs={{0,2},{1,3},{2,0},{3,1},{4,6},{5,7},{6,4},{7,5},{8,10},{9,11},{10,... | collective-permute-start | bytes 786440 | tf_op jit(solution)/shard_map/ppermute | solution.py:271
  75.3 1.3 outer.3
  77.1 1.6 collective-permute-start.21
  79.2 1.8 %outer.2 = (f32[256,512]{1,0:T(8,128)S(1)}, f32[256,512]{1,0:T(8,128)S(1)}, f32[256,512]{1,0:T(8,128)S(1)}, f32[256,512]{1,0:T(8,128)S(1)}) custom-call(bf16[2048,384]{1,0:T(8,128)(2,1)S(1)} %pick.3.own_ref, bf16[2048,384]{1,0:T(8,128)(2,1)S(1)} %collective-permute-done.sib_ref, bf16[768,512]{1,0:T(8,128)(2,1)S(1)} %get-tuple-element.48.held_ref), custom_call_target="tpu_custom_call" | custom-call | flops 805306368 | bytes 3670016 | tf_op jit(solution)/shard_map/outer/pallas_call | solution.py:193
  81.0 1.9 %collective-permute-done.17 = bf16[256,512]{1,0:T(8,128)(2,1)S(1)} collective-permute-done((bf16[256,512]{1,0:T(8,128)(2,1)S(1)}, bf16[256,512]{1,0:T(8,128)(2,1)S(1)}, u32[]{:S(2)}, u32[]{:S(2)}) %collective-permute-start.17) | collective-permute-done | bytes 262176 | tf_op jit(solution)/shard_map/ppermute | solution.py:271
  82.9 4.3 %collective-permute-start.18 = (bf16[256,512]{1,0:T(8,128)(2,1)S(1)}, bf16[256,512]{1,0:T(8,128)(2,1)S(1)}, u32[]{:S(2)}, u32[]{:S(2)}) collective-permute-start(bf16[256,512]{1,0:T(8,128)(2,1)S(1)} %add_convert_fusion.2), channel_id=1, source_target_pairs={{0,8},{1,9},{2,10},{3,11},{4,12},{5,13},{6,14},{7,15},{8,0},{9,1},... | collective-permute-start | bytes 786440 | tf_op jit(solution)/shard_map/ppermute | solution.py:274
  89.5 4.6 %collective-permute-done.21 = bf16[256,512]{1,0:T(8,128)(2,1)S(1)} collective-permute-done((bf16[256,512]{1,0:T(8,128)(2,1)S(1)}, bf16[256,512]{1,0:T(8,128)(2,1)S(1)}, u32[]{:S(2)}, u32[]{:S(2)}) %collective-permute-start.21) | collective-permute-done | bytes 262176 | tf_op jit(solution)/shard_map/ppermute | solution.py:271
  94.2 5.9 %collective-permute-start.22 = (bf16[256,512]{1,0:T(8,128)(2,1)S(1)}, bf16[256,512]{1,0:T(8,128)(2,1)S(1)}, u32[]{:S(2)}, u32[]{:S(2)}) collective-permute-start(bf16[256,512]{1,0:T(8,128)(2,1)S(1)} %add_convert_fusion), channel_id=1, source_target_pairs={{0,12},{1,13},{2,14},{3,15},{4,0},{5,1},{6,2},{7,3},{8,4},{9,5},{1... | collective-permute-start | bytes 786440 | tf_op jit(solution)/shard_map/ppermute | solution.py:274
  100.0 5.0 %collective-permute-done.18 = bf16[256,512]{1,0:T(8,128)(2,1)S(1)} collective-permute-done((bf16[256,512]{1,0:T(8,128)(2,1)S(1)}, bf16[256,512]{1,0:T(8,128)(2,1)S(1)}, u32[]{:S(2)}, u32[]{:S(2)}) %collective-permute-start.18) | collective-permute-done | bytes 262176 | tf_op jit(solution)/shard_map/ppermute | solution.py:274
  105.0 4.5 %collective-permute-done.22 = bf16[256,512]{1,0:T(8,128)(2,1)S(1)} collective-permute-done((bf16[256,512]{1,0:T(8,128)(2,1)S(1)}, bf16[256,512]{1,0:T(8,128)(2,1)S(1)}, u32[]{:S(2)}, u32[]{:S(2)}) %collective-permute-start.22) | collective-permute-done | bytes 262176 | tf_op jit(solution)/shard_map/ppermute | solution.py:274
  109.5 1.4 divide_convert_fusion
  111.8 1.4 collective-permute-start.31
  113.2 2.5 %collective-permute-start.24 = (bf16[256,256]{1,0:T(8,128)(2,1)S(1)}, bf16[256,256]{1,0:T(8,128)(2,1)S(1)}, u32[]{:S(2)}, u32[]{:S(2)}) collective-permute-start(bf16[256,256]{1,0:T(8,128)(2,1)S(1)} %get-tuple-element.75.refs_0_), channel_id=1, source_target_pairs={{0,4},{1,5},{2,6},{3,7},{4,8},{5,9},{6,10},{7,11},{8,12},{9,13},{1... | collective-permute-start | bytes 393224 | tf_op jit(solution)/shard_map/ppermute | solution.py:274
  116.3 2.9 %collective-permute-done.30.refs_5_ = bf16[256,256]{1,0:T(8,128)(2,1)S(1)} collective-permute-done((bf16[256,256]{1,0:T(8,128)(2,1)S(1)}, bf16[256,256]{1,0:T(8,128)(2,1)S(1)}, u32[]{:S(2)}, u32[]{:S(2)}) %collective-permute-start.30) | collective-permute-done | bytes 131104 | tf_op jit(solution)/shard_map/ppermute | solution.py:274
  119.2 1.5 collective-permute-start.32
  121.0 1.4 collective-permute-start.33
  123.6 3.6 %collective-permute-done.32.refs_9_ = bf16[256,256]{1,0:T(8,128)(2,1)S(1)} collective-permute-done((bf16[256,256]{1,0:T(8,128)(2,1)S(1)}, bf16[256,256]{1,0:T(8,128)(2,1)S(1)}, u32[]{:S(2)}, u32[]{:S(2)}) %collective-permute-start.32) | collective-permute-done | bytes 131104 | tf_op jit(solution)/shard_map/ppermute | solution.py:274
  127.8 1.9 %collective-permute-done.26.refs_8_ = bf16[256,256]{1,0:T(8,128)(2,1)S(1)} collective-permute-done((bf16[256,256]{1,0:T(8,128)(2,1)S(1)}, bf16[256,256]{1,0:T(8,128)(2,1)S(1)}, u32[]{:S(2)}, u32[]{:S(2)}) %collective-permute-start.26) | collective-permute-done | bytes 131104 | tf_op jit(solution)/shard_map/ppermute | solution.py:274
  129.7 1.7 %collective-permute-start.37 = (bf16[256,256]{1,0:T(8,128)(2,1)S(1)}, bf16[256,256]{1,0:T(8,128)(2,1)S(1)}, u32[]{:S(2)}, u32[]{:S(2)}) collective-permute-start(bf16[256,256]{1,0:T(8,128)(2,1)S(1)} %collective-permute-done.31.refs_3_), channel_id=1, source_target_pairs={{0,12},{1,13},{2,14},{3,15},{4,0},{5,1},{6,2},{7,3},{8,4},{9,5},{1... | collective-permute-start | bytes 393224 | tf_op jit(solution)/shard_map/ppermute | solution.py:274
  133.1 1.4 collective-permute-start.29
  137.0 1.8 %collective-permute-done.28.refs_2_ = bf16[256,256]{1,0:T(8,128)(2,1)S(1)} collective-permute-done((bf16[256,256]{1,0:T(8,128)(2,1)S(1)}, bf16[256,256]{1,0:T(8,128)(2,1)S(1)}, u32[]{:S(2)}, u32[]{:S(2)}) %collective-permute-start.28) | collective-permute-done | bytes 131104 | tf_op jit(solution)/shard_map/ppermute | solution.py:274
  140.7 2.8 %collective-permute-done.34.refs_3_ = bf16[256,256]{1,0:T(8,128)(2,1)S(1)} collective-permute-done((bf16[256,256]{1,0:T(8,128)(2,1)S(1)}, bf16[256,256]{1,0:T(8,128)(2,1)S(1)}, u32[]{:S(2)}, u32[]{:S(2)}) %collective-permute-start.34) | collective-permute-done | bytes 131104 | tf_op jit(solution)/shard_map/ppermute | solution.py:274
  147.1 2.3 %collective-permute-done.36.refs_4_ = bf16[256,256]{1,0:T(8,128)(2,1)S(1)} collective-permute-done((bf16[256,256]{1,0:T(8,128)(2,1)S(1)}, bf16[256,256]{1,0:T(8,128)(2,1)S(1)}, u32[]{:S(2)}, u32[]{:S(2)}) %collective-permute-start.36) | collective-permute-done | bytes 131104 | tf_op jit(solution)/shard_map/ppermute | solution.py:271
  159.0 4.8 %back.2.refs_12_ = bf16[4096,512]{1,0:T(8,128)(2,1)} custom-call(s32[10]{0:T(128)S(1)} %stack.159.at_ref, bf16[512,512]{1,0:T(8,128)(2,1)S(1)} %bitcast.29, bf16[256,256]{1,0:T(8,128)(2,1)S(1)} %get-tuple-element.75.refs_0_, bf16[256,256]{1,0:T(8,128)(2,1)S(1)} %get-tuple-element.74.refs_1_, bf16[256,256]{1,0:T(8,128)(2,1)S(1)} %collective-permute-done.25.refs_2_, ...), custom_call_target="tpu_custom_call" | custom-call | flops 1342177280 | bytes 5242880 | tf_op jit(solution)/shard_map/back/pallas_call | solution.py:88
  163.8 3.4 %back.3 = bf16[4096,512]{1,0:T(8,128)(2,1)} custom-call(s32[6]{0:T(128)S(1)} %stack.131.at_ref, bf16[512,512]{1,0:T(8,128)(2,1)S(1)} %bitcast.30, bf16[256,256]{1,0:T(8,128)(2,1)S(1)} %collective-permute-done.29.refs_0_, bf16[256,256]{1,0:T(8,128)(2,1)S(1)} %collective-permute-done.35.refs_1_, ...), custom_call_target="tpu_custom_call", output_to_operand_aliasing={{}: (14, {})} | custom-call | flops 805306368 | bytes 3145728 | tf_op jit(solution)/shard_map/back/pallas_call | solution.py:88
  (164 shorter events, 43.9 us)
Async XLA Ops:
  7.6 41.9 %collective-permute-start.1 = (bf16[384,4096]{1,0:T(8,128)(2,1)}, bf16[384,4096]{1,0:T(8,128)(2,1)}, u32[]{:S(2)}, u32[]{:S(2)}) collective-permute-start(bf16[384,4096]{1,0:T(8,128)(2,1)} %pick.5), channel_id=1, source_target_pairs={{0,1},{1,0},{2,3},{3,2},{4,5},{5,4},{6,7},{7,6},{8,9},{9,8},{10,11... | collective-permute-start | bytes 9437192 | tf_op jit(solution)/shard_map/ppermute | solution.py:268
  8.0 11.8 %collective-permute-start.2 = (bf16[512,256]{1,0:T(8,128)(2,1)S(1)}, bf16[512,256]{1,0:T(8,128)(2,1)S(1)}, u32[]{:S(2)}, u32[]{:S(2)}) collective-permute-start(bf16[512,256]{1,0:T(8,128)(2,1)S(1)} %get-tuple-element.73.refs_0_), channel_id=1, source_target_pairs={{0,4},{1,5},{2,6},{3,7},{4,8},{5,9},{6,10},{7,11},{8,12},{9,13},{1... | collective-permute-start | bytes 786440 | tf_op jit(solution)/shard_map/ppermute | solution.py:274
  10.7 9.2 %collective-permute-start.3 = (bf16[512,256]{1,0:T(8,128)(2,1)S(1)}, bf16[512,256]{1,0:T(8,128)(2,1)S(1)}, u32[]{:S(2)}, u32[]{:S(2)}) collective-permute-start(bf16[512,256]{1,0:T(8,128)(2,1)S(1)} %get-tuple-element.73.refs_0_), channel_id=1, source_target_pairs={{0,2},{1,3},{2,0},{3,1},{4,6},{5,7},{6,4},{7,5},{8,10},{9,11},{10,... | collective-permute-start | bytes 786440 | tf_op jit(solution)/shard_map/ppermute | solution.py:271
  12.9 12.5 %collective-permute-start.10 = (bf16[512,256]{1,0:T(8,128)(2,1)S(1)}, bf16[512,256]{1,0:T(8,128)(2,1)S(1)}, u32[]{:S(2)}, u32[]{:S(2)}) collective-permute-start(bf16[512,256]{1,0:T(8,128)(2,1)S(1)} %get-tuple-element.72.refs_5_), channel_id=1, source_target_pairs={{0,2},{1,3},{2,0},{3,1},{4,6},{5,7},{6,4},{7,5},{8,10},{9,11},{10,... | collective-permute-start | bytes 786440 | tf_op jit(solution)/shard_map/ppermute | solution.py:271
  13.4 12.1 %collective-permute-start.9 = (bf16[512,256]{1,0:T(8,128)(2,1)S(1)}, bf16[512,256]{1,0:T(8,128)(2,1)S(1)}, u32[]{:S(2)}, u32[]{:S(2)}) collective-permute-start(bf16[512,256]{1,0:T(8,128)(2,1)S(1)} %get-tuple-element.72.refs_5_), channel_id=1, source_target_pairs={{0,4},{1,5},{2,6},{3,7},{4,8},{5,9},{6,10},{7,11},{8,12},{9,13},{1... | collective-permute-start | bytes 786440 | tf_op jit(solution)/shard_map/ppermute | solution.py:274
  20.6 11.1 %collective-permute-start.4 = (bf16[512,256]{1,0:T(8,128)(2,1)S(1)}, bf16[512,256]{1,0:T(8,128)(2,1)}, u32[]{:S(2)}, u32[]{:S(2)}) collective-permute-start(bf16[512,256]{1,0:T(8,128)(2,1)S(1)} %collective-permute-done.2.refs_2_), channel_id=1, source_target_pairs={{0,4},{1,5},{2,6},{3,7},{4,8},{5,9},{6,10},{7,11},{8,12},{9,13},{1... | collective-permute-start | bytes 786440 | tf_op jit(solution)/shard_map/ppermute | solution.py:274
  22.1 9.6 %collective-permute-start.5 = (bf16[512,256]{1,0:T(8,128)(2,1)S(1)}, bf16[512,256]{1,0:T(8,128)(2,1)S(1)}, u32[]{:S(2)}, u32[]{:S(2)}) collective-permute-start(bf16[512,256]{1,0:T(8,128)(2,1)S(1)} %collective-permute-done.2.refs_2_), channel_id=1, source_target_pairs={{0,2},{1,3},{2,0},{3,1},{4,6},{5,7},{6,4},{7,5},{8,10},{9,11},{10,... | collective-permute-start | bytes 786440 | tf_op jit(solution)/shard_map/ppermute | solution.py:271
  25.5 11.9 %collective-permute-start.11 = (bf16[512,256]{1,0:T(8,128)(2,1)S(1)}, bf16[512,256]{1,0:T(8,128)(2,1)}, u32[]{:S(2)}, u32[]{:S(2)}) collective-permute-start(bf16[512,256]{1,0:T(8,128)(2,1)S(1)} %collective-permute-done.9.refs_7_), channel_id=1, source_target_pairs={{0,4},{1,5},{2,6},{3,7},{4,8},{5,9},{6,10},{7,11},{8,12},{9,13},{1... | collective-permute-start | bytes 786440 | tf_op jit(solution)/shard_map/ppermute | solution.py:274
  27.0 10.3 %collective-permute-start.12 = (bf16[512,256]{1,0:T(8,128)(2,1)S(1)}, bf16[512,256]{1,0:T(8,128)(2,1)S(1)}, u32[]{:S(2)}, u32[]{:S(2)}) collective-permute-start(bf16[512,256]{1,0:T(8,128)(2,1)S(1)} %collective-permute-done.9.refs_7_), channel_id=1, source_target_pairs={{0,2},{1,3},{2,0},{3,1},{4,6},{5,7},{6,4},{7,5},{8,10},{9,11},{10,... | collective-permute-start | bytes 786440 | tf_op jit(solution)/shard_map/ppermute | solution.py:271
  32.5 11.4 %collective-permute-start.6 = (bf16[512,256]{1,0:T(8,128)(2,1)}, bf16[512,256]{1,0:T(8,128)(2,1)}, u32[]{:S(2)}, u32[]{:S(2)}) collective-permute-start(bf16[512,256]{1,0:T(8,128)(2,1)} %collective-permute-done.4.refs_4_), channel_id=1, source_target_pairs={{0,4},{1,5},{2,6},{3,7},{4,8},{5,9},{6,10},{7,11},{8,12},{9,13},{1... | collective-permute-start | bytes 786440 | tf_op jit(solution)/shard_map/ppermute | solution.py:274
  33.6 13.0 %collective-permute-start.7 = (bf16[512,256]{1,0:T(8,128)(2,1)}, bf16[512,256]{1,0:T(8,128)(2,1)}, u32[]{:S(2)}, u32[]{:S(2)}) collective-permute-start(bf16[512,256]{1,0:T(8,128)(2,1)} %collective-permute-done.4.refs_4_), channel_id=1, source_target_pairs={{0,2},{1,3},{2,0},{3,1},{4,6},{5,7},{6,4},{7,5},{8,10},{9,11},{10,... | collective-permute-start | bytes 786440 | tf_op jit(solution)/shard_map/ppermute | solution.py:271
  38.1 11.4 %collective-permute-start.13 = (bf16[512,256]{1,0:T(8,128)(2,1)}, bf16[512,256]{1,0:T(8,128)(2,1)}, u32[]{:S(2)}, u32[]{:S(2)}) collective-permute-start(bf16[512,256]{1,0:T(8,128)(2,1)} %collective-permute-done.11.refs_9_), channel_id=1, source_target_pairs={{0,4},{1,5},{2,6},{3,7},{4,8},{5,9},{6,10},{7,11},{8,12},{9,13},{1... | collective-permute-start | bytes 786440 | tf_op jit(solution)/shard_map/ppermute | solution.py:274
  39.3 10.2 %collective-permute-start.14 = (bf16[512,256]{1,0:T(8,128)(2,1)}, bf16[512,256]{1,0:T(8,128)(2,1)}, u32[]{:S(2)}, u32[]{:S(2)}) collective-permute-start(bf16[512,256]{1,0:T(8,128)(2,1)} %collective-permute-done.11.refs_9_), channel_id=1, source_target_pairs={{0,2},{1,3},{2,0},{3,1},{4,6},{5,7},{6,4},{7,5},{8,10},{9,11},{10,... | collective-permute-start | bytes 786440 | tf_op jit(solution)/shard_map/ppermute | solution.py:271
  43.8 19.8 %collective-permute-start.15 = (bf16[512,256]{1,0:T(8,128)(2,1)}, bf16[512,256]{1,0:T(8,128)(2,1)S(1)}, u32[]{:S(2)}, u32[]{:S(2)}) collective-permute-start(bf16[512,256]{1,0:T(8,128)(2,1)} %copy-done.9), channel_id=1, source_target_pairs={{0,12},{1,13},{2,14},{3,15},{4,0},{5,1},{6,2},{7,3},{8,4},{9,5},{1... | collective-permute-start | bytes 786440 | tf_op jit(solution)/shard_map/ppermute | solution.py:274
  46.6 17.1 %collective-permute-start.8 = (bf16[512,256]{1,0:T(8,128)(2,1)}, bf16[512,256]{1,0:T(8,128)(2,1)S(1)}, u32[]{:S(2)}, u32[]{:S(2)}) collective-permute-start(bf16[512,256]{1,0:T(8,128)(2,1)} %collective-permute-done.6.refs_1_), channel_id=1, source_target_pairs={{0,2},{1,3},{2,0},{3,1},{4,6},{5,7},{6,4},{7,5},{8,10},{9,11},{10,... | collective-permute-start | bytes 786440 | tf_op jit(solution)/shard_map/ppermute | solution.py:271
  49.4 22.3 %collective-permute-start = (bf16[2048,384]{1,0:T(8,128)(2,1)}, bf16[2048,384]{1,0:T(8,128)(2,1)S(1)}, u32[]{:S(2)}, u32[]{:S(2)}) collective-permute-start(bf16[2048,384]{1,0:T(8,128)(2,1)} %copy-done.4), channel_id=1, source_target_pairs={{0,1},{1,0},{2,3},{3,2},{4,5},{5,4},{6,7},{7,6},{8,9},{9,8},{10,11... | collective-permute-start | bytes 4718600 | tf_op jit(solution)/shard_map/ppermute | solution.py:268
  73.6 9.2 %collective-permute-start.17 = (bf16[256,512]{1,0:T(8,128)(2,1)S(1)}, bf16[256,512]{1,0:T(8,128)(2,1)S(1)}, u32[]{:S(2)}, u32[]{:S(2)}) collective-permute-start(bf16[256,512]{1,0:T(8,128)(2,1)S(1)} %get-tuple-element.50), channel_id=1, source_target_pairs={{0,2},{1,3},{2,0},{3,1},{4,6},{5,7},{6,4},{7,5},{8,10},{9,11},{10,... | collective-permute-start | bytes 786440 | tf_op jit(solution)/shard_map/ppermute | solution.py:271
  76.7 11.8 %collective-permute-start.19 = (bf16[256,512]{1,0:T(8,128)(2,1)S(1)}, bf16[256,512]{1,0:T(8,128)(2,1)S(1)}, u32[]{:S(2)}, u32[]{:S(2)}) collective-permute-start(bf16[256,512]{1,0:T(8,128)(2,1)S(1)} %get-tuple-element.52), channel_id=1, source_target_pairs={{0,2},{1,3},{2,0},{3,1},{4,6},{5,7},{6,4},{7,5},{8,10},{9,11},{10,... | collective-permute-start | bytes 786440 | tf_op jit(solution)/shard_map/ppermute | solution.py:271
  77.1 17.0 %collective-permute-start.21 = (bf16[256,512]{1,0:T(8,128)(2,1)S(1)}, bf16[256,512]{1,0:T(8,128)(2,1)S(1)}, u32[]{:S(2)}, u32[]{:S(2)}) collective-permute-start(bf16[256,512]{1,0:T(8,128)(2,1)S(1)} %get-tuple-element.54), channel_id=1, source_target_pairs={{0,2},{1,3},{2,0},{3,1},{4,6},{5,7},{6,4},{7,5},{8,10},{9,11},{10,... | collective-permute-start | bytes 786440 | tf_op jit(solution)/shard_map/ppermute | solution.py:271
  78.8 21.3 %collective-permute-start.23 = (bf16[256,512]{1,0:T(8,128)(2,1)S(1)}, bf16[256,512]{1,0:T(8,128)(2,1)S(1)}, u32[]{:S(2)}, u32[]{:S(2)}) collective-permute-start(bf16[256,512]{1,0:T(8,128)(2,1)S(1)} %get-tuple-element.56), channel_id=1, source_target_pairs={{0,2},{1,3},{2,0},{3,1},{4,6},{5,7},{6,4},{7,5},{8,10},{9,11},{10,... | collective-permute-start | bytes 786440 | tf_op jit(solution)/shard_map/ppermute | solution.py:271
  82.9 22.1 %collective-permute-start.18 = (bf16[256,512]{1,0:T(8,128)(2,1)S(1)}, bf16[256,512]{1,0:T(8,128)(2,1)S(1)}, u32[]{:S(2)}, u32[]{:S(2)}) collective-permute-start(bf16[256,512]{1,0:T(8,128)(2,1)S(1)} %add_convert_fusion.2), channel_id=1, source_target_pairs={{0,8},{1,9},{2,10},{3,11},{4,12},{5,13},{6,14},{7,15},{8,0},{9,1},... | collective-permute-start | bytes 786440 | tf_op jit(solution)/shard_map/ppermute | solution.py:274
  88.5 16.4 %collective-permute-start.20 = (bf16[256,512]{1,0:T(8,128)(2,1)S(1)}, bf16[256,512]{1,0:T(8,128)(2,1)S(1)}, u32[]{:S(2)}, u32[]{:S(2)}) collective-permute-start(bf16[256,512]{1,0:T(8,128)(2,1)S(1)} %add_convert_fusion.1), channel_id=1, source_target_pairs={{0,4},{1,5},{2,6},{3,7},{4,8},{5,9},{6,10},{7,11},{8,12},{9,13},{1... | collective-permute-start | bytes 786440 | tf_op jit(solution)/shard_map/ppermute | solution.py:274
  94.2 15.3 %collective-permute-start.22 = (bf16[256,512]{1,0:T(8,128)(2,1)S(1)}, bf16[256,512]{1,0:T(8,128)(2,1)S(1)}, u32[]{:S(2)}, u32[]{:S(2)}) collective-permute-start(bf16[256,512]{1,0:T(8,128)(2,1)S(1)} %add_convert_fusion), channel_id=1, source_target_pairs={{0,12},{1,13},{2,14},{3,15},{4,0},{5,1},{6,2},{7,3},{8,4},{9,5},{1... | collective-permute-start | bytes 786440 | tf_op jit(solution)/shard_map/ppermute | solution.py:274
  111.0 8.2 %collective-permute-start.30 = (bf16[256,256]{1,0:T(8,128)(2,1)S(1)}, bf16[256,256]{1,0:T(8,128)(2,1)S(1)}, u32[]{:S(2)}, u32[]{:S(2)}) collective-permute-start(bf16[256,256]{1,0:T(8,128)(2,1)S(1)} %get-tuple-element.74.refs_1_), channel_id=1, source_target_pairs={{0,4},{1,5},{2,6},{3,7},{4,8},{5,9},{6,10},{7,11},{8,12},{9,13},{1... | collective-permute-start | bytes 393224 | tf_op jit(solution)/shard_map/ppermute | solution.py:274
  111.8 7.4 %collective-permute-start.31 = (bf16[256,256]{1,0:T(8,128)(2,1)S(1)}, bf16[256,256]{1,0:T(8,128)(2,1)S(1)}, u32[]{:S(2)}, u32[]{:S(2)}) collective-permute-start(bf16[256,256]{1,0:T(8,128)(2,1)S(1)} %get-tuple-element.74.refs_1_), channel_id=1, source_target_pairs={{0,2},{1,3},{2,0},{3,1},{4,6},{5,7},{6,4},{7,5},{8,10},{9,11},{10,... | collective-permute-start | bytes 393224 | tf_op jit(solution)/shard_map/ppermute | solution.py:271
  113.2 7.8 %collective-permute-start.24 = (bf16[256,256]{1,0:T(8,128)(2,1)S(1)}, bf16[256,256]{1,0:T(8,128)(2,1)S(1)}, u32[]{:S(2)}, u32[]{:S(2)}) collective-permute-start(bf16[256,256]{1,0:T(8,128)(2,1)S(1)} %get-tuple-element.75.refs_0_), channel_id=1, source_target_pairs={{0,4},{1,5},{2,6},{3,7},{4,8},{5,9},{6,10},{7,11},{8,12},{9,13},{1... | collective-permute-start | bytes 393224 | tf_op jit(solution)/shard_map/ppermute | solution.py:274
  115.7 6.8 %collective-permute-start.25 = (bf16[256,256]{1,0:T(8,128)(2,1)S(1)}, bf16[256,256]{1,0:T(8,128)(2,1)S(1)}, u32[]{:S(2)}, u32[]{:S(2)}) collective-permute-start(bf16[256,256]{1,0:T(8,128)(2,1)S(1)} %get-tuple-element.75.refs_0_), channel_id=1, source_target_pairs={{0,2},{1,3},{2,0},{3,1},{4,6},{5,7},{6,4},{7,5},{8,10},{9,11},{10,... | collective-permute-start | bytes 393224 | tf_op jit(solution)/shard_map/ppermute | solution.py:271
  116.3 6.2 %collective-permute-start.44 = (bf16[256,256]{1,0:T(8,128)(2,1)S(1)}, bf16[256,256]{1,0:T(8,128)(2,1)S(1)}, u32[]{:S(2)}, u32[]{:S(2)}) collective-permute-start(bf16[256,256]{1,0:T(8,128)(2,1)S(1)} %get-tuple-element.75.refs_0_), channel_id=1, source_target_pairs={{0,1},{1,0},{2,3},{3,2},{4,5},{5,4},{6,7},{7,6},{8,9},{9,8},{10,11... | collective-permute-start | bytes 393224 | tf_op jit(solution)/shard_map/ppermute | solution.py:268
  119.2 8.1 %collective-permute-start.32 = (bf16[256,256]{1,0:T(8,128)(2,1)S(1)}, bf16[256,256]{1,0:T(8,128)(2,1)S(1)}, u32[]{:S(2)}, u32[]{:S(2)}) collective-permute-start(bf16[256,256]{1,0:T(8,128)(2,1)S(1)} %collective-permute-done.30.refs_5_), channel_id=1, source_target_pairs={{0,4},{1,5},{2,6},{3,7},{4,8},{5,9},{6,10},{7,11},{8,12},{9,13},{1... | collective-permute-start | bytes 393224 | tf_op jit(solution)/shard_map/ppermute | solution.py:274
  121.0 6.2 %collective-permute-start.33 = (bf16[256,256]{1,0:T(8,128)(2,1)S(1)}, bf16[256,256]{1,0:T(8,128)(2,1)S(1)}, u32[]{:S(2)}, u32[]{:S(2)}) collective-permute-start(bf16[256,256]{1,0:T(8,128)(2,1)S(1)} %collective-permute-done.30.refs_5_), channel_id=1, source_target_pairs={{0,2},{1,3},{2,0},{3,1},{4,6},{5,7},{6,4},{7,5},{8,10},{9,11},{10,... | collective-permute-start | bytes 393224 | tf_op jit(solution)/shard_map/ppermute | solution.py:271
  122.5 7.2 %collective-permute-start.26 = (bf16[256,256]{1,0:T(8,128)(2,1)S(1)}, bf16[256,256]{1,0:T(8,128)(2,1)S(1)}, u32[]{:S(2)}, u32[]{:S(2)}) collective-permute-start(bf16[256,256]{1,0:T(8,128)(2,1)S(1)} %collective-permute-done.24.refs_4_), channel_id=1, source_target_pairs={{0,4},{1,5},{2,6},{3,7},{4,8},{5,9},{6,10},{7,11},{8,12},{9,13},{1... | collective-permute-start | bytes 393224 | tf_op jit(solution)/shard_map/ppermute | solution.py:274
  122.5 7.2 %collective-permute-start.27 = (bf16[256,256]{1,0:T(8,128)(2,1)S(1)}, bf16[256,256]{1,0:T(8,128)(2,1)S(1)}, u32[]{:S(2)}, u32[]{:S(2)}) collective-permute-start(bf16[256,256]{1,0:T(8,128)(2,1)S(1)} %collective-permute-done.24.refs_4_), channel_id=1, source_target_pairs={{0,2},{1,3},{2,0},{3,1},{4,6},{5,7},{6,4},{7,5},{8,10},{9,11},{10,... | collective-permute-start | bytes 393224 | tf_op jit(solution)/shard_map/ppermute | solution.py:271
  123.6 7.8 %collective-permute-start.47 = (bf16[256,256]{1,0:T(8,128)(2,1)S(1)}, bf16[256,256]{1,0:T(8,128)(2,1)S(1)}, u32[]{:S(2)}, u32[]{:S(2)}) collective-permute-start(bf16[256,256]{1,0:T(8,128)(2,1)S(1)} %collective-permute-done.31.refs_3_), channel_id=1, source_target_pairs={{0,1},{1,0},{2,3},{3,2},{4,5},{5,4},{6,7},{7,6},{8,9},{9,8},{10,11... | collective-permute-start | bytes 393224 | tf_op jit(solution)/shard_map/ppermute | solution.py:268
  127.3 7.2 %collective-permute-start.46 = (bf16[256,256]{1,0:T(8,128)(2,1)S(1)}, bf16[256,256]{1,0:T(8,128)(2,1)S(1)}, u32[]{:S(2)}, u32[]{:S(2)}) collective-permute-start(bf16[256,256]{1,0:T(8,128)(2,1)S(1)} %collective-permute-done.25.refs_2_), channel_id=1, source_target_pairs={{0,1},{1,0},{2,3},{3,2},{4,5},{5,4},{6,7},{7,6},{8,9},{9,8},{10,11... | collective-permute-start | bytes 393224 | tf_op jit(solution)/shard_map/ppermute | solution.py:268
  129.7 5.4 %collective-permute-start.48 = (bf16[256,256]{1,0:T(8,128)(2,1)S(1)}, bf16[256,256]{1,0:T(8,128)(2,1)S(1)}, u32[]{:S(2)}, u32[]{:S(2)}) collective-permute-start(bf16[256,256]{1,0:T(8,128)(2,1)S(1)} %collective-permute-done.24.refs_4_), channel_id=1, source_target_pairs={{0,1},{1,0},{2,3},{3,2},{4,5},{5,4},{6,7},{7,6},{8,9},{9,8},{10,11... | collective-permute-start | bytes 393224 | tf_op jit(solution)/shard_map/ppermute | solution.py:268
  129.7 7.3 %collective-permute-start.37 = (bf16[256,256]{1,0:T(8,128)(2,1)S(1)}, bf16[256,256]{1,0:T(8,128)(2,1)S(1)}, u32[]{:S(2)}, u32[]{:S(2)}) collective-permute-start(bf16[256,256]{1,0:T(8,128)(2,1)S(1)} %collective-permute-done.31.refs_3_), channel_id=1, source_target_pairs={{0,12},{1,13},{2,14},{3,15},{4,0},{5,1},{6,2},{7,3},{8,4},{9,5},{1... | collective-permute-start | bytes 393224 | tf_op jit(solution)/shard_map/ppermute | solution.py:274
  132.1 6.8 %collective-permute-start.28 = (bf16[256,256]{1,0:T(8,128)(2,1)S(1)}, bf16[256,256]{1,0:T(8,128)(2,1)S(1)}, u32[]{:S(2)}, u32[]{:S(2)}) collective-permute-start(bf16[256,256]{1,0:T(8,128)(2,1)S(1)} %collective-permute-done.26.refs_8_), channel_id=1, source_target_pairs={{0,4},{1,5},{2,6},{3,7},{4,8},{5,9},{6,10},{7,11},{8,12},{9,13},{1... | collective-permute-start | bytes 393224 | tf_op jit(solution)/shard_map/ppermute | solution.py:274
  133.1 5.8 %collective-permute-start.29 = (bf16[256,256]{1,0:T(8,128)(2,1)S(1)}, bf16[256,256]{1,0:T(8,128)(2,1)S(1)}, u32[]{:S(2)}, u32[]{:S(2)}) collective-permute-start(bf16[256,256]{1,0:T(8,128)(2,1)S(1)} %collective-permute-done.26.refs_8_), channel_id=1, source_target_pairs={{0,2},{1,3},{2,0},{3,1},{4,6},{5,7},{6,4},{7,5},{8,10},{9,11},{10,... | collective-permute-start | bytes 393224 | tf_op jit(solution)/shard_map/ppermute | solution.py:271
  135.8 7.7 %collective-permute-start.34 = (bf16[256,256]{1,0:T(8,128)(2,1)S(1)}, bf16[256,256]{1,0:T(8,128)(2,1)S(1)}, u32[]{:S(2)}, u32[]{:S(2)}) collective-permute-start(bf16[256,256]{1,0:T(8,128)(2,1)S(1)} %collective-permute-done.32.refs_9_), channel_id=1, source_target_pairs={{0,4},{1,5},{2,6},{3,7},{4,8},{5,9},{6,10},{7,11},{8,12},{9,13},{1... | collective-permute-start | bytes 393224 | tf_op jit(solution)/shard_map/ppermute | solution.py:274
  137.0 6.5 %collective-permute-start.35 = (bf16[256,256]{1,0:T(8,128)(2,1)S(1)}, bf16[256,256]{1,0:T(8,128)(2,1)S(1)}, u32[]{:S(2)}, u32[]{:S(2)}) collective-permute-start(bf16[256,256]{1,0:T(8,128)(2,1)S(1)} %collective-permute-done.32.refs_9_), channel_id=1, source_target_pairs={{0,2},{1,3},{2,0},{3,1},{4,6},{5,7},{6,4},{7,5},{8,10},{9,11},{10,... | collective-permute-start | bytes 393224 | tf_op jit(solution)/shard_map/ppermute | solution.py:271
  138.9 5.2 %collective-permute-start.53 = (bf16[256,256]{1,0:T(8,128)(2,1)S(1)}, bf16[256,256]{1,0:T(8,128)(2,1)S(1)}, u32[]{:S(2)}, u32[]{:S(2)}) collective-permute-start(bf16[256,256]{1,0:T(8,128)(2,1)S(1)} %collective-permute-done.32.refs_9_), channel_id=1, source_target_pairs={{0,1},{1,0},{2,3},{3,2},{4,5},{5,4},{6,7},{7,6},{8,9},{9,8},{10,11... | collective-permute-start | bytes 393224 | tf_op jit(solution)/shard_map/ppermute | solution.py:268
  138.9 6.1 %collective-permute-start.50 = (bf16[256,256]{1,0:T(8,128)(2,1)S(1)}, bf16[256,256]{1,0:T(8,128)(2,1)S(1)}, u32[]{:S(2)}, u32[]{:S(2)}) collective-permute-start(bf16[256,256]{1,0:T(8,128)(2,1)S(1)} %collective-permute-done.27.refs_6_), channel_id=1, source_target_pairs={{0,1},{1,0},{2,3},{3,2},{4,5},{5,4},{6,7},{7,6},{8,9},{9,8},{10,11... | collective-permute-start | bytes 393224 | tf_op jit(solution)/shard_map/ppermute | solution.py:268
  143.5 5.9 %collective-permute-start.36 = (bf16[256,256]{1,0:T(8,128)(2,1)S(1)}, bf16[256,256]{1,0:T(8,128)(2,1)S(1)}, u32[]{:S(2)}, u32[]{:S(2)}) collective-permute-start(bf16[256,256]{1,0:T(8,128)(2,1)S(1)} %collective-permute-done.28.refs_2_), channel_id=1, source_target_pairs={{0,2},{1,3},{2,0},{3,1},{4,6},{5,7},{6,4},{7,5},{8,10},{9,11},{10,... | collective-permute-start | bytes 393224 | tf_op jit(solution)/shard_map/ppermute | solution.py:271
  144.7 19.0 %collective-permute-start.40 = (bf16[256,256]{1,0:T(8,128)(2,1)S(1)}, bf16[256,256]{1,0:T(8,128)(2,1)S(1)}, u32[]{:S(2)}, u32[]{:S(2)}) collective-permute-start(bf16[256,256]{1,0:T(8,128)(2,1)S(1)} %collective-permute-done.28.refs_2_), channel_id=1, source_target_pairs={{0,1},{1,0},{2,3},{3,2},{4,5},{5,4},{6,7},{7,6},{8,9},{9,8},{10,11... | collective-permute-start | bytes 393224 | tf_op jit(solution)/shard_map/ppermute | solution.py:268
  145.6 18.1 %collective-permute-start.39 = (bf16[256,256]{1,0:T(8,128)(2,1)S(1)}, bf16[256,256]{1,0:T(8,128)(2,1)S(1)}, u32[]{:S(2)}, u32[]{:S(2)}) collective-permute-start(bf16[256,256]{1,0:T(8,128)(2,1)S(1)} %collective-permute-done.35.refs_1_), channel_id=1, source_target_pairs={{0,1},{1,0},{2,3},{3,2},{4,5},{5,4},{6,7},{7,6},{8,9},{9,8},{10,11... | collective-permute-start | bytes 393224 | tf_op jit(solution)/shard_map/ppermute | solution.py:268
  146.6 17.2 %collective-permute-start.41 = (bf16[256,256]{1,0:T(8,128)(2,1)S(1)}, bf16[256,256]{1,0:T(8,128)(2,1)S(1)}, u32[]{:S(2)}, u32[]{:S(2)}) collective-permute-start(bf16[256,256]{1,0:T(8,128)(2,1)S(1)} %collective-permute-done.34.refs_3_), channel_id=1, source_target_pairs={{0,1},{1,0},{2,3},{3,2},{4,5},{5,4},{6,7},{7,6},{8,9},{9,8},{10,11... | collective-permute-start | bytes 393224 | tf_op jit(solution)/shard_map/ppermute | solution.py:268
  146.8 17.0 %collective-permute-start.38 = (bf16[256,256]{1,0:T(8,128)(2,1)S(1)}, bf16[256,256]{1,0:T(8,128)(2,1)S(1)}, u32[]{:S(2)}, u32[]{:S(2)}) collective-permute-start(bf16[256,256]{1,0:T(8,128)(2,1)S(1)} %collective-permute-done.29.refs_0_), channel_id=1, source_target_pairs={{0,1},{1,0},{2,3},{3,2},{4,5},{5,4},{6,7},{7,6},{8,9},{9,8},{10,11... | collective-permute-start | bytes 393224 | tf_op jit(solution)/shard_map/ppermute | solution.py:268
  149.4 14.4 %collective-permute-start.42 = (bf16[256,256]{1,0:T(8,128)(2,1)S(1)}, bf16[256,256]{1,0:T(8,128)(2,1)S(1)}, u32[]{:S(2)}, u32[]{:S(2)}) collective-permute-start(bf16[256,256]{1,0:T(8,128)(2,1)S(1)} %collective-permute-done.36.refs_4_), channel_id=1, source_target_pairs={{0,1},{1,0},{2,3},{3,2},{4,5},{5,4},{6,7},{7,6},{8,9},{9,8},{10,11... | collective-permute-start | bytes 393224 | tf_op jit(solution)/shard_map/ppermute | solution.py:268
  (46 other events, 170.3 us)

commit v3 on v2

--- a/solution.py
+++ b/solution.py
@@ -14,7 +14,7 @@
 
 CHUNKS = 2
 F32, BF16 = jnp.float32, jnp.bfloat16
-VMEM_LIMIT = 40 * 1024 * 1024
+VMEM_LIMIT = 16 * 1024 * 1024
 
 
 def adam(reduced, first_moment, second_moment):
@@ -56,41 +56,68 @@
     return pl.CostEstimate(flops=flops, bytes_accessed=moved, transcendentals=0)
 
 
-def pick(array, at, width, transposed):
+def take(array, at, width):
     rows, many = array.shape[0], at.shape[0]
 
-    def kernel(at_ref, in_ref, out_ref):
-        out_ref[...] = in_ref[...].T if transposed else in_ref[...]
-
-    if transposed:
-        out_spec = pl.BlockSpec((width, rows), lambda j, at_ref: (j, 0))
-        out_shape = jax.ShapeDtypeStruct((many * width, rows), array.dtype)
-    else:
-        out_spec = pl.BlockSpec((rows, width), lambda j, at_ref: (0, j))
-        out_shape = jax.ShapeDtypeStruct((rows, many * width), array.dtype)
+    def kernel(at_ref, in_ref, out_ref, sems):
+        copies = []
+        for j in range(many):
+            source = in_ref.at[:, pl.ds(pl.multiple_of(at_ref[j] * width, width), width)]
+            copies.append(pltpu.make_async_copy(source, out_ref.at[:, pl.ds(j * width, width)], sems.at[j]))
+            copies[-1].start()
+        for copy in copies:
+            copy.wait()
+
+    return call(
+        kernel,
+        at,
+        [array],
+        [jax.ShapeDtypeStruct((rows, many * width), array.dtype)],
+        [pltpu.SemaphoreType.DMA((many,))],
+        flops=0,
+        moved=4 * rows * many * width,
+        name="take",
+        in_hbm=1,
+    )[0]
+
+
+def turn(array, at, width):
+    rows, many = array.shape[0], at.shape[0]
+    half = many // 2
+
+    def kernel(at_ref, in_ref, first_ref, second_ref, held, sem):
+        copy = pltpu.make_async_copy(in_ref, held, sem)
+        copy.start()
+        copy.wait()
+        for j in range(many):
+            block = held[:, pl.ds(pl.multiple_of(at_ref[j] * width, width), width)]
+            out_ref, i = (first_ref, j) if j < half else (second_ref, j - half)
+            out_ref[i * width : (i + 1) * width, :] = block.T
+
     return pl.pallas_call(
         kernel,
         grid_spec=pltpu.PrefetchScalarGridSpec(
             num_scalar_prefetch=1,
-            grid=(many,),
-            in_specs=[pl.BlockSpec((rows, width), lambda j, at_ref: (0, at_ref[j]))],
-            out_specs=out_spec,
+            grid=(1,),
+            in_specs=[pl.BlockSpec(memory_space=pltpu.HBM)],
+            out_specs=[pl.BlockSpec((half * width, rows), lambda j, at_ref: (0, 0))] * 2,
+            scratch_shapes=[pltpu.VMEM(array.shape, array.dtype), pltpu.SemaphoreType.DMA],
         ),
-        out_shape=out_shape,
+        out_shape=[jax.ShapeDtypeStruct((half * width, rows), array.dtype)] * 2,
         compiler_params=params(),
         cost_estimate=cost(0, 4 * rows * many * width),
-        name="pick",
+        name="turn",
     )(at, array)
 
 
-def call(kernel, scalars, arrays, outs, scratch, *, flops, moved, name, aliases=None):
+def call(kernel, scalars, arrays, outs, scratch, *, flops, moved, name, aliases=None, in_hbm=0):
     anywhere = pl.BlockSpec(memory_space=pl.ANY)
     return pl.pallas_call(
         kernel,
         grid_spec=pltpu.PrefetchScalarGridSpec(
             num_scalar_prefetch=1,
             grid=(),
-            in_specs=[anywhere] * len(arrays),
+            in_specs=[pl.BlockSpec(memory_space=pltpu.HBM)] * in_hbm + [anywhere] * (len(arrays) - in_hbm),
             out_specs=[anywhere] * len(outs),
             scratch_shapes=scratch,
         ),
@@ -102,14 +129,15 @@
     )(scalars, *arrays)
 
 
-def project(activations, sibling, first, at, blocks, before):
+def project(activations, sibling, slots, at, blocks, before):
     chunks, many = len(blocks), len(blocks[0])
     (depth, cols), rows = blocks[0][0].shape, activations.shape[0]
     copies = many * (2 + chunks)
     flat = [block for chunk in blocks for block in chunk]
-    held = [] if before is None else [before]
-
-    def kernel(at_ref, own_ref, sib_ref, *refs):
+    held = before or []
+
+    def kernel(at_ref, own_ref, *refs):
+        sib_refs, refs = refs[: len(sibling)], refs[len(sibling) :]
         block_refs, out_ref = refs[: chunks * many], refs[chunks * many + len(held)]
         a, b, total, sems = refs[chunks * many + len(held) + 1 :]
         started = []
@@ -117,15 +145,16 @@
             start = pl.multiple_of(at_ref[j] * depth, depth)
             moves = [
                 (own_ref.at[:, pl.ds(start, depth)], a.at[pl.ds(0, rows), pl.ds(j * depth, depth)]),
-                (sib_ref.at[:, pl.ds((first + j) * depth, depth)], a.at[pl.ds(rows, rows), pl.ds(j * depth, depth)]),
+                (sib_refs[slots[j][0]].at[:, pl.ds(slots[j][1] * depth, depth)], a.at[pl.ds(rows, rows), pl.ds(j * depth, depth)]),
             ]
             for i in range(chunks):
                 moves.append((block_refs[i * many + j], b.at[pl.ds(j * depth, depth), pl.ds(i * cols, cols)]))
             for source, target in moves:
                 started.append(pltpu.make_async_copy(source, target, sems.at[len(started)]))
                 started[-1].start()
-        if held:
-            started.append(pltpu.make_async_copy(refs[chunks * many], total, sems.at[len(started)]))
+        for i in range(len(held)):
+            target = total.at[:, pl.ds(i * cols, cols)]
+            started.append(pltpu.make_async_copy(refs[chunks * many + i], target, sems.at[len(started)]))
             started[-1].start()
         for copy in started:
             copy.wait()
@@ -141,17 +170,18 @@
     return call(
         kernel,
         at,
-        [activations, sibling, *flat, *held],
+        [activations, *sibling, *flat, *held],
         [jax.ShapeDtypeStruct((2 * rows, wide), F32)],
         [
             pltpu.VMEM((2 * rows, many * depth), BF16),
             pltpu.VMEM((many * depth, wide), BF16),
             pltpu.VMEM((2 * rows, wide), F32),
-            pltpu.SemaphoreType.DMA((copies + 2,)),
+            pltpu.SemaphoreType.DMA((copies + len(held) + 1,)),
         ],
         flops=4 * rows * depth * many * wide,
         moved=4 * rows * depth * many + 2 * depth * many * wide + 8 * rows * wide,
         name="project",
+        in_hbm=1,
     )[0]
 
 
@@ -206,23 +236,24 @@
     )(own, sibling, held)
 
 
-def back(blocks, projector_t, at, rows_in_all, before):
+def back(arrays, blocks, projector_t, at, rows, cols, rows_in_all, before):
     many, chunks = len(blocks), len(blocks[0])
-    (rows, cols), (rank, width) = blocks[0][0].shape, projector_t.shape
-    flat = [part for block in blocks for part in block]
+    rank, width = projector_t.shape
     held = [] if before is None else [before]
     slots = min(4, many)
 
     def kernel(at_ref, projector_ref, *refs):
-        block_refs, out_ref = refs[: many * chunks], refs[many * chunks + len(held)]
-        p, d, o, in_sems, out_sems = refs[many * chunks + len(held) + 1 :]
+        array_refs, out_ref = refs[: len(arrays)], refs[len(arrays) + len(held)]
+        p, d, o, in_sems, out_sems = refs[len(arrays) + len(held) + 1 :]
         p_copy = pltpu.make_async_copy(projector_ref, p, in_sems.at[many * chunks])
         p_copy.start()
         loads, stores = [], []
         for j in range(many):
             for i in range(chunks):
                 n = j * chunks + i
-                loads.append(pltpu.make_async_copy(block_refs[n], d.at[j, :, pl.ds(i * cols, cols)], in_sems.at[n]))
+                which, start = blocks[j][i]
+                source = array_refs[which].at[pl.ds(start, rows), :]
+                loads.append(pltpu.make_async_copy(source, d.at[j, :, pl.ds(i * cols, cols)], in_sems.at[n]))
                 loads[-1].start()
         p_copy.wait()
         for j in range(many):
@@ -240,7 +271,7 @@
     return call(
         kernel,
         at,
-        [projector_t, *flat, *held],
+        [projector_t, *arrays, *held],
         [jax.ShapeDtypeStruct((rows_in_all, width), BF16)],
         [
             pltpu.VMEM((rank, width), BF16),
@@ -252,7 +283,7 @@
         flops=2 * many * rows * width * rank,
         moved=2 * many * rows * (width + rank),
         name="back",
-        aliases={2 + len(flat): 0} if held else None,
+        aliases={2 + len(arrays): 0} if held else None,
     )[0]
 
 
@@ -279,42 +310,66 @@
     def named(order):
         return jnp.stack([index(*o) for o in order]).astype(jnp.int32)
 
-    def gather(chunks):
+    def gather(chunks, beside):
         line = [[own] for own in chunks]
         across = [[] for _ in chunks]
         for step in range(nz):
             for i in range(len(chunks)):
                 if step:
-                    line[i][step], across[i][step - 1] = lax.optimization_barrier((line[i][step], across[i][step - 1]))
+                    ready = beside(step, i, line, across)
+                    line[i][step], across[i][step - 1], *_ = lax.optimization_barrier((line[i][step], across[i][step - 1], *ready))
                 if step < nz - 1:
                     line[i].append(shift_z(line[i][step], 1))
                 if step < nz - 1 or i < len(chunks) - 1:
                     across[i].append(swap_y(line[i][step]))
                 else:
                     across[i].append(shift_z(across[i][0], nz - 1))
-        return [{(-k, dy): (line, across)[dy][i][k] for k in range(nz) for dy in (0, 1)} for i in range(len(chunks))]
-
+        return line, across
+
+    after = lambda x, *those: lax.optimization_barrier((x, *those))[0]
     ks = sorted(range(1, nz), key=lambda k: -min(k, nz - k))
     depth, rank = projector.shape
     width = first_moment.shape[0]
     cols = rank // CHUNKS
     parts = [slice(i * cols, (i + 1) * cols) for i in range(CHUNKS)]
 
-    late = [(2 - nz, 1), (1 - nz, 0), (1 - nz, 1)]
-    early = [(-k, dy) for k in range(nz) for dy in (0, 1) if (-k, dy) not in late]
+    order_in = [(-k, dy) for k in range(nz) for dy in (0, 1)]
     order_out = [(k, dy) for dy in (1, 0) for k in ks + [0]]
-
-    gathered = gather([projector[:, part] for part in parts])
-    a_sibling = swap_core(pick(activations, named([(k, dy, 1) for k, dy in early + late]), depth, False))
-    g_sibling = swap_core(pick(out_grads, named([(k, dy, 1) for k, dy in order_out]), width, True))
-    g_own = pick(out_grads, named([(k, dy, 0) for k, dy in order_out]), width, True)
-    projector_t = projector.T
-
-    mine, first = None, 0
-    for order in (early, late):
-        at = named([(k, dy, 0) for k, dy in order])
-        mine = project(activations, a_sibling, first, at, [[chunk[o] for o in order] for chunk in gathered], mine)
-        first += len(order)
+    last, half = len(order_in) - 1, len(order_in) // 2
+    at_in = named([(k, dy, 0) for k, dy in order_in])
+    at_sibling = named([(k, dy, 1) for k, dy in order_in])
+    at_out = named([(k, dy, dc) for dc in (0, 1) for k, dy in order_out])
+    slots = [(j // half, j % half) for j in range(len(order_in))]
+    made = {}
+
+    def beside_projector(step, i, line, across):
+        if (step, i) == (1, 1):
+            made["a0"] = take(activations, after(at_sibling[:half], line[0][1]), depth)
+            return [made["a0"]]
+        if (step, i) == (2, 0):
+            made["a1"] = take(activations, after(at_sibling[half:], line[1][1]), depth)
+            return [made["a1"]]
+        if (step, i) == (2, 1):
+            made["own"], other = turn(out_grads, after(at_out, line[0][2]), width)
+            made["other"] = other
+            return [made["own"], other]
+        if (step, i) == (nz - 1, 0):
+            made["pt"] = after(projector, line[1][2]).T
+            made["a"] = [swap_core(made["a0"]), swap_core(made["a1"])]
+            return [made["pt"]]
+        if (step, i) == (nz - 1, 1):
+            ready = [line[0][n // 2] if n % 2 == 0 else across[0][n // 2] for n in range(last)]
+            made["p0"] = project(activations, made["a"], slots[:last], at_in[:last], [ready], None)
+            return [made["p0"]]
+        return []
+
+    line, across = gather([projector[:, part] for part in parts], beside_projector)
+    g_own, g_sibling = made["own"], swap_core(made["other"])
+    ready = [line[1][n // 2] if n % 2 == 0 else across[1][n // 2] for n in range(last)]
+    made["p1"] = project(activations, made["a"], slots[:last], at_in[:last], [ready], None)
+    mine = project(
+        activations, made["a"], slots[last:], at_in[last:], [[across[0][-1]], [across[1][-1]]], [made["p0"], made["p1"]]
+    )
 
     held, send = outer_first(g_own, g_sibling, mine, swap_core(mine), width)
     sends = [send] + list(outer(g_own, g_sibling, held, width, 1, nz - 1, BF16))
@@ -327,13 +382,29 @@
         reduced = term if reduced is None else reduced + term
     new_first, new_second, direction = adam(reduced, first_moment, second_moment)
 
-    gathered = gather([direction[:, part] for part in parts])
+    def beside_direction(step, i, line, across):
+        if step == nz // 2 or step == nz - 1:
+            low = 0 if step == nz // 2 else half
+            high = half if step == nz // 2 else last
+            group = [line[i][n // 2] if n % 2 == 0 else across[i][n // 2] for n in range(low, high)]
+            made["group", low, i] = jnp.concatenate(group, axis=0)
+            made["swapped", low, i] = swap_core(made["group", low, i])
+        return []
+
+    line, across = gather([direction[:, part] for part in parts], beside_direction)
     update = None
-    for order in (early, late):
-        blocks = [[chunk[o] for chunk in gathered] for o in order]
-        blocks = blocks + [[swap_core(x) for x in block] for block in blocks]
-        at = named([(k, dy, dc) for dc in (0, 1) for k, dy in order])
-        update = back(blocks, projector_t, at, 4 * nz * width, update)
+    for low, high in ((0, half), (half, last + 1)):
+        arrays, blocks = [], []
+        for name in ("group", "swapped"):
+            base = len(arrays)
+            arrays += [made[name, low, i] for i in range(CHUNKS)]
+            blocks += [[(base + i, (n - low) * width) for i in range(CHUNKS)] for n in range(low, min(high, last))]
+            if high > last:
+                ends = [across[i][-1] for i in range(CHUNKS)]
+                arrays += [swap_core(x) for x in ends] if name == "swapped" else ends
+                blocks += [[(base + CHUNKS + i, 0) for i in range(CHUNKS)]]
+        at = named([(k, dy, dc) for dc in (0, 1) for k, dy in order_in[low:high]])
+        update = back(arrays, blocks, made["pt"], at, width, cols, 4 * nz * width, update)
     return update, new_first, new_second
 
 
@@ -342,7 +413,7 @@
 
     def body(activations, out_grads, projector, first_moment, second_moment):
         aligned = projector.shape[0] % 128 == 0 and first_moment.shape[0] % 128 == 0
-        if devices % 4 or devices < 8 or not aligned:
+        if devices % 4 or devices < 16 or not aligned:
             return plain(activations, out_grads, projector, first_moment, second_moment)
         return levels(activations, out_grads, projector, first_moment, second_moment, nz=devices // 4)
 

time: 168 us -> 157 us (0.935)
  waiting for transfers between devices: 47.2 us -> 71.8 us
  starting transfers between devices: 52.8 us -> 36.2 us
  local copies, waits for them, and re-layouts: 35.4 us -> 20.1 us
  Pallas kernels: 29.1 us -> 25.8 us
    ppermute x18, waiting for transfers between devices: 11.1 us -> 40 us  [swap_y(): return lax.ppermute(x, 'dp', pairs(lambda a, b, c: (a, 1 - b, c)))]
    unnamed x81 -> x46, local copies, waits for them, and re-layouts: 34.8 us -> 16.7 us
    ppermute x17, starting transfers between devices: 30.4 us -> 14.3 us  [shift_z(): return lax.ppermute(x, 'dp', pairs(lambda a, b, c: ((a + k) % nz, b, c)))]
    ppermute x17, waiting for transfers between devices: 36.1 us -> 28.4 us  [shift_z(): return lax.ppermute(x, 'dp', pairs(lambda a, b, c: ((a + k) % nz, b, c)))]
    pallas_call x3 -> x1, Pallas kernels: 7.38 us -> 1.63 us  [turn(): pl.pallas_call(kernel, grid_spec=pltpu.PrefetchScalarGridSpec(num_scalar_...]
    pallas_call x4 -> x7, Pallas kernels: 16.7 us -> 20.5 us  [call(): pl.pallas_call(kernel, grid_spec=pltpu.PrefetchScalarGridSpec(num_scalar_...]
    ppermute x19 -> x10, waiting for transfers between devices: 0.05 us -> 3.27 us  [swap_core(): return lax.ppermute(x, 'dp', pairs(lambda a, b, c: (a, b, 1 - c)))]
    optimization_barrier x0 -> x1, local copies, waits for them, and re-layouts: none -> 2.04 us  [levels(): after = lambda x, *those: lax.optimization_barrier((x, *those))[0]]
  transfers between devices with their start and end apart: 54 -> 45, of which waited for: 18 -> 21; matrix products, arithmetic and copies ran while one was open for 1% -> 2% of each run, Pallas kernels for 12% -> 12%
where the time goes in v3:
time: 157 us
  waiting for transfers between devices  71.8 us (46%)
  starting transfers between devices  36.2 us (23%)
  Pallas kernels  25.8 us (16%)
  local copies, waits for them, and re-layouts  20.1 us (13%)
  other arithmetic  1.86 us (1%)
    ppermute x18, waiting for transfers between devices, swap_y(): return lax.ppermute(x, 'dp', pairs(lambda a, b, c: (a, 1 - b, c)))  40 us
    ppermute x17, waiting for transfers between devices, shift_z(): return lax.ppermute(x, 'dp', pairs(lambda a, b, c: ((a + k) % nz, b, c)))  28.4 us
    ppermute x18, starting transfers between devices, swap_y(): return lax.ppermute(x, 'dp', pairs(lambda a, b, c: (a, 1 - b, c)))  20.5 us
    pallas_call x7, Pallas kernels, call(): pl.pallas_call(kernel, grid_spec=pltpu.PrefetchScalarGridSpec(num_scalar_...  20.5 us
    unnamed x46, local copies, waits for them, and re-layouts  16.7 us
    ppermute x17, starting transfers between devices, shift_z(): return lax.ppermute(x, 'dp', pairs(lambda a, b, c: ((a + k) % nz, b, c)))  14.3 us
    ppermute x10, waiting for transfers between devices, swap_core(): return lax.ppermute(x, 'dp', pairs(lambda a, b, c: (a, b, 1 - c)))  3.27 us
    pallas_call x2, Pallas kernels, outer(): pl.pallas_call(kernel, grid=(many,), in_specs=[pl.BlockSpec((width, rows)...  3.16 us
  transfers between devices with their start and end apart: 45, of which 21 were waited for; matrix products, arithmetic and copies ran while one was open for 2% of the time, Pallas kernels for 12%

profile of v3, /device:TPU:0, one launch (start us, length us, event | category | flops | bytes accessed | tf_op | source)
XLA Modules:
  0.0 156.9 jit_solution(2130671745663616545)
XLA Ops:
  1.7 3.0 %collective-permute-start.3 = (bf16[512,256]{1,0:T(8,128)(2,1)S(1)}, bf16[512,256]{1,0:T(8,128)(2,1)S(1)}, u32[]{:S(2)}, u32[]{:S(2)}) collective-permute-start(bf16[512,256]{1,0:T(8,128)(2,1)S(1)} %get-tuple-element.74.refs_2_), channel_id=1, source_target_pairs={{0,2},{1,3},{2,0},{3,1},{4,6},{5,7},{6,4},{7,5},{8,10},{9,11},{10,... | collective-permute-start | bytes 786440 | tf_op jit(solution)/shard_map/ppermute | solution.py:302
  4.7 1.6 %collective-permute-start.2 = (bf16[512,256]{1,0:T(8,128)(2,1)S(1)}, bf16[512,256]{1,0:T(8,128)(2,1)S(1)}, u32[]{:S(2)}, u32[]{:S(2)}) collective-permute-start(bf16[512,256]{1,0:T(8,128)(2,1)S(1)} %get-tuple-element.74.refs_2_), channel_id=1, source_target_pairs={{0,4},{1,5},{2,6},{3,7},{4,8},{5,9},{6,10},{7,11},{8,12},{9,13},{1... | collective-permute-start | bytes 786440 | tf_op jit(solution)/shard_map/ppermute | solution.py:305
  6.8 1.6 %collective-permute-start = (bf16[512,256]{1,0:T(8,128)(2,1)S(1)}, bf16[512,256]{1,0:T(8,128)(2,1)}, u32[]{:S(2)}, u32[]{:S(2)}) collective-permute-start(bf16[512,256]{1,0:T(8,128)(2,1)S(1)} %get-tuple-element.75.refs_2_), channel_id=1, source_target_pairs={{0,4},{1,5},{2,6},{3,7},{4,8},{5,9},{6,10},{7,11},{8,12},{9,13},{1... | collective-permute-start | bytes 786440 | tf_op jit(solution)/shard_map/ppermute | solution.py:305
  8.6 3.3 %collective-permute-done.3.refs_3_ = bf16[512,256]{1,0:T(8,128)(2,1)S(1)} collective-permute-done((bf16[512,256]{1,0:T(8,128)(2,1)S(1)}, bf16[512,256]{1,0:T(8,128)(2,1)S(1)}, u32[]{:S(2)}, u32[]{:S(2)}) %collective-permute-start.3) | collective-permute-done | bytes 262176 | tf_op jit(solution)/shard_map/ppermute | solution.py:302
  11.9 3.9 %collective-permute-done.2.refs_4_ = bf16[512,256]{1,0:T(8,128)(2,1)S(1)} collective-permute-done((bf16[512,256]{1,0:T(8,128)(2,1)S(1)}, bf16[512,256]{1,0:T(8,128)(2,1)S(1)}, u32[]{:S(2)}, u32[]{:S(2)}) %collective-permute-start.2) | collective-permute-done | bytes 262176 | tf_op jit(solution)/shard_map/ppermute | solution.py:305
  15.8 2.8 %copy-done = bf16[384,8192]{1,0:T(8,128)(2,1)S(1)} copy-done((bf16[384,8192]{1,0:T(8,128)(2,1)S(1)}, bf16[384,8192]{1,0:T(8,128)(2,1)}, u32[]{:S(2)}) %copy-start) | copy-done | bytes 6291480
  18.6 1.8 %take.2 = bf16[384,2048]{1,0:T(8,128)(2,1)} custom-call(s32[4]{0:T(128)S(1)} %pad_add_fusion.at_ref, bf16[384,8192]{1,0:T(8,128)(2,1)S(1)} %copy-done), custom_call_target="tpu_custom_call" | custom-call | bytes 3145728 | tf_op jit(solution)/shard_map/take/pallas_call | solution.py:115
  20.4 1.6 %copy-done.1 = bf16[384,8192]{1,0:T(8,128)(2,1)S(1)} copy-done((bf16[384,8192]{1,0:T(8,128)(2,1)S(1)}, bf16[384,8192]{1,0:T(8,128)(2,1)}, u32[]{:S(2)}) %copy-start.1) | copy-done | bytes 6291480
  22.0 1.7 %take.3 = bf16[384,2048]{1,0:T(8,128)(2,1)} custom-call(s32[4]{0:T(128)S(1)} %pad_add_fusion.1.at_ref, bf16[384,8192]{1,0:T(8,128)(2,1)S(1)} %copy-done.1), custom_call_target="tpu_custom_call" | custom-call | bytes 3145728 | tf_op jit(solution)/shard_map/take/pallas_call | solution.py:115
  24.6 1.7 %collective-permute-start.5 = (bf16[512,256]{1,0:T(8,128)(2,1)}, bf16[512,256]{1,0:T(8,128)(2,1)S(1)}, u32[]{:S(2)}, u32[]{:S(2)}) collective-permute-start(bf16[512,256]{1,0:T(8,128)(2,1)} %collective-permute-done.refs_4_), channel_id=1, source_target_pairs={{0,2},{1,3},{2,0},{3,1},{4,6},{5,7},{6,4},{7,5},{8,10},{9,11},{10,... | collective-permute-start | bytes 786440 | tf_op jit(solution)/shard_map/ppermute | solution.py:302
  26.4 7.1 %collective-permute-done.7.refs_5_ = bf16[512,256]{1,0:T(8,128)(2,1)S(1)} collective-permute-done((bf16[512,256]{1,0:T(8,128)(2,1)S(1)}, bf16[512,256]{1,0:T(8,128)(2,1)S(1)}, u32[]{:S(2)}, u32[]{:S(2)}) %collective-permute-start.7) | collective-permute-done | bytes 262176 | tf_op jit(solution)/shard_map/ppermute | solution.py:302
  34.5 1.7 %collective-permute-start.12 = (bf16[512,256]{1,0:T(8,128)(2,1)}, bf16[512,256]{1,0:T(8,128)(2,1)}, u32[]{:S(2)}, u32[]{:S(2)}) collective-permute-start(bf16[512,256]{1,0:T(8,128)(2,1)} %collective-permute-done.6.refs_6_), channel_id=1, source_target_pairs={{0,2},{1,3},{2,0},{3,1},{4,6},{5,7},{6,4},{7,5},{8,10},{9,11},{10,... | collective-permute-start | bytes 786440 | tf_op jit(solution)/shard_map/ppermute | solution.py:302
  36.3 2.8 %collective-permute-done.5.refs_5_ = bf16[512,256]{1,0:T(8,128)(2,1)S(1)} collective-permute-done((bf16[512,256]{1,0:T(8,128)(2,1)}, bf16[512,256]{1,0:T(8,128)(2,1)S(1)}, u32[]{:S(2)}, u32[]{:S(2)}) %collective-permute-start.5) | collective-permute-done | bytes 262176 | tf_op jit(solution)/shard_map/ppermute | solution.py:302
  39.9 1.9 %copy-done.6 = bf16[384,4096]{1,0:T(8,128)(2,1)S(1)} copy-done((bf16[384,4096]{1,0:T(8,128)(2,1)S(1)}, bf16[384,4096]{1,0:T(8,128)(2,1)}, u32[]{:S(2)}) %copy-start.6) | copy-done | bytes 3145752
  41.8 1.6 %turn.1 = (bf16[2048,384]{1,0:T(8,128)(2,1)S(1)}, bf16[2048,384]{1,0:T(8,128)(2,1)S(1)}) custom-call(s32[16]{0:T(128)S(1)} %stack.149.at_ref, bf16[384,4096]{1,0:T(8,128)(2,1)S(1)} %copy-done.6), custom_call_target="tpu_custom_call" | custom-call | bytes 6291456 | tf_op jit(solution)/shard_map/turn/pallas_call | solution.py:97
  46.1 1.6 %collective-permute-start.15 = (bf16[512,256]{1,0:T(8,128)(2,1)}, bf16[512,256]{1,0:T(8,128)(2,1)}, u32[]{:S(2)}, u32[]{:S(2)}) collective-permute-start(bf16[512,256]{1,0:T(8,128)(2,1)} %collective-permute-done.4.refs_6_), channel_id=1, source_target_pairs={{0,4},{1,5},{2,6},{3,7},{4,8},{5,9},{6,10},{7,11},{8,12},{9,13},{1... | collective-permute-start | bytes 786440 | tf_op jit(solution)/shard_map/ppermute | solution.py:305
  47.7 2.0 %copy.9 = bf16[512,512]{0,1:T(8,128)(2,1)} copy(bf16[512,512]{1,0:T(8,128)(2,1)} %param.7) | data formatting | bytes 1048576 | tf_op jit(solution)/shard_map/optimization_barrier | solution.py:329
  49.8 2.2 %collective-permute-start.14 = (bf16[512,256]{1,0:T(8,128)(2,1)}, bf16[512,256]{1,0:T(8,128)(2,1)S(1)}, u32[]{:S(2)}, u32[]{:S(2)}) collective-permute-start(bf16[512,256]{1,0:T(8,128)(2,1)} %collective-permute-done.1.refs_3_), channel_id=1, source_target_pairs={{0,12},{1,13},{2,14},{3,15},{4,0},{5,1},{6,2},{7,3},{8,4},{9,5},{1... | collective-permute-start | bytes 786440 | tf_op jit(solution)/shard_map/ppermute | solution.py:305
  52.0 1.8 %collective-permute-start.13 = (bf16[512,256]{1,0:T(8,128)(2,1)}, bf16[512,256]{1,0:T(8,128)(2,1)S(1)}, u32[]{:S(2)}, u32[]{:S(2)}) collective-permute-start(bf16[512,256]{1,0:T(8,128)(2,1)} %collective-permute-done.11.refs_8_), channel_id=1, source_target_pairs={{0,2},{1,3},{2,0},{3,1},{4,6},{5,7},{6,4},{7,5},{8,10},{9,11},{10,... | collective-permute-start | bytes 786440 | tf_op jit(solution)/shard_map/ppermute | solution.py:302
  53.8 2.8 %copy-done.2 = bf16[384,8192]{1,0:T(8,128)(2,1)S(1)} copy-done((bf16[384,8192]{1,0:T(8,128)(2,1)S(1)}, bf16[384,8192]{1,0:T(8,128)(2,1)}, u32[]{:S(2)}) %copy-start.2) | copy-done | bytes 6291480
  60.4 3.9 %project.3.refs_4_ = f32[768,256]{1,0:T(8,128)S(1)} custom-call(s32[7]{0:T(128)S(1)} %stack.153.at_ref, bf16[384,8192]{1,0:T(8,128)(2,1)S(1)} %copy-done.2, bf16[384,2048]{1,0:T(8,128)(2,1)S(1)} %collective-permute-done.9.refs_0_, bf16[384,2048]{1,0:T(8,128)(2,1)S(1)} %collective-permute-done.10.refs_1_, bf16[512,256]{1,0:T(8,128)(2,1)S(1)} %copy-done.8, ...), custom_call_target="tpu_custom_call" | custom-call | flops 1409286144 | bytes 8126464 | tf_op jit(solution)/shard_map/project/pallas_call | solution.py:115
  64.4 3.9 %project.4.refs_5_ = f32[768,256]{1,0:T(8,128)S(1)} custom-call(s32[7]{0:T(128)S(1)} %stack.153.at_ref, bf16[384,8192]{1,0:T(8,128)(2,1)S(1)} %copy-done.2, bf16[384,2048]{1,0:T(8,128)(2,1)S(1)} %collective-permute-done.9.refs_0_, bf16[384,2048]{1,0:T(8,128)(2,1)S(1)} %collective-permute-done.10.refs_1_, bf16[512,256]{1,0:T(8,128)(2,1)S(1)} %get-tuple-element.75.refs_2_, ...), custom_call_target="tpu_custom_call" | custom-call | flops 1409286144 | bytes 8126464 | tf_op jit(solution)/shard_map/project/pallas_call | solution.py:115
  69.6 3.3 %collective-permute-done.17.theirs_ref = f32[768,512]{1,0:T(8,128)S(1)} collective-permute-done((f32[768,512]{1,0:T(8,128)S(1)}, f32[768,512]{1,0:T(8,128)S(1)}, u32[]{:S(2)}, u32[]{:S(2)}) %collective-permute-start.17) | collective-permute-done | bytes 1572896 | tf_op jit(solution)/shard_map/ppermute | solution.py:299
  73.4 1.4 outer.3
  75.1 1.7 %collective-permute-start.18 = (bf16[256,512]{1,0:T(8,128)(2,1)S(1)}, bf16[256,512]{1,0:T(8,128)(2,1)S(1)}, u32[]{:S(2)}, u32[]{:S(2)}) collective-permute-start(bf16[256,512]{1,0:T(8,128)(2,1)S(1)} %get-tuple-element.57), channel_id=1, source_target_pairs={{0,2},{1,3},{2,0},{3,1},{4,6},{5,7},{6,4},{7,5},{8,10},{9,11},{10,... | collective-permute-start | bytes 786440 | tf_op jit(solution)/shard_map/ppermute | solution.py:302
  77.1 1.7 %collective-permute-start.24 = (bf16[256,512]{1,0:T(8,128)(2,1)S(1)}, bf16[256,512]{1,0:T(8,128)(2,1)S(1)}, u32[]{:S(2)}, u32[]{:S(2)}) collective-permute-start(bf16[256,512]{1,0:T(8,128)(2,1)S(1)} %get-tuple-element.63), channel_id=1, source_target_pairs={{0,2},{1,3},{2,0},{3,1},{4,6},{5,7},{6,4},{7,5},{8,10},{9,11},{10,... | collective-permute-start | bytes 786440 | tf_op jit(solution)/shard_map/ppermute | solution.py:302
  78.9 1.8 %outer.2 = (f32[256,512]{1,0:T(8,128)S(1)}, f32[256,512]{1,0:T(8,128)S(1)}, f32[256,512]{1,0:T(8,128)S(1)}, f32[256,512]{1,0:T(8,128)S(1)}) custom-call(bf16[2048,384]{1,0:T(8,128)(2,1)S(1)} %copy-done.4, bf16[2048,384]{1,0:T(8,128)(2,1)S(1)} %collective-permute-done.8.sib_ref, bf16[768,512]{1,0:T(8,128)(2,1)S(1)} %get-tuple-element.55.held_ref), custom_call_target="tpu_custom_call" | custom-call | flops 805306368 | bytes 3670016 | tf_op jit(solution)/shard_map/outer/pallas_call | solution.py:223
  80.7 3.3 %collective-permute-done.20 = bf16[256,512]{1,0:T(8,128)(2,1)S(1)} collective-permute-done((bf16[256,512]{1,0:T(8,128)(2,1)S(1)}, bf16[256,512]{1,0:T(8,128)(2,1)S(1)}, u32[]{:S(2)}, u32[]{:S(2)}) %collective-permute-start.20) | collective-permute-done | bytes 262176 | tf_op jit(solution)/shard_map/ppermute | solution.py:302
  84.1 11.1 %collective-permute-done.22 = bf16[256,512]{1,0:T(8,128)(2,1)S(1)} collective-permute-done((bf16[256,512]{1,0:T(8,128)(2,1)S(1)}, bf16[256,512]{1,0:T(8,128)(2,1)S(1)}, u32[]{:S(2)}, u32[]{:S(2)}) %collective-permute-start.22) | collective-permute-done | bytes 262176 | tf_op jit(solution)/shard_map/ppermute | solution.py:302
  95.3 2.1 %collective-permute-start.23 = (bf16[256,512]{1,0:T(8,128)(2,1)S(1)}, bf16[256,512]{1,0:T(8,128)(2,1)S(1)}, u32[]{:S(2)}, u32[]{:S(2)}) collective-permute-start(bf16[256,512]{1,0:T(8,128)(2,1)S(1)} %add_convert_fusion), channel_id=1, source_target_pairs={{0,12},{1,13},{2,14},{3,15},{4,0},{5,1},{6,2},{7,3},{8,4},{9,5},{1... | collective-permute-start | bytes 786440 | tf_op jit(solution)/shard_map/ppermute | solution.py:305
  97.5 2.5 %collective-permute-done.24 = bf16[256,512]{1,0:T(8,128)(2,1)S(1)} collective-permute-done((bf16[256,512]{1,0:T(8,128)(2,1)S(1)}, bf16[256,512]{1,0:T(8,128)(2,1)S(1)}, u32[]{:S(2)}, u32[]{:S(2)}) %collective-permute-start.24) | collective-permute-done | bytes 262176 | tf_op jit(solution)/shard_map/ppermute | solution.py:302
  100.0 4.1 %collective-permute-done.23 = bf16[256,512]{1,0:T(8,128)(2,1)S(1)} collective-permute-done((bf16[256,512]{1,0:T(8,128)(2,1)S(1)}, bf16[256,512]{1,0:T(8,128)(2,1)S(1)}, u32[]{:S(2)}, u32[]{:S(2)}) %collective-permute-start.23) | collective-permute-done | bytes 262176 | tf_op jit(solution)/shard_map/ppermute | solution.py:305
  104.1 8.2 %collective-permute-done.19 = bf16[256,512]{1,0:T(8,128)(2,1)S(1)} collective-permute-done((bf16[256,512]{1,0:T(8,128)(2,1)S(1)}, bf16[256,512]{1,0:T(8,128)(2,1)S(1)}, u32[]{:S(2)}, u32[]{:S(2)}) %collective-permute-start.19) | collective-permute-done | bytes 262176 | tf_op jit(solution)/shard_map/ppermute | solution.py:305
  112.3 1.4 divide_convert_fusion
  114.3 1.3 collective-permute-start.31
  115.6 1.5 collective-permute-start.26
  117.1 2.5 %collective-permute-done.32 = bf16[256,256]{1,0:T(8,128)(2,1)S(1)} collective-permute-done((bf16[256,256]{1,0:T(8,128)(2,1)S(1)}, bf16[256,256]{1,0:T(8,128)(2,1)S(1)}, u32[]{:S(2)}, u32[]{:S(2)}) %collective-permute-start.32) | collective-permute-done | bytes 131104 | tf_op jit(solution)/shard_map/ppermute | solution.py:302
  119.7 3.0 %collective-permute-done.31 = bf16[256,256]{1,0:T(8,128)(2,1)S(1)} collective-permute-done((bf16[256,256]{1,0:T(8,128)(2,1)S(1)}, bf16[256,256]{1,0:T(8,128)(2,1)S(1)}, u32[]{:S(2)}, u32[]{:S(2)}) %collective-permute-start.31) | collective-permute-done | bytes 131104 | tf_op jit(solution)/shard_map/ppermute | solution.py:305
  122.7 1.2 collective-permute-start.34
  124.1 1.2 collective-permute-start.28
  125.4 3.8 %collective-permute-start.38 = (bf16[256,256]{1,0:T(8,128)(2,1)S(1)}, bf16[256,256]{1,0:T(8,128)(2,1)S(1)}, u32[]{:S(2)}, u32[]{:S(2)}) collective-permute-start(bf16[256,256]{1,0:T(8,128)(2,1)S(1)} %collective-permute-done.32), channel_id=1, source_target_pairs={{0,12},{1,13},{2,14},{3,15},{4,0},{5,1},{6,2},{7,3},{8,4},{9,5},{1... | collective-permute-start | bytes 393224 | tf_op jit(solution)/shard_map/ppermute | solution.py:305
  129.2 3.0 %collective-permute-done.33 = bf16[256,256]{1,0:T(8,128)(2,1)S(1)} collective-permute-done((bf16[256,256]{1,0:T(8,128)(2,1)S(1)}, bf16[256,256]{1,0:T(8,128)(2,1)S(1)}, u32[]{:S(2)}, u32[]{:S(2)}) %collective-permute-start.33) | collective-permute-done | bytes 131104 | tf_op jit(solution)/shard_map/ppermute | solution.py:305
  132.9 2.1 %collective-permute-done.27 = bf16[256,256]{1,0:T(8,128)(2,1)S(1)} collective-permute-done((bf16[256,256]{1,0:T(8,128)(2,1)S(1)}, bf16[256,256]{1,0:T(8,128)(2,1)S(1)}, u32[]{:S(2)}, u32[]{:S(2)}) %collective-permute-start.27) | collective-permute-done | bytes 131104 | tf_op jit(solution)/shard_map/ppermute | solution.py:305
  137.2 1.8 %collective-permute-done.36 = bf16[256,256]{1,0:T(8,128)(2,1)S(1)} collective-permute-done((bf16[256,256]{1,0:T(8,128)(2,1)S(1)}, bf16[256,256]{1,0:T(8,128)(2,1)S(1)}, u32[]{:S(2)}, u32[]{:S(2)}) %collective-permute-start.36) | collective-permute-done | bytes 131104 | tf_op jit(solution)/shard_map/ppermute | solution.py:305
  140.1 1.8 %collective-permute-done.30 = bf16[256,256]{1,0:T(8,128)(2,1)S(1)} collective-permute-done((bf16[256,256]{1,0:T(8,128)(2,1)S(1)}, bf16[256,256]{1,0:T(8,128)(2,1)S(1)}, u32[]{:S(2)}, u32[]{:S(2)}) %collective-permute-start.30) | collective-permute-done | bytes 131104 | tf_op jit(solution)/shard_map/ppermute | solution.py:305
  142.8 5.1 %collective-permute-done.37.refs_2_ = bf16[256,256]{1,0:T(8,128)(2,1)} collective-permute-done((bf16[256,256]{1,0:T(8,128)(2,1)S(1)}, bf16[256,256]{1,0:T(8,128)(2,1)}, u32[]{:S(2)}, u32[]{:S(2)}) %collective-permute-start.37) | collective-permute-done | bytes 131104 | tf_op jit(solution)/shard_map/ppermute | solution.py:302
  148.6 4.1 %back.2.refs_8_ = bf16[4096,512]{1,0:T(8,128)(2,1)} custom-call(s32[8]{0:T(128)S(1)} %stack.154.at_ref, bf16[512,512]{1,0:T(8,128)(2,1)S(1)} %bitcast.29, bf16[1024,256]{1,0:T(8,128)(2,1)S(1)} %pad_maximum_fusion.refs_0_, bf16[1024,256]{1,0:T(8,128)(2,1)S(1)} %pad_maximum_fusion.1.refs_1_, bf16[1024,256]{1,0:T(8,128)(2,1)S(1)} %collective-permute-done.43.refs_2_, ...), custom_call_target="tpu_custom_call" | custom-call | flops 1073741824 | bytes 4194304 | tf_op jit(solution)/shard_map/back/pallas_call | solution.py:115
  152.8 4.0 %back.3 = bf16[4096,512]{1,0:T(8,128)(2,1)} custom-call(s32[8]{0:T(128)S(1)} %stack.129.at_ref, bf16[512,512]{1,0:T(8,128)(2,1)S(1)} %bitcast.30, bf16[768,256]{1,0:T(8,128)(2,1)S(1)} %constant_dynamic-update-slice_fusion.refs_0_, bf16[768,256]{1,0:T(8,128)(2,1)S(1)} %constant_dynamic-update-slice_fusion.3.refs_1_, ...), custom_call_target="tpu_custom_call", output_to_operand_aliasing={{}: (10, {})} | custom-call | flops 1073741824 | bytes 4194304 | tf_op jit(solution)/shard_map/back/pallas_call | solution.py:115
  (116 shorter events, 20.0 us)
Async XLA Ops:
  1.7 18.6 %copy-start.7 = (bf16[512,256]{1,0:T(8,128)(2,1)}, bf16[512,256]{1,0:T(8,128)(2,1)S(1)}, u32[]{:S(2)}) copy-start(bf16[512,256]{1,0:T(8,128)(2,1)S(1)} %get-tuple-element.74.refs_2_) | copy-start | bytes 786436
  1.7 10.2 %collective-permute-start.3 = (bf16[512,256]{1,0:T(8,128)(2,1)S(1)}, bf16[512,256]{1,0:T(8,128)(2,1)S(1)}, u32[]{:S(2)}, u32[]{:S(2)}) collective-permute-start(bf16[512,256]{1,0:T(8,128)(2,1)S(1)} %get-tuple-element.74.refs_2_), channel_id=1, source_target_pairs={{0,2},{1,3},{2,0},{3,1},{4,6},{5,7},{6,4},{7,5},{8,10},{9,11},{10,... | collective-permute-start | bytes 786440 | tf_op jit(solution)/shard_map/ppermute | solution.py:302
  4.7 11.0 %collective-permute-start.2 = (bf16[512,256]{1,0:T(8,128)(2,1)S(1)}, bf16[512,256]{1,0:T(8,128)(2,1)S(1)}, u32[]{:S(2)}, u32[]{:S(2)}) collective-permute-start(bf16[512,256]{1,0:T(8,128)(2,1)S(1)} %get-tuple-element.74.refs_2_), channel_id=1, source_target_pairs={{0,4},{1,5},{2,6},{3,7},{4,8},{5,9},{6,10},{7,11},{8,12},{9,13},{1... | collective-permute-start | bytes 786440 | tf_op jit(solution)/shard_map/ppermute | solution.py:305
  6.3 14.1 %collective-permute-start.1 = (bf16[512,256]{1,0:T(8,128)(2,1)S(1)}, bf16[512,256]{1,0:T(8,128)(2,1)}, u32[]{:S(2)}, u32[]{:S(2)}) collective-permute-start(bf16[512,256]{1,0:T(8,128)(2,1)S(1)} %get-tuple-element.75.refs_2_), channel_id=1, source_target_pairs={{0,2},{1,3},{2,0},{3,1},{4,6},{5,7},{6,4},{7,5},{8,10},{9,11},{10,... | collective-permute-start | bytes 786440 | tf_op jit(solution)/shard_map/ppermute | solution.py:302
  6.8 13.6 %collective-permute-start = (bf16[512,256]{1,0:T(8,128)(2,1)S(1)}, bf16[512,256]{1,0:T(8,128)(2,1)}, u32[]{:S(2)}, u32[]{:S(2)}) collective-permute-start(bf16[512,256]{1,0:T(8,128)(2,1)S(1)} %get-tuple-element.75.refs_2_), channel_id=1, source_target_pairs={{0,4},{1,5},{2,6},{3,7},{4,8},{5,9},{6,10},{7,11},{8,12},{9,13},{1... | collective-permute-start | bytes 786440 | tf_op jit(solution)/shard_map/ppermute | solution.py:305
  23.7 28.3 %collective-permute-start.10 = (bf16[384,2048]{1,0:T(8,128)(2,1)}, bf16[384,2048]{1,0:T(8,128)(2,1)S(1)}, u32[]{:S(2)}, u32[]{:S(2)}) collective-permute-start(bf16[384,2048]{1,0:T(8,128)(2,1)} %take.3), channel_id=1, source_target_pairs={{0,1},{1,0},{2,3},{3,2},{4,5},{5,4},{6,7},{7,6},{8,9},{9,8},{10,11... | collective-permute-start | bytes 4718600 | tf_op jit(solution)/shard_map/ppermute | solution.py:299
  23.8 28.2 %collective-permute-start.9 = (bf16[384,2048]{1,0:T(8,128)(2,1)}, bf16[384,2048]{1,0:T(8,128)(2,1)S(1)}, u32[]{:S(2)}, u32[]{:S(2)}) collective-permute-start(bf16[384,2048]{1,0:T(8,128)(2,1)} %take.2), channel_id=1, source_target_pairs={{0,1},{1,0},{2,3},{3,2},{4,5},{5,4},{6,7},{7,6},{8,9},{9,8},{10,11... | collective-permute-start | bytes 4718600 | tf_op jit(solution)/shard_map/ppermute | solution.py:299
  24.3 9.2 %collective-permute-start.7 = (bf16[512,256]{1,0:T(8,128)(2,1)S(1)}, bf16[512,256]{1,0:T(8,128)(2,1)S(1)}, u32[]{:S(2)}, u32[]{:S(2)}) collective-permute-start(bf16[512,256]{1,0:T(8,128)(2,1)S(1)} %copy-done.12), channel_id=1, source_target_pairs={{0,2},{1,3},{2,0},{3,1},{4,6},{5,7},{6,4},{7,5},{8,10},{9,11},{10,... | collective-permute-start | bytes 786440 | tf_op jit(solution)/shard_map/ppermute | solution.py:302
  24.6 9.9 %collective-permute-start.6 = (bf16[512,256]{1,0:T(8,128)(2,1)S(1)}, bf16[512,256]{1,0:T(8,128)(2,1)}, u32[]{:S(2)}, u32[]{:S(2)}) collective-permute-start(bf16[512,256]{1,0:T(8,128)(2,1)S(1)} %copy-done.12), channel_id=1, source_target_pairs={{0,4},{1,5},{2,6},{3,7},{4,8},{5,9},{6,10},{7,11},{8,12},{9,13},{1... | collective-permute-start | bytes 786440 | tf_op jit(solution)/shard_map/ppermute | solution.py:305
  24.6 14.5 %collective-permute-start.5 = (bf16[512,256]{1,0:T(8,128)(2,1)}, bf16[512,256]{1,0:T(8,128)(2,1)S(1)}, u32[]{:S(2)}, u32[]{:S(2)}) collective-permute-start(bf16[512,256]{1,0:T(8,128)(2,1)} %collective-permute-done.refs_4_), channel_id=1, source_target_pairs={{0,2},{1,3},{2,0},{3,1},{4,6},{5,7},{6,4},{7,5},{8,10},{9,11},{10,... | collective-permute-start | bytes 786440 | tf_op jit(solution)/shard_map/ppermute | solution.py:302
  34.2 11.6 %collective-permute-start.4 = (bf16[512,256]{1,0:T(8,128)(2,1)}, bf16[512,256]{1,0:T(8,128)(2,1)}, u32[]{:S(2)}, u32[]{:S(2)}) collective-permute-start(bf16[512,256]{1,0:T(8,128)(2,1)} %collective-permute-done.refs_4_), channel_id=1, source_target_pairs={{0,4},{1,5},{2,6},{3,7},{4,8},{5,9},{6,10},{7,11},{8,12},{9,13},{1... | collective-permute-start | bytes 786440 | tf_op jit(solution)/shard_map/ppermute | solution.py:305
  34.5 11.5 %collective-permute-start.12 = (bf16[512,256]{1,0:T(8,128)(2,1)}, bf16[512,256]{1,0:T(8,128)(2,1)}, u32[]{:S(2)}, u32[]{:S(2)}) collective-permute-start(bf16[512,256]{1,0:T(8,128)(2,1)} %collective-permute-done.6.refs_6_), channel_id=1, source_target_pairs={{0,2},{1,3},{2,0},{3,1},{4,6},{5,7},{6,4},{7,5},{8,10},{9,11},{10,... | collective-permute-start | bytes 786440 | tf_op jit(solution)/shard_map/ppermute | solution.py:302
  39.8 9.9 %collective-permute-start.11 = (bf16[512,256]{1,0:T(8,128)(2,1)}, bf16[512,256]{1,0:T(8,128)(2,1)}, u32[]{:S(2)}, u32[]{:S(2)}) collective-permute-start(bf16[512,256]{1,0:T(8,128)(2,1)} %collective-permute-done.6.refs_6_), channel_id=1, source_target_pairs={{0,4},{1,5},{2,6},{3,7},{4,8},{5,9},{6,10},{7,11},{8,12},{9,13},{1... | collective-permute-start | bytes 786440 | tf_op jit(solution)/shard_map/ppermute | solution.py:305
  45.8 18.6 %collective-permute-start.16 = (bf16[512,256]{1,0:T(8,128)(2,1)}, bf16[512,256]{1,0:T(8,128)(2,1)}, u32[]{:S(2)}, u32[]{:S(2)}) collective-permute-start(bf16[512,256]{1,0:T(8,128)(2,1)} %collective-permute-done.4.refs_6_), channel_id=1, source_target_pairs={{0,2},{1,3},{2,0},{3,1},{4,6},{5,7},{6,4},{7,5},{8,10},{9,11},{10,... | collective-permute-start | bytes 786440 | tf_op jit(solution)/shard_map/ppermute | solution.py:302
  46.1 18.3 %collective-permute-start.15 = (bf16[512,256]{1,0:T(8,128)(2,1)}, bf16[512,256]{1,0:T(8,128)(2,1)}, u32[]{:S(2)}, u32[]{:S(2)}) collective-permute-start(bf16[512,256]{1,0:T(8,128)(2,1)} %collective-permute-done.4.refs_6_), channel_id=1, source_target_pairs={{0,4},{1,5},{2,6},{3,7},{4,8},{5,9},{6,10},{7,11},{8,12},{9,13},{1... | collective-permute-start | bytes 786440 | tf_op jit(solution)/shard_map/ppermute | solution.py:305
  49.8 18.5 %collective-permute-start.14 = (bf16[512,256]{1,0:T(8,128)(2,1)}, bf16[512,256]{1,0:T(8,128)(2,1)S(1)}, u32[]{:S(2)}, u32[]{:S(2)}) collective-permute-start(bf16[512,256]{1,0:T(8,128)(2,1)} %collective-permute-done.1.refs_3_), channel_id=1, source_target_pairs={{0,12},{1,13},{2,14},{3,15},{4,0},{5,1},{6,2},{7,3},{8,4},{9,5},{1... | collective-permute-start | bytes 786440 | tf_op jit(solution)/shard_map/ppermute | solution.py:305
  52.0 17.6 %collective-permute-start.8 = (bf16[2048,384]{1,0:T(8,128)(2,1)}, bf16[2048,384]{1,0:T(8,128)(2,1)S(1)}, u32[]{:S(2)}, u32[]{:S(2)}) collective-permute-start(bf16[2048,384]{1,0:T(8,128)(2,1)} %copy-done.18), channel_id=1, source_target_pairs={{0,1},{1,0},{2,3},{3,2},{4,5},{5,4},{6,7},{7,6},{8,9},{9,8},{10,11... | collective-permute-start | bytes 4718600 | tf_op jit(solution)/shard_map/ppermute | solution.py:299
  52.0 16.3 %collective-permute-start.13 = (bf16[512,256]{1,0:T(8,128)(2,1)}, bf16[512,256]{1,0:T(8,128)(2,1)S(1)}, u32[]{:S(2)}, u32[]{:S(2)}) collective-permute-start(bf16[512,256]{1,0:T(8,128)(2,1)} %collective-permute-done.11.refs_8_), channel_id=1, source_target_pairs={{0,2},{1,3},{2,0},{3,1},{4,6},{5,7},{6,4},{7,5},{8,10},{9,11},{10,... | collective-permute-start | bytes 786440 | tf_op jit(solution)/shard_map/ppermute | solution.py:302
  69.4 3.5 %collective-permute-start.17 = (f32[768,512]{1,0:T(8,128)S(1)}, f32[768,512]{1,0:T(8,128)S(1)}, u32[]{:S(2)}, u32[]{:S(2)}) collective-permute-start(f32[768,512]{1,0:T(8,128)S(1)} %project.5.mine_ref), channel_id=1, source_target_pairs={{0,1},{1,0},{2,3},{3,2},{4,5},{5,4},{6,7},{7,6},{8,9},{9,8},{10,11... | collective-permute-start | bytes 4718600 | tf_op jit(solution)/shard_map/ppermute | solution.py:299
  74.7 9.2 %collective-permute-start.20 = (bf16[256,512]{1,0:T(8,128)(2,1)S(1)}, bf16[256,512]{1,0:T(8,128)(2,1)S(1)}, u32[]{:S(2)}, u32[]{:S(2)}) collective-permute-start(bf16[256,512]{1,0:T(8,128)(2,1)S(1)} %get-tuple-element.59), channel_id=1, source_target_pairs={{0,2},{1,3},{2,0},{3,1},{4,6},{5,7},{6,4},{7,5},{8,10},{9,11},{10,... | collective-permute-start | bytes 786440 | tf_op jit(solution)/shard_map/ppermute | solution.py:302
  75.1 22.2 %collective-permute-start.18 = (bf16[256,512]{1,0:T(8,128)(2,1)S(1)}, bf16[256,512]{1,0:T(8,128)(2,1)S(1)}, u32[]{:S(2)}, u32[]{:S(2)}) collective-permute-start(bf16[256,512]{1,0:T(8,128)(2,1)S(1)} %get-tuple-element.57), channel_id=1, source_target_pairs={{0,2},{1,3},{2,0},{3,1},{4,6},{5,7},{6,4},{7,5},{8,10},{9,11},{10,... | collective-permute-start | bytes 786440 | tf_op jit(solution)/shard_map/ppermute | solution.py:302
  76.8 18.4 %collective-permute-start.22 = (bf16[256,512]{1,0:T(8,128)(2,1)S(1)}, bf16[256,512]{1,0:T(8,128)(2,1)S(1)}, u32[]{:S(2)}, u32[]{:S(2)}) collective-permute-start(bf16[256,512]{1,0:T(8,128)(2,1)S(1)} %get-tuple-element.61), channel_id=1, source_target_pairs={{0,2},{1,3},{2,0},{3,1},{4,6},{5,7},{6,4},{7,5},{8,10},{9,11},{10,... | collective-permute-start | bytes 786440 | tf_op jit(solution)/shard_map/ppermute | solution.py:302
  77.1 22.9 %collective-permute-start.24 = (bf16[256,512]{1,0:T(8,128)(2,1)S(1)}, bf16[256,512]{1,0:T(8,128)(2,1)S(1)}, u32[]{:S(2)}, u32[]{:S(2)}) collective-permute-start(bf16[256,512]{1,0:T(8,128)(2,1)S(1)} %get-tuple-element.63), channel_id=1, source_target_pairs={{0,2},{1,3},{2,0},{3,1},{4,6},{5,7},{6,4},{7,5},{8,10},{9,11},{10,... | collective-permute-start | bytes 786440 | tf_op jit(solution)/shard_map/ppermute | solution.py:302
  84.0 28.3 %copy-start.19 = (f32[256,512]{1,0:T(8,128)S(1)}, f32[256,512]{1,0:T(8,128)}, u32[]{:S(2)}) copy-start(f32[256,512]{1,0:T(8,128)} %param.8) | copy-start | bytes 1572868
  84.0 28.3 %copy-start.20 = (f32[256,512]{1,0:T(8,128)S(1)}, f32[256,512]{1,0:T(8,128)}, u32[]{:S(2)}) copy-start(f32[256,512]{1,0:T(8,128)} %param.9) | copy-start | bytes 1572868
  84.0 16.0 %collective-permute-start.21 = (bf16[256,512]{1,0:T(8,128)(2,1)S(1)}, bf16[256,512]{1,0:T(8,128)(2,1)S(1)}, u32[]{:S(2)}, u32[]{:S(2)}) collective-permute-start(bf16[256,512]{1,0:T(8,128)(2,1)S(1)} %add_convert_fusion.1), channel_id=1, source_target_pairs={{0,4},{1,5},{2,6},{3,7},{4,8},{5,9},{6,10},{7,11},{8,12},{9,13},{1... | collective-permute-start | bytes 786440 | tf_op jit(solution)/shard_map/ppermute | solution.py:305
  95.3 8.8 %collective-permute-start.23 = (bf16[256,512]{1,0:T(8,128)(2,1)S(1)}, bf16[256,512]{1,0:T(8,128)(2,1)S(1)}, u32[]{:S(2)}, u32[]{:S(2)}) collective-permute-start(bf16[256,512]{1,0:T(8,128)(2,1)S(1)} %add_convert_fusion), channel_id=1, source_target_pairs={{0,12},{1,13},{2,14},{3,15},{4,0},{5,1},{6,2},{7,3},{8,4},{9,5},{1... | collective-permute-start | bytes 786440 | tf_op jit(solution)/shard_map/ppermute | solution.py:305
  97.4 14.9 %collective-permute-start.19 = (bf16[256,512]{1,0:T(8,128)(2,1)S(1)}, bf16[256,512]{1,0:T(8,128)(2,1)S(1)}, u32[]{:S(2)}, u32[]{:S(2)}) collective-permute-start(bf16[256,512]{1,0:T(8,128)(2,1)S(1)} %add_convert_fusion.2), channel_id=1, source_target_pairs={{0,8},{1,9},{2,10},{3,11},{4,12},{5,13},{6,14},{7,15},{8,0},{9,1},... | collective-permute-start | bytes 786440 | tf_op jit(solution)/shard_map/ppermute | solution.py:305
  113.7 5.9 %collective-permute-start.32 = (bf16[256,256]{1,0:T(8,128)(2,1)S(1)}, bf16[256,256]{1,0:T(8,128)(2,1)S(1)}, u32[]{:S(2)}, u32[]{:S(2)}) collective-permute-start(bf16[256,256]{1,0:T(8,128)(2,1)S(1)} %get-tuple-element.76), channel_id=1, source_target_pairs={{0,2},{1,3},{2,0},{3,1},{4,6},{5,7},{6,4},{7,5},{8,10},{9,11},{10,... | collective-permute-start | bytes 393224 | tf_op jit(solution)/shard_map/ppermute | solution.py:302
  114.3 8.4 %collective-permute-start.31 = (bf16[256,256]{1,0:T(8,128)(2,1)S(1)}, bf16[256,256]{1,0:T(8,128)(2,1)S(1)}, u32[]{:S(2)}, u32[]{:S(2)}) collective-permute-start(bf16[256,256]{1,0:T(8,128)(2,1)S(1)} %get-tuple-element.76), channel_id=1, source_target_pairs={{0,4},{1,5},{2,6},{3,7},{4,8},{5,9},{6,10},{7,11},{8,12},{9,13},{1... | collective-permute-start | bytes 393224 | tf_op jit(solution)/shard_map/ppermute | solution.py:305
  115.6 8.3 %collective-permute-start.26 = (bf16[256,256]{1,0:T(8,128)(2,1)S(1)}, bf16[256,256]{1,0:T(8,128)(2,1)S(1)}, u32[]{:S(2)}, u32[]{:S(2)}) collective-permute-start(bf16[256,256]{1,0:T(8,128)(2,1)S(1)} %get-tuple-element.77), channel_id=1, source_target_pairs={{0,2},{1,3},{2,0},{3,1},{4,6},{5,7},{6,4},{7,5},{8,10},{9,11},{10,... | collective-permute-start | bytes 393224 | tf_op jit(solution)/shard_map/ppermute | solution.py:302
  117.1 7.0 %collective-permute-start.25 = (bf16[256,256]{1,0:T(8,128)(2,1)S(1)}, bf16[256,256]{1,0:T(8,128)(2,1)S(1)}, u32[]{:S(2)}, u32[]{:S(2)}) collective-permute-start(bf16[256,256]{1,0:T(8,128)(2,1)S(1)} %get-tuple-element.77), channel_id=1, source_target_pairs={{0,4},{1,5},{2,6},{3,7},{4,8},{5,9},{6,10},{7,11},{8,12},{9,13},{1... | collective-permute-start | bytes 393224 | tf_op jit(solution)/shard_map/ppermute | solution.py:305
  122.7 6.5 %collective-permute-start.34 = (bf16[256,256]{1,0:T(8,128)(2,1)S(1)}, bf16[256,256]{1,0:T(8,128)(2,1)S(1)}, u32[]{:S(2)}, u32[]{:S(2)}) collective-permute-start(bf16[256,256]{1,0:T(8,128)(2,1)S(1)} %collective-permute-done.31), channel_id=1, source_target_pairs={{0,2},{1,3},{2,0},{3,1},{4,6},{5,7},{6,4},{7,5},{8,10},{9,11},{10,... | collective-permute-start | bytes 393224 | tf_op jit(solution)/shard_map/ppermute | solution.py:302
  123.9 8.3 %collective-permute-start.33 = (bf16[256,256]{1,0:T(8,128)(2,1)S(1)}, bf16[256,256]{1,0:T(8,128)(2,1)S(1)}, u32[]{:S(2)}, u32[]{:S(2)}) collective-permute-start(bf16[256,256]{1,0:T(8,128)(2,1)S(1)} %collective-permute-done.31), channel_id=1, source_target_pairs={{0,4},{1,5},{2,6},{3,7},{4,8},{5,9},{6,10},{7,11},{8,12},{9,13},{1... | collective-permute-start | bytes 393224 | tf_op jit(solution)/shard_map/ppermute | solution.py:305
  124.1 8.8 %collective-permute-start.28 = (bf16[256,256]{1,0:T(8,128)(2,1)S(1)}, bf16[256,256]{1,0:T(8,128)(2,1)S(1)}, u32[]{:S(2)}, u32[]{:S(2)}) collective-permute-start(bf16[256,256]{1,0:T(8,128)(2,1)S(1)} %collective-permute-done.25), channel_id=1, source_target_pairs={{0,2},{1,3},{2,0},{3,1},{4,6},{5,7},{6,4},{7,5},{8,10},{9,11},{10,... | collective-permute-start | bytes 393224 | tf_op jit(solution)/shard_map/ppermute | solution.py:302
  125.4 9.7 %collective-permute-start.27 = (bf16[256,256]{1,0:T(8,128)(2,1)S(1)}, bf16[256,256]{1,0:T(8,128)(2,1)S(1)}, u32[]{:S(2)}, u32[]{:S(2)}) collective-permute-start(bf16[256,256]{1,0:T(8,128)(2,1)S(1)} %collective-permute-done.25), channel_id=1, source_target_pairs={{0,4},{1,5},{2,6},{3,7},{4,8},{5,9},{6,10},{7,11},{8,12},{9,13},{1... | collective-permute-start | bytes 393224 | tf_op jit(solution)/shard_map/ppermute | solution.py:305
  125.4 16.6 %collective-permute-start.38 = (bf16[256,256]{1,0:T(8,128)(2,1)S(1)}, bf16[256,256]{1,0:T(8,128)(2,1)S(1)}, u32[]{:S(2)}, u32[]{:S(2)}) collective-permute-start(bf16[256,256]{1,0:T(8,128)(2,1)S(1)} %collective-permute-done.32), channel_id=1, source_target_pairs={{0,12},{1,13},{2,14},{3,15},{4,0},{5,1},{6,2},{7,3},{8,4},{9,5},{1... | collective-permute-start | bytes 393224 | tf_op jit(solution)/shard_map/ppermute | solution.py:305
  132.2 6.8 %collective-permute-start.36 = (bf16[256,256]{1,0:T(8,128)(2,1)S(1)}, bf16[256,256]{1,0:T(8,128)(2,1)S(1)}, u32[]{:S(2)}, u32[]{:S(2)}) collective-permute-start(bf16[256,256]{1,0:T(8,128)(2,1)S(1)} %collective-permute-done.33), channel_id=1, source_target_pairs={{0,4},{1,5},{2,6},{3,7},{4,8},{5,9},{6,10},{7,11},{8,12},{9,13},{1... | collective-permute-start | bytes 393224 | tf_op jit(solution)/shard_map/ppermute | solution.py:305
  132.2 5.0 %collective-permute-start.35 = (bf16[256,256]{1,0:T(8,128)(2,1)S(1)}, bf16[256,256]{1,0:T(8,128)(2,1)S(1)}, u32[]{:S(2)}, u32[]{:S(2)}) collective-permute-start(bf16[256,256]{1,0:T(8,128)(2,1)S(1)} %collective-permute-done.33), channel_id=1, source_target_pairs={{0,2},{1,3},{2,0},{3,1},{4,6},{5,7},{6,4},{7,5},{8,10},{9,11},{10,... | collective-permute-start | bytes 393224 | tf_op jit(solution)/shard_map/ppermute | solution.py:302
  135.1 6.8 %collective-permute-start.30 = (bf16[256,256]{1,0:T(8,128)(2,1)S(1)}, bf16[256,256]{1,0:T(8,128)(2,1)S(1)}, u32[]{:S(2)}, u32[]{:S(2)}) collective-permute-start(bf16[256,256]{1,0:T(8,128)(2,1)S(1)} %collective-permute-done.27), channel_id=1, source_target_pairs={{0,4},{1,5},{2,6},{3,7},{4,8},{5,9},{6,10},{7,11},{8,12},{9,13},{1... | collective-permute-start | bytes 393224 | tf_op jit(solution)/shard_map/ppermute | solution.py:305
  135.1 5.0 %collective-permute-start.29 = (bf16[256,256]{1,0:T(8,128)(2,1)S(1)}, bf16[256,256]{1,0:T(8,128)(2,1)S(1)}, u32[]{:S(2)}, u32[]{:S(2)}) collective-permute-start(bf16[256,256]{1,0:T(8,128)(2,1)S(1)} %collective-permute-done.27), channel_id=1, source_target_pairs={{0,2},{1,3},{2,0},{3,1},{4,6},{5,7},{6,4},{7,5},{8,10},{9,11},{10,... | collective-permute-start | bytes 393224 | tf_op jit(solution)/shard_map/ppermute | solution.py:302
  137.2 10.8 %collective-permute-start.44 = (bf16[1024,256]{1,0:T(8,128)(2,1)S(1)}, bf16[1024,256]{1,0:T(8,128)(2,1)S(1)}, u32[]{:S(2)}, u32[]{:S(2)}) collective-permute-start(bf16[1024,256]{1,0:T(8,128)(2,1)S(1)} %pad_maximum_fusion.1.refs_1_), channel_id=1, source_target_pairs={{0,1},{1,0},{2,3},{3,2},{4,5},{5,4},{6,7},{7,6},{8,9},{9,8},{10,11... | collective-permute-start | bytes 1572872 | tf_op jit(solution)/shard_map/ppermute | solution.py:299
  139.0 9.6 %collective-permute-start.43 = (bf16[1024,256]{1,0:T(8,128)(2,1)S(1)}, bf16[1024,256]{1,0:T(8,128)(2,1)S(1)}, u32[]{:S(2)}, u32[]{:S(2)}) collective-permute-start(bf16[1024,256]{1,0:T(8,128)(2,1)S(1)} %pad_maximum_fusion.refs_0_), channel_id=1, source_target_pairs={{0,1},{1,0},{2,3},{3,2},{4,5},{5,4},{6,7},{7,6},{8,9},{9,8},{10,11... | collective-permute-start | bytes 1572872 | tf_op jit(solution)/shard_map/ppermute | solution.py:299
  140.0 12.7 %collective-permute-start.40 = (bf16[768,256]{1,0:T(8,128)(2,1)S(1)}, bf16[768,256]{1,0:T(8,128)(2,1)}, u32[]{:S(2)}, u32[]{:S(2)}) collective-permute-start(bf16[768,256]{1,0:T(8,128)(2,1)S(1)} %constant_dynamic-update-slice_fusion.3.refs_1_), channel_id=1, source_target_pairs={{0,1},{1,0},{2,3},{3,2},{4,5},{5,4},{6,7},{7,6},{8,9},{9,8},{10,11... | collective-permute-start | bytes 1179656 | tf_op jit(solution)/shard_map/ppermute | solution.py:299
  141.8 10.9 %collective-permute-start.39 = (bf16[768,256]{1,0:T(8,128)(2,1)S(1)}, bf16[768,256]{1,0:T(8,128)(2,1)}, u32[]{:S(2)}, u32[]{:S(2)}) collective-permute-start(bf16[768,256]{1,0:T(8,128)(2,1)S(1)} %constant_dynamic-update-slice_fusion.refs_0_), channel_id=1, source_target_pairs={{0,1},{1,0},{2,3},{3,2},{4,5},{5,4},{6,7},{7,6},{8,9},{9,8},{10,11... | collective-permute-start | bytes 1179656 | tf_op jit(solution)/shard_map/ppermute | solution.py:299
  141.9 6.0 %collective-permute-start.37 = (bf16[256,256]{1,0:T(8,128)(2,1)S(1)}, bf16[256,256]{1,0:T(8,128)(2,1)}, u32[]{:S(2)}, u32[]{:S(2)}) collective-permute-start(bf16[256,256]{1,0:T(8,128)(2,1)S(1)} %collective-permute-done.30), channel_id=1, source_target_pairs={{0,2},{1,3},{2,0},{3,1},{4,6},{5,7},{6,4},{7,5},{8,10},{9,11},{10,... | collective-permute-start | bytes 393224 | tf_op jit(solution)/shard_map/ppermute | solution.py:302
  147.9 4.8 %collective-permute-start.42 = (bf16[256,256]{1,0:T(8,128)(2,1)S(1)}, bf16[256,256]{1,0:T(8,128)(2,1)}, u32[]{:S(2)}, u32[]{:S(2)}) collective-permute-start(bf16[256,256]{1,0:T(8,128)(2,1)S(1)} %collective-permute-done.38.refs_3_), channel_id=1, source_target_pairs={{0,1},{1,0},{2,3},{3,2},{4,5},{5,4},{6,7},{7,6},{8,9},{9,8},{10,11... | collective-permute-start | bytes 393224 | tf_op jit(solution)/shard_map/ppermute | solution.py:299
  148.0 4.8 %collective-permute-start.41 = (bf16[256,256]{1,0:T(8,128)(2,1)}, bf16[256,256]{1,0:T(8,128)(2,1)}, u32[]{:S(2)}, u32[]{:S(2)}) collective-permute-start(bf16[256,256]{1,0:T(8,128)(2,1)} %collective-permute-done.37.refs_2_), channel_id=1, source_target_pairs={{0,1},{1,0},{2,3},{3,2},{4,5},{5,4},{6,7},{7,6},{8,9},{9,8},{10,11... | collective-permute-start | bytes 393224 | tf_op jit(solution)/shard_map/ppermute | solution.py:299
  (18 other events, 53.9 us)

commit v4 on v3

--- a/solution.py
+++ b/solution.py
@@ -99,7 +99,7 @@
         grid_spec=pltpu.PrefetchScalarGridSpec(
             num_scalar_prefetch=1,
             grid=(1,),
-            in_specs=[pl.BlockSpec(memory_space=pltpu.HBM)],
+            in_specs=[pl.BlockSpec(memory_space=pl.ANY)],
             out_specs=[pl.BlockSpec((half * width, rows), lambda j, at_ref: (0, 0))] * 2,
             scratch_shapes=[pltpu.VMEM(array.shape, array.dtype), pltpu.SemaphoreType.DMA],
         ),
@@ -107,7 +107,11 @@
         compiler_params=params(),
         cost_estimate=cost(0, 4 * rows * many * width),
         name="turn",
-    )(at, array)
+    )(at, pinned(array))
+
+
+def pinned(x):
+    return pltpu.with_memory_space_constraint(x, pltpu.HBM)
 
 
 def call(kernel, scalars, arrays, outs, scratch, *, flops, moved, name, aliases=None, in_hbm=0):
@@ -117,7 +121,7 @@
         grid_spec=pltpu.PrefetchScalarGridSpec(
             num_scalar_prefetch=1,
             grid=(),
-            in_specs=[pl.BlockSpec(memory_space=pltpu.HBM)] * in_hbm + [anywhere] * (len(arrays) - in_hbm),
+            in_specs=[anywhere] * len(arrays),
             out_specs=[anywhere] * len(outs),
             scratch_shapes=scratch,
         ),
@@ -126,7 +130,7 @@
         compiler_params=params(),
         cost_estimate=cost(flops, moved),
         name=name,
-    )(scalars, *arrays)
+    )(scalars, *[pinned(x) for x in arrays[:in_hbm]], *arrays[in_hbm:])
 
 
 def project(activations, sibling, slots, at, blocks, before):
@@ -134,7 +138,7 @@
     (depth, cols), rows = blocks[0][0].shape, activations.shape[0]
     copies = many * (2 + chunks)
     flat = [block for chunk in blocks for block in chunk]
-    held = before or []
+    held = [] if before is None else [before]
 
     def kernel(at_ref, own_ref, *refs):
         sib_refs, refs = refs[: len(sibling)], refs[len(sibling) :]
@@ -152,9 +156,8 @@
             for source, target in moves:
                 started.append(pltpu.make_async_copy(source, target, sems.at[len(started)]))
                 started[-1].start()
-        for i in range(len(held)):
-            target = total.at[:, pl.ds(i * cols, cols)]
-            started.append(pltpu.make_async_copy(refs[chunks * many + i], target, sems.at[len(started)]))
+        if held:
+            started.append(pltpu.make_async_copy(refs[chunks * many], total, sems.at[len(started)]))
             started[-1].start()
         for copy in started:
             copy.wait()
@@ -236,32 +239,35 @@
     )(own, sibling, held)
 
 
-def back(arrays, blocks, projector_t, at, rows, cols, rows_in_all, before):
-    many, chunks = len(blocks), len(blocks[0])
+def back(groups, projector_t, at, rows, rows_in_all, before):
+    many, chunks, cols = at.shape[0], len(groups[0]), groups[0][0].shape[1]
     rank, width = projector_t.shape
+    arrays = [x for group in groups for x in group]
     held = [] if before is None else [before]
     slots = min(4, many)
 
     def kernel(at_ref, projector_ref, *refs):
         array_refs, out_ref = refs[: len(arrays)], refs[len(arrays) + len(held)]
         p, d, o, in_sems, out_sems = refs[len(arrays) + len(held) + 1 :]
-        p_copy = pltpu.make_async_copy(projector_ref, p, in_sems.at[many * chunks])
-        p_copy.start()
-        loads, stores = [], []
+        loads, stores, waits = [pltpu.make_async_copy(projector_ref, p, in_sems.at[len(arrays)])], [], {}
+        start = 0
+        for g, group in enumerate(groups):
+            size = group[0].shape[0]
+            for i in range(chunks):
+                target = d.at[pl.ds(start, size), pl.ds(i * cols, cols)]
+                loads.append(pltpu.make_async_copy(array_refs[g * chunks + i], target, in_sems.at[g * chunks + i]))
+            waits[start // rows] = loads[-chunks:]
+            start += size
+        for copy in loads:
+            copy.start()
+        loads[0].wait()
         for j in range(many):
-            for i in range(chunks):
-                n = j * chunks + i
-                which, start = blocks[j][i]
-                source = array_refs[which].at[pl.ds(start, rows), :]
-                loads.append(pltpu.make_async_copy(source, d.at[j, :, pl.ds(i * cols, cols)], in_sems.at[n]))
-                loads[-1].start()
-        p_copy.wait()
-        for j in range(many):
-            for i in range(chunks):
-                loads[j * chunks + i].wait()
+            for copy in waits.get(j, []):
+                copy.wait()
             if j >= slots:
                 stores[j - slots].wait()
-            o[j % slots] = jnp.dot(d[j], p[...], preferred_element_type=F32).astype(BF16)
+            block = d[j * rows : (j + 1) * rows, :]
+            o[j % slots] = jnp.dot(block, p[...], preferred_element_type=F32).astype(BF16)
             target = out_ref.at[pl.ds(pl.multiple_of(at_ref[j] * rows, rows), rows), :]
             stores.append(pltpu.make_async_copy(o.at[j % slots], target, out_sems.at[j % slots]))
             stores[-1].start()
@@ -275,9 +281,9 @@
         [jax.ShapeDtypeStruct((rows_in_all, width), BF16)],
         [
             pltpu.VMEM((rank, width), BF16),
-            pltpu.VMEM((many, rows, rank), BF16),
+            pltpu.VMEM((many * rows, rank), BF16),
             pltpu.VMEM((slots, rows, width), BF16),
-            pltpu.SemaphoreType.DMA((many * chunks + 1,)),
+            pltpu.SemaphoreType.DMA((len(arrays) + 1,)),
             pltpu.SemaphoreType.DMA((slots,)),
         ],
         flops=2 * many * rows * width * rank,
@@ -327,7 +333,7 @@
         return line, across
 
     after = lambda x, *those: lax.optimization_barrier((x, *those))[0]
-    ks = sorted(range(1, nz), key=lambda k: -min(k, nz - k))
+    ks = list(range(nz - 2, 0, -1)) + [nz - 1]
     depth, rank = projector.shape
     width = first_moment.shape[0]
     cols = rank // CHUNKS
@@ -342,69 +348,60 @@
     slots = [(j // half, j % half) for j in range(len(order_in))]
     made = {}
 
+    def ready(line, across, i, low, high):
+        return [(across if n % 2 else line)[i][n // 2] for n in range(low, high)]
+
     def beside_projector(step, i, line, across):
         if (step, i) == (1, 1):
-            made["a0"] = take(activations, after(at_sibling[:half], line[0][1]), depth)
+            made["a0"] = take(activations, after(at_sibling[:half], line[1][1]), depth)
             return [made["a0"]]
         if (step, i) == (2, 0):
-            made["a1"] = take(activations, after(at_sibling[half:], line[1][1]), depth)
+            made["a1"] = take(activations, after(at_sibling[half:], line[0][2]), depth)
+            made["a"] = [swap_core(made["a0"]), swap_core(made["a1"])]
             return [made["a1"]]
         if (step, i) == (2, 1):
-            made["own"], other = turn(out_grads, after(at_out, line[0][2]), width)
-            made["other"] = other
-            return [made["own"], other]
+            made["own"], made["other"] = turn(out_grads, after(at_out, line[1][2]), width)
+            return [made["own"], made["other"]]
         if (step, i) == (nz - 1, 0):
-            made["pt"] = after(projector, line[1][2]).T
-            made["a"] = [swap_core(made["a0"]), swap_core(made["a1"])]
-            return [made["pt"]]
-        if (step, i) == (nz - 1, 1):
-            ready = [line[0][n // 2] if n % 2 == 0 else across[0][n // 2] for n in range(last)]
-            made["p0"] = project(activations, made["a"], slots[:last], at_in[:last], [ready], None)
-            return [made["p0"]]
+            blocks = [ready(line, across, n, 0, soon) for n in range(CHUNKS)]
+            made["early"] = project(activations, made["a"], slots[:soon], after(at_in[:soon], line[0][nz - 1]), blocks, None)
+            return [made["early"]]
         return []
 
+    soon = last - 2
     line, across = gather([projector[:, part] for part in parts], beside_projector)
     g_own, g_sibling = made["own"], swap_core(made["other"])
-    ready = [line[1][n // 2] if n % 2 == 0 else across[1][n // 2] for n in range(last)]
-    made["p1"] = project(activations, made["a"], slots[:last], at_in[:last], [ready], None)
-    mine = project(
-        activations, made["a"], slots[last:], at_in[last:], [[across[0][-1]], [across[1][-1]]], [made["p0"], made["p1"]]
-    )
+    middle = [ready(line, across, i, soon, last) for i in range(CHUNKS)]
+    middle = project(activations, made["a"], slots[soon:last], at_in[soon:last], middle, made["early"])
+    ends = [ready(line, across, i, last, last + 1) for i in range(CHUNKS)]
+    mine = project(activations, made["a"], slots[last:], at_in[last:], ends, middle)
 
     held, send = outer_first(g_own, g_sibling, mine, swap_core(mine), width)
     sends = [send] + list(outer(g_own, g_sibling, held, width, 1, nz - 1, BF16))
     keeps = list(outer(g_own, g_sibling, held, width, nz, nz, F32))
-    reduced = None
-    for at, k in enumerate(ks + [0]):
-        term = keeps[at] + swap_y(sends[at]).astype(F32)
-        if k:
-            term = shift_z(term.astype(BF16), k).astype(F32)
-        reduced = term if reduced is None else reduced + term
+    terms = [keep + swap_y(send).astype(F32) for keep, send in zip(keeps, sends)]
+    passed = terms[0]
+    for term in terms[1 : nz - 2]:
+        passed = term + shift_z(passed.astype(BF16), 1).astype(F32)
+    reduced = terms[nz - 1] + shift_z(terms[nz - 2].astype(BF16), nz - 1).astype(F32) + shift_z(passed.astype(BF16), 1).astype(F32)
     new_first, new_second, direction = adam(reduced, first_moment, second_moment)
+    projector_t = after(projector, terms[0]).T
 
     def beside_direction(step, i, line, across):
         if step == nz // 2 or step == nz - 1:
-            low = 0 if step == nz // 2 else half
-            high = half if step == nz // 2 else last
-            group = [line[i][n // 2] if n % 2 == 0 else across[i][n // 2] for n in range(low, high)]
-            made["group", low, i] = jnp.concatenate(group, axis=0)
-            made["swapped", low, i] = swap_core(made["group", low, i])
+            low, high = (0, half) if step == nz // 2 else (half, last)
+            made[low, i] = jnp.concatenate(ready(line, across, i, low, high), axis=0)
+            made["swapped", low, i] = swap_core(made[low, i])
         return []
 
     line, across = gather([direction[:, part] for part in parts], beside_direction)
-    update = None
-    for low, high in ((0, half), (half, last + 1)):
-        arrays, blocks = [], []
-        for name in ("group", "swapped"):
-            base = len(arrays)
-            arrays += [made[name, low, i] for i in range(CHUNKS)]
-            blocks += [[(base + i, (n - low) * width) for i in range(CHUNKS)] for n in range(low, min(high, last))]
-            if high > last:
-                ends = [across[i][-1] for i in range(CHUNKS)]
-                arrays += [swap_core(x) for x in ends] if name == "swapped" else ends
-                blocks += [[(base + CHUNKS + i, 0) for i in range(CHUNKS)]]
-        at = named([(k, dy, dc) for dc in (0, 1) for k, dy in order_in[low:high]])
-        update = back(arrays, blocks, made["pt"], at, width, cols, 4 * nz * width, update)
+    chunks = range(CHUNKS)
+    at_back = [named([(k, dy, dc) for dc in (0, 1) for k, dy in order]) for order in (order_in[:half], order_in[half:])]
+    groups = [[made[0, i] for i in chunks], [made["swapped", 0, i] for i in chunks]]
+    update = back(groups, projector_t, at_back[0], width, 4 * nz * width, None)
+    ends = [across[i][-1] for i in chunks]
+    groups = [[made[half, i] for i in chunks], ends, [made["swapped", half, i] for i in chunks], [swap_core(x) for x in ends]]
+    update = back(groups, projector_t, at_back[1], width, 4 * nz * width, update)
     return update, new_first, new_second
 
 

time: 157 us -> 242 us (1.54)
  Pallas kernels: 25.8 us -> 124 us
  local copies, waits for them, and re-layouts: 20.1 us -> 6.04 us
    pallas_call x7, Pallas kernels: 20.5 us -> 117 us  [call(): pl.pallas_call(kernel, grid_spec=pltpu.PrefetchScalarGridSpec(num_scalar_...]
    unnamed x46 -> x30, local copies, waits for them, and re-layouts: 16.7 us -> 3.33 us
    ppermute x17, waiting for transfers between devices: 28.4 us -> 32.1 us  [shift_z(): return lax.ppermute(x, 'dp', pairs(lambda a, b, c: ((a + k) % nz, b, c)))]
  transfers between devices with their start and end apart: 45 -> 45, of which waited for: 21 -> 24; matrix products, arithmetic and copies ran while one was open for 2% -> 1% of each run, Pallas kernels for 12% -> 49%
where the time goes in v4:
time: 242 us; the launch traced here: 241 us
  Pallas kernels  124 us (51%)
  waiting for transfers between devices  73.2 us (30%)
  starting transfers between devices  35.3 us (15%)
  local copies, waits for them, and re-layouts  6.04 us (2%)
    pallas_call x7, Pallas kernels, call(): pl.pallas_call(kernel, grid_spec=pltpu.PrefetchScalarGridSpec(num_scalar_...  117 us
    ppermute x18, waiting for transfers between devices, swap_y(): return lax.ppermute(x, 'dp', pairs(lambda a, b, c: (a, 1 - b, c)))  37.8 us
    ppermute x17, waiting for transfers between devices, shift_z(): return lax.ppermute(x, 'dp', pairs(lambda a, b, c: ((a + k) % nz, b, c)))  32.1 us
    ppermute x18, starting transfers between devices, swap_y(): return lax.ppermute(x, 'dp', pairs(lambda a, b, c: (a, 1 - b, c)))  19.5 us
    ppermute x17, starting transfers between devices, shift_z(): return lax.ppermute(x, 'dp', pairs(lambda a, b, c: ((a + k) % nz, b, c)))  14.5 us
  transfers between devices with their start and end apart: 45, of which 24 were waited for; matrix products, arithmetic and copies ran while one was open for 1% of the time, Pallas kernels for 49%

profile of v4, /device:TPU:0, one launch (start us, length us, event | category | flops | bytes accessed | tf_op | source)
XLA Modules:
  0.0 241.4 jit_solution(12864557060184168748)
XLA Ops:
  1.7 3.0 %collective-permute-start.6 = (bf16[512,256]{1,0:T(8,128)(2,1)S(1)}, bf16[512,256]{1,0:T(8,128)(2,1)S(1)}, u32[]{:S(2)}, u32[]{:S(2)}) collective-permute-start(bf16[512,256]{1,0:T(8,128)(2,1)S(1)} %get-tuple-element.76.refs_2_), channel_id=1, source_target_pairs={{0,2},{1,3},{2,0},{3,1},{4,6},{5,7},{6,4},{7,5},{8,10},{9,11},{10,... | collective-permute-start | bytes 786440 | tf_op jit(solution)/shard_map/ppermute | solution.py:308
  4.7 1.6 collective-permute-start.5
  6.3 1.6 collective-permute-start
  7.9 3.2 %collective-permute-done.6.refs_3_ = bf16[512,256]{1,0:T(8,128)(2,1)S(1)} collective-permute-done((bf16[512,256]{1,0:T(8,128)(2,1)S(1)}, bf16[512,256]{1,0:T(8,128)(2,1)S(1)}, u32[]{:S(2)}, u32[]{:S(2)}) %collective-permute-start.6) | collective-permute-done | bytes 262176 | tf_op jit(solution)/shard_map/ppermute | solution.py:308
  11.0 4.7 %collective-permute-done.5.refs_4_ = bf16[512,256]{1,0:T(8,128)(2,1)S(1)} collective-permute-done((bf16[512,256]{1,0:T(8,128)(2,1)S(1)}, bf16[512,256]{1,0:T(8,128)(2,1)S(1)}, u32[]{:S(2)}, u32[]{:S(2)}) %collective-permute-start.5) | collective-permute-done | bytes 262176 | tf_op jit(solution)/shard_map/ppermute | solution.py:311
  15.9 5.6 %collective-permute-done.refs_9_ = bf16[512,256]{1,0:T(8,128)(2,1)} collective-permute-done((bf16[512,256]{1,0:T(8,128)(2,1)S(1)}, bf16[512,256]{1,0:T(8,128)(2,1)}, u32[]{:S(2)}, u32[]{:S(2)}) %collective-permute-start) | collective-permute-done | bytes 262176 | tf_op jit(solution)/shard_map/ppermute | solution.py:311
  21.5 49.3 %take.2 = bf16[384,2048]{1,0:T(8,128)(2,1)} custom-call(s32[4]{0:T(128)S(1)} %pad_add_fusion.at_ref, bf16[384,8192]{1,0:T(8,128)(2,1)} %own_ref.5), custom_call_target="tpu_custom_call" | custom-call | bytes 3145728 | tf_op jit(solution)/shard_map/take/pallas_call | solution.py:119
  70.9 49.3 %take.3 = bf16[384,2048]{1,0:T(8,128)(2,1)} custom-call(s32[4]{0:T(128)S(1)} %pad_add_fusion.1.at_ref, bf16[384,8192]{1,0:T(8,128)(2,1)} %own_ref.5), custom_call_target="tpu_custom_call" | custom-call | bytes 3145728 | tf_op jit(solution)/shard_map/take/pallas_call | solution.py:119
  121.1 1.8 collective-permute-start.9
  122.8 7.2 %collective-permute-done.1.refs_8_ = bf16[512,256]{1,0:T(8,128)(2,1)} collective-permute-done((bf16[512,256]{1,0:T(8,128)(2,1)S(1)}, bf16[512,256]{1,0:T(8,128)(2,1)}, u32[]{:S(2)}, u32[]{:S(2)}) %collective-permute-start.1) | collective-permute-done | bytes 262176 | tf_op jit(solution)/shard_map/ppermute | solution.py:308
  130.4 5.2 %collective-permute-done.9.refs_5_ = bf16[512,256]{1,0:T(8,128)(2,1)S(1)} collective-permute-done((bf16[512,256]{1,0:T(8,128)(2,1)S(1)}, bf16[512,256]{1,0:T(8,128)(2,1)S(1)}, u32[]{:S(2)}, u32[]{:S(2)}) %collective-permute-start.9) | collective-permute-done | bytes 262176 | tf_op jit(solution)/shard_map/ppermute | solution.py:308
  136.3 2.5 %collective-permute-done.2.refs_11_ = bf16[512,256]{1,0:T(8,128)(2,1)} collective-permute-done((bf16[512,256]{1,0:T(8,128)(2,1)}, bf16[512,256]{1,0:T(8,128)(2,1)}, u32[]{:S(2)}, u32[]{:S(2)}) %collective-permute-start.2) | collective-permute-done | bytes 262176 | tf_op jit(solution)/shard_map/ppermute | solution.py:311
  139.3 3.3 %turn.1 = (bf16[2048,384]{1,0:T(8,128)(2,1)S(1)}, bf16[2048,384]{1,0:T(8,128)(2,1)S(1)}) custom-call(s32[16]{0:T(128)S(1)} %stack.148.at_ref, bf16[384,4096]{1,0:T(8,128)(2,1)} %in_ref.4), custom_call_target="tpu_custom_call" | custom-call | bytes 6291456 | tf_op jit(solution)/shard_map/turn/pallas_call | solution.py:97
  142.7 1.3 collective-permute-start.14
  144.0 3.0 %collective-permute-done.10.refs_3_ = bf16[512,256]{1,0:T(8,128)(2,1)} collective-permute-done((bf16[512,256]{1,0:T(8,128)(2,1)}, bf16[512,256]{1,0:T(8,128)(2,1)}, u32[]{:S(2)}, u32[]{:S(2)}) %collective-permute-start.10) | collective-permute-done | bytes 262176 | tf_op jit(solution)/shard_map/ppermute | solution.py:311
  147.0 5.1 %project.3.refs_6_ = f32[768,512]{1,0:T(8,128)S(1)} custom-call(s32[5]{0:T(128)S(1)} %stack.155.at_ref, bf16[384,8192]{1,0:T(8,128)(2,1)} %own_ref.5, bf16[384,2048]{1,0:T(8,128)(2,1)S(1)} %collective-permute-done.4.refs_0_, bf16[384,2048]{1,0:T(8,128)(2,1)} %collective-permute-done.8.refs_1_, bf16[512,256]{1,0:T(8,128)(2,1)S(1)} %get-tuple-element.76.refs_2_, ...), custom_call_target="tpu_custom_call" | custom-call | flops 2013265920 | bytes 8126464 | tf_op jit(solution)/shard_map/project/pallas_call | solution.py:119
  152.1 1.1 copy-done
  153.3 2.0 collective-permute-start.13
  156.3 1.4 copy-done.1
  157.7 3.4 %project.4.refs_4_ = f32[768,512]{1,0:T(8,128)S(1)} custom-call(s32[2]{0:T(128)S(1)} %pad_add_fusion.2.at_ref, bf16[384,8192]{1,0:T(8,128)(2,1)} %own_ref.5, bf16[384,2048]{1,0:T(8,128)(2,1)S(1)} %collective-permute-done.4.refs_0_, bf16[384,2048]{1,0:T(8,128)(2,1)} %collective-permute-done.8.refs_1_, bf16[512,256]{1,0:T(8,128)(2,1)} %collective-permute-done.11.refs_2_, ...), custom_call_target="tpu_custom_call" | custom-call | flops 805306368 | bytes 4194304 | tf_op jit(solution)/shard_map/project/pallas_call | solution.py:119
  161.2 1.9 project.5.mine_ref
  163.2 3.4 %collective-permute-done.17.theirs_ref = f32[768,512]{1,0:T(8,128)S(1)} collective-permute-done((f32[768,512]{1,0:T(8,128)S(1)}, f32[768,512]{1,0:T(8,128)S(1)}, u32[]{:S(2)}, u32[]{:S(2)}) %collective-permute-start.17) | collective-permute-done | bytes 1572896 | tf_op jit(solution)/shard_map/ppermute | solution.py:305
  167.1 1.2 collective-permute-start.18
  168.3 1.3 outer.3
  171.7 1.8 outer.2
  173.5 2.8 %collective-permute-done.18 = bf16[256,512]{1,0:T(8,128)(2,1)S(1)} collective-permute-done((bf16[256,512]{1,0:T(8,128)(2,1)S(1)}, bf16[256,512]{1,0:T(8,128)(2,1)S(1)}, u32[]{:S(2)}, u32[]{:S(2)}) %collective-permute-start.18) | collective-permute-done | bytes 262176 | tf_op jit(solution)/shard_map/ppermute | solution.py:308
  176.4 1.4 collective-permute-start.19
  177.9 4.0 %collective-permute-done.20 = bf16[256,512]{1,0:T(8,128)(2,1)S(1)} collective-permute-done((bf16[256,512]{1,0:T(8,128)(2,1)S(1)}, bf16[256,512]{1,0:T(8,128)(2,1)S(1)}, u32[]{:S(2)}, u32[]{:S(2)}) %collective-permute-start.20) | collective-permute-done | bytes 262176 | tf_op jit(solution)/shard_map/ppermute | solution.py:308
  182.0 3.0 %collective-permute-start.21 = (bf16[256,512]{1,0:T(8,128)(2,1)S(1)}, bf16[256,512]{1,0:T(8,128)(2,1)S(1)}, u32[]{:S(2)}, u32[]{:S(2)}) collective-permute-start(bf16[256,512]{1,0:T(8,128)(2,1)S(1)} %add_convert_fusion.1), channel_id=1, source_target_pairs={{0,12},{1,13},{2,14},{3,15},{4,0},{5,1},{6,2},{7,3},{8,4},{9,5},{1... | collective-permute-start | bytes 786440 | tf_op jit(solution)/shard_map/ppermute | solution.py:311
  185.0 2.5 %collective-permute-done.22 = bf16[256,512]{1,0:T(8,128)(2,1)S(1)} collective-permute-done((bf16[256,512]{1,0:T(8,128)(2,1)S(1)}, bf16[256,512]{1,0:T(8,128)(2,1)S(1)}, u32[]{:S(2)}, u32[]{:S(2)}) %collective-permute-start.22) | collective-permute-done | bytes 262176 | tf_op jit(solution)/shard_map/ppermute | solution.py:308
  187.7 4.6 %collective-permute-done.19 = bf16[256,512]{1,0:T(8,128)(2,1)S(1)} collective-permute-done((bf16[256,512]{1,0:T(8,128)(2,1)S(1)}, bf16[256,512]{1,0:T(8,128)(2,1)S(1)}, u32[]{:S(2)}, u32[]{:S(2)}) %collective-permute-start.19) | collective-permute-done | bytes 262176 | tf_op jit(solution)/shard_map/ppermute | solution.py:308
  192.3 3.9 %collective-permute-done.24 = bf16[256,512]{1,0:T(8,128)(2,1)S(1)} collective-permute-done((bf16[256,512]{1,0:T(8,128)(2,1)S(1)}, bf16[256,512]{1,0:T(8,128)(2,1)S(1)}, u32[]{:S(2)}, u32[]{:S(2)}) %collective-permute-start.24) | collective-permute-done | bytes 262176 | tf_op jit(solution)/shard_map/ppermute | solution.py:311
  196.3 1.4 divide_convert_fusion
  197.7 1.2 collective-permute-start.32
  198.8 1.6 collective-permute-start.31
  201.4 1.4 collective-permute-start.25
  202.9 1.1 collective-permute-done.32
  204.0 2.4 collective-permute-done.31
  206.4 1.1 collective-permute-start.34
  210.3 2.7 %collective-permute-start.38 = (bf16[256,256]{1,0:T(8,128)(2,1)S(1)}, bf16[256,256]{1,0:T(8,128)(2,1)S(1)}, u32[]{:S(2)}, u32[]{:S(2)}) collective-permute-start(bf16[256,256]{1,0:T(8,128)(2,1)S(1)} %collective-permute-done.32), channel_id=1, source_target_pairs={{0,12},{1,13},{2,14},{3,15},{4,0},{5,1},{6,2},{7,3},{8,4},{9,5},{1... | collective-permute-start | bytes 393224 | tf_op jit(solution)/shard_map/ppermute | solution.py:311
  213.0 2.7 %collective-permute-done.33 = bf16[256,256]{1,0:T(8,128)(2,1)S(1)} collective-permute-done((bf16[256,256]{1,0:T(8,128)(2,1)S(1)}, bf16[256,256]{1,0:T(8,128)(2,1)S(1)}, u32[]{:S(2)}, u32[]{:S(2)}) %collective-permute-start.33) | collective-permute-done | bytes 131104 | tf_op jit(solution)/shard_map/ppermute | solution.py:311
  216.7 2.0 collective-permute-done.27
  220.8 2.0 collective-permute-done.36
  223.7 1.8 collective-permute-done.30
  226.5 5.1 %collective-permute-done.37.refs_2_ = bf16[256,256]{1,0:T(8,128)(2,1)} collective-permute-done((bf16[256,256]{1,0:T(8,128)(2,1)S(1)}, bf16[256,256]{1,0:T(8,128)(2,1)}, u32[]{:S(2)}, u32[]{:S(2)}) %collective-permute-start.37) | collective-permute-done | bytes 131104 | tf_op jit(solution)/shard_map/ppermute | solution.py:308
  232.3 1.3 copy.9
  233.5 3.7 %back.2.refs_8_ = bf16[4096,512]{1,0:T(8,128)(2,1)} custom-call(s32[8]{0:T(128)S(1)} %stack.157.at_ref, bf16[512,512]{1,0:T(8,128)(2,1)S(1)} %bitcast.29, bf16[1024,256]{1,0:T(8,128)(2,1)S(1)} %pad_maximum_fusion.refs_0_, bf16[1024,256]{1,0:T(8,128)(2,1)S(1)} %pad_maximum_fusion.1.refs_1_, bf16[1024,256]{1,0:T(8,128)(2,1)S(1)} %collective-permute-done.43.refs_2_, ...), custom_call_target="tpu_custom_call" | custom-call | flops 1073741824 | bytes 4194304 | tf_op jit(solution)/shard_map/back/pallas_call | solution.py:119
  237.3 3.9 %back.3 = bf16[4096,512]{1,0:T(8,128)(2,1)} custom-call(s32[8]{0:T(128)S(1)} %stack.131.at_ref, bf16[512,512]{1,0:T(8,128)(2,1)S(1)} %bitcast.30, bf16[768,256]{1,0:T(8,128)(2,1)S(1)} %constant_dynamic-update-slice_fusion.refs_0_, bf16[768,256]{1,0:T(8,128)(2,1)S(1)} %constant_dynamic-update-slice_fusion.3.refs_1_, ...), custom_call_target="tpu_custom_call", output_to_operand_aliasing={{}: (10, {})} | custom-call | flops 1073741824 | bytes 4194304 | tf_op jit(solution)/shard_map/back/pallas_call | solution.py:119
  (101 shorter events, 17.1 us)
Async XLA Ops:
  1.7 119.1 %copy-start.2 = (bf16[512,256]{1,0:T(8,128)(2,1)}, bf16[512,256]{1,0:T(8,128)(2,1)S(1)}, u32[]{:S(2)}) copy-start(bf16[512,256]{1,0:T(8,128)(2,1)S(1)} %get-tuple-element.77.refs_7_) | copy-start | bytes 786436
  1.7 9.3 %collective-permute-start.6 = (bf16[512,256]{1,0:T(8,128)(2,1)S(1)}, bf16[512,256]{1,0:T(8,128)(2,1)S(1)}, u32[]{:S(2)}, u32[]{:S(2)}) collective-permute-start(bf16[512,256]{1,0:T(8,128)(2,1)S(1)} %get-tuple-element.76.refs_2_), channel_id=1, source_target_pairs={{0,2},{1,3},{2,0},{3,1},{4,6},{5,7},{6,4},{7,5},{8,10},{9,11},{10,... | collective-permute-start | bytes 786440 | tf_op jit(solution)/shard_map/ppermute | solution.py:308
  4.7 11.0 %collective-permute-start.5 = (bf16[512,256]{1,0:T(8,128)(2,1)S(1)}, bf16[512,256]{1,0:T(8,128)(2,1)S(1)}, u32[]{:S(2)}, u32[]{:S(2)}) collective-permute-start(bf16[512,256]{1,0:T(8,128)(2,1)S(1)} %get-tuple-element.76.refs_2_), channel_id=1, source_target_pairs={{0,4},{1,5},{2,6},{3,7},{4,8},{5,9},{6,10},{7,11},{8,12},{9,13},{1... | collective-permute-start | bytes 786440 | tf_op jit(solution)/shard_map/ppermute | solution.py:311
  6.3 15.2 %collective-permute-start = (bf16[512,256]{1,0:T(8,128)(2,1)S(1)}, bf16[512,256]{1,0:T(8,128)(2,1)}, u32[]{:S(2)}, u32[]{:S(2)}) collective-permute-start(bf16[512,256]{1,0:T(8,128)(2,1)S(1)} %get-tuple-element.77.refs_7_), channel_id=1, source_target_pairs={{0,4},{1,5},{2,6},{3,7},{4,8},{5,9},{6,10},{7,11},{8,12},{9,13},{1... | collective-permute-start | bytes 786440 | tf_op jit(solution)/shard_map/ppermute | solution.py:311
  11.0 59.8 %copy-start.4 = (bf16[512,256]{1,0:T(8,128)(2,1)}, bf16[512,256]{1,0:T(8,128)(2,1)S(1)}, u32[]{:S(2)}) copy-start(bf16[512,256]{1,0:T(8,128)(2,1)S(1)} %collective-permute-done.6.refs_3_) | copy-start | bytes 786436
  15.8 105.3 %copy-start.6 = (bf16[512,256]{1,0:T(8,128)(2,1)}, bf16[512,256]{1,0:T(8,128)(2,1)S(1)}, u32[]{:S(2)}) copy-start(bf16[512,256]{1,0:T(8,128)(2,1)S(1)} %collective-permute-done.5.refs_4_) | copy-start | bytes 786436
  15.8 55.1 %collective-permute-start.7 = (bf16[512,256]{1,0:T(8,128)(2,1)S(1)}, bf16[512,256]{1,0:T(8,128)(2,1)}, u32[]{:S(2)}, u32[]{:S(2)}) collective-permute-start(bf16[512,256]{1,0:T(8,128)(2,1)S(1)} %collective-permute-done.5.refs_4_), channel_id=1, source_target_pairs={{0,4},{1,5},{2,6},{3,7},{4,8},{5,9},{6,10},{7,11},{8,12},{9,13},{1... | collective-permute-start | bytes 786440 | tf_op jit(solution)/shard_map/ppermute | solution.py:311
  70.8 76.1 %collective-permute-start.4 = (bf16[384,2048]{1,0:T(8,128)(2,1)}, bf16[384,2048]{1,0:T(8,128)(2,1)S(1)}, u32[]{:S(2)}, u32[]{:S(2)}) collective-permute-start(bf16[384,2048]{1,0:T(8,128)(2,1)} %take.2), channel_id=1, source_target_pairs={{0,1},{1,0},{2,3},{3,2},{4,5},{5,4},{6,7},{7,6},{8,9},{9,8},{10,11... | collective-permute-start | bytes 4718600 | tf_op jit(solution)/shard_map/ppermute | solution.py:305
  120.3 26.7 %collective-permute-start.8 = (bf16[384,2048]{1,0:T(8,128)(2,1)}, bf16[384,2048]{1,0:T(8,128)(2,1)}, u32[]{:S(2)}, u32[]{:S(2)}) collective-permute-start(bf16[384,2048]{1,0:T(8,128)(2,1)} %take.3), channel_id=1, source_target_pairs={{0,1},{1,0},{2,3},{3,2},{4,5},{5,4},{6,7},{7,6},{8,9},{9,8},{10,11... | collective-permute-start | bytes 4718600 | tf_op jit(solution)/shard_map/ppermute | solution.py:305
  120.8 9.3 %collective-permute-start.1 = (bf16[512,256]{1,0:T(8,128)(2,1)S(1)}, bf16[512,256]{1,0:T(8,128)(2,1)}, u32[]{:S(2)}, u32[]{:S(2)}) collective-permute-start(bf16[512,256]{1,0:T(8,128)(2,1)S(1)} %get-tuple-element.77.refs_7_), channel_id=1, source_target_pairs={{0,2},{1,3},{2,0},{3,1},{4,6},{5,7},{6,4},{7,5},{8,10},{9,11},{10,... | collective-permute-start | bytes 786440 | tf_op jit(solution)/shard_map/ppermute | solution.py:308
  121.1 14.5 %collective-permute-start.9 = (bf16[512,256]{1,0:T(8,128)(2,1)S(1)}, bf16[512,256]{1,0:T(8,128)(2,1)S(1)}, u32[]{:S(2)}, u32[]{:S(2)}) collective-permute-start(bf16[512,256]{1,0:T(8,128)(2,1)S(1)} %collective-permute-done.5.refs_4_), channel_id=1, source_target_pairs={{0,2},{1,3},{2,0},{3,1},{4,6},{5,7},{6,4},{7,5},{8,10},{9,11},{10,... | collective-permute-start | bytes 786440 | tf_op jit(solution)/shard_map/ppermute | solution.py:308
  130.1 8.7 %collective-permute-start.2 = (bf16[512,256]{1,0:T(8,128)(2,1)}, bf16[512,256]{1,0:T(8,128)(2,1)}, u32[]{:S(2)}, u32[]{:S(2)}) collective-permute-start(bf16[512,256]{1,0:T(8,128)(2,1)} %collective-permute-done.refs_9_), channel_id=1, source_target_pairs={{0,4},{1,5},{2,6},{3,7},{4,8},{5,9},{6,10},{7,11},{8,12},{9,13},{1... | collective-permute-start | bytes 786440 | tf_op jit(solution)/shard_map/ppermute | solution.py:311
  130.1 12.6 %collective-permute-start.12 = (bf16[512,256]{1,0:T(8,128)(2,1)}, bf16[512,256]{1,0:T(8,128)(2,1)}, u32[]{:S(2)}, u32[]{:S(2)}) collective-permute-start(bf16[512,256]{1,0:T(8,128)(2,1)} %collective-permute-done.refs_9_), channel_id=1, source_target_pairs={{0,2},{1,3},{2,0},{3,1},{4,6},{5,7},{6,4},{7,5},{8,10},{9,11},{10,... | collective-permute-start | bytes 786440 | tf_op jit(solution)/shard_map/ppermute | solution.py:308
  136.3 10.6 %collective-permute-start.10 = (bf16[512,256]{1,0:T(8,128)(2,1)}, bf16[512,256]{1,0:T(8,128)(2,1)}, u32[]{:S(2)}, u32[]{:S(2)}) collective-permute-start(bf16[512,256]{1,0:T(8,128)(2,1)} %collective-permute-done.7.refs_6_), channel_id=1, source_target_pairs={{0,4},{1,5},{2,6},{3,7},{4,8},{5,9},{6,10},{7,11},{8,12},{9,13},{1... | collective-permute-start | bytes 786440 | tf_op jit(solution)/shard_map/ppermute | solution.py:311
  138.8 14.5 %collective-permute-start.11 = (bf16[512,256]{1,0:T(8,128)(2,1)}, bf16[512,256]{1,0:T(8,128)(2,1)}, u32[]{:S(2)}, u32[]{:S(2)}) collective-permute-start(bf16[512,256]{1,0:T(8,128)(2,1)} %collective-permute-done.7.refs_6_), channel_id=1, source_target_pairs={{0,2},{1,3},{2,0},{3,1},{4,6},{5,7},{6,4},{7,5},{8,10},{9,11},{10,... | collective-permute-start | bytes 786440 | tf_op jit(solution)/shard_map/ppermute | solution.py:308
  142.7 18.5 %collective-permute-start.14 = (bf16[512,256]{1,0:T(8,128)(2,1)}, bf16[512,256]{1,0:T(8,128)(2,1)}, u32[]{:S(2)}, u32[]{:S(2)}) collective-permute-start(bf16[512,256]{1,0:T(8,128)(2,1)} %collective-permute-done.1.refs_8_), channel_id=1, source_target_pairs={{0,12},{1,13},{2,14},{3,15},{4,0},{5,1},{6,2},{7,3},{8,4},{9,5},{1... | collective-permute-start | bytes 786440 | tf_op jit(solution)/shard_map/ppermute | solution.py:311
  146.9 8.4 %collective-permute-start.16 = (bf16[512,256]{1,0:T(8,128)(2,1)}, bf16[512,256]{1,0:T(8,128)(2,1)}, u32[]{:S(2)}, u32[]{:S(2)}) collective-permute-start(bf16[512,256]{1,0:T(8,128)(2,1)} %collective-permute-done.2.refs_11_), channel_id=1, source_target_pairs={{0,2},{1,3},{2,0},{3,1},{4,6},{5,7},{6,4},{7,5},{8,10},{9,11},{10,... | collective-permute-start | bytes 786440 | tf_op jit(solution)/shard_map/ppermute | solution.py:308
  146.9 9.4 %collective-permute-start.15 = (bf16[512,256]{1,0:T(8,128)(2,1)}, bf16[512,256]{1,0:T(8,128)(2,1)}, u32[]{:S(2)}, u32[]{:S(2)}) collective-permute-start(bf16[512,256]{1,0:T(8,128)(2,1)} %collective-permute-done.2.refs_11_), channel_id=1, source_target_pairs={{0,4},{1,5},{2,6},{3,7},{4,8},{5,9},{6,10},{7,11},{8,12},{9,13},{1... | collective-permute-start | bytes 786440 | tf_op jit(solution)/shard_map/ppermute | solution.py:311
  153.3 7.9 %collective-permute-start.13 = (bf16[512,256]{1,0:T(8,128)(2,1)}, bf16[512,256]{1,0:T(8,128)(2,1)S(1)}, u32[]{:S(2)}, u32[]{:S(2)}) collective-permute-start(bf16[512,256]{1,0:T(8,128)(2,1)} %collective-permute-done.10.refs_3_), channel_id=1, source_target_pairs={{0,2},{1,3},{2,0},{3,1},{4,6},{5,7},{6,4},{7,5},{8,10},{9,11},{10,... | collective-permute-start | bytes 786440 | tf_op jit(solution)/shard_map/ppermute | solution.py:308
  155.4 7.8 %collective-permute-start.3 = (bf16[2048,384]{1,0:T(8,128)(2,1)}, bf16[2048,384]{1,0:T(8,128)(2,1)S(1)}, u32[]{:S(2)}, u32[]{:S(2)}) collective-permute-start(bf16[2048,384]{1,0:T(8,128)(2,1)} %copy-done.10), channel_id=1, source_target_pairs={{0,1},{1,0},{2,3},{3,2},{4,5},{5,4},{6,7},{7,6},{8,9},{9,8},{10,11... | collective-permute-start | bytes 4718600 | tf_op jit(solution)/shard_map/ppermute | solution.py:305
  163.1 3.5 %collective-permute-start.17 = (f32[768,512]{1,0:T(8,128)S(1)}, f32[768,512]{1,0:T(8,128)S(1)}, u32[]{:S(2)}, u32[]{:S(2)}) collective-permute-start(f32[768,512]{1,0:T(8,128)S(1)} %project.5.mine_ref), channel_id=1, source_target_pairs={{0,1},{1,0},{2,3},{3,2},{4,5},{5,4},{6,7},{7,6},{8,9},{9,8},{10,11... | collective-permute-start | bytes 4718600 | tf_op jit(solution)/shard_map/ppermute | solution.py:305
  167.1 9.2 %collective-permute-start.18 = (bf16[256,512]{1,0:T(8,128)(2,1)S(1)}, bf16[256,512]{1,0:T(8,128)(2,1)S(1)}, u32[]{:S(2)}, u32[]{:S(2)}) collective-permute-start(bf16[256,512]{1,0:T(8,128)(2,1)S(1)} %get-tuple-element.58), channel_id=1, source_target_pairs={{0,2},{1,3},{2,0},{3,1},{4,6},{5,7},{6,4},{7,5},{8,10},{9,11},{10,... | collective-permute-start | bytes 786440 | tf_op jit(solution)/shard_map/ppermute | solution.py:308
  169.6 12.3 %collective-permute-start.20 = (bf16[256,512]{1,0:T(8,128)(2,1)S(1)}, bf16[256,512]{1,0:T(8,128)(2,1)S(1)}, u32[]{:S(2)}, u32[]{:S(2)}) collective-permute-start(bf16[256,512]{1,0:T(8,128)(2,1)S(1)} %get-tuple-element.63), channel_id=1, source_target_pairs={{0,2},{1,3},{2,0},{3,1},{4,6},{5,7},{6,4},{7,5},{8,10},{9,11},{10,... | collective-permute-start | bytes 786440 | tf_op jit(solution)/shard_map/ppermute | solution.py:308
  170.6 16.9 %collective-permute-start.22 = (bf16[256,512]{1,0:T(8,128)(2,1)S(1)}, bf16[256,512]{1,0:T(8,128)(2,1)S(1)}, u32[]{:S(2)}, u32[]{:S(2)}) collective-permute-start(bf16[256,512]{1,0:T(8,128)(2,1)S(1)} %get-tuple-element.65), channel_id=1, source_target_pairs={{0,2},{1,3},{2,0},{3,1},{4,6},{5,7},{6,4},{7,5},{8,10},{9,11},{10,... | collective-permute-start | bytes 786440 | tf_op jit(solution)/shard_map/ppermute | solution.py:308
  176.4 11.2 %collective-permute-start.23 = (bf16[256,512]{1,0:T(8,128)(2,1)S(1)}, bf16[256,512]{1,0:T(8,128)(2,1)S(1)}, u32[]{:S(2)}, u32[]{:S(2)}) collective-permute-start(bf16[256,512]{1,0:T(8,128)(2,1)S(1)} %convert_add_fusion.1), channel_id=1, source_target_pairs={{0,4},{1,5},{2,6},{3,7},{4,8},{5,9},{6,10},{7,11},{8,12},{9,13},{1... | collective-permute-start | bytes 786440 | tf_op jit(solution)/shard_map/ppermute | solution.py:311
  176.4 15.9 %collective-permute-start.19 = (bf16[256,512]{1,0:T(8,128)(2,1)S(1)}, bf16[256,512]{1,0:T(8,128)(2,1)S(1)}, u32[]{:S(2)}, u32[]{:S(2)}) collective-permute-start(bf16[256,512]{1,0:T(8,128)(2,1)S(1)} %get-tuple-element.61), channel_id=1, source_target_pairs={{0,2},{1,3},{2,0},{3,1},{4,6},{5,7},{6,4},{7,5},{8,10},{9,11},{10,... | collective-permute-start | bytes 786440 | tf_op jit(solution)/shard_map/ppermute | solution.py:308
  182.0 10.4 %collective-permute-start.21 = (bf16[256,512]{1,0:T(8,128)(2,1)S(1)}, bf16[256,512]{1,0:T(8,128)(2,1)S(1)}, u32[]{:S(2)}, u32[]{:S(2)}) collective-permute-start(bf16[256,512]{1,0:T(8,128)(2,1)S(1)} %add_convert_fusion.1), channel_id=1, source_target_pairs={{0,12},{1,13},{2,14},{3,15},{4,0},{5,1},{6,2},{7,3},{8,4},{9,5},{1... | collective-permute-start | bytes 786440 | tf_op jit(solution)/shard_map/ppermute | solution.py:311
  187.6 8.6 %collective-permute-start.24 = (bf16[256,512]{1,0:T(8,128)(2,1)S(1)}, bf16[256,512]{1,0:T(8,128)(2,1)S(1)}, u32[]{:S(2)}, u32[]{:S(2)}) collective-permute-start(bf16[256,512]{1,0:T(8,128)(2,1)S(1)} %add_convert_fusion), channel_id=1, source_target_pairs={{0,4},{1,5},{2,6},{3,7},{4,8},{5,9},{6,10},{7,11},{8,12},{9,13},{1... | collective-permute-start | bytes 786440 | tf_op jit(solution)/shard_map/ppermute | solution.py:311
  197.7 6.3 %collective-permute-start.32 = (bf16[256,256]{1,0:T(8,128)(2,1)S(1)}, bf16[256,256]{1,0:T(8,128)(2,1)S(1)}, u32[]{:S(2)}, u32[]{:S(2)}) collective-permute-start(bf16[256,256]{1,0:T(8,128)(2,1)S(1)} %get-tuple-element.78), channel_id=1, source_target_pairs={{0,2},{1,3},{2,0},{3,1},{4,6},{5,7},{6,4},{7,5},{8,10},{9,11},{10,... | collective-permute-start | bytes 393224 | tf_op jit(solution)/shard_map/ppermute | solution.py:308
  198.8 7.6 %collective-permute-start.31 = (bf16[256,256]{1,0:T(8,128)(2,1)S(1)}, bf16[256,256]{1,0:T(8,128)(2,1)S(1)}, u32[]{:S(2)}, u32[]{:S(2)}) collective-permute-start(bf16[256,256]{1,0:T(8,128)(2,1)S(1)} %get-tuple-element.78), channel_id=1, source_target_pairs={{0,4},{1,5},{2,6},{3,7},{4,8},{5,9},{6,10},{7,11},{8,12},{9,13},{1... | collective-permute-start | bytes 393224 | tf_op jit(solution)/shard_map/ppermute | solution.py:311
  200.4 7.1 %collective-permute-start.26 = (bf16[256,256]{1,0:T(8,128)(2,1)S(1)}, bf16[256,256]{1,0:T(8,128)(2,1)S(1)}, u32[]{:S(2)}, u32[]{:S(2)}) collective-permute-start(bf16[256,256]{1,0:T(8,128)(2,1)S(1)} %get-tuple-element.79), channel_id=1, source_target_pairs={{0,2},{1,3},{2,0},{3,1},{4,6},{5,7},{6,4},{7,5},{8,10},{9,11},{10,... | collective-permute-start | bytes 393224 | tf_op jit(solution)/shard_map/ppermute | solution.py:308
  201.4 6.8 %collective-permute-start.25 = (bf16[256,256]{1,0:T(8,128)(2,1)S(1)}, bf16[256,256]{1,0:T(8,128)(2,1)S(1)}, u32[]{:S(2)}, u32[]{:S(2)}) collective-permute-start(bf16[256,256]{1,0:T(8,128)(2,1)S(1)} %get-tuple-element.79), channel_id=1, source_target_pairs={{0,4},{1,5},{2,6},{3,7},{4,8},{5,9},{6,10},{7,11},{8,12},{9,13},{1... | collective-permute-start | bytes 393224 | tf_op jit(solution)/shard_map/ppermute | solution.py:311
  206.4 6.6 %collective-permute-start.34 = (bf16[256,256]{1,0:T(8,128)(2,1)S(1)}, bf16[256,256]{1,0:T(8,128)(2,1)S(1)}, u32[]{:S(2)}, u32[]{:S(2)}) collective-permute-start(bf16[256,256]{1,0:T(8,128)(2,1)S(1)} %collective-permute-done.31), channel_id=1, source_target_pairs={{0,2},{1,3},{2,0},{3,1},{4,6},{5,7},{6,4},{7,5},{8,10},{9,11},{10,... | collective-permute-start | bytes 393224 | tf_op jit(solution)/shard_map/ppermute | solution.py:308
  207.5 8.2 %collective-permute-start.33 = (bf16[256,256]{1,0:T(8,128)(2,1)S(1)}, bf16[256,256]{1,0:T(8,128)(2,1)S(1)}, u32[]{:S(2)}, u32[]{:S(2)}) collective-permute-start(bf16[256,256]{1,0:T(8,128)(2,1)S(1)} %collective-permute-done.31), channel_id=1, source_target_pairs={{0,4},{1,5},{2,6},{3,7},{4,8},{5,9},{6,10},{7,11},{8,12},{9,13},{1... | collective-permute-start | bytes 393224 | tf_op jit(solution)/shard_map/ppermute | solution.py:311
  208.2 8.6 %collective-permute-start.28 = (bf16[256,256]{1,0:T(8,128)(2,1)S(1)}, bf16[256,256]{1,0:T(8,128)(2,1)S(1)}, u32[]{:S(2)}, u32[]{:S(2)}) collective-permute-start(bf16[256,256]{1,0:T(8,128)(2,1)S(1)} %collective-permute-done.25), channel_id=1, source_target_pairs={{0,2},{1,3},{2,0},{3,1},{4,6},{5,7},{6,4},{7,5},{8,10},{9,11},{10,... | collective-permute-start | bytes 393224 | tf_op jit(solution)/shard_map/ppermute | solution.py:308
  209.2 9.5 %collective-permute-start.27 = (bf16[256,256]{1,0:T(8,128)(2,1)S(1)}, bf16[256,256]{1,0:T(8,128)(2,1)S(1)}, u32[]{:S(2)}, u32[]{:S(2)}) collective-permute-start(bf16[256,256]{1,0:T(8,128)(2,1)S(1)} %collective-permute-done.25), channel_id=1, source_target_pairs={{0,4},{1,5},{2,6},{3,7},{4,8},{5,9},{6,10},{7,11},{8,12},{9,13},{1... | collective-permute-start | bytes 393224 | tf_op jit(solution)/shard_map/ppermute | solution.py:311
  210.3 15.2 %collective-permute-start.38 = (bf16[256,256]{1,0:T(8,128)(2,1)S(1)}, bf16[256,256]{1,0:T(8,128)(2,1)S(1)}, u32[]{:S(2)}, u32[]{:S(2)}) collective-permute-start(bf16[256,256]{1,0:T(8,128)(2,1)S(1)} %collective-permute-done.32), channel_id=1, source_target_pairs={{0,12},{1,13},{2,14},{3,15},{4,0},{5,1},{6,2},{7,3},{8,4},{9,5},{1... | collective-permute-start | bytes 393224 | tf_op jit(solution)/shard_map/ppermute | solution.py:311
  215.8 7.0 %collective-permute-start.36 = (bf16[256,256]{1,0:T(8,128)(2,1)S(1)}, bf16[256,256]{1,0:T(8,128)(2,1)S(1)}, u32[]{:S(2)}, u32[]{:S(2)}) collective-permute-start(bf16[256,256]{1,0:T(8,128)(2,1)S(1)} %collective-permute-done.33), channel_id=1, source_target_pairs={{0,4},{1,5},{2,6},{3,7},{4,8},{5,9},{6,10},{7,11},{8,12},{9,13},{1... | collective-permute-start | bytes 393224 | tf_op jit(solution)/shard_map/ppermute | solution.py:311
  215.8 5.0 %collective-permute-start.35 = (bf16[256,256]{1,0:T(8,128)(2,1)S(1)}, bf16[256,256]{1,0:T(8,128)(2,1)S(1)}, u32[]{:S(2)}, u32[]{:S(2)}) collective-permute-start(bf16[256,256]{1,0:T(8,128)(2,1)S(1)} %collective-permute-done.33), channel_id=1, source_target_pairs={{0,2},{1,3},{2,0},{3,1},{4,6},{5,7},{6,4},{7,5},{8,10},{9,11},{10,... | collective-permute-start | bytes 393224 | tf_op jit(solution)/shard_map/ppermute | solution.py:308
  218.7 6.8 %collective-permute-start.30 = (bf16[256,256]{1,0:T(8,128)(2,1)S(1)}, bf16[256,256]{1,0:T(8,128)(2,1)S(1)}, u32[]{:S(2)}, u32[]{:S(2)}) collective-permute-start(bf16[256,256]{1,0:T(8,128)(2,1)S(1)} %collective-permute-done.27), channel_id=1, source_target_pairs={{0,4},{1,5},{2,6},{3,7},{4,8},{5,9},{6,10},{7,11},{8,12},{9,13},{1... | collective-permute-start | bytes 393224 | tf_op jit(solution)/shard_map/ppermute | solution.py:311
  218.7 5.0 %collective-permute-start.29 = (bf16[256,256]{1,0:T(8,128)(2,1)S(1)}, bf16[256,256]{1,0:T(8,128)(2,1)S(1)}, u32[]{:S(2)}, u32[]{:S(2)}) collective-permute-start(bf16[256,256]{1,0:T(8,128)(2,1)S(1)} %collective-permute-done.27), channel_id=1, source_target_pairs={{0,2},{1,3},{2,0},{3,1},{4,6},{5,7},{6,4},{7,5},{8,10},{9,11},{10,... | collective-permute-start | bytes 393224 | tf_op jit(solution)/shard_map/ppermute | solution.py:308
  220.8 10.8 %collective-permute-start.44 = (bf16[1024,256]{1,0:T(8,128)(2,1)S(1)}, bf16[1024,256]{1,0:T(8,128)(2,1)S(1)}, u32[]{:S(2)}, u32[]{:S(2)}) collective-permute-start(bf16[1024,256]{1,0:T(8,128)(2,1)S(1)} %pad_maximum_fusion.1.refs_1_), channel_id=1, source_target_pairs={{0,1},{1,0},{2,3},{3,2},{4,5},{5,4},{6,7},{7,6},{8,9},{9,8},{10,11... | collective-permute-start | bytes 1572872 | tf_op jit(solution)/shard_map/ppermute | solution.py:305
  222.7 10.8 %collective-permute-start.43 = (bf16[1024,256]{1,0:T(8,128)(2,1)S(1)}, bf16[1024,256]{1,0:T(8,128)(2,1)S(1)}, u32[]{:S(2)}, u32[]{:S(2)}) collective-permute-start(bf16[1024,256]{1,0:T(8,128)(2,1)S(1)} %pad_maximum_fusion.refs_0_), channel_id=1, source_target_pairs={{0,1},{1,0},{2,3},{3,2},{4,5},{5,4},{6,7},{7,6},{8,9},{9,8},{10,11... | collective-permute-start | bytes 1572872 | tf_op jit(solution)/shard_map/ppermute | solution.py:305
  223.7 13.6 %collective-permute-start.40 = (bf16[768,256]{1,0:T(8,128)(2,1)S(1)}, bf16[768,256]{1,0:T(8,128)(2,1)}, u32[]{:S(2)}, u32[]{:S(2)}) collective-permute-start(bf16[768,256]{1,0:T(8,128)(2,1)S(1)} %constant_dynamic-update-slice_fusion.3.refs_1_), channel_id=1, source_target_pairs={{0,1},{1,0},{2,3},{3,2},{4,5},{5,4},{6,7},{7,6},{8,9},{9,8},{10,11... | collective-permute-start | bytes 1179656 | tf_op jit(solution)/shard_map/ppermute | solution.py:305
  225.5 11.8 %collective-permute-start.39 = (bf16[768,256]{1,0:T(8,128)(2,1)S(1)}, bf16[768,256]{1,0:T(8,128)(2,1)}, u32[]{:S(2)}, u32[]{:S(2)}) collective-permute-start(bf16[768,256]{1,0:T(8,128)(2,1)S(1)} %constant_dynamic-update-slice_fusion.refs_0_), channel_id=1, source_target_pairs={{0,1},{1,0},{2,3},{3,2},{4,5},{5,4},{6,7},{7,6},{8,9},{9,8},{10,11... | collective-permute-start | bytes 1179656 | tf_op jit(solution)/shard_map/ppermute | solution.py:305
  225.6 6.0 %collective-permute-start.37 = (bf16[256,256]{1,0:T(8,128)(2,1)S(1)}, bf16[256,256]{1,0:T(8,128)(2,1)}, u32[]{:S(2)}, u32[]{:S(2)}) collective-permute-start(bf16[256,256]{1,0:T(8,128)(2,1)S(1)} %collective-permute-done.30), channel_id=1, source_target_pairs={{0,2},{1,3},{2,0},{3,1},{4,6},{5,7},{6,4},{7,5},{8,10},{9,11},{10,... | collective-permute-start | bytes 393224 | tf_op jit(solution)/shard_map/ppermute | solution.py:308
  231.6 5.7 %collective-permute-start.42 = (bf16[256,256]{1,0:T(8,128)(2,1)S(1)}, bf16[256,256]{1,0:T(8,128)(2,1)}, u32[]{:S(2)}, u32[]{:S(2)}) collective-permute-start(bf16[256,256]{1,0:T(8,128)(2,1)S(1)} %collective-permute-done.38.refs_3_), channel_id=1, source_target_pairs={{0,1},{1,0},{2,3},{3,2},{4,5},{5,4},{6,7},{7,6},{8,9},{9,8},{10,11... | collective-permute-start | bytes 393224 | tf_op jit(solution)/shard_map/ppermute | solution.py:305
  231.6 5.7 %collective-permute-start.41 = (bf16[256,256]{1,0:T(8,128)(2,1)}, bf16[256,256]{1,0:T(8,128)(2,1)}, u32[]{:S(2)}, u32[]{:S(2)}) collective-permute-start(bf16[256,256]{1,0:T(8,128)(2,1)} %collective-permute-done.37.refs_2_), channel_id=1, source_target_pairs={{0,1},{1,0},{2,3},{3,2},{4,5},{5,4},{6,7},{7,6},{8,9},{9,8},{10,11... | collective-permute-start | bytes 393224 | tf_op jit(solution)/shard_map/ppermute | solution.py:305
  (10 other events, 78.2 us)

commit v5 on v4

--- a/solution.py
+++ b/solution.py
@@ -68,17 +68,20 @@
         for copy in copies:
             copy.wait()
 
-    return call(
-        kernel,
-        at,
-        [array],
-        [jax.ShapeDtypeStruct((rows, many * width), array.dtype)],
-        [pltpu.SemaphoreType.DMA((many,))],
-        flops=0,
-        moved=4 * rows * many * width,
+    return pl.pallas_call(
+        kernel,
+        grid_spec=pltpu.PrefetchScalarGridSpec(
+            num_scalar_prefetch=1,
+            grid=(1,),
+            in_specs=[pl.BlockSpec(memory_space=pl.ANY)],
+            out_specs=pl.BlockSpec((rows, many * width), lambda j, at_ref: (0, 0)),
+            scratch_shapes=[pltpu.SemaphoreType.DMA((many,))],
+        ),
+        out_shape=jax.ShapeDtypeStruct((rows, many * width), array.dtype),
+        compiler_params=params(),
+        cost_estimate=cost(0, 4 * rows * many * width),
         name="take",
-        in_hbm=1,
-    )[0]
+    )(at, pinned(array))
 
 
 def turn(array, at, width):
@@ -392,7 +395,7 @@
             low, high = (0, half) if step == nz // 2 else (half, last)
             made[low, i] = jnp.concatenate(ready(line, across, i, low, high), axis=0)
             made["swapped", low, i] = swap_core(made[low, i])
-        return []
+        return [projector_t] if (step, i) == (1, 1) else []
 
     line, across = gather([direction[:, part] for part in parts], beside_direction)
     chunks = range(CHUNKS)
@@ -400,7 +403,7 @@
     groups = [[made[0, i] for i in chunks], [made["swapped", 0, i] for i in chunks]]
     update = back(groups, projector_t, at_back[0], width, 4 * nz * width, None)
     ends = [across[i][-1] for i in chunks]
-    groups = [[made[half, i] for i in chunks], ends, [made["swapped", half, i] for i in chunks], [swap_core(x) for x in ends]]
+    groups = [[made[half, i] for i in chunks], ends, [made["swapped", half, i] for i in chunks], [swap_core(after(x, update)) for x in ends]]
     update = back(groups, projector_t, at_back[1], width, 4 * nz * width, update)
     return update, new_first, new_second
 

time: 242 us -> 147 us (0.61)
  Pallas kernels: 124 us -> 31.2 us
  waiting for transfers between devices: 73.2 us -> 70.7 us
    pallas_call x7 -> x5, Pallas kernels: 117 us -> 18.1 us  [call(): pl.pallas_call(kernel, grid_spec=pltpu.PrefetchScalarGridSpec(num_scalar_...]
    pallas_call x0 -> x2, Pallas kernels: none -> 6.19 us  [take(): pl.pallas_call(kernel, grid_spec=pltpu.PrefetchScalarGridSpec(num_scalar_...]
    ppermute x18, waiting for transfers between devices: 37.8 us -> 32.4 us  [swap_y(): return lax.ppermute(x, 'dp', pairs(lambda a, b, c: (a, 1 - b, c)))]
  transfers between devices with their start and end apart: 45 -> 45, of which waited for: 24 -> 26; matrix products, arithmetic and copies ran while one was open for 1% -> 2% of each run, Pallas kernels for 49% -> 18%
where the time goes in v5:
time: 147 us; the launch traced here: 146 us
  waiting for transfers between devices  70.7 us (48%)
  starting transfers between devices  34.6 us (24%)
  Pallas kernels  31.2 us (21%)
  local copies, waits for them, and re-layouts  5.89 us (4%)
  other arithmetic  2.85 us (2%)
    ppermute x17, waiting for transfers between devices, shift_z(): return lax.ppermute(x, 'dp', pairs(lambda a, b, c: ((a + k) % nz, b, c)))  33.8 us
    ppermute x18, waiting for transfers between devices, swap_y(): return lax.ppermute(x, 'dp', pairs(lambda a, b, c: (a, 1 - b, c)))  32.4 us
    ppermute x18, starting transfers between devices, swap_y(): return lax.ppermute(x, 'dp', pairs(lambda a, b, c: (a, 1 - b, c)))  19.7 us
    pallas_call x5, Pallas kernels, call(): pl.pallas_call(kernel, grid_spec=pltpu.PrefetchScalarGridSpec(num_scalar_...  18.1 us
    ppermute x17, starting transfers between devices, shift_z(): return lax.ppermute(x, 'dp', pairs(lambda a, b, c: ((a + k) % nz, b, c)))  13.4 us
    pallas_call x2, Pallas kernels, take(): pl.pallas_call(kernel, grid_spec=pltpu.PrefetchScalarGridSpec(num_scalar_...  6.19 us
    ppermute x10, waiting for transfers between devices, swap_core(): return lax.ppermute(x, 'dp', pairs(lambda a, b, c: (a, b, 1 - c)))  4.51 us
    unnamed x32, local copies, waits for them, and re-layouts  3.33 us
  transfers between devices with their start and end apart: 45, of which 26 were waited for; matrix products, arithmetic and copies ran while one was open for 2% of the time, Pallas kernels for 18%

profile of v5, /device:TPU:0, one launch (start us, length us, event | category | flops | bytes accessed | tf_op | source)
XLA Modules:
  0.0 146.5 jit_solution(7326581611809747642)
XLA Ops:
  0.6 1.1 fusion.2
  1.7 3.0 %collective-permute-start.6 = (bf16[512,256]{1,0:T(8,128)(2,1)S(1)}, bf16[512,256]{1,0:T(8,128)(2,1)S(1)}, u32[]{:S(2)}, u32[]{:S(2)}) collective-permute-start(bf16[512,256]{1,0:T(8,128)(2,1)S(1)} %get-tuple-element.80.refs_2_), channel_id=1, source_target_pairs={{0,2},{1,3},{2,0},{3,1},{4,6},{5,7},{6,4},{7,5},{8,10},{9,11},{10,... | collective-permute-start | bytes 786440 | tf_op jit(solution)/shard_map/ppermute | solution.py:311
  4.7 1.6 %collective-permute-start.5 = (bf16[512,256]{1,0:T(8,128)(2,1)S(1)}, bf16[512,256]{1,0:T(8,128)(2,1)S(1)}, u32[]{:S(2)}, u32[]{:S(2)}) collective-permute-start(bf16[512,256]{1,0:T(8,128)(2,1)S(1)} %get-tuple-element.80.refs_2_), channel_id=1, source_target_pairs={{0,4},{1,5},{2,6},{3,7},{4,8},{5,9},{6,10},{7,11},{8,12},{9,13},{1... | collective-permute-start | bytes 786440 | tf_op jit(solution)/shard_map/ppermute | solution.py:314
  6.3 1.6 %collective-permute-start = (bf16[512,256]{1,0:T(8,128)(2,1)S(1)}, bf16[512,256]{1,0:T(8,128)(2,1)}, u32[]{:S(2)}, u32[]{:S(2)}) collective-permute-start(bf16[512,256]{1,0:T(8,128)(2,1)S(1)} %get-tuple-element.81.refs_7_), channel_id=1, source_target_pairs={{0,4},{1,5},{2,6},{3,7},{4,8},{5,9},{6,10},{7,11},{8,12},{9,13},{1... | collective-permute-start | bytes 786440 | tf_op jit(solution)/shard_map/ppermute | solution.py:314
  7.9 3.2 %collective-permute-done.6.refs_3_ = bf16[512,256]{1,0:T(8,128)(2,1)S(1)} collective-permute-done((bf16[512,256]{1,0:T(8,128)(2,1)S(1)}, bf16[512,256]{1,0:T(8,128)(2,1)S(1)}, u32[]{:S(2)}, u32[]{:S(2)}) %collective-permute-start.6) | collective-permute-done | bytes 262176 | tf_op jit(solution)/shard_map/ppermute | solution.py:311
  11.0 4.7 %collective-permute-done.5.refs_4_ = bf16[512,256]{1,0:T(8,128)(2,1)S(1)} collective-permute-done((bf16[512,256]{1,0:T(8,128)(2,1)S(1)}, bf16[512,256]{1,0:T(8,128)(2,1)S(1)}, u32[]{:S(2)}, u32[]{:S(2)}) %collective-permute-start.5) | collective-permute-done | bytes 262176 | tf_op jit(solution)/shard_map/ppermute | solution.py:314
  15.9 5.6 %collective-permute-done.refs_9_ = bf16[512,256]{1,0:T(8,128)(2,1)} collective-permute-done((bf16[512,256]{1,0:T(8,128)(2,1)S(1)}, bf16[512,256]{1,0:T(8,128)(2,1)}, u32[]{:S(2)}, u32[]{:S(2)}) %collective-permute-start) | collective-permute-done | bytes 262176 | tf_op jit(solution)/shard_map/ppermute | solution.py:314
  21.5 3.1 %take.2 = bf16[384,2048]{1,0:T(8,128)(2,1)} custom-call(s32[4]{0:T(128)S(1)} %pad_add_fusion.at_ref, bf16[384,8192]{1,0:T(8,128)(2,1)} %own_ref.5), custom_call_target="tpu_custom_call" | custom-call | bytes 3145728 | tf_op jit(solution)/shard_map/take/pallas_call | solution.py:71
  25.7 3.1 %take.3 = bf16[384,2048]{1,0:T(8,128)(2,1)} custom-call(s32[4]{0:T(128)S(1)} %pad_add_fusion.1.at_ref, bf16[384,8192]{1,0:T(8,128)(2,1)} %own_ref.5), custom_call_target="tpu_custom_call" | custom-call | bytes 3145728 | tf_op jit(solution)/shard_map/take/pallas_call | solution.py:71
  29.5 1.5 %collective-permute-start.9 = (bf16[512,256]{1,0:T(8,128)(2,1)S(1)}, bf16[512,256]{1,0:T(8,128)(2,1)S(1)}, u32[]{:S(2)}, u32[]{:S(2)}) collective-permute-start(bf16[512,256]{1,0:T(8,128)(2,1)S(1)} %collective-permute-done.5.refs_4_), channel_id=1, source_target_pairs={{0,2},{1,3},{2,0},{3,1},{4,6},{5,7},{6,4},{7,5},{8,10},{9,11},{10,... | collective-permute-start | bytes 786440 | tf_op jit(solution)/shard_map/ppermute | solution.py:311
  31.0 7.2 %collective-permute-done.1.refs_8_ = bf16[512,256]{1,0:T(8,128)(2,1)} collective-permute-done((bf16[512,256]{1,0:T(8,128)(2,1)S(1)}, bf16[512,256]{1,0:T(8,128)(2,1)}, u32[]{:S(2)}, u32[]{:S(2)}) %collective-permute-start.1) | collective-permute-done | bytes 262176 | tf_op jit(solution)/shard_map/ppermute | solution.py:311
  38.7 5.0 %collective-permute-done.9.refs_5_ = bf16[512,256]{1,0:T(8,128)(2,1)S(1)} collective-permute-done((bf16[512,256]{1,0:T(8,128)(2,1)S(1)}, bf16[512,256]{1,0:T(8,128)(2,1)S(1)}, u32[]{:S(2)}, u32[]{:S(2)}) %collective-permute-start.9) | collective-permute-done | bytes 262176 | tf_op jit(solution)/shard_map/ppermute | solution.py:311
  44.4 3.3 %collective-permute-done.2.refs_11_ = bf16[512,256]{1,0:T(8,128)(2,1)} collective-permute-done((bf16[512,256]{1,0:T(8,128)(2,1)}, bf16[512,256]{1,0:T(8,128)(2,1)}, u32[]{:S(2)}, u32[]{:S(2)}) %collective-permute-start.2) | collective-permute-done | bytes 262176 | tf_op jit(solution)/shard_map/ppermute | solution.py:314
  48.4 3.3 %turn.1 = (bf16[2048,384]{1,0:T(8,128)(2,1)S(1)}, bf16[2048,384]{1,0:T(8,128)(2,1)S(1)}) custom-call(s32[16]{0:T(128)S(1)} %stack.148.at_ref, bf16[384,4096]{1,0:T(8,128)(2,1)} %in_ref.4), custom_call_target="tpu_custom_call" | custom-call | bytes 6291456 | tf_op jit(solution)/shard_map/turn/pallas_call | solution.py:100
  52.3 3.3 %collective-permute-done.10.refs_3_ = bf16[512,256]{1,0:T(8,128)(2,1)} collective-permute-done((bf16[512,256]{1,0:T(8,128)(2,1)}, bf16[512,256]{1,0:T(8,128)(2,1)}, u32[]{:S(2)}, u32[]{:S(2)}) %collective-permute-start.10) | collective-permute-done | bytes 262176 | tf_op jit(solution)/shard_map/ppermute | solution.py:314
  55.7 5.1 %project.3.refs_6_ = f32[768,512]{1,0:T(8,128)S(1)} custom-call(s32[5]{0:T(128)S(1)} %stack.155.at_ref, bf16[384,8192]{1,0:T(8,128)(2,1)} %own_ref.5, bf16[384,2048]{1,0:T(8,128)(2,1)S(1)} %collective-permute-done.4.refs_0_, bf16[384,2048]{1,0:T(8,128)(2,1)} %collective-permute-done.8.refs_1_, bf16[512,256]{1,0:T(8,128)(2,1)S(1)} %get-tuple-element.80.refs_2_, ...), custom_call_target="tpu_custom_call" | custom-call | flops 2013265920 | bytes 8126464 | tf_op jit(solution)/shard_map/project/pallas_call | solution.py:122
  60.8 1.1 copy-done
  61.9 2.0 %collective-permute-start.13 = (bf16[512,256]{1,0:T(8,128)(2,1)}, bf16[512,256]{1,0:T(8,128)(2,1)S(1)}, u32[]{:S(2)}, u32[]{:S(2)}) collective-permute-start(bf16[512,256]{1,0:T(8,128)(2,1)} %collective-permute-done.10.refs_3_), channel_id=1, source_target_pairs={{0,2},{1,3},{2,0},{3,1},{4,6},{5,7},{6,4},{7,5},{8,10},{9,11},{10,... | collective-permute-start | bytes 786440 | tf_op jit(solution)/shard_map/ppermute | solution.py:311
  64.0 1.2 collective-permute-done.15.refs_5_
  65.2 1.4 copy-done.1
  66.6 3.4 %project.4.refs_4_ = f32[768,512]{1,0:T(8,128)S(1)} custom-call(s32[2]{0:T(128)S(1)} %pad_add_fusion.2.at_ref, bf16[384,8192]{1,0:T(8,128)(2,1)} %own_ref.5, bf16[384,2048]{1,0:T(8,128)(2,1)S(1)} %collective-permute-done.4.refs_0_, bf16[384,2048]{1,0:T(8,128)(2,1)} %collective-permute-done.8.refs_1_, bf16[512,256]{1,0:T(8,128)(2,1)} %collective-permute-done.11.refs_2_, ...), custom_call_target="tpu_custom_call" | custom-call | flops 805306368 | bytes 4194304 | tf_op jit(solution)/shard_map/project/pallas_call | solution.py:122
  70.1 1.9 %project.5.mine_ref = f32[768,512]{1,0:T(8,128)S(1)} custom-call(s32[1]{0:T(128)} %bitcast.3.at_ref, bf16[384,8192]{1,0:T(8,128)(2,1)} %own_ref.5, bf16[384,2048]{1,0:T(8,128)(2,1)S(1)} %collective-permute-done.4.refs_0_, bf16[384,2048]{1,0:T(8,128)(2,1)} %collective-permute-done.8.refs_1_, bf16[512,256]{1,0:T(8,128)(2,1)S(1)} %collective-permute-done.13.refs_2_, ...), custom_call_target="tpu_custom_call" | custom-call | flops 402653184 | bytes 2883584 | tf_op jit(solution)/shard_map/project/pallas_call | solution.py:122
  72.1 3.4 %collective-permute-done.17.theirs_ref = f32[768,512]{1,0:T(8,128)S(1)} collective-permute-done((f32[768,512]{1,0:T(8,128)S(1)}, f32[768,512]{1,0:T(8,128)S(1)}, u32[]{:S(2)}, u32[]{:S(2)}) %collective-permute-start.17) | collective-permute-done | bytes 1572896 | tf_op jit(solution)/shard_map/ppermute | solution.py:308
  76.9 1.3 outer.3
  78.3 1.2 collective-permute-start.20
  80.3 1.8 %outer.2 = (f32[256,512]{1,0:T(8,128)S(1)}, f32[256,512]{1,0:T(8,128)S(1)}, f32[256,512]{1,0:T(8,128)S(1)}, f32[256,512]{1,0:T(8,128)S(1)}) custom-call(bf16[2048,384]{1,0:T(8,128)(2,1)S(1)} %get-tuple-element.43.own_ref, bf16[2048,384]{1,0:T(8,128)(2,1)S(1)} %collective-permute-done.3.sib_ref, bf16[768,512]{1,0:T(8,128)(2,1)S(1)} %get-tuple-element.58.held_ref), custom_call_target="tpu_custom_call" | custom-call | flops 805306368 | bytes 3670016 | tf_op jit(solution)/shard_map/outer/pallas_call | solution.py:229
  82.2 3.0 %collective-permute-done.18 = bf16[256,512]{1,0:T(8,128)(2,1)S(1)} collective-permute-done((bf16[256,512]{1,0:T(8,128)(2,1)S(1)}, bf16[256,512]{1,0:T(8,128)(2,1)S(1)}, u32[]{:S(2)}, u32[]{:S(2)}) %collective-permute-start.18) | collective-permute-done | bytes 262176 | tf_op jit(solution)/shard_map/ppermute | solution.py:311
  85.3 1.4 collective-permute-start.19
  86.7 4.1 %collective-permute-done.20 = bf16[256,512]{1,0:T(8,128)(2,1)S(1)} collective-permute-done((bf16[256,512]{1,0:T(8,128)(2,1)S(1)}, bf16[256,512]{1,0:T(8,128)(2,1)S(1)}, u32[]{:S(2)}, u32[]{:S(2)}) %collective-permute-start.20) | collective-permute-done | bytes 262176 | tf_op jit(solution)/shard_map/ppermute | solution.py:311
  90.9 2.7 %collective-permute-start.21 = (bf16[256,512]{1,0:T(8,128)(2,1)S(1)}, bf16[256,512]{1,0:T(8,128)(2,1)S(1)}, u32[]{:S(2)}, u32[]{:S(2)}) collective-permute-start(bf16[256,512]{1,0:T(8,128)(2,1)S(1)} %add_convert_fusion.1), channel_id=1, source_target_pairs={{0,12},{1,13},{2,14},{3,15},{4,0},{5,1},{6,2},{7,3},{8,4},{9,5},{1... | collective-permute-start | bytes 786440 | tf_op jit(solution)/shard_map/ppermute | solution.py:314
  93.6 2.8 %collective-permute-done.22 = bf16[256,512]{1,0:T(8,128)(2,1)S(1)} collective-permute-done((bf16[256,512]{1,0:T(8,128)(2,1)S(1)}, bf16[256,512]{1,0:T(8,128)(2,1)S(1)}, u32[]{:S(2)}, u32[]{:S(2)}) %collective-permute-start.22) | collective-permute-done | bytes 262176 | tf_op jit(solution)/shard_map/ppermute | solution.py:311
  96.6 4.6 %collective-permute-done.19 = bf16[256,512]{1,0:T(8,128)(2,1)S(1)} collective-permute-done((bf16[256,512]{1,0:T(8,128)(2,1)S(1)}, bf16[256,512]{1,0:T(8,128)(2,1)S(1)}, u32[]{:S(2)}, u32[]{:S(2)}) %collective-permute-start.19) | collective-permute-done | bytes 262176 | tf_op jit(solution)/shard_map/ppermute | solution.py:311
  101.2 3.9 %collective-permute-done.24 = bf16[256,512]{1,0:T(8,128)(2,1)S(1)} collective-permute-done((bf16[256,512]{1,0:T(8,128)(2,1)S(1)}, bf16[256,512]{1,0:T(8,128)(2,1)S(1)}, u32[]{:S(2)}, u32[]{:S(2)}) %collective-permute-start.24) | collective-permute-done | bytes 262176 | tf_op jit(solution)/shard_map/ppermute | solution.py:314
  105.1 1.4 divide_convert_fusion
  107.5 1.5 %collective-permute-start.25 = (bf16[256,256]{1,0:T(8,128)(2,1)S(1)}, bf16[256,256]{1,0:T(8,128)(2,1)S(1)}, u32[]{:S(2)}, u32[]{:S(2)}) collective-permute-start(bf16[256,256]{1,0:T(8,128)(2,1)S(1)} %get-tuple-element.83), channel_id=1, source_target_pairs={{0,4},{1,5},{2,6},{3,7},{4,8},{5,9},{6,10},{7,11},{8,12},{9,13},{1... | collective-permute-start | bytes 393224 | tf_op jit(solution)/shard_map/ppermute | solution.py:314
  110.0 1.5 collective-permute-start.31
  111.9 2.9 %collective-permute-done.25 = bf16[256,256]{1,0:T(8,128)(2,1)S(1)} collective-permute-done((bf16[256,256]{1,0:T(8,128)(2,1)S(1)}, bf16[256,256]{1,0:T(8,128)(2,1)S(1)}, u32[]{:S(2)}, u32[]{:S(2)}) %collective-permute-start.25) | collective-permute-done | bytes 131104 | tf_op jit(solution)/shard_map/ppermute | solution.py:314
  117.8 1.2 collective-permute-start.33
  119.7 2.8 %collective-permute-done.27 = bf16[256,256]{1,0:T(8,128)(2,1)S(1)} collective-permute-done((bf16[256,256]{1,0:T(8,128)(2,1)S(1)}, bf16[256,256]{1,0:T(8,128)(2,1)S(1)}, u32[]{:S(2)}, u32[]{:S(2)}) %collective-permute-start.27) | collective-permute-done | bytes 131104 | tf_op jit(solution)/shard_map/ppermute | solution.py:314
  122.5 1.1 collective-permute-start.29
  123.6 2.2 %collective-permute-done.33 = bf16[256,256]{1,0:T(8,128)(2,1)S(1)} collective-permute-done((bf16[256,256]{1,0:T(8,128)(2,1)S(1)}, bf16[256,256]{1,0:T(8,128)(2,1)S(1)}, u32[]{:S(2)}, u32[]{:S(2)}) %collective-permute-start.33) | collective-permute-done | bytes 131104 | tf_op jit(solution)/shard_map/ppermute | solution.py:314
  125.9 1.0 collective-permute-start.35
  130.9 1.8 %collective-permute-done.36 = bf16[256,256]{1,0:T(8,128)(2,1)S(1)} collective-permute-done((bf16[256,256]{1,0:T(8,128)(2,1)S(1)}, bf16[256,256]{1,0:T(8,128)(2,1)S(1)}, u32[]{:S(2)}, u32[]{:S(2)}) %collective-permute-start.36) | collective-permute-done | bytes 131104 | tf_op jit(solution)/shard_map/ppermute | solution.py:314
  132.7 2.3 %collective-permute-start.38 = (bf16[256,256]{1,0:T(8,128)(2,1)}, bf16[256,256]{1,0:T(8,128)(2,1)S(1)}, u32[]{:S(2)}, u32[]{:S(2)}) collective-permute-start(bf16[256,256]{1,0:T(8,128)(2,1)} %collective-permute-done.32), channel_id=1, source_target_pairs={{0,12},{1,13},{2,14},{3,15},{4,0},{5,1},{6,2},{7,3},{8,4},{9,5},{1... | collective-permute-start | bytes 393224 | tf_op jit(solution)/shard_map/ppermute | solution.py:314
  135.0 1.0 collective-permute-start.37
  136.1 3.7 %back.2.refs_8_ = bf16[4096,512]{1,0:T(8,128)(2,1)} custom-call(s32[8]{0:T(128)S(1)} %stack.157.at_ref, bf16[512,512]{1,0:T(8,128)(2,1)S(1)} %bitcast.29, bf16[1024,256]{1,0:T(8,128)(2,1)S(1)} %pad_maximum_fusion.refs_0_, bf16[1024,256]{1,0:T(8,128)(2,1)S(1)} %pad_maximum_fusion.1.refs_1_, bf16[1024,256]{1,0:T(8,128)(2,1)S(1)} %collective-permute-done.41.refs_2_, ...), custom_call_target="tpu_custom_call" | custom-call | flops 1073741824 | bytes 4194304 | tf_op jit(solution)/shard_map/back/pallas_call | solution.py:122
  141.3 1.1 collective-permute-done.43.refs_6_
  142.4 3.9 %back.3 = bf16[4096,512]{1,0:T(8,128)(2,1)} custom-call(s32[8]{0:T(128)S(1)} %stack.131.at_ref, bf16[512,512]{1,0:T(8,128)(2,1)S(1)} %bitcast.30, bf16[768,256]{1,0:T(8,128)(2,1)S(1)} %constant_dynamic-update-slice_fusion.refs_0_, bf16[768,256]{1,0:T(8,128)(2,1)S(1)} %constant_dynamic-update-slice_fusion.3.refs_1_, ...), custom_call_target="tpu_custom_call", output_to_operand_aliasing={{}: (10, {})} | custom-call | flops 1073741824 | bytes 4194304 | tf_op jit(solution)/shard_map/back/pallas_call | solution.py:122
  (103 shorter events, 18.9 us)
Async XLA Ops:
  1.7 27.2 %copy-start.2 = (bf16[512,256]{1,0:T(8,128)(2,1)}, bf16[512,256]{1,0:T(8,128)(2,1)S(1)}, u32[]{:S(2)}) copy-start(bf16[512,256]{1,0:T(8,128)(2,1)S(1)} %get-tuple-element.81.refs_7_) | copy-start | bytes 786436
  1.7 9.3 %collective-permute-start.6 = (bf16[512,256]{1,0:T(8,128)(2,1)S(1)}, bf16[512,256]{1,0:T(8,128)(2,1)S(1)}, u32[]{:S(2)}, u32[]{:S(2)}) collective-permute-start(bf16[512,256]{1,0:T(8,128)(2,1)S(1)} %get-tuple-element.80.refs_2_), channel_id=1, source_target_pairs={{0,2},{1,3},{2,0},{3,1},{4,6},{5,7},{6,4},{7,5},{8,10},{9,11},{10,... | collective-permute-start | bytes 786440 | tf_op jit(solution)/shard_map/ppermute | solution.py:311
  4.7 11.0 %collective-permute-start.5 = (bf16[512,256]{1,0:T(8,128)(2,1)S(1)}, bf16[512,256]{1,0:T(8,128)(2,1)S(1)}, u32[]{:S(2)}, u32[]{:S(2)}) collective-permute-start(bf16[512,256]{1,0:T(8,128)(2,1)S(1)} %get-tuple-element.80.refs_2_), channel_id=1, source_target_pairs={{0,4},{1,5},{2,6},{3,7},{4,8},{5,9},{6,10},{7,11},{8,12},{9,13},{1... | collective-permute-start | bytes 786440 | tf_op jit(solution)/shard_map/ppermute | solution.py:314
  6.3 15.2 %collective-permute-start = (bf16[512,256]{1,0:T(8,128)(2,1)S(1)}, bf16[512,256]{1,0:T(8,128)(2,1)}, u32[]{:S(2)}, u32[]{:S(2)}) collective-permute-start(bf16[512,256]{1,0:T(8,128)(2,1)S(1)} %get-tuple-element.81.refs_7_), channel_id=1, source_target_pairs={{0,4},{1,5},{2,6},{3,7},{4,8},{5,9},{6,10},{7,11},{8,12},{9,13},{1... | collective-permute-start | bytes 786440 | tf_op jit(solution)/shard_map/ppermute | solution.py:314
  15.8 9.9 %collective-permute-start.7 = (bf16[512,256]{1,0:T(8,128)(2,1)S(1)}, bf16[512,256]{1,0:T(8,128)(2,1)}, u32[]{:S(2)}, u32[]{:S(2)}) collective-permute-start(bf16[512,256]{1,0:T(8,128)(2,1)S(1)} %collective-permute-done.5.refs_4_), channel_id=1, source_target_pairs={{0,4},{1,5},{2,6},{3,7},{4,8},{5,9},{6,10},{7,11},{8,12},{9,13},{1... | collective-permute-start | bytes 786440 | tf_op jit(solution)/shard_map/ppermute | solution.py:314
  24.6 31.0 %collective-permute-start.4 = (bf16[384,2048]{1,0:T(8,128)(2,1)}, bf16[384,2048]{1,0:T(8,128)(2,1)S(1)}, u32[]{:S(2)}, u32[]{:S(2)}) collective-permute-start(bf16[384,2048]{1,0:T(8,128)(2,1)} %take.2), channel_id=1, source_target_pairs={{0,1},{1,0},{2,3},{3,2},{4,5},{5,4},{6,7},{7,6},{8,9},{9,8},{10,11... | collective-permute-start | bytes 4718600 | tf_op jit(solution)/shard_map/ppermute | solution.py:308
  28.8 26.8 %collective-permute-start.8 = (bf16[384,2048]{1,0:T(8,128)(2,1)}, bf16[384,2048]{1,0:T(8,128)(2,1)}, u32[]{:S(2)}, u32[]{:S(2)}) collective-permute-start(bf16[384,2048]{1,0:T(8,128)(2,1)} %take.3), channel_id=1, source_target_pairs={{0,1},{1,0},{2,3},{3,2},{4,5},{5,4},{6,7},{7,6},{8,9},{9,8},{10,11... | collective-permute-start | bytes 4718600 | tf_op jit(solution)/shard_map/ppermute | solution.py:308
  28.9 9.3 %collective-permute-start.1 = (bf16[512,256]{1,0:T(8,128)(2,1)S(1)}, bf16[512,256]{1,0:T(8,128)(2,1)}, u32[]{:S(2)}, u32[]{:S(2)}) collective-permute-start(bf16[512,256]{1,0:T(8,128)(2,1)S(1)} %get-tuple-element.81.refs_7_), channel_id=1, source_target_pairs={{0,2},{1,3},{2,0},{3,1},{4,6},{5,7},{6,4},{7,5},{8,10},{9,11},{10,... | collective-permute-start | bytes 786440 | tf_op jit(solution)/shard_map/ppermute | solution.py:311
  29.5 14.2 %collective-permute-start.9 = (bf16[512,256]{1,0:T(8,128)(2,1)S(1)}, bf16[512,256]{1,0:T(8,128)(2,1)S(1)}, u32[]{:S(2)}, u32[]{:S(2)}) collective-permute-start(bf16[512,256]{1,0:T(8,128)(2,1)S(1)} %collective-permute-done.5.refs_4_), channel_id=1, source_target_pairs={{0,2},{1,3},{2,0},{3,1},{4,6},{5,7},{6,4},{7,5},{8,10},{9,11},{10,... | collective-permute-start | bytes 786440 | tf_op jit(solution)/shard_map/ppermute | solution.py:311
  38.2 9.5 %collective-permute-start.2 = (bf16[512,256]{1,0:T(8,128)(2,1)}, bf16[512,256]{1,0:T(8,128)(2,1)}, u32[]{:S(2)}, u32[]{:S(2)}) collective-permute-start(bf16[512,256]{1,0:T(8,128)(2,1)} %collective-permute-done.refs_9_), channel_id=1, source_target_pairs={{0,4},{1,5},{2,6},{3,7},{4,8},{5,9},{6,10},{7,11},{8,12},{9,13},{1... | collective-permute-start | bytes 786440 | tf_op jit(solution)/shard_map/ppermute | solution.py:314
  38.2 13.6 %collective-permute-start.12 = (bf16[512,256]{1,0:T(8,128)(2,1)}, bf16[512,256]{1,0:T(8,128)(2,1)}, u32[]{:S(2)}, u32[]{:S(2)}) collective-permute-start(bf16[512,256]{1,0:T(8,128)(2,1)} %collective-permute-done.refs_9_), channel_id=1, source_target_pairs={{0,2},{1,3},{2,0},{3,1},{4,6},{5,7},{6,4},{7,5},{8,10},{9,11},{10,... | collective-permute-start | bytes 786440 | tf_op jit(solution)/shard_map/ppermute | solution.py:311
  44.4 11.2 %collective-permute-start.10 = (bf16[512,256]{1,0:T(8,128)(2,1)}, bf16[512,256]{1,0:T(8,128)(2,1)}, u32[]{:S(2)}, u32[]{:S(2)}) collective-permute-start(bf16[512,256]{1,0:T(8,128)(2,1)} %collective-permute-done.7.refs_6_), channel_id=1, source_target_pairs={{0,4},{1,5},{2,6},{3,7},{4,8},{5,9},{6,10},{7,11},{8,12},{9,13},{1... | collective-permute-start | bytes 786440 | tf_op jit(solution)/shard_map/ppermute | solution.py:314
  47.7 14.2 %collective-permute-start.11 = (bf16[512,256]{1,0:T(8,128)(2,1)}, bf16[512,256]{1,0:T(8,128)(2,1)}, u32[]{:S(2)}, u32[]{:S(2)}) collective-permute-start(bf16[512,256]{1,0:T(8,128)(2,1)} %collective-permute-done.7.refs_6_), channel_id=1, source_target_pairs={{0,2},{1,3},{2,0},{3,1},{4,6},{5,7},{6,4},{7,5},{8,10},{9,11},{10,... | collective-permute-start | bytes 786440 | tf_op jit(solution)/shard_map/ppermute | solution.py:311
  51.7 18.3 %collective-permute-start.14 = (bf16[512,256]{1,0:T(8,128)(2,1)}, bf16[512,256]{1,0:T(8,128)(2,1)}, u32[]{:S(2)}, u32[]{:S(2)}) collective-permute-start(bf16[512,256]{1,0:T(8,128)(2,1)} %collective-permute-done.1.refs_8_), channel_id=1, source_target_pairs={{0,12},{1,13},{2,14},{3,15},{4,0},{5,1},{6,2},{7,3},{8,4},{9,5},{1... | collective-permute-start | bytes 786440 | tf_op jit(solution)/shard_map/ppermute | solution.py:314
  55.6 8.4 %collective-permute-start.16 = (bf16[512,256]{1,0:T(8,128)(2,1)}, bf16[512,256]{1,0:T(8,128)(2,1)}, u32[]{:S(2)}, u32[]{:S(2)}) collective-permute-start(bf16[512,256]{1,0:T(8,128)(2,1)} %collective-permute-done.2.refs_11_), channel_id=1, source_target_pairs={{0,2},{1,3},{2,0},{3,1},{4,6},{5,7},{6,4},{7,5},{8,10},{9,11},{10,... | collective-permute-start | bytes 786440 | tf_op jit(solution)/shard_map/ppermute | solution.py:311
  55.6 9.6 %collective-permute-start.15 = (bf16[512,256]{1,0:T(8,128)(2,1)}, bf16[512,256]{1,0:T(8,128)(2,1)}, u32[]{:S(2)}, u32[]{:S(2)}) collective-permute-start(bf16[512,256]{1,0:T(8,128)(2,1)} %collective-permute-done.2.refs_11_), channel_id=1, source_target_pairs={{0,4},{1,5},{2,6},{3,7},{4,8},{5,9},{6,10},{7,11},{8,12},{9,13},{1... | collective-permute-start | bytes 786440 | tf_op jit(solution)/shard_map/ppermute | solution.py:314
  61.9 8.2 %collective-permute-start.13 = (bf16[512,256]{1,0:T(8,128)(2,1)}, bf16[512,256]{1,0:T(8,128)(2,1)S(1)}, u32[]{:S(2)}, u32[]{:S(2)}) collective-permute-start(bf16[512,256]{1,0:T(8,128)(2,1)} %collective-permute-done.10.refs_3_), channel_id=1, source_target_pairs={{0,2},{1,3},{2,0},{3,1},{4,6},{5,7},{6,4},{7,5},{8,10},{9,11},{10,... | collective-permute-start | bytes 786440 | tf_op jit(solution)/shard_map/ppermute | solution.py:311
  64.0 8.1 %collective-permute-start.3 = (bf16[2048,384]{1,0:T(8,128)(2,1)}, bf16[2048,384]{1,0:T(8,128)(2,1)S(1)}, u32[]{:S(2)}, u32[]{:S(2)}) collective-permute-start(bf16[2048,384]{1,0:T(8,128)(2,1)} %copy-done.10), channel_id=1, source_target_pairs={{0,1},{1,0},{2,3},{3,2},{4,5},{5,4},{6,7},{7,6},{8,9},{9,8},{10,11... | collective-permute-start | bytes 4718600 | tf_op jit(solution)/shard_map/ppermute | solution.py:308
  72.0 3.5 %collective-permute-start.17 = (f32[768,512]{1,0:T(8,128)S(1)}, f32[768,512]{1,0:T(8,128)S(1)}, u32[]{:S(2)}, u32[]{:S(2)}) collective-permute-start(f32[768,512]{1,0:T(8,128)S(1)} %project.5.mine_ref), channel_id=1, source_target_pairs={{0,1},{1,0},{2,3},{3,2},{4,5},{5,4},{6,7},{7,6},{8,9},{9,8},{10,11... | collective-permute-start | bytes 4718600 | tf_op jit(solution)/shard_map/ppermute | solution.py:308
  76.0 9.2 %collective-permute-start.18 = (bf16[256,512]{1,0:T(8,128)(2,1)S(1)}, bf16[256,512]{1,0:T(8,128)(2,1)S(1)}, u32[]{:S(2)}, u32[]{:S(2)}) collective-permute-start(bf16[256,512]{1,0:T(8,128)(2,1)S(1)} %get-tuple-element.60), channel_id=1, source_target_pairs={{0,2},{1,3},{2,0},{3,1},{4,6},{5,7},{6,4},{7,5},{8,10},{9,11},{10,... | collective-permute-start | bytes 786440 | tf_op jit(solution)/shard_map/ppermute | solution.py:311
  78.3 12.5 %collective-permute-start.20 = (bf16[256,512]{1,0:T(8,128)(2,1)S(1)}, bf16[256,512]{1,0:T(8,128)(2,1)S(1)}, u32[]{:S(2)}, u32[]{:S(2)}) collective-permute-start(bf16[256,512]{1,0:T(8,128)(2,1)S(1)} %get-tuple-element.65), channel_id=1, source_target_pairs={{0,2},{1,3},{2,0},{3,1},{4,6},{5,7},{6,4},{7,5},{8,10},{9,11},{10,... | collective-permute-start | bytes 786440 | tf_op jit(solution)/shard_map/ppermute | solution.py:311
  79.5 16.9 %collective-permute-start.22 = (bf16[256,512]{1,0:T(8,128)(2,1)S(1)}, bf16[256,512]{1,0:T(8,128)(2,1)S(1)}, u32[]{:S(2)}, u32[]{:S(2)}) collective-permute-start(bf16[256,512]{1,0:T(8,128)(2,1)S(1)} %get-tuple-element.67), channel_id=1, source_target_pairs={{0,2},{1,3},{2,0},{3,1},{4,6},{5,7},{6,4},{7,5},{8,10},{9,11},{10,... | collective-permute-start | bytes 786440 | tf_op jit(solution)/shard_map/ppermute | solution.py:311
  85.2 19.9 %copy-start.12 = (f32[256,512]{1,0:T(8,128)S(1)}, f32[256,512]{1,0:T(8,128)}, u32[]{:S(2)}) copy-start(f32[256,512]{1,0:T(8,128)} %param.8) | copy-start | bytes 1572868
  85.2 19.9 %copy-start.13 = (f32[256,512]{1,0:T(8,128)S(1)}, f32[256,512]{1,0:T(8,128)}, u32[]{:S(2)}) copy-start(f32[256,512]{1,0:T(8,128)} %param.9) | copy-start | bytes 1572868
  85.3 11.2 %collective-permute-start.23 = (bf16[256,512]{1,0:T(8,128)(2,1)S(1)}, bf16[256,512]{1,0:T(8,128)(2,1)S(1)}, u32[]{:S(2)}, u32[]{:S(2)}) collective-permute-start(bf16[256,512]{1,0:T(8,128)(2,1)S(1)} %convert_add_fusion.1), channel_id=1, source_target_pairs={{0,4},{1,5},{2,6},{3,7},{4,8},{5,9},{6,10},{7,11},{8,12},{9,13},{1... | collective-permute-start | bytes 786440 | tf_op jit(solution)/shard_map/ppermute | solution.py:314
  85.3 15.9 %collective-permute-start.19 = (bf16[256,512]{1,0:T(8,128)(2,1)S(1)}, bf16[256,512]{1,0:T(8,128)(2,1)S(1)}, u32[]{:S(2)}, u32[]{:S(2)}) collective-permute-start(bf16[256,512]{1,0:T(8,128)(2,1)S(1)} %get-tuple-element.63), channel_id=1, source_target_pairs={{0,2},{1,3},{2,0},{3,1},{4,6},{5,7},{6,4},{7,5},{8,10},{9,11},{10,... | collective-permute-start | bytes 786440 | tf_op jit(solution)/shard_map/ppermute | solution.py:311
  90.9 10.4 %collective-permute-start.21 = (bf16[256,512]{1,0:T(8,128)(2,1)S(1)}, bf16[256,512]{1,0:T(8,128)(2,1)S(1)}, u32[]{:S(2)}, u32[]{:S(2)}) collective-permute-start(bf16[256,512]{1,0:T(8,128)(2,1)S(1)} %add_convert_fusion.1), channel_id=1, source_target_pairs={{0,12},{1,13},{2,14},{3,15},{4,0},{5,1},{6,2},{7,3},{8,4},{9,5},{1... | collective-permute-start | bytes 786440 | tf_op jit(solution)/shard_map/ppermute | solution.py:314
  96.5 8.6 %collective-permute-start.24 = (bf16[256,512]{1,0:T(8,128)(2,1)S(1)}, bf16[256,512]{1,0:T(8,128)(2,1)S(1)}, u32[]{:S(2)}, u32[]{:S(2)}) collective-permute-start(bf16[256,512]{1,0:T(8,128)(2,1)S(1)} %add_convert_fusion), channel_id=1, source_target_pairs={{0,4},{1,5},{2,6},{3,7},{4,8},{5,9},{6,10},{7,11},{8,12},{9,13},{1... | collective-permute-start | bytes 786440 | tf_op jit(solution)/shard_map/ppermute | solution.py:314
  106.5 5.4 %collective-permute-start.26 = (bf16[256,256]{1,0:T(8,128)(2,1)S(1)}, bf16[256,256]{1,0:T(8,128)(2,1)S(1)}, u32[]{:S(2)}, u32[]{:S(2)}) collective-permute-start(bf16[256,256]{1,0:T(8,128)(2,1)S(1)} %get-tuple-element.83), channel_id=1, source_target_pairs={{0,2},{1,3},{2,0},{3,1},{4,6},{5,7},{6,4},{7,5},{8,10},{9,11},{10,... | collective-permute-start | bytes 393224 | tf_op jit(solution)/shard_map/ppermute | solution.py:311
  107.5 7.3 %collective-permute-start.25 = (bf16[256,256]{1,0:T(8,128)(2,1)S(1)}, bf16[256,256]{1,0:T(8,128)(2,1)S(1)}, u32[]{:S(2)}, u32[]{:S(2)}) collective-permute-start(bf16[256,256]{1,0:T(8,128)(2,1)S(1)} %get-tuple-element.83), channel_id=1, source_target_pairs={{0,4},{1,5},{2,6},{3,7},{4,8},{5,9},{6,10},{7,11},{8,12},{9,13},{1... | collective-permute-start | bytes 393224 | tf_op jit(solution)/shard_map/ppermute | solution.py:314
  109.0 7.4 %collective-permute-start.32 = (bf16[256,256]{1,0:T(8,128)(2,1)S(1)}, bf16[256,256]{1,0:T(8,128)(2,1)}, u32[]{:S(2)}, u32[]{:S(2)}) collective-permute-start(bf16[256,256]{1,0:T(8,128)(2,1)S(1)} %get-tuple-element.82), channel_id=1, source_target_pairs={{0,2},{1,3},{2,0},{3,1},{4,6},{5,7},{6,4},{7,5},{8,10},{9,11},{10,... | collective-permute-start | bytes 393224 | tf_op jit(solution)/shard_map/ppermute | solution.py:311
  110.0 6.8 %collective-permute-start.31 = (bf16[256,256]{1,0:T(8,128)(2,1)S(1)}, bf16[256,256]{1,0:T(8,128)(2,1)S(1)}, u32[]{:S(2)}, u32[]{:S(2)}) collective-permute-start(bf16[256,256]{1,0:T(8,128)(2,1)S(1)} %get-tuple-element.82), channel_id=1, source_target_pairs={{0,4},{1,5},{2,6},{3,7},{4,8},{5,9},{6,10},{7,11},{8,12},{9,13},{1... | collective-permute-start | bytes 393224 | tf_op jit(solution)/shard_map/ppermute | solution.py:314
  114.8 5.0 %collective-permute-start.28 = (bf16[256,256]{1,0:T(8,128)(2,1)S(1)}, bf16[256,256]{1,0:T(8,128)(2,1)S(1)}, u32[]{:S(2)}, u32[]{:S(2)}) collective-permute-start(bf16[256,256]{1,0:T(8,128)(2,1)S(1)} %collective-permute-done.25), channel_id=1, source_target_pairs={{0,2},{1,3},{2,0},{3,1},{4,6},{5,7},{6,4},{7,5},{8,10},{9,11},{10,... | collective-permute-start | bytes 393224 | tf_op jit(solution)/shard_map/ppermute | solution.py:311
  115.8 6.8 %collective-permute-start.27 = (bf16[256,256]{1,0:T(8,128)(2,1)S(1)}, bf16[256,256]{1,0:T(8,128)(2,1)S(1)}, u32[]{:S(2)}, u32[]{:S(2)}) collective-permute-start(bf16[256,256]{1,0:T(8,128)(2,1)S(1)} %collective-permute-done.25), channel_id=1, source_target_pairs={{0,4},{1,5},{2,6},{3,7},{4,8},{5,9},{6,10},{7,11},{8,12},{9,13},{1... | collective-permute-start | bytes 393224 | tf_op jit(solution)/shard_map/ppermute | solution.py:314
  116.7 6.9 %collective-permute-start.34 = (bf16[256,256]{1,0:T(8,128)(2,1)S(1)}, bf16[256,256]{1,0:T(8,128)(2,1)S(1)}, u32[]{:S(2)}, u32[]{:S(2)}) collective-permute-start(bf16[256,256]{1,0:T(8,128)(2,1)S(1)} %collective-permute-done.31), channel_id=1, source_target_pairs={{0,2},{1,3},{2,0},{3,1},{4,6},{5,7},{6,4},{7,5},{8,10},{9,11},{10,... | collective-permute-start | bytes 393224 | tf_op jit(solution)/shard_map/ppermute | solution.py:311
  117.8 8.1 %collective-permute-start.33 = (bf16[256,256]{1,0:T(8,128)(2,1)S(1)}, bf16[256,256]{1,0:T(8,128)(2,1)S(1)}, u32[]{:S(2)}, u32[]{:S(2)}) collective-permute-start(bf16[256,256]{1,0:T(8,128)(2,1)S(1)} %collective-permute-done.31), channel_id=1, source_target_pairs={{0,4},{1,5},{2,6},{3,7},{4,8},{5,9},{6,10},{7,11},{8,12},{9,13},{1... | collective-permute-start | bytes 393224 | tf_op jit(solution)/shard_map/ppermute | solution.py:314
  122.5 6.9 %collective-permute-start.30 = (bf16[256,256]{1,0:T(8,128)(2,1)S(1)}, bf16[256,256]{1,0:T(8,128)(2,1)}, u32[]{:S(2)}, u32[]{:S(2)}) collective-permute-start(bf16[256,256]{1,0:T(8,128)(2,1)S(1)} %collective-permute-done.27), channel_id=1, source_target_pairs={{0,4},{1,5},{2,6},{3,7},{4,8},{5,9},{6,10},{7,11},{8,12},{9,13},{1... | collective-permute-start | bytes 393224 | tf_op jit(solution)/shard_map/ppermute | solution.py:314
  122.5 5.5 %collective-permute-start.29 = (bf16[256,256]{1,0:T(8,128)(2,1)S(1)}, bf16[256,256]{1,0:T(8,128)(2,1)S(1)}, u32[]{:S(2)}, u32[]{:S(2)}) collective-permute-start(bf16[256,256]{1,0:T(8,128)(2,1)S(1)} %collective-permute-done.27), channel_id=1, source_target_pairs={{0,2},{1,3},{2,0},{3,1},{4,6},{5,7},{6,4},{7,5},{8,10},{9,11},{10,... | collective-permute-start | bytes 393224 | tf_op jit(solution)/shard_map/ppermute | solution.py:311
  125.9 6.8 %collective-permute-start.36 = (bf16[256,256]{1,0:T(8,128)(2,1)S(1)}, bf16[256,256]{1,0:T(8,128)(2,1)S(1)}, u32[]{:S(2)}, u32[]{:S(2)}) collective-permute-start(bf16[256,256]{1,0:T(8,128)(2,1)S(1)} %collective-permute-done.33), channel_id=1, source_target_pairs={{0,4},{1,5},{2,6},{3,7},{4,8},{5,9},{6,10},{7,11},{8,12},{9,13},{1... | collective-permute-start | bytes 393224 | tf_op jit(solution)/shard_map/ppermute | solution.py:314
  125.9 5.0 %collective-permute-start.35 = (bf16[256,256]{1,0:T(8,128)(2,1)S(1)}, bf16[256,256]{1,0:T(8,128)(2,1)S(1)}, u32[]{:S(2)}, u32[]{:S(2)}) collective-permute-start(bf16[256,256]{1,0:T(8,128)(2,1)S(1)} %collective-permute-done.33), channel_id=1, source_target_pairs={{0,2},{1,3},{2,0},{3,1},{4,6},{5,7},{6,4},{7,5},{8,10},{9,11},{10,... | collective-permute-start | bytes 393224 | tf_op jit(solution)/shard_map/ppermute | solution.py:311
  127.9 7.2 %collective-permute-start.42 = (bf16[1024,256]{1,0:T(8,128)(2,1)S(1)}, bf16[1024,256]{1,0:T(8,128)(2,1)S(1)}, u32[]{:S(2)}, u32[]{:S(2)}) collective-permute-start(bf16[1024,256]{1,0:T(8,128)(2,1)S(1)} %pad_maximum_fusion.1.refs_1_), channel_id=1, source_target_pairs={{0,1},{1,0},{2,3},{3,2},{4,5},{5,4},{6,7},{7,6},{8,9},{9,8},{10,11... | collective-permute-start | bytes 1572872 | tf_op jit(solution)/shard_map/ppermute | solution.py:308
  128.0 8.1 %collective-permute-start.41 = (bf16[1024,256]{1,0:T(8,128)(2,1)S(1)}, bf16[1024,256]{1,0:T(8,128)(2,1)S(1)}, u32[]{:S(2)}, u32[]{:S(2)}) collective-permute-start(bf16[1024,256]{1,0:T(8,128)(2,1)S(1)} %pad_maximum_fusion.refs_0_), channel_id=1, source_target_pairs={{0,1},{1,0},{2,3},{3,2},{4,5},{5,4},{6,7},{7,6},{8,9},{9,8},{10,11... | collective-permute-start | bytes 1572872 | tf_op jit(solution)/shard_map/ppermute | solution.py:308
  130.3 11.0 %collective-permute-start.39 = (bf16[768,256]{1,0:T(8,128)(2,1)S(1)}, bf16[768,256]{1,0:T(8,128)(2,1)}, u32[]{:S(2)}, u32[]{:S(2)}) collective-permute-start(bf16[768,256]{1,0:T(8,128)(2,1)S(1)} %constant_dynamic-update-slice_fusion.refs_0_), channel_id=1, source_target_pairs={{0,1},{1,0},{2,3},{3,2},{4,5},{5,4},{6,7},{7,6},{8,9},{9,8},{10,11... | collective-permute-start | bytes 1179656 | tf_op jit(solution)/shard_map/ppermute | solution.py:308
  132.7 8.7 %collective-permute-start.40 = (bf16[768,256]{1,0:T(8,128)(2,1)S(1)}, bf16[768,256]{1,0:T(8,128)(2,1)}, u32[]{:S(2)}, u32[]{:S(2)}) collective-permute-start(bf16[768,256]{1,0:T(8,128)(2,1)S(1)} %constant_dynamic-update-slice_fusion.3.refs_1_), channel_id=1, source_target_pairs={{0,1},{1,0},{2,3},{3,2},{4,5},{5,4},{6,7},{7,6},{8,9},{9,8},{10,11... | collective-permute-start | bytes 1179656 | tf_op jit(solution)/shard_map/ppermute | solution.py:308
  132.7 7.2 %collective-permute-start.38 = (bf16[256,256]{1,0:T(8,128)(2,1)}, bf16[256,256]{1,0:T(8,128)(2,1)S(1)}, u32[]{:S(2)}, u32[]{:S(2)}) collective-permute-start(bf16[256,256]{1,0:T(8,128)(2,1)} %collective-permute-done.32), channel_id=1, source_target_pairs={{0,12},{1,13},{2,14},{3,15},{4,0},{5,1},{6,2},{7,3},{8,4},{9,5},{1... | collective-permute-start | bytes 393224 | tf_op jit(solution)/shard_map/ppermute | solution.py:314
  135.0 5.7 %collective-permute-start.37 = (bf16[256,256]{1,0:T(8,128)(2,1)}, bf16[256,256]{1,0:T(8,128)(2,1)}, u32[]{:S(2)}, u32[]{:S(2)}) collective-permute-start(bf16[256,256]{1,0:T(8,128)(2,1)} %collective-permute-done.30), channel_id=1, source_target_pairs={{0,2},{1,3},{2,0},{3,1},{4,6},{5,7},{6,4},{7,5},{8,10},{9,11},{10,... | collective-permute-start | bytes 393224 | tf_op jit(solution)/shard_map/ppermute | solution.py:311
  140.7 1.7 %collective-permute-start.43 = (bf16[256,256]{1,0:T(8,128)(2,1)}, bf16[256,256]{1,0:T(8,128)(2,1)S(1)}, u32[]{:S(2)}, u32[]{:S(2)}) collective-permute-start(bf16[256,256]{1,0:T(8,128)(2,1)} %collective-permute-done.37.refs_2_), channel_id=1, source_target_pairs={{0,1},{1,0},{2,3},{3,2},{4,5},{5,4},{6,7},{7,6},{8,9},{9,8},{10,11... | collective-permute-start | bytes 393224 | tf_op jit(solution)/shard_map/ppermute | solution.py:308
  140.7 1.7 %collective-permute-start.44 = (bf16[256,256]{1,0:T(8,128)(2,1)S(1)}, bf16[256,256]{1,0:T(8,128)(2,1)S(1)}, u32[]{:S(2)}, u32[]{:S(2)}) collective-permute-start(bf16[256,256]{1,0:T(8,128)(2,1)S(1)} %collective-permute-done.38.refs_3_), channel_id=1, source_target_pairs={{0,1},{1,0},{2,3},{3,2},{4,5},{5,4},{6,7},{7,6},{8,9},{9,8},{10,11... | collective-permute-start | bytes 393224 | tf_op jit(solution)/shard_map/ppermute | solution.py:308
  (11 other events, 74.5 us)

commit v6 on v2

v6 whole, which is shorter than its diff:
```python
import functools
import jax
import jax.numpy as jnp
from jax import lax
from jax.experimental import pallas as pl
from jax.experimental.pallas import tpu as pltpu
from jax.sharding import PartitionSpec as P

STEP = 100

decay_first = 0.9
decay_second = 0.999
epsilon = 1e-08

CHUNKS = 2
COSTX = 30
F32, BF16 = jnp.float32, jnp.bfloat16
VMEM_LIMIT = 16 * 1024 * 1024


def adam(reduced, first_moment, second_moment):
    new_first = decay_first * first_moment + (1.0 - decay_first) * reduced
    new_second = decay_second * second_moment + (1.0 - decay_second) * reduced * reduced
    first_fix = 1.0 - decay_first**STEP
    second_fix = 1.0 - decay_second**STEP
    direction = (new_first / first_fix / (jnp.sqrt(new_second / second_fix) + epsilon)).astype(BF16)
    return new_first, new_second, direction


def plain(activations, out_grads, projector, first_moment, second_moment):
    projected = jnp.dot(
        activations,
        lax.all_gather(projector, "dp", axis=0, tiled=True),
        preferred_element_type=F32,
    ).astype(BF16)
    reduced = lax.psum_scatter(
        lax.dot_general(out_grads, projected, (((0,), (0,)), ((), ())), preferred_element_type=F32),
        "dp",
        scatter_dimension=0,
        tiled=True,
    )
    new_first, new_second, direction = adam(reduced, first_moment, second_moment)
    update = lax.dot_general(
        lax.all_gather(direction, "dp", axis=0, tiled=True),
        projector,
        (((1,), (1,)), ((), ())),
        preferred_element_type=F32,
    ).astype(BF16)
    return update, new_first, new_second


def params():
    return pltpu.CompilerParams(vmem_limit_bytes=VMEM_LIMIT)


def cost(flops, moved):
    return pl.CostEstimate(flops=COSTX * flops, bytes_accessed=COSTX * moved, transcendentals=0)


def pinned(x):
    return pltpu.with_memory_space_constraint(x, pltpu.HBM)


def call(kernel, scalars, arrays, outs, scratch, *, flops, moved, name, aliases=None, in_hbm=0):
    anywhere = pl.BlockSpec(memory_space=pl.ANY)
    return pl.pallas_call(
        kernel,
        grid_spec=pltpu.PrefetchScalarGridSpec(
            num_scalar_prefetch=1,
            grid=(),
            in_specs=[anywhere] * len(arrays),
            out_specs=[anywhere] * len(outs),
            scratch_shapes=scratch,
        ),
        out_shape=outs,
        input_output_aliases=aliases or {},
        compiler_params=params(),
        cost_estimate=cost(flops, moved),
        name=name,
    )(scalars, *[pinned(x) for x in arrays[:in_hbm]], *arrays[in_hbm:])


def project(activations, sibling, at, blocks, before):
    chunks, many = len(blocks), len(blocks[0])
    (depth, cols), rows = blocks[0][0].shape, activations.shape[0]
    copies = many * (2 + chunks)
    flat = [block for chunk in blocks for block in chunk]
    held = [] if before is None else [before]

    def kernel(at_ref, own_ref, sib_ref, *refs):
        block_refs, out_ref = refs[: chunks * many], refs[chunks * many + len(held)]
        a, b, total, sems = refs[chunks * many + len(held) + 1 :]
        started = []
        for j in range(many):
            columns = pl.ds(pl.multiple_of(at_ref[j] * depth, depth), depth)
            moves = [
                (own_ref.at[:, columns], a.at[pl.ds(0, rows), pl.ds(j * depth, depth)]),
                (sib_ref.at[:, columns], a.at[pl.ds(rows, rows), pl.ds(j * depth, depth)]),
            ]
            for i in range(chunks):
                moves.append((block_refs[i * many + j], b.at[pl.ds(j * depth, depth), pl.ds(i * cols, cols)]))
            for source, target in moves:
                started.append(pltpu.make_async_copy(source, target, sems.at[len(started)]))
                started[-1].start()
        if held:
            started.append(pltpu.make_async_copy(refs[chunks * many], total, sems.at[len(started)]))
            started[-1].start()
        groups = [(0, (many + 1) // 2), ((many + 1) // 2, many)] if many > 1 else [(0, 1)]
        for at, (low, high) in enumerate(groups):
            for copy in started[low * (2 + chunks) : high * (2 + chunks)] + (started[copies:] if at == 0 else []):
                copy.wait()
            deep = slice(low * depth, high * depth)
            term = jnp.dot(a[:, deep], b[deep, :], preferred_element_type=F32)
            total[...] = total[...] + term if held or at else term
        back_copy = pltpu.make_async_copy(total, out_ref, sems.at[len(started)])
        back_copy.start()
        back_copy.wait()

    wide = chunks * cols
    return call(
        kernel,
        at,
        [activations, sibling, *flat, *held],
        [jax.ShapeDtypeStruct((2 * rows, wide), F32)],
        [
            pltpu.VMEM((2 * rows, many * depth), BF16),
            pltpu.VMEM((many * depth, wide), BF16),
            pltpu.VMEM((2 * rows, wide), F32),
            pltpu.SemaphoreType.DMA((copies + 2,)),
        ],
        flops=4 * rows * depth * many * wide,
        moved=4 * rows * depth * many + 2 * depth * many * wide + 8 * rows * wide,
        name="project",
        in_hbm=2,
    )[0]


def outer(out_grads, sibling, at, width, dtype, projected):
    rows, many, cols = out_grads.shape[0], at.shape[0], projected.shape[1]

    def kernel(at_ref, own_ref, sib_ref, projected_ref, *refs):
        outs, (g, sems) = refs[:-2], refs[-2:]
        copies = []
        for j in range(many):
            columns = pl.ds(pl.multiple_of(at_ref[j] * width, width), width)
            for i, ref in enumerate((own_ref, sib_ref)):
                target = g.at[pl.ds(i * rows, rows), pl.ds(j * width, width)]
                copies.append(pltpu.make_async_copy(ref.at[:, columns], target, sems.at[len(copies)]))
                copies[-1].start()
        for j in range(many):
            copies[2 * j].wait()
            copies[2 * j + 1].wait()
            block = g[:, j * width : (j + 1) * width].T
            outs[j][...] = jnp.dot(block, projected_ref[...], preferred_element_type=F32).astype(dtype)

    whole = lambda *shape: pl.BlockSpec(shape, lambda j, at_ref: (0, 0))
    return pl.pallas_call(
        kernel,
        grid_spec=pltpu.PrefetchScalarGridSpec(
            num_scalar_prefetch=1,
            grid=(1,),
            in_specs=[pl.BlockSpec(memory_space=pl.ANY)] * 2 + [whole(2 * rows, cols)],
            out_specs=[whole(width, cols)] * many,
            scratch_shapes=[pltpu.VMEM((2 * rows, many * width), BF16), pltpu.SemaphoreType.DMA((2 * many,))],
        ),
        out_shape=[jax.ShapeDtypeStruct((width, cols), dtype)] * many,
        compiler_params=params(),
        cost_estimate=cost(4 * rows * width * many * cols, many * (4 * rows * width + 4 * width * cols)),
        name="outer",
    )(at, pinned(out_grads), pinned(sibling), projected)


def back(blocks, projectors_t, at, rows_in_all, before):
    many, chunks = len(blocks), len(blocks[0])
    (rows, cols), (rank, both) = blocks[0][0].shape, projectors_t.shape
    width = both // 2
    arrays = [x for block in blocks for x in block]
    held = [] if before is None else [before]

    def kernel(at_ref, projector_ref, *refs):
        array_refs, (out_ref, other_ref) = refs[: len(arrays)], refs[len(arrays) + len(held) :][:2]
        p, d, o, in_sems, out_sems = refs[len(arrays) + len(held) + 2 :]
        p_copy = pltpu.make_async_copy(projector_ref, p, in_sems.at[len(arrays)])
        p_copy.start()
        loads, stores = [], []
        for n, ref in enumerate(array_refs):
            j, i = n // chunks, n % chunks
            loads.append(pltpu.make_async_copy(ref, d.at[pl.ds(j * rows, rows), pl.ds(i * cols, cols)], in_sems.at[n]))
            loads[-1].start()
        p_copy.wait()
        for j in range(many):
            for copy in loads[j * chunks : (j + 1) * chunks]:
                copy.wait()
            here = pl.ds(j * rows, rows)
            o[here, :] = jnp.dot(d[here, :], p[...], preferred_element_type=F32).astype(BF16)
            for n, (columns, target) in enumerate(
                (
                    (pl.ds(0, width), out_ref.at[pl.ds(pl.multiple_of(at_ref[j] * rows, rows), rows), :]),
                    (pl.ds(width, width), other_ref.at[here, :]),
                )
            ):
                stores.append(pltpu.make_async_copy(o.at[here, columns], target, out_sems.at[2 * j + n]))
                stores[-1].start()
        for copy in stores:
            copy.wait()

    return call(
        kernel,
        at,
        [projectors_t, *arrays, *held],
        [jax.ShapeDtypeStruct((rows_in_all, width), BF16), jax.ShapeDtypeStruct((many * rows, width), BF16)],
        [
            pltpu.VMEM((rank, both), BF16),
            pltpu.VMEM((many * rows, rank), BF16),
            pltpu.VMEM((many * rows, both), BF16),
            pltpu.SemaphoreType.DMA((len(arrays) + 1,)),
            pltpu.SemaphoreType.DMA((2 * many,)),
        ],
        flops=2 * many * rows * both * rank,
        moved=2 * many * rows * (both + rank),
        name="back",
        aliases={2 + len(arrays): 0} if held else None,
    )


def place(whole, pieces, at, rows):
    many, width, sizes = at.shape[0], whole.shape[1], [piece.shape[0] for piece in pieces]

    def kernel(at_ref, *refs):
        piece_refs, (out_ref, held, sems) = refs[: len(pieces)], refs[len(pieces) + 1 :]
        copies, start = [], 0
        for n, ref in enumerate(piece_refs):
            copies.append(pltpu.make_async_copy(ref, held.at[pl.ds(start, sizes[n]), :], sems.at[n]))
            copies[-1].start()
            start += sizes[n]
        for copy in copies:
            copy.wait()
        copies = []
        for j in range(many):
            target = out_ref.at[pl.ds(pl.multiple_of(at_ref[j] * rows, rows), rows), :]
            copies.append(pltpu.make_async_copy(held.at[pl.ds(j * rows, rows), :], target, sems.at[len(pieces) + j]))
            copies[-1].start()
        for copy in copies:
            copy.wait()

    return call(
        kernel,
        at,
        [*pieces, whole],
        [jax.ShapeDtypeStruct(whole.shape, whole.dtype)],
        [pltpu.VMEM((many * rows, width), whole.dtype), pltpu.SemaphoreType.DMA((len(pieces) + many,))],
        flops=0,
        moved=4 * many * rows * width,
        name="place",
        aliases={1 + len(pieces): 0},
    )[0]


def levels(activations, out_grads, projector, first_moment, second_moment, *, nz):
    me = lax.axis_index("dp")
    z, y, core = me // 4, me // 2 % 2, me % 2
    grid = [(a, b, c) for a in range(nz) for b in range(2) for c in range(2)]

    def pairs(to):
        return [((a * 2 + b) * 2 + c, (to(a, b, c)[0] * 2 + to(a, b, c)[1]) * 2 + to(a, b, c)[2]) for a, b, c in grid]

    def swap_core(x):
        return lax.ppermute(x, "dp", pairs(lambda a, b, c: (a, b, 1 - c)))

    def swap_y(x):
        return lax.ppermute(x, "dp", pairs(lambda a, b, c: (a, 1 - b, c)))

    def shift_z(x, k):
        return lax.ppermute(x, "dp", pairs(lambda a, b, c: ((a + k) % nz, b, c)))

    def index(k, dy, dc):
        return (lax.rem(z + nz + k, nz) * 2 + (1 - y if dy else y)) * 2 + (1 - core if dc else core)

    def named(order):
        return jnp.stack([index(*o) for o in order]).astype(jnp.int32)

    def gather(chunks):
        line = [[own] for own in chunks]
        across = [[] for _ in chunks]
        for step in range(nz):
            for i in range(len(chunks)):
                if step:
                    line[i][step], across[i][step - 1] = lax.optimization_barrier((line[i][step], across[i][step - 1]))
                if step < nz - 1:
                    line[i].append(shift_z(line[i][step], 1))
                if step < nz - 1 or i < len(chunks) - 1:
                    across[i].append(swap_y(line[i][step]))
                else:
                    across[i].append(shift_z(across[i][0], nz - 1))
        return line, across

    after = lambda x, *those: lax.optimization_barrier((x, *those))[0]
    ks = list(range(nz - 2, 0, -1)) + [nz - 1]
    depth, rank = projector.shape
    width = first_moment.shape[0]
    cols = rank // CHUNKS
    parts = [slice(i * cols, (i + 1) * cols) for i in range(CHUNKS)]

    order_in = [(-k, dy) for k in range(nz) for dy in (0, 1)]
    order_out = [(k, dy) for dy in (1, 0) for k in ks + [0]]
    last = len(order_in) - 1
    at_in = named([(k, dy, 0) for k, dy in order_in])
    at_out = named([(k, dy, 0) for k, dy in order_out])
    at_sibling = named([(k, dy, 1) for k, dy in order_in])

    def ready(line, across, low, high):
        return [[(across if n % 2 else line)[i][n // 2] for n in range(low, high)] for i in range(CHUNKS)]

    a_sibling = swap_core(activations)
    made = {"end": 0, "mine": None}

    def project_to(end, line, across):
        low = made["end"]
        made["mine"] = project(activations, a_sibling, at_in[low:end], ready(line, across, low, end), made["mine"])
        made["end"] = end
        return made["mine"]

    line, across = gather([projector[:, part] for part in parts])
    p_sibling = swap_core(after(projector, a_sibling, line[0][2]))
    g_sibling = swap_core(after(out_grads, p_sibling))
    project_to(last, line, across)
    mine = project_to(last + 1, line, across)

    projectors_t = jnp.concatenate([after(projector, mine).T, after(p_sibling, mine).T], axis=1)
    theirs = after(swap_core(mine), projectors_t)
    rows = activations.shape[0]
    projected = (mine + jnp.concatenate([theirs[rows:], theirs[:rows]], axis=0)).astype(BF16)
    sends, keeps = [], []
    for low, high in ((0, 1), (1, nz)):
        sends += list(outer(out_grads, g_sibling, at_out[low:high], width, BF16, projected))
    keeps = list(outer(out_grads, g_sibling, at_out[nz:], width, F32, projected))
    terms = [keep + swap_y(send).astype(F32) for keep, send in zip(keeps, sends)]
    passed = terms[0]
    for term in terms[1 : nz - 2]:
        passed = term + shift_z(passed.astype(BF16), 1).astype(F32)
    reduced = terms[nz - 1] + shift_z(terms[nz - 2].astype(BF16), nz - 1).astype(F32) + shift_z(passed.astype(BF16), 1).astype(F32)
    new_first, new_second, direction = adam(reduced, first_moment, second_moment)

    line, across = gather([direction[:, part] for part in parts])
    rows_in_all = 4 * nz * width
    update, early = back(list(zip(*ready(line, across, 0, last))), projectors_t, at_in[:last], rows_in_all, None)
    early = swap_core(early)
    ends = [x[0] for x in ready(line, across, last, last + 1)]
    update, late = back([ends], projectors_t, at_in[last:], rows_in_all, update)
    update = place(update, [early, swap_core(late)], at_sibling, width)
    return update, new_first, new_second


def solution(mesh):
    devices = mesh.shape["dp"]

    def body(activations, out_grads, projector, first_moment, second_moment):
        aligned = projector.shape[0] % 128 == 0 and first_moment.shape[0] % 128 == 0
        if devices % 4 or devices < 16 or not aligned:
            return plain(activations, out_grads, projector, first_moment, second_moment)
        return levels(activations, out_grads, projector, first_moment, second_moment, nz=devices // 4)

    placed = P(("groups", "dp"), None)
    return jax.shard_map(
        body,
        mesh=mesh,
        in_specs=(placed,) * 5,
        out_specs=(P("groups", "dp"), placed, placed),
        check_vma=False,
    )
```

time: 168 us -> 142 us (0.85)
  local copies, waits for them, and re-layouts: 35.4 us -> 5.22 us
  waiting for transfers between devices: 47.2 us -> 74.8 us
  starting transfers between devices: 52.8 us -> 34.9 us
  Pallas kernels: 29.1 us -> 23.7 us
    unnamed x81 -> x10, local copies, waits for them, and re-layouts: 34.8 us -> 0.23 us
    ppermute x18, waiting for transfers between devices: 11.1 us -> 25.7 us  [swap_y(): return lax.ppermute(x, 'dp', pairs(lambda a, b, c: (a, 1 - b, c)))]
    ppermute x17, starting transfers between devices: 30.4 us -> 18.2 us  [shift_z(): return lax.ppermute(x, 'dp', pairs(lambda a, b, c: ((a + k) % nz, b, c)))]
    ppermute x17, waiting for transfers between devices: 36.1 us -> 43.4 us  [shift_z(): return lax.ppermute(x, 'dp', pairs(lambda a, b, c: ((a + k) % nz, b, c)))]
    ppermute x19 -> x6, waiting for transfers between devices: 0.05 us -> 5.67 us  [swap_core(): return lax.ppermute(x, 'dp', pairs(lambda a, b, c: (a, b, 1 - c)))]
    pallas_call x6 -> x3, Pallas kernels: 12.4 us -> 7.52 us  [outer(): pl.pallas_call(kernel, grid_spec=pltpu.PrefetchScalarGridSpec(num_scalar_...]
    ppermute x18, starting transfers between devices: 19.3 us -> 14.9 us  [swap_y(): return lax.ppermute(x, 'dp', pairs(lambda a, b, c: (a, 1 - b, c)))]
    slice x2 -> x3, local copies, waits for them, and re-layouts: 0.05 us -> 2.57 us  [the longest x1 1.49 us: levels(): theirs[rows:]]
  transfers between devices with their start and end apart: 54 -> 41, of which waited for: 18 -> 31; matrix products, arithmetic and copies ran while one was open for 1% -> 4% of each run, Pallas kernels for 12% -> 11%
where the time goes in v6:
time: 142 us
  waiting for transfers between devices  74.8 us (53%)
  starting transfers between devices  34.9 us (25%)
  Pallas kernels  23.7 us (17%)
  local copies, waits for them, and re-layouts  5.22 us (4%)
  other arithmetic  2.35 us (2%)
    ppermute x17, waiting for transfers between devices, shift_z(): return lax.ppermute(x, 'dp', pairs(lambda a, b, c: ((a + k) % nz, b, c)))  43.4 us
    ppermute x18, waiting for transfers between devices, swap_y(): return lax.ppermute(x, 'dp', pairs(lambda a, b, c: (a, 1 - b, c)))  25.7 us
    ppermute x17, starting transfers between devices, shift_z(): return lax.ppermute(x, 'dp', pairs(lambda a, b, c: ((a + k) % nz, b, c)))  18.2 us
    pallas_call x5, Pallas kernels, call(): pl.pallas_call(kernel, grid_spec=pltpu.PrefetchScalarGridSpec(num_scalar_...  16.2 us
    ppermute x18, starting transfers between devices, swap_y(): return lax.ppermute(x, 'dp', pairs(lambda a, b, c: (a, 1 - b, c)))  14.9 us
    pallas_call x3, Pallas kernels, outer(): pl.pallas_call(kernel, grid_spec=pltpu.PrefetchScalarGridSpec(num_scalar_...  7.52 us
    ppermute x6, waiting for transfers between devices, swap_core(): return lax.ppermute(x, 'dp', pairs(lambda a, b, c: (a, b, 1 - c)))  5.67 us
  transfers between devices with their start and end apart: 41, of which 31 were waited for; matrix products, arithmetic and copies ran while one was open for 4% of the time, Pallas kernels for 11%

profile of v6, /device:TPU:0, one launch (start us, length us, event | category | flops | bytes accessed | tf_op | source)
XLA Modules:
  0.0 141.9 jit_solution(16014512995671568825)
XLA Ops:
  2.2 2.6 %collective-permute-start.9 = (bf16[512,256]{1,0:T(8,128)(2,1)S(1)}, bf16[512,256]{1,0:T(8,128)(2,1)S(1)}, u32[]{:S(2)}, u32[]{:S(2)}) collective-permute-start(bf16[512,256]{1,0:T(8,128)(2,1)S(1)} %get-tuple-element.88.refs_7_), channel_id=1, source_target_pairs={{0,2},{1,3},{2,0},{3,1},{4,6},{5,7},{6,4},{7,5},{8,10},{9,11},{10,... | collective-permute-start | bytes 786440 | tf_op jit(solution)/shard_map/ppermute | solution.py:271
  4.8 1.6 %collective-permute-start.8 = (bf16[512,256]{1,0:T(8,128)(2,1)S(1)}, bf16[512,256]{1,0:T(8,128)(2,1)S(1)}, u32[]{:S(2)}, u32[]{:S(2)}) collective-permute-start(bf16[512,256]{1,0:T(8,128)(2,1)S(1)} %get-tuple-element.88.refs_7_), channel_id=1, source_target_pairs={{0,4},{1,5},{2,6},{3,7},{4,8},{5,9},{6,10},{7,11},{8,12},{9,13},{1... | collective-permute-start | bytes 786440 | tf_op jit(solution)/shard_map/ppermute | solution.py:274
  6.9 1.6 %collective-permute-start.1 = (bf16[512,256]{1,0:T(8,128)(2,1)S(1)}, bf16[512,256]{1,0:T(8,128)(2,1)S(1)}, u32[]{:S(2)}, u32[]{:S(2)}) collective-permute-start(bf16[512,256]{1,0:T(8,128)(2,1)S(1)} %get-tuple-element.89.refs_0_), channel_id=1, source_target_pairs={{0,4},{1,5},{2,6},{3,7},{4,8},{5,9},{6,10},{7,11},{8,12},{9,13},{1... | collective-permute-start | bytes 786440 | tf_op jit(solution)/shard_map/ppermute | solution.py:274
  8.5 3.5 %collective-permute-done.9.refs_8_ = bf16[512,256]{1,0:T(8,128)(2,1)S(1)} collective-permute-done((bf16[512,256]{1,0:T(8,128)(2,1)S(1)}, bf16[512,256]{1,0:T(8,128)(2,1)S(1)}, u32[]{:S(2)}, u32[]{:S(2)}) %collective-permute-start.9) | collective-permute-done | bytes 262176 | tf_op jit(solution)/shard_map/ppermute | solution.py:271
  12.0 3.8 %collective-permute-done.8.refs_9_ = bf16[512,256]{1,0:T(8,128)(2,1)S(1)} collective-permute-done((bf16[512,256]{1,0:T(8,128)(2,1)S(1)}, bf16[512,256]{1,0:T(8,128)(2,1)S(1)}, u32[]{:S(2)}, u32[]{:S(2)}) %collective-permute-start.8) | collective-permute-done | bytes 262176 | tf_op jit(solution)/shard_map/ppermute | solution.py:274
  16.0 1.6 %collective-permute-done.2.refs_1_ = bf16[512,256]{1,0:T(8,128)(2,1)S(1)} collective-permute-done((bf16[512,256]{1,0:T(8,128)(2,1)S(1)}, bf16[512,256]{1,0:T(8,128)(2,1)S(1)}, u32[]{:S(2)}, u32[]{:S(2)}) %collective-permute-start.2) | collective-permute-done | bytes 262176 | tf_op jit(solution)/shard_map/ppermute | solution.py:271
  17.6 3.8 %collective-permute-done.1.refs_2_ = bf16[512,256]{1,0:T(8,128)(2,1)S(1)} collective-permute-done((bf16[512,256]{1,0:T(8,128)(2,1)S(1)}, bf16[512,256]{1,0:T(8,128)(2,1)S(1)}, u32[]{:S(2)}, u32[]{:S(2)}) %collective-permute-start.1) | collective-permute-done | bytes 262176 | tf_op jit(solution)/shard_map/ppermute | solution.py:274
  21.7 1.5 %collective-permute-done.12.refs_10_ = bf16[512,256]{1,0:T(8,128)(2,1)S(1)} collective-permute-done((bf16[512,256]{1,0:T(8,128)(2,1)S(1)}, bf16[512,256]{1,0:T(8,128)(2,1)S(1)}, u32[]{:S(2)}, u32[]{:S(2)}) %collective-permute-start.12) | collective-permute-done | bytes 262176 | tf_op jit(solution)/shard_map/ppermute | solution.py:271
  23.2 3.8 %collective-permute-done.11.refs_11_ = bf16[512,256]{1,0:T(8,128)(2,1)S(1)} collective-permute-done((bf16[512,256]{1,0:T(8,128)(2,1)S(1)}, bf16[512,256]{1,0:T(8,128)(2,1)S(1)}, u32[]{:S(2)}, u32[]{:S(2)}) %collective-permute-start.11) | collective-permute-done | bytes 262176 | tf_op jit(solution)/shard_map/ppermute | solution.py:274
  27.3 1.5 %collective-permute-done.4.refs_3_ = bf16[512,256]{1,0:T(8,128)(2,1)S(1)} collective-permute-done((bf16[512,256]{1,0:T(8,128)(2,1)S(1)}, bf16[512,256]{1,0:T(8,128)(2,1)S(1)}, u32[]{:S(2)}, u32[]{:S(2)}) %collective-permute-start.4) | collective-permute-done | bytes 262176 | tf_op jit(solution)/shard_map/ppermute | solution.py:271
  28.8 3.8 %collective-permute-done.3.refs_4_ = bf16[512,256]{1,0:T(8,128)(2,1)S(1)} collective-permute-done((bf16[512,256]{1,0:T(8,128)(2,1)S(1)}, bf16[512,256]{1,0:T(8,128)(2,1)S(1)}, u32[]{:S(2)}, u32[]{:S(2)}) %collective-permute-start.3) | collective-permute-done | bytes 262176 | tf_op jit(solution)/shard_map/ppermute | solution.py:274
  33.0 1.4 %collective-permute-done.14.refs_12_ = bf16[512,256]{1,0:T(8,128)(2,1)S(1)} collective-permute-done((bf16[512,256]{1,0:T(8,128)(2,1)S(1)}, bf16[512,256]{1,0:T(8,128)(2,1)S(1)}, u32[]{:S(2)}, u32[]{:S(2)}) %collective-permute-start.14) | collective-permute-done | bytes 262176 | tf_op jit(solution)/shard_map/ppermute | solution.py:271
  34.4 4.0 %collective-permute-start.10 = (bf16[512,256]{1,0:T(8,128)(2,1)S(1)}, bf16[512,256]{1,0:T(8,128)(2,1)}, u32[]{:S(2)}, u32[]{:S(2)}) collective-permute-start(bf16[512,256]{1,0:T(8,128)(2,1)S(1)} %collective-permute-done.9.refs_8_), channel_id=1, source_target_pairs={{0,12},{1,13},{2,14},{3,15},{4,0},{5,1},{6,2},{7,3},{8,4},{9,5},{1... | collective-permute-start | bytes 786440 | tf_op jit(solution)/shard_map/ppermute | solution.py:274
  38.5 1.5 %collective-permute-done.6.refs_5_ = bf16[512,256]{1,0:T(8,128)(2,1)} collective-permute-done((bf16[512,256]{1,0:T(8,128)(2,1)S(1)}, bf16[512,256]{1,0:T(8,128)(2,1)}, u32[]{:S(2)}, u32[]{:S(2)}) %collective-permute-start.6) | collective-permute-done | bytes 262176 | tf_op jit(solution)/shard_map/ppermute | solution.py:271
  40.0 4.0 %collective-permute-done.5.refs_6_ = bf16[512,256]{1,0:T(8,128)(2,1)S(1)} collective-permute-done((bf16[512,256]{1,0:T(8,128)(2,1)S(1)}, bf16[512,256]{1,0:T(8,128)(2,1)S(1)}, u32[]{:S(2)}, u32[]{:S(2)}) %collective-permute-start.5) | collective-permute-done | bytes 262176 | tf_op jit(solution)/shard_map/ppermute | solution.py:274
  44.0 1.7 %collective-permute-start.7 = (bf16[512,256]{1,0:T(8,128)(2,1)S(1)}, bf16[512,256]{1,0:T(8,128)(2,1)}, u32[]{:S(2)}, u32[]{:S(2)}) collective-permute-start(bf16[512,256]{1,0:T(8,128)(2,1)S(1)} %collective-permute-done.5.refs_6_), channel_id=1, source_target_pairs={{0,2},{1,3},{2,0},{3,1},{4,6},{5,7},{6,4},{7,5},{8,10},{9,11},{10,... | collective-permute-start | bytes 786440 | tf_op jit(solution)/shard_map/ppermute | solution.py:271
  45.7 2.0 %copy.11 = bf16[512,512]{0,1:T(8,128)(2,1)} copy(bf16[512,512]{1,0:T(8,128)(2,1)} %param.7) | data formatting | bytes 1048576 | tf_op jit(solution)/shard_map/optimization_barrier | solution.py:297
  47.8 5.9 %project.2.refs_2_ = f32[768,512]{1,0:T(8,128)S(1)} custom-call(s32[7]{0:T(128)S(1)} %stack.95.at_ref, bf16[384,8192]{1,0:T(8,128)(2,1)} %own_ref.6, bf16[384,8192]{1,0:T(8,128)(2,1)} %collective-permute-done.sib_ref, bf16[512,256]{1,0:T(8,128)(2,1)S(1)} %get-tuple-element.89.refs_0_, bf16[512,256]{1,0:T(8,128)(2,1)S(1)} %collective-permute-done.2.refs_1_, ...), custom_call_target="tpu_custom_call" | custom-call | flops 84557168640 | bytes 322437120 | tf_op jit(solution)/shard_map/project/pallas_call | solution.py:66
  54.5 2.1 %project.3 = f32[768,512]{1,0:T(8,128)S(1)} custom-call(s32[1]{0:T(128)} %bitcast.15.at_ref, bf16[384,8192]{1,0:T(8,128)(2,1)} %own_ref.6, bf16[384,8192]{1,0:T(8,128)(2,1)} %collective-permute-done.sib_ref, bf16[512,256]{1,0:T(8,128)(2,1)} %collective-permute-done.7.refs_0_, bf16[512,256]{1,0:T(8,128)(2,1)} %collective-permute-done.10.refs_1_, ...), custom_call_target="tpu_custom_call" | custom-call | flops 12079595520 | bytes 86507520 | tf_op jit(solution)/shard_map/project/pallas_call | solution.py:66
  57.6 4.3 %collective-permute-done.17 = f32[768,512]{1,0:T(8,128)} collective-permute-done((f32[768,512]{1,0:T(8,128)S(1)}, f32[768,512]{1,0:T(8,128)}, u32[]{:S(2)}, u32[]{:S(2)}) %collective-permute-start.17) | collective-permute-done | bytes 1572896 | tf_op jit(solution)/shard_map/ppermute | solution.py:268
  61.9 1.5 %fusion.3 = (f32[384,512]{1,0:T(8,128)S(1)}, f32[384,512]{1,0:T(8,128)S(1)}) fusion(f32[768,512]{1,0:T(8,128)} %collective-permute-done.17), kind=kLoop, calls=%fused_computation.13 | loop fusion | bytes 3145728 | tf_op jit(solution)/shard_map/slice | solution.py:332
  63.8 1.4 %outer.5 = bf16[256,512]{1,0:T(8,128)(2,1)S(1)} custom-call(s32[1]{0:T(128)} %bitcast.23.at_ref, bf16[384,4096]{1,0:T(8,128)(2,1)} %own_ref.9, bf16[384,4096]{1,0:T(8,128)(2,1)} %collective-permute-done.16.sib_ref, bf16[768,512]{1,0:T(8,128)(2,1)S(1)} %fusion.projected_ref), custom_call_target="tpu_custom_call" | custom-call | flops 6039797760 | bytes 27525120 | tf_op jit(solution)/shard_map/outer/pallas_call | solution.py:157
  65.7 2.8 %outer.4 = (bf16[256,512]{1,0:T(8,128)(2,1)S(1)}, bf16[256,512]{1,0:T(8,128)(2,1)S(1)}, bf16[256,512]{1,0:T(8,128)(2,1)S(1)}) custom-call(s32[3]{0:T(128)S(1)} %pad_add_fusion.1.at_ref, bf16[384,4096]{1,0:T(8,128)(2,1)} %own_ref.9, bf16[384,4096]{1,0:T(8,128)(2,1)} %collective-permute-done.16.sib_ref, bf16[768,512]{1,0:T(8,128)(2,1)S(1)} %fusion.projected_ref), custom_call_target="tpu_custom_call" | custom-call | flops 18119393280 | bytes 82575360 | tf_op jit(solution)/shard_map/outer/pallas_call | solution.py:157
  68.5 1.8 %collective-permute-start.19 = (bf16[256,512]{1,0:T(8,128)(2,1)S(1)}, bf16[256,512]{1,0:T(8,128)(2,1)S(1)}, u32[]{:S(2)}, u32[]{:S(2)}) collective-permute-start(bf16[256,512]{1,0:T(8,128)(2,1)S(1)} %get-tuple-element.63), channel_id=1, source_target_pairs={{0,2},{1,3},{2,0},{3,1},{4,6},{5,7},{6,4},{7,5},{8,10},{9,11},{10,... | collective-permute-start | bytes 786440 | tf_op jit(solution)/shard_map/ppermute | solution.py:271
  70.6 3.3 %outer.3 = (f32[256,512]{1,0:T(8,128)S(1)}, f32[256,512]{1,0:T(8,128)S(1)}, f32[256,512]{1,0:T(8,128)S(1)}, f32[256,512]{1,0:T(8,128)S(1)}) custom-call(s32[4]{0:T(128)S(1)} %pad_add_fusion.at_ref, bf16[384,4096]{1,0:T(8,128)(2,1)} %own_ref.9, bf16[384,4096]{1,0:T(8,128)(2,1)} %collective-permute-done.16.sib_ref, bf16[768,512]{1,0:T(8,128)(2,1)S(1)} %fusion.projected_ref), custom_call_target="tpu_custom_call" | custom-call | flops 24159191040 | bytes 110100480 | tf_op jit(solution)/shard_map/outer/pallas_call | solution.py:157
  75.8 4.3 %collective-permute-done.19 = bf16[256,512]{1,0:T(8,128)(2,1)S(1)} collective-permute-done((bf16[256,512]{1,0:T(8,128)(2,1)S(1)}, bf16[256,512]{1,0:T(8,128)(2,1)S(1)}, u32[]{:S(2)}, u32[]{:S(2)}) %collective-permute-start.19) | collective-permute-done | bytes 262176 | tf_op jit(solution)/shard_map/ppermute | solution.py:271
  80.2 5.4 %collective-permute-start.20 = (bf16[256,512]{1,0:T(8,128)(2,1)S(1)}, bf16[256,512]{1,0:T(8,128)(2,1)S(1)}, u32[]{:S(2)}, u32[]{:S(2)}) collective-permute-start(bf16[256,512]{1,0:T(8,128)(2,1)S(1)} %add_convert_fusion.2), channel_id=1, source_target_pairs={{0,12},{1,13},{2,14},{3,15},{4,0},{5,1},{6,2},{7,3},{8,4},{9,5},{1... | collective-permute-start | bytes 786440 | tf_op jit(solution)/shard_map/ppermute | solution.py:274
  85.7 1.8 %collective-permute-done.23 = bf16[256,512]{1,0:T(8,128)(2,1)S(1)} collective-permute-done((bf16[256,512]{1,0:T(8,128)(2,1)S(1)}, bf16[256,512]{1,0:T(8,128)(2,1)S(1)}, u32[]{:S(2)}, u32[]{:S(2)}) %collective-permute-start.23) | collective-permute-done | bytes 262176 | tf_op jit(solution)/shard_map/ppermute | solution.py:274
  87.7 3.1 %collective-permute-done.18 = bf16[256,512]{1,0:T(8,128)(2,1)S(1)} collective-permute-done((bf16[256,512]{1,0:T(8,128)(2,1)S(1)}, bf16[256,512]{1,0:T(8,128)(2,1)S(1)}, u32[]{:S(2)}, u32[]{:S(2)}) %collective-permute-start.18) | collective-permute-done | bytes 262176 | tf_op jit(solution)/shard_map/ppermute | solution.py:271
  90.8 2.4 %collective-permute-done.20 = bf16[256,512]{1,0:T(8,128)(2,1)S(1)} collective-permute-done((bf16[256,512]{1,0:T(8,128)(2,1)S(1)}, bf16[256,512]{1,0:T(8,128)(2,1)S(1)}, u32[]{:S(2)}, u32[]{:S(2)}) %collective-permute-start.20) | collective-permute-done | bytes 262176 | tf_op jit(solution)/shard_map/ppermute | solution.py:274
  93.2 4.7 %collective-permute-done.24 = bf16[256,512]{1,0:T(8,128)(2,1)S(1)} collective-permute-done((bf16[256,512]{1,0:T(8,128)(2,1)S(1)}, bf16[256,512]{1,0:T(8,128)(2,1)S(1)}, u32[]{:S(2)}, u32[]{:S(2)}) %collective-permute-start.24) | collective-permute-done | bytes 262176 | tf_op jit(solution)/shard_map/ppermute | solution.py:274
  97.9 1.4 divide_convert_fusion
  99.8 1.6 %collective-permute-start.27 = (bf16[256,256]{1,0:T(8,128)(2,1)S(1)}, bf16[256,256]{1,0:T(8,128)(2,1)S(1)}, u32[]{:S(2)}, u32[]{:S(2)}) collective-permute-start(bf16[256,256]{1,0:T(8,128)(2,1)S(1)} %get-tuple-element.90.refs_1_), channel_id=1, source_target_pairs={{0,4},{1,5},{2,6},{3,7},{4,8},{5,9},{6,10},{7,11},{8,12},{9,13},{1... | collective-permute-start | bytes 393224 | tf_op jit(solution)/shard_map/ppermute | solution.py:274
  101.9 1.6 %collective-permute-start.25 = (bf16[256,256]{1,0:T(8,128)(2,1)S(1)}, bf16[256,256]{1,0:T(8,128)(2,1)S(1)}, u32[]{:S(2)}, u32[]{:S(2)}) collective-permute-start(bf16[256,256]{1,0:T(8,128)(2,1)S(1)} %get-tuple-element.91.refs_0_), channel_id=1, source_target_pairs={{0,4},{1,5},{2,6},{3,7},{4,8},{5,9},{6,10},{7,11},{8,12},{9,13},{1... | collective-permute-start | bytes 393224 | tf_op jit(solution)/shard_map/ppermute | solution.py:274
  103.5 1.8 %collective-permute-done.28.refs_3_ = bf16[256,256]{1,0:T(8,128)(2,1)S(1)} collective-permute-done((bf16[256,256]{1,0:T(8,128)(2,1)S(1)}, bf16[256,256]{1,0:T(8,128)(2,1)S(1)}, u32[]{:S(2)}, u32[]{:S(2)}) %collective-permute-start.28) | collective-permute-done | bytes 131104 | tf_op jit(solution)/shard_map/ppermute | solution.py:271
  105.2 2.0 %collective-permute-done.27.refs_5_ = bf16[256,256]{1,0:T(8,128)(2,1)S(1)} collective-permute-done((bf16[256,256]{1,0:T(8,128)(2,1)S(1)}, bf16[256,256]{1,0:T(8,128)(2,1)S(1)}, u32[]{:S(2)}, u32[]{:S(2)}) %collective-permute-start.27) | collective-permute-done | bytes 131104 | tf_op jit(solution)/shard_map/ppermute | solution.py:274
  107.2 1.6 %collective-permute-start.32 = (bf16[256,256]{1,0:T(8,128)(2,1)S(1)}, bf16[256,256]{1,0:T(8,128)(2,1)S(1)}, u32[]{:S(2)}, u32[]{:S(2)}) collective-permute-start(bf16[256,256]{1,0:T(8,128)(2,1)S(1)} %collective-permute-done.27.refs_5_), channel_id=1, source_target_pairs={{0,2},{1,3},{2,0},{3,1},{4,6},{5,7},{6,4},{7,5},{8,10},{9,11},{10,... | collective-permute-start | bytes 393224 | tf_op jit(solution)/shard_map/ppermute | solution.py:271
  108.8 1.4 %collective-permute-start.30 = (bf16[256,256]{1,0:T(8,128)(2,1)S(1)}, bf16[256,256]{1,0:T(8,128)(2,1)S(1)}, u32[]{:S(2)}, u32[]{:S(2)}) collective-permute-start(bf16[256,256]{1,0:T(8,128)(2,1)S(1)} %collective-permute-done.25.refs_4_), channel_id=1, source_target_pairs={{0,2},{1,3},{2,0},{3,1},{4,6},{5,7},{6,4},{7,5},{8,10},{9,11},{10,... | collective-permute-start | bytes 393224 | tf_op jit(solution)/shard_map/ppermute | solution.py:271
  112.2 3.4 %collective-permute-done.31.refs_9_ = bf16[256,256]{1,0:T(8,128)(2,1)S(1)} collective-permute-done((bf16[256,256]{1,0:T(8,128)(2,1)S(1)}, bf16[256,256]{1,0:T(8,128)(2,1)S(1)}, u32[]{:S(2)}, u32[]{:S(2)}) %collective-permute-start.31) | collective-permute-done | bytes 131104 | tf_op jit(solution)/shard_map/ppermute | solution.py:274
  116.0 2.3 %collective-permute-done.29.refs_8_ = bf16[256,256]{1,0:T(8,128)(2,1)S(1)} collective-permute-done((bf16[256,256]{1,0:T(8,128)(2,1)S(1)}, bf16[256,256]{1,0:T(8,128)(2,1)S(1)}, u32[]{:S(2)}, u32[]{:S(2)}) %collective-permute-start.29) | collective-permute-done | bytes 131104 | tf_op jit(solution)/shard_map/ppermute | solution.py:274
  118.3 2.2 %collective-permute-done.36.refs_11_ = bf16[256,256]{1,0:T(8,128)(2,1)S(1)} collective-permute-done((bf16[256,256]{1,0:T(8,128)(2,1)S(1)}, bf16[256,256]{1,0:T(8,128)(2,1)S(1)}, u32[]{:S(2)}, u32[]{:S(2)}) %collective-permute-start.36) | collective-permute-done | bytes 131104 | tf_op jit(solution)/shard_map/ppermute | solution.py:271
  120.5 2.3 %collective-permute-done.35.refs_13_ = bf16[256,256]{1,0:T(8,128)(2,1)S(1)} collective-permute-done((bf16[256,256]{1,0:T(8,128)(2,1)S(1)}, bf16[256,256]{1,0:T(8,128)(2,1)S(1)}, u32[]{:S(2)}, u32[]{:S(2)}) %collective-permute-start.35) | collective-permute-done | bytes 131104 | tf_op jit(solution)/shard_map/ppermute | solution.py:274
  123.2 1.8 %collective-permute-done.33.refs_12_ = bf16[256,256]{1,0:T(8,128)(2,1)S(1)} collective-permute-done((bf16[256,256]{1,0:T(8,128)(2,1)S(1)}, bf16[256,256]{1,0:T(8,128)(2,1)S(1)}, u32[]{:S(2)}, u32[]{:S(2)}) %collective-permute-start.33) | collective-permute-done | bytes 131104 | tf_op jit(solution)/shard_map/ppermute | solution.py:274
  125.0 4.9 %back.2 = (bf16[4096,512]{1,0:T(8,128)(2,1)}, bf16[1792,512]{1,0:T(8,128)(2,1)}) custom-call(s32[7]{0:T(128)S(1)} %stack.95.at_ref, bf16[512,1024]{1,0:T(8,128)(2,1)S(1)} %pad_maximum_fusion.projector_ref, bf16[256,256]{1,0:T(8,128)(2,1)S(1)} %get-tuple-element.91.refs_0_, bf16[256,256]{1,0:T(8,128)(2,1)S(1)} %get-tuple-element.90.refs_1_, ...), custom_call_target="tpu_custom_call" | custom-call | flops 56371445760 | bytes 165150720 | tf_op jit(solution)/shard_map/back/pallas_call | solution.py:66
  130.0 1.4 collective-permute-start.39
  132.2 3.7 %collective-permute-done.39.refs_1_ = bf16[256,256]{1,0:T(8,128)(2,1)S(1)} collective-permute-done((bf16[256,256]{1,0:T(8,128)(2,1)S(1)}, bf16[256,256]{1,0:T(8,128)(2,1)S(1)}, u32[]{:S(2)}, u32[]{:S(2)}) %collective-permute-start.39) | collective-permute-done | bytes 131104 | tf_op jit(solution)/shard_map/ppermute | solution.py:274
  138.5 1.4 collective-permute-done.40.refs_1_
  139.9 2.1 %place.1 = bf16[4096,512]{1,0:T(8,128)(2,1)} custom-call(s32[8]{0:T(128)S(1)} %stack.87.at_ref, bf16[1792,512]{1,0:T(8,128)(2,1)S(1)} %collective-permute-done.37.refs_0_, bf16[256,512]{1,0:T(8,128)(2,1)S(1)} %collective-permute-done.40.refs_1_, bf16[4096,512]{1,0:T(8,128)(2,1)} %get-tuple-element.82.refs_2_), custom_call_target="tpu_custom_call", output_to_operand_aliasing={{}: (3, {})} | custom-call | bytes 125829120 | tf_op jit(solution)/shard_map/place/pallas_call | solution.py:66
  (67 shorter events, 16.0 us)
Async XLA Ops:
  0.6 45.1 %collective-permute-start = (bf16[384,8192]{1,0:T(8,128)(2,1)}, bf16[384,8192]{1,0:T(8,128)(2,1)}, u32[]{:S(2)}, u32[]{:S(2)}) collective-permute-start(bf16[384,8192]{1,0:T(8,128)(2,1)} %own_ref.6), channel_id=1, source_target_pairs={{0,1},{1,0},{2,3},{3,2},{4,5},{5,4},{6,7},{7,6},{8,9},{9,8},{10,11... | collective-permute-start | bytes 18874376 | tf_op jit(solution)/shard_map/ppermute | solution.py:268
  2.2 9.8 %collective-permute-start.9 = (bf16[512,256]{1,0:T(8,128)(2,1)S(1)}, bf16[512,256]{1,0:T(8,128)(2,1)S(1)}, u32[]{:S(2)}, u32[]{:S(2)}) collective-permute-start(bf16[512,256]{1,0:T(8,128)(2,1)S(1)} %get-tuple-element.88.refs_7_), channel_id=1, source_target_pairs={{0,2},{1,3},{2,0},{3,1},{4,6},{5,7},{6,4},{7,5},{8,10},{9,11},{10,... | collective-permute-start | bytes 786440 | tf_op jit(solution)/shard_map/ppermute | solution.py:271
  4.8 10.9 %collective-permute-start.8 = (bf16[512,256]{1,0:T(8,128)(2,1)S(1)}, bf16[512,256]{1,0:T(8,128)(2,1)S(1)}, u32[]{:S(2)}, u32[]{:S(2)}) collective-permute-start(bf16[512,256]{1,0:T(8,128)(2,1)S(1)} %get-tuple-element.88.refs_7_), channel_id=1, source_target_pairs={{0,4},{1,5},{2,6},{3,7},{4,8},{5,9},{6,10},{7,11},{8,12},{9,13},{1... | collective-permute-start | bytes 786440 | tf_op jit(solution)/shard_map/ppermute | solution.py:274
  6.4 11.2 %collective-permute-start.2 = (bf16[512,256]{1,0:T(8,128)(2,1)S(1)}, bf16[512,256]{1,0:T(8,128)(2,1)S(1)}, u32[]{:S(2)}, u32[]{:S(2)}) collective-permute-start(bf16[512,256]{1,0:T(8,128)(2,1)S(1)} %get-tuple-element.89.refs_0_), channel_id=1, source_target_pairs={{0,2},{1,3},{2,0},{3,1},{4,6},{5,7},{6,4},{7,5},{8,10},{9,11},{10,... | collective-permute-start | bytes 786440 | tf_op jit(solution)/shard_map/ppermute | solution.py:271
  6.9 14.5 %collective-permute-start.1 = (bf16[512,256]{1,0:T(8,128)(2,1)S(1)}, bf16[512,256]{1,0:T(8,128)(2,1)S(1)}, u32[]{:S(2)}, u32[]{:S(2)}) collective-permute-start(bf16[512,256]{1,0:T(8,128)(2,1)S(1)} %get-tuple-element.89.refs_0_), channel_id=1, source_target_pairs={{0,4},{1,5},{2,6},{3,7},{4,8},{5,9},{6,10},{7,11},{8,12},{9,13},{1... | collective-permute-start | bytes 786440 | tf_op jit(solution)/shard_map/ppermute | solution.py:274
  15.7 7.4 %collective-permute-start.12 = (bf16[512,256]{1,0:T(8,128)(2,1)S(1)}, bf16[512,256]{1,0:T(8,128)(2,1)S(1)}, u32[]{:S(2)}, u32[]{:S(2)}) collective-permute-start(bf16[512,256]{1,0:T(8,128)(2,1)S(1)} %collective-permute-done.8.refs_9_), channel_id=1, source_target_pairs={{0,2},{1,3},{2,0},{3,1},{4,6},{5,7},{6,4},{7,5},{8,10},{9,11},{10,... | collective-permute-start | bytes 786440 | tf_op jit(solution)/shard_map/ppermute | solution.py:271
  16.0 11.0 %collective-permute-start.11 = (bf16[512,256]{1,0:T(8,128)(2,1)S(1)}, bf16[512,256]{1,0:T(8,128)(2,1)S(1)}, u32[]{:S(2)}, u32[]{:S(2)}) collective-permute-start(bf16[512,256]{1,0:T(8,128)(2,1)S(1)} %collective-permute-done.8.refs_9_), channel_id=1, source_target_pairs={{0,4},{1,5},{2,6},{3,7},{4,8},{5,9},{6,10},{7,11},{8,12},{9,13},{1... | collective-permute-start | bytes 786440 | tf_op jit(solution)/shard_map/ppermute | solution.py:274
  21.4 7.4 %collective-permute-start.4 = (bf16[512,256]{1,0:T(8,128)(2,1)S(1)}, bf16[512,256]{1,0:T(8,128)(2,1)S(1)}, u32[]{:S(2)}, u32[]{:S(2)}) collective-permute-start(bf16[512,256]{1,0:T(8,128)(2,1)S(1)} %collective-permute-done.1.refs_2_), channel_id=1, source_target_pairs={{0,2},{1,3},{2,0},{3,1},{4,6},{5,7},{6,4},{7,5},{8,10},{9,11},{10,... | collective-permute-start | bytes 786440 | tf_op jit(solution)/shard_map/ppermute | solution.py:271
  21.6 11.0 %collective-permute-start.3 = (bf16[512,256]{1,0:T(8,128)(2,1)S(1)}, bf16[512,256]{1,0:T(8,128)(2,1)S(1)}, u32[]{:S(2)}, u32[]{:S(2)}) collective-permute-start(bf16[512,256]{1,0:T(8,128)(2,1)S(1)} %collective-permute-done.1.refs_2_), channel_id=1, source_target_pairs={{0,4},{1,5},{2,6},{3,7},{4,8},{5,9},{6,10},{7,11},{8,12},{9,13},{1... | collective-permute-start | bytes 786440 | tf_op jit(solution)/shard_map/ppermute | solution.py:274
  27.0 7.4 %collective-permute-start.14 = (bf16[512,256]{1,0:T(8,128)(2,1)S(1)}, bf16[512,256]{1,0:T(8,128)(2,1)S(1)}, u32[]{:S(2)}, u32[]{:S(2)}) collective-permute-start(bf16[512,256]{1,0:T(8,128)(2,1)S(1)} %collective-permute-done.11.refs_11_), channel_id=1, source_target_pairs={{0,2},{1,3},{2,0},{3,1},{4,6},{5,7},{6,4},{7,5},{8,10},{9,11},{10,... | collective-permute-start | bytes 786440 | tf_op jit(solution)/shard_map/ppermute | solution.py:271
  27.3 11.2 %collective-permute-start.13 = (bf16[512,256]{1,0:T(8,128)(2,1)S(1)}, bf16[512,256]{1,0:T(8,128)(2,1)S(1)}, u32[]{:S(2)}, u32[]{:S(2)}) collective-permute-start(bf16[512,256]{1,0:T(8,128)(2,1)S(1)} %collective-permute-done.11.refs_11_), channel_id=1, source_target_pairs={{0,4},{1,5},{2,6},{3,7},{4,8},{5,9},{6,10},{7,11},{8,12},{9,13},{1... | collective-permute-start | bytes 786440 | tf_op jit(solution)/shard_map/ppermute | solution.py:274
  32.6 7.4 %collective-permute-start.6 = (bf16[512,256]{1,0:T(8,128)(2,1)S(1)}, bf16[512,256]{1,0:T(8,128)(2,1)}, u32[]{:S(2)}, u32[]{:S(2)}) collective-permute-start(bf16[512,256]{1,0:T(8,128)(2,1)S(1)} %collective-permute-done.3.refs_4_), channel_id=1, source_target_pairs={{0,2},{1,3},{2,0},{3,1},{4,6},{5,7},{6,4},{7,5},{8,10},{9,11},{10,... | collective-permute-start | bytes 786440 | tf_op jit(solution)/shard_map/ppermute | solution.py:271
  32.9 11.1 %collective-permute-start.5 = (bf16[512,256]{1,0:T(8,128)(2,1)S(1)}, bf16[512,256]{1,0:T(8,128)(2,1)S(1)}, u32[]{:S(2)}, u32[]{:S(2)}) collective-permute-start(bf16[512,256]{1,0:T(8,128)(2,1)S(1)} %collective-permute-done.3.refs_4_), channel_id=1, source_target_pairs={{0,4},{1,5},{2,6},{3,7},{4,8},{5,9},{6,10},{7,11},{8,12},{9,13},{1... | collective-permute-start | bytes 786440 | tf_op jit(solution)/shard_map/ppermute | solution.py:274
  34.4 19.8 %collective-permute-start.10 = (bf16[512,256]{1,0:T(8,128)(2,1)S(1)}, bf16[512,256]{1,0:T(8,128)(2,1)}, u32[]{:S(2)}, u32[]{:S(2)}) collective-permute-start(bf16[512,256]{1,0:T(8,128)(2,1)S(1)} %collective-permute-done.9.refs_8_), channel_id=1, source_target_pairs={{0,12},{1,13},{2,14},{3,15},{4,0},{5,1},{6,2},{7,3},{8,4},{9,5},{1... | collective-permute-start | bytes 786440 | tf_op jit(solution)/shard_map/ppermute | solution.py:274
  44.0 10.2 %collective-permute-start.7 = (bf16[512,256]{1,0:T(8,128)(2,1)S(1)}, bf16[512,256]{1,0:T(8,128)(2,1)}, u32[]{:S(2)}, u32[]{:S(2)}) collective-permute-start(bf16[512,256]{1,0:T(8,128)(2,1)S(1)} %collective-permute-done.5.refs_6_), channel_id=1, source_target_pairs={{0,2},{1,3},{2,0},{3,1},{4,6},{5,7},{6,4},{7,5},{8,10},{9,11},{10,... | collective-permute-start | bytes 786440 | tf_op jit(solution)/shard_map/ppermute | solution.py:271
  47.8 5.9 %collective-permute-start.15 = (bf16[512,512]{0,1:T(8,128)(2,1)}, bf16[512,512]{0,1:T(8,128)(2,1)S(1)}, u32[]{:S(2)}, u32[]{:S(2)}) collective-permute-start(bf16[512,512]{0,1:T(8,128)(2,1)} %copy.11), channel_id=1, source_target_pairs={{0,1},{1,0},{2,3},{3,2},{4,5},{5,4},{6,7},{7,6},{8,9},{9,8},{10,11... | collective-permute-start | bytes 1572872 | tf_op jit(solution)/shard_map/ppermute | solution.py:268
  53.6 0.8 copy-start.3
  53.7 10.1 %collective-permute-start.16 = (bf16[384,4096]{1,0:T(8,128)(2,1)}, bf16[384,4096]{1,0:T(8,128)(2,1)}, u32[]{:S(2)}, u32[]{:S(2)}) collective-permute-start(bf16[384,4096]{1,0:T(8,128)(2,1)} %own_ref.9), channel_id=1, source_target_pairs={{0,1},{1,0},{2,3},{3,2},{4,5},{5,4},{6,7},{7,6},{8,9},{9,8},{10,11... | collective-permute-start | bytes 9437192 | tf_op jit(solution)/shard_map/ppermute | solution.py:268
  54.4 2.8 %copy-start = (bf16[512,512]{1,0:T(8,128)(2,1)S(1)}, bf16[512,512]{1,0:T(8,128)(2,1)}, u32[]{:S(2)}) copy-start(bf16[512,512]{1,0:T(8,128)(2,1)} %param.7) | copy-start | bytes 1572868
  54.4 3.1 %copy-start.4 = (bf16[512,512]{0,1:T(8,128)(2,1)S(1)}, bf16[512,512]{0,1:T(8,128)(2,1)}, u32[]{:S(2)}) copy-start(bf16[512,512]{0,1:T(8,128)(2,1)} %copy-done.3) | copy-start | bytes 1572868
  56.6 5.3 %collective-permute-start.17 = (f32[768,512]{1,0:T(8,128)S(1)}, f32[768,512]{1,0:T(8,128)}, u32[]{:S(2)}, u32[]{:S(2)}) collective-permute-start(f32[768,512]{1,0:T(8,128)S(1)} %project.3), channel_id=1, source_target_pairs={{0,1},{1,0},{2,3},{3,2},{4,5},{5,4},{6,7},{7,6},{8,9},{9,8},{10,11... | collective-permute-start | bytes 4718600 | tf_op jit(solution)/shard_map/ppermute | solution.py:268
  65.3 9.2 %collective-permute-start.22 = (bf16[256,512]{1,0:T(8,128)(2,1)S(1)}, bf16[256,512]{1,0:T(8,128)(2,1)S(1)}, u32[]{:S(2)}, u32[]{:S(2)}) collective-permute-start(bf16[256,512]{1,0:T(8,128)(2,1)S(1)} %outer.5), channel_id=1, source_target_pairs={{0,2},{1,3},{2,0},{3,1},{4,6},{5,7},{6,4},{7,5},{8,10},{9,11},{10,... | collective-permute-start | bytes 786440 | tf_op jit(solution)/shard_map/ppermute | solution.py:271
  68.5 11.6 %collective-permute-start.19 = (bf16[256,512]{1,0:T(8,128)(2,1)S(1)}, bf16[256,512]{1,0:T(8,128)(2,1)S(1)}, u32[]{:S(2)}, u32[]{:S(2)}) collective-permute-start(bf16[256,512]{1,0:T(8,128)(2,1)S(1)} %get-tuple-element.63), channel_id=1, source_target_pairs={{0,2},{1,3},{2,0},{3,1},{4,6},{5,7},{6,4},{7,5},{8,10},{9,11},{10,... | collective-permute-start | bytes 786440 | tf_op jit(solution)/shard_map/ppermute | solution.py:271
  70.3 15.4 %collective-permute-start.21 = (bf16[256,512]{1,0:T(8,128)(2,1)S(1)}, bf16[256,512]{1,0:T(8,128)(2,1)S(1)}, u32[]{:S(2)}, u32[]{:S(2)}) collective-permute-start(bf16[256,512]{1,0:T(8,128)(2,1)S(1)} %get-tuple-element.65), channel_id=1, source_target_pairs={{0,2},{1,3},{2,0},{3,1},{4,6},{5,7},{6,4},{7,5},{8,10},{9,11},{10,... | collective-permute-start | bytes 786440 | tf_op jit(solution)/shard_map/ppermute | solution.py:271
  73.8 24.0 %copy-start.1 = (f32[256,512]{1,0:T(8,128)S(1)}, f32[256,512]{1,0:T(8,128)}, u32[]{:S(2)}) copy-start(f32[256,512]{1,0:T(8,128)} %param.8) | copy-start | bytes 1572868
  73.9 24.0 %copy-start.2 = (f32[256,512]{1,0:T(8,128)S(1)}, f32[256,512]{1,0:T(8,128)}, u32[]{:S(2)}) copy-start(f32[256,512]{1,0:T(8,128)} %param.9) | copy-start | bytes 1572868
  74.6 13.0 %collective-permute-start.23 = (bf16[256,512]{1,0:T(8,128)(2,1)S(1)}, bf16[256,512]{1,0:T(8,128)(2,1)S(1)}, u32[]{:S(2)}, u32[]{:S(2)}) collective-permute-start(bf16[256,512]{1,0:T(8,128)(2,1)S(1)} %add_convert_fusion.1), channel_id=1, source_target_pairs={{0,4},{1,5},{2,6},{3,7},{4,8},{5,9},{6,10},{7,11},{8,12},{9,13},{1... | collective-permute-start | bytes 786440 | tf_op jit(solution)/shard_map/ppermute | solution.py:274
  74.6 16.2 %collective-permute-start.18 = (bf16[256,512]{1,0:T(8,128)(2,1)S(1)}, bf16[256,512]{1,0:T(8,128)(2,1)S(1)}, u32[]{:S(2)}, u32[]{:S(2)}) collective-permute-start(bf16[256,512]{1,0:T(8,128)(2,1)S(1)} %get-tuple-element.61), channel_id=1, source_target_pairs={{0,2},{1,3},{2,0},{3,1},{4,6},{5,7},{6,4},{7,5},{8,10},{9,11},{10,... | collective-permute-start | bytes 786440 | tf_op jit(solution)/shard_map/ppermute | solution.py:271
  80.2 13.0 %collective-permute-start.20 = (bf16[256,512]{1,0:T(8,128)(2,1)S(1)}, bf16[256,512]{1,0:T(8,128)(2,1)S(1)}, u32[]{:S(2)}, u32[]{:S(2)}) collective-permute-start(bf16[256,512]{1,0:T(8,128)(2,1)S(1)} %add_convert_fusion.2), channel_id=1, source_target_pairs={{0,12},{1,13},{2,14},{3,15},{4,0},{5,1},{6,2},{7,3},{8,4},{9,5},{1... | collective-permute-start | bytes 786440 | tf_op jit(solution)/shard_map/ppermute | solution.py:274
  87.6 10.2 %collective-permute-start.24 = (bf16[256,512]{1,0:T(8,128)(2,1)S(1)}, bf16[256,512]{1,0:T(8,128)(2,1)S(1)}, u32[]{:S(2)}, u32[]{:S(2)}) collective-permute-start(bf16[256,512]{1,0:T(8,128)(2,1)S(1)} %add_convert_fusion), channel_id=1, source_target_pairs={{0,4},{1,5},{2,6},{3,7},{4,8},{5,9},{6,10},{7,11},{8,12},{9,13},{1... | collective-permute-start | bytes 786440 | tf_op jit(solution)/shard_map/ppermute | solution.py:274
  99.3 5.9 %collective-permute-start.28 = (bf16[256,256]{1,0:T(8,128)(2,1)S(1)}, bf16[256,256]{1,0:T(8,128)(2,1)S(1)}, u32[]{:S(2)}, u32[]{:S(2)}) collective-permute-start(bf16[256,256]{1,0:T(8,128)(2,1)S(1)} %get-tuple-element.90.refs_1_), channel_id=1, source_target_pairs={{0,2},{1,3},{2,0},{3,1},{4,6},{5,7},{6,4},{7,5},{8,10},{9,11},{10,... | collective-permute-start | bytes 393224 | tf_op jit(solution)/shard_map/ppermute | solution.py:271
  99.8 7.4 %collective-permute-start.27 = (bf16[256,256]{1,0:T(8,128)(2,1)S(1)}, bf16[256,256]{1,0:T(8,128)(2,1)S(1)}, u32[]{:S(2)}, u32[]{:S(2)}) collective-permute-start(bf16[256,256]{1,0:T(8,128)(2,1)S(1)} %get-tuple-element.90.refs_1_), channel_id=1, source_target_pairs={{0,4},{1,5},{2,6},{3,7},{4,8},{5,9},{6,10},{7,11},{8,12},{9,13},{1... | collective-permute-start | bytes 393224 | tf_op jit(solution)/shard_map/ppermute | solution.py:274
  101.4 7.4 %collective-permute-start.26 = (bf16[256,256]{1,0:T(8,128)(2,1)S(1)}, bf16[256,256]{1,0:T(8,128)(2,1)S(1)}, u32[]{:S(2)}, u32[]{:S(2)}) collective-permute-start(bf16[256,256]{1,0:T(8,128)(2,1)S(1)} %get-tuple-element.91.refs_0_), channel_id=1, source_target_pairs={{0,2},{1,3},{2,0},{3,1},{4,6},{5,7},{6,4},{7,5},{8,10},{9,11},{10,... | collective-permute-start | bytes 393224 | tf_op jit(solution)/shard_map/ppermute | solution.py:271
  101.9 6.9 %collective-permute-start.25 = (bf16[256,256]{1,0:T(8,128)(2,1)S(1)}, bf16[256,256]{1,0:T(8,128)(2,1)S(1)}, u32[]{:S(2)}, u32[]{:S(2)}) collective-permute-start(bf16[256,256]{1,0:T(8,128)(2,1)S(1)} %get-tuple-element.91.refs_0_), channel_id=1, source_target_pairs={{0,4},{1,5},{2,6},{3,7},{4,8},{5,9},{6,10},{7,11},{8,12},{9,13},{1... | collective-permute-start | bytes 393224 | tf_op jit(solution)/shard_map/ppermute | solution.py:274
  107.2 5.0 %collective-permute-start.32 = (bf16[256,256]{1,0:T(8,128)(2,1)S(1)}, bf16[256,256]{1,0:T(8,128)(2,1)S(1)}, u32[]{:S(2)}, u32[]{:S(2)}) collective-permute-start(bf16[256,256]{1,0:T(8,128)(2,1)S(1)} %collective-permute-done.27.refs_5_), channel_id=1, source_target_pairs={{0,2},{1,3},{2,0},{3,1},{4,6},{5,7},{6,4},{7,5},{8,10},{9,11},{10,... | collective-permute-start | bytes 393224 | tf_op jit(solution)/shard_map/ppermute | solution.py:271
  108.8 6.8 %collective-permute-start.31 = (bf16[256,256]{1,0:T(8,128)(2,1)S(1)}, bf16[256,256]{1,0:T(8,128)(2,1)S(1)}, u32[]{:S(2)}, u32[]{:S(2)}) collective-permute-start(bf16[256,256]{1,0:T(8,128)(2,1)S(1)} %collective-permute-done.27.refs_5_), channel_id=1, source_target_pairs={{0,4},{1,5},{2,6},{3,7},{4,8},{5,9},{6,10},{7,11},{8,12},{9,13},{1... | collective-permute-start | bytes 393224 | tf_op jit(solution)/shard_map/ppermute | solution.py:274
  108.8 7.2 %collective-permute-start.30 = (bf16[256,256]{1,0:T(8,128)(2,1)S(1)}, bf16[256,256]{1,0:T(8,128)(2,1)S(1)}, u32[]{:S(2)}, u32[]{:S(2)}) collective-permute-start(bf16[256,256]{1,0:T(8,128)(2,1)S(1)} %collective-permute-done.25.refs_4_), channel_id=1, source_target_pairs={{0,2},{1,3},{2,0},{3,1},{4,6},{5,7},{6,4},{7,5},{8,10},{9,11},{10,... | collective-permute-start | bytes 393224 | tf_op jit(solution)/shard_map/ppermute | solution.py:271
  110.2 8.0 %collective-permute-start.29 = (bf16[256,256]{1,0:T(8,128)(2,1)S(1)}, bf16[256,256]{1,0:T(8,128)(2,1)S(1)}, u32[]{:S(2)}, u32[]{:S(2)}) collective-permute-start(bf16[256,256]{1,0:T(8,128)(2,1)S(1)} %collective-permute-done.25.refs_4_), channel_id=1, source_target_pairs={{0,4},{1,5},{2,6},{3,7},{4,8},{5,9},{6,10},{7,11},{8,12},{9,13},{1... | collective-permute-start | bytes 393224 | tf_op jit(solution)/shard_map/ppermute | solution.py:274
  115.5 5.0 %collective-permute-start.36 = (bf16[256,256]{1,0:T(8,128)(2,1)S(1)}, bf16[256,256]{1,0:T(8,128)(2,1)S(1)}, u32[]{:S(2)}, u32[]{:S(2)}) collective-permute-start(bf16[256,256]{1,0:T(8,128)(2,1)S(1)} %collective-permute-done.31.refs_9_), channel_id=1, source_target_pairs={{0,2},{1,3},{2,0},{3,1},{4,6},{5,7},{6,4},{7,5},{8,10},{9,11},{10,... | collective-permute-start | bytes 393224 | tf_op jit(solution)/shard_map/ppermute | solution.py:271
  116.0 6.8 %collective-permute-start.35 = (bf16[256,256]{1,0:T(8,128)(2,1)S(1)}, bf16[256,256]{1,0:T(8,128)(2,1)S(1)}, u32[]{:S(2)}, u32[]{:S(2)}) collective-permute-start(bf16[256,256]{1,0:T(8,128)(2,1)S(1)} %collective-permute-done.31.refs_9_), channel_id=1, source_target_pairs={{0,4},{1,5},{2,6},{3,7},{4,8},{5,9},{6,10},{7,11},{8,12},{9,13},{1... | collective-permute-start | bytes 393224 | tf_op jit(solution)/shard_map/ppermute | solution.py:274
  118.3 5.0 %collective-permute-start.34 = (bf16[256,256]{1,0:T(8,128)(2,1)S(1)}, bf16[256,256]{1,0:T(8,128)(2,1)S(1)}, u32[]{:S(2)}, u32[]{:S(2)}) collective-permute-start(bf16[256,256]{1,0:T(8,128)(2,1)S(1)} %collective-permute-done.29.refs_8_), channel_id=1, source_target_pairs={{0,2},{1,3},{2,0},{3,1},{4,6},{5,7},{6,4},{7,5},{8,10},{9,11},{10,... | collective-permute-start | bytes 393224 | tf_op jit(solution)/shard_map/ppermute | solution.py:271
  118.3 6.8 %collective-permute-start.33 = (bf16[256,256]{1,0:T(8,128)(2,1)S(1)}, bf16[256,256]{1,0:T(8,128)(2,1)S(1)}, u32[]{:S(2)}, u32[]{:S(2)}) collective-permute-start(bf16[256,256]{1,0:T(8,128)(2,1)S(1)} %collective-permute-done.29.refs_8_), channel_id=1, source_target_pairs={{0,4},{1,5},{2,6},{3,7},{4,8},{5,9},{6,10},{7,11},{8,12},{9,13},{1... | collective-permute-start | bytes 393224 | tf_op jit(solution)/shard_map/ppermute | solution.py:274
  129.9 9.9 %collective-permute-start.37 = (bf16[1792,512]{1,0:T(8,128)(2,1)}, bf16[1792,512]{1,0:T(8,128)(2,1)S(1)}, u32[]{:S(2)}, u32[]{:S(2)}) collective-permute-start(bf16[1792,512]{1,0:T(8,128)(2,1)} %get-tuple-element.79), channel_id=1, source_target_pairs={{0,1},{1,0},{2,3},{3,2},{4,5},{5,4},{6,7},{7,6},{8,9},{9,8},{10,11... | collective-permute-start | bytes 5505032 | tf_op jit(solution)/shard_map/ppermute | solution.py:268
  130.0 5.9 %collective-permute-start.39 = (bf16[256,256]{1,0:T(8,128)(2,1)S(1)}, bf16[256,256]{1,0:T(8,128)(2,1)S(1)}, u32[]{:S(2)}, u32[]{:S(2)}) collective-permute-start(bf16[256,256]{1,0:T(8,128)(2,1)S(1)} %collective-permute-done.28.refs_3_), channel_id=1, source_target_pairs={{0,12},{1,13},{2,14},{3,15},{4,0},{5,1},{6,2},{7,3},{8,4},{9,5},{1... | collective-permute-start | bytes 393224 | tf_op jit(solution)/shard_map/ppermute | solution.py:274
  131.4 5.6 %collective-permute-start.38 = (bf16[256,256]{1,0:T(8,128)(2,1)S(1)}, bf16[256,256]{1,0:T(8,128)(2,1)S(1)}, u32[]{:S(2)}, u32[]{:S(2)}) collective-permute-start(bf16[256,256]{1,0:T(8,128)(2,1)S(1)} %collective-permute-done.33.refs_12_), channel_id=1, source_target_pairs={{0,2},{1,3},{2,0},{3,1},{4,6},{5,7},{6,4},{7,5},{8,10},{9,11},{10,... | collective-permute-start | bytes 393224 | tf_op jit(solution)/shard_map/ppermute | solution.py:271
  138.3 1.6 %collective-permute-start.40 = (bf16[256,512]{1,0:T(8,128)(2,1)S(1)}, bf16[256,512]{1,0:T(8,128)(2,1)S(1)}, u32[]{:S(2)}, u32[]{:S(2)}) collective-permute-start(bf16[256,512]{1,0:T(8,128)(2,1)S(1)} %get-tuple-element.81), channel_id=1, source_target_pairs={{0,1},{1,0},{2,3},{3,2},{4,5},{5,4},{6,7},{7,6},{8,9},{9,8},{10,11... | collective-permute-start | bytes 786440 | tf_op jit(solution)/shard_map/ppermute | solution.py:268

commit v7 on v6

v7 whole, which is shorter than its diff:
```python
import functools
import jax
import jax.numpy as jnp
from jax import lax
from jax.experimental import pallas as pl
from jax.experimental.pallas import tpu as pltpu
from jax.sharding import PartitionSpec as P

STEP = 100

decay_first = 0.9
decay_second = 0.999
epsilon = 1e-08

CHUNKS = 2
W_EARLY, W_LATE, W_OUTER, W_BACK, W_LAST = 30, 30, 30, 30, 30000
F32, BF16 = jnp.float32, jnp.bfloat16
VMEM_LIMIT = 16 * 1024 * 1024


def adam(reduced, first_moment, second_moment):
    new_first = decay_first * first_moment + (1.0 - decay_first) * reduced
    new_second = decay_second * second_moment + (1.0 - decay_second) * reduced * reduced
    first_fix = 1.0 - decay_first**STEP
    second_fix = 1.0 - decay_second**STEP
    direction = (new_first / first_fix / (jnp.sqrt(new_second / second_fix) + epsilon)).astype(BF16)
    return new_first, new_second, direction


def plain(activations, out_grads, projector, first_moment, second_moment):
    projected = jnp.dot(
        activations,
        lax.all_gather(projector, "dp", axis=0, tiled=True),
        preferred_element_type=F32,
    ).astype(BF16)
    reduced = lax.psum_scatter(
        lax.dot_general(out_grads, projected, (((0,), (0,)), ((), ())), preferred_element_type=F32),
        "dp",
        scatter_dimension=0,
        tiled=True,
    )
    new_first, new_second, direction = adam(reduced, first_moment, second_moment)
    update = lax.dot_general(
        lax.all_gather(direction, "dp", axis=0, tiled=True),
        projector,
        (((1,), (1,)), ((), ())),
        preferred_element_type=F32,
    ).astype(BF16)
    return update, new_first, new_second


def params():
    return pltpu.CompilerParams(vmem_limit_bytes=VMEM_LIMIT)


def cost(weight, flops, moved):
    return pl.CostEstimate(flops=weight * flops, bytes_accessed=weight * moved, transcendentals=0)


def pinned(x):
    return pltpu.with_memory_space_constraint(x, pltpu.HBM)


def call(kernel, scalars, arrays, outs, scratch, *, weight, flops, moved, name, aliases=None, in_hbm=0):
    anywhere = pl.BlockSpec(memory_space=pl.ANY)
    return pl.pallas_call(
        kernel,
        grid_spec=pltpu.PrefetchScalarGridSpec(
            num_scalar_prefetch=1,
            grid=(),
            in_specs=[anywhere] * len(arrays),
            out_specs=[anywhere] * len(outs),
            scratch_shapes=scratch,
        ),
        out_shape=outs,
        input_output_aliases=aliases or {},
        compiler_params=params(),
        cost_estimate=cost(weight, flops, moved),
        name=name,
    )(scalars, *[pinned(x) for x in arrays[:in_hbm]], *arrays[in_hbm:])


def project(activations, sibling, at, blocks, before, weight):
    chunks, many = len(blocks), at.shape[0]
    flat = [chunk[j] for chunk in blocks for j in sorted(chunk)]
    (depth, cols), rows = flat[0].shape, activations.shape[0]
    held = [] if before is None else [before]
    copies = 2 * many + len(flat) + len(held)

    def kernel(at_ref, own_ref, sib_ref, *refs):
        block_refs, out_ref = refs[: len(flat)], refs[len(flat) + len(held)]
        a, b, total, sems = refs[len(flat) + len(held) + 1 :]
        started = []

        def start(source, target):
            started.append(pltpu.make_async_copy(source, target, sems.at[len(started)]))
            started[-1].start()

        core = lax.rem(lax.axis_index("dp"), 2)
        here, there = (pl.ds(pl.multiple_of(c * rows, rows), rows) for c in (core, 1 - core))
        for j in range(many):
            columns = pl.ds(pl.multiple_of(at_ref[j] * depth, depth), depth)
            start(own_ref.at[:, columns], a.at[here, pl.ds(j * depth, depth)])
            start(sib_ref.at[:, columns], a.at[there, pl.ds(j * depth, depth)])
        places = [(i, j) for i, chunk in enumerate(blocks) for j in sorted(chunk)]
        for ref, (i, j) in zip(block_refs, places):
            start(ref, b.at[pl.ds(j * depth, depth), pl.ds(i * cols, cols)])
        if held:
            start(refs[len(flat)], total)
        for copy in started:
            copy.wait()
        for i, chunk in enumerate(blocks):
            part = slice(i * cols, (i + 1) * cols)
            deep = slice(min(chunk) * depth, (max(chunk) + 1) * depth)
            term = jnp.dot(a[:, deep], b[deep, part], preferred_element_type=F32)
            total[:, part] = total[:, part] + term if held else term
        back_copy = pltpu.make_async_copy(total, out_ref, sems.at[copies])
        back_copy.start()
        back_copy.wait()

    wide = chunks * cols
    return call(
        kernel,
        at,
        [activations, sibling, *flat, *held],
        [jax.ShapeDtypeStruct((2 * rows, wide), F32)],
        [
            pltpu.VMEM((2 * rows, many * depth), BF16),
            pltpu.VMEM((many * depth, wide), BF16),
            pltpu.VMEM((2 * rows, wide), F32),
            pltpu.SemaphoreType.DMA((copies + 1,)),
        ],
        weight=weight,
        flops=4 * rows * depth * len(flat) * cols,
        moved=4 * rows * depth * many + 2 * depth * len(flat) * cols + 8 * rows * wide,
        name="project",
        in_hbm=2,
    )[0]


def outer(out_grads, sibling, at, width, dtypes, projected):
    rows, many, cols = out_grads.shape[0], at.shape[0], projected.shape[1]

    def kernel(at_ref, own_ref, sib_ref, projected_ref, *refs):
        outs, (g, sems) = refs[:-2], refs[-2:]
        copies = []
        core = lax.rem(lax.axis_index("dp"), 2)
        for j in range(many):
            columns = pl.ds(pl.multiple_of(at_ref[j] * width, width), width)
            for c, ref in ((core, own_ref), (1 - core, sib_ref)):
                target = g.at[pl.ds(pl.multiple_of(c * rows, rows), rows), pl.ds(j * width, width)]
                copies.append(pltpu.make_async_copy(ref.at[:, columns], target, sems.at[len(copies)]))
                copies[-1].start()
        for j in range(many):
            copies[2 * j].wait()
            copies[2 * j + 1].wait()
            block = g[:, j * width : (j + 1) * width].T
            outs[j][...] = jnp.dot(block, projected_ref[...], preferred_element_type=F32).astype(dtypes[j])

    whole = lambda *shape: pl.BlockSpec(shape, lambda j, at_ref: (0, 0))
    return pl.pallas_call(
        kernel,
        grid_spec=pltpu.PrefetchScalarGridSpec(
            num_scalar_prefetch=1,
            grid=(1,),
            in_specs=[pl.BlockSpec(memory_space=pl.ANY)] * 2 + [whole(2 * rows, cols)],
            out_specs=[whole(width, cols)] * many,
            scratch_shapes=[pltpu.VMEM((2 * rows, many * width), BF16), pltpu.SemaphoreType.DMA((2 * many,))],
        ),
        out_shape=[jax.ShapeDtypeStruct((width, cols), dtype) for dtype in dtypes],
        compiler_params=params(),
        cost_estimate=cost(W_OUTER, 4 * rows * width * many * cols, many * (4 * rows * width + 4 * width * cols)),
        name="outer",
    )(at, pinned(out_grads), pinned(sibling), projected)


def back(groups, projector, at, rows, rows_in_all, before, weight):
    many, (width, rank) = at.shape[0], projector.shape
    arrays = [x for group in groups for x in group]
    held = [] if before is None else [before]

    def kernel(at_ref, projector_ref, *refs):
        array_refs, out_ref = refs[: len(arrays)], refs[len(arrays) + len(held)]
        p, pt, d, o, in_sems, out_sems = refs[len(arrays) + len(held) + 1 :]
        loads, starts, start = [], [], 0
        p_copy = pltpu.make_async_copy(projector_ref, p, in_sems.at[len(arrays)])
        p_copy.start()
        for group in groups:
            size, column, copies = group[0].shape[0], 0, []
            for x in group:
                n = sum(len(some) for some in loads) + len(copies)
                target = d.at[pl.ds(start, size), pl.ds(column, x.shape[1])]
                copies.append(pltpu.make_async_copy(array_refs[n], target, in_sems.at[n]))
                copies[-1].start()
                column += x.shape[1]
            loads.append(copies)
            starts.append(start)
            start += size
        p_copy.wait()
        pt[...] = p[...].T
        stores = []
        for group, copies, start in zip(groups, loads, starts):
            for copy in copies:
                copy.wait()
            size = group[0].shape[0]
            here = slice(start, start + size)
            o[here, :] = jnp.dot(d[here, :], pt[...], preferred_element_type=F32).astype(BF16)
            for j in range(start // rows, (start + size) // rows):
                target = out_ref.at[pl.ds(pl.multiple_of(at_ref[j] * rows, rows), rows), :]
                stores.append(pltpu.make_async_copy(o.at[pl.ds(j * rows, rows), :], target, out_sems.at[j]))
                stores[-1].start()
        for copy in stores:
            copy.wait()

    return call(
        kernel,
        at,
        [projector, *arrays, *held],
        [jax.ShapeDtypeStruct((rows_in_all, width), BF16)],
        [
            pltpu.VMEM((width, rank), BF16),
            pltpu.VMEM((rank, width), BF16),
            pltpu.VMEM((many * rows, rank), BF16),
            pltpu.VMEM((many * rows, width), BF16),
            pltpu.SemaphoreType.DMA((len(arrays) + 1,)),
            pltpu.SemaphoreType.DMA((many,)),
        ],
        weight=weight,
        flops=2 * many * rows * width * rank,
        moved=2 * many * rows * (width + rank),
        name="back",
        aliases={2 + len(arrays): 0} if held else None,
    )[0]


def levels(activations, out_grads, projector, first_moment, second_moment, *, nz):
    me = lax.axis_index("dp")
    z, y, core = me // 4, me // 2 % 2, me % 2
    grid = [(a, b, c) for a in range(nz) for b in range(2) for c in range(2)]

    def pairs(to):
        return [((a * 2 + b) * 2 + c, (to(a, b, c)[0] * 2 + to(a, b, c)[1]) * 2 + to(a, b, c)[2]) for a, b, c in grid]

    def swap_core(x):
        return lax.ppermute(x, "dp", pairs(lambda a, b, c: (a, b, 1 - c)))

    def swap_y(x):
        return lax.ppermute(x, "dp", pairs(lambda a, b, c: (a, 1 - b, c)))

    def shift_z(x, k):
        return lax.ppermute(x, "dp", pairs(lambda a, b, c: ((a + k) % nz, b, c)))

    def index(k, dy, dc):
        return (lax.rem(z + nz + k, nz) * 2 + (1 - y if dy else y)) * 2 + (1 - core if dc else core)

    def named(order):
        return jnp.stack([index(*o) for o in order]).astype(jnp.int32)

    def gather(chunks):
        line = [[own] for own in chunks]
        across = [[] for _ in chunks]
        for step in range(nz):
            for i in range(len(chunks)):
                if step:
                    line[i][step], across[i][step - 1] = lax.optimization_barrier((line[i][step], across[i][step - 1]))
                if step < nz - 1:
                    line[i].append(shift_z(line[i][step], 1))
                if step < nz - 1 or i < len(chunks) - 1:
                    across[i].append(swap_y(line[i][step]))
                else:
                    across[i].append(shift_z(after(across[i][0], line[i][step]), nz - 1))
        return line, across

    after = lambda x, *those: lax.optimization_barrier((x, *those))[0]
    ks = list(range(nz - 2, 0, -1)) + [nz - 1]
    depth, rank = projector.shape
    width = first_moment.shape[0]
    cols = rank // CHUNKS
    parts = [slice(i * cols, (i + 1) * cols) for i in range(CHUNKS)]

    order_in = [(-k, dy) for k in range(nz) for dy in (0, 1)]
    order_out = [(k, dy) for dy in (1, 0) for k in ks + [0]]
    last = len(order_in) - 1
    at_in = named([(k, dy, 0) for k, dy in order_in])
    at_out = named([(k, dy, 0) for k, dy in order_out])

    a_sibling = swap_core(activations)
    line, across = gather([projector[:, part] for part in parts])
    g_sibling = swap_core(after(out_grads, a_sibling, line[0][2]))
    block = lambda i, n: (across if n % 2 else line)[i][n // 2]
    soon = [last] * (CHUNKS - 1) + [last - 2]
    blocks = [{n: block(i, n) for n in range(soon[i])} for i in range(CHUNKS)]
    mine = project(activations, a_sibling, at_in[:last], blocks, None, W_EARLY)
    low = min(soon)
    blocks = [{n - low: block(i, n) for n in range(soon[i], last + 1)} for i in range(CHUNKS)]
    mine = project(activations, a_sibling, at_in[low:], blocks, mine, W_LATE)
    projected = (mine + swap_core(mine)).astype(BF16)
    (send,) = outer(out_grads, g_sibling, at_out[:1], width, [BF16], projected)
    at = after(at_out[1 : nz + 1], send)
    *sends, keep = outer(out_grads, g_sibling, at, width, [BF16] * (nz - 1) + [F32], projected)
    passed = keep + swap_y(send).astype(F32)
    at = after(at_out[nz + 1 :], passed)
    keeps = outer(out_grads, g_sibling, at, width, [F32] * (nz - 1), projected)
    terms = [keep + swap_y(send).astype(F32) for keep, send in zip(keeps, sends)]
    for term in terms[: nz - 3]:
        passed = term + shift_z(passed.astype(BF16), 1).astype(F32)
    back_term = after(terms[nz - 3].astype(BF16), passed)
    reduced = terms[nz - 2] + shift_z(back_term, nz - 1).astype(F32) + shift_z(passed.astype(BF16), 1).astype(F32)
    new_first, new_second, direction = adam(reduced, first_moment, second_moment)

    line, across = gather([direction[:, part] for part in parts])
    rows_in_all = 4 * nz * width
    steps = range(1, nz)
    mine = [(direction,)] + [tuple(jnp.concatenate([line[i][k], across[i][k - 1]]) for i in range(CHUNKS)) for k in steps]
    mine.append(tuple(across[i][-1] for i in range(CHUNKS)))
    theirs = [tuple(swap_core(x) for x in group) for group in mine]
    order = [[(0, 0)]] + [[(-k, 0), (1 - k, 1)] for k in steps] + [[(1 - nz, 1)]]
    update = None
    for low, high, weight in ((0, nz - 1, W_BACK), (nz - 1, nz + 1, W_LAST)):
        at = named([(k, dy, dc) for dc in (0, 1) for some in order[low:high] for k, dy in some])
        update = back(mine[low:high] + theirs[low:high], projector, at, width, rows_in_all, update, weight)
    return update, new_first, new_second


def solution(mesh):
    devices = mesh.shape["dp"]

    def body(activations, out_grads, projector, first_moment, second_moment):
        aligned = projector.shape[0] % 128 == 0 and first_moment.shape[0] % 128 == 0
        if devices % 4 or devices < 16 or not aligned:
            return plain(activations, out_grads, projector, first_moment, second_moment)
        return levels(activations, out_grads, projector, first_moment, second_moment, nz=devices // 4)

    placed = P(("groups", "dp"), None)
    return jax.shard_map(
        body,
        mesh=mesh,
        in_specs=(placed,) * 5,
        out_specs=(P("groups", "dp"), placed, placed),
        check_vma=False,
    )
```

time: 142 us -> 135 us (0.951)
  waiting for transfers between devices: 74.8 us -> 65 us
  starting transfers between devices: 34.9 us -> 40.6 us
  local copies, waits for them, and re-layouts: 5.22 us -> 1.47 us
    ppermute x18, waiting for transfers between devices: 25.7 us -> 15.1 us  [swap_y(): return lax.ppermute(x, 'dp', pairs(lambda a, b, c: (a, 1 - b, c)))]
    ppermute x17, waiting for transfers between devices: 43.4 us -> 47 us  [shift_z(): return lax.ppermute(x, 'dp', pairs(lambda a, b, c: ((a + k) % nz, b, c)))]
    ppermute x18, starting transfers between devices: 14.9 us -> 18.4 us  [swap_y(): return lax.ppermute(x, 'dp', pairs(lambda a, b, c: (a, 1 - b, c)))]
    ppermute x6 -> x12, waiting for transfers between devices: 5.67 us -> 2.91 us  [swap_core(): return lax.ppermute(x, 'dp', pairs(lambda a, b, c: (a, b, 1 - c)))]
    optimization_barrier x2 -> x0, local copies, waits for them, and re-layouts: 2.26 us -> none  [levels(): after = lambda x, *those: lax.optimization_barrier((x, *those))[0]]
    slice x1 -> x0, local copies, waits for them, and re-layouts: 1.49 us -> none  [levels(): theirs[rows:]]
    ppermute x6 -> x12, starting transfers between devices: 1.81 us -> 3.28 us  [swap_core(): return lax.ppermute(x, 'dp', pairs(lambda a, b, c: (a, b, 1 - c)))]
    pallas_call x5 -> x4, Pallas kernels: 16.2 us -> 17.1 us  [call(): pl.pallas_call(kernel, grid_spec=pltpu.PrefetchScalarGridSpec(num_scalar_...]
  transfers between devices with their start and end apart: 41 -> 47, of which waited for: 31 -> 20; matrix products, arithmetic and copies ran while one was open for 4% -> 2% of each run, Pallas kernels for 11% -> 15%
where the time goes in v7:
time: 135 us
  waiting for transfers between devices  65 us (48%)
  starting transfers between devices  40.6 us (30%)
  Pallas kernels  24.7 us (18%)
  other arithmetic  2.29 us (2%)
  local copies, waits for them, and re-layouts  1.47 us (1%)
    ppermute x17, waiting for transfers between devices, shift_z(): return lax.ppermute(x, 'dp', pairs(lambda a, b, c: ((a + k) % nz, b, c)))  47 us
    ppermute x17, starting transfers between devices, shift_z(): return lax.ppermute(x, 'dp', pairs(lambda a, b, c: ((a + k) % nz, b, c)))  19 us
    ppermute x18, starting transfers between devices, swap_y(): return lax.ppermute(x, 'dp', pairs(lambda a, b, c: (a, 1 - b, c)))  18.4 us
    pallas_call x4, Pallas kernels, call(): pl.pallas_call(kernel, grid_spec=pltpu.PrefetchScalarGridSpec(num_scalar_...  17.1 us
    ppermute x18, waiting for transfers between devices, swap_y(): return lax.ppermute(x, 'dp', pairs(lambda a, b, c: (a, 1 - b, c)))  15.1 us
    pallas_call x3, Pallas kernels, outer(): pl.pallas_call(kernel, grid_spec=pltpu.PrefetchScalarGridSpec(num_scalar_...  7.57 us
    ppermute x12, starting transfers between devices, swap_core(): return lax.ppermute(x, 'dp', pairs(lambda a, b, c: (a, b, 1 - c)))  3.28 us
    ppermute x12, waiting for transfers between devices, swap_core(): return lax.ppermute(x, 'dp', pairs(lambda a, b, c: (a, b, 1 - c)))  2.91 us
  transfers between devices with their start and end apart: 47, of which 20 were waited for; matrix products, arithmetic and copies ran while one was open for 2% of the time, Pallas kernels for 15%

profile of v7, /device:TPU:0, one launch (start us, length us, event | category | flops | bytes accessed | tf_op | source)
XLA Modules:
  0.0 135.2 jit_solution(14489848232725032772)
XLA Ops:
  2.2 2.6 %collective-permute-start.1 = (bf16[512,256]{1,0:T(8,128)(2,1)S(1)}, bf16[512,256]{1,0:T(8,128)(2,1)S(1)}, u32[]{:S(2)}, u32[]{:S(2)}) collective-permute-start(bf16[512,256]{1,0:T(8,128)(2,1)S(1)} %get-tuple-element.81.refs_0_), channel_id=1, source_target_pairs={{0,4},{1,5},{2,6},{3,7},{4,8},{5,9},{6,10},{7,11},{8,12},{9,13},{1... | collective-permute-start | bytes 786440 | tf_op jit(solution)/shard_map/ppermute | solution.py:251
  4.9 1.5 %collective-permute-start.2 = (bf16[512,256]{1,0:T(8,128)(2,1)S(1)}, bf16[512,256]{1,0:T(8,128)(2,1)S(1)}, u32[]{:S(2)}, u32[]{:S(2)}) collective-permute-start(bf16[512,256]{1,0:T(8,128)(2,1)S(1)} %get-tuple-element.81.refs_0_), channel_id=1, source_target_pairs={{0,2},{1,3},{2,0},{3,1},{4,6},{5,7},{6,4},{7,5},{8,10},{9,11},{10,... | collective-permute-start | bytes 786440 | tf_op jit(solution)/shard_map/ppermute | solution.py:248
  6.9 1.6 %collective-permute-start.9 = (bf16[512,256]{1,0:T(8,128)(2,1)S(1)}, bf16[512,256]{1,0:T(8,128)(2,1)S(1)}, u32[]{:S(2)}, u32[]{:S(2)}) collective-permute-start(bf16[512,256]{1,0:T(8,128)(2,1)S(1)} %get-tuple-element.80.refs_7_), channel_id=1, source_target_pairs={{0,4},{1,5},{2,6},{3,7},{4,8},{5,9},{6,10},{7,11},{8,12},{9,13},{1... | collective-permute-start | bytes 786440 | tf_op jit(solution)/shard_map/ppermute | solution.py:251
  8.5 5.6 %collective-permute-done.1.refs_2_ = bf16[512,256]{1,0:T(8,128)(2,1)S(1)} collective-permute-done((bf16[512,256]{1,0:T(8,128)(2,1)S(1)}, bf16[512,256]{1,0:T(8,128)(2,1)S(1)}, u32[]{:S(2)}, u32[]{:S(2)}) %collective-permute-start.1) | collective-permute-done | bytes 262176 | tf_op jit(solution)/shard_map/ppermute | solution.py:251
  14.0 1.5 %collective-permute-start.3 = (bf16[512,256]{1,0:T(8,128)(2,1)S(1)}, bf16[512,256]{1,0:T(8,128)(2,1)S(1)}, u32[]{:S(2)}, u32[]{:S(2)}) collective-permute-start(bf16[512,256]{1,0:T(8,128)(2,1)S(1)} %collective-permute-done.1.refs_2_), channel_id=1, source_target_pairs={{0,4},{1,5},{2,6},{3,7},{4,8},{5,9},{6,10},{7,11},{8,12},{9,13},{1... | collective-permute-start | bytes 786440 | tf_op jit(solution)/shard_map/ppermute | solution.py:251
  15.6 1.5 %collective-permute-start.4 = (bf16[512,256]{1,0:T(8,128)(2,1)S(1)}, bf16[512,256]{1,0:T(8,128)(2,1)S(1)}, u32[]{:S(2)}, u32[]{:S(2)}) collective-permute-start(bf16[512,256]{1,0:T(8,128)(2,1)S(1)} %collective-permute-done.1.refs_2_), channel_id=1, source_target_pairs={{0,2},{1,3},{2,0},{3,1},{4,6},{5,7},{6,4},{7,5},{8,10},{9,11},{10,... | collective-permute-start | bytes 786440 | tf_op jit(solution)/shard_map/ppermute | solution.py:248
  17.1 2.5 %collective-permute-done.10.refs_8_ = bf16[512,256]{1,0:T(8,128)(2,1)S(1)} collective-permute-done((bf16[512,256]{1,0:T(8,128)(2,1)S(1)}, bf16[512,256]{1,0:T(8,128)(2,1)S(1)}, u32[]{:S(2)}, u32[]{:S(2)}) %collective-permute-start.10) | collective-permute-done | bytes 262176 | tf_op jit(solution)/shard_map/ppermute | solution.py:248
  19.7 1.5 %collective-permute-start.11 = (bf16[512,256]{1,0:T(8,128)(2,1)S(1)}, bf16[512,256]{1,0:T(8,128)(2,1)S(1)}, u32[]{:S(2)}, u32[]{:S(2)}) collective-permute-start(bf16[512,256]{1,0:T(8,128)(2,1)S(1)} %collective-permute-done.9.refs_9_), channel_id=1, source_target_pairs={{0,4},{1,5},{2,6},{3,7},{4,8},{5,9},{6,10},{7,11},{8,12},{9,13},{1... | collective-permute-start | bytes 786440 | tf_op jit(solution)/shard_map/ppermute | solution.py:251
  21.2 1.5 %collective-permute-start.12 = (bf16[512,256]{1,0:T(8,128)(2,1)S(1)}, bf16[512,256]{1,0:T(8,128)(2,1)S(1)}, u32[]{:S(2)}, u32[]{:S(2)}) collective-permute-start(bf16[512,256]{1,0:T(8,128)(2,1)S(1)} %collective-permute-done.9.refs_9_), channel_id=1, source_target_pairs={{0,2},{1,3},{2,0},{3,1},{4,6},{5,7},{6,4},{7,5},{8,10},{9,11},{10,... | collective-permute-start | bytes 786440 | tf_op jit(solution)/shard_map/ppermute | solution.py:248
  22.7 2.6 %collective-permute-done.3.refs_4_ = bf16[512,256]{1,0:T(8,128)(2,1)S(1)} collective-permute-done((bf16[512,256]{1,0:T(8,128)(2,1)S(1)}, bf16[512,256]{1,0:T(8,128)(2,1)S(1)}, u32[]{:S(2)}, u32[]{:S(2)}) %collective-permute-start.3) | collective-permute-done | bytes 262176 | tf_op jit(solution)/shard_map/ppermute | solution.py:251
  25.3 1.5 %collective-permute-start.6 = (bf16[512,256]{1,0:T(8,128)(2,1)S(1)}, bf16[512,256]{1,0:T(8,128)(2,1)S(1)}, u32[]{:S(2)}, u32[]{:S(2)}) collective-permute-start(bf16[512,256]{1,0:T(8,128)(2,1)S(1)} %collective-permute-done.3.refs_4_), channel_id=1, source_target_pairs={{0,4},{1,5},{2,6},{3,7},{4,8},{5,9},{6,10},{7,11},{8,12},{9,13},{1... | collective-permute-start | bytes 786440 | tf_op jit(solution)/shard_map/ppermute | solution.py:251
  26.8 1.5 %collective-permute-start.7 = (bf16[512,256]{1,0:T(8,128)(2,1)S(1)}, bf16[512,256]{1,0:T(8,128)(2,1)S(1)}, u32[]{:S(2)}, u32[]{:S(2)}) collective-permute-start(bf16[512,256]{1,0:T(8,128)(2,1)S(1)} %collective-permute-done.3.refs_4_), channel_id=1, source_target_pairs={{0,2},{1,3},{2,0},{3,1},{4,6},{5,7},{6,4},{7,5},{8,10},{9,11},{10,... | collective-permute-start | bytes 786440 | tf_op jit(solution)/shard_map/ppermute | solution.py:248
  28.3 2.6 %collective-permute-done.11.refs_11_ = bf16[512,256]{1,0:T(8,128)(2,1)S(1)} collective-permute-done((bf16[512,256]{1,0:T(8,128)(2,1)S(1)}, bf16[512,256]{1,0:T(8,128)(2,1)S(1)}, u32[]{:S(2)}, u32[]{:S(2)}) %collective-permute-start.11) | collective-permute-done | bytes 262176 | tf_op jit(solution)/shard_map/ppermute | solution.py:251
  30.9 1.5 %collective-permute-start.13 = (bf16[512,256]{1,0:T(8,128)(2,1)S(1)}, bf16[512,256]{1,0:T(8,128)(2,1)S(1)}, u32[]{:S(2)}, u32[]{:S(2)}) collective-permute-start(bf16[512,256]{1,0:T(8,128)(2,1)S(1)} %collective-permute-done.11.refs_11_), channel_id=1, source_target_pairs={{0,4},{1,5},{2,6},{3,7},{4,8},{5,9},{6,10},{7,11},{8,12},{9,13},{1... | collective-permute-start | bytes 786440 | tf_op jit(solution)/shard_map/ppermute | solution.py:251
  32.4 1.5 %collective-permute-start.14 = (bf16[512,256]{1,0:T(8,128)(2,1)S(1)}, bf16[512,256]{1,0:T(8,128)(2,1)}, u32[]{:S(2)}, u32[]{:S(2)}) collective-permute-start(bf16[512,256]{1,0:T(8,128)(2,1)S(1)} %collective-permute-done.11.refs_11_), channel_id=1, source_target_pairs={{0,2},{1,3},{2,0},{3,1},{4,6},{5,7},{6,4},{7,5},{8,10},{9,11},{10,... | collective-permute-start | bytes 786440 | tf_op jit(solution)/shard_map/ppermute | solution.py:248
  34.1 2.4 %collective-permute-done.6.refs_6_ = bf16[512,256]{1,0:T(8,128)(2,1)S(1)} collective-permute-done((bf16[512,256]{1,0:T(8,128)(2,1)S(1)}, bf16[512,256]{1,0:T(8,128)(2,1)S(1)}, u32[]{:S(2)}, u32[]{:S(2)}) %collective-permute-start.6) | collective-permute-done | bytes 262176 | tf_op jit(solution)/shard_map/ppermute | solution.py:251
  36.5 5.4 %collective-permute-done.13.refs_2_ = bf16[512,256]{1,0:T(8,128)(2,1)S(1)} collective-permute-done((bf16[512,256]{1,0:T(8,128)(2,1)S(1)}, bf16[512,256]{1,0:T(8,128)(2,1)S(1)}, u32[]{:S(2)}, u32[]{:S(2)}) %collective-permute-start.13) | collective-permute-done | bytes 262176 | tf_op jit(solution)/shard_map/ppermute | solution.py:251
  41.9 1.9 %collective-permute-start.15 = (bf16[512,256]{1,0:T(8,128)(2,1)S(1)}, bf16[512,256]{1,0:T(8,128)(2,1)S(1)}, u32[]{:S(2)}, u32[]{:S(2)}) collective-permute-start(bf16[512,256]{1,0:T(8,128)(2,1)S(1)} %collective-permute-done.10.refs_8_), channel_id=1, source_target_pairs={{0,12},{1,13},{2,14},{3,15},{4,0},{5,1},{6,2},{7,3},{8,4},{9,5},{1... | collective-permute-start | bytes 786440 | tf_op jit(solution)/shard_map/ppermute | solution.py:251
  43.9 1.5 %collective-permute-start.8 = (bf16[512,256]{1,0:T(8,128)(2,1)S(1)}, bf16[512,256]{1,0:T(8,128)(2,1)S(1)}, u32[]{:S(2)}, u32[]{:S(2)}) collective-permute-start(bf16[512,256]{1,0:T(8,128)(2,1)S(1)} %collective-permute-done.6.refs_6_), channel_id=1, source_target_pairs={{0,2},{1,3},{2,0},{3,1},{4,6},{5,7},{6,4},{7,5},{8,10},{9,11},{10,... | collective-permute-start | bytes 786440 | tf_op jit(solution)/shard_map/ppermute | solution.py:248
  45.4 6.1 %project.2.refs_4_ = f32[768,512]{1,0:T(8,128)S(1)} custom-call(s32[7]{0:T(128)S(1)} %stack.113.at_ref, bf16[384,8192]{1,0:T(8,128)(2,1)} %own_ref.6, bf16[384,8192]{1,0:T(8,128)(2,1)} %collective-permute-done.sib_ref, bf16[512,256]{1,0:T(8,128)(2,1)S(1)} %get-tuple-element.81.refs_0_, bf16[512,256]{1,0:T(8,128)(2,1)S(1)} %collective-permute-done.2.refs_1_, ...), custom_call_target="tpu_custom_call" | custom-call | flops 72477573120 | bytes 306708480 | tf_op jit(solution)/shard_map/project/pallas_call | solution.py:66
  51.5 3.5 %project.3 = f32[768,512]{1,0:T(8,128)S(1)} custom-call(s32[3]{0:T(128)S(1)} %pad_add_fusion.2.at_ref, bf16[384,8192]{1,0:T(8,128)(2,1)} %own_ref.6, bf16[384,8192]{1,0:T(8,128)(2,1)} %collective-permute-done.sib_ref, bf16[512,256]{1,0:T(8,128)(2,1)S(1)} %collective-permute-done.8.refs_0_, bf16[512,256]{1,0:T(8,128)(2,1)} %collective-permute-done.14.refs_1_, ...), custom_call_target="tpu_custom_call" | custom-call | flops 24159191040 | bytes 149422080 | tf_op jit(solution)/shard_map/project/pallas_call | solution.py:66
  55.7 2.9 %collective-permute-done.16 = f32[768,512]{1,0:T(8,128)S(1)} collective-permute-done((f32[768,512]{1,0:T(8,128)S(1)}, f32[768,512]{1,0:T(8,128)S(1)}, u32[]{:S(2)}, u32[]{:S(2)}) %collective-permute-start.16) | collective-permute-done | bytes 1572896 | tf_op jit(solution)/shard_map/ppermute | solution.py:245
  59.0 1.5 %outer.3 = bf16[256,512]{1,0:T(8,128)(2,1)S(1)} custom-call(s32[1]{0:T(128)} %bitcast.13.at_ref, bf16[384,4096]{1,0:T(8,128)(2,1)} %own_ref.9, bf16[384,4096]{1,0:T(8,128)(2,1)} %collective-permute-done.5.sib_ref, bf16[768,512]{1,0:T(8,128)(2,1)S(1)} %add_convert_fusion.projected_ref), custom_call_target="tpu_custom_call" | custom-call | flops 6039797760 | bytes 27525120 | tf_op jit(solution)/shard_map/outer/pallas_call | solution.py:161
  60.5 1.3 collective-permute-start.17
  61.8 3.3 %outer.4 = (bf16[256,512]{1,0:T(8,128)(2,1)S(1)}, bf16[256,512]{1,0:T(8,128)(2,1)S(1)}, bf16[256,512]{1,0:T(8,128)(2,1)S(1)}, f32[256,512]{1,0:T(8,128)S(1)}) custom-call(s32[4]{0:T(128)S(1)} %pad_add_fusion.1.at_ref, bf16[384,4096]{1,0:T(8,128)(2,1)} %own_ref.9, bf16[384,4096]{1,0:T(8,128)(2,1)} %collective-permute-done.5.sib_ref, ...), custom_call_target="tpu_custom_call" | custom-call | flops 24159191040 | bytes 110100480 | tf_op jit(solution)/shard_map/outer/pallas_call | solution.py:161
  65.9 1.3 collective-permute-start.20
  67.9 1.7 %collective-permute-done.17 = bf16[256,512]{1,0:T(8,128)(2,1)S(1)} collective-permute-done((bf16[256,512]{1,0:T(8,128)(2,1)S(1)}, bf16[256,512]{1,0:T(8,128)(2,1)S(1)}, u32[]{:S(2)}, u32[]{:S(2)}) %collective-permute-start.17) | collective-permute-done | bytes 262176 | tf_op jit(solution)/shard_map/ppermute | solution.py:248
  70.0 2.8 %outer.5 = (f32[256,512]{1,0:T(8,128)S(1)}, f32[256,512]{1,0:T(8,128)S(1)}, f32[256,512]{1,0:T(8,128)S(1)}) custom-call(s32[3]{0:T(128)S(1)} %pad_add_fusion.at_ref, bf16[384,4096]{1,0:T(8,128)(2,1)} %own_ref.9, bf16[384,4096]{1,0:T(8,128)(2,1)} %collective-permute-done.5.sib_ref, bf16[768,512]{1,0:T(8,128)(2,1)S(1)} %add_convert_fusion.projected_ref), custom_call_target="tpu_custom_call" | custom-call | flops 18119393280 | bytes 82575360 | tf_op jit(solution)/shard_map/outer/pallas_call | solution.py:161
  72.8 2.4 %collective-permute-done.19 = bf16[256,512]{1,0:T(8,128)(2,1)S(1)} collective-permute-done((bf16[256,512]{1,0:T(8,128)(2,1)S(1)}, bf16[256,512]{1,0:T(8,128)(2,1)S(1)}, u32[]{:S(2)}, u32[]{:S(2)}) %collective-permute-start.19) | collective-permute-done | bytes 262176 | tf_op jit(solution)/shard_map/ppermute | solution.py:248
  75.4 5.5 %collective-permute-done.20 = bf16[256,512]{1,0:T(8,128)(2,1)S(1)} collective-permute-done((bf16[256,512]{1,0:T(8,128)(2,1)S(1)}, bf16[256,512]{1,0:T(8,128)(2,1)S(1)}, u32[]{:S(2)}, u32[]{:S(2)}) %collective-permute-start.20) | collective-permute-done | bytes 262176 | tf_op jit(solution)/shard_map/ppermute | solution.py:248
  81.0 2.0 %collective-permute-start.22 = (bf16[256,512]{1,0:T(8,128)(2,1)S(1)}, bf16[256,512]{1,0:T(8,128)(2,1)S(1)}, u32[]{:S(2)}, u32[]{:S(2)}) collective-permute-start(bf16[256,512]{1,0:T(8,128)(2,1)S(1)} %add_convert_fusion.1), channel_id=1, source_target_pairs={{0,12},{1,13},{2,14},{3,15},{4,0},{5,1},{6,2},{7,3},{8,4},{9,5},{1... | collective-permute-start | bytes 786440 | tf_op jit(solution)/shard_map/ppermute | solution.py:251
  83.1 2.9 %collective-permute-done.18 = bf16[256,512]{1,0:T(8,128)(2,1)S(1)} collective-permute-done((bf16[256,512]{1,0:T(8,128)(2,1)S(1)}, bf16[256,512]{1,0:T(8,128)(2,1)S(1)}, u32[]{:S(2)}, u32[]{:S(2)}) %collective-permute-start.18) | collective-permute-done | bytes 262176 | tf_op jit(solution)/shard_map/ppermute | solution.py:248
  86.0 4.2 %collective-permute-done.22 = bf16[256,512]{1,0:T(8,128)(2,1)S(1)} collective-permute-done((bf16[256,512]{1,0:T(8,128)(2,1)S(1)}, bf16[256,512]{1,0:T(8,128)(2,1)S(1)}, u32[]{:S(2)}, u32[]{:S(2)}) %collective-permute-start.22) | collective-permute-done | bytes 262176 | tf_op jit(solution)/shard_map/ppermute | solution.py:251
  90.2 3.8 %collective-permute-done.23 = bf16[256,512]{1,0:T(8,128)(2,1)S(1)} collective-permute-done((bf16[256,512]{1,0:T(8,128)(2,1)S(1)}, bf16[256,512]{1,0:T(8,128)(2,1)S(1)}, u32[]{:S(2)}, u32[]{:S(2)}) %collective-permute-start.23) | collective-permute-done | bytes 262176 | tf_op jit(solution)/shard_map/ppermute | solution.py:251
  94.0 1.4 %divide_convert_fusion = (bf16[256,512]{1,0:T(8,128)(2,1)S(1)}, f32[256,512]{1,0:T(8,128)}, f32[256,512]{1,0:T(8,128)}) fusion(bf16[256,512]{1,0:T(8,128)(2,1)S(1)} %collective-permute-done.23, bf16[256,512]{1,0:T(8,128)(2,1)S(1)} %collective-permute-done.22, f32[256,512]{1,0:T(8,128)S(1)} %get-tuple-element.57, ...), kind=kLoop, calls=%fused_computation.3 | loop fusion | flops 2359296 | bytes 3670016 | tf_op jit(solution)/shard_map/convert_element_type | solution.py:26
  95.4 1.5 %collective-permute-start.30 = (bf16[256,256]{1,0:T(8,128)(2,1)S(1)}, bf16[256,256]{1,0:T(8,128)(2,1)S(1)}, u32[]{:S(2)}, u32[]{:S(2)}) collective-permute-start(bf16[256,256]{1,0:T(8,128)(2,1)S(1)} %get-tuple-element.82), channel_id=1, source_target_pairs={{0,4},{1,5},{2,6},{3,7},{4,8},{5,9},{6,10},{7,11},{8,12},{9,13},{1... | collective-permute-start | bytes 393224 | tf_op jit(solution)/shard_map/ppermute | solution.py:251
  96.9 1.4 %collective-permute-start.31 = (bf16[256,256]{1,0:T(8,128)(2,1)S(1)}, bf16[256,256]{1,0:T(8,128)(2,1)S(1)}, u32[]{:S(2)}, u32[]{:S(2)}) collective-permute-start(bf16[256,256]{1,0:T(8,128)(2,1)S(1)} %get-tuple-element.82), channel_id=1, source_target_pairs={{0,2},{1,3},{2,0},{3,1},{4,6},{5,7},{6,4},{7,5},{8,10},{9,11},{10,... | collective-permute-start | bytes 393224 | tf_op jit(solution)/shard_map/ppermute | solution.py:248
  99.6 2.9 %collective-permute-done.30 = bf16[256,256]{1,0:T(8,128)(2,1)S(1)} collective-permute-done((bf16[256,256]{1,0:T(8,128)(2,1)S(1)}, bf16[256,256]{1,0:T(8,128)(2,1)S(1)}, u32[]{:S(2)}, u32[]{:S(2)}) %collective-permute-start.30) | collective-permute-done | bytes 131104 | tf_op jit(solution)/shard_map/ppermute | solution.py:251
  103.4 2.2 %collective-permute-done.24 = bf16[256,256]{1,0:T(8,128)(2,1)S(1)} collective-permute-done((bf16[256,256]{1,0:T(8,128)(2,1)S(1)}, bf16[256,256]{1,0:T(8,128)(2,1)S(1)}, u32[]{:S(2)}, u32[]{:S(2)}) %collective-permute-start.24) | collective-permute-done | bytes 131104 | tf_op jit(solution)/shard_map/ppermute | solution.py:251
  106.0 3.3 %collective-permute-done.32 = bf16[256,256]{1,0:T(8,128)(2,1)S(1)} collective-permute-done((bf16[256,256]{1,0:T(8,128)(2,1)S(1)}, bf16[256,256]{1,0:T(8,128)(2,1)S(1)}, u32[]{:S(2)}, u32[]{:S(2)}) %collective-permute-start.32) | collective-permute-done | bytes 131104 | tf_op jit(solution)/shard_map/ppermute | solution.py:251
  110.0 1.2 collective-permute-start.35
  111.2 2.6 %collective-permute-done.26 = bf16[256,256]{1,0:T(8,128)(2,1)S(1)} collective-permute-done((bf16[256,256]{1,0:T(8,128)(2,1)S(1)}, bf16[256,256]{1,0:T(8,128)(2,1)S(1)}, u32[]{:S(2)}, u32[]{:S(2)}) %collective-permute-start.26) | collective-permute-done | bytes 131104 | tf_op jit(solution)/shard_map/ppermute | solution.py:251
  114.0 2.3 %collective-permute-done.34 = bf16[256,256]{1,0:T(8,128)(2,1)S(1)} collective-permute-done((bf16[256,256]{1,0:T(8,128)(2,1)S(1)}, bf16[256,256]{1,0:T(8,128)(2,1)S(1)}, u32[]{:S(2)}, u32[]{:S(2)}) %collective-permute-start.34) | collective-permute-done | bytes 131104 | tf_op jit(solution)/shard_map/ppermute | solution.py:251
  116.9 3.7 %collective-permute-done.28 = bf16[256,256]{1,0:T(8,128)(2,1)S(1)} collective-permute-done((bf16[256,256]{1,0:T(8,128)(2,1)S(1)}, bf16[256,256]{1,0:T(8,128)(2,1)S(1)}, u32[]{:S(2)}, u32[]{:S(2)}) %collective-permute-start.28) | collective-permute-done | bytes 131104 | tf_op jit(solution)/shard_map/ppermute | solution.py:251
  121.3 1.7 %collective-permute-start.37 = (bf16[256,256]{1,0:T(8,128)(2,1)S(1)}, bf16[256,256]{1,0:T(8,128)(2,1)S(1)}, u32[]{:S(2)}, u32[]{:S(2)}) collective-permute-start(bf16[256,256]{1,0:T(8,128)(2,1)S(1)} %collective-permute-done.31), channel_id=1, source_target_pairs={{0,12},{1,13},{2,14},{3,15},{4,0},{5,1},{6,2},{7,3},{8,4},{9,5},{1... | collective-permute-start | bytes 393224 | tf_op jit(solution)/shard_map/ppermute | solution.py:251
  123.7 3.3 %collective-permute-done.37.refs_3_ = bf16[256,256]{1,0:T(8,128)(2,1)S(1)} collective-permute-done((bf16[256,256]{1,0:T(8,128)(2,1)S(1)}, bf16[256,256]{1,0:T(8,128)(2,1)S(1)}, u32[]{:S(2)}, u32[]{:S(2)}) %collective-permute-start.37) | collective-permute-done | bytes 131104 | tf_op jit(solution)/shard_map/ppermute | solution.py:251
  127.4 4.3 %back.2.refs_8_ = bf16[4096,512]{1,0:T(8,128)(2,1)} custom-call(s32[10]{0:T(128)S(1)} %stack.119.at_ref, bf16[512,512]{1,0:T(8,128)(2,1)S(1)} %copy-done, bf16[256,512]{1,0:T(8,128)(2,1)S(1)} %get-tuple-element.77.refs_0_, bf16[512,256]{1,0:T(8,128)(2,1)S(1)} %constant_dynamic-update-slice_fusion.4.refs_1_, ...), custom_call_target="tpu_custom_call" | custom-call | flops 40265318400 | bytes 157286400 | tf_op jit(solution)/shard_map/back/pallas_call | solution.py:66
  131.8 3.2 %back.3 = bf16[4096,512]{1,0:T(8,128)(2,1)} custom-call(s32[6]{0:T(128)S(1)} %stack.98.at_ref, bf16[512,512]{1,0:T(8,128)(2,1)S(1)} %copy-done, bf16[512,256]{1,0:T(8,128)(2,1)S(1)} %constant_dynamic-update-slice_fusion.refs_0_, bf16[512,256]{1,0:T(8,128)(2,1)S(1)} %constant_dynamic-update-slice_fusion.2.refs_1_, ...), custom_call_target="tpu_custom_call", output_to_operand_aliasing={{}: (10, {})} | custom-call | flops 24159191040000 | bytes 94371840000 | tf_op jit(solution)/shard_map/back/pallas_call | solution.py:66
  (84 shorter events, 11.3 us)
Async XLA Ops:
  0.6 44.8 %collective-permute-start = (bf16[384,8192]{1,0:T(8,128)(2,1)}, bf16[384,8192]{1,0:T(8,128)(2,1)}, u32[]{:S(2)}, u32[]{:S(2)}) collective-permute-start(bf16[384,8192]{1,0:T(8,128)(2,1)} %own_ref.6), channel_id=1, source_target_pairs={{0,1},{1,0},{2,3},{3,2},{4,5},{5,4},{6,7},{7,6},{8,9},{9,8},{10,11... | collective-permute-start | bytes 18874376 | tf_op jit(solution)/shard_map/ppermute | solution.py:245
  2.2 11.8 %collective-permute-start.1 = (bf16[512,256]{1,0:T(8,128)(2,1)S(1)}, bf16[512,256]{1,0:T(8,128)(2,1)S(1)}, u32[]{:S(2)}, u32[]{:S(2)}) collective-permute-start(bf16[512,256]{1,0:T(8,128)(2,1)S(1)} %get-tuple-element.81.refs_0_), channel_id=1, source_target_pairs={{0,4},{1,5},{2,6},{3,7},{4,8},{5,9},{6,10},{7,11},{8,12},{9,13},{1... | collective-permute-start | bytes 786440 | tf_op jit(solution)/shard_map/ppermute | solution.py:251
  4.9 9.2 %collective-permute-start.2 = (bf16[512,256]{1,0:T(8,128)(2,1)S(1)}, bf16[512,256]{1,0:T(8,128)(2,1)S(1)}, u32[]{:S(2)}, u32[]{:S(2)}) collective-permute-start(bf16[512,256]{1,0:T(8,128)(2,1)S(1)} %get-tuple-element.81.refs_0_), channel_id=1, source_target_pairs={{0,2},{1,3},{2,0},{3,1},{4,6},{5,7},{6,4},{7,5},{8,10},{9,11},{10,... | collective-permute-start | bytes 786440 | tf_op jit(solution)/shard_map/ppermute | solution.py:248
  6.4 13.2 %collective-permute-start.10 = (bf16[512,256]{1,0:T(8,128)(2,1)S(1)}, bf16[512,256]{1,0:T(8,128)(2,1)S(1)}, u32[]{:S(2)}, u32[]{:S(2)}) collective-permute-start(bf16[512,256]{1,0:T(8,128)(2,1)S(1)} %get-tuple-element.80.refs_7_), channel_id=1, source_target_pairs={{0,2},{1,3},{2,0},{3,1},{4,6},{5,7},{6,4},{7,5},{8,10},{9,11},{10,... | collective-permute-start | bytes 786440 | tf_op jit(solution)/shard_map/ppermute | solution.py:248
  6.9 12.8 %collective-permute-start.9 = (bf16[512,256]{1,0:T(8,128)(2,1)S(1)}, bf16[512,256]{1,0:T(8,128)(2,1)S(1)}, u32[]{:S(2)}, u32[]{:S(2)}) collective-permute-start(bf16[512,256]{1,0:T(8,128)(2,1)S(1)} %get-tuple-element.80.refs_7_), channel_id=1, source_target_pairs={{0,4},{1,5},{2,6},{3,7},{4,8},{5,9},{6,10},{7,11},{8,12},{9,13},{1... | collective-permute-start | bytes 786440 | tf_op jit(solution)/shard_map/ppermute | solution.py:251
  14.0 11.2 %collective-permute-start.3 = (bf16[512,256]{1,0:T(8,128)(2,1)S(1)}, bf16[512,256]{1,0:T(8,128)(2,1)S(1)}, u32[]{:S(2)}, u32[]{:S(2)}) collective-permute-start(bf16[512,256]{1,0:T(8,128)(2,1)S(1)} %collective-permute-done.1.refs_2_), channel_id=1, source_target_pairs={{0,4},{1,5},{2,6},{3,7},{4,8},{5,9},{6,10},{7,11},{8,12},{9,13},{1... | collective-permute-start | bytes 786440 | tf_op jit(solution)/shard_map/ppermute | solution.py:251
  15.6 9.7 %collective-permute-start.4 = (bf16[512,256]{1,0:T(8,128)(2,1)S(1)}, bf16[512,256]{1,0:T(8,128)(2,1)S(1)}, u32[]{:S(2)}, u32[]{:S(2)}) collective-permute-start(bf16[512,256]{1,0:T(8,128)(2,1)S(1)} %collective-permute-done.1.refs_2_), channel_id=1, source_target_pairs={{0,2},{1,3},{2,0},{3,1},{4,6},{5,7},{6,4},{7,5},{8,10},{9,11},{10,... | collective-permute-start | bytes 786440 | tf_op jit(solution)/shard_map/ppermute | solution.py:248
  19.7 11.2 %collective-permute-start.11 = (bf16[512,256]{1,0:T(8,128)(2,1)S(1)}, bf16[512,256]{1,0:T(8,128)(2,1)S(1)}, u32[]{:S(2)}, u32[]{:S(2)}) collective-permute-start(bf16[512,256]{1,0:T(8,128)(2,1)S(1)} %collective-permute-done.9.refs_9_), channel_id=1, source_target_pairs={{0,4},{1,5},{2,6},{3,7},{4,8},{5,9},{6,10},{7,11},{8,12},{9,13},{1... | collective-permute-start | bytes 786440 | tf_op jit(solution)/shard_map/ppermute | solution.py:251
  21.2 9.7 %collective-permute-start.12 = (bf16[512,256]{1,0:T(8,128)(2,1)S(1)}, bf16[512,256]{1,0:T(8,128)(2,1)S(1)}, u32[]{:S(2)}, u32[]{:S(2)}) collective-permute-start(bf16[512,256]{1,0:T(8,128)(2,1)S(1)} %collective-permute-done.9.refs_9_), channel_id=1, source_target_pairs={{0,2},{1,3},{2,0},{3,1},{4,6},{5,7},{6,4},{7,5},{8,10},{9,11},{10,... | collective-permute-start | bytes 786440 | tf_op jit(solution)/shard_map/ppermute | solution.py:248
  25.3 11.2 %collective-permute-start.6 = (bf16[512,256]{1,0:T(8,128)(2,1)S(1)}, bf16[512,256]{1,0:T(8,128)(2,1)S(1)}, u32[]{:S(2)}, u32[]{:S(2)}) collective-permute-start(bf16[512,256]{1,0:T(8,128)(2,1)S(1)} %collective-permute-done.3.refs_4_), channel_id=1, source_target_pairs={{0,4},{1,5},{2,6},{3,7},{4,8},{5,9},{6,10},{7,11},{8,12},{9,13},{1... | collective-permute-start | bytes 786440 | tf_op jit(solution)/shard_map/ppermute | solution.py:251
  26.8 9.7 %collective-permute-start.7 = (bf16[512,256]{1,0:T(8,128)(2,1)S(1)}, bf16[512,256]{1,0:T(8,128)(2,1)S(1)}, u32[]{:S(2)}, u32[]{:S(2)}) collective-permute-start(bf16[512,256]{1,0:T(8,128)(2,1)S(1)} %collective-permute-done.3.refs_4_), channel_id=1, source_target_pairs={{0,2},{1,3},{2,0},{3,1},{4,6},{5,7},{6,4},{7,5},{8,10},{9,11},{10,... | collective-permute-start | bytes 786440 | tf_op jit(solution)/shard_map/ppermute | solution.py:248
  30.9 11.0 %collective-permute-start.13 = (bf16[512,256]{1,0:T(8,128)(2,1)S(1)}, bf16[512,256]{1,0:T(8,128)(2,1)S(1)}, u32[]{:S(2)}, u32[]{:S(2)}) collective-permute-start(bf16[512,256]{1,0:T(8,128)(2,1)S(1)} %collective-permute-done.11.refs_11_), channel_id=1, source_target_pairs={{0,4},{1,5},{2,6},{3,7},{4,8},{5,9},{6,10},{7,11},{8,12},{9,13},{1... | collective-permute-start | bytes 786440 | tf_op jit(solution)/shard_map/ppermute | solution.py:251
  32.4 9.5 %collective-permute-start.14 = (bf16[512,256]{1,0:T(8,128)(2,1)S(1)}, bf16[512,256]{1,0:T(8,128)(2,1)}, u32[]{:S(2)}, u32[]{:S(2)}) collective-permute-start(bf16[512,256]{1,0:T(8,128)(2,1)S(1)} %collective-permute-done.11.refs_11_), channel_id=1, source_target_pairs={{0,2},{1,3},{2,0},{3,1},{4,6},{5,7},{6,4},{7,5},{8,10},{9,11},{10,... | collective-permute-start | bytes 786440 | tf_op jit(solution)/shard_map/ppermute | solution.py:248
  41.9 9.6 %collective-permute-start.15 = (bf16[512,256]{1,0:T(8,128)(2,1)S(1)}, bf16[512,256]{1,0:T(8,128)(2,1)S(1)}, u32[]{:S(2)}, u32[]{:S(2)}) collective-permute-start(bf16[512,256]{1,0:T(8,128)(2,1)S(1)} %collective-permute-done.10.refs_8_), channel_id=1, source_target_pairs={{0,12},{1,13},{2,14},{3,15},{4,0},{5,1},{6,2},{7,3},{8,4},{9,5},{1... | collective-permute-start | bytes 786440 | tf_op jit(solution)/shard_map/ppermute | solution.py:251
  43.9 7.7 %collective-permute-start.8 = (bf16[512,256]{1,0:T(8,128)(2,1)S(1)}, bf16[512,256]{1,0:T(8,128)(2,1)S(1)}, u32[]{:S(2)}, u32[]{:S(2)}) collective-permute-start(bf16[512,256]{1,0:T(8,128)(2,1)S(1)} %collective-permute-done.6.refs_6_), channel_id=1, source_target_pairs={{0,2},{1,3},{2,0},{3,1},{4,6},{5,7},{6,4},{7,5},{8,10},{9,11},{10,... | collective-permute-start | bytes 786440 | tf_op jit(solution)/shard_map/ppermute | solution.py:248
  45.4 13.6 %collective-permute-start.5 = (bf16[384,4096]{1,0:T(8,128)(2,1)}, bf16[384,4096]{1,0:T(8,128)(2,1)}, u32[]{:S(2)}, u32[]{:S(2)}) collective-permute-start(bf16[384,4096]{1,0:T(8,128)(2,1)} %own_ref.9), channel_id=1, source_target_pairs={{0,1},{1,0},{2,3},{3,2},{4,5},{5,4},{6,7},{7,6},{8,9},{9,8},{10,11... | collective-permute-start | bytes 9437192 | tf_op jit(solution)/shard_map/ppermute | solution.py:245
  55.0 3.6 %collective-permute-start.16 = (f32[768,512]{1,0:T(8,128)S(1)}, f32[768,512]{1,0:T(8,128)S(1)}, u32[]{:S(2)}, u32[]{:S(2)}) collective-permute-start(f32[768,512]{1,0:T(8,128)S(1)} %project.3), channel_id=1, source_target_pairs={{0,1},{1,0},{2,3},{3,2},{4,5},{5,4},{6,7},{7,6},{8,9},{9,8},{10,11... | collective-permute-start | bytes 4718600 | tf_op jit(solution)/shard_map/ppermute | solution.py:245
  60.5 9.2 %collective-permute-start.17 = (bf16[256,512]{1,0:T(8,128)(2,1)S(1)}, bf16[256,512]{1,0:T(8,128)(2,1)S(1)}, u32[]{:S(2)}, u32[]{:S(2)}) collective-permute-start(bf16[256,512]{1,0:T(8,128)(2,1)S(1)} %outer.3), channel_id=1, source_target_pairs={{0,2},{1,3},{2,0},{3,1},{4,6},{5,7},{6,4},{7,5},{8,10},{9,11},{10,... | collective-permute-start | bytes 786440 | tf_op jit(solution)/shard_map/ppermute | solution.py:248
  65.1 10.2 %collective-permute-start.19 = (bf16[256,512]{1,0:T(8,128)(2,1)S(1)}, bf16[256,512]{1,0:T(8,128)(2,1)S(1)}, u32[]{:S(2)}, u32[]{:S(2)}) collective-permute-start(bf16[256,512]{1,0:T(8,128)(2,1)S(1)} %get-tuple-element.60), channel_id=1, source_target_pairs={{0,2},{1,3},{2,0},{3,1},{4,6},{5,7},{6,4},{7,5},{8,10},{9,11},{10,... | collective-permute-start | bytes 786440 | tf_op jit(solution)/shard_map/ppermute | solution.py:248
  65.9 15.0 %collective-permute-start.20 = (bf16[256,512]{1,0:T(8,128)(2,1)S(1)}, bf16[256,512]{1,0:T(8,128)(2,1)S(1)}, u32[]{:S(2)}, u32[]{:S(2)}) collective-permute-start(bf16[256,512]{1,0:T(8,128)(2,1)S(1)} %get-tuple-element.62), channel_id=1, source_target_pairs={{0,2},{1,3},{2,0},{3,1},{4,6},{5,7},{6,4},{7,5},{8,10},{9,11},{10,... | collective-permute-start | bytes 786440 | tf_op jit(solution)/shard_map/ppermute | solution.py:248
  67.2 18.8 %collective-permute-start.18 = (bf16[256,512]{1,0:T(8,128)(2,1)S(1)}, bf16[256,512]{1,0:T(8,128)(2,1)S(1)}, u32[]{:S(2)}, u32[]{:S(2)}) collective-permute-start(bf16[256,512]{1,0:T(8,128)(2,1)S(1)} %get-tuple-element.58), channel_id=1, source_target_pairs={{0,2},{1,3},{2,0},{3,1},{4,6},{5,7},{6,4},{7,5},{8,10},{9,11},{10,... | collective-permute-start | bytes 786440 | tf_op jit(solution)/shard_map/ppermute | solution.py:248
  69.8 11.1 %collective-permute-start.21 = (bf16[256,512]{1,0:T(8,128)(2,1)S(1)}, bf16[256,512]{1,0:T(8,128)(2,1)S(1)}, u32[]{:S(2)}, u32[]{:S(2)}) collective-permute-start(bf16[256,512]{1,0:T(8,128)(2,1)S(1)} %convert_add_fusion.2), channel_id=1, source_target_pairs={{0,4},{1,5},{2,6},{3,7},{4,8},{5,9},{6,10},{7,11},{8,12},{9,13},{1... | collective-permute-start | bytes 786440 | tf_op jit(solution)/shard_map/ppermute | solution.py:251
  81.0 9.2 %collective-permute-start.22 = (bf16[256,512]{1,0:T(8,128)(2,1)S(1)}, bf16[256,512]{1,0:T(8,128)(2,1)S(1)}, u32[]{:S(2)}, u32[]{:S(2)}) collective-permute-start(bf16[256,512]{1,0:T(8,128)(2,1)S(1)} %add_convert_fusion.1), channel_id=1, source_target_pairs={{0,12},{1,13},{2,14},{3,15},{4,0},{5,1},{6,2},{7,3},{8,4},{9,5},{1... | collective-permute-start | bytes 786440 | tf_op jit(solution)/shard_map/ppermute | solution.py:251
  83.0 11.0 %collective-permute-start.23 = (bf16[256,512]{1,0:T(8,128)(2,1)S(1)}, bf16[256,512]{1,0:T(8,128)(2,1)S(1)}, u32[]{:S(2)}, u32[]{:S(2)}) collective-permute-start(bf16[256,512]{1,0:T(8,128)(2,1)S(1)} %convert_add_fusion.1), channel_id=1, source_target_pairs={{0,4},{1,5},{2,6},{3,7},{4,8},{5,9},{6,10},{7,11},{8,12},{9,13},{1... | collective-permute-start | bytes 786440 | tf_op jit(solution)/shard_map/ppermute | solution.py:251
  94.0 33.4 %copy-start = (bf16[512,512]{1,0:T(8,128)(2,1)S(1)}, bf16[512,512]{1,0:T(8,128)(2,1)}, u32[]{:S(2)}) copy-start(bf16[512,512]{1,0:T(8,128)(2,1)} %projector_ref.3) | copy-start | bytes 1572868
  95.4 7.1 %collective-permute-start.30 = (bf16[256,256]{1,0:T(8,128)(2,1)S(1)}, bf16[256,256]{1,0:T(8,128)(2,1)S(1)}, u32[]{:S(2)}, u32[]{:S(2)}) collective-permute-start(bf16[256,256]{1,0:T(8,128)(2,1)S(1)} %get-tuple-element.82), channel_id=1, source_target_pairs={{0,4},{1,5},{2,6},{3,7},{4,8},{5,9},{6,10},{7,11},{8,12},{9,13},{1... | collective-permute-start | bytes 393224 | tf_op jit(solution)/shard_map/ppermute | solution.py:251
  96.9 5.7 %collective-permute-start.31 = (bf16[256,256]{1,0:T(8,128)(2,1)S(1)}, bf16[256,256]{1,0:T(8,128)(2,1)S(1)}, u32[]{:S(2)}, u32[]{:S(2)}) collective-permute-start(bf16[256,256]{1,0:T(8,128)(2,1)S(1)} %get-tuple-element.82), channel_id=1, source_target_pairs={{0,2},{1,3},{2,0},{3,1},{4,6},{5,7},{6,4},{7,5},{8,10},{9,11},{10,... | collective-permute-start | bytes 393224 | tf_op jit(solution)/shard_map/ppermute | solution.py:248
  98.3 7.3 %collective-permute-start.24 = (bf16[256,256]{1,0:T(8,128)(2,1)S(1)}, bf16[256,256]{1,0:T(8,128)(2,1)S(1)}, u32[]{:S(2)}, u32[]{:S(2)}) collective-permute-start(bf16[256,256]{1,0:T(8,128)(2,1)S(1)} %get-tuple-element.83), channel_id=1, source_target_pairs={{0,4},{1,5},{2,6},{3,7},{4,8},{5,9},{6,10},{7,11},{8,12},{9,13},{1... | collective-permute-start | bytes 393224 | tf_op jit(solution)/shard_map/ppermute | solution.py:251
  98.4 7.2 %collective-permute-start.25 = (bf16[256,256]{1,0:T(8,128)(2,1)S(1)}, bf16[256,256]{1,0:T(8,128)(2,1)S(1)}, u32[]{:S(2)}, u32[]{:S(2)}) collective-permute-start(bf16[256,256]{1,0:T(8,128)(2,1)S(1)} %get-tuple-element.83), channel_id=1, source_target_pairs={{0,2},{1,3},{2,0},{3,1},{4,6},{5,7},{6,4},{7,5},{8,10},{9,11},{10,... | collective-permute-start | bytes 393224 | tf_op jit(solution)/shard_map/ppermute | solution.py:248
  99.6 21.6 %collective-permute-start.42 = (bf16[256,512]{1,0:T(8,128)(2,1)S(1)}, bf16[256,512]{1,0:T(8,128)(2,1)S(1)}, u32[]{:S(2)}, u32[]{:S(2)}) collective-permute-start(bf16[256,512]{1,0:T(8,128)(2,1)S(1)} %get-tuple-element.77.refs_0_), channel_id=1, source_target_pairs={{0,1},{1,0},{2,3},{3,2},{4,5},{5,4},{6,7},{7,6},{8,9},{9,8},{10,11... | collective-permute-start | bytes 786440 | tf_op jit(solution)/shard_map/ppermute | solution.py:245
  102.6 6.8 %collective-permute-start.32 = (bf16[256,256]{1,0:T(8,128)(2,1)S(1)}, bf16[256,256]{1,0:T(8,128)(2,1)S(1)}, u32[]{:S(2)}, u32[]{:S(2)}) collective-permute-start(bf16[256,256]{1,0:T(8,128)(2,1)S(1)} %collective-permute-done.30), channel_id=1, source_target_pairs={{0,4},{1,5},{2,6},{3,7},{4,8},{5,9},{6,10},{7,11},{8,12},{9,13},{1... | collective-permute-start | bytes 393224 | tf_op jit(solution)/shard_map/ppermute | solution.py:251
  103.0 6.4 %collective-permute-start.33 = (bf16[256,256]{1,0:T(8,128)(2,1)S(1)}, bf16[256,256]{1,0:T(8,128)(2,1)S(1)}, u32[]{:S(2)}, u32[]{:S(2)}) collective-permute-start(bf16[256,256]{1,0:T(8,128)(2,1)S(1)} %collective-permute-done.30), channel_id=1, source_target_pairs={{0,2},{1,3},{2,0},{3,1},{4,6},{5,7},{6,4},{7,5},{8,10},{9,11},{10,... | collective-permute-start | bytes 393224 | tf_op jit(solution)/shard_map/ppermute | solution.py:248
  105.6 8.2 %collective-permute-start.26 = (bf16[256,256]{1,0:T(8,128)(2,1)S(1)}, bf16[256,256]{1,0:T(8,128)(2,1)S(1)}, u32[]{:S(2)}, u32[]{:S(2)}) collective-permute-start(bf16[256,256]{1,0:T(8,128)(2,1)S(1)} %collective-permute-done.24), channel_id=1, source_target_pairs={{0,4},{1,5},{2,6},{3,7},{4,8},{5,9},{6,10},{7,11},{8,12},{9,13},{1... | collective-permute-start | bytes 393224 | tf_op jit(solution)/shard_map/ppermute | solution.py:251
  105.6 8.2 %collective-permute-start.27 = (bf16[256,256]{1,0:T(8,128)(2,1)S(1)}, bf16[256,256]{1,0:T(8,128)(2,1)S(1)}, u32[]{:S(2)}, u32[]{:S(2)}) collective-permute-start(bf16[256,256]{1,0:T(8,128)(2,1)S(1)} %collective-permute-done.24), channel_id=1, source_target_pairs={{0,2},{1,3},{2,0},{3,1},{4,6},{5,7},{6,4},{7,5},{8,10},{9,11},{10,... | collective-permute-start | bytes 393224 | tf_op jit(solution)/shard_map/ppermute | solution.py:248
  109.3 7.0 %collective-permute-start.34 = (bf16[256,256]{1,0:T(8,128)(2,1)S(1)}, bf16[256,256]{1,0:T(8,128)(2,1)S(1)}, u32[]{:S(2)}, u32[]{:S(2)}) collective-permute-start(bf16[256,256]{1,0:T(8,128)(2,1)S(1)} %collective-permute-done.32), channel_id=1, source_target_pairs={{0,4},{1,5},{2,6},{3,7},{4,8},{5,9},{6,10},{7,11},{8,12},{9,13},{1... | collective-permute-start | bytes 393224 | tf_op jit(solution)/shard_map/ppermute | solution.py:251
  110.0 6.3 %collective-permute-start.35 = (bf16[256,256]{1,0:T(8,128)(2,1)S(1)}, bf16[256,256]{1,0:T(8,128)(2,1)S(1)}, u32[]{:S(2)}, u32[]{:S(2)}) collective-permute-start(bf16[256,256]{1,0:T(8,128)(2,1)S(1)} %collective-permute-done.32), channel_id=1, source_target_pairs={{0,2},{1,3},{2,0},{3,1},{4,6},{5,7},{6,4},{7,5},{8,10},{9,11},{10,... | collective-permute-start | bytes 393224 | tf_op jit(solution)/shard_map/ppermute | solution.py:248
  113.8 6.8 %collective-permute-start.28 = (bf16[256,256]{1,0:T(8,128)(2,1)S(1)}, bf16[256,256]{1,0:T(8,128)(2,1)S(1)}, u32[]{:S(2)}, u32[]{:S(2)}) collective-permute-start(bf16[256,256]{1,0:T(8,128)(2,1)S(1)} %collective-permute-done.26), channel_id=1, source_target_pairs={{0,4},{1,5},{2,6},{3,7},{4,8},{5,9},{6,10},{7,11},{8,12},{9,13},{1... | collective-permute-start | bytes 393224 | tf_op jit(solution)/shard_map/ppermute | solution.py:251
  113.9 6.8 %collective-permute-start.29 = (bf16[256,256]{1,0:T(8,128)(2,1)S(1)}, bf16[256,256]{1,0:T(8,128)(2,1)S(1)}, u32[]{:S(2)}, u32[]{:S(2)}) collective-permute-start(bf16[256,256]{1,0:T(8,128)(2,1)S(1)} %collective-permute-done.26), channel_id=1, source_target_pairs={{0,2},{1,3},{2,0},{3,1},{4,6},{5,7},{6,4},{7,5},{8,10},{9,11},{10,... | collective-permute-start | bytes 393224 | tf_op jit(solution)/shard_map/ppermute | solution.py:248
  116.3 5.0 %collective-permute-start.44 = (bf16[512,256]{1,0:T(8,128)(2,1)S(1)}, bf16[512,256]{1,0:T(8,128)(2,1)S(1)}, u32[]{:S(2)}, u32[]{:S(2)}) collective-permute-start(bf16[512,256]{1,0:T(8,128)(2,1)S(1)} %constant_dynamic-update-slice_fusion.6.refs_2_), channel_id=1, source_target_pairs={{0,1},{1,0},{2,3},{3,2},{4,5},{5,4},{6,7},{7,6},{8,9},{9,8},{10,11... | collective-permute-start | bytes 786440 | tf_op jit(solution)/shard_map/ppermute | solution.py:245
  116.3 6.7 %collective-permute-start.43 = (bf16[512,256]{1,0:T(8,128)(2,1)S(1)}, bf16[512,256]{1,0:T(8,128)(2,1)S(1)}, u32[]{:S(2)}, u32[]{:S(2)}) collective-permute-start(bf16[512,256]{1,0:T(8,128)(2,1)S(1)} %constant_dynamic-update-slice_fusion.4.refs_1_), channel_id=1, source_target_pairs={{0,1},{1,0},{2,3},{3,2},{4,5},{5,4},{6,7},{7,6},{8,9},{9,8},{10,11... | collective-permute-start | bytes 786440 | tf_op jit(solution)/shard_map/ppermute | solution.py:245
  120.6 2.7 %collective-permute-start.46 = (bf16[512,256]{1,0:T(8,128)(2,1)S(1)}, bf16[512,256]{1,0:T(8,128)(2,1)S(1)}, u32[]{:S(2)}, u32[]{:S(2)}) collective-permute-start(bf16[512,256]{1,0:T(8,128)(2,1)S(1)} %constant_dynamic-update-slice_fusion.10.refs_4_), channel_id=1, source_target_pairs={{0,1},{1,0},{2,3},{3,2},{4,5},{5,4},{6,7},{7,6},{8,9},{9,8},{10,11... | collective-permute-start | bytes 786440 | tf_op jit(solution)/shard_map/ppermute | solution.py:245
  120.6 6.8 %collective-permute-start.45 = (bf16[512,256]{1,0:T(8,128)(2,1)S(1)}, bf16[512,256]{1,0:T(8,128)(2,1)S(1)}, u32[]{:S(2)}, u32[]{:S(2)}) collective-permute-start(bf16[512,256]{1,0:T(8,128)(2,1)S(1)} %constant_dynamic-update-slice_fusion.8.refs_3_), channel_id=1, source_target_pairs={{0,1},{1,0},{2,3},{3,2},{4,5},{5,4},{6,7},{7,6},{8,9},{9,8},{10,11... | collective-permute-start | bytes 786440 | tf_op jit(solution)/shard_map/ppermute | solution.py:245
  121.2 5.7 %collective-permute-start.36 = (bf16[256,256]{1,0:T(8,128)(2,1)S(1)}, bf16[256,256]{1,0:T(8,128)(2,1)S(1)}, u32[]{:S(2)}, u32[]{:S(2)}) collective-permute-start(bf16[256,256]{1,0:T(8,128)(2,1)S(1)} %collective-permute-done.28), channel_id=1, source_target_pairs={{0,2},{1,3},{2,0},{3,1},{4,6},{5,7},{6,4},{7,5},{8,10},{9,11},{10,... | collective-permute-start | bytes 393224 | tf_op jit(solution)/shard_map/ppermute | solution.py:248
  121.3 5.6 %collective-permute-start.37 = (bf16[256,256]{1,0:T(8,128)(2,1)S(1)}, bf16[256,256]{1,0:T(8,128)(2,1)S(1)}, u32[]{:S(2)}, u32[]{:S(2)}) collective-permute-start(bf16[256,256]{1,0:T(8,128)(2,1)S(1)} %collective-permute-done.31), channel_id=1, source_target_pairs={{0,12},{1,13},{2,14},{3,15},{4,0},{5,1},{6,2},{7,3},{8,4},{9,5},{1... | collective-permute-start | bytes 393224 | tf_op jit(solution)/shard_map/ppermute | solution.py:251
  123.1 8.7 %collective-permute-start.39 = (bf16[512,256]{1,0:T(8,128)(2,1)S(1)}, bf16[512,256]{1,0:T(8,128)(2,1)S(1)}, u32[]{:S(2)}, u32[]{:S(2)}) collective-permute-start(bf16[512,256]{1,0:T(8,128)(2,1)S(1)} %constant_dynamic-update-slice_fusion.2.refs_1_), channel_id=1, source_target_pairs={{0,1},{1,0},{2,3},{3,2},{4,5},{5,4},{6,7},{7,6},{8,9},{9,8},{10,11... | collective-permute-start | bytes 786440 | tf_op jit(solution)/shard_map/ppermute | solution.py:245
  123.4 8.4 %collective-permute-start.38 = (bf16[512,256]{1,0:T(8,128)(2,1)S(1)}, bf16[512,256]{1,0:T(8,128)(2,1)S(1)}, u32[]{:S(2)}, u32[]{:S(2)}) collective-permute-start(bf16[512,256]{1,0:T(8,128)(2,1)S(1)} %constant_dynamic-update-slice_fusion.refs_0_), channel_id=1, source_target_pairs={{0,1},{1,0},{2,3},{3,2},{4,5},{5,4},{6,7},{7,6},{8,9},{9,8},{10,11... | collective-permute-start | bytes 786440 | tf_op jit(solution)/shard_map/ppermute | solution.py:245
  126.9 4.8 %collective-permute-start.41 = (bf16[256,256]{1,0:T(8,128)(2,1)S(1)}, bf16[256,256]{1,0:T(8,128)(2,1)S(1)}, u32[]{:S(2)}, u32[]{:S(2)}) collective-permute-start(bf16[256,256]{1,0:T(8,128)(2,1)S(1)} %collective-permute-done.37.refs_3_), channel_id=1, source_target_pairs={{0,1},{1,0},{2,3},{3,2},{4,5},{5,4},{6,7},{7,6},{8,9},{9,8},{10,11... | collective-permute-start | bytes 393224 | tf_op jit(solution)/shard_map/ppermute | solution.py:245
  126.9 4.9 %collective-permute-start.40 = (bf16[256,256]{1,0:T(8,128)(2,1)S(1)}, bf16[256,256]{1,0:T(8,128)(2,1)S(1)}, u32[]{:S(2)}, u32[]{:S(2)}) collective-permute-start(bf16[256,256]{1,0:T(8,128)(2,1)S(1)} %collective-permute-done.36.refs_2_), channel_id=1, source_target_pairs={{0,1},{1,0},{2,3},{3,2},{4,5},{5,4},{6,7},{7,6},{8,9},{9,8},{10,11... | collective-permute-start | bytes 393224 | tf_op jit(solution)/shard_map/ppermute | solution.py:245
  (2 other events, 48.5 us)

commit v8 on v7

--- a/solution.py
+++ b/solution.py
@@ -288,7 +288,7 @@
     line, across = gather([projector[:, part] for part in parts])
     g_sibling = swap_core(after(out_grads, a_sibling, line[0][2]))
     block = lambda i, n: (across if n % 2 else line)[i][n // 2]
-    soon = [last] * (CHUNKS - 1) + [last - 2]
+    soon = [last] * CHUNKS
     blocks = [{n: block(i, n) for n in range(soon[i])} for i in range(CHUNKS)]
     mine = project(activations, a_sibling, at_in[:last], blocks, None, W_EARLY)
     low = min(soon)
@@ -304,7 +304,7 @@
     terms = [keep + swap_y(send).astype(F32) for keep, send in zip(keeps, sends)]
     for term in terms[: nz - 3]:
         passed = term + shift_z(passed.astype(BF16), 1).astype(F32)
-    back_term = after(terms[nz - 3].astype(BF16), passed)
+    back_term = terms[nz - 3].astype(BF16)
     reduced = terms[nz - 2] + shift_z(back_term, nz - 1).astype(F32) + shift_z(passed.astype(BF16), 1).astype(F32)
     new_first, new_second, direction = adam(reduced, first_moment, second_moment)
 
@@ -313,10 +313,12 @@
     steps = range(1, nz)
     mine = [(direction,)] + [tuple(jnp.concatenate([line[i][k], across[i][k - 1]]) for i in range(CHUNKS)) for k in steps]
     mine.append(tuple(across[i][-1] for i in range(CHUNKS)))
-    theirs = [tuple(swap_core(x) for x in group) for group in mine]
+    theirs = [tuple(swap_core(x) for x in group) for group in mine[:-1]]
     order = [[(0, 0)]] + [[(-k, 0), (1 - k, 1)] for k in steps] + [[(1 - nz, 1)]]
     update = None
     for low, high, weight in ((0, nz - 1, W_BACK), (nz - 1, nz + 1, W_LAST)):
+        if low:
+            theirs.append(tuple(swap_core(after(x, update)) for x in mine[-1]))
         at = named([(k, dy, dc) for dc in (0, 1) for some in order[low:high] for k, dy in some])
         update = back(mine[low:high] + theirs[low:high], projector, at, width, rows_in_all, update, weight)
     return update, new_first, new_second

time: 135 us -> 127 us (0.941)
  waiting for transfers between devices: 65 us -> 52.8 us
  starting transfers between devices: 40.6 us -> 45.6 us
    ppermute x17, waiting for transfers between devices: 47 us -> 33.6 us  [shift_z(): return lax.ppermute(x, 'dp', pairs(lambda a, b, c: ((a + k) % nz, b, c)))]
    ppermute x18, starting transfers between devices: 18.4 us -> 21 us  [swap_y(): return lax.ppermute(x, 'dp', pairs(lambda a, b, c: (a, 1 - b, c)))]
    ppermute x17, starting transfers between devices: 19 us -> 21.4 us  [shift_z(): return lax.ppermute(x, 'dp', pairs(lambda a, b, c: ((a + k) % nz, b, c)))]
where the time goes in v8:
time: 127 us
  waiting for transfers between devices  52.8 us (42%)
  starting transfers between devices  45.6 us (36%)
  Pallas kernels  23.6 us (19%)
  other arithmetic  2.22 us (2%)
  local copies, waits for them, and re-layouts  1.47 us (1%)
    ppermute x17, waiting for transfers between devices, shift_z(): return lax.ppermute(x, 'dp', pairs(lambda a, b, c: ((a + k) % nz, b, c)))  33.6 us
    ppermute x17, starting transfers between devices, shift_z(): return lax.ppermute(x, 'dp', pairs(lambda a, b, c: ((a + k) % nz, b, c)))  21.4 us
    ppermute x18, starting transfers between devices, swap_y(): return lax.ppermute(x, 'dp', pairs(lambda a, b, c: (a, 1 - b, c)))  21 us
    pallas_call x4, Pallas kernels, call(): pl.pallas_call(kernel, grid_spec=pltpu.PrefetchScalarGridSpec(num_scalar_...  16 us
    ppermute x18, waiting for transfers between devices, swap_y(): return lax.ppermute(x, 'dp', pairs(lambda a, b, c: (a, 1 - b, c)))  15.4 us
    pallas_call x3, Pallas kernels, outer(): pl.pallas_call(kernel, grid_spec=pltpu.PrefetchScalarGridSpec(num_scalar_...  7.55 us
    ppermute x12, waiting for transfers between devices, swap_core(): return lax.ppermute(x, 'dp', pairs(lambda a, b, c: (a, b, 1 - c)))  3.84 us
    ppermute x12, starting transfers between devices, swap_core(): return lax.ppermute(x, 'dp', pairs(lambda a, b, c: (a, b, 1 - c)))  3.23 us
  transfers between devices with their start and end apart: 47, of which 20 were waited for; matrix products, arithmetic and copies ran while one was open for 2% of the time, Pallas kernels for 15%

profile of v8, /device:TPU:0, one launch (start us, length us, event | category | flops | bytes accessed | tf_op | source)
XLA Modules:
  0.0 126.7 jit_solution(8388066812322188552)
XLA Ops:
  2.2 2.6 %collective-permute-start.1 = (bf16[512,256]{1,0:T(8,128)(2,1)S(1)}, bf16[512,256]{1,0:T(8,128)(2,1)S(1)}, u32[]{:S(2)}, u32[]{:S(2)}) collective-permute-start(bf16[512,256]{1,0:T(8,128)(2,1)S(1)} %get-tuple-element.83.refs_0_), channel_id=1, source_target_pairs={{0,4},{1,5},{2,6},{3,7},{4,8},{5,9},{6,10},{7,11},{8,12},{9,13},{1... | collective-permute-start | bytes 786440 | tf_op jit(solution)/shard_map/ppermute | solution.py:251
  4.9 1.5 %collective-permute-start.2 = (bf16[512,256]{1,0:T(8,128)(2,1)S(1)}, bf16[512,256]{1,0:T(8,128)(2,1)S(1)}, u32[]{:S(2)}, u32[]{:S(2)}) collective-permute-start(bf16[512,256]{1,0:T(8,128)(2,1)S(1)} %get-tuple-element.83.refs_0_), channel_id=1, source_target_pairs={{0,2},{1,3},{2,0},{3,1},{4,6},{5,7},{6,4},{7,5},{8,10},{9,11},{10,... | collective-permute-start | bytes 786440 | tf_op jit(solution)/shard_map/ppermute | solution.py:248
  6.9 1.6 %collective-permute-start.9 = (bf16[512,256]{1,0:T(8,128)(2,1)S(1)}, bf16[512,256]{1,0:T(8,128)(2,1)S(1)}, u32[]{:S(2)}, u32[]{:S(2)}) collective-permute-start(bf16[512,256]{1,0:T(8,128)(2,1)S(1)} %get-tuple-element.82.refs_7_), channel_id=1, source_target_pairs={{0,4},{1,5},{2,6},{3,7},{4,8},{5,9},{6,10},{7,11},{8,12},{9,13},{1... | collective-permute-start | bytes 786440 | tf_op jit(solution)/shard_map/ppermute | solution.py:251
  8.5 5.6 %collective-permute-done.1.refs_2_ = bf16[512,256]{1,0:T(8,128)(2,1)S(1)} collective-permute-done((bf16[512,256]{1,0:T(8,128)(2,1)S(1)}, bf16[512,256]{1,0:T(8,128)(2,1)S(1)}, u32[]{:S(2)}, u32[]{:S(2)}) %collective-permute-start.1) | collective-permute-done | bytes 262176 | tf_op jit(solution)/shard_map/ppermute | solution.py:251
  14.0 1.5 %collective-permute-start.3 = (bf16[512,256]{1,0:T(8,128)(2,1)S(1)}, bf16[512,256]{1,0:T(8,128)(2,1)S(1)}, u32[]{:S(2)}, u32[]{:S(2)}) collective-permute-start(bf16[512,256]{1,0:T(8,128)(2,1)S(1)} %collective-permute-done.1.refs_2_), channel_id=1, source_target_pairs={{0,4},{1,5},{2,6},{3,7},{4,8},{5,9},{6,10},{7,11},{8,12},{9,13},{1... | collective-permute-start | bytes 786440 | tf_op jit(solution)/shard_map/ppermute | solution.py:251
  15.6 1.5 %collective-permute-start.4 = (bf16[512,256]{1,0:T(8,128)(2,1)S(1)}, bf16[512,256]{1,0:T(8,128)(2,1)S(1)}, u32[]{:S(2)}, u32[]{:S(2)}) collective-permute-start(bf16[512,256]{1,0:T(8,128)(2,1)S(1)} %collective-permute-done.1.refs_2_), channel_id=1, source_target_pairs={{0,2},{1,3},{2,0},{3,1},{4,6},{5,7},{6,4},{7,5},{8,10},{9,11},{10,... | collective-permute-start | bytes 786440 | tf_op jit(solution)/shard_map/ppermute | solution.py:248
  17.1 2.5 %collective-permute-done.10.refs_8_ = bf16[512,256]{1,0:T(8,128)(2,1)S(1)} collective-permute-done((bf16[512,256]{1,0:T(8,128)(2,1)S(1)}, bf16[512,256]{1,0:T(8,128)(2,1)S(1)}, u32[]{:S(2)}, u32[]{:S(2)}) %collective-permute-start.10) | collective-permute-done | bytes 262176 | tf_op jit(solution)/shard_map/ppermute | solution.py:248
  19.7 1.5 %collective-permute-start.11 = (bf16[512,256]{1,0:T(8,128)(2,1)S(1)}, bf16[512,256]{1,0:T(8,128)(2,1)S(1)}, u32[]{:S(2)}, u32[]{:S(2)}) collective-permute-start(bf16[512,256]{1,0:T(8,128)(2,1)S(1)} %collective-permute-done.9.refs_9_), channel_id=1, source_target_pairs={{0,4},{1,5},{2,6},{3,7},{4,8},{5,9},{6,10},{7,11},{8,12},{9,13},{1... | collective-permute-start | bytes 786440 | tf_op jit(solution)/shard_map/ppermute | solution.py:251
  21.2 1.5 %collective-permute-start.12 = (bf16[512,256]{1,0:T(8,128)(2,1)S(1)}, bf16[512,256]{1,0:T(8,128)(2,1)S(1)}, u32[]{:S(2)}, u32[]{:S(2)}) collective-permute-start(bf16[512,256]{1,0:T(8,128)(2,1)S(1)} %collective-permute-done.9.refs_9_), channel_id=1, source_target_pairs={{0,2},{1,3},{2,0},{3,1},{4,6},{5,7},{6,4},{7,5},{8,10},{9,11},{10,... | collective-permute-start | bytes 786440 | tf_op jit(solution)/shard_map/ppermute | solution.py:248
  22.7 2.6 %collective-permute-done.3.refs_4_ = bf16[512,256]{1,0:T(8,128)(2,1)S(1)} collective-permute-done((bf16[512,256]{1,0:T(8,128)(2,1)S(1)}, bf16[512,256]{1,0:T(8,128)(2,1)S(1)}, u32[]{:S(2)}, u32[]{:S(2)}) %collective-permute-start.3) | collective-permute-done | bytes 262176 | tf_op jit(solution)/shard_map/ppermute | solution.py:251
  25.3 1.5 %collective-permute-start.6 = (bf16[512,256]{1,0:T(8,128)(2,1)S(1)}, bf16[512,256]{1,0:T(8,128)(2,1)S(1)}, u32[]{:S(2)}, u32[]{:S(2)}) collective-permute-start(bf16[512,256]{1,0:T(8,128)(2,1)S(1)} %collective-permute-done.3.refs_4_), channel_id=1, source_target_pairs={{0,4},{1,5},{2,6},{3,7},{4,8},{5,9},{6,10},{7,11},{8,12},{9,13},{1... | collective-permute-start | bytes 786440 | tf_op jit(solution)/shard_map/ppermute | solution.py:251
  26.8 1.5 %collective-permute-start.7 = (bf16[512,256]{1,0:T(8,128)(2,1)S(1)}, bf16[512,256]{1,0:T(8,128)(2,1)S(1)}, u32[]{:S(2)}, u32[]{:S(2)}) collective-permute-start(bf16[512,256]{1,0:T(8,128)(2,1)S(1)} %collective-permute-done.3.refs_4_), channel_id=1, source_target_pairs={{0,2},{1,3},{2,0},{3,1},{4,6},{5,7},{6,4},{7,5},{8,10},{9,11},{10,... | collective-permute-start | bytes 786440 | tf_op jit(solution)/shard_map/ppermute | solution.py:248
  28.3 2.6 %collective-permute-done.11.refs_11_ = bf16[512,256]{1,0:T(8,128)(2,1)S(1)} collective-permute-done((bf16[512,256]{1,0:T(8,128)(2,1)S(1)}, bf16[512,256]{1,0:T(8,128)(2,1)S(1)}, u32[]{:S(2)}, u32[]{:S(2)}) %collective-permute-start.11) | collective-permute-done | bytes 262176 | tf_op jit(solution)/shard_map/ppermute | solution.py:251
  30.9 1.5 %collective-permute-start.13 = (bf16[512,256]{1,0:T(8,128)(2,1)S(1)}, bf16[512,256]{1,0:T(8,128)(2,1)S(1)}, u32[]{:S(2)}, u32[]{:S(2)}) collective-permute-start(bf16[512,256]{1,0:T(8,128)(2,1)S(1)} %collective-permute-done.11.refs_11_), channel_id=1, source_target_pairs={{0,4},{1,5},{2,6},{3,7},{4,8},{5,9},{6,10},{7,11},{8,12},{9,13},{1... | collective-permute-start | bytes 786440 | tf_op jit(solution)/shard_map/ppermute | solution.py:251
  32.4 1.5 %collective-permute-start.14 = (bf16[512,256]{1,0:T(8,128)(2,1)S(1)}, bf16[512,256]{1,0:T(8,128)(2,1)}, u32[]{:S(2)}, u32[]{:S(2)}) collective-permute-start(bf16[512,256]{1,0:T(8,128)(2,1)S(1)} %collective-permute-done.11.refs_11_), channel_id=1, source_target_pairs={{0,2},{1,3},{2,0},{3,1},{4,6},{5,7},{6,4},{7,5},{8,10},{9,11},{10,... | collective-permute-start | bytes 786440 | tf_op jit(solution)/shard_map/ppermute | solution.py:248
  34.0 2.5 %collective-permute-done.6.refs_6_ = bf16[512,256]{1,0:T(8,128)(2,1)S(1)} collective-permute-done((bf16[512,256]{1,0:T(8,128)(2,1)S(1)}, bf16[512,256]{1,0:T(8,128)(2,1)S(1)}, u32[]{:S(2)}, u32[]{:S(2)}) %collective-permute-start.6) | collective-permute-done | bytes 262176 | tf_op jit(solution)/shard_map/ppermute | solution.py:251
  36.5 5.4 %collective-permute-done.13.refs_13_ = bf16[512,256]{1,0:T(8,128)(2,1)S(1)} collective-permute-done((bf16[512,256]{1,0:T(8,128)(2,1)S(1)}, bf16[512,256]{1,0:T(8,128)(2,1)S(1)}, u32[]{:S(2)}, u32[]{:S(2)}) %collective-permute-start.13) | collective-permute-done | bytes 262176 | tf_op jit(solution)/shard_map/ppermute | solution.py:251
  41.9 1.9 %collective-permute-start.15 = (bf16[512,256]{1,0:T(8,128)(2,1)S(1)}, bf16[512,256]{1,0:T(8,128)(2,1)S(1)}, u32[]{:S(2)}, u32[]{:S(2)}) collective-permute-start(bf16[512,256]{1,0:T(8,128)(2,1)S(1)} %collective-permute-done.10.refs_8_), channel_id=1, source_target_pairs={{0,12},{1,13},{2,14},{3,15},{4,0},{5,1},{6,2},{7,3},{8,4},{9,5},{1... | collective-permute-start | bytes 786440 | tf_op jit(solution)/shard_map/ppermute | solution.py:251
  43.9 1.5 %collective-permute-start.8 = (bf16[512,256]{1,0:T(8,128)(2,1)S(1)}, bf16[512,256]{1,0:T(8,128)(2,1)S(1)}, u32[]{:S(2)}, u32[]{:S(2)}) collective-permute-start(bf16[512,256]{1,0:T(8,128)(2,1)S(1)} %collective-permute-done.6.refs_6_), channel_id=1, source_target_pairs={{0,2},{1,3},{2,0},{3,1},{4,6},{5,7},{6,4},{7,5},{8,10},{9,11},{10,... | collective-permute-start | bytes 786440 | tf_op jit(solution)/shard_map/ppermute | solution.py:248
  45.4 6.6 %project.2.refs_2_ = f32[768,512]{1,0:T(8,128)S(1)} custom-call(s32[7]{0:T(128)S(1)} %stack.110.at_ref, bf16[384,8192]{1,0:T(8,128)(2,1)} %own_ref.6, bf16[384,8192]{1,0:T(8,128)(2,1)} %collective-permute-done.sib_ref, bf16[512,256]{1,0:T(8,128)(2,1)S(1)} %get-tuple-element.83.refs_0_, bf16[512,256]{1,0:T(8,128)(2,1)S(1)} %collective-permute-done.2.refs_1_, ...), custom_call_target="tpu_custom_call" | custom-call | flops 84557168640 | bytes 322437120 | tf_op jit(solution)/shard_map/project/pallas_call | solution.py:66
  52.0 1.9 %project.3 = f32[768,512]{1,0:T(8,128)S(1)} custom-call(s32[1]{0:T(128)} %bitcast.2.at_ref, bf16[384,8192]{1,0:T(8,128)(2,1)} %own_ref.6, bf16[384,8192]{1,0:T(8,128)(2,1)} %collective-permute-done.sib_ref, bf16[512,256]{1,0:T(8,128)(2,1)S(1)} %collective-permute-done.8.refs_0_, bf16[512,256]{1,0:T(8,128)(2,1)S(1)} %collective-permute-done.15.refs_1_, ...), custom_call_target="tpu_custom_call" | custom-call | flops 12079595520 | bytes 86507520 | tf_op jit(solution)/shard_map/project/pallas_call | solution.py:66
  54.7 2.9 %collective-permute-done.16 = f32[768,512]{1,0:T(8,128)S(1)} collective-permute-done((f32[768,512]{1,0:T(8,128)S(1)}, f32[768,512]{1,0:T(8,128)S(1)}, u32[]{:S(2)}, u32[]{:S(2)}) %collective-permute-start.16) | collective-permute-done | bytes 1572896 | tf_op jit(solution)/shard_map/ppermute | solution.py:245
  58.0 1.5 %outer.3 = bf16[256,512]{1,0:T(8,128)(2,1)S(1)} custom-call(s32[1]{0:T(128)} %bitcast.13.at_ref, bf16[384,4096]{1,0:T(8,128)(2,1)} %own_ref.9, bf16[384,4096]{1,0:T(8,128)(2,1)} %collective-permute-done.5.sib_ref, bf16[768,512]{1,0:T(8,128)(2,1)S(1)} %add_convert_fusion.projected_ref), custom_call_target="tpu_custom_call" | custom-call | flops 6039797760 | bytes 27525120 | tf_op jit(solution)/shard_map/outer/pallas_call | solution.py:161
  60.2 3.3 %outer.4 = (bf16[256,512]{1,0:T(8,128)(2,1)S(1)}, bf16[256,512]{1,0:T(8,128)(2,1)S(1)}, bf16[256,512]{1,0:T(8,128)(2,1)S(1)}, f32[256,512]{1,0:T(8,128)S(1)}) custom-call(s32[4]{0:T(128)S(1)} %pad_add_fusion.1.at_ref, bf16[384,4096]{1,0:T(8,128)(2,1)} %own_ref.9, bf16[384,4096]{1,0:T(8,128)(2,1)} %collective-permute-done.5.sib_ref, ...), custom_call_target="tpu_custom_call" | custom-call | flops 24159191040 | bytes 110100480 | tf_op jit(solution)/shard_map/outer/pallas_call | solution.py:161
  63.5 1.3 %collective-permute-start.19 = (bf16[256,512]{1,0:T(8,128)(2,1)S(1)}, bf16[256,512]{1,0:T(8,128)(2,1)S(1)}, u32[]{:S(2)}, u32[]{:S(2)}) collective-permute-start(bf16[256,512]{1,0:T(8,128)(2,1)S(1)} %get-tuple-element.61), channel_id=1, source_target_pairs={{0,2},{1,3},{2,0},{3,1},{4,6},{5,7},{6,4},{7,5},{8,10},{9,11},{10,... | collective-permute-start | bytes 786440 | tf_op jit(solution)/shard_map/ppermute | solution.py:248
  65.6 1.3 %collective-permute-start.18 = (bf16[256,512]{1,0:T(8,128)(2,1)S(1)}, bf16[256,512]{1,0:T(8,128)(2,1)S(1)}, u32[]{:S(2)}, u32[]{:S(2)}) collective-permute-start(bf16[256,512]{1,0:T(8,128)(2,1)S(1)} %get-tuple-element.59), channel_id=1, source_target_pairs={{0,2},{1,3},{2,0},{3,1},{4,6},{5,7},{6,4},{7,5},{8,10},{9,11},{10,... | collective-permute-start | bytes 786440 | tf_op jit(solution)/shard_map/ppermute | solution.py:248
  66.9 1.7 %collective-permute-done.17 = bf16[256,512]{1,0:T(8,128)(2,1)S(1)} collective-permute-done((bf16[256,512]{1,0:T(8,128)(2,1)S(1)}, bf16[256,512]{1,0:T(8,128)(2,1)S(1)}, u32[]{:S(2)}, u32[]{:S(2)}) %collective-permute-start.17) | collective-permute-done | bytes 262176 | tf_op jit(solution)/shard_map/ppermute | solution.py:248
  68.9 2.8 %outer.5 = (f32[256,512]{1,0:T(8,128)S(1)}, f32[256,512]{1,0:T(8,128)S(1)}, f32[256,512]{1,0:T(8,128)S(1)}) custom-call(s32[3]{0:T(128)S(1)} %pad_add_fusion.at_ref, bf16[384,4096]{1,0:T(8,128)(2,1)} %own_ref.9, bf16[384,4096]{1,0:T(8,128)(2,1)} %collective-permute-done.5.sib_ref, bf16[768,512]{1,0:T(8,128)(2,1)S(1)} %add_convert_fusion.projected_ref), custom_call_target="tpu_custom_call" | custom-call | flops 18119393280 | bytes 82575360 | tf_op jit(solution)/shard_map/outer/pallas_call | solution.py:161
  71.7 2.5 %collective-permute-done.19 = bf16[256,512]{1,0:T(8,128)(2,1)S(1)} collective-permute-done((bf16[256,512]{1,0:T(8,128)(2,1)S(1)}, bf16[256,512]{1,0:T(8,128)(2,1)S(1)}, u32[]{:S(2)}, u32[]{:S(2)}) %collective-permute-start.19) | collective-permute-done | bytes 262176 | tf_op jit(solution)/shard_map/ppermute | solution.py:248
  74.3 1.7 %collective-permute-start.20 = (bf16[256,512]{1,0:T(8,128)(2,1)S(1)}, bf16[256,512]{1,0:T(8,128)(2,1)S(1)}, u32[]{:S(2)}, u32[]{:S(2)}) collective-permute-start(bf16[256,512]{1,0:T(8,128)(2,1)S(1)} %add_convert_fusion.2), channel_id=1, source_target_pairs={{0,12},{1,13},{2,14},{3,15},{4,0},{5,1},{6,2},{7,3},{8,4},{9,5},{1... | collective-permute-start | bytes 786440 | tf_op jit(solution)/shard_map/ppermute | solution.py:251
  76.0 3.8 %collective-permute-done.21 = bf16[256,512]{1,0:T(8,128)(2,1)S(1)} collective-permute-done((bf16[256,512]{1,0:T(8,128)(2,1)S(1)}, bf16[256,512]{1,0:T(8,128)(2,1)S(1)}, u32[]{:S(2)}, u32[]{:S(2)}) %collective-permute-start.21) | collective-permute-done | bytes 262176 | tf_op jit(solution)/shard_map/ppermute | solution.py:248
  80.1 4.8 %collective-permute-done.18 = bf16[256,512]{1,0:T(8,128)(2,1)S(1)} collective-permute-done((bf16[256,512]{1,0:T(8,128)(2,1)S(1)}, bf16[256,512]{1,0:T(8,128)(2,1)S(1)}, u32[]{:S(2)}, u32[]{:S(2)}) %collective-permute-start.18) | collective-permute-done | bytes 262176 | tf_op jit(solution)/shard_map/ppermute | solution.py:248
  84.9 4.1 %collective-permute-done.23 = bf16[256,512]{1,0:T(8,128)(2,1)S(1)} collective-permute-done((bf16[256,512]{1,0:T(8,128)(2,1)S(1)}, bf16[256,512]{1,0:T(8,128)(2,1)S(1)}, u32[]{:S(2)}, u32[]{:S(2)}) %collective-permute-start.23) | collective-permute-done | bytes 262176 | tf_op jit(solution)/shard_map/ppermute | solution.py:251
  89.1 1.4 %divide_convert_fusion = (bf16[256,512]{1,0:T(8,128)(2,1)S(1)}, f32[256,512]{1,0:T(8,128)}, f32[256,512]{1,0:T(8,128)}) fusion(bf16[256,512]{1,0:T(8,128)(2,1)S(1)} %collective-permute-done.23, bf16[256,512]{1,0:T(8,128)(2,1)S(1)} %collective-permute-done.20, f32[256,512]{1,0:T(8,128)S(1)} %get-tuple-element.58, ...), kind=kLoop, calls=%fused_computation.3 | loop fusion | flops 2359296 | bytes 3670016 | tf_op jit(solution)/shard_map/convert_element_type | solution.py:26
  91.0 1.5 %collective-permute-start.24 = (bf16[256,256]{1,0:T(8,128)(2,1)S(1)}, bf16[256,256]{1,0:T(8,128)(2,1)S(1)}, u32[]{:S(2)}, u32[]{:S(2)}) collective-permute-start(bf16[256,256]{1,0:T(8,128)(2,1)S(1)} %get-tuple-element.85), channel_id=1, source_target_pairs={{0,4},{1,5},{2,6},{3,7},{4,8},{5,9},{6,10},{7,11},{8,12},{9,13},{1... | collective-permute-start | bytes 393224 | tf_op jit(solution)/shard_map/ppermute | solution.py:251
  92.5 1.4 %collective-permute-start.25 = (bf16[256,256]{1,0:T(8,128)(2,1)S(1)}, bf16[256,256]{1,0:T(8,128)(2,1)S(1)}, u32[]{:S(2)}, u32[]{:S(2)}) collective-permute-start(bf16[256,256]{1,0:T(8,128)(2,1)S(1)} %get-tuple-element.85), channel_id=1, source_target_pairs={{0,2},{1,3},{2,0},{3,1},{4,6},{5,7},{6,4},{7,5},{8,10},{9,11},{10,... | collective-permute-start | bytes 393224 | tf_op jit(solution)/shard_map/ppermute | solution.py:248
  94.0 3.4 %collective-permute-done.30 = bf16[256,256]{1,0:T(8,128)(2,1)S(1)} collective-permute-done((bf16[256,256]{1,0:T(8,128)(2,1)S(1)}, bf16[256,256]{1,0:T(8,128)(2,1)S(1)}, u32[]{:S(2)}, u32[]{:S(2)}) %collective-permute-start.30) | collective-permute-done | bytes 131104 | tf_op jit(solution)/shard_map/ppermute | solution.py:251
  98.7 1.4 %collective-permute-start.26 = (bf16[256,256]{1,0:T(8,128)(2,1)S(1)}, bf16[256,256]{1,0:T(8,128)(2,1)S(1)}, u32[]{:S(2)}, u32[]{:S(2)}) collective-permute-start(bf16[256,256]{1,0:T(8,128)(2,1)S(1)} %collective-permute-done.24), channel_id=1, source_target_pairs={{0,4},{1,5},{2,6},{3,7},{4,8},{5,9},{6,10},{7,11},{8,12},{9,13},{1... | collective-permute-start | bytes 393224 | tf_op jit(solution)/shard_map/ppermute | solution.py:251
  101.2 2.9 %collective-permute-done.32 = bf16[256,256]{1,0:T(8,128)(2,1)S(1)} collective-permute-done((bf16[256,256]{1,0:T(8,128)(2,1)S(1)}, bf16[256,256]{1,0:T(8,128)(2,1)S(1)}, u32[]{:S(2)}, u32[]{:S(2)}) %collective-permute-start.32) | collective-permute-done | bytes 131104 | tf_op jit(solution)/shard_map/ppermute | solution.py:251
  105.2 1.2 collective-permute-done.26
  106.5 1.5 %collective-permute-start.28 = (bf16[256,256]{1,0:T(8,128)(2,1)S(1)}, bf16[256,256]{1,0:T(8,128)(2,1)S(1)}, u32[]{:S(2)}, u32[]{:S(2)}) collective-permute-start(bf16[256,256]{1,0:T(8,128)(2,1)S(1)} %collective-permute-done.26), channel_id=1, source_target_pairs={{0,4},{1,5},{2,6},{3,7},{4,8},{5,9},{6,10},{7,11},{8,12},{9,13},{1... | collective-permute-start | bytes 393224 | tf_op jit(solution)/shard_map/ppermute | solution.py:251
  108.0 1.6 %collective-permute-start.29 = (bf16[256,256]{1,0:T(8,128)(2,1)S(1)}, bf16[256,256]{1,0:T(8,128)(2,1)S(1)}, u32[]{:S(2)}, u32[]{:S(2)}) collective-permute-start(bf16[256,256]{1,0:T(8,128)(2,1)S(1)} %collective-permute-done.26), channel_id=1, source_target_pairs={{0,2},{1,3},{2,0},{3,1},{4,6},{5,7},{6,4},{7,5},{8,10},{9,11},{10,... | collective-permute-start | bytes 393224 | tf_op jit(solution)/shard_map/ppermute | solution.py:248
  109.6 1.3 %collective-permute-done.34 = bf16[256,256]{1,0:T(8,128)(2,1)S(1)} collective-permute-done((bf16[256,256]{1,0:T(8,128)(2,1)S(1)}, bf16[256,256]{1,0:T(8,128)(2,1)S(1)}, u32[]{:S(2)}, u32[]{:S(2)}) %collective-permute-start.34) | collective-permute-done | bytes 131104 | tf_op jit(solution)/shard_map/ppermute | solution.py:251
  111.4 1.9 %collective-permute-done.28 = bf16[256,256]{1,0:T(8,128)(2,1)S(1)} collective-permute-done((bf16[256,256]{1,0:T(8,128)(2,1)S(1)}, bf16[256,256]{1,0:T(8,128)(2,1)S(1)}, u32[]{:S(2)}, u32[]{:S(2)}) %collective-permute-start.28) | collective-permute-done | bytes 131104 | tf_op jit(solution)/shard_map/ppermute | solution.py:251
  113.9 1.5 %collective-permute-start.36 = (bf16[256,256]{1,0:T(8,128)(2,1)S(1)}, bf16[256,256]{1,0:T(8,128)(2,1)S(1)}, u32[]{:S(2)}, u32[]{:S(2)}) collective-permute-start(bf16[256,256]{1,0:T(8,128)(2,1)S(1)} %collective-permute-done.28), channel_id=1, source_target_pairs={{0,2},{1,3},{2,0},{3,1},{4,6},{5,7},{6,4},{7,5},{8,10},{9,11},{10,... | collective-permute-start | bytes 393224 | tf_op jit(solution)/shard_map/ppermute | solution.py:248
  115.4 1.5 %collective-permute-start.37 = (bf16[256,256]{1,0:T(8,128)(2,1)S(1)}, bf16[256,256]{1,0:T(8,128)(2,1)S(1)}, u32[]{:S(2)}, u32[]{:S(2)}) collective-permute-start(bf16[256,256]{1,0:T(8,128)(2,1)S(1)} %collective-permute-done.31), channel_id=1, source_target_pairs={{0,12},{1,13},{2,14},{3,15},{4,0},{5,1},{6,2},{7,3},{8,4},{9,5},{1... | collective-permute-start | bytes 393224 | tf_op jit(solution)/shard_map/ppermute | solution.py:251
  117.4 4.3 %back.2.refs_8_ = bf16[4096,512]{1,0:T(8,128)(2,1)} custom-call(s32[10]{0:T(128)S(1)} %stack.116.at_ref, bf16[512,512]{1,0:T(8,128)(2,1)S(1)} %copy-done, bf16[256,512]{1,0:T(8,128)(2,1)S(1)} %get-tuple-element.79.refs_0_, bf16[512,256]{1,0:T(8,128)(2,1)S(1)} %constant_dynamic-update-slice_fusion.4.refs_1_, ...), custom_call_target="tpu_custom_call" | custom-call | flops 40265318400 | bytes 157286400 | tf_op jit(solution)/shard_map/back/pallas_call | solution.py:66
  123.3 3.2 %back.3 = bf16[4096,512]{1,0:T(8,128)(2,1)} custom-call(s32[6]{0:T(128)S(1)} %stack.96.at_ref, bf16[512,512]{1,0:T(8,128)(2,1)S(1)} %copy-done, bf16[512,256]{1,0:T(8,128)(2,1)S(1)} %constant_dynamic-update-slice_fusion.refs_0_, bf16[512,256]{1,0:T(8,128)(2,1)S(1)} %constant_dynamic-update-slice_fusion.2.refs_1_, ...), custom_call_target="tpu_custom_call", output_to_operand_aliasing={{}: (10, {})} | custom-call | flops 24159191040000 | bytes 94371840000 | tf_op jit(solution)/shard_map/back/pallas_call | solution.py:66
  (83 shorter events, 13.0 us)
Async XLA Ops:
  0.6 44.8 %collective-permute-start = (bf16[384,8192]{1,0:T(8,128)(2,1)}, bf16[384,8192]{1,0:T(8,128)(2,1)}, u32[]{:S(2)}, u32[]{:S(2)}) collective-permute-start(bf16[384,8192]{1,0:T(8,128)(2,1)} %own_ref.6), channel_id=1, source_target_pairs={{0,1},{1,0},{2,3},{3,2},{4,5},{5,4},{6,7},{7,6},{8,9},{9,8},{10,11... | collective-permute-start | bytes 18874376 | tf_op jit(solution)/shard_map/ppermute | solution.py:245
  2.2 11.8 %collective-permute-start.1 = (bf16[512,256]{1,0:T(8,128)(2,1)S(1)}, bf16[512,256]{1,0:T(8,128)(2,1)S(1)}, u32[]{:S(2)}, u32[]{:S(2)}) collective-permute-start(bf16[512,256]{1,0:T(8,128)(2,1)S(1)} %get-tuple-element.83.refs_0_), channel_id=1, source_target_pairs={{0,4},{1,5},{2,6},{3,7},{4,8},{5,9},{6,10},{7,11},{8,12},{9,13},{1... | collective-permute-start | bytes 786440 | tf_op jit(solution)/shard_map/ppermute | solution.py:251
  4.9 9.2 %collective-permute-start.2 = (bf16[512,256]{1,0:T(8,128)(2,1)S(1)}, bf16[512,256]{1,0:T(8,128)(2,1)S(1)}, u32[]{:S(2)}, u32[]{:S(2)}) collective-permute-start(bf16[512,256]{1,0:T(8,128)(2,1)S(1)} %get-tuple-element.83.refs_0_), channel_id=1, source_target_pairs={{0,2},{1,3},{2,0},{3,1},{4,6},{5,7},{6,4},{7,5},{8,10},{9,11},{10,... | collective-permute-start | bytes 786440 | tf_op jit(solution)/shard_map/ppermute | solution.py:248
  6.4 13.2 %collective-permute-start.10 = (bf16[512,256]{1,0:T(8,128)(2,1)S(1)}, bf16[512,256]{1,0:T(8,128)(2,1)S(1)}, u32[]{:S(2)}, u32[]{:S(2)}) collective-permute-start(bf16[512,256]{1,0:T(8,128)(2,1)S(1)} %get-tuple-element.82.refs_7_), channel_id=1, source_target_pairs={{0,2},{1,3},{2,0},{3,1},{4,6},{5,7},{6,4},{7,5},{8,10},{9,11},{10,... | collective-permute-start | bytes 786440 | tf_op jit(solution)/shard_map/ppermute | solution.py:248
  6.9 12.8 %collective-permute-start.9 = (bf16[512,256]{1,0:T(8,128)(2,1)S(1)}, bf16[512,256]{1,0:T(8,128)(2,1)S(1)}, u32[]{:S(2)}, u32[]{:S(2)}) collective-permute-start(bf16[512,256]{1,0:T(8,128)(2,1)S(1)} %get-tuple-element.82.refs_7_), channel_id=1, source_target_pairs={{0,4},{1,5},{2,6},{3,7},{4,8},{5,9},{6,10},{7,11},{8,12},{9,13},{1... | collective-permute-start | bytes 786440 | tf_op jit(solution)/shard_map/ppermute | solution.py:251
  14.0 11.2 %collective-permute-start.3 = (bf16[512,256]{1,0:T(8,128)(2,1)S(1)}, bf16[512,256]{1,0:T(8,128)(2,1)S(1)}, u32[]{:S(2)}, u32[]{:S(2)}) collective-permute-start(bf16[512,256]{1,0:T(8,128)(2,1)S(1)} %collective-permute-done.1.refs_2_), channel_id=1, source_target_pairs={{0,4},{1,5},{2,6},{3,7},{4,8},{5,9},{6,10},{7,11},{8,12},{9,13},{1... | collective-permute-start | bytes 786440 | tf_op jit(solution)/shard_map/ppermute | solution.py:251
  15.6 9.7 %collective-permute-start.4 = (bf16[512,256]{1,0:T(8,128)(2,1)S(1)}, bf16[512,256]{1,0:T(8,128)(2,1)S(1)}, u32[]{:S(2)}, u32[]{:S(2)}) collective-permute-start(bf16[512,256]{1,0:T(8,128)(2,1)S(1)} %collective-permute-done.1.refs_2_), channel_id=1, source_target_pairs={{0,2},{1,3},{2,0},{3,1},{4,6},{5,7},{6,4},{7,5},{8,10},{9,11},{10,... | collective-permute-start | bytes 786440 | tf_op jit(solution)/shard_map/ppermute | solution.py:248
  19.7 11.2 %collective-permute-start.11 = (bf16[512,256]{1,0:T(8,128)(2,1)S(1)}, bf16[512,256]{1,0:T(8,128)(2,1)S(1)}, u32[]{:S(2)}, u32[]{:S(2)}) collective-permute-start(bf16[512,256]{1,0:T(8,128)(2,1)S(1)} %collective-permute-done.9.refs_9_), channel_id=1, source_target_pairs={{0,4},{1,5},{2,6},{3,7},{4,8},{5,9},{6,10},{7,11},{8,12},{9,13},{1... | collective-permute-start | bytes 786440 | tf_op jit(solution)/shard_map/ppermute | solution.py:251
  21.2 9.7 %collective-permute-start.12 = (bf16[512,256]{1,0:T(8,128)(2,1)S(1)}, bf16[512,256]{1,0:T(8,128)(2,1)S(1)}, u32[]{:S(2)}, u32[]{:S(2)}) collective-permute-start(bf16[512,256]{1,0:T(8,128)(2,1)S(1)} %collective-permute-done.9.refs_9_), channel_id=1, source_target_pairs={{0,2},{1,3},{2,0},{3,1},{4,6},{5,7},{6,4},{7,5},{8,10},{9,11},{10,... | collective-permute-start | bytes 786440 | tf_op jit(solution)/shard_map/ppermute | solution.py:248
  25.3 11.2 %collective-permute-start.6 = (bf16[512,256]{1,0:T(8,128)(2,1)S(1)}, bf16[512,256]{1,0:T(8,128)(2,1)S(1)}, u32[]{:S(2)}, u32[]{:S(2)}) collective-permute-start(bf16[512,256]{1,0:T(8,128)(2,1)S(1)} %collective-permute-done.3.refs_4_), channel_id=1, source_target_pairs={{0,4},{1,5},{2,6},{3,7},{4,8},{5,9},{6,10},{7,11},{8,12},{9,13},{1... | collective-permute-start | bytes 786440 | tf_op jit(solution)/shard_map/ppermute | solution.py:251
  26.8 9.7 %collective-permute-start.7 = (bf16[512,256]{1,0:T(8,128)(2,1)S(1)}, bf16[512,256]{1,0:T(8,128)(2,1)S(1)}, u32[]{:S(2)}, u32[]{:S(2)}) collective-permute-start(bf16[512,256]{1,0:T(8,128)(2,1)S(1)} %collective-permute-done.3.refs_4_), channel_id=1, source_target_pairs={{0,2},{1,3},{2,0},{3,1},{4,6},{5,7},{6,4},{7,5},{8,10},{9,11},{10,... | collective-permute-start | bytes 786440 | tf_op jit(solution)/shard_map/ppermute | solution.py:248
  30.9 11.0 %collective-permute-start.13 = (bf16[512,256]{1,0:T(8,128)(2,1)S(1)}, bf16[512,256]{1,0:T(8,128)(2,1)S(1)}, u32[]{:S(2)}, u32[]{:S(2)}) collective-permute-start(bf16[512,256]{1,0:T(8,128)(2,1)S(1)} %collective-permute-done.11.refs_11_), channel_id=1, source_target_pairs={{0,4},{1,5},{2,6},{3,7},{4,8},{5,9},{6,10},{7,11},{8,12},{9,13},{1... | collective-permute-start | bytes 786440 | tf_op jit(solution)/shard_map/ppermute | solution.py:251
  32.4 9.5 %collective-permute-start.14 = (bf16[512,256]{1,0:T(8,128)(2,1)S(1)}, bf16[512,256]{1,0:T(8,128)(2,1)}, u32[]{:S(2)}, u32[]{:S(2)}) collective-permute-start(bf16[512,256]{1,0:T(8,128)(2,1)S(1)} %collective-permute-done.11.refs_11_), channel_id=1, source_target_pairs={{0,2},{1,3},{2,0},{3,1},{4,6},{5,7},{6,4},{7,5},{8,10},{9,11},{10,... | collective-permute-start | bytes 786440 | tf_op jit(solution)/shard_map/ppermute | solution.py:248
  41.9 10.1 %collective-permute-start.15 = (bf16[512,256]{1,0:T(8,128)(2,1)S(1)}, bf16[512,256]{1,0:T(8,128)(2,1)S(1)}, u32[]{:S(2)}, u32[]{:S(2)}) collective-permute-start(bf16[512,256]{1,0:T(8,128)(2,1)S(1)} %collective-permute-done.10.refs_8_), channel_id=1, source_target_pairs={{0,12},{1,13},{2,14},{3,15},{4,0},{5,1},{6,2},{7,3},{8,4},{9,5},{1... | collective-permute-start | bytes 786440 | tf_op jit(solution)/shard_map/ppermute | solution.py:251
  43.9 8.2 %collective-permute-start.8 = (bf16[512,256]{1,0:T(8,128)(2,1)S(1)}, bf16[512,256]{1,0:T(8,128)(2,1)S(1)}, u32[]{:S(2)}, u32[]{:S(2)}) collective-permute-start(bf16[512,256]{1,0:T(8,128)(2,1)S(1)} %collective-permute-done.6.refs_6_), channel_id=1, source_target_pairs={{0,2},{1,3},{2,0},{3,1},{4,6},{5,7},{6,4},{7,5},{8,10},{9,11},{10,... | collective-permute-start | bytes 786440 | tf_op jit(solution)/shard_map/ppermute | solution.py:248
  45.4 12.6 %collective-permute-start.5 = (bf16[384,4096]{1,0:T(8,128)(2,1)}, bf16[384,4096]{1,0:T(8,128)(2,1)}, u32[]{:S(2)}, u32[]{:S(2)}) collective-permute-start(bf16[384,4096]{1,0:T(8,128)(2,1)} %own_ref.9), channel_id=1, source_target_pairs={{0,1},{1,0},{2,3},{3,2},{4,5},{5,4},{6,7},{7,6},{8,9},{9,8},{10,11... | collective-permute-start | bytes 9437192 | tf_op jit(solution)/shard_map/ppermute | solution.py:245
  53.9 3.6 %collective-permute-start.16 = (f32[768,512]{1,0:T(8,128)S(1)}, f32[768,512]{1,0:T(8,128)S(1)}, u32[]{:S(2)}, u32[]{:S(2)}) collective-permute-start(f32[768,512]{1,0:T(8,128)S(1)} %project.3), channel_id=1, source_target_pairs={{0,1},{1,0},{2,3},{3,2},{4,5},{5,4},{6,7},{7,6},{8,9},{9,8},{10,11... | collective-permute-start | bytes 4718600 | tf_op jit(solution)/shard_map/ppermute | solution.py:245
  59.4 9.2 %collective-permute-start.17 = (bf16[256,512]{1,0:T(8,128)(2,1)S(1)}, bf16[256,512]{1,0:T(8,128)(2,1)S(1)}, u32[]{:S(2)}, u32[]{:S(2)}) collective-permute-start(bf16[256,512]{1,0:T(8,128)(2,1)S(1)} %outer.3), channel_id=1, source_target_pairs={{0,2},{1,3},{2,0},{3,1},{4,6},{5,7},{6,4},{7,5},{8,10},{9,11},{10,... | collective-permute-start | bytes 786440 | tf_op jit(solution)/shard_map/ppermute | solution.py:248
  63.5 10.7 %collective-permute-start.19 = (bf16[256,512]{1,0:T(8,128)(2,1)S(1)}, bf16[256,512]{1,0:T(8,128)(2,1)S(1)}, u32[]{:S(2)}, u32[]{:S(2)}) collective-permute-start(bf16[256,512]{1,0:T(8,128)(2,1)S(1)} %get-tuple-element.61), channel_id=1, source_target_pairs={{0,2},{1,3},{2,0},{3,1},{4,6},{5,7},{6,4},{7,5},{8,10},{9,11},{10,... | collective-permute-start | bytes 786440 | tf_op jit(solution)/shard_map/ppermute | solution.py:248
  64.9 15.0 %collective-permute-start.21 = (bf16[256,512]{1,0:T(8,128)(2,1)S(1)}, bf16[256,512]{1,0:T(8,128)(2,1)S(1)}, u32[]{:S(2)}, u32[]{:S(2)}) collective-permute-start(bf16[256,512]{1,0:T(8,128)(2,1)S(1)} %get-tuple-element.63), channel_id=1, source_target_pairs={{0,2},{1,3},{2,0},{3,1},{4,6},{5,7},{6,4},{7,5},{8,10},{9,11},{10,... | collective-permute-start | bytes 786440 | tf_op jit(solution)/shard_map/ppermute | solution.py:248
  65.6 19.3 %collective-permute-start.18 = (bf16[256,512]{1,0:T(8,128)(2,1)S(1)}, bf16[256,512]{1,0:T(8,128)(2,1)S(1)}, u32[]{:S(2)}, u32[]{:S(2)}) collective-permute-start(bf16[256,512]{1,0:T(8,128)(2,1)S(1)} %get-tuple-element.59), channel_id=1, source_target_pairs={{0,2},{1,3},{2,0},{3,1},{4,6},{5,7},{6,4},{7,5},{8,10},{9,11},{10,... | collective-permute-start | bytes 786440 | tf_op jit(solution)/shard_map/ppermute | solution.py:248
  68.7 11.1 %collective-permute-start.22 = (bf16[256,512]{1,0:T(8,128)(2,1)S(1)}, bf16[256,512]{1,0:T(8,128)(2,1)S(1)}, u32[]{:S(2)}, u32[]{:S(2)}) collective-permute-start(bf16[256,512]{1,0:T(8,128)(2,1)S(1)} %convert_add_fusion.1), channel_id=1, source_target_pairs={{0,4},{1,5},{2,6},{3,7},{4,8},{5,9},{6,10},{7,11},{8,12},{9,13},{1... | collective-permute-start | bytes 786440 | tf_op jit(solution)/shard_map/ppermute | solution.py:251
  74.3 10.6 %collective-permute-start.20 = (bf16[256,512]{1,0:T(8,128)(2,1)S(1)}, bf16[256,512]{1,0:T(8,128)(2,1)S(1)}, u32[]{:S(2)}, u32[]{:S(2)}) collective-permute-start(bf16[256,512]{1,0:T(8,128)(2,1)S(1)} %add_convert_fusion.2), channel_id=1, source_target_pairs={{0,12},{1,13},{2,14},{3,15},{4,0},{5,1},{6,2},{7,3},{8,4},{9,5},{1... | collective-permute-start | bytes 786440 | tf_op jit(solution)/shard_map/ppermute | solution.py:251
  80.0 9.1 %collective-permute-start.23 = (bf16[256,512]{1,0:T(8,128)(2,1)S(1)}, bf16[256,512]{1,0:T(8,128)(2,1)S(1)}, u32[]{:S(2)}, u32[]{:S(2)}) collective-permute-start(bf16[256,512]{1,0:T(8,128)(2,1)S(1)} %add_convert_fusion.1), channel_id=1, source_target_pairs={{0,4},{1,5},{2,6},{3,7},{4,8},{5,9},{6,10},{7,11},{8,12},{9,13},{1... | collective-permute-start | bytes 786440 | tf_op jit(solution)/shard_map/ppermute | solution.py:251
  89.1 28.3 %copy-start = (bf16[512,512]{1,0:T(8,128)(2,1)S(1)}, bf16[512,512]{1,0:T(8,128)(2,1)}, u32[]{:S(2)}) copy-start(bf16[512,512]{1,0:T(8,128)(2,1)} %projector_ref.3) | copy-start | bytes 1572868
  90.5 6.8 %collective-permute-start.30 = (bf16[256,256]{1,0:T(8,128)(2,1)S(1)}, bf16[256,256]{1,0:T(8,128)(2,1)S(1)}, u32[]{:S(2)}, u32[]{:S(2)}) collective-permute-start(bf16[256,256]{1,0:T(8,128)(2,1)S(1)} %get-tuple-element.84), channel_id=1, source_target_pairs={{0,4},{1,5},{2,6},{3,7},{4,8},{5,9},{6,10},{7,11},{8,12},{9,13},{1... | collective-permute-start | bytes 393224 | tf_op jit(solution)/shard_map/ppermute | solution.py:251
  90.6 6.8 %collective-permute-start.31 = (bf16[256,256]{1,0:T(8,128)(2,1)S(1)}, bf16[256,256]{1,0:T(8,128)(2,1)S(1)}, u32[]{:S(2)}, u32[]{:S(2)}) collective-permute-start(bf16[256,256]{1,0:T(8,128)(2,1)S(1)} %get-tuple-element.84), channel_id=1, source_target_pairs={{0,2},{1,3},{2,0},{3,1},{4,6},{5,7},{6,4},{7,5},{8,10},{9,11},{10,... | collective-permute-start | bytes 393224 | tf_op jit(solution)/shard_map/ppermute | solution.py:248
  91.0 7.7 %collective-permute-start.24 = (bf16[256,256]{1,0:T(8,128)(2,1)S(1)}, bf16[256,256]{1,0:T(8,128)(2,1)S(1)}, u32[]{:S(2)}, u32[]{:S(2)}) collective-permute-start(bf16[256,256]{1,0:T(8,128)(2,1)S(1)} %get-tuple-element.85), channel_id=1, source_target_pairs={{0,4},{1,5},{2,6},{3,7},{4,8},{5,9},{6,10},{7,11},{8,12},{9,13},{1... | collective-permute-start | bytes 393224 | tf_op jit(solution)/shard_map/ppermute | solution.py:251
  92.5 6.2 %collective-permute-start.25 = (bf16[256,256]{1,0:T(8,128)(2,1)S(1)}, bf16[256,256]{1,0:T(8,128)(2,1)S(1)}, u32[]{:S(2)}, u32[]{:S(2)}) collective-permute-start(bf16[256,256]{1,0:T(8,128)(2,1)S(1)} %get-tuple-element.85), channel_id=1, source_target_pairs={{0,2},{1,3},{2,0},{3,1},{4,6},{5,7},{6,4},{7,5},{8,10},{9,11},{10,... | collective-permute-start | bytes 393224 | tf_op jit(solution)/shard_map/ppermute | solution.py:248
  93.9 19.9 %collective-permute-start.40 = (bf16[256,512]{1,0:T(8,128)(2,1)S(1)}, bf16[256,512]{1,0:T(8,128)(2,1)S(1)}, u32[]{:S(2)}, u32[]{:S(2)}) collective-permute-start(bf16[256,512]{1,0:T(8,128)(2,1)S(1)} %get-tuple-element.79.refs_0_), channel_id=1, source_target_pairs={{0,1},{1,0},{2,3},{3,2},{4,5},{5,4},{6,7},{7,6},{8,9},{9,8},{10,11... | collective-permute-start | bytes 786440 | tf_op jit(solution)/shard_map/ppermute | solution.py:245
  97.3 6.8 %collective-permute-start.32 = (bf16[256,256]{1,0:T(8,128)(2,1)S(1)}, bf16[256,256]{1,0:T(8,128)(2,1)S(1)}, u32[]{:S(2)}, u32[]{:S(2)}) collective-permute-start(bf16[256,256]{1,0:T(8,128)(2,1)S(1)} %collective-permute-done.30), channel_id=1, source_target_pairs={{0,4},{1,5},{2,6},{3,7},{4,8},{5,9},{6,10},{7,11},{8,12},{9,13},{1... | collective-permute-start | bytes 393224 | tf_op jit(solution)/shard_map/ppermute | solution.py:251
  97.7 6.4 %collective-permute-start.33 = (bf16[256,256]{1,0:T(8,128)(2,1)S(1)}, bf16[256,256]{1,0:T(8,128)(2,1)S(1)}, u32[]{:S(2)}, u32[]{:S(2)}) collective-permute-start(bf16[256,256]{1,0:T(8,128)(2,1)S(1)} %collective-permute-done.30), channel_id=1, source_target_pairs={{0,2},{1,3},{2,0},{3,1},{4,6},{5,7},{6,4},{7,5},{8,10},{9,11},{10,... | collective-permute-start | bytes 393224 | tf_op jit(solution)/shard_map/ppermute | solution.py:248
  98.7 7.7 %collective-permute-start.26 = (bf16[256,256]{1,0:T(8,128)(2,1)S(1)}, bf16[256,256]{1,0:T(8,128)(2,1)S(1)}, u32[]{:S(2)}, u32[]{:S(2)}) collective-permute-start(bf16[256,256]{1,0:T(8,128)(2,1)S(1)} %collective-permute-done.24), channel_id=1, source_target_pairs={{0,4},{1,5},{2,6},{3,7},{4,8},{5,9},{6,10},{7,11},{8,12},{9,13},{1... | collective-permute-start | bytes 393224 | tf_op jit(solution)/shard_map/ppermute | solution.py:251
  100.2 6.3 %collective-permute-start.27 = (bf16[256,256]{1,0:T(8,128)(2,1)S(1)}, bf16[256,256]{1,0:T(8,128)(2,1)S(1)}, u32[]{:S(2)}, u32[]{:S(2)}) collective-permute-start(bf16[256,256]{1,0:T(8,128)(2,1)S(1)} %collective-permute-done.24), channel_id=1, source_target_pairs={{0,2},{1,3},{2,0},{3,1},{4,6},{5,7},{6,4},{7,5},{8,10},{9,11},{10,... | collective-permute-start | bytes 393224 | tf_op jit(solution)/shard_map/ppermute | solution.py:248
  104.1 6.8 %collective-permute-start.34 = (bf16[256,256]{1,0:T(8,128)(2,1)S(1)}, bf16[256,256]{1,0:T(8,128)(2,1)S(1)}, u32[]{:S(2)}, u32[]{:S(2)}) collective-permute-start(bf16[256,256]{1,0:T(8,128)(2,1)S(1)} %collective-permute-done.32), channel_id=1, source_target_pairs={{0,4},{1,5},{2,6},{3,7},{4,8},{5,9},{6,10},{7,11},{8,12},{9,13},{1... | collective-permute-start | bytes 393224 | tf_op jit(solution)/shard_map/ppermute | solution.py:251
  104.7 6.1 %collective-permute-start.35 = (bf16[256,256]{1,0:T(8,128)(2,1)S(1)}, bf16[256,256]{1,0:T(8,128)(2,1)S(1)}, u32[]{:S(2)}, u32[]{:S(2)}) collective-permute-start(bf16[256,256]{1,0:T(8,128)(2,1)S(1)} %collective-permute-done.32), channel_id=1, source_target_pairs={{0,2},{1,3},{2,0},{3,1},{4,6},{5,7},{6,4},{7,5},{8,10},{9,11},{10,... | collective-permute-start | bytes 393224 | tf_op jit(solution)/shard_map/ppermute | solution.py:248
  106.5 6.8 %collective-permute-start.28 = (bf16[256,256]{1,0:T(8,128)(2,1)S(1)}, bf16[256,256]{1,0:T(8,128)(2,1)S(1)}, u32[]{:S(2)}, u32[]{:S(2)}) collective-permute-start(bf16[256,256]{1,0:T(8,128)(2,1)S(1)} %collective-permute-done.26), channel_id=1, source_target_pairs={{0,4},{1,5},{2,6},{3,7},{4,8},{5,9},{6,10},{7,11},{8,12},{9,13},{1... | collective-permute-start | bytes 393224 | tf_op jit(solution)/shard_map/ppermute | solution.py:251
  108.0 5.3 %collective-permute-start.29 = (bf16[256,256]{1,0:T(8,128)(2,1)S(1)}, bf16[256,256]{1,0:T(8,128)(2,1)S(1)}, u32[]{:S(2)}, u32[]{:S(2)}) collective-permute-start(bf16[256,256]{1,0:T(8,128)(2,1)S(1)} %collective-permute-done.26), channel_id=1, source_target_pairs={{0,2},{1,3},{2,0},{3,1},{4,6},{5,7},{6,4},{7,5},{8,10},{9,11},{10,... | collective-permute-start | bytes 393224 | tf_op jit(solution)/shard_map/ppermute | solution.py:248
  110.9 4.5 %collective-permute-start.42 = (bf16[512,256]{1,0:T(8,128)(2,1)S(1)}, bf16[512,256]{1,0:T(8,128)(2,1)S(1)}, u32[]{:S(2)}, u32[]{:S(2)}) collective-permute-start(bf16[512,256]{1,0:T(8,128)(2,1)S(1)} %constant_dynamic-update-slice_fusion.6.refs_2_), channel_id=1, source_target_pairs={{0,1},{1,0},{2,3},{3,2},{4,5},{5,4},{6,7},{7,6},{8,9},{9,8},{10,11... | collective-permute-start | bytes 786440 | tf_op jit(solution)/shard_map/ppermute | solution.py:245
  110.9 6.0 %collective-permute-start.41 = (bf16[512,256]{1,0:T(8,128)(2,1)S(1)}, bf16[512,256]{1,0:T(8,128)(2,1)S(1)}, u32[]{:S(2)}, u32[]{:S(2)}) collective-permute-start(bf16[512,256]{1,0:T(8,128)(2,1)S(1)} %constant_dynamic-update-slice_fusion.4.refs_1_), channel_id=1, source_target_pairs={{0,1},{1,0},{2,3},{3,2},{4,5},{5,4},{6,7},{7,6},{8,9},{9,8},{10,11... | collective-permute-start | bytes 786440 | tf_op jit(solution)/shard_map/ppermute | solution.py:245
  113.3 3.6 %collective-permute-start.44 = (bf16[512,256]{1,0:T(8,128)(2,1)S(1)}, bf16[512,256]{1,0:T(8,128)(2,1)S(1)}, u32[]{:S(2)}, u32[]{:S(2)}) collective-permute-start(bf16[512,256]{1,0:T(8,128)(2,1)S(1)} %constant_dynamic-update-slice_fusion.10.refs_4_), channel_id=1, source_target_pairs={{0,1},{1,0},{2,3},{3,2},{4,5},{5,4},{6,7},{7,6},{8,9},{9,8},{10,11... | collective-permute-start | bytes 786440 | tf_op jit(solution)/shard_map/ppermute | solution.py:245
  113.3 4.1 %collective-permute-start.43 = (bf16[512,256]{1,0:T(8,128)(2,1)S(1)}, bf16[512,256]{1,0:T(8,128)(2,1)S(1)}, u32[]{:S(2)}, u32[]{:S(2)}) collective-permute-start(bf16[512,256]{1,0:T(8,128)(2,1)S(1)} %constant_dynamic-update-slice_fusion.8.refs_3_), channel_id=1, source_target_pairs={{0,1},{1,0},{2,3},{3,2},{4,5},{5,4},{6,7},{7,6},{8,9},{9,8},{10,11... | collective-permute-start | bytes 786440 | tf_op jit(solution)/shard_map/ppermute | solution.py:245
  113.9 8.0 %collective-permute-start.36 = (bf16[256,256]{1,0:T(8,128)(2,1)S(1)}, bf16[256,256]{1,0:T(8,128)(2,1)S(1)}, u32[]{:S(2)}, u32[]{:S(2)}) collective-permute-start(bf16[256,256]{1,0:T(8,128)(2,1)S(1)} %collective-permute-done.28), channel_id=1, source_target_pairs={{0,2},{1,3},{2,0},{3,1},{4,6},{5,7},{6,4},{7,5},{8,10},{9,11},{10,... | collective-permute-start | bytes 393224 | tf_op jit(solution)/shard_map/ppermute | solution.py:248
  115.4 6.4 %collective-permute-start.37 = (bf16[256,256]{1,0:T(8,128)(2,1)S(1)}, bf16[256,256]{1,0:T(8,128)(2,1)S(1)}, u32[]{:S(2)}, u32[]{:S(2)}) collective-permute-start(bf16[256,256]{1,0:T(8,128)(2,1)S(1)} %collective-permute-done.31), channel_id=1, source_target_pairs={{0,12},{1,13},{2,14},{3,15},{4,0},{5,1},{6,2},{7,3},{8,4},{9,5},{1... | collective-permute-start | bytes 393224 | tf_op jit(solution)/shard_map/ppermute | solution.py:251
  116.9 6.4 %collective-permute-start.39 = (bf16[512,256]{1,0:T(8,128)(2,1)S(1)}, bf16[512,256]{1,0:T(8,128)(2,1)S(1)}, u32[]{:S(2)}, u32[]{:S(2)}) collective-permute-start(bf16[512,256]{1,0:T(8,128)(2,1)S(1)} %constant_dynamic-update-slice_fusion.2.refs_1_), channel_id=1, source_target_pairs={{0,1},{1,0},{2,3},{3,2},{4,5},{5,4},{6,7},{7,6},{8,9},{9,8},{10,11... | collective-permute-start | bytes 786440 | tf_op jit(solution)/shard_map/ppermute | solution.py:245
  116.9 6.4 %collective-permute-start.38 = (bf16[512,256]{1,0:T(8,128)(2,1)S(1)}, bf16[512,256]{1,0:T(8,128)(2,1)S(1)}, u32[]{:S(2)}, u32[]{:S(2)}) collective-permute-start(bf16[512,256]{1,0:T(8,128)(2,1)S(1)} %constant_dynamic-update-slice_fusion.refs_0_), channel_id=1, source_target_pairs={{0,1},{1,0},{2,3},{3,2},{4,5},{5,4},{6,7},{7,6},{8,9},{9,8},{10,11... | collective-permute-start | bytes 786440 | tf_op jit(solution)/shard_map/ppermute | solution.py:245
  121.7 1.4 %collective-permute-start.46 = (bf16[256,256]{1,0:T(8,128)(2,1)S(1)}, bf16[256,256]{1,0:T(8,128)(2,1)S(1)}, u32[]{:S(2)}, u32[]{:S(2)}) collective-permute-start(bf16[256,256]{1,0:T(8,128)(2,1)S(1)} %collective-permute-done.37.refs_3_), channel_id=1, source_target_pairs={{0,1},{1,0},{2,3},{3,2},{4,5},{5,4},{6,7},{7,6},{8,9},{9,8},{10,11... | collective-permute-start | bytes 393224 | tf_op jit(solution)/shard_map/ppermute | solution.py:245
  121.9 1.5 %collective-permute-start.45 = (bf16[256,256]{1,0:T(8,128)(2,1)S(1)}, bf16[256,256]{1,0:T(8,128)(2,1)S(1)}, u32[]{:S(2)}, u32[]{:S(2)}) collective-permute-start(bf16[256,256]{1,0:T(8,128)(2,1)S(1)} %collective-permute-done.36.refs_2_), channel_id=1, source_target_pairs={{0,1},{1,0},{2,3},{3,2},{4,5},{5,4},{6,7},{7,6},{8,9},{9,8},{10,11... | collective-permute-start | bytes 393224 | tf_op jit(solution)/shard_map/ppermute | solution.py:245
  (2 other events, 40.7 us)

commit v9 on v8

--- a/solution.py
+++ b/solution.py
@@ -61,23 +61,23 @@
     return pltpu.with_memory_space_constraint(x, pltpu.HBM)
 
 
-def call(kernel, scalars, arrays, outs, scratch, *, weight, flops, moved, name, aliases=None, in_hbm=0):
-    anywhere = pl.BlockSpec(memory_space=pl.ANY)
+def call(kernel, scalars, far, near, outs, scratch, *, weight, flops, moved, name, aliases=None):
+    anywhere, vmem = pl.BlockSpec(memory_space=pl.ANY), pl.BlockSpec(memory_space=pltpu.VMEM)
     return pl.pallas_call(
         kernel,
         grid_spec=pltpu.PrefetchScalarGridSpec(
             num_scalar_prefetch=1,
             grid=(),
-            in_specs=[anywhere] * len(arrays),
-            out_specs=[anywhere] * len(outs),
+            in_specs=[anywhere] * len(far) + [vmem] * len(near),
+            out_specs=[vmem if inside else anywhere for inside, _ in outs],
             scratch_shapes=scratch,
         ),
-        out_shape=outs,
+        out_shape=[shape for _, shape in outs],
         input_output_aliases=aliases or {},
         compiler_params=params(),
         cost_estimate=cost(weight, flops, moved),
         name=name,
-    )(scalars, *[pinned(x) for x in arrays[:in_hbm]], *arrays[in_hbm:])
+    )(scalars, *far, *near)
 
 
 def project(activations, sibling, at, blocks, before, weight):
@@ -122,8 +122,9 @@
     return call(
         kernel,
         at,
-        [activations, sibling, *flat, *held],
-        [jax.ShapeDtypeStruct((2 * rows, wide), F32)],
+        [pinned(activations), pinned(sibling), *flat, *held],
+        [],
+        [(False, jax.ShapeDtypeStruct((2 * rows, wide), F32))],
         [
             pltpu.VMEM((2 * rows, many * depth), BF16),
             pltpu.VMEM((many * depth, wide), BF16),
@@ -134,7 +135,60 @@
         flops=4 * rows * depth * len(flat) * cols,
         moved=4 * rows * depth * many + 2 * depth * len(flat) * cols + 8 * rows * wide,
         name="project",
-        in_hbm=2,
+    )[0]
+
+
+def project_late(activations, sibling, at, blocks, before, weight):
+    chunks, many = len(blocks), at.shape[0]
+    flat = [chunk[j] for chunk in blocks for j in sorted(chunk)]
+    (depth, cols), rows = flat[0].shape, activations.shape[0]
+    wide, held = chunks * cols, [] if before is None else [before]
+    moved = flat if len(flat) > chunks else []
+
+    def kernel(at_ref, own_ref, sib_ref, *refs):
+        block_refs, out_ref = refs[: len(flat)], refs[len(flat) + len(held)]
+        a, b, sems = refs[len(flat) + len(held) + 1 :]
+        started = []
+
+        def start(source, target):
+            started.append(pltpu.make_async_copy(source, target, sems.at[len(started)]))
+            started[-1].start()
+
+        core = lax.rem(lax.axis_index("dp"), 2)
+        here, there = (pl.ds(pl.multiple_of(c * rows, rows), rows) for c in (core, 1 - core))
+        for j in range(many):
+            columns = pl.ds(pl.multiple_of(at_ref[j] * depth, depth), depth)
+            start(own_ref.at[:, columns], a.at[here, pl.ds(j * depth, depth)])
+            start(sib_ref.at[:, columns], a.at[there, pl.ds(j * depth, depth)])
+        places = [(i, j) for i, chunk in enumerate(blocks) for j in sorted(chunk)]
+        if moved:
+            for ref, (i, j) in zip(block_refs, places):
+                start(ref, b.at[pl.ds(j * depth, depth), pl.ds(i * cols, cols)])
+        for copy in started:
+            copy.wait()
+        for i, chunk in enumerate(blocks):
+            part = slice(i * cols, (i + 1) * cols)
+            deep = slice(min(chunk) * depth, (max(chunk) + 1) * depth)
+            block = b[deep, part] if moved else block_refs[i][...]
+            term = jnp.dot(a[:, deep], block, preferred_element_type=F32)
+            out_ref[:, part] = refs[len(flat)][:, part] + term if held else term
+
+    far = [pinned(activations), pinned(sibling)]
+    return call(
+        kernel,
+        at,
+        far + moved,
+        ([] if moved else flat) + held,
+        [(True, jax.ShapeDtypeStruct((2 * rows, wide), F32))],
+        [
+            pltpu.VMEM((2 * rows, many * depth), BF16),
+            pltpu.VMEM((many * depth, wide) if moved else (16, 128), BF16),
+            pltpu.SemaphoreType.DMA((2 * many + len(moved),)),
+        ],
+        weight=weight,
+        flops=4 * rows * depth * len(flat) * cols,
+        moved=4 * rows * depth * many + 2 * depth * len(flat) * cols + 8 * rows * wide,
+        name="project",
     )[0]
 
 
@@ -157,21 +211,18 @@
             block = g[:, j * width : (j + 1) * width].T
             outs[j][...] = jnp.dot(block, projected_ref[...], preferred_element_type=F32).astype(dtypes[j])
 
-    whole = lambda *shape: pl.BlockSpec(shape, lambda j, at_ref: (0, 0))
-    return pl.pallas_call(
-        kernel,
-        grid_spec=pltpu.PrefetchScalarGridSpec(
-            num_scalar_prefetch=1,
-            grid=(1,),
-            in_specs=[pl.BlockSpec(memory_space=pl.ANY)] * 2 + [whole(2 * rows, cols)],
-            out_specs=[whole(width, cols)] * many,
-            scratch_shapes=[pltpu.VMEM((2 * rows, many * width), BF16), pltpu.SemaphoreType.DMA((2 * many,))],
-        ),
-        out_shape=[jax.ShapeDtypeStruct((width, cols), dtype) for dtype in dtypes],
-        compiler_params=params(),
-        cost_estimate=cost(W_OUTER, 4 * rows * width * many * cols, many * (4 * rows * width + 4 * width * cols)),
+    return call(
+        kernel,
+        at,
+        [pinned(out_grads), pinned(sibling)],
+        [projected],
+        [(True, jax.ShapeDtypeStruct((width, cols), dtype)) for dtype in dtypes],
+        [pltpu.VMEM((2 * rows, many * width), BF16), pltpu.SemaphoreType.DMA((2 * many,))],
+        weight=W_OUTER,
+        flops=4 * rows * width * many * cols,
+        moved=many * (4 * rows * width + 4 * width * cols),
         name="outer",
-    )(at, pinned(out_grads), pinned(sibling), projected)
+    )
 
 
 def back(groups, projector, at, rows, rows_in_all, before, weight):
@@ -179,57 +230,43 @@
     arrays = [x for group in groups for x in group]
     held = [] if before is None else [before]
 
-    def kernel(at_ref, projector_ref, *refs):
-        array_refs, out_ref = refs[: len(arrays)], refs[len(arrays) + len(held)]
-        p, pt, d, o, in_sems, out_sems = refs[len(arrays) + len(held) + 1 :]
-        loads, starts, start = [], [], 0
-        p_copy = pltpu.make_async_copy(projector_ref, p, in_sems.at[len(arrays)])
-        p_copy.start()
+    def kernel(at_ref, *refs):
+        projector_ref, *array_refs = refs[len(held) : len(held) + 1 + len(arrays)]
+        out_ref, pt, o, out_sems = refs[len(held) + 1 + len(arrays) :]
+        pt[...] = projector_ref[...].T
+        stores, start = [], 0
         for group in groups:
-            size, column, copies = group[0].shape[0], 0, []
+            size, column, total = group[0].shape[0], 0, None
             for x in group:
-                n = sum(len(some) for some in loads) + len(copies)
-                target = d.at[pl.ds(start, size), pl.ds(column, x.shape[1])]
-                copies.append(pltpu.make_async_copy(array_refs[n], target, in_sems.at[n]))
-                copies[-1].start()
+                deep = slice(column, column + x.shape[1])
+                term = jnp.dot(array_refs.pop(0)[...], pt[deep, :], preferred_element_type=F32)
+                total = term if total is None else total + term
                 column += x.shape[1]
-            loads.append(copies)
-            starts.append(start)
-            start += size
-        p_copy.wait()
-        pt[...] = p[...].T
-        stores = []
-        for group, copies, start in zip(groups, loads, starts):
-            for copy in copies:
-                copy.wait()
-            size = group[0].shape[0]
-            here = slice(start, start + size)
-            o[here, :] = jnp.dot(d[here, :], pt[...], preferred_element_type=F32).astype(BF16)
+            o[start : start + size, :] = total.astype(BF16)
             for j in range(start // rows, (start + size) // rows):
                 target = out_ref.at[pl.ds(pl.multiple_of(at_ref[j] * rows, rows), rows), :]
                 stores.append(pltpu.make_async_copy(o.at[pl.ds(j * rows, rows), :], target, out_sems.at[j]))
                 stores[-1].start()
+            start += size
         for copy in stores:
             copy.wait()
 
     return call(
         kernel,
         at,
-        [projector, *arrays, *held],
-        [jax.ShapeDtypeStruct((rows_in_all, width), BF16)],
+        held,
+        [projector, *arrays],
+        [(False, jax.ShapeDtypeStruct((rows_in_all, width), BF16))],
         [
-            pltpu.VMEM((width, rank), BF16),
             pltpu.VMEM((rank, width), BF16),
-            pltpu.VMEM((many * rows, rank), BF16),
             pltpu.VMEM((many * rows, width), BF16),
-            pltpu.SemaphoreType.DMA((len(arrays) + 1,)),
             pltpu.SemaphoreType.DMA((many,)),
         ],
         weight=weight,
         flops=2 * many * rows * width * rank,
         moved=2 * many * rows * (width + rank),
         name="back",
-        aliases={2 + len(arrays): 0} if held else None,
+        aliases={1: 0} if held else None,
     )[0]
 
 
@@ -293,7 +330,7 @@
     mine = project(activations, a_sibling, at_in[:last], blocks, None, W_EARLY)
     low = min(soon)
     blocks = [{n - low: block(i, n) for n in range(soon[i], last + 1)} for i in range(CHUNKS)]
-    mine = project(activations, a_sibling, at_in[low:], blocks, mine, W_LATE)
+    mine = project_late(activations, a_sibling, at_in[low:], blocks, mine, W_LATE)
     projected = (mine + swap_core(mine)).astype(BF16)
     (send,) = outer(out_grads, g_sibling, at_out[:1], width, [BF16], projected)
     at = after(at_out[1 : nz + 1], send)

time: 127 us -> 125 us (0.984)
  Pallas kernels: 23.6 us -> 21.3 us
    pallas_call x3 -> x0, Pallas kernels: 7.55 us -> none  [outer(): pl.pallas_call(kernel, grid_spec=pltpu.PrefetchScalarGridSpec(num_scalar_...]
    pallas_call x4 -> x7, Pallas kernels: 16 us -> 21.3 us  [call(): pl.pallas_call(kernel, grid_spec=pltpu.PrefetchScalarGridSpec(num_scalar_...]
  transfers between devices with their start and end apart: 47 -> 47, of which waited for: 20 -> 20; matrix products, arithmetic and copies ran while one was open for 2% -> 2% of each run, Pallas kernels for 15% -> 14%
where the time goes in v9:
time: 125 us; the launch traced here: 124 us
  waiting for transfers between devices  52.9 us (42%)
  starting transfers between devices  45.5 us (36%)
  Pallas kernels  21.3 us (17%)
  other arithmetic  2.22 us (2%)
  local copies, waits for them, and re-layouts  1.47 us (1%)
    ppermute x17, waiting for transfers between devices, shift_z(): return lax.ppermute(x, 'dp', pairs(lambda a, b, c: ((a + k) % nz, b, c)))  33.6 us
    ppermute x17, starting transfers between devices, shift_z(): return lax.ppermute(x, 'dp', pairs(lambda a, b, c: ((a + k) % nz, b, c)))  21.3 us
    pallas_call x7, Pallas kernels, call(): pl.pallas_call(kernel, grid_spec=pltpu.PrefetchScalarGridSpec(num_scalar_...  21.3 us
    ppermute x18, starting transfers between devices, swap_y(): return lax.ppermute(x, 'dp', pairs(lambda a, b, c: (a, 1 - b, c)))  20.9 us
    ppermute x18, waiting for transfers between devices, swap_y(): return lax.ppermute(x, 'dp', pairs(lambda a, b, c: (a, 1 - b, c)))  15.4 us
    ppermute x12, waiting for transfers between devices, swap_core(): return lax.ppermute(x, 'dp', pairs(lambda a, b, c: (a, b, 1 - c)))  3.84 us
    ppermute x12, starting transfers between devices, swap_core(): return lax.ppermute(x, 'dp', pairs(lambda a, b, c: (a, b, 1 - c)))  3.2 us
  transfers between devices with their start and end apart: 47, of which 20 were waited for; matrix products, arithmetic and copies ran while one was open for 2% of the time, Pallas kernels for 14%

profile of v9, /device:TPU:0, one launch (start us, length us, event | category | flops | bytes accessed | tf_op | source)
XLA Modules:
  0.0 124.4 jit_solution(8628970512826725175)
XLA Ops:
  2.2 2.6 %collective-permute-start.1 = (bf16[512,256]{1,0:T(8,128)(2,1)S(1)}, bf16[512,256]{1,0:T(8,128)(2,1)S(1)}, u32[]{:S(2)}, u32[]{:S(2)}) collective-permute-start(bf16[512,256]{1,0:T(8,128)(2,1)S(1)} %get-tuple-element.83.refs_0_), channel_id=1, source_target_pairs={{0,4},{1,5},{2,6},{3,7},{4,8},{5,9},{6,10},{7,11},{8,12},{9,13},{1... | collective-permute-start | bytes 786440 | tf_op jit(solution)/shard_map/ppermute | solution.py:288
  4.9 1.5 %collective-permute-start.2 = (bf16[512,256]{1,0:T(8,128)(2,1)S(1)}, bf16[512,256]{1,0:T(8,128)(2,1)S(1)}, u32[]{:S(2)}, u32[]{:S(2)}) collective-permute-start(bf16[512,256]{1,0:T(8,128)(2,1)S(1)} %get-tuple-element.83.refs_0_), channel_id=1, source_target_pairs={{0,2},{1,3},{2,0},{3,1},{4,6},{5,7},{6,4},{7,5},{8,10},{9,11},{10,... | collective-permute-start | bytes 786440 | tf_op jit(solution)/shard_map/ppermute | solution.py:285
  6.9 1.6 %collective-permute-start.9 = (bf16[512,256]{1,0:T(8,128)(2,1)S(1)}, bf16[512,256]{1,0:T(8,128)(2,1)S(1)}, u32[]{:S(2)}, u32[]{:S(2)}) collective-permute-start(bf16[512,256]{1,0:T(8,128)(2,1)S(1)} %get-tuple-element.82.refs_7_), channel_id=1, source_target_pairs={{0,4},{1,5},{2,6},{3,7},{4,8},{5,9},{6,10},{7,11},{8,12},{9,13},{1... | collective-permute-start | bytes 786440 | tf_op jit(solution)/shard_map/ppermute | solution.py:288
  8.5 5.6 %collective-permute-done.1.refs_2_ = bf16[512,256]{1,0:T(8,128)(2,1)S(1)} collective-permute-done((bf16[512,256]{1,0:T(8,128)(2,1)S(1)}, bf16[512,256]{1,0:T(8,128)(2,1)S(1)}, u32[]{:S(2)}, u32[]{:S(2)}) %collective-permute-start.1) | collective-permute-done | bytes 262176 | tf_op jit(solution)/shard_map/ppermute | solution.py:288
  14.0 1.5 %collective-permute-start.3 = (bf16[512,256]{1,0:T(8,128)(2,1)S(1)}, bf16[512,256]{1,0:T(8,128)(2,1)S(1)}, u32[]{:S(2)}, u32[]{:S(2)}) collective-permute-start(bf16[512,256]{1,0:T(8,128)(2,1)S(1)} %collective-permute-done.1.refs_2_), channel_id=1, source_target_pairs={{0,4},{1,5},{2,6},{3,7},{4,8},{5,9},{6,10},{7,11},{8,12},{9,13},{1... | collective-permute-start | bytes 786440 | tf_op jit(solution)/shard_map/ppermute | solution.py:288
  15.6 1.5 %collective-permute-start.4 = (bf16[512,256]{1,0:T(8,128)(2,1)S(1)}, bf16[512,256]{1,0:T(8,128)(2,1)S(1)}, u32[]{:S(2)}, u32[]{:S(2)}) collective-permute-start(bf16[512,256]{1,0:T(8,128)(2,1)S(1)} %collective-permute-done.1.refs_2_), channel_id=1, source_target_pairs={{0,2},{1,3},{2,0},{3,1},{4,6},{5,7},{6,4},{7,5},{8,10},{9,11},{10,... | collective-permute-start | bytes 786440 | tf_op jit(solution)/shard_map/ppermute | solution.py:285
  17.1 2.5 %collective-permute-done.10.refs_8_ = bf16[512,256]{1,0:T(8,128)(2,1)S(1)} collective-permute-done((bf16[512,256]{1,0:T(8,128)(2,1)S(1)}, bf16[512,256]{1,0:T(8,128)(2,1)S(1)}, u32[]{:S(2)}, u32[]{:S(2)}) %collective-permute-start.10) | collective-permute-done | bytes 262176 | tf_op jit(solution)/shard_map/ppermute | solution.py:285
  19.7 1.5 %collective-permute-start.11 = (bf16[512,256]{1,0:T(8,128)(2,1)S(1)}, bf16[512,256]{1,0:T(8,128)(2,1)S(1)}, u32[]{:S(2)}, u32[]{:S(2)}) collective-permute-start(bf16[512,256]{1,0:T(8,128)(2,1)S(1)} %collective-permute-done.9.refs_9_), channel_id=1, source_target_pairs={{0,4},{1,5},{2,6},{3,7},{4,8},{5,9},{6,10},{7,11},{8,12},{9,13},{1... | collective-permute-start | bytes 786440 | tf_op jit(solution)/shard_map/ppermute | solution.py:288
  21.2 1.5 %collective-permute-start.12 = (bf16[512,256]{1,0:T(8,128)(2,1)S(1)}, bf16[512,256]{1,0:T(8,128)(2,1)S(1)}, u32[]{:S(2)}, u32[]{:S(2)}) collective-permute-start(bf16[512,256]{1,0:T(8,128)(2,1)S(1)} %collective-permute-done.9.refs_9_), channel_id=1, source_target_pairs={{0,2},{1,3},{2,0},{3,1},{4,6},{5,7},{6,4},{7,5},{8,10},{9,11},{10,... | collective-permute-start | bytes 786440 | tf_op jit(solution)/shard_map/ppermute | solution.py:285
  22.7 2.6 %collective-permute-done.3.refs_4_ = bf16[512,256]{1,0:T(8,128)(2,1)S(1)} collective-permute-done((bf16[512,256]{1,0:T(8,128)(2,1)S(1)}, bf16[512,256]{1,0:T(8,128)(2,1)S(1)}, u32[]{:S(2)}, u32[]{:S(2)}) %collective-permute-start.3) | collective-permute-done | bytes 262176 | tf_op jit(solution)/shard_map/ppermute | solution.py:288
  25.3 1.5 %collective-permute-start.6 = (bf16[512,256]{1,0:T(8,128)(2,1)S(1)}, bf16[512,256]{1,0:T(8,128)(2,1)S(1)}, u32[]{:S(2)}, u32[]{:S(2)}) collective-permute-start(bf16[512,256]{1,0:T(8,128)(2,1)S(1)} %collective-permute-done.3.refs_4_), channel_id=1, source_target_pairs={{0,4},{1,5},{2,6},{3,7},{4,8},{5,9},{6,10},{7,11},{8,12},{9,13},{1... | collective-permute-start | bytes 786440 | tf_op jit(solution)/shard_map/ppermute | solution.py:288
  26.8 1.5 %collective-permute-start.7 = (bf16[512,256]{1,0:T(8,128)(2,1)S(1)}, bf16[512,256]{1,0:T(8,128)(2,1)S(1)}, u32[]{:S(2)}, u32[]{:S(2)}) collective-permute-start(bf16[512,256]{1,0:T(8,128)(2,1)S(1)} %collective-permute-done.3.refs_4_), channel_id=1, source_target_pairs={{0,2},{1,3},{2,0},{3,1},{4,6},{5,7},{6,4},{7,5},{8,10},{9,11},{10,... | collective-permute-start | bytes 786440 | tf_op jit(solution)/shard_map/ppermute | solution.py:285
  28.3 2.6 %collective-permute-done.11.refs_11_ = bf16[512,256]{1,0:T(8,128)(2,1)S(1)} collective-permute-done((bf16[512,256]{1,0:T(8,128)(2,1)S(1)}, bf16[512,256]{1,0:T(8,128)(2,1)S(1)}, u32[]{:S(2)}, u32[]{:S(2)}) %collective-permute-start.11) | collective-permute-done | bytes 262176 | tf_op jit(solution)/shard_map/ppermute | solution.py:288
  30.9 1.5 %collective-permute-start.13 = (bf16[512,256]{1,0:T(8,128)(2,1)S(1)}, bf16[512,256]{1,0:T(8,128)(2,1)S(1)}, u32[]{:S(2)}, u32[]{:S(2)}) collective-permute-start(bf16[512,256]{1,0:T(8,128)(2,1)S(1)} %collective-permute-done.11.refs_11_), channel_id=1, source_target_pairs={{0,4},{1,5},{2,6},{3,7},{4,8},{5,9},{6,10},{7,11},{8,12},{9,13},{1... | collective-permute-start | bytes 786440 | tf_op jit(solution)/shard_map/ppermute | solution.py:288
  32.4 1.5 %collective-permute-start.14 = (bf16[512,256]{1,0:T(8,128)(2,1)S(1)}, bf16[512,256]{1,0:T(8,128)(2,1)}, u32[]{:S(2)}, u32[]{:S(2)}) collective-permute-start(bf16[512,256]{1,0:T(8,128)(2,1)S(1)} %collective-permute-done.11.refs_11_), channel_id=1, source_target_pairs={{0,2},{1,3},{2,0},{3,1},{4,6},{5,7},{6,4},{7,5},{8,10},{9,11},{10,... | collective-permute-start | bytes 786440 | tf_op jit(solution)/shard_map/ppermute | solution.py:285
  34.0 2.5 %collective-permute-done.6.refs_6_ = bf16[512,256]{1,0:T(8,128)(2,1)S(1)} collective-permute-done((bf16[512,256]{1,0:T(8,128)(2,1)S(1)}, bf16[512,256]{1,0:T(8,128)(2,1)S(1)}, u32[]{:S(2)}, u32[]{:S(2)}) %collective-permute-start.6) | collective-permute-done | bytes 262176 | tf_op jit(solution)/shard_map/ppermute | solution.py:288
  36.5 5.4 %collective-permute-done.13.refs_13_ = bf16[512,256]{1,0:T(8,128)(2,1)S(1)} collective-permute-done((bf16[512,256]{1,0:T(8,128)(2,1)S(1)}, bf16[512,256]{1,0:T(8,128)(2,1)S(1)}, u32[]{:S(2)}, u32[]{:S(2)}) %collective-permute-start.13) | collective-permute-done | bytes 262176 | tf_op jit(solution)/shard_map/ppermute | solution.py:288
  41.9 1.9 %collective-permute-start.15 = (bf16[512,256]{1,0:T(8,128)(2,1)S(1)}, bf16[512,256]{1,0:T(8,128)(2,1)S(1)}, u32[]{:S(2)}, u32[]{:S(2)}) collective-permute-start(bf16[512,256]{1,0:T(8,128)(2,1)S(1)} %collective-permute-done.10.refs_8_), channel_id=1, source_target_pairs={{0,12},{1,13},{2,14},{3,15},{4,0},{5,1},{6,2},{7,3},{8,4},{9,5},{1... | collective-permute-start | bytes 786440 | tf_op jit(solution)/shard_map/ppermute | solution.py:288
  43.9 1.5 %collective-permute-start.8 = (bf16[512,256]{1,0:T(8,128)(2,1)S(1)}, bf16[512,256]{1,0:T(8,128)(2,1)S(1)}, u32[]{:S(2)}, u32[]{:S(2)}) collective-permute-start(bf16[512,256]{1,0:T(8,128)(2,1)S(1)} %collective-permute-done.6.refs_6_), channel_id=1, source_target_pairs={{0,2},{1,3},{2,0},{3,1},{4,6},{5,7},{6,4},{7,5},{8,10},{9,11},{10,... | collective-permute-start | bytes 786440 | tf_op jit(solution)/shard_map/ppermute | solution.py:285
  45.4 6.6 %project.2.refs_2_ = f32[768,512]{1,0:T(8,128)S(1)} custom-call(s32[7]{0:T(128)S(1)} %stack.116.at_ref, bf16[384,8192]{1,0:T(8,128)(2,1)} %own_ref.6, bf16[384,8192]{1,0:T(8,128)(2,1)} %collective-permute-done.sib_ref, bf16[512,256]{1,0:T(8,128)(2,1)S(1)} %get-tuple-element.83.refs_0_, bf16[512,256]{1,0:T(8,128)(2,1)S(1)} %collective-permute-done.2.refs_1_, ...), custom_call_target="tpu_custom_call" | custom-call | flops 84557168640 | bytes 322437120 | tf_op jit(solution)/shard_map/project/pallas_call | solution.py:66
  52.0 1.7 %project.3 = f32[768,512]{1,0:T(8,128)S(1)} custom-call(s32[1]{0:T(128)} %bitcast.2.at_ref, bf16[384,8192]{1,0:T(8,128)(2,1)} %own_ref.6, bf16[384,8192]{1,0:T(8,128)(2,1)} %collective-permute-done.sib_ref, bf16[512,256]{1,0:T(8,128)(2,1)S(1)} %collective-permute-done.8.refs_0_, bf16[512,256]{1,0:T(8,128)(2,1)S(1)} %collective-permute-done.15.refs_1_, ...), custom_call_target="tpu_custom_call" | custom-call | flops 12079595520 | bytes 86507520 | tf_op jit(solution)/shard_map/project/pallas_call | solution.py:66
  54.5 2.9 %collective-permute-done.16 = f32[768,512]{1,0:T(8,128)S(1)} collective-permute-done((f32[768,512]{1,0:T(8,128)S(1)}, f32[768,512]{1,0:T(8,128)S(1)}, u32[]{:S(2)}, u32[]{:S(2)}) %collective-permute-start.16) | collective-permute-done | bytes 1572896 | tf_op jit(solution)/shard_map/ppermute | solution.py:282
  57.8 1.5 %outer.3 = bf16[256,512]{1,0:T(8,128)(2,1)S(1)} custom-call(s32[1]{0:T(128)} %bitcast.21.at_ref, bf16[384,4096]{1,0:T(8,128)(2,1)} %own_ref.9, bf16[384,4096]{1,0:T(8,128)(2,1)} %collective-permute-done.5.sib_ref, bf16[768,512]{1,0:T(8,128)(2,1)S(1)} %add_convert_fusion.projected_ref), custom_call_target="tpu_custom_call" | custom-call | flops 6039797760 | bytes 27525120 | tf_op jit(solution)/shard_map/outer/pallas_call | solution.py:66
  60.1 3.3 %outer.4 = (bf16[256,512]{1,0:T(8,128)(2,1)S(1)}, bf16[256,512]{1,0:T(8,128)(2,1)S(1)}, bf16[256,512]{1,0:T(8,128)(2,1)S(1)}, f32[256,512]{1,0:T(8,128)S(1)}) custom-call(s32[4]{0:T(128)S(1)} %pad_add_fusion.1.at_ref, bf16[384,4096]{1,0:T(8,128)(2,1)} %own_ref.9, bf16[384,4096]{1,0:T(8,128)(2,1)} %collective-permute-done.5.sib_ref, ...), custom_call_target="tpu_custom_call" | custom-call | flops 24159191040 | bytes 110100480 | tf_op jit(solution)/shard_map/outer/pallas_call | solution.py:66
  63.3 1.4 %collective-permute-start.19 = (bf16[256,512]{1,0:T(8,128)(2,1)S(1)}, bf16[256,512]{1,0:T(8,128)(2,1)S(1)}, u32[]{:S(2)}, u32[]{:S(2)}) collective-permute-start(bf16[256,512]{1,0:T(8,128)(2,1)S(1)} %get-tuple-element.61), channel_id=1, source_target_pairs={{0,2},{1,3},{2,0},{3,1},{4,6},{5,7},{6,4},{7,5},{8,10},{9,11},{10,... | collective-permute-start | bytes 786440 | tf_op jit(solution)/shard_map/ppermute | solution.py:285
  65.4 1.3 %collective-permute-start.18 = (bf16[256,512]{1,0:T(8,128)(2,1)S(1)}, bf16[256,512]{1,0:T(8,128)(2,1)S(1)}, u32[]{:S(2)}, u32[]{:S(2)}) collective-permute-start(bf16[256,512]{1,0:T(8,128)(2,1)S(1)} %get-tuple-element.59), channel_id=1, source_target_pairs={{0,2},{1,3},{2,0},{3,1},{4,6},{5,7},{6,4},{7,5},{8,10},{9,11},{10,... | collective-permute-start | bytes 786440 | tf_op jit(solution)/shard_map/ppermute | solution.py:285
  66.7 1.7 %collective-permute-done.17 = bf16[256,512]{1,0:T(8,128)(2,1)S(1)} collective-permute-done((bf16[256,512]{1,0:T(8,128)(2,1)S(1)}, bf16[256,512]{1,0:T(8,128)(2,1)S(1)}, u32[]{:S(2)}, u32[]{:S(2)}) %collective-permute-start.17) | collective-permute-done | bytes 262176 | tf_op jit(solution)/shard_map/ppermute | solution.py:285
  68.7 2.8 %outer.5 = (f32[256,512]{1,0:T(8,128)S(1)}, f32[256,512]{1,0:T(8,128)S(1)}, f32[256,512]{1,0:T(8,128)S(1)}) custom-call(s32[3]{0:T(128)S(1)} %pad_add_fusion.at_ref, bf16[384,4096]{1,0:T(8,128)(2,1)} %own_ref.9, bf16[384,4096]{1,0:T(8,128)(2,1)} %collective-permute-done.5.sib_ref, bf16[768,512]{1,0:T(8,128)(2,1)S(1)} %add_convert_fusion.projected_ref), custom_call_target="tpu_custom_call" | custom-call | flops 18119393280 | bytes 82575360 | tf_op jit(solution)/shard_map/outer/pallas_call | solution.py:66
  71.6 2.5 %collective-permute-done.19 = bf16[256,512]{1,0:T(8,128)(2,1)S(1)} collective-permute-done((bf16[256,512]{1,0:T(8,128)(2,1)S(1)}, bf16[256,512]{1,0:T(8,128)(2,1)S(1)}, u32[]{:S(2)}, u32[]{:S(2)}) %collective-permute-start.19) | collective-permute-done | bytes 262176 | tf_op jit(solution)/shard_map/ppermute | solution.py:285
  74.2 1.7 %collective-permute-start.20 = (bf16[256,512]{1,0:T(8,128)(2,1)S(1)}, bf16[256,512]{1,0:T(8,128)(2,1)S(1)}, u32[]{:S(2)}, u32[]{:S(2)}) collective-permute-start(bf16[256,512]{1,0:T(8,128)(2,1)S(1)} %add_convert_fusion.2), channel_id=1, source_target_pairs={{0,12},{1,13},{2,14},{3,15},{4,0},{5,1},{6,2},{7,3},{8,4},{9,5},{1... | collective-permute-start | bytes 786440 | tf_op jit(solution)/shard_map/ppermute | solution.py:288
  75.9 3.8 %collective-permute-done.21 = bf16[256,512]{1,0:T(8,128)(2,1)S(1)} collective-permute-done((bf16[256,512]{1,0:T(8,128)(2,1)S(1)}, bf16[256,512]{1,0:T(8,128)(2,1)S(1)}, u32[]{:S(2)}, u32[]{:S(2)}) %collective-permute-start.21) | collective-permute-done | bytes 262176 | tf_op jit(solution)/shard_map/ppermute | solution.py:285
  80.0 4.8 %collective-permute-done.18 = bf16[256,512]{1,0:T(8,128)(2,1)S(1)} collective-permute-done((bf16[256,512]{1,0:T(8,128)(2,1)S(1)}, bf16[256,512]{1,0:T(8,128)(2,1)S(1)}, u32[]{:S(2)}, u32[]{:S(2)}) %collective-permute-start.18) | collective-permute-done | bytes 262176 | tf_op jit(solution)/shard_map/ppermute | solution.py:285
  84.8 4.1 %collective-permute-done.23 = bf16[256,512]{1,0:T(8,128)(2,1)S(1)} collective-permute-done((bf16[256,512]{1,0:T(8,128)(2,1)S(1)}, bf16[256,512]{1,0:T(8,128)(2,1)S(1)}, u32[]{:S(2)}, u32[]{:S(2)}) %collective-permute-start.23) | collective-permute-done | bytes 262176 | tf_op jit(solution)/shard_map/ppermute | solution.py:288
  88.9 1.4 %divide_convert_fusion = (bf16[256,512]{1,0:T(8,128)(2,1)S(1)}, f32[256,512]{1,0:T(8,128)}, f32[256,512]{1,0:T(8,128)}) fusion(bf16[256,512]{1,0:T(8,128)(2,1)S(1)} %collective-permute-done.23, bf16[256,512]{1,0:T(8,128)(2,1)S(1)} %collective-permute-done.20, f32[256,512]{1,0:T(8,128)S(1)} %get-tuple-element.58, ...), kind=kLoop, calls=%fused_computation.3 | loop fusion | flops 2359296 | bytes 3670016 | tf_op jit(solution)/shard_map/convert_element_type | solution.py:26
  90.9 1.5 %collective-permute-start.24 = (bf16[256,256]{1,0:T(8,128)(2,1)S(1)}, bf16[256,256]{1,0:T(8,128)(2,1)S(1)}, u32[]{:S(2)}, u32[]{:S(2)}) collective-permute-start(bf16[256,256]{1,0:T(8,128)(2,1)S(1)} %get-tuple-element.85), channel_id=1, source_target_pairs={{0,4},{1,5},{2,6},{3,7},{4,8},{5,9},{6,10},{7,11},{8,12},{9,13},{1... | collective-permute-start | bytes 393224 | tf_op jit(solution)/shard_map/ppermute | solution.py:288
  92.3 1.3 %collective-permute-start.25 = (bf16[256,256]{1,0:T(8,128)(2,1)S(1)}, bf16[256,256]{1,0:T(8,128)(2,1)S(1)}, u32[]{:S(2)}, u32[]{:S(2)}) collective-permute-start(bf16[256,256]{1,0:T(8,128)(2,1)S(1)} %get-tuple-element.85), channel_id=1, source_target_pairs={{0,2},{1,3},{2,0},{3,1},{4,6},{5,7},{6,4},{7,5},{8,10},{9,11},{10,... | collective-permute-start | bytes 393224 | tf_op jit(solution)/shard_map/ppermute | solution.py:285
  93.8 3.4 %collective-permute-done.26 = bf16[256,256]{1,0:T(8,128)(2,1)S(1)} collective-permute-done((bf16[256,256]{1,0:T(8,128)(2,1)S(1)}, bf16[256,256]{1,0:T(8,128)(2,1)S(1)}, u32[]{:S(2)}, u32[]{:S(2)}) %collective-permute-start.26) | collective-permute-done | bytes 131104 | tf_op jit(solution)/shard_map/ppermute | solution.py:288
  98.6 1.4 %collective-permute-start.28 = (bf16[256,256]{1,0:T(8,128)(2,1)S(1)}, bf16[256,256]{1,0:T(8,128)(2,1)S(1)}, u32[]{:S(2)}, u32[]{:S(2)}) collective-permute-start(bf16[256,256]{1,0:T(8,128)(2,1)S(1)} %collective-permute-done.24), channel_id=1, source_target_pairs={{0,4},{1,5},{2,6},{3,7},{4,8},{5,9},{6,10},{7,11},{8,12},{9,13},{1... | collective-permute-start | bytes 393224 | tf_op jit(solution)/shard_map/ppermute | solution.py:288
  101.0 2.9 %collective-permute-done.30 = bf16[256,256]{1,0:T(8,128)(2,1)S(1)} collective-permute-done((bf16[256,256]{1,0:T(8,128)(2,1)S(1)}, bf16[256,256]{1,0:T(8,128)(2,1)S(1)}, u32[]{:S(2)}, u32[]{:S(2)}) %collective-permute-start.30) | collective-permute-done | bytes 131104 | tf_op jit(solution)/shard_map/ppermute | solution.py:288
  105.0 1.3 %collective-permute-done.28 = bf16[256,256]{1,0:T(8,128)(2,1)S(1)} collective-permute-done((bf16[256,256]{1,0:T(8,128)(2,1)S(1)}, bf16[256,256]{1,0:T(8,128)(2,1)S(1)}, u32[]{:S(2)}, u32[]{:S(2)}) %collective-permute-start.28) | collective-permute-done | bytes 131104 | tf_op jit(solution)/shard_map/ppermute | solution.py:288
  106.3 1.6 %collective-permute-start.37 = (bf16[256,256]{1,0:T(8,128)(2,1)S(1)}, bf16[256,256]{1,0:T(8,128)(2,1)S(1)}, u32[]{:S(2)}, u32[]{:S(2)}) collective-permute-start(bf16[256,256]{1,0:T(8,128)(2,1)S(1)} %collective-permute-done.28), channel_id=1, source_target_pairs={{0,4},{1,5},{2,6},{3,7},{4,8},{5,9},{6,10},{7,11},{8,12},{9,13},{1... | collective-permute-start | bytes 393224 | tf_op jit(solution)/shard_map/ppermute | solution.py:288
  107.8 1.6 %collective-permute-start.38 = (bf16[256,256]{1,0:T(8,128)(2,1)S(1)}, bf16[256,256]{1,0:T(8,128)(2,1)S(1)}, u32[]{:S(2)}, u32[]{:S(2)}) collective-permute-start(bf16[256,256]{1,0:T(8,128)(2,1)S(1)} %collective-permute-done.28), channel_id=1, source_target_pairs={{0,2},{1,3},{2,0},{3,1},{4,6},{5,7},{6,4},{7,5},{8,10},{9,11},{10,... | collective-permute-start | bytes 393224 | tf_op jit(solution)/shard_map/ppermute | solution.py:285
  109.4 1.3 %collective-permute-done.39 = bf16[256,256]{1,0:T(8,128)(2,1)S(1)} collective-permute-done((bf16[256,256]{1,0:T(8,128)(2,1)S(1)}, bf16[256,256]{1,0:T(8,128)(2,1)S(1)}, u32[]{:S(2)}, u32[]{:S(2)}) %collective-permute-start.39) | collective-permute-done | bytes 131104 | tf_op jit(solution)/shard_map/ppermute | solution.py:288
  111.2 1.9 %collective-permute-done.37 = bf16[256,256]{1,0:T(8,128)(2,1)S(1)} collective-permute-done((bf16[256,256]{1,0:T(8,128)(2,1)S(1)}, bf16[256,256]{1,0:T(8,128)(2,1)S(1)}, u32[]{:S(2)}, u32[]{:S(2)}) %collective-permute-start.37) | collective-permute-done | bytes 131104 | tf_op jit(solution)/shard_map/ppermute | solution.py:288
  113.7 1.5 %collective-permute-start.41 = (bf16[256,256]{1,0:T(8,128)(2,1)S(1)}, bf16[256,256]{1,0:T(8,128)(2,1)S(1)}, u32[]{:S(2)}, u32[]{:S(2)}) collective-permute-start(bf16[256,256]{1,0:T(8,128)(2,1)S(1)} %collective-permute-done.37), channel_id=1, source_target_pairs={{0,2},{1,3},{2,0},{3,1},{4,6},{5,7},{6,4},{7,5},{8,10},{9,11},{10,... | collective-permute-start | bytes 393224 | tf_op jit(solution)/shard_map/ppermute | solution.py:285
  115.2 1.5 %collective-permute-start.42 = (bf16[256,256]{1,0:T(8,128)(2,1)S(1)}, bf16[256,256]{1,0:T(8,128)(2,1)S(1)}, u32[]{:S(2)}, u32[]{:S(2)}) collective-permute-start(bf16[256,256]{1,0:T(8,128)(2,1)S(1)} %collective-permute-done.27), channel_id=1, source_target_pairs={{0,12},{1,13},{2,14},{3,15},{4,0},{5,1},{6,2},{7,3},{8,4},{9,5},{1... | collective-permute-start | bytes 393224 | tf_op jit(solution)/shard_map/ppermute | solution.py:288
  117.2 3.0 %back.2.refs_0_ = bf16[4096,512]{1,0:T(8,128)(2,1)} custom-call(s32[10]{0:T(128)S(1)} %stack.107.at_ref, bf16[512,512]{1,0:T(8,128)(2,1)S(1)} %copy-done, bf16[256,512]{1,0:T(8,128)(2,1)S(1)} %get-tuple-element.79.refs_1_, bf16[512,256]{1,0:T(8,128)(2,1)S(1)} %constant_dynamic-update-slice_fusion.refs_2_, ...), custom_call_target="tpu_custom_call" | custom-call | flops 40265318400 | bytes 157286400 | tf_op jit(solution)/shard_map/back/pallas_call | solution.py:66
  121.9 2.4 %back.3 = bf16[4096,512]{1,0:T(8,128)(2,1)} custom-call(s32[6]{0:T(128)S(1)} %stack.96.at_ref, bf16[4096,512]{1,0:T(8,128)(2,1)} %back.2.refs_0_, bf16[512,512]{1,0:T(8,128)(2,1)S(1)} %copy-done, bf16[512,256]{1,0:T(8,128)(2,1)S(1)} %constant_dynamic-update-slice_fusion.8.refs_2_, ...), custom_call_target="tpu_custom_call", output_to_operand_aliasing={{}: (1, {})} | custom-call | flops 24159191040000 | bytes 94371840000 | tf_op jit(solution)/shard_map/back/pallas_call | solution.py:66
  (83 shorter events, 12.9 us)
Async XLA Ops:
  0.6 44.8 %collective-permute-start = (bf16[384,8192]{1,0:T(8,128)(2,1)}, bf16[384,8192]{1,0:T(8,128)(2,1)}, u32[]{:S(2)}, u32[]{:S(2)}) collective-permute-start(bf16[384,8192]{1,0:T(8,128)(2,1)} %own_ref.6), channel_id=1, source_target_pairs={{0,1},{1,0},{2,3},{3,2},{4,5},{5,4},{6,7},{7,6},{8,9},{9,8},{10,11... | collective-permute-start | bytes 18874376 | tf_op jit(solution)/shard_map/ppermute | solution.py:282
  2.2 11.8 %collective-permute-start.1 = (bf16[512,256]{1,0:T(8,128)(2,1)S(1)}, bf16[512,256]{1,0:T(8,128)(2,1)S(1)}, u32[]{:S(2)}, u32[]{:S(2)}) collective-permute-start(bf16[512,256]{1,0:T(8,128)(2,1)S(1)} %get-tuple-element.83.refs_0_), channel_id=1, source_target_pairs={{0,4},{1,5},{2,6},{3,7},{4,8},{5,9},{6,10},{7,11},{8,12},{9,13},{1... | collective-permute-start | bytes 786440 | tf_op jit(solution)/shard_map/ppermute | solution.py:288
  4.9 9.2 %collective-permute-start.2 = (bf16[512,256]{1,0:T(8,128)(2,1)S(1)}, bf16[512,256]{1,0:T(8,128)(2,1)S(1)}, u32[]{:S(2)}, u32[]{:S(2)}) collective-permute-start(bf16[512,256]{1,0:T(8,128)(2,1)S(1)} %get-tuple-element.83.refs_0_), channel_id=1, source_target_pairs={{0,2},{1,3},{2,0},{3,1},{4,6},{5,7},{6,4},{7,5},{8,10},{9,11},{10,... | collective-permute-start | bytes 786440 | tf_op jit(solution)/shard_map/ppermute | solution.py:285
  6.4 13.2 %collective-permute-start.10 = (bf16[512,256]{1,0:T(8,128)(2,1)S(1)}, bf16[512,256]{1,0:T(8,128)(2,1)S(1)}, u32[]{:S(2)}, u32[]{:S(2)}) collective-permute-start(bf16[512,256]{1,0:T(8,128)(2,1)S(1)} %get-tuple-element.82.refs_7_), channel_id=1, source_target_pairs={{0,2},{1,3},{2,0},{3,1},{4,6},{5,7},{6,4},{7,5},{8,10},{9,11},{10,... | collective-permute-start | bytes 786440 | tf_op jit(solution)/shard_map/ppermute | solution.py:285
  6.9 12.8 %collective-permute-start.9 = (bf16[512,256]{1,0:T(8,128)(2,1)S(1)}, bf16[512,256]{1,0:T(8,128)(2,1)S(1)}, u32[]{:S(2)}, u32[]{:S(2)}) collective-permute-start(bf16[512,256]{1,0:T(8,128)(2,1)S(1)} %get-tuple-element.82.refs_7_), channel_id=1, source_target_pairs={{0,4},{1,5},{2,6},{3,7},{4,8},{5,9},{6,10},{7,11},{8,12},{9,13},{1... | collective-permute-start | bytes 786440 | tf_op jit(solution)/shard_map/ppermute | solution.py:288
  14.0 11.2 %collective-permute-start.3 = (bf16[512,256]{1,0:T(8,128)(2,1)S(1)}, bf16[512,256]{1,0:T(8,128)(2,1)S(1)}, u32[]{:S(2)}, u32[]{:S(2)}) collective-permute-start(bf16[512,256]{1,0:T(8,128)(2,1)S(1)} %collective-permute-done.1.refs_2_), channel_id=1, source_target_pairs={{0,4},{1,5},{2,6},{3,7},{4,8},{5,9},{6,10},{7,11},{8,12},{9,13},{1... | collective-permute-start | bytes 786440 | tf_op jit(solution)/shard_map/ppermute | solution.py:288
  15.6 9.7 %collective-permute-start.4 = (bf16[512,256]{1,0:T(8,128)(2,1)S(1)}, bf16[512,256]{1,0:T(8,128)(2,1)S(1)}, u32[]{:S(2)}, u32[]{:S(2)}) collective-permute-start(bf16[512,256]{1,0:T(8,128)(2,1)S(1)} %collective-permute-done.1.refs_2_), channel_id=1, source_target_pairs={{0,2},{1,3},{2,0},{3,1},{4,6},{5,7},{6,4},{7,5},{8,10},{9,11},{10,... | collective-permute-start | bytes 786440 | tf_op jit(solution)/shard_map/ppermute | solution.py:285
  19.7 11.2 %collective-permute-start.11 = (bf16[512,256]{1,0:T(8,128)(2,1)S(1)}, bf16[512,256]{1,0:T(8,128)(2,1)S(1)}, u32[]{:S(2)}, u32[]{:S(2)}) collective-permute-start(bf16[512,256]{1,0:T(8,128)(2,1)S(1)} %collective-permute-done.9.refs_9_), channel_id=1, source_target_pairs={{0,4},{1,5},{2,6},{3,7},{4,8},{5,9},{6,10},{7,11},{8,12},{9,13},{1... | collective-permute-start | bytes 786440 | tf_op jit(solution)/shard_map/ppermute | solution.py:288
  21.2 9.7 %collective-permute-start.12 = (bf16[512,256]{1,0:T(8,128)(2,1)S(1)}, bf16[512,256]{1,0:T(8,128)(2,1)S(1)}, u32[]{:S(2)}, u32[]{:S(2)}) collective-permute-start(bf16[512,256]{1,0:T(8,128)(2,1)S(1)} %collective-permute-done.9.refs_9_), channel_id=1, source_target_pairs={{0,2},{1,3},{2,0},{3,1},{4,6},{5,7},{6,4},{7,5},{8,10},{9,11},{10,... | collective-permute-start | bytes 786440 | tf_op jit(solution)/shard_map/ppermute | solution.py:285
  25.3 11.2 %collective-permute-start.6 = (bf16[512,256]{1,0:T(8,128)(2,1)S(1)}, bf16[512,256]{1,0:T(8,128)(2,1)S(1)}, u32[]{:S(2)}, u32[]{:S(2)}) collective-permute-start(bf16[512,256]{1,0:T(8,128)(2,1)S(1)} %collective-permute-done.3.refs_4_), channel_id=1, source_target_pairs={{0,4},{1,5},{2,6},{3,7},{4,8},{5,9},{6,10},{7,11},{8,12},{9,13},{1... | collective-permute-start | bytes 786440 | tf_op jit(solution)/shard_map/ppermute | solution.py:288
  26.8 9.7 %collective-permute-start.7 = (bf16[512,256]{1,0:T(8,128)(2,1)S(1)}, bf16[512,256]{1,0:T(8,128)(2,1)S(1)}, u32[]{:S(2)}, u32[]{:S(2)}) collective-permute-start(bf16[512,256]{1,0:T(8,128)(2,1)S(1)} %collective-permute-done.3.refs_4_), channel_id=1, source_target_pairs={{0,2},{1,3},{2,0},{3,1},{4,6},{5,7},{6,4},{7,5},{8,10},{9,11},{10,... | collective-permute-start | bytes 786440 | tf_op jit(solution)/shard_map/ppermute | solution.py:285
  30.9 11.0 %collective-permute-start.13 = (bf16[512,256]{1,0:T(8,128)(2,1)S(1)}, bf16[512,256]{1,0:T(8,128)(2,1)S(1)}, u32[]{:S(2)}, u32[]{:S(2)}) collective-permute-start(bf16[512,256]{1,0:T(8,128)(2,1)S(1)} %collective-permute-done.11.refs_11_), channel_id=1, source_target_pairs={{0,4},{1,5},{2,6},{3,7},{4,8},{5,9},{6,10},{7,11},{8,12},{9,13},{1... | collective-permute-start | bytes 786440 | tf_op jit(solution)/shard_map/ppermute | solution.py:288
  32.4 9.5 %collective-permute-start.14 = (bf16[512,256]{1,0:T(8,128)(2,1)S(1)}, bf16[512,256]{1,0:T(8,128)(2,1)}, u32[]{:S(2)}, u32[]{:S(2)}) collective-permute-start(bf16[512,256]{1,0:T(8,128)(2,1)S(1)} %collective-permute-done.11.refs_11_), channel_id=1, source_target_pairs={{0,2},{1,3},{2,0},{3,1},{4,6},{5,7},{6,4},{7,5},{8,10},{9,11},{10,... | collective-permute-start | bytes 786440 | tf_op jit(solution)/shard_map/ppermute | solution.py:285
  41.9 10.1 %collective-permute-start.15 = (bf16[512,256]{1,0:T(8,128)(2,1)S(1)}, bf16[512,256]{1,0:T(8,128)(2,1)S(1)}, u32[]{:S(2)}, u32[]{:S(2)}) collective-permute-start(bf16[512,256]{1,0:T(8,128)(2,1)S(1)} %collective-permute-done.10.refs_8_), channel_id=1, source_target_pairs={{0,12},{1,13},{2,14},{3,15},{4,0},{5,1},{6,2},{7,3},{8,4},{9,5},{1... | collective-permute-start | bytes 786440 | tf_op jit(solution)/shard_map/ppermute | solution.py:288
  43.9 8.2 %collective-permute-start.8 = (bf16[512,256]{1,0:T(8,128)(2,1)S(1)}, bf16[512,256]{1,0:T(8,128)(2,1)S(1)}, u32[]{:S(2)}, u32[]{:S(2)}) collective-permute-start(bf16[512,256]{1,0:T(8,128)(2,1)S(1)} %collective-permute-done.6.refs_6_), channel_id=1, source_target_pairs={{0,2},{1,3},{2,0},{3,1},{4,6},{5,7},{6,4},{7,5},{8,10},{9,11},{10,... | collective-permute-start | bytes 786440 | tf_op jit(solution)/shard_map/ppermute | solution.py:285
  45.4 12.4 %collective-permute-start.5 = (bf16[384,4096]{1,0:T(8,128)(2,1)}, bf16[384,4096]{1,0:T(8,128)(2,1)}, u32[]{:S(2)}, u32[]{:S(2)}) collective-permute-start(bf16[384,4096]{1,0:T(8,128)(2,1)} %own_ref.9), channel_id=1, source_target_pairs={{0,1},{1,0},{2,3},{3,2},{4,5},{5,4},{6,7},{7,6},{8,9},{9,8},{10,11... | collective-permute-start | bytes 9437192 | tf_op jit(solution)/shard_map/ppermute | solution.py:282
  53.8 3.6 %collective-permute-start.16 = (f32[768,512]{1,0:T(8,128)S(1)}, f32[768,512]{1,0:T(8,128)S(1)}, u32[]{:S(2)}, u32[]{:S(2)}) collective-permute-start(f32[768,512]{1,0:T(8,128)S(1)} %project.3), channel_id=1, source_target_pairs={{0,1},{1,0},{2,3},{3,2},{4,5},{5,4},{6,7},{7,6},{8,9},{9,8},{10,11... | collective-permute-start | bytes 4718600 | tf_op jit(solution)/shard_map/ppermute | solution.py:282
  59.3 9.2 %collective-permute-start.17 = (bf16[256,512]{1,0:T(8,128)(2,1)S(1)}, bf16[256,512]{1,0:T(8,128)(2,1)S(1)}, u32[]{:S(2)}, u32[]{:S(2)}) collective-permute-start(bf16[256,512]{1,0:T(8,128)(2,1)S(1)} %outer.3), channel_id=1, source_target_pairs={{0,2},{1,3},{2,0},{3,1},{4,6},{5,7},{6,4},{7,5},{8,10},{9,11},{10,... | collective-permute-start | bytes 786440 | tf_op jit(solution)/shard_map/ppermute | solution.py:285
  63.3 10.7 %collective-permute-start.19 = (bf16[256,512]{1,0:T(8,128)(2,1)S(1)}, bf16[256,512]{1,0:T(8,128)(2,1)S(1)}, u32[]{:S(2)}, u32[]{:S(2)}) collective-permute-start(bf16[256,512]{1,0:T(8,128)(2,1)S(1)} %get-tuple-element.61), channel_id=1, source_target_pairs={{0,2},{1,3},{2,0},{3,1},{4,6},{5,7},{6,4},{7,5},{8,10},{9,11},{10,... | collective-permute-start | bytes 786440 | tf_op jit(solution)/shard_map/ppermute | solution.py:285
  64.7 15.0 %collective-permute-start.21 = (bf16[256,512]{1,0:T(8,128)(2,1)S(1)}, bf16[256,512]{1,0:T(8,128)(2,1)S(1)}, u32[]{:S(2)}, u32[]{:S(2)}) collective-permute-start(bf16[256,512]{1,0:T(8,128)(2,1)S(1)} %get-tuple-element.63), channel_id=1, source_target_pairs={{0,2},{1,3},{2,0},{3,1},{4,6},{5,7},{6,4},{7,5},{8,10},{9,11},{10,... | collective-permute-start | bytes 786440 | tf_op jit(solution)/shard_map/ppermute | solution.py:285
  65.4 19.3 %collective-permute-start.18 = (bf16[256,512]{1,0:T(8,128)(2,1)S(1)}, bf16[256,512]{1,0:T(8,128)(2,1)S(1)}, u32[]{:S(2)}, u32[]{:S(2)}) collective-permute-start(bf16[256,512]{1,0:T(8,128)(2,1)S(1)} %get-tuple-element.59), channel_id=1, source_target_pairs={{0,2},{1,3},{2,0},{3,1},{4,6},{5,7},{6,4},{7,5},{8,10},{9,11},{10,... | collective-permute-start | bytes 786440 | tf_op jit(solution)/shard_map/ppermute | solution.py:285
  68.6 11.1 %collective-permute-start.22 = (bf16[256,512]{1,0:T(8,128)(2,1)S(1)}, bf16[256,512]{1,0:T(8,128)(2,1)S(1)}, u32[]{:S(2)}, u32[]{:S(2)}) collective-permute-start(bf16[256,512]{1,0:T(8,128)(2,1)S(1)} %convert_add_fusion.1), channel_id=1, source_target_pairs={{0,4},{1,5},{2,6},{3,7},{4,8},{5,9},{6,10},{7,11},{8,12},{9,13},{1... | collective-permute-start | bytes 786440 | tf_op jit(solution)/shard_map/ppermute | solution.py:288
  74.2 10.6 %collective-permute-start.20 = (bf16[256,512]{1,0:T(8,128)(2,1)S(1)}, bf16[256,512]{1,0:T(8,128)(2,1)S(1)}, u32[]{:S(2)}, u32[]{:S(2)}) collective-permute-start(bf16[256,512]{1,0:T(8,128)(2,1)S(1)} %add_convert_fusion.2), channel_id=1, source_target_pairs={{0,12},{1,13},{2,14},{3,15},{4,0},{5,1},{6,2},{7,3},{8,4},{9,5},{1... | collective-permute-start | bytes 786440 | tf_op jit(solution)/shard_map/ppermute | solution.py:288
  79.8 9.1 %collective-permute-start.23 = (bf16[256,512]{1,0:T(8,128)(2,1)S(1)}, bf16[256,512]{1,0:T(8,128)(2,1)S(1)}, u32[]{:S(2)}, u32[]{:S(2)}) collective-permute-start(bf16[256,512]{1,0:T(8,128)(2,1)S(1)} %add_convert_fusion.1), channel_id=1, source_target_pairs={{0,4},{1,5},{2,6},{3,7},{4,8},{5,9},{6,10},{7,11},{8,12},{9,13},{1... | collective-permute-start | bytes 786440 | tf_op jit(solution)/shard_map/ppermute | solution.py:288
  88.9 28.3 %copy-start = (bf16[512,512]{1,0:T(8,128)(2,1)S(1)}, bf16[512,512]{1,0:T(8,128)(2,1)}, u32[]{:S(2)}) copy-start(bf16[512,512]{1,0:T(8,128)(2,1)} %refs_1_.1) | copy-start | bytes 1572868
  90.3 6.8 %collective-permute-start.26 = (bf16[256,256]{1,0:T(8,128)(2,1)S(1)}, bf16[256,256]{1,0:T(8,128)(2,1)S(1)}, u32[]{:S(2)}, u32[]{:S(2)}) collective-permute-start(bf16[256,256]{1,0:T(8,128)(2,1)S(1)} %get-tuple-element.84), channel_id=1, source_target_pairs={{0,4},{1,5},{2,6},{3,7},{4,8},{5,9},{6,10},{7,11},{8,12},{9,13},{1... | collective-permute-start | bytes 393224 | tf_op jit(solution)/shard_map/ppermute | solution.py:288
  90.4 6.8 %collective-permute-start.27 = (bf16[256,256]{1,0:T(8,128)(2,1)S(1)}, bf16[256,256]{1,0:T(8,128)(2,1)S(1)}, u32[]{:S(2)}, u32[]{:S(2)}) collective-permute-start(bf16[256,256]{1,0:T(8,128)(2,1)S(1)} %get-tuple-element.84), channel_id=1, source_target_pairs={{0,2},{1,3},{2,0},{3,1},{4,6},{5,7},{6,4},{7,5},{8,10},{9,11},{10,... | collective-permute-start | bytes 393224 | tf_op jit(solution)/shard_map/ppermute | solution.py:285
  90.9 7.7 %collective-permute-start.24 = (bf16[256,256]{1,0:T(8,128)(2,1)S(1)}, bf16[256,256]{1,0:T(8,128)(2,1)S(1)}, u32[]{:S(2)}, u32[]{:S(2)}) collective-permute-start(bf16[256,256]{1,0:T(8,128)(2,1)S(1)} %get-tuple-element.85), channel_id=1, source_target_pairs={{0,4},{1,5},{2,6},{3,7},{4,8},{5,9},{6,10},{7,11},{8,12},{9,13},{1... | collective-permute-start | bytes 393224 | tf_op jit(solution)/shard_map/ppermute | solution.py:288
  92.3 6.2 %collective-permute-start.25 = (bf16[256,256]{1,0:T(8,128)(2,1)S(1)}, bf16[256,256]{1,0:T(8,128)(2,1)S(1)}, u32[]{:S(2)}, u32[]{:S(2)}) collective-permute-start(bf16[256,256]{1,0:T(8,128)(2,1)S(1)} %get-tuple-element.85), channel_id=1, source_target_pairs={{0,2},{1,3},{2,0},{3,1},{4,6},{5,7},{6,4},{7,5},{8,10},{9,11},{10,... | collective-permute-start | bytes 393224 | tf_op jit(solution)/shard_map/ppermute | solution.py:285
  93.8 19.9 %collective-permute-start.32 = (bf16[256,512]{1,0:T(8,128)(2,1)S(1)}, bf16[256,512]{1,0:T(8,128)(2,1)S(1)}, u32[]{:S(2)}, u32[]{:S(2)}) collective-permute-start(bf16[256,512]{1,0:T(8,128)(2,1)S(1)} %get-tuple-element.79.refs_1_), channel_id=1, source_target_pairs={{0,1},{1,0},{2,3},{3,2},{4,5},{5,4},{6,7},{7,6},{8,9},{9,8},{10,11... | collective-permute-start | bytes 786440 | tf_op jit(solution)/shard_map/ppermute | solution.py:282
  97.2 6.8 %collective-permute-start.30 = (bf16[256,256]{1,0:T(8,128)(2,1)S(1)}, bf16[256,256]{1,0:T(8,128)(2,1)S(1)}, u32[]{:S(2)}, u32[]{:S(2)}) collective-permute-start(bf16[256,256]{1,0:T(8,128)(2,1)S(1)} %collective-permute-done.26), channel_id=1, source_target_pairs={{0,4},{1,5},{2,6},{3,7},{4,8},{5,9},{6,10},{7,11},{8,12},{9,13},{1... | collective-permute-start | bytes 393224 | tf_op jit(solution)/shard_map/ppermute | solution.py:288
  97.5 6.4 %collective-permute-start.31 = (bf16[256,256]{1,0:T(8,128)(2,1)S(1)}, bf16[256,256]{1,0:T(8,128)(2,1)S(1)}, u32[]{:S(2)}, u32[]{:S(2)}) collective-permute-start(bf16[256,256]{1,0:T(8,128)(2,1)S(1)} %collective-permute-done.26), channel_id=1, source_target_pairs={{0,2},{1,3},{2,0},{3,1},{4,6},{5,7},{6,4},{7,5},{8,10},{9,11},{10,... | collective-permute-start | bytes 393224 | tf_op jit(solution)/shard_map/ppermute | solution.py:285
  98.6 7.7 %collective-permute-start.28 = (bf16[256,256]{1,0:T(8,128)(2,1)S(1)}, bf16[256,256]{1,0:T(8,128)(2,1)S(1)}, u32[]{:S(2)}, u32[]{:S(2)}) collective-permute-start(bf16[256,256]{1,0:T(8,128)(2,1)S(1)} %collective-permute-done.24), channel_id=1, source_target_pairs={{0,4},{1,5},{2,6},{3,7},{4,8},{5,9},{6,10},{7,11},{8,12},{9,13},{1... | collective-permute-start | bytes 393224 | tf_op jit(solution)/shard_map/ppermute | solution.py:288
  100.0 6.3 %collective-permute-start.29 = (bf16[256,256]{1,0:T(8,128)(2,1)S(1)}, bf16[256,256]{1,0:T(8,128)(2,1)S(1)}, u32[]{:S(2)}, u32[]{:S(2)}) collective-permute-start(bf16[256,256]{1,0:T(8,128)(2,1)S(1)} %collective-permute-done.24), channel_id=1, source_target_pairs={{0,2},{1,3},{2,0},{3,1},{4,6},{5,7},{6,4},{7,5},{8,10},{9,11},{10,... | collective-permute-start | bytes 393224 | tf_op jit(solution)/shard_map/ppermute | solution.py:285
  103.9 6.8 %collective-permute-start.39 = (bf16[256,256]{1,0:T(8,128)(2,1)S(1)}, bf16[256,256]{1,0:T(8,128)(2,1)S(1)}, u32[]{:S(2)}, u32[]{:S(2)}) collective-permute-start(bf16[256,256]{1,0:T(8,128)(2,1)S(1)} %collective-permute-done.30), channel_id=1, source_target_pairs={{0,4},{1,5},{2,6},{3,7},{4,8},{5,9},{6,10},{7,11},{8,12},{9,13},{1... | collective-permute-start | bytes 393224 | tf_op jit(solution)/shard_map/ppermute | solution.py:288
  104.6 6.1 %collective-permute-start.40 = (bf16[256,256]{1,0:T(8,128)(2,1)S(1)}, bf16[256,256]{1,0:T(8,128)(2,1)S(1)}, u32[]{:S(2)}, u32[]{:S(2)}) collective-permute-start(bf16[256,256]{1,0:T(8,128)(2,1)S(1)} %collective-permute-done.30), channel_id=1, source_target_pairs={{0,2},{1,3},{2,0},{3,1},{4,6},{5,7},{6,4},{7,5},{8,10},{9,11},{10,... | collective-permute-start | bytes 393224 | tf_op jit(solution)/shard_map/ppermute | solution.py:285
  106.3 6.8 %collective-permute-start.37 = (bf16[256,256]{1,0:T(8,128)(2,1)S(1)}, bf16[256,256]{1,0:T(8,128)(2,1)S(1)}, u32[]{:S(2)}, u32[]{:S(2)}) collective-permute-start(bf16[256,256]{1,0:T(8,128)(2,1)S(1)} %collective-permute-done.28), channel_id=1, source_target_pairs={{0,4},{1,5},{2,6},{3,7},{4,8},{5,9},{6,10},{7,11},{8,12},{9,13},{1... | collective-permute-start | bytes 393224 | tf_op jit(solution)/shard_map/ppermute | solution.py:288
  107.8 5.3 %collective-permute-start.38 = (bf16[256,256]{1,0:T(8,128)(2,1)S(1)}, bf16[256,256]{1,0:T(8,128)(2,1)S(1)}, u32[]{:S(2)}, u32[]{:S(2)}) collective-permute-start(bf16[256,256]{1,0:T(8,128)(2,1)S(1)} %collective-permute-done.28), channel_id=1, source_target_pairs={{0,2},{1,3},{2,0},{3,1},{4,6},{5,7},{6,4},{7,5},{8,10},{9,11},{10,... | collective-permute-start | bytes 393224 | tf_op jit(solution)/shard_map/ppermute | solution.py:285
  110.7 4.5 %collective-permute-start.34 = (bf16[512,256]{1,0:T(8,128)(2,1)S(1)}, bf16[512,256]{1,0:T(8,128)(2,1)S(1)}, u32[]{:S(2)}, u32[]{:S(2)}) collective-permute-start(bf16[512,256]{1,0:T(8,128)(2,1)S(1)} %constant_dynamic-update-slice_fusion.2.refs_3_), channel_id=1, source_target_pairs={{0,1},{1,0},{2,3},{3,2},{4,5},{5,4},{6,7},{7,6},{8,9},{9,8},{10,11... | collective-permute-start | bytes 786440 | tf_op jit(solution)/shard_map/ppermute | solution.py:282
  110.7 6.0 %collective-permute-start.33 = (bf16[512,256]{1,0:T(8,128)(2,1)S(1)}, bf16[512,256]{1,0:T(8,128)(2,1)S(1)}, u32[]{:S(2)}, u32[]{:S(2)}) collective-permute-start(bf16[512,256]{1,0:T(8,128)(2,1)S(1)} %constant_dynamic-update-slice_fusion.refs_2_), channel_id=1, source_target_pairs={{0,1},{1,0},{2,3},{3,2},{4,5},{5,4},{6,7},{7,6},{8,9},{9,8},{10,11... | collective-permute-start | bytes 786440 | tf_op jit(solution)/shard_map/ppermute | solution.py:282
  113.1 3.6 %collective-permute-start.36 = (bf16[512,256]{1,0:T(8,128)(2,1)S(1)}, bf16[512,256]{1,0:T(8,128)(2,1)S(1)}, u32[]{:S(2)}, u32[]{:S(2)}) collective-permute-start(bf16[512,256]{1,0:T(8,128)(2,1)S(1)} %constant_dynamic-update-slice_fusion.6.refs_5_), channel_id=1, source_target_pairs={{0,1},{1,0},{2,3},{3,2},{4,5},{5,4},{6,7},{7,6},{8,9},{9,8},{10,11... | collective-permute-start | bytes 786440 | tf_op jit(solution)/shard_map/ppermute | solution.py:282
  113.1 4.1 %collective-permute-start.35 = (bf16[512,256]{1,0:T(8,128)(2,1)S(1)}, bf16[512,256]{1,0:T(8,128)(2,1)S(1)}, u32[]{:S(2)}, u32[]{:S(2)}) collective-permute-start(bf16[512,256]{1,0:T(8,128)(2,1)S(1)} %constant_dynamic-update-slice_fusion.4.refs_4_), channel_id=1, source_target_pairs={{0,1},{1,0},{2,3},{3,2},{4,5},{5,4},{6,7},{7,6},{8,9},{9,8},{10,11... | collective-permute-start | bytes 786440 | tf_op jit(solution)/shard_map/ppermute | solution.py:282
  113.7 6.7 %collective-permute-start.41 = (bf16[256,256]{1,0:T(8,128)(2,1)S(1)}, bf16[256,256]{1,0:T(8,128)(2,1)S(1)}, u32[]{:S(2)}, u32[]{:S(2)}) collective-permute-start(bf16[256,256]{1,0:T(8,128)(2,1)S(1)} %collective-permute-done.37), channel_id=1, source_target_pairs={{0,2},{1,3},{2,0},{3,1},{4,6},{5,7},{6,4},{7,5},{8,10},{9,11},{10,... | collective-permute-start | bytes 393224 | tf_op jit(solution)/shard_map/ppermute | solution.py:285
  115.2 5.1 %collective-permute-start.42 = (bf16[256,256]{1,0:T(8,128)(2,1)S(1)}, bf16[256,256]{1,0:T(8,128)(2,1)S(1)}, u32[]{:S(2)}, u32[]{:S(2)}) collective-permute-start(bf16[256,256]{1,0:T(8,128)(2,1)S(1)} %collective-permute-done.27), channel_id=1, source_target_pairs={{0,12},{1,13},{2,14},{3,15},{4,0},{5,1},{6,2},{7,3},{8,4},{9,5},{1... | collective-permute-start | bytes 393224 | tf_op jit(solution)/shard_map/ppermute | solution.py:288
  116.7 5.2 %collective-permute-start.44 = (bf16[512,256]{1,0:T(8,128)(2,1)S(1)}, bf16[512,256]{1,0:T(8,128)(2,1)S(1)}, u32[]{:S(2)}, u32[]{:S(2)}) collective-permute-start(bf16[512,256]{1,0:T(8,128)(2,1)S(1)} %constant_dynamic-update-slice_fusion.10.refs_3_), channel_id=1, source_target_pairs={{0,1},{1,0},{2,3},{3,2},{4,5},{5,4},{6,7},{7,6},{8,9},{9,8},{10,11... | collective-permute-start | bytes 786440 | tf_op jit(solution)/shard_map/ppermute | solution.py:282
  116.7 5.2 %collective-permute-start.43 = (bf16[512,256]{1,0:T(8,128)(2,1)S(1)}, bf16[512,256]{1,0:T(8,128)(2,1)S(1)}, u32[]{:S(2)}, u32[]{:S(2)}) collective-permute-start(bf16[512,256]{1,0:T(8,128)(2,1)S(1)} %constant_dynamic-update-slice_fusion.8.refs_2_), channel_id=1, source_target_pairs={{0,1},{1,0},{2,3},{3,2},{4,5},{5,4},{6,7},{7,6},{8,9},{9,8},{10,11... | collective-permute-start | bytes 786440 | tf_op jit(solution)/shard_map/ppermute | solution.py:282
  120.3 1.4 %collective-permute-start.46 = (bf16[256,256]{1,0:T(8,128)(2,1)S(1)}, bf16[256,256]{1,0:T(8,128)(2,1)S(1)}, u32[]{:S(2)}, u32[]{:S(2)}) collective-permute-start(bf16[256,256]{1,0:T(8,128)(2,1)S(1)} %collective-permute-done.42.refs_5_), channel_id=1, source_target_pairs={{0,1},{1,0},{2,3},{3,2},{4,5},{5,4},{6,7},{7,6},{8,9},{9,8},{10,11... | collective-permute-start | bytes 393224 | tf_op jit(solution)/shard_map/ppermute | solution.py:282
  120.4 1.5 %collective-permute-start.45 = (bf16[256,256]{1,0:T(8,128)(2,1)S(1)}, bf16[256,256]{1,0:T(8,128)(2,1)S(1)}, u32[]{:S(2)}, u32[]{:S(2)}) collective-permute-start(bf16[256,256]{1,0:T(8,128)(2,1)S(1)} %collective-permute-done.41.refs_4_), channel_id=1, source_target_pairs={{0,1},{1,0},{2,3},{3,2},{4,5},{5,4},{6,7},{7,6},{8,9},{9,8},{10,11... | collective-permute-start | bytes 393224 | tf_op jit(solution)/shard_map/ppermute | solution.py:282
  (2 other events, 40.7 us)

commit v10 on v9

--- a/solution.py
+++ b/solution.py
@@ -107,13 +107,15 @@
             start(ref, b.at[pl.ds(j * depth, depth), pl.ds(i * cols, cols)])
         if held:
             start(refs[len(flat)], total)
-        for copy in started:
-            copy.wait()
-        for i, chunk in enumerate(blocks):
-            part = slice(i * cols, (i + 1) * cols)
-            deep = slice(min(chunk) * depth, (max(chunk) + 1) * depth)
-            term = jnp.dot(a[:, deep], b[deep, part], preferred_element_type=F32)
-            total[:, part] = total[:, part] + term if held else term
+        cut = (many + 1) // 2
+        for low, high in ((0, cut), (cut, many)):
+            for n, copy in enumerate(started):
+                j = n // 2 if n < 2 * many else places[n - 2 * many][1]
+                if low <= j < high:
+                    copy.wait()
+            deep = slice(low * depth, high * depth)
+            term = jnp.dot(a[:, deep], b[deep, :], preferred_element_type=F32)
+            total[...] = total[...] + term if low else term
         back_copy = pltpu.make_async_copy(total, out_ref, sems.at[copies])
         back_copy.start()
         back_copy.wait()
@@ -193,10 +195,13 @@
 
 
 def outer(out_grads, sibling, at, width, dtypes, projected):
-    rows, many, cols = out_grads.shape[0], at.shape[0], projected.shape[1]
-
-    def kernel(at_ref, own_ref, sib_ref, projected_ref, *refs):
-        outs, (g, sems) = refs[:-2], refs[-2:]
+    given = projected if isinstance(projected, tuple) else (projected,)
+    rows, many, cols = out_grads.shape[0], at.shape[0], given[0].shape[1]
+    first = len(given) > 1
+
+    def kernel(at_ref, own_ref, sib_ref, *refs):
+        projected_ref, (g, sems) = refs[2 if first else 0], refs[-2:]
+        outs = refs[len(given) + first : -2]
         copies = []
         core = lax.rem(lax.axis_index("dp"), 2)
         for j in range(many):
@@ -205,6 +210,8 @@
                 target = g.at[pl.ds(pl.multiple_of(c * rows, rows), rows), pl.ds(j * width, width)]
                 copies.append(pltpu.make_async_copy(ref.at[:, columns], target, sems.at[len(copies)]))
                 copies[-1].start()
+        if first:
+            projected_ref[...] = (refs[0][...] + refs[1][...]).astype(BF16)
         for j in range(many):
             copies[2 * j].wait()
             copies[2 * j + 1].wait()
@@ -215,8 +222,8 @@
         kernel,
         at,
         [pinned(out_grads), pinned(sibling)],
-        [projected],
-        [(True, jax.ShapeDtypeStruct((width, cols), dtype)) for dtype in dtypes],
+        [*given],
+        [(True, jax.ShapeDtypeStruct((2 * rows, cols), BF16))] * first + [(True, jax.ShapeDtypeStruct((width, cols), dtype)) for dtype in dtypes],
         [pltpu.VMEM((2 * rows, many * width), BF16), pltpu.SemaphoreType.DMA((2 * many,))],
         weight=W_OUTER,
         flops=4 * rows * width * many * cols,
@@ -331,8 +338,7 @@
     low = min(soon)
     blocks = [{n - low: block(i, n) for n in range(soon[i], last + 1)} for i in range(CHUNKS)]
     mine = project_late(activations, a_sibling, at_in[low:], blocks, mine, W_LATE)
-    projected = (mine + swap_core(mine)).astype(BF16)
-    (send,) = outer(out_grads, g_sibling, at_out[:1], width, [BF16], projected)
+    projected, send = outer(out_grads, g_sibling, at_out[:1], width, [BF16], (mine, swap_core(mine)))
     at = after(at_out[1 : nz + 1], send)
     *sends, keep = outer(out_grads, g_sibling, at, width, [BF16] * (nz - 1) + [F32], projected)
     passed = keep + swap_y(send).astype(F32)

time: 125 us -> 123 us (0.984)
  transfers between devices with their start and end apart: 47 -> 47, of which waited for: 20 -> 20; matrix products, arithmetic and copies ran while one was open for 2% -> 1% of each run, Pallas kernels for 14% -> 14%
where the time goes in v10:
time: 123 us
  waiting for transfers between devices  53.3 us (43%)
  starting transfers between devices  45.2 us (37%)
  Pallas kernels  20.6 us (17%)
  other arithmetic  1.8 us (1%)
  local copies, waits for them, and re-layouts  1.47 us (1%)
    ppermute x17, waiting for transfers between devices, shift_z(): return lax.ppermute(x, 'dp', pairs(lambda a, b, c: ((a + k) % nz, b, c)))  34.7 us
    ppermute x17, starting transfers between devices, shift_z(): return lax.ppermute(x, 'dp', pairs(lambda a, b, c: ((a + k) % nz, b, c)))  22.2 us
    pallas_call x7, Pallas kernels, call(): pl.pallas_call(kernel, grid_spec=pltpu.PrefetchScalarGridSpec(num_scalar_...  20.6 us
    ppermute x18, starting transfers between devices, swap_y(): return lax.ppermute(x, 'dp', pairs(lambda a, b, c: (a, 1 - b, c)))  20 us
    ppermute x18, waiting for transfers between devices, swap_y(): return lax.ppermute(x, 'dp', pairs(lambda a, b, c: (a, 1 - b, c)))  14.7 us
    ppermute x12, waiting for transfers between devices, swap_core(): return lax.ppermute(x, 'dp', pairs(lambda a, b, c: (a, b, 1 - c)))  3.93 us
    ppermute x12, starting transfers between devices, swap_core(): return lax.ppermute(x, 'dp', pairs(lambda a, b, c: (a, b, 1 - c)))  2.98 us
  transfers between devices with their start and end apart: 47, of which 20 were waited for; matrix products, arithmetic and copies ran while one was open for 1% of the time, Pallas kernels for 14%

profile of v10, /device:TPU:0, one launch (start us, length us, event | category | flops | bytes accessed | tf_op | source)
XLA Modules:
  0.0 123.2 jit_solution(17347352362022238871)
XLA Ops:
  1.1 1.1 fusion.2
  2.2 2.6 %collective-permute-start.1 = (bf16[512,256]{1,0:T(8,128)(2,1)S(1)}, bf16[512,256]{1,0:T(8,128)(2,1)S(1)}, u32[]{:S(2)}, u32[]{:S(2)}) collective-permute-start(bf16[512,256]{1,0:T(8,128)(2,1)S(1)} %get-tuple-element.87.refs_0_), channel_id=1, source_target_pairs={{0,4},{1,5},{2,6},{3,7},{4,8},{5,9},{6,10},{7,11},{8,12},{9,13},{1... | collective-permute-start | bytes 786440 | tf_op jit(solution)/shard_map/ppermute | solution.py:295
  4.9 1.5 %collective-permute-start.2 = (bf16[512,256]{1,0:T(8,128)(2,1)S(1)}, bf16[512,256]{1,0:T(8,128)(2,1)S(1)}, u32[]{:S(2)}, u32[]{:S(2)}) collective-permute-start(bf16[512,256]{1,0:T(8,128)(2,1)S(1)} %get-tuple-element.87.refs_0_), channel_id=1, source_target_pairs={{0,2},{1,3},{2,0},{3,1},{4,6},{5,7},{6,4},{7,5},{8,10},{9,11},{10,... | collective-permute-start | bytes 786440 | tf_op jit(solution)/shard_map/ppermute | solution.py:292
  6.9 1.6 %collective-permute-start.9 = (bf16[512,256]{1,0:T(8,128)(2,1)S(1)}, bf16[512,256]{1,0:T(8,128)(2,1)S(1)}, u32[]{:S(2)}, u32[]{:S(2)}) collective-permute-start(bf16[512,256]{1,0:T(8,128)(2,1)S(1)} %get-tuple-element.86.refs_7_), channel_id=1, source_target_pairs={{0,4},{1,5},{2,6},{3,7},{4,8},{5,9},{6,10},{7,11},{8,12},{9,13},{1... | collective-permute-start | bytes 786440 | tf_op jit(solution)/shard_map/ppermute | solution.py:295
  8.5 5.6 %collective-permute-done.1.refs_2_ = bf16[512,256]{1,0:T(8,128)(2,1)S(1)} collective-permute-done((bf16[512,256]{1,0:T(8,128)(2,1)S(1)}, bf16[512,256]{1,0:T(8,128)(2,1)S(1)}, u32[]{:S(2)}, u32[]{:S(2)}) %collective-permute-start.1) | collective-permute-done | bytes 262176 | tf_op jit(solution)/shard_map/ppermute | solution.py:295
  14.0 1.5 %collective-permute-start.3 = (bf16[512,256]{1,0:T(8,128)(2,1)S(1)}, bf16[512,256]{1,0:T(8,128)(2,1)S(1)}, u32[]{:S(2)}, u32[]{:S(2)}) collective-permute-start(bf16[512,256]{1,0:T(8,128)(2,1)S(1)} %collective-permute-done.1.refs_2_), channel_id=1, source_target_pairs={{0,4},{1,5},{2,6},{3,7},{4,8},{5,9},{6,10},{7,11},{8,12},{9,13},{1... | collective-permute-start | bytes 786440 | tf_op jit(solution)/shard_map/ppermute | solution.py:295
  15.6 1.5 %collective-permute-start.4 = (bf16[512,256]{1,0:T(8,128)(2,1)S(1)}, bf16[512,256]{1,0:T(8,128)(2,1)S(1)}, u32[]{:S(2)}, u32[]{:S(2)}) collective-permute-start(bf16[512,256]{1,0:T(8,128)(2,1)S(1)} %collective-permute-done.1.refs_2_), channel_id=1, source_target_pairs={{0,2},{1,3},{2,0},{3,1},{4,6},{5,7},{6,4},{7,5},{8,10},{9,11},{10,... | collective-permute-start | bytes 786440 | tf_op jit(solution)/shard_map/ppermute | solution.py:292
  17.1 2.5 %collective-permute-done.10.refs_8_ = bf16[512,256]{1,0:T(8,128)(2,1)S(1)} collective-permute-done((bf16[512,256]{1,0:T(8,128)(2,1)S(1)}, bf16[512,256]{1,0:T(8,128)(2,1)S(1)}, u32[]{:S(2)}, u32[]{:S(2)}) %collective-permute-start.10) | collective-permute-done | bytes 262176 | tf_op jit(solution)/shard_map/ppermute | solution.py:292
  19.7 1.5 %collective-permute-start.11 = (bf16[512,256]{1,0:T(8,128)(2,1)S(1)}, bf16[512,256]{1,0:T(8,128)(2,1)S(1)}, u32[]{:S(2)}, u32[]{:S(2)}) collective-permute-start(bf16[512,256]{1,0:T(8,128)(2,1)S(1)} %collective-permute-done.9.refs_9_), channel_id=1, source_target_pairs={{0,4},{1,5},{2,6},{3,7},{4,8},{5,9},{6,10},{7,11},{8,12},{9,13},{1... | collective-permute-start | bytes 786440 | tf_op jit(solution)/shard_map/ppermute | solution.py:295
  21.2 1.5 %collective-permute-start.12 = (bf16[512,256]{1,0:T(8,128)(2,1)S(1)}, bf16[512,256]{1,0:T(8,128)(2,1)S(1)}, u32[]{:S(2)}, u32[]{:S(2)}) collective-permute-start(bf16[512,256]{1,0:T(8,128)(2,1)S(1)} %collective-permute-done.9.refs_9_), channel_id=1, source_target_pairs={{0,2},{1,3},{2,0},{3,1},{4,6},{5,7},{6,4},{7,5},{8,10},{9,11},{10,... | collective-permute-start | bytes 786440 | tf_op jit(solution)/shard_map/ppermute | solution.py:292
  22.7 2.6 %collective-permute-done.3.refs_4_ = bf16[512,256]{1,0:T(8,128)(2,1)S(1)} collective-permute-done((bf16[512,256]{1,0:T(8,128)(2,1)S(1)}, bf16[512,256]{1,0:T(8,128)(2,1)S(1)}, u32[]{:S(2)}, u32[]{:S(2)}) %collective-permute-start.3) | collective-permute-done | bytes 262176 | tf_op jit(solution)/shard_map/ppermute | solution.py:295
  25.3 1.5 %collective-permute-start.6 = (bf16[512,256]{1,0:T(8,128)(2,1)S(1)}, bf16[512,256]{1,0:T(8,128)(2,1)S(1)}, u32[]{:S(2)}, u32[]{:S(2)}) collective-permute-start(bf16[512,256]{1,0:T(8,128)(2,1)S(1)} %collective-permute-done.3.refs_4_), channel_id=1, source_target_pairs={{0,4},{1,5},{2,6},{3,7},{4,8},{5,9},{6,10},{7,11},{8,12},{9,13},{1... | collective-permute-start | bytes 786440 | tf_op jit(solution)/shard_map/ppermute | solution.py:295
  26.8 1.5 %collective-permute-start.7 = (bf16[512,256]{1,0:T(8,128)(2,1)S(1)}, bf16[512,256]{1,0:T(8,128)(2,1)S(1)}, u32[]{:S(2)}, u32[]{:S(2)}) collective-permute-start(bf16[512,256]{1,0:T(8,128)(2,1)S(1)} %collective-permute-done.3.refs_4_), channel_id=1, source_target_pairs={{0,2},{1,3},{2,0},{3,1},{4,6},{5,7},{6,4},{7,5},{8,10},{9,11},{10,... | collective-permute-start | bytes 786440 | tf_op jit(solution)/shard_map/ppermute | solution.py:292
  28.3 2.6 %collective-permute-done.11.refs_11_ = bf16[512,256]{1,0:T(8,128)(2,1)S(1)} collective-permute-done((bf16[512,256]{1,0:T(8,128)(2,1)S(1)}, bf16[512,256]{1,0:T(8,128)(2,1)S(1)}, u32[]{:S(2)}, u32[]{:S(2)}) %collective-permute-start.11) | collective-permute-done | bytes 262176 | tf_op jit(solution)/shard_map/ppermute | solution.py:295
  30.9 1.5 %collective-permute-start.13 = (bf16[512,256]{1,0:T(8,128)(2,1)S(1)}, bf16[512,256]{1,0:T(8,128)(2,1)S(1)}, u32[]{:S(2)}, u32[]{:S(2)}) collective-permute-start(bf16[512,256]{1,0:T(8,128)(2,1)S(1)} %collective-permute-done.11.refs_11_), channel_id=1, source_target_pairs={{0,4},{1,5},{2,6},{3,7},{4,8},{5,9},{6,10},{7,11},{8,12},{9,13},{1... | collective-permute-start | bytes 786440 | tf_op jit(solution)/shard_map/ppermute | solution.py:295
  32.4 1.5 %collective-permute-start.14 = (bf16[512,256]{1,0:T(8,128)(2,1)S(1)}, bf16[512,256]{1,0:T(8,128)(2,1)}, u32[]{:S(2)}, u32[]{:S(2)}) collective-permute-start(bf16[512,256]{1,0:T(8,128)(2,1)S(1)} %collective-permute-done.11.refs_11_), channel_id=1, source_target_pairs={{0,2},{1,3},{2,0},{3,1},{4,6},{5,7},{6,4},{7,5},{8,10},{9,11},{10,... | collective-permute-start | bytes 786440 | tf_op jit(solution)/shard_map/ppermute | solution.py:292
  34.0 2.5 %collective-permute-done.6.refs_6_ = bf16[512,256]{1,0:T(8,128)(2,1)S(1)} collective-permute-done((bf16[512,256]{1,0:T(8,128)(2,1)S(1)}, bf16[512,256]{1,0:T(8,128)(2,1)S(1)}, u32[]{:S(2)}, u32[]{:S(2)}) %collective-permute-start.6) | collective-permute-done | bytes 262176 | tf_op jit(solution)/shard_map/ppermute | solution.py:295
  36.5 5.4 %collective-permute-done.13.refs_13_ = bf16[512,256]{1,0:T(8,128)(2,1)S(1)} collective-permute-done((bf16[512,256]{1,0:T(8,128)(2,1)S(1)}, bf16[512,256]{1,0:T(8,128)(2,1)S(1)}, u32[]{:S(2)}, u32[]{:S(2)}) %collective-permute-start.13) | collective-permute-done | bytes 262176 | tf_op jit(solution)/shard_map/ppermute | solution.py:295
  41.9 1.9 %collective-permute-start.15 = (bf16[512,256]{1,0:T(8,128)(2,1)S(1)}, bf16[512,256]{1,0:T(8,128)(2,1)S(1)}, u32[]{:S(2)}, u32[]{:S(2)}) collective-permute-start(bf16[512,256]{1,0:T(8,128)(2,1)S(1)} %collective-permute-done.10.refs_8_), channel_id=1, source_target_pairs={{0,12},{1,13},{2,14},{3,15},{4,0},{5,1},{6,2},{7,3},{8,4},{9,5},{1... | collective-permute-start | bytes 786440 | tf_op jit(solution)/shard_map/ppermute | solution.py:295
  43.9 1.5 %collective-permute-start.8 = (bf16[512,256]{1,0:T(8,128)(2,1)S(1)}, bf16[512,256]{1,0:T(8,128)(2,1)S(1)}, u32[]{:S(2)}, u32[]{:S(2)}) collective-permute-start(bf16[512,256]{1,0:T(8,128)(2,1)S(1)} %collective-permute-done.6.refs_6_), channel_id=1, source_target_pairs={{0,2},{1,3},{2,0},{3,1},{4,6},{5,7},{6,4},{7,5},{8,10},{9,11},{10,... | collective-permute-start | bytes 786440 | tf_op jit(solution)/shard_map/ppermute | solution.py:292
  45.4 5.8 %project.2.refs_2_ = f32[768,512]{1,0:T(8,128)S(1)} custom-call(s32[7]{0:T(128)S(1)} %stack.116.at_ref, bf16[384,8192]{1,0:T(8,128)(2,1)} %own_ref.6, bf16[384,8192]{1,0:T(8,128)(2,1)} %collective-permute-done.sib_ref, bf16[512,256]{1,0:T(8,128)(2,1)S(1)} %get-tuple-element.87.refs_0_, bf16[512,256]{1,0:T(8,128)(2,1)S(1)} %collective-permute-done.2.refs_1_, ...), custom_call_target="tpu_custom_call" | custom-call | flops 84557168640 | bytes 322437120 | tf_op jit(solution)/shard_map/project/pallas_call | solution.py:66
  51.5 1.7 %project.3.refs_0_ = f32[768,512]{1,0:T(8,128)S(1)} custom-call(s32[1]{0:T(128)} %bitcast.2.at_ref, bf16[384,8192]{1,0:T(8,128)(2,1)} %own_ref.6, bf16[384,8192]{1,0:T(8,128)(2,1)} %collective-permute-done.sib_ref, bf16[512,256]{1,0:T(8,128)(2,1)S(1)} %collective-permute-done.8.refs_0_, bf16[512,256]{1,0:T(8,128)(2,1)S(1)} %collective-permute-done.15.refs_1_, ...), custom_call_target="tpu_custom_call" | custom-call | flops 12079595520 | bytes 86507520 | tf_op jit(solution)/shard_map/project/pallas_call | solution.py:66
  53.7 3.0 %collective-permute-done.16.refs_1_ = f32[768,512]{1,0:T(8,128)S(1)} collective-permute-done((f32[768,512]{1,0:T(8,128)S(1)}, f32[768,512]{1,0:T(8,128)S(1)}, u32[]{:S(2)}, u32[]{:S(2)}) %collective-permute-start.16) | collective-permute-done | bytes 1572896 | tf_op jit(solution)/shard_map/ppermute | solution.py:289
  56.7 1.5 %outer.3 = (bf16[768,512]{1,0:T(8,128)(2,1)S(1)}, bf16[256,512]{1,0:T(8,128)(2,1)S(1)}) custom-call(s32[1]{0:T(128)} %bitcast.21.at_ref, bf16[384,4096]{1,0:T(8,128)(2,1)} %own_ref.9, bf16[384,4096]{1,0:T(8,128)(2,1)} %collective-permute-done.5.sib_ref, f32[768,512]{1,0:T(8,128)S(1)} %project.3.refs_0_, f32[768,512]{1,0:T(8,128)S(1)} %collective-permute-done.16.refs_1_), custom_call_target="tpu_custom_call" | custom-call | flops 6039797760 | bytes 27525120 | tf_op jit(solution)/shard_map/outer/pallas_call | solution.py:66
  58.2 1.5 %collective-permute-start.17 = (bf16[256,512]{1,0:T(8,128)(2,1)S(1)}, bf16[256,512]{1,0:T(8,128)(2,1)S(1)}, u32[]{:S(2)}, u32[]{:S(2)}) collective-permute-start(bf16[256,512]{1,0:T(8,128)(2,1)S(1)} %get-tuple-element.57), channel_id=1, source_target_pairs={{0,2},{1,3},{2,0},{3,1},{4,6},{5,7},{6,4},{7,5},{8,10},{9,11},{10,... | collective-permute-start | bytes 786440 | tf_op jit(solution)/shard_map/ppermute | solution.py:292
  59.7 3.3 %outer.4 = (bf16[256,512]{1,0:T(8,128)(2,1)S(1)}, bf16[256,512]{1,0:T(8,128)(2,1)S(1)}, bf16[256,512]{1,0:T(8,128)(2,1)S(1)}, f32[256,512]{1,0:T(8,128)S(1)}) custom-call(s32[4]{0:T(128)S(1)} %pad_add_fusion.1.at_ref, bf16[384,4096]{1,0:T(8,128)(2,1)} %own_ref.9, bf16[384,4096]{1,0:T(8,128)(2,1)} %collective-permute-done.5.sib_ref, ...), custom_call_target="tpu_custom_call" | custom-call | flops 24159191040 | bytes 110100480 | tf_op jit(solution)/shard_map/outer/pallas_call | solution.py:66
  63.6 1.4 %collective-permute-start.21 = (bf16[256,512]{1,0:T(8,128)(2,1)S(1)}, bf16[256,512]{1,0:T(8,128)(2,1)S(1)}, u32[]{:S(2)}, u32[]{:S(2)}) collective-permute-start(bf16[256,512]{1,0:T(8,128)(2,1)S(1)} %get-tuple-element.67), channel_id=1, source_target_pairs={{0,2},{1,3},{2,0},{3,1},{4,6},{5,7},{6,4},{7,5},{8,10},{9,11},{10,... | collective-permute-start | bytes 786440 | tf_op jit(solution)/shard_map/ppermute | solution.py:292
  65.7 1.7 %collective-permute-done.17 = bf16[256,512]{1,0:T(8,128)(2,1)S(1)} collective-permute-done((bf16[256,512]{1,0:T(8,128)(2,1)S(1)}, bf16[256,512]{1,0:T(8,128)(2,1)S(1)}, u32[]{:S(2)}, u32[]{:S(2)}) %collective-permute-start.17) | collective-permute-done | bytes 262176 | tf_op jit(solution)/shard_map/ppermute | solution.py:292
  67.8 2.8 %outer.5 = (f32[256,512]{1,0:T(8,128)S(1)}, f32[256,512]{1,0:T(8,128)S(1)}, f32[256,512]{1,0:T(8,128)S(1)}) custom-call(s32[3]{0:T(128)S(1)} %pad_add_fusion.at_ref, bf16[384,4096]{1,0:T(8,128)(2,1)} %own_ref.9, bf16[384,4096]{1,0:T(8,128)(2,1)} %collective-permute-done.5.sib_ref, bf16[768,512]{1,0:T(8,128)(2,1)S(1)} %get-tuple-element.59.refs_0_), custom_call_target="tpu_custom_call" | custom-call | flops 18119393280 | bytes 82575360 | tf_op jit(solution)/shard_map/outer/pallas_call | solution.py:66
  70.7 2.3 %collective-permute-done.19 = bf16[256,512]{1,0:T(8,128)(2,1)S(1)} collective-permute-done((bf16[256,512]{1,0:T(8,128)(2,1)S(1)}, bf16[256,512]{1,0:T(8,128)(2,1)S(1)}, u32[]{:S(2)}, u32[]{:S(2)}) %collective-permute-start.19) | collective-permute-done | bytes 262176 | tf_op jit(solution)/shard_map/ppermute | solution.py:292
  73.1 2.1 %collective-permute-start.20 = (bf16[256,512]{1,0:T(8,128)(2,1)S(1)}, bf16[256,512]{1,0:T(8,128)(2,1)S(1)}, u32[]{:S(2)}, u32[]{:S(2)}) collective-permute-start(bf16[256,512]{1,0:T(8,128)(2,1)S(1)} %add_convert_fusion.1), channel_id=1, source_target_pairs={{0,12},{1,13},{2,14},{3,15},{4,0},{5,1},{6,2},{7,3},{8,4},{9,5},{1... | collective-permute-start | bytes 786440 | tf_op jit(solution)/shard_map/ppermute | solution.py:295
  75.2 3.4 %collective-permute-done.21 = bf16[256,512]{1,0:T(8,128)(2,1)S(1)} collective-permute-done((bf16[256,512]{1,0:T(8,128)(2,1)S(1)}, bf16[256,512]{1,0:T(8,128)(2,1)S(1)}, u32[]{:S(2)}, u32[]{:S(2)}) %collective-permute-start.21) | collective-permute-done | bytes 262176 | tf_op jit(solution)/shard_map/ppermute | solution.py:292
  79.1 4.5 %collective-permute-done.18 = bf16[256,512]{1,0:T(8,128)(2,1)S(1)} collective-permute-done((bf16[256,512]{1,0:T(8,128)(2,1)S(1)}, bf16[256,512]{1,0:T(8,128)(2,1)S(1)}, u32[]{:S(2)}, u32[]{:S(2)}) %collective-permute-start.18) | collective-permute-done | bytes 262176 | tf_op jit(solution)/shard_map/ppermute | solution.py:292
  83.6 4.1 %collective-permute-done.23 = bf16[256,512]{1,0:T(8,128)(2,1)S(1)} collective-permute-done((bf16[256,512]{1,0:T(8,128)(2,1)S(1)}, bf16[256,512]{1,0:T(8,128)(2,1)S(1)}, u32[]{:S(2)}, u32[]{:S(2)}) %collective-permute-start.23) | collective-permute-done | bytes 262176 | tf_op jit(solution)/shard_map/ppermute | solution.py:295
  87.6 1.4 %divide_convert_fusion = (bf16[256,512]{1,0:T(8,128)(2,1)S(1)}, f32[256,512]{1,0:T(8,128)}, f32[256,512]{1,0:T(8,128)}) fusion(bf16[256,512]{1,0:T(8,128)(2,1)S(1)} %collective-permute-done.23, bf16[256,512]{1,0:T(8,128)(2,1)S(1)} %collective-permute-done.20, f32[256,512]{1,0:T(8,128)S(1)} %get-tuple-element.62, ...), kind=kLoop, calls=%fused_computation.2 | loop fusion | flops 2359296 | bytes 3670016 | tf_op jit(solution)/shard_map/convert_element_type | solution.py:26
  89.1 1.3 %collective-permute-start.27 = (bf16[256,256]{1,0:T(8,128)(2,1)S(1)}, bf16[256,256]{1,0:T(8,128)(2,1)S(1)}, u32[]{:S(2)}, u32[]{:S(2)}) collective-permute-start(bf16[256,256]{1,0:T(8,128)(2,1)S(1)} %get-tuple-element.88), channel_id=1, source_target_pairs={{0,2},{1,3},{2,0},{3,1},{4,6},{5,7},{6,4},{7,5},{8,10},{9,11},{10,... | collective-permute-start | bytes 393224 | tf_op jit(solution)/shard_map/ppermute | solution.py:292
  90.4 1.5 %collective-permute-start.24 = (bf16[256,256]{1,0:T(8,128)(2,1)S(1)}, bf16[256,256]{1,0:T(8,128)(2,1)S(1)}, u32[]{:S(2)}, u32[]{:S(2)}) collective-permute-start(bf16[256,256]{1,0:T(8,128)(2,1)S(1)} %get-tuple-element.89), channel_id=1, source_target_pairs={{0,4},{1,5},{2,6},{3,7},{4,8},{5,9},{6,10},{7,11},{8,12},{9,13},{1... | collective-permute-start | bytes 393224 | tf_op jit(solution)/shard_map/ppermute | solution.py:295
  92.6 3.2 %collective-permute-done.26 = bf16[256,256]{1,0:T(8,128)(2,1)S(1)} collective-permute-done((bf16[256,256]{1,0:T(8,128)(2,1)S(1)}, bf16[256,256]{1,0:T(8,128)(2,1)S(1)}, u32[]{:S(2)}, u32[]{:S(2)}) %collective-permute-start.26) | collective-permute-done | bytes 131104 | tf_op jit(solution)/shard_map/ppermute | solution.py:295
  97.7 1.2 collective-permute-start.28
  99.6 3.3 %collective-permute-done.30 = bf16[256,256]{1,0:T(8,128)(2,1)S(1)} collective-permute-done((bf16[256,256]{1,0:T(8,128)(2,1)S(1)}, bf16[256,256]{1,0:T(8,128)(2,1)S(1)}, u32[]{:S(2)}, u32[]{:S(2)}) %collective-permute-start.30) | collective-permute-done | bytes 131104 | tf_op jit(solution)/shard_map/ppermute | solution.py:295
  103.2 1.1 collective-permute-start.40
  104.4 1.4 %collective-permute-done.28 = bf16[256,256]{1,0:T(8,128)(2,1)S(1)} collective-permute-done((bf16[256,256]{1,0:T(8,128)(2,1)S(1)}, bf16[256,256]{1,0:T(8,128)(2,1)S(1)}, u32[]{:S(2)}, u32[]{:S(2)}) %collective-permute-start.28) | collective-permute-done | bytes 131104 | tf_op jit(solution)/shard_map/ppermute | solution.py:295
  105.8 1.6 %collective-permute-start.37 = (bf16[256,256]{1,0:T(8,128)(2,1)S(1)}, bf16[256,256]{1,0:T(8,128)(2,1)S(1)}, u32[]{:S(2)}, u32[]{:S(2)}) collective-permute-start(bf16[256,256]{1,0:T(8,128)(2,1)S(1)} %collective-permute-done.28), channel_id=1, source_target_pairs={{0,4},{1,5},{2,6},{3,7},{4,8},{5,9},{6,10},{7,11},{8,12},{9,13},{1... | collective-permute-start | bytes 393224 | tf_op jit(solution)/shard_map/ppermute | solution.py:295
  108.1 1.6 %collective-permute-done.39 = bf16[256,256]{1,0:T(8,128)(2,1)S(1)} collective-permute-done((bf16[256,256]{1,0:T(8,128)(2,1)S(1)}, bf16[256,256]{1,0:T(8,128)(2,1)S(1)}, u32[]{:S(2)}, u32[]{:S(2)}) %collective-permute-start.39) | collective-permute-done | bytes 131104 | tf_op jit(solution)/shard_map/ppermute | solution.py:295
  110.2 2.4 %collective-permute-done.37 = bf16[256,256]{1,0:T(8,128)(2,1)S(1)} collective-permute-done((bf16[256,256]{1,0:T(8,128)(2,1)S(1)}, bf16[256,256]{1,0:T(8,128)(2,1)S(1)}, u32[]{:S(2)}, u32[]{:S(2)}) %collective-permute-start.37) | collective-permute-done | bytes 131104 | tf_op jit(solution)/shard_map/ppermute | solution.py:295
  114.1 1.5 %collective-permute-start.42 = (bf16[256,256]{1,0:T(8,128)(2,1)S(1)}, bf16[256,256]{1,0:T(8,128)(2,1)S(1)}, u32[]{:S(2)}, u32[]{:S(2)}) collective-permute-start(bf16[256,256]{1,0:T(8,128)(2,1)S(1)} %collective-permute-done.27), channel_id=1, source_target_pairs={{0,12},{1,13},{2,14},{3,15},{4,0},{5,1},{6,2},{7,3},{8,4},{9,5},{1... | collective-permute-start | bytes 393224 | tf_op jit(solution)/shard_map/ppermute | solution.py:295
  116.2 3.0 %back.2.refs_0_ = bf16[4096,512]{1,0:T(8,128)(2,1)} custom-call(s32[10]{0:T(128)S(1)} %stack.107.at_ref, bf16[512,512]{1,0:T(8,128)(2,1)S(1)} %copy-done, bf16[256,512]{1,0:T(8,128)(2,1)S(1)} %get-tuple-element.83.refs_1_, bf16[512,256]{1,0:T(8,128)(2,1)S(1)} %constant_dynamic-update-slice_fusion.refs_2_, ...), custom_call_target="tpu_custom_call" | custom-call | flops 40265318400 | bytes 157286400 | tf_op jit(solution)/shard_map/back/pallas_call | solution.py:66
  120.8 2.4 %back.3 = bf16[4096,512]{1,0:T(8,128)(2,1)} custom-call(s32[6]{0:T(128)S(1)} %stack.96.at_ref, bf16[4096,512]{1,0:T(8,128)(2,1)} %back.2.refs_0_, bf16[512,512]{1,0:T(8,128)(2,1)S(1)} %copy-done, bf16[512,256]{1,0:T(8,128)(2,1)S(1)} %constant_dynamic-update-slice_fusion.8.refs_2_, ...), custom_call_target="tpu_custom_call", output_to_operand_aliasing={{}: (1, {})} | custom-call | flops 24159191040000 | bytes 94371840000 | tf_op jit(solution)/shard_map/back/pallas_call | solution.py:66
  (82 shorter events, 12.7 us)
Async XLA Ops:
  0.6 44.8 %collective-permute-start = (bf16[384,8192]{1,0:T(8,128)(2,1)}, bf16[384,8192]{1,0:T(8,128)(2,1)}, u32[]{:S(2)}, u32[]{:S(2)}) collective-permute-start(bf16[384,8192]{1,0:T(8,128)(2,1)} %own_ref.6), channel_id=1, source_target_pairs={{0,1},{1,0},{2,3},{3,2},{4,5},{5,4},{6,7},{7,6},{8,9},{9,8},{10,11... | collective-permute-start | bytes 18874376 | tf_op jit(solution)/shard_map/ppermute | solution.py:289
  2.2 11.8 %collective-permute-start.1 = (bf16[512,256]{1,0:T(8,128)(2,1)S(1)}, bf16[512,256]{1,0:T(8,128)(2,1)S(1)}, u32[]{:S(2)}, u32[]{:S(2)}) collective-permute-start(bf16[512,256]{1,0:T(8,128)(2,1)S(1)} %get-tuple-element.87.refs_0_), channel_id=1, source_target_pairs={{0,4},{1,5},{2,6},{3,7},{4,8},{5,9},{6,10},{7,11},{8,12},{9,13},{1... | collective-permute-start | bytes 786440 | tf_op jit(solution)/shard_map/ppermute | solution.py:295
  4.9 9.2 %collective-permute-start.2 = (bf16[512,256]{1,0:T(8,128)(2,1)S(1)}, bf16[512,256]{1,0:T(8,128)(2,1)S(1)}, u32[]{:S(2)}, u32[]{:S(2)}) collective-permute-start(bf16[512,256]{1,0:T(8,128)(2,1)S(1)} %get-tuple-element.87.refs_0_), channel_id=1, source_target_pairs={{0,2},{1,3},{2,0},{3,1},{4,6},{5,7},{6,4},{7,5},{8,10},{9,11},{10,... | collective-permute-start | bytes 786440 | tf_op jit(solution)/shard_map/ppermute | solution.py:292
  6.4 13.2 %collective-permute-start.10 = (bf16[512,256]{1,0:T(8,128)(2,1)S(1)}, bf16[512,256]{1,0:T(8,128)(2,1)S(1)}, u32[]{:S(2)}, u32[]{:S(2)}) collective-permute-start(bf16[512,256]{1,0:T(8,128)(2,1)S(1)} %get-tuple-element.86.refs_7_), channel_id=1, source_target_pairs={{0,2},{1,3},{2,0},{3,1},{4,6},{5,7},{6,4},{7,5},{8,10},{9,11},{10,... | collective-permute-start | bytes 786440 | tf_op jit(solution)/shard_map/ppermute | solution.py:292
  6.9 12.8 %collective-permute-start.9 = (bf16[512,256]{1,0:T(8,128)(2,1)S(1)}, bf16[512,256]{1,0:T(8,128)(2,1)S(1)}, u32[]{:S(2)}, u32[]{:S(2)}) collective-permute-start(bf16[512,256]{1,0:T(8,128)(2,1)S(1)} %get-tuple-element.86.refs_7_), channel_id=1, source_target_pairs={{0,4},{1,5},{2,6},{3,7},{4,8},{5,9},{6,10},{7,11},{8,12},{9,13},{1... | collective-permute-start | bytes 786440 | tf_op jit(solution)/shard_map/ppermute | solution.py:295
  14.0 11.2 %collective-permute-start.3 = (bf16[512,256]{1,0:T(8,128)(2,1)S(1)}, bf16[512,256]{1,0:T(8,128)(2,1)S(1)}, u32[]{:S(2)}, u32[]{:S(2)}) collective-permute-start(bf16[512,256]{1,0:T(8,128)(2,1)S(1)} %collective-permute-done.1.refs_2_), channel_id=1, source_target_pairs={{0,4},{1,5},{2,6},{3,7},{4,8},{5,9},{6,10},{7,11},{8,12},{9,13},{1... | collective-permute-start | bytes 786440 | tf_op jit(solution)/shard_map/ppermute | solution.py:295
  15.6 9.7 %collective-permute-start.4 = (bf16[512,256]{1,0:T(8,128)(2,1)S(1)}, bf16[512,256]{1,0:T(8,128)(2,1)S(1)}, u32[]{:S(2)}, u32[]{:S(2)}) collective-permute-start(bf16[512,256]{1,0:T(8,128)(2,1)S(1)} %collective-permute-done.1.refs_2_), channel_id=1, source_target_pairs={{0,2},{1,3},{2,0},{3,1},{4,6},{5,7},{6,4},{7,5},{8,10},{9,11},{10,... | collective-permute-start | bytes 786440 | tf_op jit(solution)/shard_map/ppermute | solution.py:292
  19.7 11.2 %collective-permute-start.11 = (bf16[512,256]{1,0:T(8,128)(2,1)S(1)}, bf16[512,256]{1,0:T(8,128)(2,1)S(1)}, u32[]{:S(2)}, u32[]{:S(2)}) collective-permute-start(bf16[512,256]{1,0:T(8,128)(2,1)S(1)} %collective-permute-done.9.refs_9_), channel_id=1, source_target_pairs={{0,4},{1,5},{2,6},{3,7},{4,8},{5,9},{6,10},{7,11},{8,12},{9,13},{1... | collective-permute-start | bytes 786440 | tf_op jit(solution)/shard_map/ppermute | solution.py:295
  21.2 9.7 %collective-permute-start.12 = (bf16[512,256]{1,0:T(8,128)(2,1)S(1)}, bf16[512,256]{1,0:T(8,128)(2,1)S(1)}, u32[]{:S(2)}, u32[]{:S(2)}) collective-permute-start(bf16[512,256]{1,0:T(8,128)(2,1)S(1)} %collective-permute-done.9.refs_9_), channel_id=1, source_target_pairs={{0,2},{1,3},{2,0},{3,1},{4,6},{5,7},{6,4},{7,5},{8,10},{9,11},{10,... | collective-permute-start | bytes 786440 | tf_op jit(solution)/shard_map/ppermute | solution.py:292
  25.3 11.2 %collective-permute-start.6 = (bf16[512,256]{1,0:T(8,128)(2,1)S(1)}, bf16[512,256]{1,0:T(8,128)(2,1)S(1)}, u32[]{:S(2)}, u32[]{:S(2)}) collective-permute-start(bf16[512,256]{1,0:T(8,128)(2,1)S(1)} %collective-permute-done.3.refs_4_), channel_id=1, source_target_pairs={{0,4},{1,5},{2,6},{3,7},{4,8},{5,9},{6,10},{7,11},{8,12},{9,13},{1... | collective-permute-start | bytes 786440 | tf_op jit(solution)/shard_map/ppermute | solution.py:295
  26.8 9.7 %collective-permute-start.7 = (bf16[512,256]{1,0:T(8,128)(2,1)S(1)}, bf16[512,256]{1,0:T(8,128)(2,1)S(1)}, u32[]{:S(2)}, u32[]{:S(2)}) collective-permute-start(bf16[512,256]{1,0:T(8,128)(2,1)S(1)} %collective-permute-done.3.refs_4_), channel_id=1, source_target_pairs={{0,2},{1,3},{2,0},{3,1},{4,6},{5,7},{6,4},{7,5},{8,10},{9,11},{10,... | collective-permute-start | bytes 786440 | tf_op jit(solution)/shard_map/ppermute | solution.py:292
  30.9 11.0 %collective-permute-start.13 = (bf16[512,256]{1,0:T(8,128)(2,1)S(1)}, bf16[512,256]{1,0:T(8,128)(2,1)S(1)}, u32[]{:S(2)}, u32[]{:S(2)}) collective-permute-start(bf16[512,256]{1,0:T(8,128)(2,1)S(1)} %collective-permute-done.11.refs_11_), channel_id=1, source_target_pairs={{0,4},{1,5},{2,6},{3,7},{4,8},{5,9},{6,10},{7,11},{8,12},{9,13},{1... | collective-permute-start | bytes 786440 | tf_op jit(solution)/shard_map/ppermute | solution.py:295
  32.4 9.5 %collective-permute-start.14 = (bf16[512,256]{1,0:T(8,128)(2,1)S(1)}, bf16[512,256]{1,0:T(8,128)(2,1)}, u32[]{:S(2)}, u32[]{:S(2)}) collective-permute-start(bf16[512,256]{1,0:T(8,128)(2,1)S(1)} %collective-permute-done.11.refs_11_), channel_id=1, source_target_pairs={{0,2},{1,3},{2,0},{3,1},{4,6},{5,7},{6,4},{7,5},{8,10},{9,11},{10,... | collective-permute-start | bytes 786440 | tf_op jit(solution)/shard_map/ppermute | solution.py:292
  41.9 9.3 %collective-permute-start.15 = (bf16[512,256]{1,0:T(8,128)(2,1)S(1)}, bf16[512,256]{1,0:T(8,128)(2,1)S(1)}, u32[]{:S(2)}, u32[]{:S(2)}) collective-permute-start(bf16[512,256]{1,0:T(8,128)(2,1)S(1)} %collective-permute-done.10.refs_8_), channel_id=1, source_target_pairs={{0,12},{1,13},{2,14},{3,15},{4,0},{5,1},{6,2},{7,3},{8,4},{9,5},{1... | collective-permute-start | bytes 786440 | tf_op jit(solution)/shard_map/ppermute | solution.py:295
  43.9 7.6 %collective-permute-start.8 = (bf16[512,256]{1,0:T(8,128)(2,1)S(1)}, bf16[512,256]{1,0:T(8,128)(2,1)S(1)}, u32[]{:S(2)}, u32[]{:S(2)}) collective-permute-start(bf16[512,256]{1,0:T(8,128)(2,1)S(1)} %collective-permute-done.6.refs_6_), channel_id=1, source_target_pairs={{0,2},{1,3},{2,0},{3,1},{4,6},{5,7},{6,4},{7,5},{8,10},{9,11},{10,... | collective-permute-start | bytes 786440 | tf_op jit(solution)/shard_map/ppermute | solution.py:292
  45.4 11.3 %collective-permute-start.5 = (bf16[384,4096]{1,0:T(8,128)(2,1)}, bf16[384,4096]{1,0:T(8,128)(2,1)}, u32[]{:S(2)}, u32[]{:S(2)}) collective-permute-start(bf16[384,4096]{1,0:T(8,128)(2,1)} %own_ref.9), channel_id=1, source_target_pairs={{0,1},{1,0},{2,3},{3,2},{4,5},{5,4},{6,7},{7,6},{8,9},{9,8},{10,11... | collective-permute-start | bytes 9437192 | tf_op jit(solution)/shard_map/ppermute | solution.py:289
  53.2 3.5 %collective-permute-start.16 = (f32[768,512]{1,0:T(8,128)S(1)}, f32[768,512]{1,0:T(8,128)S(1)}, u32[]{:S(2)}, u32[]{:S(2)}) collective-permute-start(f32[768,512]{1,0:T(8,128)S(1)} %project.3.refs_0_), channel_id=1, source_target_pairs={{0,1},{1,0},{2,3},{3,2},{4,5},{5,4},{6,7},{7,6},{8,9},{9,8},{10,11... | collective-permute-start | bytes 4718600 | tf_op jit(solution)/shard_map/ppermute | solution.py:289
  58.2 9.2 %collective-permute-start.17 = (bf16[256,512]{1,0:T(8,128)(2,1)S(1)}, bf16[256,512]{1,0:T(8,128)(2,1)S(1)}, u32[]{:S(2)}, u32[]{:S(2)}) collective-permute-start(bf16[256,512]{1,0:T(8,128)(2,1)S(1)} %get-tuple-element.57), channel_id=1, source_target_pairs={{0,2},{1,3},{2,0},{3,1},{4,6},{5,7},{6,4},{7,5},{8,10},{9,11},{10,... | collective-permute-start | bytes 786440 | tf_op jit(solution)/shard_map/ppermute | solution.py:292
  63.0 10.0 %collective-permute-start.19 = (bf16[256,512]{1,0:T(8,128)(2,1)S(1)}, bf16[256,512]{1,0:T(8,128)(2,1)S(1)}, u32[]{:S(2)}, u32[]{:S(2)}) collective-permute-start(bf16[256,512]{1,0:T(8,128)(2,1)S(1)} %get-tuple-element.65), channel_id=1, source_target_pairs={{0,2},{1,3},{2,0},{3,1},{4,6},{5,7},{6,4},{7,5},{8,10},{9,11},{10,... | collective-permute-start | bytes 786440 | tf_op jit(solution)/shard_map/ppermute | solution.py:292
  63.6 15.0 %collective-permute-start.21 = (bf16[256,512]{1,0:T(8,128)(2,1)S(1)}, bf16[256,512]{1,0:T(8,128)(2,1)S(1)}, u32[]{:S(2)}, u32[]{:S(2)}) collective-permute-start(bf16[256,512]{1,0:T(8,128)(2,1)S(1)} %get-tuple-element.67), channel_id=1, source_target_pairs={{0,2},{1,3},{2,0},{3,1},{4,6},{5,7},{6,4},{7,5},{8,10},{9,11},{10,... | collective-permute-start | bytes 786440 | tf_op jit(solution)/shard_map/ppermute | solution.py:292
  65.1 18.5 %collective-permute-start.18 = (bf16[256,512]{1,0:T(8,128)(2,1)S(1)}, bf16[256,512]{1,0:T(8,128)(2,1)S(1)}, u32[]{:S(2)}, u32[]{:S(2)}) collective-permute-start(bf16[256,512]{1,0:T(8,128)(2,1)S(1)} %get-tuple-element.63), channel_id=1, source_target_pairs={{0,2},{1,3},{2,0},{3,1},{4,6},{5,7},{6,4},{7,5},{8,10},{9,11},{10,... | collective-permute-start | bytes 786440 | tf_op jit(solution)/shard_map/ppermute | solution.py:292
  67.5 11.1 %collective-permute-start.22 = (bf16[256,512]{1,0:T(8,128)(2,1)S(1)}, bf16[256,512]{1,0:T(8,128)(2,1)S(1)}, u32[]{:S(2)}, u32[]{:S(2)}) collective-permute-start(bf16[256,512]{1,0:T(8,128)(2,1)S(1)} %convert_add_fusion.1), channel_id=1, source_target_pairs={{0,4},{1,5},{2,6},{3,7},{4,8},{5,9},{6,10},{7,11},{8,12},{9,13},{1... | collective-permute-start | bytes 786440 | tf_op jit(solution)/shard_map/ppermute | solution.py:295
  73.1 10.5 %collective-permute-start.20 = (bf16[256,512]{1,0:T(8,128)(2,1)S(1)}, bf16[256,512]{1,0:T(8,128)(2,1)S(1)}, u32[]{:S(2)}, u32[]{:S(2)}) collective-permute-start(bf16[256,512]{1,0:T(8,128)(2,1)S(1)} %add_convert_fusion.1), channel_id=1, source_target_pairs={{0,12},{1,13},{2,14},{3,15},{4,0},{5,1},{6,2},{7,3},{8,4},{9,5},{1... | collective-permute-start | bytes 786440 | tf_op jit(solution)/shard_map/ppermute | solution.py:295
  78.7 8.9 %collective-permute-start.23 = (bf16[256,512]{1,0:T(8,128)(2,1)S(1)}, bf16[256,512]{1,0:T(8,128)(2,1)S(1)}, u32[]{:S(2)}, u32[]{:S(2)}) collective-permute-start(bf16[256,512]{1,0:T(8,128)(2,1)S(1)} %add_convert_fusion), channel_id=1, source_target_pairs={{0,4},{1,5},{2,6},{3,7},{4,8},{5,9},{6,10},{7,11},{8,12},{9,13},{1... | collective-permute-start | bytes 786440 | tf_op jit(solution)/shard_map/ppermute | solution.py:295
  87.6 28.5 %copy-start = (bf16[512,512]{1,0:T(8,128)(2,1)S(1)}, bf16[512,512]{1,0:T(8,128)(2,1)}, u32[]{:S(2)}) copy-start(bf16[512,512]{1,0:T(8,128)(2,1)} %refs_1_.1) | copy-start | bytes 1572868
  89.1 6.8 %collective-permute-start.26 = (bf16[256,256]{1,0:T(8,128)(2,1)S(1)}, bf16[256,256]{1,0:T(8,128)(2,1)S(1)}, u32[]{:S(2)}, u32[]{:S(2)}) collective-permute-start(bf16[256,256]{1,0:T(8,128)(2,1)S(1)} %get-tuple-element.88), channel_id=1, source_target_pairs={{0,4},{1,5},{2,6},{3,7},{4,8},{5,9},{6,10},{7,11},{8,12},{9,13},{1... | collective-permute-start | bytes 393224 | tf_op jit(solution)/shard_map/ppermute | solution.py:295
  89.1 6.8 %collective-permute-start.27 = (bf16[256,256]{1,0:T(8,128)(2,1)S(1)}, bf16[256,256]{1,0:T(8,128)(2,1)S(1)}, u32[]{:S(2)}, u32[]{:S(2)}) collective-permute-start(bf16[256,256]{1,0:T(8,128)(2,1)S(1)} %get-tuple-element.88), channel_id=1, source_target_pairs={{0,2},{1,3},{2,0},{3,1},{4,6},{5,7},{6,4},{7,5},{8,10},{9,11},{10,... | collective-permute-start | bytes 393224 | tf_op jit(solution)/shard_map/ppermute | solution.py:292
  90.4 7.2 %collective-permute-start.24 = (bf16[256,256]{1,0:T(8,128)(2,1)S(1)}, bf16[256,256]{1,0:T(8,128)(2,1)S(1)}, u32[]{:S(2)}, u32[]{:S(2)}) collective-permute-start(bf16[256,256]{1,0:T(8,128)(2,1)S(1)} %get-tuple-element.89), channel_id=1, source_target_pairs={{0,4},{1,5},{2,6},{3,7},{4,8},{5,9},{6,10},{7,11},{8,12},{9,13},{1... | collective-permute-start | bytes 393224 | tf_op jit(solution)/shard_map/ppermute | solution.py:295
  91.9 5.8 %collective-permute-start.25 = (bf16[256,256]{1,0:T(8,128)(2,1)S(1)}, bf16[256,256]{1,0:T(8,128)(2,1)S(1)}, u32[]{:S(2)}, u32[]{:S(2)}) collective-permute-start(bf16[256,256]{1,0:T(8,128)(2,1)S(1)} %get-tuple-element.89), channel_id=1, source_target_pairs={{0,2},{1,3},{2,0},{3,1},{4,6},{5,7},{6,4},{7,5},{8,10},{9,11},{10,... | collective-permute-start | bytes 393224 | tf_op jit(solution)/shard_map/ppermute | solution.py:292
  92.6 20.6 %collective-permute-start.32 = (bf16[256,512]{1,0:T(8,128)(2,1)S(1)}, bf16[256,512]{1,0:T(8,128)(2,1)S(1)}, u32[]{:S(2)}, u32[]{:S(2)}) collective-permute-start(bf16[256,512]{1,0:T(8,128)(2,1)S(1)} %get-tuple-element.83.refs_1_), channel_id=1, source_target_pairs={{0,1},{1,0},{2,3},{3,2},{4,5},{5,4},{6,7},{7,6},{8,9},{9,8},{10,11... | collective-permute-start | bytes 786440 | tf_op jit(solution)/shard_map/ppermute | solution.py:289
  95.9 7.0 %collective-permute-start.30 = (bf16[256,256]{1,0:T(8,128)(2,1)S(1)}, bf16[256,256]{1,0:T(8,128)(2,1)S(1)}, u32[]{:S(2)}, u32[]{:S(2)}) collective-permute-start(bf16[256,256]{1,0:T(8,128)(2,1)S(1)} %collective-permute-done.26), channel_id=1, source_target_pairs={{0,4},{1,5},{2,6},{3,7},{4,8},{5,9},{6,10},{7,11},{8,12},{9,13},{1... | collective-permute-start | bytes 393224 | tf_op jit(solution)/shard_map/ppermute | solution.py:295
  96.8 6.1 %collective-permute-start.31 = (bf16[256,256]{1,0:T(8,128)(2,1)S(1)}, bf16[256,256]{1,0:T(8,128)(2,1)S(1)}, u32[]{:S(2)}, u32[]{:S(2)}) collective-permute-start(bf16[256,256]{1,0:T(8,128)(2,1)S(1)} %collective-permute-done.26), channel_id=1, source_target_pairs={{0,2},{1,3},{2,0},{3,1},{4,6},{5,7},{6,4},{7,5},{8,10},{9,11},{10,... | collective-permute-start | bytes 393224 | tf_op jit(solution)/shard_map/ppermute | solution.py:292
  97.7 8.1 %collective-permute-start.28 = (bf16[256,256]{1,0:T(8,128)(2,1)S(1)}, bf16[256,256]{1,0:T(8,128)(2,1)S(1)}, u32[]{:S(2)}, u32[]{:S(2)}) collective-permute-start(bf16[256,256]{1,0:T(8,128)(2,1)S(1)} %collective-permute-done.24), channel_id=1, source_target_pairs={{0,4},{1,5},{2,6},{3,7},{4,8},{5,9},{6,10},{7,11},{8,12},{9,13},{1... | collective-permute-start | bytes 393224 | tf_op jit(solution)/shard_map/ppermute | solution.py:295
  98.9 6.8 %collective-permute-start.29 = (bf16[256,256]{1,0:T(8,128)(2,1)S(1)}, bf16[256,256]{1,0:T(8,128)(2,1)S(1)}, u32[]{:S(2)}, u32[]{:S(2)}) collective-permute-start(bf16[256,256]{1,0:T(8,128)(2,1)S(1)} %collective-permute-done.24), channel_id=1, source_target_pairs={{0,2},{1,3},{2,0},{3,1},{4,6},{5,7},{6,4},{7,5},{8,10},{9,11},{10,... | collective-permute-start | bytes 393224 | tf_op jit(solution)/shard_map/ppermute | solution.py:292
  102.9 6.8 %collective-permute-start.39 = (bf16[256,256]{1,0:T(8,128)(2,1)S(1)}, bf16[256,256]{1,0:T(8,128)(2,1)S(1)}, u32[]{:S(2)}, u32[]{:S(2)}) collective-permute-start(bf16[256,256]{1,0:T(8,128)(2,1)S(1)} %collective-permute-done.30), channel_id=1, source_target_pairs={{0,4},{1,5},{2,6},{3,7},{4,8},{5,9},{6,10},{7,11},{8,12},{9,13},{1... | collective-permute-start | bytes 393224 | tf_op jit(solution)/shard_map/ppermute | solution.py:295
  103.2 6.4 %collective-permute-start.40 = (bf16[256,256]{1,0:T(8,128)(2,1)S(1)}, bf16[256,256]{1,0:T(8,128)(2,1)S(1)}, u32[]{:S(2)}, u32[]{:S(2)}) collective-permute-start(bf16[256,256]{1,0:T(8,128)(2,1)S(1)} %collective-permute-done.30), channel_id=1, source_target_pairs={{0,2},{1,3},{2,0},{3,1},{4,6},{5,7},{6,4},{7,5},{8,10},{9,11},{10,... | collective-permute-start | bytes 393224 | tf_op jit(solution)/shard_map/ppermute | solution.py:292
  105.8 6.8 %collective-permute-start.37 = (bf16[256,256]{1,0:T(8,128)(2,1)S(1)}, bf16[256,256]{1,0:T(8,128)(2,1)S(1)}, u32[]{:S(2)}, u32[]{:S(2)}) collective-permute-start(bf16[256,256]{1,0:T(8,128)(2,1)S(1)} %collective-permute-done.28), channel_id=1, source_target_pairs={{0,4},{1,5},{2,6},{3,7},{4,8},{5,9},{6,10},{7,11},{8,12},{9,13},{1... | collective-permute-start | bytes 393224 | tf_op jit(solution)/shard_map/ppermute | solution.py:295
  107.3 5.3 %collective-permute-start.38 = (bf16[256,256]{1,0:T(8,128)(2,1)S(1)}, bf16[256,256]{1,0:T(8,128)(2,1)S(1)}, u32[]{:S(2)}, u32[]{:S(2)}) collective-permute-start(bf16[256,256]{1,0:T(8,128)(2,1)S(1)} %collective-permute-done.28), channel_id=1, source_target_pairs={{0,2},{1,3},{2,0},{3,1},{4,6},{5,7},{6,4},{7,5},{8,10},{9,11},{10,... | collective-permute-start | bytes 393224 | tf_op jit(solution)/shard_map/ppermute | solution.py:292
  109.7 4.5 %collective-permute-start.34 = (bf16[512,256]{1,0:T(8,128)(2,1)S(1)}, bf16[512,256]{1,0:T(8,128)(2,1)S(1)}, u32[]{:S(2)}, u32[]{:S(2)}) collective-permute-start(bf16[512,256]{1,0:T(8,128)(2,1)S(1)} %constant_dynamic-update-slice_fusion.2.refs_3_), channel_id=1, source_target_pairs={{0,1},{1,0},{2,3},{3,2},{4,5},{5,4},{6,7},{7,6},{8,9},{9,8},{10,11... | collective-permute-start | bytes 786440 | tf_op jit(solution)/shard_map/ppermute | solution.py:289
  109.7 6.0 %collective-permute-start.33 = (bf16[512,256]{1,0:T(8,128)(2,1)S(1)}, bf16[512,256]{1,0:T(8,128)(2,1)S(1)}, u32[]{:S(2)}, u32[]{:S(2)}) collective-permute-start(bf16[512,256]{1,0:T(8,128)(2,1)S(1)} %constant_dynamic-update-slice_fusion.refs_2_), channel_id=1, source_target_pairs={{0,1},{1,0},{2,3},{3,2},{4,5},{5,4},{6,7},{7,6},{8,9},{9,8},{10,11... | collective-permute-start | bytes 786440 | tf_op jit(solution)/shard_map/ppermute | solution.py:289
  112.6 3.1 %collective-permute-start.36 = (bf16[512,256]{1,0:T(8,128)(2,1)S(1)}, bf16[512,256]{1,0:T(8,128)(2,1)S(1)}, u32[]{:S(2)}, u32[]{:S(2)}) collective-permute-start(bf16[512,256]{1,0:T(8,128)(2,1)S(1)} %constant_dynamic-update-slice_fusion.6.refs_5_), channel_id=1, source_target_pairs={{0,1},{1,0},{2,3},{3,2},{4,5},{5,4},{6,7},{7,6},{8,9},{9,8},{10,11... | collective-permute-start | bytes 786440 | tf_op jit(solution)/shard_map/ppermute | solution.py:289
  112.6 3.6 %collective-permute-start.35 = (bf16[512,256]{1,0:T(8,128)(2,1)S(1)}, bf16[512,256]{1,0:T(8,128)(2,1)S(1)}, u32[]{:S(2)}, u32[]{:S(2)}) collective-permute-start(bf16[512,256]{1,0:T(8,128)(2,1)S(1)} %constant_dynamic-update-slice_fusion.4.refs_4_), channel_id=1, source_target_pairs={{0,1},{1,0},{2,3},{3,2},{4,5},{5,4},{6,7},{7,6},{8,9},{9,8},{10,11... | collective-permute-start | bytes 786440 | tf_op jit(solution)/shard_map/ppermute | solution.py:289
  113.2 6.2 %collective-permute-start.41 = (bf16[256,256]{1,0:T(8,128)(2,1)S(1)}, bf16[256,256]{1,0:T(8,128)(2,1)S(1)}, u32[]{:S(2)}, u32[]{:S(2)}) collective-permute-start(bf16[256,256]{1,0:T(8,128)(2,1)S(1)} %collective-permute-done.37), channel_id=1, source_target_pairs={{0,2},{1,3},{2,0},{3,1},{4,6},{5,7},{6,4},{7,5},{8,10},{9,11},{10,... | collective-permute-start | bytes 393224 | tf_op jit(solution)/shard_map/ppermute | solution.py:292
  114.1 5.1 %collective-permute-start.42 = (bf16[256,256]{1,0:T(8,128)(2,1)S(1)}, bf16[256,256]{1,0:T(8,128)(2,1)S(1)}, u32[]{:S(2)}, u32[]{:S(2)}) collective-permute-start(bf16[256,256]{1,0:T(8,128)(2,1)S(1)} %collective-permute-done.27), channel_id=1, source_target_pairs={{0,12},{1,13},{2,14},{3,15},{4,0},{5,1},{6,2},{7,3},{8,4},{9,5},{1... | collective-permute-start | bytes 393224 | tf_op jit(solution)/shard_map/ppermute | solution.py:295
  115.6 5.2 %collective-permute-start.44 = (bf16[512,256]{1,0:T(8,128)(2,1)S(1)}, bf16[512,256]{1,0:T(8,128)(2,1)S(1)}, u32[]{:S(2)}, u32[]{:S(2)}) collective-permute-start(bf16[512,256]{1,0:T(8,128)(2,1)S(1)} %constant_dynamic-update-slice_fusion.10.refs_3_), channel_id=1, source_target_pairs={{0,1},{1,0},{2,3},{3,2},{4,5},{5,4},{6,7},{7,6},{8,9},{9,8},{10,11... | collective-permute-start | bytes 786440 | tf_op jit(solution)/shard_map/ppermute | solution.py:289
  115.6 5.2 %collective-permute-start.43 = (bf16[512,256]{1,0:T(8,128)(2,1)S(1)}, bf16[512,256]{1,0:T(8,128)(2,1)S(1)}, u32[]{:S(2)}, u32[]{:S(2)}) collective-permute-start(bf16[512,256]{1,0:T(8,128)(2,1)S(1)} %constant_dynamic-update-slice_fusion.8.refs_2_), channel_id=1, source_target_pairs={{0,1},{1,0},{2,3},{3,2},{4,5},{5,4},{6,7},{7,6},{8,9},{9,8},{10,11... | collective-permute-start | bytes 786440 | tf_op jit(solution)/shard_map/ppermute | solution.py:289
  119.2 1.4 %collective-permute-start.46 = (bf16[256,256]{1,0:T(8,128)(2,1)S(1)}, bf16[256,256]{1,0:T(8,128)(2,1)S(1)}, u32[]{:S(2)}, u32[]{:S(2)}) collective-permute-start(bf16[256,256]{1,0:T(8,128)(2,1)S(1)} %collective-permute-done.42.refs_5_), channel_id=1, source_target_pairs={{0,1},{1,0},{2,3},{3,2},{4,5},{5,4},{6,7},{7,6},{8,9},{9,8},{10,11... | collective-permute-start | bytes 393224 | tf_op jit(solution)/shard_map/ppermute | solution.py:289
  119.3 1.5 %collective-permute-start.45 = (bf16[256,256]{1,0:T(8,128)(2,1)S(1)}, bf16[256,256]{1,0:T(8,128)(2,1)S(1)}, u32[]{:S(2)}, u32[]{:S(2)}) collective-permute-start(bf16[256,256]{1,0:T(8,128)(2,1)S(1)} %collective-permute-done.41.refs_4_), channel_id=1, source_target_pairs={{0,1},{1,0},{2,3},{3,2},{4,5},{5,4},{6,7},{7,6},{8,9},{9,8},{10,11... | collective-permute-start | bytes 393224 | tf_op jit(solution)/shard_map/ppermute | solution.py:289
  (2 other events, 40.4 us)

commit v11 on v10

--- a/solution.py
+++ b/solution.py
@@ -80,117 +80,90 @@
     )(scalars, *far, *near)
 
 
-def project(activations, sibling, at, blocks, before, weight):
+def project(activations, sibling, at, blocks):
     chunks, many = len(blocks), at.shape[0]
-    flat = [chunk[j] for chunk in blocks for j in sorted(chunk)]
+    flat = [block for chunk in blocks for block in chunk]
     (depth, cols), rows = flat[0].shape, activations.shape[0]
-    held = [] if before is None else [before]
-    copies = 2 * many + len(flat) + len(held)
+    wide = chunks * cols
 
     def kernel(at_ref, own_ref, sib_ref, *refs):
-        block_refs, out_ref = refs[: len(flat)], refs[len(flat) + len(held)]
-        a, b, total, sems = refs[len(flat) + len(held) + 1 :]
-        started = []
-
-        def start(source, target):
-            started.append(pltpu.make_async_copy(source, target, sems.at[len(started)]))
-            started[-1].start()
+        block_refs, (out_ref, a, b, total, sems) = refs[: len(flat)], refs[len(flat) :]
+        started = [[] for _ in range(many)]
+
+        def start(j, source, target):
+            n = sum(len(copies) for copies in started)
+            started[j].append(pltpu.make_async_copy(source, target, sems.at[n]))
+            started[j][-1].start()
 
         core = lax.rem(lax.axis_index("dp"), 2)
         here, there = (pl.ds(pl.multiple_of(c * rows, rows), rows) for c in (core, 1 - core))
         for j in range(many):
             columns = pl.ds(pl.multiple_of(at_ref[j] * depth, depth), depth)
-            start(own_ref.at[:, columns], a.at[here, pl.ds(j * depth, depth)])
-            start(sib_ref.at[:, columns], a.at[there, pl.ds(j * depth, depth)])
-        places = [(i, j) for i, chunk in enumerate(blocks) for j in sorted(chunk)]
-        for ref, (i, j) in zip(block_refs, places):
-            start(ref, b.at[pl.ds(j * depth, depth), pl.ds(i * cols, cols)])
-        if held:
-            start(refs[len(flat)], total)
+            start(j, own_ref.at[:, columns], a.at[here, pl.ds(j * depth, depth)])
+            start(j, sib_ref.at[:, columns], a.at[there, pl.ds(j * depth, depth)])
+        for n, ref in enumerate(block_refs):
+            i, j = n // many, n % many
+            start(j, ref, b.at[pl.ds(j * depth, depth), pl.ds(i * cols, cols)])
         cut = (many + 1) // 2
         for low, high in ((0, cut), (cut, many)):
-            for n, copy in enumerate(started):
-                j = n // 2 if n < 2 * many else places[n - 2 * many][1]
-                if low <= j < high:
+            for copies in started[low:high]:
+                for copy in copies:
                     copy.wait()
             deep = slice(low * depth, high * depth)
             term = jnp.dot(a[:, deep], b[deep, :], preferred_element_type=F32)
             total[...] = total[...] + term if low else term
-        back_copy = pltpu.make_async_copy(total, out_ref, sems.at[copies])
+        back_copy = pltpu.make_async_copy(total, out_ref, sems.at[2 * many + len(flat)])
         back_copy.start()
         back_copy.wait()
 
-    wide = chunks * cols
     return call(
         kernel,
         at,
-        [pinned(activations), pinned(sibling), *flat, *held],
+        [pinned(activations), pinned(sibling), *flat],
         [],
         [(False, jax.ShapeDtypeStruct((2 * rows, wide), F32))],
         [
             pltpu.VMEM((2 * rows, many * depth), BF16),
             pltpu.VMEM((many * depth, wide), BF16),
             pltpu.VMEM((2 * rows, wide), F32),
-            pltpu.SemaphoreType.DMA((copies + 1,)),
+            pltpu.SemaphoreType.DMA((2 * many + len(flat) + 1,)),
         ],
-        weight=weight,
+        weight=W_EARLY,
         flops=4 * rows * depth * len(flat) * cols,
         moved=4 * rows * depth * many + 2 * depth * len(flat) * cols + 8 * rows * wide,
         name="project",
     )[0]
 
 
-def project_late(activations, sibling, at, blocks, before, weight):
-    chunks, many = len(blocks), at.shape[0]
-    flat = [chunk[j] for chunk in blocks for j in sorted(chunk)]
-    (depth, cols), rows = flat[0].shape, activations.shape[0]
-    wide, held = chunks * cols, [] if before is None else [before]
-    moved = flat if len(flat) > chunks else []
+def project_last(activations, sibling, at, blocks, before):
+    (depth, cols), rows = blocks[0].shape, activations.shape[0]
 
     def kernel(at_ref, own_ref, sib_ref, *refs):
-        block_refs, out_ref = refs[: len(flat)], refs[len(flat) + len(held)]
-        a, b, sems = refs[len(flat) + len(held) + 1 :]
-        started = []
-
-        def start(source, target):
-            started.append(pltpu.make_async_copy(source, target, sems.at[len(started)]))
-            started[-1].start()
-
+        block_refs, (before_ref, out_ref, a, sems) = refs[: len(blocks)], refs[len(blocks) :]
         core = lax.rem(lax.axis_index("dp"), 2)
-        here, there = (pl.ds(pl.multiple_of(c * rows, rows), rows) for c in (core, 1 - core))
-        for j in range(many):
-            columns = pl.ds(pl.multiple_of(at_ref[j] * depth, depth), depth)
-            start(own_ref.at[:, columns], a.at[here, pl.ds(j * depth, depth)])
-            start(sib_ref.at[:, columns], a.at[there, pl.ds(j * depth, depth)])
-        places = [(i, j) for i, chunk in enumerate(blocks) for j in sorted(chunk)]
-        if moved:
-            for ref, (i, j) in zip(block_refs, places):
-                start(ref, b.at[pl.ds(j * depth, depth), pl.ds(i * cols, cols)])
-        for copy in started:
+        columns = pl.ds(pl.multiple_of(at_ref[0] * depth, depth), depth)
+        copies = []
+        for n, (c, ref) in enumerate(((core, own_ref), (1 - core, sib_ref))):
+            target = a.at[pl.ds(pl.multiple_of(c * rows, rows), rows), :]
+            copies.append(pltpu.make_async_copy(ref.at[:, columns], target, sems.at[n]))
+            copies[-1].start()
+        for copy in copies:
             copy.wait()
-        for i, chunk in enumerate(blocks):
+        for i, ref in enumerate(block_refs):
             part = slice(i * cols, (i + 1) * cols)
-            deep = slice(min(chunk) * depth, (max(chunk) + 1) * depth)
-            block = b[deep, part] if moved else block_refs[i][...]
-            term = jnp.dot(a[:, deep], block, preferred_element_type=F32)
-            out_ref[:, part] = refs[len(flat)][:, part] + term if held else term
-
-    far = [pinned(activations), pinned(sibling)]
+            out_ref[:, part] = before_ref[:, part] + jnp.dot(a[...], ref[...], preferred_element_type=F32)
+
     return call(
         kernel,
         at,
-        far + moved,
-        ([] if moved else flat) + held,
-        [(True, jax.ShapeDtypeStruct((2 * rows, wide), F32))],
-        [
-            pltpu.VMEM((2 * rows, many * depth), BF16),
-            pltpu.VMEM((many * depth, wide) if moved else (16, 128), BF16),
-            pltpu.SemaphoreType.DMA((2 * many + len(moved),)),
-        ],
-        weight=weight,
-        flops=4 * rows * depth * len(flat) * cols,
-        moved=4 * rows * depth * many + 2 * depth * len(flat) * cols + 8 * rows * wide,
-        name="project",
+        [pinned(activations), pinned(sibling)],
+        [*blocks, before],
+        [(True, jax.ShapeDtypeStruct(before.shape, F32))],
+        [pltpu.VMEM((2 * rows, depth), BF16), pltpu.SemaphoreType.DMA((2,))],
+        weight=W_LATE,
+        flops=4 * rows * depth * len(blocks) * cols,
+        moved=4 * rows * depth + 2 * depth * len(blocks) * cols + 8 * rows * len(blocks) * cols,
+        name="project_last",
     )[0]
 
 
@@ -332,12 +305,9 @@
     line, across = gather([projector[:, part] for part in parts])
     g_sibling = swap_core(after(out_grads, a_sibling, line[0][2]))
     block = lambda i, n: (across if n % 2 else line)[i][n // 2]
-    soon = [last] * CHUNKS
-    blocks = [{n: block(i, n) for n in range(soon[i])} for i in range(CHUNKS)]
-    mine = project(activations, a_sibling, at_in[:last], blocks, None, W_EARLY)
-    low = min(soon)
-    blocks = [{n - low: block(i, n) for n in range(soon[i], last + 1)} for i in range(CHUNKS)]
-    mine = project_late(activations, a_sibling, at_in[low:], blocks, mine, W_LATE)
+    mine = project(activations, a_sibling, at_in[:last], [[block(i, n) for n in range(last)] for i in range(CHUNKS)])
+    mine = project_last(activations, a_sibling, at_in[last:], [block(i, last) for i in range(CHUNKS)], mine)
+
     projected, send = outer(out_grads, g_sibling, at_out[:1], width, [BF16], (mine, swap_core(mine)))
     at = after(at_out[1 : nz + 1], send)
     *sends, keep = outer(out_grads, g_sibling, at, width, [BF16] * (nz - 1) + [F32], projected)
@@ -356,7 +326,8 @@
     steps = range(1, nz)
     mine = [(direction,)] + [tuple(jnp.concatenate([line[i][k], across[i][k - 1]]) for i in range(CHUNKS)) for k in steps]
     mine.append(tuple(across[i][-1] for i in range(CHUNKS)))
-    theirs = [tuple(swap_core(x) for x in group) for group in mine[:-1]]
+    theirs = [tuple(swap_core(after(x, line[0][1])) for x in mine[0])]
+    theirs += [tuple(swap_core(x) for x in group) for group in mine[1:-1]]
     order = [[(0, 0)]] + [[(-k, 0), (1 - k, 1)] for k in steps] + [[(1 - nz, 1)]]
     update = None
     for low, high, weight in ((0, nz - 1, W_BACK), (nz - 1, nz + 1, W_LAST)):

time: 123 us -> 123 us (level)
    ppermute x18, starting transfers between devices: 20 us -> 18.3 us  [swap_y(): return lax.ppermute(x, 'dp', pairs(lambda a, b, c: (a, 1 - b, c)))]
  transfers between devices with their start and end apart: 47 -> 47, of which waited for: 20 -> 22; matrix products, arithmetic and copies ran while one was open for 1% -> 2% of each run, Pallas kernels for 14% -> 14%
where the time goes in v11:
time: 123 us
  waiting for transfers between devices  53.8 us (44%)
  starting transfers between devices  44.1 us (36%)
  Pallas kernels  20.6 us (17%)
  other arithmetic  1.8 us (1%)
  local copies, waits for them, and re-layouts  1.47 us (1%)
    ppermute x17, waiting for transfers between devices, shift_z(): return lax.ppermute(x, 'dp', pairs(lambda a, b, c: ((a + k) % nz, b, c)))  34.8 us
    ppermute x17, starting transfers between devices, shift_z(): return lax.ppermute(x, 'dp', pairs(lambda a, b, c: ((a + k) % nz, b, c)))  22.9 us
    pallas_call x7, Pallas kernels, call(): pl.pallas_call(kernel, grid_spec=pltpu.PrefetchScalarGridSpec(num_scalar_...  20.6 us
    ppermute x18, starting transfers between devices, swap_y(): return lax.ppermute(x, 'dp', pairs(lambda a, b, c: (a, 1 - b, c)))  18.3 us
    ppermute x18, waiting for transfers between devices, swap_y(): return lax.ppermute(x, 'dp', pairs(lambda a, b, c: (a, 1 - b, c)))  15 us
    ppermute x12, waiting for transfers between devices, swap_core(): return lax.ppermute(x, 'dp', pairs(lambda a, b, c: (a, b, 1 - c)))  3.94 us
    ppermute x12, starting transfers between devices, swap_core(): return lax.ppermute(x, 'dp', pairs(lambda a, b, c: (a, b, 1 - c)))  2.97 us
  transfers between devices with their start and end apart: 47, of which 22 were waited for; matrix products, arithmetic and copies ran while one was open for 2% of the time, Pallas kernels for 14%

profile of v11, /device:TPU:0, one launch (start us, length us, event | category | flops | bytes accessed | tf_op | source)
XLA Modules:
  0.0 122.7 jit_solution(7477154899096934341)
XLA Ops:
  1.1 1.1 fusion.2
  2.2 2.6 %collective-permute-start.1 = (bf16[512,256]{1,0:T(8,128)(2,1)S(1)}, bf16[512,256]{1,0:T(8,128)(2,1)S(1)}, u32[]{:S(2)}, u32[]{:S(2)}) collective-permute-start(bf16[512,256]{1,0:T(8,128)(2,1)S(1)} %get-tuple-element.89.refs_0_), channel_id=1, source_target_pairs={{0,4},{1,5},{2,6},{3,7},{4,8},{5,9},{6,10},{7,11},{8,12},{9,13},{1... | collective-permute-start | bytes 786440 | tf_op jit(solution)/shard_map/ppermute | solution.py:268
  4.9 1.5 %collective-permute-start.2 = (bf16[512,256]{1,0:T(8,128)(2,1)S(1)}, bf16[512,256]{1,0:T(8,128)(2,1)S(1)}, u32[]{:S(2)}, u32[]{:S(2)}) collective-permute-start(bf16[512,256]{1,0:T(8,128)(2,1)S(1)} %get-tuple-element.89.refs_0_), channel_id=1, source_target_pairs={{0,2},{1,3},{2,0},{3,1},{4,6},{5,7},{6,4},{7,5},{8,10},{9,11},{10,... | collective-permute-start | bytes 786440 | tf_op jit(solution)/shard_map/ppermute | solution.py:265
  6.9 1.6 %collective-permute-start.9 = (bf16[512,256]{1,0:T(8,128)(2,1)S(1)}, bf16[512,256]{1,0:T(8,128)(2,1)S(1)}, u32[]{:S(2)}, u32[]{:S(2)}) collective-permute-start(bf16[512,256]{1,0:T(8,128)(2,1)S(1)} %get-tuple-element.88.refs_7_), channel_id=1, source_target_pairs={{0,4},{1,5},{2,6},{3,7},{4,8},{5,9},{6,10},{7,11},{8,12},{9,13},{1... | collective-permute-start | bytes 786440 | tf_op jit(solution)/shard_map/ppermute | solution.py:268
  8.5 5.6 %collective-permute-done.1.refs_2_ = bf16[512,256]{1,0:T(8,128)(2,1)S(1)} collective-permute-done((bf16[512,256]{1,0:T(8,128)(2,1)S(1)}, bf16[512,256]{1,0:T(8,128)(2,1)S(1)}, u32[]{:S(2)}, u32[]{:S(2)}) %collective-permute-start.1) | collective-permute-done | bytes 262176 | tf_op jit(solution)/shard_map/ppermute | solution.py:268
  14.0 1.5 %collective-permute-start.3 = (bf16[512,256]{1,0:T(8,128)(2,1)S(1)}, bf16[512,256]{1,0:T(8,128)(2,1)S(1)}, u32[]{:S(2)}, u32[]{:S(2)}) collective-permute-start(bf16[512,256]{1,0:T(8,128)(2,1)S(1)} %collective-permute-done.1.refs_2_), channel_id=1, source_target_pairs={{0,4},{1,5},{2,6},{3,7},{4,8},{5,9},{6,10},{7,11},{8,12},{9,13},{1... | collective-permute-start | bytes 786440 | tf_op jit(solution)/shard_map/ppermute | solution.py:268
  15.6 1.5 %collective-permute-start.4 = (bf16[512,256]{1,0:T(8,128)(2,1)S(1)}, bf16[512,256]{1,0:T(8,128)(2,1)S(1)}, u32[]{:S(2)}, u32[]{:S(2)}) collective-permute-start(bf16[512,256]{1,0:T(8,128)(2,1)S(1)} %collective-permute-done.1.refs_2_), channel_id=1, source_target_pairs={{0,2},{1,3},{2,0},{3,1},{4,6},{5,7},{6,4},{7,5},{8,10},{9,11},{10,... | collective-permute-start | bytes 786440 | tf_op jit(solution)/shard_map/ppermute | solution.py:265
  17.1 2.5 %collective-permute-done.10.refs_8_ = bf16[512,256]{1,0:T(8,128)(2,1)S(1)} collective-permute-done((bf16[512,256]{1,0:T(8,128)(2,1)S(1)}, bf16[512,256]{1,0:T(8,128)(2,1)S(1)}, u32[]{:S(2)}, u32[]{:S(2)}) %collective-permute-start.10) | collective-permute-done | bytes 262176 | tf_op jit(solution)/shard_map/ppermute | solution.py:265
  19.7 1.5 %collective-permute-start.11 = (bf16[512,256]{1,0:T(8,128)(2,1)S(1)}, bf16[512,256]{1,0:T(8,128)(2,1)S(1)}, u32[]{:S(2)}, u32[]{:S(2)}) collective-permute-start(bf16[512,256]{1,0:T(8,128)(2,1)S(1)} %collective-permute-done.9.refs_9_), channel_id=1, source_target_pairs={{0,4},{1,5},{2,6},{3,7},{4,8},{5,9},{6,10},{7,11},{8,12},{9,13},{1... | collective-permute-start | bytes 786440 | tf_op jit(solution)/shard_map/ppermute | solution.py:268
  21.2 1.5 %collective-permute-start.12 = (bf16[512,256]{1,0:T(8,128)(2,1)S(1)}, bf16[512,256]{1,0:T(8,128)(2,1)S(1)}, u32[]{:S(2)}, u32[]{:S(2)}) collective-permute-start(bf16[512,256]{1,0:T(8,128)(2,1)S(1)} %collective-permute-done.9.refs_9_), channel_id=1, source_target_pairs={{0,2},{1,3},{2,0},{3,1},{4,6},{5,7},{6,4},{7,5},{8,10},{9,11},{10,... | collective-permute-start | bytes 786440 | tf_op jit(solution)/shard_map/ppermute | solution.py:265
  22.7 2.6 %collective-permute-done.3.refs_4_ = bf16[512,256]{1,0:T(8,128)(2,1)S(1)} collective-permute-done((bf16[512,256]{1,0:T(8,128)(2,1)S(1)}, bf16[512,256]{1,0:T(8,128)(2,1)S(1)}, u32[]{:S(2)}, u32[]{:S(2)}) %collective-permute-start.3) | collective-permute-done | bytes 262176 | tf_op jit(solution)/shard_map/ppermute | solution.py:268
  25.3 1.5 %collective-permute-start.6 = (bf16[512,256]{1,0:T(8,128)(2,1)S(1)}, bf16[512,256]{1,0:T(8,128)(2,1)S(1)}, u32[]{:S(2)}, u32[]{:S(2)}) collective-permute-start(bf16[512,256]{1,0:T(8,128)(2,1)S(1)} %collective-permute-done.3.refs_4_), channel_id=1, source_target_pairs={{0,4},{1,5},{2,6},{3,7},{4,8},{5,9},{6,10},{7,11},{8,12},{9,13},{1... | collective-permute-start | bytes 786440 | tf_op jit(solution)/shard_map/ppermute | solution.py:268
  26.8 1.5 %collective-permute-start.7 = (bf16[512,256]{1,0:T(8,128)(2,1)S(1)}, bf16[512,256]{1,0:T(8,128)(2,1)S(1)}, u32[]{:S(2)}, u32[]{:S(2)}) collective-permute-start(bf16[512,256]{1,0:T(8,128)(2,1)S(1)} %collective-permute-done.3.refs_4_), channel_id=1, source_target_pairs={{0,2},{1,3},{2,0},{3,1},{4,6},{5,7},{6,4},{7,5},{8,10},{9,11},{10,... | collective-permute-start | bytes 786440 | tf_op jit(solution)/shard_map/ppermute | solution.py:265
  28.3 2.6 %collective-permute-done.11.refs_11_ = bf16[512,256]{1,0:T(8,128)(2,1)S(1)} collective-permute-done((bf16[512,256]{1,0:T(8,128)(2,1)S(1)}, bf16[512,256]{1,0:T(8,128)(2,1)S(1)}, u32[]{:S(2)}, u32[]{:S(2)}) %collective-permute-start.11) | collective-permute-done | bytes 262176 | tf_op jit(solution)/shard_map/ppermute | solution.py:268
  30.9 1.5 %collective-permute-start.13 = (bf16[512,256]{1,0:T(8,128)(2,1)S(1)}, bf16[512,256]{1,0:T(8,128)(2,1)S(1)}, u32[]{:S(2)}, u32[]{:S(2)}) collective-permute-start(bf16[512,256]{1,0:T(8,128)(2,1)S(1)} %collective-permute-done.11.refs_11_), channel_id=1, source_target_pairs={{0,4},{1,5},{2,6},{3,7},{4,8},{5,9},{6,10},{7,11},{8,12},{9,13},{1... | collective-permute-start | bytes 786440 | tf_op jit(solution)/shard_map/ppermute | solution.py:268
  32.4 1.5 %collective-permute-start.14 = (bf16[512,256]{1,0:T(8,128)(2,1)S(1)}, bf16[512,256]{1,0:T(8,128)(2,1)}, u32[]{:S(2)}, u32[]{:S(2)}) collective-permute-start(bf16[512,256]{1,0:T(8,128)(2,1)S(1)} %collective-permute-done.11.refs_11_), channel_id=1, source_target_pairs={{0,2},{1,3},{2,0},{3,1},{4,6},{5,7},{6,4},{7,5},{8,10},{9,11},{10,... | collective-permute-start | bytes 786440 | tf_op jit(solution)/shard_map/ppermute | solution.py:265
  34.0 2.5 %collective-permute-done.6.refs_6_ = bf16[512,256]{1,0:T(8,128)(2,1)S(1)} collective-permute-done((bf16[512,256]{1,0:T(8,128)(2,1)S(1)}, bf16[512,256]{1,0:T(8,128)(2,1)S(1)}, u32[]{:S(2)}, u32[]{:S(2)}) %collective-permute-start.6) | collective-permute-done | bytes 262176 | tf_op jit(solution)/shard_map/ppermute | solution.py:268
  36.5 5.4 %collective-permute-done.13.refs_13_ = bf16[512,256]{1,0:T(8,128)(2,1)S(1)} collective-permute-done((bf16[512,256]{1,0:T(8,128)(2,1)S(1)}, bf16[512,256]{1,0:T(8,128)(2,1)S(1)}, u32[]{:S(2)}, u32[]{:S(2)}) %collective-permute-start.13) | collective-permute-done | bytes 262176 | tf_op jit(solution)/shard_map/ppermute | solution.py:268
  41.9 1.9 %collective-permute-start.15 = (bf16[512,256]{1,0:T(8,128)(2,1)S(1)}, bf16[512,256]{1,0:T(8,128)(2,1)S(1)}, u32[]{:S(2)}, u32[]{:S(2)}) collective-permute-start(bf16[512,256]{1,0:T(8,128)(2,1)S(1)} %collective-permute-done.10.refs_8_), channel_id=1, source_target_pairs={{0,12},{1,13},{2,14},{3,15},{4,0},{5,1},{6,2},{7,3},{8,4},{9,5},{1... | collective-permute-start | bytes 786440 | tf_op jit(solution)/shard_map/ppermute | solution.py:268
  43.9 1.5 %collective-permute-start.8 = (bf16[512,256]{1,0:T(8,128)(2,1)S(1)}, bf16[512,256]{1,0:T(8,128)(2,1)S(1)}, u32[]{:S(2)}, u32[]{:S(2)}) collective-permute-start(bf16[512,256]{1,0:T(8,128)(2,1)S(1)} %collective-permute-done.6.refs_6_), channel_id=1, source_target_pairs={{0,2},{1,3},{2,0},{3,1},{4,6},{5,7},{6,4},{7,5},{8,10},{9,11},{10,... | collective-permute-start | bytes 786440 | tf_op jit(solution)/shard_map/ppermute | solution.py:265
  45.4 5.8 %project.1.refs_2_ = f32[768,512]{1,0:T(8,128)S(1)} custom-call(s32[7]{0:T(128)S(1)} %stack.116.at_ref, bf16[384,8192]{1,0:T(8,128)(2,1)} %own_ref.6, bf16[384,8192]{1,0:T(8,128)(2,1)} %collective-permute-done.sib_ref, bf16[512,256]{1,0:T(8,128)(2,1)S(1)} %get-tuple-element.89.refs_0_, bf16[512,256]{1,0:T(8,128)(2,1)S(1)} %collective-permute-done.2.refs_1_, ...), custom_call_target="tpu_custom_call" | custom-call | flops 84557168640 | bytes 322437120 | tf_op jit(solution)/shard_map/project/pallas_call | solution.py:66
  51.5 1.7 %project_last.1.refs_0_ = f32[768,512]{1,0:T(8,128)S(1)} custom-call(s32[1]{0:T(128)} %bitcast.2.at_ref, bf16[384,8192]{1,0:T(8,128)(2,1)} %own_ref.6, bf16[384,8192]{1,0:T(8,128)(2,1)} %collective-permute-done.sib_ref, bf16[512,256]{1,0:T(8,128)(2,1)S(1)} %collective-permute-done.8.refs_0_, bf16[512,256]{1,0:T(8,128)(2,1)S(1)} %collective-permute-done.15.refs_1_, ...), custom_call_target="tpu_custom_call" | custom-call | flops 12079595520 | bytes 86507520 | tf_op jit(solution)/shard_map/project_last/pallas_call | solution.py:66
  53.7 3.0 %collective-permute-done.16.refs_1_ = f32[768,512]{1,0:T(8,128)S(1)} collective-permute-done((f32[768,512]{1,0:T(8,128)S(1)}, f32[768,512]{1,0:T(8,128)S(1)}, u32[]{:S(2)}, u32[]{:S(2)}) %collective-permute-start.16) | collective-permute-done | bytes 1572896 | tf_op jit(solution)/shard_map/ppermute | solution.py:262
  56.7 1.5 %outer.3 = (bf16[768,512]{1,0:T(8,128)(2,1)S(1)}, bf16[256,512]{1,0:T(8,128)(2,1)S(1)}) custom-call(s32[1]{0:T(128)} %bitcast.21.at_ref, bf16[384,4096]{1,0:T(8,128)(2,1)} %own_ref.9, bf16[384,4096]{1,0:T(8,128)(2,1)} %collective-permute-done.5.sib_ref, f32[768,512]{1,0:T(8,128)S(1)} %project_last.1.refs_0_, f32[768,512]{1,0:T(8,128)S(1)} %collective-permute-done.16.refs_1_), custom_call_target="tpu_custom_call" | custom-call | flops 6039797760 | bytes 27525120 | tf_op jit(solution)/shard_map/outer/pallas_call | solution.py:66
  58.2 1.5 %collective-permute-start.17 = (bf16[256,512]{1,0:T(8,128)(2,1)S(1)}, bf16[256,512]{1,0:T(8,128)(2,1)S(1)}, u32[]{:S(2)}, u32[]{:S(2)}) collective-permute-start(bf16[256,512]{1,0:T(8,128)(2,1)S(1)} %get-tuple-element.58), channel_id=1, source_target_pairs={{0,2},{1,3},{2,0},{3,1},{4,6},{5,7},{6,4},{7,5},{8,10},{9,11},{10,... | collective-permute-start | bytes 786440 | tf_op jit(solution)/shard_map/ppermute | solution.py:265
  59.7 3.3 %outer.4 = (bf16[256,512]{1,0:T(8,128)(2,1)S(1)}, bf16[256,512]{1,0:T(8,128)(2,1)S(1)}, bf16[256,512]{1,0:T(8,128)(2,1)S(1)}, f32[256,512]{1,0:T(8,128)S(1)}) custom-call(s32[4]{0:T(128)S(1)} %pad_add_fusion.1.at_ref, bf16[384,4096]{1,0:T(8,128)(2,1)} %own_ref.9, bf16[384,4096]{1,0:T(8,128)(2,1)} %collective-permute-done.5.sib_ref, ...), custom_call_target="tpu_custom_call" | custom-call | flops 24159191040 | bytes 110100480 | tf_op jit(solution)/shard_map/outer/pallas_call | solution.py:66
  63.6 1.4 %collective-permute-start.21 = (bf16[256,512]{1,0:T(8,128)(2,1)S(1)}, bf16[256,512]{1,0:T(8,128)(2,1)S(1)}, u32[]{:S(2)}, u32[]{:S(2)}) collective-permute-start(bf16[256,512]{1,0:T(8,128)(2,1)S(1)} %get-tuple-element.68), channel_id=1, source_target_pairs={{0,2},{1,3},{2,0},{3,1},{4,6},{5,7},{6,4},{7,5},{8,10},{9,11},{10,... | collective-permute-start | bytes 786440 | tf_op jit(solution)/shard_map/ppermute | solution.py:265
  65.7 1.7 %collective-permute-done.17 = bf16[256,512]{1,0:T(8,128)(2,1)S(1)} collective-permute-done((bf16[256,512]{1,0:T(8,128)(2,1)S(1)}, bf16[256,512]{1,0:T(8,128)(2,1)S(1)}, u32[]{:S(2)}, u32[]{:S(2)}) %collective-permute-start.17) | collective-permute-done | bytes 262176 | tf_op jit(solution)/shard_map/ppermute | solution.py:265
  67.8 2.8 %outer.5 = (f32[256,512]{1,0:T(8,128)S(1)}, f32[256,512]{1,0:T(8,128)S(1)}, f32[256,512]{1,0:T(8,128)S(1)}) custom-call(s32[3]{0:T(128)S(1)} %pad_add_fusion.at_ref, bf16[384,4096]{1,0:T(8,128)(2,1)} %own_ref.9, bf16[384,4096]{1,0:T(8,128)(2,1)} %collective-permute-done.5.sib_ref, bf16[768,512]{1,0:T(8,128)(2,1)S(1)} %get-tuple-element.60.refs_0_), custom_call_target="tpu_custom_call" | custom-call | flops 18119393280 | bytes 82575360 | tf_op jit(solution)/shard_map/outer/pallas_call | solution.py:66
  70.7 2.3 %collective-permute-done.19 = bf16[256,512]{1,0:T(8,128)(2,1)S(1)} collective-permute-done((bf16[256,512]{1,0:T(8,128)(2,1)S(1)}, bf16[256,512]{1,0:T(8,128)(2,1)S(1)}, u32[]{:S(2)}, u32[]{:S(2)}) %collective-permute-start.19) | collective-permute-done | bytes 262176 | tf_op jit(solution)/shard_map/ppermute | solution.py:265
  73.0 2.2 %collective-permute-start.20 = (bf16[256,512]{1,0:T(8,128)(2,1)S(1)}, bf16[256,512]{1,0:T(8,128)(2,1)S(1)}, u32[]{:S(2)}, u32[]{:S(2)}) collective-permute-start(bf16[256,512]{1,0:T(8,128)(2,1)S(1)} %add_convert_fusion.1), channel_id=1, source_target_pairs={{0,12},{1,13},{2,14},{3,15},{4,0},{5,1},{6,2},{7,3},{8,4},{9,5},{1... | collective-permute-start | bytes 786440 | tf_op jit(solution)/shard_map/ppermute | solution.py:268
  75.2 3.4 %collective-permute-done.21 = bf16[256,512]{1,0:T(8,128)(2,1)S(1)} collective-permute-done((bf16[256,512]{1,0:T(8,128)(2,1)S(1)}, bf16[256,512]{1,0:T(8,128)(2,1)S(1)}, u32[]{:S(2)}, u32[]{:S(2)}) %collective-permute-start.21) | collective-permute-done | bytes 262176 | tf_op jit(solution)/shard_map/ppermute | solution.py:265
  79.1 4.5 %collective-permute-done.18 = bf16[256,512]{1,0:T(8,128)(2,1)S(1)} collective-permute-done((bf16[256,512]{1,0:T(8,128)(2,1)S(1)}, bf16[256,512]{1,0:T(8,128)(2,1)S(1)}, u32[]{:S(2)}, u32[]{:S(2)}) %collective-permute-start.18) | collective-permute-done | bytes 262176 | tf_op jit(solution)/shard_map/ppermute | solution.py:265
  83.6 4.0 %collective-permute-done.23 = bf16[256,512]{1,0:T(8,128)(2,1)S(1)} collective-permute-done((bf16[256,512]{1,0:T(8,128)(2,1)S(1)}, bf16[256,512]{1,0:T(8,128)(2,1)S(1)}, u32[]{:S(2)}, u32[]{:S(2)}) %collective-permute-start.23) | collective-permute-done | bytes 262176 | tf_op jit(solution)/shard_map/ppermute | solution.py:268
  87.6 1.4 %divide_convert_fusion = (bf16[256,512]{1,0:T(8,128)(2,1)S(1)}, f32[256,512]{1,0:T(8,128)}, f32[256,512]{1,0:T(8,128)}) fusion(bf16[256,512]{1,0:T(8,128)(2,1)S(1)} %collective-permute-done.23, bf16[256,512]{1,0:T(8,128)(2,1)S(1)} %collective-permute-done.20, f32[256,512]{1,0:T(8,128)S(1)} %get-tuple-element.63, ...), kind=kLoop, calls=%fused_computation.2 | loop fusion | flops 2359296 | bytes 3670016 | tf_op jit(solution)/shard_map/convert_element_type | solution.py:26
  89.1 1.3 %collective-permute-start.27 = (bf16[256,256]{1,0:T(8,128)(2,1)S(1)}, bf16[256,256]{1,0:T(8,128)(2,1)S(1)}, u32[]{:S(2)}, u32[]{:S(2)}) collective-permute-start(bf16[256,256]{1,0:T(8,128)(2,1)S(1)} %get-tuple-element.90), channel_id=1, source_target_pairs={{0,2},{1,3},{2,0},{3,1},{4,6},{5,7},{6,4},{7,5},{8,10},{9,11},{10,... | collective-permute-start | bytes 393224 | tf_op jit(solution)/shard_map/ppermute | solution.py:265
  90.4 1.5 %collective-permute-start.24 = (bf16[256,256]{1,0:T(8,128)(2,1)S(1)}, bf16[256,256]{1,0:T(8,128)(2,1)S(1)}, u32[]{:S(2)}, u32[]{:S(2)}) collective-permute-start(bf16[256,256]{1,0:T(8,128)(2,1)S(1)} %get-tuple-element.91), channel_id=1, source_target_pairs={{0,4},{1,5},{2,6},{3,7},{4,8},{5,9},{6,10},{7,11},{8,12},{9,13},{1... | collective-permute-start | bytes 393224 | tf_op jit(solution)/shard_map/ppermute | solution.py:268
  92.6 3.3 %collective-permute-done.26 = bf16[256,256]{1,0:T(8,128)(2,1)S(1)} collective-permute-done((bf16[256,256]{1,0:T(8,128)(2,1)S(1)}, bf16[256,256]{1,0:T(8,128)(2,1)S(1)}, u32[]{:S(2)}, u32[]{:S(2)}) %collective-permute-start.26) | collective-permute-done | bytes 131104 | tf_op jit(solution)/shard_map/ppermute | solution.py:268
  95.9 0.9 collective-permute-start.30
  96.8 0.9 collective-permute-start.31
  98.0 1.7 %collective-permute-start.28 = (bf16[256,256]{1,0:T(8,128)(2,1)S(1)}, bf16[256,256]{1,0:T(8,128)(2,1)S(1)}, u32[]{:S(2)}, u32[]{:S(2)}) collective-permute-start(bf16[256,256]{1,0:T(8,128)(2,1)S(1)} %collective-permute-done.24), channel_id=1, source_target_pairs={{0,4},{1,5},{2,6},{3,7},{4,8},{5,9},{6,10},{7,11},{8,12},{9,13},{1... | collective-permute-start | bytes 393224 | tf_op jit(solution)/shard_map/ppermute | solution.py:268
  99.9 3.0 %collective-permute-done.30 = bf16[256,256]{1,0:T(8,128)(2,1)S(1)} collective-permute-done((bf16[256,256]{1,0:T(8,128)(2,1)S(1)}, bf16[256,256]{1,0:T(8,128)(2,1)S(1)}, u32[]{:S(2)}, u32[]{:S(2)}) %collective-permute-start.30) | collective-permute-done | bytes 131104 | tf_op jit(solution)/shard_map/ppermute | solution.py:268
  102.9 1.0 collective-permute-start.40
  104.8 2.3 %collective-permute-start.37 = (bf16[256,256]{1,0:T(8,128)(2,1)S(1)}, bf16[256,256]{1,0:T(8,128)(2,1)S(1)}, u32[]{:S(2)}, u32[]{:S(2)}) collective-permute-start(bf16[256,256]{1,0:T(8,128)(2,1)S(1)} %collective-permute-done.28), channel_id=1, source_target_pairs={{0,4},{1,5},{2,6},{3,7},{4,8},{5,9},{6,10},{7,11},{8,12},{9,13},{1... | collective-permute-start | bytes 393224 | tf_op jit(solution)/shard_map/ppermute | solution.py:268
  107.2 3.8 %collective-permute-done.39 = bf16[256,256]{1,0:T(8,128)(2,1)S(1)} collective-permute-done((bf16[256,256]{1,0:T(8,128)(2,1)S(1)}, bf16[256,256]{1,0:T(8,128)(2,1)S(1)}, u32[]{:S(2)}, u32[]{:S(2)}) %collective-permute-start.39) | collective-permute-done | bytes 131104 | tf_op jit(solution)/shard_map/ppermute | solution.py:268
  113.6 1.2 %collective-permute-start.42 = (bf16[256,256]{1,0:T(8,128)(2,1)S(1)}, bf16[256,256]{1,0:T(8,128)(2,1)S(1)}, u32[]{:S(2)}, u32[]{:S(2)}) collective-permute-start(bf16[256,256]{1,0:T(8,128)(2,1)S(1)} %collective-permute-done.27), channel_id=1, source_target_pairs={{0,12},{1,13},{2,14},{3,15},{4,0},{5,1},{6,2},{7,3},{8,4},{9,5},{1... | collective-permute-start | bytes 393224 | tf_op jit(solution)/shard_map/ppermute | solution.py:268
  115.3 3.0 %back.2.refs_0_ = bf16[4096,512]{1,0:T(8,128)(2,1)} custom-call(s32[10]{0:T(128)S(1)} %stack.107.at_ref, bf16[512,512]{1,0:T(8,128)(2,1)S(1)} %copy-done, bf16[256,512]{1,0:T(8,128)(2,1)S(1)} %get-tuple-element.77.refs_1_, bf16[512,256]{1,0:T(8,128)(2,1)S(1)} %constant_dynamic-update-slice_fusion.refs_2_, ...), custom_call_target="tpu_custom_call" | custom-call | flops 40265318400 | bytes 157286400 | tf_op jit(solution)/shard_map/back/pallas_call | solution.py:66
  120.2 2.4 %back.3 = bf16[4096,512]{1,0:T(8,128)(2,1)} custom-call(s32[6]{0:T(128)S(1)} %stack.96.at_ref, bf16[4096,512]{1,0:T(8,128)(2,1)} %back.2.refs_0_, bf16[512,512]{1,0:T(8,128)(2,1)S(1)} %copy-done, bf16[512,256]{1,0:T(8,128)(2,1)S(1)} %constant_dynamic-update-slice_fusion.8.refs_2_, ...), custom_call_target="tpu_custom_call", output_to_operand_aliasing={{}: (1, {})} | custom-call | flops 24159191040000 | bytes 94371840000 | tf_op jit(solution)/shard_map/back/pallas_call | solution.py:66
  (82 shorter events, 11.3 us)
Async XLA Ops:
  0.6 44.8 %collective-permute-start = (bf16[384,8192]{1,0:T(8,128)(2,1)}, bf16[384,8192]{1,0:T(8,128)(2,1)}, u32[]{:S(2)}, u32[]{:S(2)}) collective-permute-start(bf16[384,8192]{1,0:T(8,128)(2,1)} %own_ref.6), channel_id=1, source_target_pairs={{0,1},{1,0},{2,3},{3,2},{4,5},{5,4},{6,7},{7,6},{8,9},{9,8},{10,11... | collective-permute-start | bytes 18874376 | tf_op jit(solution)/shard_map/ppermute | solution.py:262
  2.2 11.8 %collective-permute-start.1 = (bf16[512,256]{1,0:T(8,128)(2,1)S(1)}, bf16[512,256]{1,0:T(8,128)(2,1)S(1)}, u32[]{:S(2)}, u32[]{:S(2)}) collective-permute-start(bf16[512,256]{1,0:T(8,128)(2,1)S(1)} %get-tuple-element.89.refs_0_), channel_id=1, source_target_pairs={{0,4},{1,5},{2,6},{3,7},{4,8},{5,9},{6,10},{7,11},{8,12},{9,13},{1... | collective-permute-start | bytes 786440 | tf_op jit(solution)/shard_map/ppermute | solution.py:268
  4.9 9.2 %collective-permute-start.2 = (bf16[512,256]{1,0:T(8,128)(2,1)S(1)}, bf16[512,256]{1,0:T(8,128)(2,1)S(1)}, u32[]{:S(2)}, u32[]{:S(2)}) collective-permute-start(bf16[512,256]{1,0:T(8,128)(2,1)S(1)} %get-tuple-element.89.refs_0_), channel_id=1, source_target_pairs={{0,2},{1,3},{2,0},{3,1},{4,6},{5,7},{6,4},{7,5},{8,10},{9,11},{10,... | collective-permute-start | bytes 786440 | tf_op jit(solution)/shard_map/ppermute | solution.py:265
  6.4 13.2 %collective-permute-start.10 = (bf16[512,256]{1,0:T(8,128)(2,1)S(1)}, bf16[512,256]{1,0:T(8,128)(2,1)S(1)}, u32[]{:S(2)}, u32[]{:S(2)}) collective-permute-start(bf16[512,256]{1,0:T(8,128)(2,1)S(1)} %get-tuple-element.88.refs_7_), channel_id=1, source_target_pairs={{0,2},{1,3},{2,0},{3,1},{4,6},{5,7},{6,4},{7,5},{8,10},{9,11},{10,... | collective-permute-start | bytes 786440 | tf_op jit(solution)/shard_map/ppermute | solution.py:265
  6.9 12.8 %collective-permute-start.9 = (bf16[512,256]{1,0:T(8,128)(2,1)S(1)}, bf16[512,256]{1,0:T(8,128)(2,1)S(1)}, u32[]{:S(2)}, u32[]{:S(2)}) collective-permute-start(bf16[512,256]{1,0:T(8,128)(2,1)S(1)} %get-tuple-element.88.refs_7_), channel_id=1, source_target_pairs={{0,4},{1,5},{2,6},{3,7},{4,8},{5,9},{6,10},{7,11},{8,12},{9,13},{1... | collective-permute-start | bytes 786440 | tf_op jit(solution)/shard_map/ppermute | solution.py:268
  14.0 11.2 %collective-permute-start.3 = (bf16[512,256]{1,0:T(8,128)(2,1)S(1)}, bf16[512,256]{1,0:T(8,128)(2,1)S(1)}, u32[]{:S(2)}, u32[]{:S(2)}) collective-permute-start(bf16[512,256]{1,0:T(8,128)(2,1)S(1)} %collective-permute-done.1.refs_2_), channel_id=1, source_target_pairs={{0,4},{1,5},{2,6},{3,7},{4,8},{5,9},{6,10},{7,11},{8,12},{9,13},{1... | collective-permute-start | bytes 786440 | tf_op jit(solution)/shard_map/ppermute | solution.py:268
  15.6 9.7 %collective-permute-start.4 = (bf16[512,256]{1,0:T(8,128)(2,1)S(1)}, bf16[512,256]{1,0:T(8,128)(2,1)S(1)}, u32[]{:S(2)}, u32[]{:S(2)}) collective-permute-start(bf16[512,256]{1,0:T(8,128)(2,1)S(1)} %collective-permute-done.1.refs_2_), channel_id=1, source_target_pairs={{0,2},{1,3},{2,0},{3,1},{4,6},{5,7},{6,4},{7,5},{8,10},{9,11},{10,... | collective-permute-start | bytes 786440 | tf_op jit(solution)/shard_map/ppermute | solution.py:265
  19.7 11.2 %collective-permute-start.11 = (bf16[512,256]{1,0:T(8,128)(2,1)S(1)}, bf16[512,256]{1,0:T(8,128)(2,1)S(1)}, u32[]{:S(2)}, u32[]{:S(2)}) collective-permute-start(bf16[512,256]{1,0:T(8,128)(2,1)S(1)} %collective-permute-done.9.refs_9_), channel_id=1, source_target_pairs={{0,4},{1,5},{2,6},{3,7},{4,8},{5,9},{6,10},{7,11},{8,12},{9,13},{1... | collective-permute-start | bytes 786440 | tf_op jit(solution)/shard_map/ppermute | solution.py:268
  21.2 9.7 %collective-permute-start.12 = (bf16[512,256]{1,0:T(8,128)(2,1)S(1)}, bf16[512,256]{1,0:T(8,128)(2,1)S(1)}, u32[]{:S(2)}, u32[]{:S(2)}) collective-permute-start(bf16[512,256]{1,0:T(8,128)(2,1)S(1)} %collective-permute-done.9.refs_9_), channel_id=1, source_target_pairs={{0,2},{1,3},{2,0},{3,1},{4,6},{5,7},{6,4},{7,5},{8,10},{9,11},{10,... | collective-permute-start | bytes 786440 | tf_op jit(solution)/shard_map/ppermute | solution.py:265
  25.3 11.2 %collective-permute-start.6 = (bf16[512,256]{1,0:T(8,128)(2,1)S(1)}, bf16[512,256]{1,0:T(8,128)(2,1)S(1)}, u32[]{:S(2)}, u32[]{:S(2)}) collective-permute-start(bf16[512,256]{1,0:T(8,128)(2,1)S(1)} %collective-permute-done.3.refs_4_), channel_id=1, source_target_pairs={{0,4},{1,5},{2,6},{3,7},{4,8},{5,9},{6,10},{7,11},{8,12},{9,13},{1... | collective-permute-start | bytes 786440 | tf_op jit(solution)/shard_map/ppermute | solution.py:268
  26.8 9.7 %collective-permute-start.7 = (bf16[512,256]{1,0:T(8,128)(2,1)S(1)}, bf16[512,256]{1,0:T(8,128)(2,1)S(1)}, u32[]{:S(2)}, u32[]{:S(2)}) collective-permute-start(bf16[512,256]{1,0:T(8,128)(2,1)S(1)} %collective-permute-done.3.refs_4_), channel_id=1, source_target_pairs={{0,2},{1,3},{2,0},{3,1},{4,6},{5,7},{6,4},{7,5},{8,10},{9,11},{10,... | collective-permute-start | bytes 786440 | tf_op jit(solution)/shard_map/ppermute | solution.py:265
  30.9 11.0 %collective-permute-start.13 = (bf16[512,256]{1,0:T(8,128)(2,1)S(1)}, bf16[512,256]{1,0:T(8,128)(2,1)S(1)}, u32[]{:S(2)}, u32[]{:S(2)}) collective-permute-start(bf16[512,256]{1,0:T(8,128)(2,1)S(1)} %collective-permute-done.11.refs_11_), channel_id=1, source_target_pairs={{0,4},{1,5},{2,6},{3,7},{4,8},{5,9},{6,10},{7,11},{8,12},{9,13},{1... | collective-permute-start | bytes 786440 | tf_op jit(solution)/shard_map/ppermute | solution.py:268
  32.4 9.5 %collective-permute-start.14 = (bf16[512,256]{1,0:T(8,128)(2,1)S(1)}, bf16[512,256]{1,0:T(8,128)(2,1)}, u32[]{:S(2)}, u32[]{:S(2)}) collective-permute-start(bf16[512,256]{1,0:T(8,128)(2,1)S(1)} %collective-permute-done.11.refs_11_), channel_id=1, source_target_pairs={{0,2},{1,3},{2,0},{3,1},{4,6},{5,7},{6,4},{7,5},{8,10},{9,11},{10,... | collective-permute-start | bytes 786440 | tf_op jit(solution)/shard_map/ppermute | solution.py:265
  41.9 9.3 %collective-permute-start.15 = (bf16[512,256]{1,0:T(8,128)(2,1)S(1)}, bf16[512,256]{1,0:T(8,128)(2,1)S(1)}, u32[]{:S(2)}, u32[]{:S(2)}) collective-permute-start(bf16[512,256]{1,0:T(8,128)(2,1)S(1)} %collective-permute-done.10.refs_8_), channel_id=1, source_target_pairs={{0,12},{1,13},{2,14},{3,15},{4,0},{5,1},{6,2},{7,3},{8,4},{9,5},{1... | collective-permute-start | bytes 786440 | tf_op jit(solution)/shard_map/ppermute | solution.py:268
  43.9 7.6 %collective-permute-start.8 = (bf16[512,256]{1,0:T(8,128)(2,1)S(1)}, bf16[512,256]{1,0:T(8,128)(2,1)S(1)}, u32[]{:S(2)}, u32[]{:S(2)}) collective-permute-start(bf16[512,256]{1,0:T(8,128)(2,1)S(1)} %collective-permute-done.6.refs_6_), channel_id=1, source_target_pairs={{0,2},{1,3},{2,0},{3,1},{4,6},{5,7},{6,4},{7,5},{8,10},{9,11},{10,... | collective-permute-start | bytes 786440 | tf_op jit(solution)/shard_map/ppermute | solution.py:265
  45.4 11.3 %collective-permute-start.5 = (bf16[384,4096]{1,0:T(8,128)(2,1)}, bf16[384,4096]{1,0:T(8,128)(2,1)}, u32[]{:S(2)}, u32[]{:S(2)}) collective-permute-start(bf16[384,4096]{1,0:T(8,128)(2,1)} %own_ref.9), channel_id=1, source_target_pairs={{0,1},{1,0},{2,3},{3,2},{4,5},{5,4},{6,7},{7,6},{8,9},{9,8},{10,11... | collective-permute-start | bytes 9437192 | tf_op jit(solution)/shard_map/ppermute | solution.py:262
  53.2 3.5 %collective-permute-start.16 = (f32[768,512]{1,0:T(8,128)S(1)}, f32[768,512]{1,0:T(8,128)S(1)}, u32[]{:S(2)}, u32[]{:S(2)}) collective-permute-start(f32[768,512]{1,0:T(8,128)S(1)} %project_last.1.refs_0_), channel_id=1, source_target_pairs={{0,1},{1,0},{2,3},{3,2},{4,5},{5,4},{6,7},{7,6},{8,9},{9,8},{10,11... | collective-permute-start | bytes 4718600 | tf_op jit(solution)/shard_map/ppermute | solution.py:262
  58.2 9.2 %collective-permute-start.17 = (bf16[256,512]{1,0:T(8,128)(2,1)S(1)}, bf16[256,512]{1,0:T(8,128)(2,1)S(1)}, u32[]{:S(2)}, u32[]{:S(2)}) collective-permute-start(bf16[256,512]{1,0:T(8,128)(2,1)S(1)} %get-tuple-element.58), channel_id=1, source_target_pairs={{0,2},{1,3},{2,0},{3,1},{4,6},{5,7},{6,4},{7,5},{8,10},{9,11},{10,... | collective-permute-start | bytes 786440 | tf_op jit(solution)/shard_map/ppermute | solution.py:265
  63.0 10.0 %collective-permute-start.19 = (bf16[256,512]{1,0:T(8,128)(2,1)S(1)}, bf16[256,512]{1,0:T(8,128)(2,1)S(1)}, u32[]{:S(2)}, u32[]{:S(2)}) collective-permute-start(bf16[256,512]{1,0:T(8,128)(2,1)S(1)} %get-tuple-element.66), channel_id=1, source_target_pairs={{0,2},{1,3},{2,0},{3,1},{4,6},{5,7},{6,4},{7,5},{8,10},{9,11},{10,... | collective-permute-start | bytes 786440 | tf_op jit(solution)/shard_map/ppermute | solution.py:265
  63.6 15.0 %collective-permute-start.21 = (bf16[256,512]{1,0:T(8,128)(2,1)S(1)}, bf16[256,512]{1,0:T(8,128)(2,1)S(1)}, u32[]{:S(2)}, u32[]{:S(2)}) collective-permute-start(bf16[256,512]{1,0:T(8,128)(2,1)S(1)} %get-tuple-element.68), channel_id=1, source_target_pairs={{0,2},{1,3},{2,0},{3,1},{4,6},{5,7},{6,4},{7,5},{8,10},{9,11},{10,... | collective-permute-start | bytes 786440 | tf_op jit(solution)/shard_map/ppermute | solution.py:265
  65.1 18.5 %collective-permute-start.18 = (bf16[256,512]{1,0:T(8,128)(2,1)S(1)}, bf16[256,512]{1,0:T(8,128)(2,1)S(1)}, u32[]{:S(2)}, u32[]{:S(2)}) collective-permute-start(bf16[256,512]{1,0:T(8,128)(2,1)S(1)} %get-tuple-element.64), channel_id=1, source_target_pairs={{0,2},{1,3},{2,0},{3,1},{4,6},{5,7},{6,4},{7,5},{8,10},{9,11},{10,... | collective-permute-start | bytes 786440 | tf_op jit(solution)/shard_map/ppermute | solution.py:265
  67.5 11.1 %collective-permute-start.22 = (bf16[256,512]{1,0:T(8,128)(2,1)S(1)}, bf16[256,512]{1,0:T(8,128)(2,1)S(1)}, u32[]{:S(2)}, u32[]{:S(2)}) collective-permute-start(bf16[256,512]{1,0:T(8,128)(2,1)S(1)} %convert_add_fusion.1), channel_id=1, source_target_pairs={{0,4},{1,5},{2,6},{3,7},{4,8},{5,9},{6,10},{7,11},{8,12},{9,13},{1... | collective-permute-start | bytes 786440 | tf_op jit(solution)/shard_map/ppermute | solution.py:268
  73.0 10.5 %collective-permute-start.20 = (bf16[256,512]{1,0:T(8,128)(2,1)S(1)}, bf16[256,512]{1,0:T(8,128)(2,1)S(1)}, u32[]{:S(2)}, u32[]{:S(2)}) collective-permute-start(bf16[256,512]{1,0:T(8,128)(2,1)S(1)} %add_convert_fusion.1), channel_id=1, source_target_pairs={{0,12},{1,13},{2,14},{3,15},{4,0},{5,1},{6,2},{7,3},{8,4},{9,5},{1... | collective-permute-start | bytes 786440 | tf_op jit(solution)/shard_map/ppermute | solution.py:268
  78.7 8.9 %collective-permute-start.23 = (bf16[256,512]{1,0:T(8,128)(2,1)S(1)}, bf16[256,512]{1,0:T(8,128)(2,1)S(1)}, u32[]{:S(2)}, u32[]{:S(2)}) collective-permute-start(bf16[256,512]{1,0:T(8,128)(2,1)S(1)} %add_convert_fusion), channel_id=1, source_target_pairs={{0,4},{1,5},{2,6},{3,7},{4,8},{5,9},{6,10},{7,11},{8,12},{9,13},{1... | collective-permute-start | bytes 786440 | tf_op jit(solution)/shard_map/ppermute | solution.py:268
  87.6 27.7 %copy-start = (bf16[512,512]{1,0:T(8,128)(2,1)S(1)}, bf16[512,512]{1,0:T(8,128)(2,1)}, u32[]{:S(2)}) copy-start(bf16[512,512]{1,0:T(8,128)(2,1)} %refs_1_.1) | copy-start | bytes 1572868
  89.0 6.8 %collective-permute-start.26 = (bf16[256,256]{1,0:T(8,128)(2,1)S(1)}, bf16[256,256]{1,0:T(8,128)(2,1)S(1)}, u32[]{:S(2)}, u32[]{:S(2)}) collective-permute-start(bf16[256,256]{1,0:T(8,128)(2,1)S(1)} %get-tuple-element.90), channel_id=1, source_target_pairs={{0,4},{1,5},{2,6},{3,7},{4,8},{5,9},{6,10},{7,11},{8,12},{9,13},{1... | collective-permute-start | bytes 393224 | tf_op jit(solution)/shard_map/ppermute | solution.py:268
  89.1 6.8 %collective-permute-start.27 = (bf16[256,256]{1,0:T(8,128)(2,1)S(1)}, bf16[256,256]{1,0:T(8,128)(2,1)S(1)}, u32[]{:S(2)}, u32[]{:S(2)}) collective-permute-start(bf16[256,256]{1,0:T(8,128)(2,1)S(1)} %get-tuple-element.90), channel_id=1, source_target_pairs={{0,2},{1,3},{2,0},{3,1},{4,6},{5,7},{6,4},{7,5},{8,10},{9,11},{10,... | collective-permute-start | bytes 393224 | tf_op jit(solution)/shard_map/ppermute | solution.py:265
  90.4 7.2 %collective-permute-start.24 = (bf16[256,256]{1,0:T(8,128)(2,1)S(1)}, bf16[256,256]{1,0:T(8,128)(2,1)S(1)}, u32[]{:S(2)}, u32[]{:S(2)}) collective-permute-start(bf16[256,256]{1,0:T(8,128)(2,1)S(1)} %get-tuple-element.91), channel_id=1, source_target_pairs={{0,4},{1,5},{2,6},{3,7},{4,8},{5,9},{6,10},{7,11},{8,12},{9,13},{1... | collective-permute-start | bytes 393224 | tf_op jit(solution)/shard_map/ppermute | solution.py:268
  91.9 6.1 %collective-permute-start.25 = (bf16[256,256]{1,0:T(8,128)(2,1)S(1)}, bf16[256,256]{1,0:T(8,128)(2,1)S(1)}, u32[]{:S(2)}, u32[]{:S(2)}) collective-permute-start(bf16[256,256]{1,0:T(8,128)(2,1)S(1)} %get-tuple-element.91), channel_id=1, source_target_pairs={{0,2},{1,3},{2,0},{3,1},{4,6},{5,7},{6,4},{7,5},{8,10},{9,11},{10,... | collective-permute-start | bytes 393224 | tf_op jit(solution)/shard_map/ppermute | solution.py:265
  95.9 7.0 %collective-permute-start.30 = (bf16[256,256]{1,0:T(8,128)(2,1)S(1)}, bf16[256,256]{1,0:T(8,128)(2,1)S(1)}, u32[]{:S(2)}, u32[]{:S(2)}) collective-permute-start(bf16[256,256]{1,0:T(8,128)(2,1)S(1)} %collective-permute-done.26), channel_id=1, source_target_pairs={{0,4},{1,5},{2,6},{3,7},{4,8},{5,9},{6,10},{7,11},{8,12},{9,13},{1... | collective-permute-start | bytes 393224 | tf_op jit(solution)/shard_map/ppermute | solution.py:268
  96.8 6.1 %collective-permute-start.31 = (bf16[256,256]{1,0:T(8,128)(2,1)S(1)}, bf16[256,256]{1,0:T(8,128)(2,1)S(1)}, u32[]{:S(2)}, u32[]{:S(2)}) collective-permute-start(bf16[256,256]{1,0:T(8,128)(2,1)S(1)} %collective-permute-done.26), channel_id=1, source_target_pairs={{0,2},{1,3},{2,0},{3,1},{4,6},{5,7},{6,4},{7,5},{8,10},{9,11},{10,... | collective-permute-start | bytes 393224 | tf_op jit(solution)/shard_map/ppermute | solution.py:265
  98.0 6.8 %collective-permute-start.28 = (bf16[256,256]{1,0:T(8,128)(2,1)S(1)}, bf16[256,256]{1,0:T(8,128)(2,1)S(1)}, u32[]{:S(2)}, u32[]{:S(2)}) collective-permute-start(bf16[256,256]{1,0:T(8,128)(2,1)S(1)} %collective-permute-done.24), channel_id=1, source_target_pairs={{0,4},{1,5},{2,6},{3,7},{4,8},{5,9},{6,10},{7,11},{8,12},{9,13},{1... | collective-permute-start | bytes 393224 | tf_op jit(solution)/shard_map/ppermute | solution.py:268
  99.7 5.1 %collective-permute-start.29 = (bf16[256,256]{1,0:T(8,128)(2,1)S(1)}, bf16[256,256]{1,0:T(8,128)(2,1)S(1)}, u32[]{:S(2)}, u32[]{:S(2)}) collective-permute-start(bf16[256,256]{1,0:T(8,128)(2,1)S(1)} %collective-permute-done.24), channel_id=1, source_target_pairs={{0,2},{1,3},{2,0},{3,1},{4,6},{5,7},{6,4},{7,5},{8,10},{9,11},{10,... | collective-permute-start | bytes 393224 | tf_op jit(solution)/shard_map/ppermute | solution.py:265
  99.8 13.2 %collective-permute-start.32 = (bf16[256,512]{1,0:T(8,128)(2,1)S(1)}, bf16[256,512]{1,0:T(8,128)(2,1)S(1)}, u32[]{:S(2)}, u32[]{:S(2)}) collective-permute-start(bf16[256,512]{1,0:T(8,128)(2,1)S(1)} %get-tuple-element.77.refs_1_), channel_id=1, source_target_pairs={{0,1},{1,0},{2,3},{3,2},{4,5},{5,4},{6,7},{7,6},{8,9},{9,8},{10,11... | collective-permute-start | bytes 786440 | tf_op jit(solution)/shard_map/ppermute | solution.py:262
  102.9 8.1 %collective-permute-start.39 = (bf16[256,256]{1,0:T(8,128)(2,1)S(1)}, bf16[256,256]{1,0:T(8,128)(2,1)S(1)}, u32[]{:S(2)}, u32[]{:S(2)}) collective-permute-start(bf16[256,256]{1,0:T(8,128)(2,1)S(1)} %collective-permute-done.30), channel_id=1, source_target_pairs={{0,4},{1,5},{2,6},{3,7},{4,8},{5,9},{6,10},{7,11},{8,12},{9,13},{1... | collective-permute-start | bytes 393224 | tf_op jit(solution)/shard_map/ppermute | solution.py:268
  102.9 8.1 %collective-permute-start.40 = (bf16[256,256]{1,0:T(8,128)(2,1)S(1)}, bf16[256,256]{1,0:T(8,128)(2,1)S(1)}, u32[]{:S(2)}, u32[]{:S(2)}) collective-permute-start(bf16[256,256]{1,0:T(8,128)(2,1)S(1)} %collective-permute-done.30), channel_id=1, source_target_pairs={{0,2},{1,3},{2,0},{3,1},{4,6},{5,7},{6,4},{7,5},{8,10},{9,11},{10,... | collective-permute-start | bytes 393224 | tf_op jit(solution)/shard_map/ppermute | solution.py:265
  104.8 7.6 %collective-permute-start.37 = (bf16[256,256]{1,0:T(8,128)(2,1)S(1)}, bf16[256,256]{1,0:T(8,128)(2,1)S(1)}, u32[]{:S(2)}, u32[]{:S(2)}) collective-permute-start(bf16[256,256]{1,0:T(8,128)(2,1)S(1)} %collective-permute-done.28), channel_id=1, source_target_pairs={{0,4},{1,5},{2,6},{3,7},{4,8},{5,9},{6,10},{7,11},{8,12},{9,13},{1... | collective-permute-start | bytes 393224 | tf_op jit(solution)/shard_map/ppermute | solution.py:268
  107.2 5.2 %collective-permute-start.38 = (bf16[256,256]{1,0:T(8,128)(2,1)S(1)}, bf16[256,256]{1,0:T(8,128)(2,1)S(1)}, u32[]{:S(2)}, u32[]{:S(2)}) collective-permute-start(bf16[256,256]{1,0:T(8,128)(2,1)S(1)} %collective-permute-done.28), channel_id=1, source_target_pairs={{0,2},{1,3},{2,0},{3,1},{4,6},{5,7},{6,4},{7,5},{8,10},{9,11},{10,... | collective-permute-start | bytes 393224 | tf_op jit(solution)/shard_map/ppermute | solution.py:265
  111.0 2.6 %collective-permute-start.34 = (bf16[512,256]{1,0:T(8,128)(2,1)S(1)}, bf16[512,256]{1,0:T(8,128)(2,1)S(1)}, u32[]{:S(2)}, u32[]{:S(2)}) collective-permute-start(bf16[512,256]{1,0:T(8,128)(2,1)S(1)} %constant_dynamic-update-slice_fusion.2.refs_3_), channel_id=1, source_target_pairs={{0,1},{1,0},{2,3},{3,2},{4,5},{5,4},{6,7},{7,6},{8,9},{9,8},{10,11... | collective-permute-start | bytes 786440 | tf_op jit(solution)/shard_map/ppermute | solution.py:262
  111.0 3.8 %collective-permute-start.33 = (bf16[512,256]{1,0:T(8,128)(2,1)S(1)}, bf16[512,256]{1,0:T(8,128)(2,1)S(1)}, u32[]{:S(2)}, u32[]{:S(2)}) collective-permute-start(bf16[512,256]{1,0:T(8,128)(2,1)S(1)} %constant_dynamic-update-slice_fusion.refs_2_), channel_id=1, source_target_pairs={{0,1},{1,0},{2,3},{3,2},{4,5},{5,4},{6,7},{7,6},{8,9},{9,8},{10,11... | collective-permute-start | bytes 786440 | tf_op jit(solution)/shard_map/ppermute | solution.py:262
  112.4 2.4 %collective-permute-start.36 = (bf16[512,256]{1,0:T(8,128)(2,1)S(1)}, bf16[512,256]{1,0:T(8,128)(2,1)S(1)}, u32[]{:S(2)}, u32[]{:S(2)}) collective-permute-start(bf16[512,256]{1,0:T(8,128)(2,1)S(1)} %constant_dynamic-update-slice_fusion.6.refs_5_), channel_id=1, source_target_pairs={{0,1},{1,0},{2,3},{3,2},{4,5},{5,4},{6,7},{7,6},{8,9},{9,8},{10,11... | collective-permute-start | bytes 786440 | tf_op jit(solution)/shard_map/ppermute | solution.py:262
  112.4 2.9 %collective-permute-start.35 = (bf16[512,256]{1,0:T(8,128)(2,1)S(1)}, bf16[512,256]{1,0:T(8,128)(2,1)S(1)}, u32[]{:S(2)}, u32[]{:S(2)}) collective-permute-start(bf16[512,256]{1,0:T(8,128)(2,1)S(1)} %constant_dynamic-update-slice_fusion.4.refs_4_), channel_id=1, source_target_pairs={{0,1},{1,0},{2,3},{3,2},{4,5},{5,4},{6,7},{7,6},{8,9},{9,8},{10,11... | collective-permute-start | bytes 786440 | tf_op jit(solution)/shard_map/ppermute | solution.py:262
  113.0 5.7 %collective-permute-start.41 = (bf16[256,256]{1,0:T(8,128)(2,1)S(1)}, bf16[256,256]{1,0:T(8,128)(2,1)S(1)}, u32[]{:S(2)}, u32[]{:S(2)}) collective-permute-start(bf16[256,256]{1,0:T(8,128)(2,1)S(1)} %collective-permute-done.37), channel_id=1, source_target_pairs={{0,2},{1,3},{2,0},{3,1},{4,6},{5,7},{6,4},{7,5},{8,10},{9,11},{10,... | collective-permute-start | bytes 393224 | tf_op jit(solution)/shard_map/ppermute | solution.py:265
  113.6 5.1 %collective-permute-start.42 = (bf16[256,256]{1,0:T(8,128)(2,1)S(1)}, bf16[256,256]{1,0:T(8,128)(2,1)S(1)}, u32[]{:S(2)}, u32[]{:S(2)}) collective-permute-start(bf16[256,256]{1,0:T(8,128)(2,1)S(1)} %collective-permute-done.27), channel_id=1, source_target_pairs={{0,12},{1,13},{2,14},{3,15},{4,0},{5,1},{6,2},{7,3},{8,4},{9,5},{1... | collective-permute-start | bytes 393224 | tf_op jit(solution)/shard_map/ppermute | solution.py:268
  114.8 5.4 %collective-permute-start.44 = (bf16[512,256]{1,0:T(8,128)(2,1)S(1)}, bf16[512,256]{1,0:T(8,128)(2,1)S(1)}, u32[]{:S(2)}, u32[]{:S(2)}) collective-permute-start(bf16[512,256]{1,0:T(8,128)(2,1)S(1)} %constant_dynamic-update-slice_fusion.10.refs_3_), channel_id=1, source_target_pairs={{0,1},{1,0},{2,3},{3,2},{4,5},{5,4},{6,7},{7,6},{8,9},{9,8},{10,11... | collective-permute-start | bytes 786440 | tf_op jit(solution)/shard_map/ppermute | solution.py:262
  114.8 5.4 %collective-permute-start.43 = (bf16[512,256]{1,0:T(8,128)(2,1)S(1)}, bf16[512,256]{1,0:T(8,128)(2,1)S(1)}, u32[]{:S(2)}, u32[]{:S(2)}) collective-permute-start(bf16[512,256]{1,0:T(8,128)(2,1)S(1)} %constant_dynamic-update-slice_fusion.8.refs_2_), channel_id=1, source_target_pairs={{0,1},{1,0},{2,3},{3,2},{4,5},{5,4},{6,7},{7,6},{8,9},{9,8},{10,11... | collective-permute-start | bytes 786440 | tf_op jit(solution)/shard_map/ppermute | solution.py:262
  118.7 1.3 %collective-permute-start.46 = (bf16[256,256]{1,0:T(8,128)(2,1)S(1)}, bf16[256,256]{1,0:T(8,128)(2,1)S(1)}, u32[]{:S(2)}, u32[]{:S(2)}) collective-permute-start(bf16[256,256]{1,0:T(8,128)(2,1)S(1)} %collective-permute-done.42.refs_5_), channel_id=1, source_target_pairs={{0,1},{1,0},{2,3},{3,2},{4,5},{5,4},{6,7},{7,6},{8,9},{9,8},{10,11... | collective-permute-start | bytes 393224 | tf_op jit(solution)/shard_map/ppermute | solution.py:262
  118.7 1.5 %collective-permute-start.45 = (bf16[256,256]{1,0:T(8,128)(2,1)S(1)}, bf16[256,256]{1,0:T(8,128)(2,1)S(1)}, u32[]{:S(2)}, u32[]{:S(2)}) collective-permute-start(bf16[256,256]{1,0:T(8,128)(2,1)S(1)} %collective-permute-done.41.refs_4_), channel_id=1, source_target_pairs={{0,1},{1,0},{2,3},{3,2},{4,5},{5,4},{6,7},{7,6},{8,9},{9,8},{10,11... | collective-permute-start | bytes 393224 | tf_op jit(solution)/shard_map/ppermute | solution.py:262
  (2 other events, 40.3 us)

commit v12 on v11

--- a/solution.py
+++ b/solution.py
@@ -81,14 +81,14 @@
 
 
 def project(activations, sibling, at, blocks):
-    chunks, many = len(blocks), at.shape[0]
+    chunks, many = len(blocks), len(blocks[0])
     flat = [block for chunk in blocks for block in chunk]
     (depth, cols), rows = flat[0].shape, activations.shape[0]
     wide = chunks * cols
 
     def kernel(at_ref, own_ref, sib_ref, *refs):
-        block_refs, (out_ref, a, b, total, sems) = refs[: len(flat)], refs[len(flat) :]
-        started = [[] for _ in range(many)]
+        block_refs, (out_ref, next_ref, a, b, total, sems) = refs[: len(flat)], refs[len(flat) :]
+        started = [[] for _ in range(many + 1)]
 
         def start(j, source, target):
             n = sum(len(copies) for copies in started)
@@ -104,6 +104,9 @@
         for n, ref in enumerate(block_refs):
             i, j = n // many, n % many
             start(j, ref, b.at[pl.ds(j * depth, depth), pl.ds(i * cols, cols)])
+        columns = pl.ds(pl.multiple_of(at_ref[many] * depth, depth), depth)
+        start(many, own_ref.at[:, columns], next_ref.at[here, :])
+        start(many, sib_ref.at[:, columns], next_ref.at[there, :])
         cut = (many + 1) // 2
         for low, high in ((0, cut), (cut, many)):
             for copies in started[low:high]:
@@ -112,8 +115,10 @@
             deep = slice(low * depth, high * depth)
             term = jnp.dot(a[:, deep], b[deep, :], preferred_element_type=F32)
             total[...] = total[...] + term if low else term
-        back_copy = pltpu.make_async_copy(total, out_ref, sems.at[2 * many + len(flat)])
+        back_copy = pltpu.make_async_copy(total, out_ref, sems.at[2 * many + 2 + len(flat)])
         back_copy.start()
+        for copy in started[many]:
+            copy.wait()
         back_copy.wait()
 
     return call(
@@ -121,60 +126,94 @@
         at,
         [pinned(activations), pinned(sibling), *flat],
         [],
-        [(False, jax.ShapeDtypeStruct((2 * rows, wide), F32))],
+        [(False, jax.ShapeDtypeStruct((2 * rows, wide), F32)), (True, jax.ShapeDtypeStruct((2 * rows, depth), BF16))],
         [
             pltpu.VMEM((2 * rows, many * depth), BF16),
             pltpu.VMEM((many * depth, wide), BF16),
             pltpu.VMEM((2 * rows, wide), F32),
-            pltpu.SemaphoreType.DMA((2 * many + len(flat) + 1,)),
+            pltpu.SemaphoreType.DMA((2 * many + len(flat) + 3,)),
         ],
         weight=W_EARLY,
         flops=4 * rows * depth * len(flat) * cols,
         moved=4 * rows * depth * many + 2 * depth * len(flat) * cols + 8 * rows * wide,
         name="project",
-    )[0]
-
-
-def project_last(activations, sibling, at, blocks, before):
-    (depth, cols), rows = blocks[0].shape, activations.shape[0]
-
-    def kernel(at_ref, own_ref, sib_ref, *refs):
-        block_refs, (before_ref, out_ref, a, sems) = refs[: len(blocks)], refs[len(blocks) :]
+    )
+
+
+def project_last(columns, blocks, before):
+    (rows, depth), cols = columns.shape, blocks[0].shape[1]
+
+    def kernel(columns_ref, *refs):
+        block_refs, (before_ref, out_ref) = refs[: len(blocks)], refs[len(blocks) :]
+        for i, ref in enumerate(block_refs):
+            part = slice(i * cols, (i + 1) * cols)
+            out_ref[:, part] = before_ref[:, part] + jnp.dot(columns_ref[...], ref[...], preferred_element_type=F32)
+
+    vmem = pl.BlockSpec(memory_space=pltpu.VMEM)
+    return pl.pallas_call(
+        kernel,
+        in_specs=[vmem] * (len(blocks) + 2),
+        out_specs=vmem,
+        out_shape=jax.ShapeDtypeStruct(before.shape, F32),
+        compiler_params=params(),
+        cost_estimate=cost(W_LATE, 2 * rows * depth * len(blocks) * cols, 2 * rows * depth + 10 * rows * len(blocks) * cols),
+        name="project_last",
+    )(columns, *blocks, before)
+
+
+def turn(out_grads, sibling, at, width):
+    rows = out_grads.shape[0]
+
+    def kernel(at_ref, own_ref, sib_ref, out_ref, g, sems):
         core = lax.rem(lax.axis_index("dp"), 2)
-        columns = pl.ds(pl.multiple_of(at_ref[0] * depth, depth), depth)
+        columns = pl.ds(pl.multiple_of(at_ref[0] * width, width), width)
         copies = []
         for n, (c, ref) in enumerate(((core, own_ref), (1 - core, sib_ref))):
-            target = a.at[pl.ds(pl.multiple_of(c * rows, rows), rows), :]
+            target = g.at[pl.ds(pl.multiple_of(c * rows, rows), rows), :]
             copies.append(pltpu.make_async_copy(ref.at[:, columns], target, sems.at[n]))
             copies[-1].start()
         for copy in copies:
             copy.wait()
-        for i, ref in enumerate(block_refs):
-            part = slice(i * cols, (i + 1) * cols)
-            out_ref[:, part] = before_ref[:, part] + jnp.dot(a[...], ref[...], preferred_element_type=F32)
+        out_ref[...] = g[...].T
 
     return call(
         kernel,
         at,
-        [pinned(activations), pinned(sibling)],
-        [*blocks, before],
-        [(True, jax.ShapeDtypeStruct(before.shape, F32))],
-        [pltpu.VMEM((2 * rows, depth), BF16), pltpu.SemaphoreType.DMA((2,))],
-        weight=W_LATE,
-        flops=4 * rows * depth * len(blocks) * cols,
-        moved=4 * rows * depth + 2 * depth * len(blocks) * cols + 8 * rows * len(blocks) * cols,
-        name="project_last",
+        [pinned(out_grads), pinned(sibling)],
+        [],
+        [(True, jax.ShapeDtypeStruct((width, 2 * rows), BF16))],
+        [pltpu.VMEM((2 * rows, width), BF16), pltpu.SemaphoreType.DMA((2,))],
+        weight=W_OUTER,
+        flops=0,
+        moved=8 * rows * width,
+        name="turn",
     )[0]
 
 
+def outer_first(turned, mine, theirs):
+    (width, rows), cols = turned.shape, mine.shape[1]
+
+    def kernel(turned_ref, mine_ref, theirs_ref, projected_ref, out_ref):
+        projected_ref[...] = (mine_ref[...] + theirs_ref[...]).astype(BF16)
+        out_ref[...] = jnp.dot(turned_ref[...], projected_ref[...], preferred_element_type=F32).astype(BF16)
+
+    vmem = pl.BlockSpec(memory_space=pltpu.VMEM)
+    return pl.pallas_call(
+        kernel,
+        in_specs=[vmem] * 3,
+        out_specs=[vmem] * 2,
+        out_shape=[jax.ShapeDtypeStruct((rows, cols), BF16), jax.ShapeDtypeStruct((width, cols), BF16)],
+        compiler_params=params(),
+        cost_estimate=cost(W_OUTER, 2 * rows * width * cols, 10 * rows * cols),
+        name="outer_first",
+    )(turned, mine, theirs)
+
+
 def outer(out_grads, sibling, at, width, dtypes, projected):
-    given = projected if isinstance(projected, tuple) else (projected,)
-    rows, many, cols = out_grads.shape[0], at.shape[0], given[0].shape[1]
-    first = len(given) > 1
-
-    def kernel(at_ref, own_ref, sib_ref, *refs):
-        projected_ref, (g, sems) = refs[2 if first else 0], refs[-2:]
-        outs = refs[len(given) + first : -2]
+    rows, many, cols = out_grads.shape[0], at.shape[0], projected.shape[1]
+
+    def kernel(at_ref, own_ref, sib_ref, projected_ref, *refs):
+        outs, (g, sems) = refs[:-2], refs[-2:]
         copies = []
         core = lax.rem(lax.axis_index("dp"), 2)
         for j in range(many):
@@ -183,8 +222,6 @@
                 target = g.at[pl.ds(pl.multiple_of(c * rows, rows), rows), pl.ds(j * width, width)]
                 copies.append(pltpu.make_async_copy(ref.at[:, columns], target, sems.at[len(copies)]))
                 copies[-1].start()
-        if first:
-            projected_ref[...] = (refs[0][...] + refs[1][...]).astype(BF16)
         for j in range(many):
             copies[2 * j].wait()
             copies[2 * j + 1].wait()
@@ -195,8 +232,8 @@
         kernel,
         at,
         [pinned(out_grads), pinned(sibling)],
-        [*given],
-        [(True, jax.ShapeDtypeStruct((2 * rows, cols), BF16))] * first + [(True, jax.ShapeDtypeStruct((width, cols), dtype)) for dtype in dtypes],
+        [projected],
+        [(True, jax.ShapeDtypeStruct((width, cols), dtype)) for dtype in dtypes],
         [pltpu.VMEM((2 * rows, many * width), BF16), pltpu.SemaphoreType.DMA((2 * many,))],
         weight=W_OUTER,
         flops=4 * rows * width * many * cols,
@@ -305,10 +342,11 @@
     line, across = gather([projector[:, part] for part in parts])
     g_sibling = swap_core(after(out_grads, a_sibling, line[0][2]))
     block = lambda i, n: (across if n % 2 else line)[i][n // 2]
-    mine = project(activations, a_sibling, at_in[:last], [[block(i, n) for n in range(last)] for i in range(CHUNKS)])
-    mine = project_last(activations, a_sibling, at_in[last:], [block(i, last) for i in range(CHUNKS)], mine)
-
-    projected, send = outer(out_grads, g_sibling, at_out[:1], width, [BF16], (mine, swap_core(mine)))
+    mine, columns = project(activations, a_sibling, at_in, [[block(i, n) for n in range(last)] for i in range(CHUNKS)])
+    mine = project_last(columns, [block(i, last) for i in range(CHUNKS)], mine)
+
+    turned = turn(out_grads, g_sibling, at_out[:1], width)
+    projected, send = outer_first(turned, mine, swap_core(mine))
     at = after(at_out[1 : nz + 1], send)
     *sends, keep = outer(out_grads, g_sibling, at, width, [BF16] * (nz - 1) + [F32], projected)
     passed = keep + swap_y(send).astype(F32)

time: 123 us -> 120 us (0.976)
    ppermute x17, waiting for transfers between devices: 34.8 us -> 37.9 us  [shift_z(): return lax.ppermute(x, 'dp', pairs(lambda a, b, c: ((a + k) % nz, b, c)))]
    ppermute x18, waiting for transfers between devices: 15 us -> 12.5 us  [swap_y(): return lax.ppermute(x, 'dp', pairs(lambda a, b, c: (a, 1 - b, c)))]
    pallas_call x7 -> x6, Pallas kernels: 20.6 us -> 18.7 us  [call(): pl.pallas_call(kernel, grid_spec=pltpu.PrefetchScalarGridSpec(num_scalar_...]
    ppermute x12, waiting for transfers between devices: 3.94 us -> 2.68 us  [swap_core(): return lax.ppermute(x, 'dp', pairs(lambda a, b, c: (a, b, 1 - c)))]
where the time goes in v12:
time: 120 us
  waiting for transfers between devices  53.1 us (44%)
  starting transfers between devices  43.3 us (36%)
  Pallas kernels  19.6 us (16%)
  other arithmetic  1.8 us (2%)
  local copies, waits for them, and re-layouts  1.47 us (1%)
    ppermute x17, waiting for transfers between devices, shift_z(): return lax.ppermute(x, 'dp', pairs(lambda a, b, c: ((a + k) % nz, b, c)))  37.9 us
    ppermute x17, starting transfers between devices, shift_z(): return lax.ppermute(x, 'dp', pairs(lambda a, b, c: ((a + k) % nz, b, c)))  22.5 us
    pallas_call x6, Pallas kernels, call(): pl.pallas_call(kernel, grid_spec=pltpu.PrefetchScalarGridSpec(num_scalar_...  18.7 us
    ppermute x18, starting transfers between devices, swap_y(): return lax.ppermute(x, 'dp', pairs(lambda a, b, c: (a, 1 - b, c)))  17.8 us
    ppermute x18, waiting for transfers between devices, swap_y(): return lax.ppermute(x, 'dp', pairs(lambda a, b, c: (a, 1 - b, c)))  12.5 us
    ppermute x12, starting transfers between devices, swap_core(): return lax.ppermute(x, 'dp', pairs(lambda a, b, c: (a, b, 1 - c)))  3.02 us
    ppermute x12, waiting for transfers between devices, swap_core(): return lax.ppermute(x, 'dp', pairs(lambda a, b, c: (a, b, 1 - c)))  2.68 us
  transfers between devices with their start and end apart: 47, of which 22 were waited for; matrix products, arithmetic and copies ran while one was open for 2% of the time, Pallas kernels for 14%

profile of v12, /device:TPU:0, one launch (start us, length us, event | category | flops | bytes accessed | tf_op | source)
XLA Modules:
  0.0 120.3 jit_solution(2856948395519709400)
XLA Ops:
  1.1 1.1 fusion.2
  2.2 2.6 %collective-permute-start.1 = (bf16[512,256]{1,0:T(8,128)(2,1)S(1)}, bf16[512,256]{1,0:T(8,128)(2,1)S(1)}, u32[]{:S(2)}, u32[]{:S(2)}) collective-permute-start(bf16[512,256]{1,0:T(8,128)(2,1)S(1)} %get-tuple-element.93.refs_0_), channel_id=1, source_target_pairs={{0,4},{1,5},{2,6},{3,7},{4,8},{5,9},{6,10},{7,11},{8,12},{9,13},{1... | collective-permute-start | bytes 786440 | tf_op jit(solution)/shard_map/ppermute | solution.py:305
  4.9 1.5 %collective-permute-start.2 = (bf16[512,256]{1,0:T(8,128)(2,1)S(1)}, bf16[512,256]{1,0:T(8,128)(2,1)S(1)}, u32[]{:S(2)}, u32[]{:S(2)}) collective-permute-start(bf16[512,256]{1,0:T(8,128)(2,1)S(1)} %get-tuple-element.93.refs_0_), channel_id=1, source_target_pairs={{0,2},{1,3},{2,0},{3,1},{4,6},{5,7},{6,4},{7,5},{8,10},{9,11},{10,... | collective-permute-start | bytes 786440 | tf_op jit(solution)/shard_map/ppermute | solution.py:302
  6.4 1.6 %collective-permute-start.8 = (bf16[512,256]{1,0:T(8,128)(2,1)S(1)}, bf16[512,256]{1,0:T(8,128)(2,1)S(1)}, u32[]{:S(2)}, u32[]{:S(2)}) collective-permute-start(bf16[512,256]{1,0:T(8,128)(2,1)S(1)} %get-tuple-element.92.refs_7_), channel_id=1, source_target_pairs={{0,4},{1,5},{2,6},{3,7},{4,8},{5,9},{6,10},{7,11},{8,12},{9,13},{1... | collective-permute-start | bytes 786440 | tf_op jit(solution)/shard_map/ppermute | solution.py:305
  8.5 5.6 %collective-permute-done.1.refs_2_ = bf16[512,256]{1,0:T(8,128)(2,1)S(1)} collective-permute-done((bf16[512,256]{1,0:T(8,128)(2,1)S(1)}, bf16[512,256]{1,0:T(8,128)(2,1)S(1)}, u32[]{:S(2)}, u32[]{:S(2)}) %collective-permute-start.1) | collective-permute-done | bytes 262176 | tf_op jit(solution)/shard_map/ppermute | solution.py:305
  14.0 1.5 %collective-permute-start.3 = (bf16[512,256]{1,0:T(8,128)(2,1)S(1)}, bf16[512,256]{1,0:T(8,128)(2,1)S(1)}, u32[]{:S(2)}, u32[]{:S(2)}) collective-permute-start(bf16[512,256]{1,0:T(8,128)(2,1)S(1)} %collective-permute-done.1.refs_2_), channel_id=1, source_target_pairs={{0,4},{1,5},{2,6},{3,7},{4,8},{5,9},{6,10},{7,11},{8,12},{9,13},{1... | collective-permute-start | bytes 786440 | tf_op jit(solution)/shard_map/ppermute | solution.py:305
  15.6 1.5 %collective-permute-start.4 = (bf16[512,256]{1,0:T(8,128)(2,1)S(1)}, bf16[512,256]{1,0:T(8,128)(2,1)S(1)}, u32[]{:S(2)}, u32[]{:S(2)}) collective-permute-start(bf16[512,256]{1,0:T(8,128)(2,1)S(1)} %collective-permute-done.1.refs_2_), channel_id=1, source_target_pairs={{0,2},{1,3},{2,0},{3,1},{4,6},{5,7},{6,4},{7,5},{8,10},{9,11},{10,... | collective-permute-start | bytes 786440 | tf_op jit(solution)/shard_map/ppermute | solution.py:302
  17.1 2.6 %collective-permute-done.8.refs_9_ = bf16[512,256]{1,0:T(8,128)(2,1)S(1)} collective-permute-done((bf16[512,256]{1,0:T(8,128)(2,1)S(1)}, bf16[512,256]{1,0:T(8,128)(2,1)S(1)}, u32[]{:S(2)}, u32[]{:S(2)}) %collective-permute-start.8) | collective-permute-done | bytes 262176 | tf_op jit(solution)/shard_map/ppermute | solution.py:305
  19.7 1.5 %collective-permute-start.10 = (bf16[512,256]{1,0:T(8,128)(2,1)S(1)}, bf16[512,256]{1,0:T(8,128)(2,1)S(1)}, u32[]{:S(2)}, u32[]{:S(2)}) collective-permute-start(bf16[512,256]{1,0:T(8,128)(2,1)S(1)} %collective-permute-done.8.refs_9_), channel_id=1, source_target_pairs={{0,4},{1,5},{2,6},{3,7},{4,8},{5,9},{6,10},{7,11},{8,12},{9,13},{1... | collective-permute-start | bytes 786440 | tf_op jit(solution)/shard_map/ppermute | solution.py:305
  21.2 1.5 %collective-permute-start.11 = (bf16[512,256]{1,0:T(8,128)(2,1)S(1)}, bf16[512,256]{1,0:T(8,128)(2,1)S(1)}, u32[]{:S(2)}, u32[]{:S(2)}) collective-permute-start(bf16[512,256]{1,0:T(8,128)(2,1)S(1)} %collective-permute-done.8.refs_9_), channel_id=1, source_target_pairs={{0,2},{1,3},{2,0},{3,1},{4,6},{5,7},{6,4},{7,5},{8,10},{9,11},{10,... | collective-permute-start | bytes 786440 | tf_op jit(solution)/shard_map/ppermute | solution.py:302
  22.7 2.6 %collective-permute-done.3.refs_4_ = bf16[512,256]{1,0:T(8,128)(2,1)S(1)} collective-permute-done((bf16[512,256]{1,0:T(8,128)(2,1)S(1)}, bf16[512,256]{1,0:T(8,128)(2,1)S(1)}, u32[]{:S(2)}, u32[]{:S(2)}) %collective-permute-start.3) | collective-permute-done | bytes 262176 | tf_op jit(solution)/shard_map/ppermute | solution.py:305
  25.3 1.5 %collective-permute-start.6 = (bf16[512,256]{1,0:T(8,128)(2,1)S(1)}, bf16[512,256]{1,0:T(8,128)(2,1)S(1)}, u32[]{:S(2)}, u32[]{:S(2)}) collective-permute-start(bf16[512,256]{1,0:T(8,128)(2,1)S(1)} %collective-permute-done.3.refs_4_), channel_id=1, source_target_pairs={{0,4},{1,5},{2,6},{3,7},{4,8},{5,9},{6,10},{7,11},{8,12},{9,13},{1... | collective-permute-start | bytes 786440 | tf_op jit(solution)/shard_map/ppermute | solution.py:305
  26.8 1.5 %collective-permute-start.7 = (bf16[512,256]{1,0:T(8,128)(2,1)S(1)}, bf16[512,256]{1,0:T(8,128)(2,1)S(1)}, u32[]{:S(2)}, u32[]{:S(2)}) collective-permute-start(bf16[512,256]{1,0:T(8,128)(2,1)S(1)} %collective-permute-done.3.refs_4_), channel_id=1, source_target_pairs={{0,2},{1,3},{2,0},{3,1},{4,6},{5,7},{6,4},{7,5},{8,10},{9,11},{10,... | collective-permute-start | bytes 786440 | tf_op jit(solution)/shard_map/ppermute | solution.py:302
  28.3 2.6 %collective-permute-done.10.refs_11_ = bf16[512,256]{1,0:T(8,128)(2,1)S(1)} collective-permute-done((bf16[512,256]{1,0:T(8,128)(2,1)S(1)}, bf16[512,256]{1,0:T(8,128)(2,1)S(1)}, u32[]{:S(2)}, u32[]{:S(2)}) %collective-permute-start.10) | collective-permute-done | bytes 262176 | tf_op jit(solution)/shard_map/ppermute | solution.py:305
  30.9 1.5 %collective-permute-start.12 = (bf16[512,256]{1,0:T(8,128)(2,1)S(1)}, bf16[512,256]{1,0:T(8,128)(2,1)S(1)}, u32[]{:S(2)}, u32[]{:S(2)}) collective-permute-start(bf16[512,256]{1,0:T(8,128)(2,1)S(1)} %collective-permute-done.10.refs_11_), channel_id=1, source_target_pairs={{0,4},{1,5},{2,6},{3,7},{4,8},{5,9},{6,10},{7,11},{8,12},{9,13},{1... | collective-permute-start | bytes 786440 | tf_op jit(solution)/shard_map/ppermute | solution.py:305
  32.4 1.5 %collective-permute-start.13 = (bf16[512,256]{1,0:T(8,128)(2,1)S(1)}, bf16[512,256]{1,0:T(8,128)(2,1)}, u32[]{:S(2)}, u32[]{:S(2)}) collective-permute-start(bf16[512,256]{1,0:T(8,128)(2,1)S(1)} %collective-permute-done.10.refs_11_), channel_id=1, source_target_pairs={{0,2},{1,3},{2,0},{3,1},{4,6},{5,7},{6,4},{7,5},{8,10},{9,11},{10,... | collective-permute-start | bytes 786440 | tf_op jit(solution)/shard_map/ppermute | solution.py:302
  34.0 2.5 %collective-permute-done.6.refs_6_ = bf16[512,256]{1,0:T(8,128)(2,1)S(1)} collective-permute-done((bf16[512,256]{1,0:T(8,128)(2,1)S(1)}, bf16[512,256]{1,0:T(8,128)(2,1)S(1)}, u32[]{:S(2)}, u32[]{:S(2)}) %collective-permute-start.6) | collective-permute-done | bytes 262176 | tf_op jit(solution)/shard_map/ppermute | solution.py:305
  36.5 5.4 %collective-permute-done.12.refs_13_ = bf16[512,256]{1,0:T(8,128)(2,1)S(1)} collective-permute-done((bf16[512,256]{1,0:T(8,128)(2,1)S(1)}, bf16[512,256]{1,0:T(8,128)(2,1)S(1)}, u32[]{:S(2)}, u32[]{:S(2)}) %collective-permute-start.12) | collective-permute-done | bytes 262176 | tf_op jit(solution)/shard_map/ppermute | solution.py:305
  41.9 1.9 %collective-permute-start.15 = (bf16[512,256]{1,0:T(8,128)(2,1)S(1)}, bf16[512,256]{1,0:T(8,128)(2,1)S(1)}, u32[]{:S(2)}, u32[]{:S(2)}) collective-permute-start(bf16[512,256]{1,0:T(8,128)(2,1)S(1)} %collective-permute-done.9.refs_8_), channel_id=1, source_target_pairs={{0,12},{1,13},{2,14},{3,15},{4,0},{5,1},{6,2},{7,3},{8,4},{9,5},{1... | collective-permute-start | bytes 786440 | tf_op jit(solution)/shard_map/ppermute | solution.py:305
  43.9 1.5 %collective-permute-start.14 = (bf16[512,256]{1,0:T(8,128)(2,1)S(1)}, bf16[512,256]{1,0:T(8,128)(2,1)S(1)}, u32[]{:S(2)}, u32[]{:S(2)}) collective-permute-start(bf16[512,256]{1,0:T(8,128)(2,1)S(1)} %collective-permute-done.6.refs_6_), channel_id=1, source_target_pairs={{0,2},{1,3},{2,0},{3,1},{4,6},{5,7},{6,4},{7,5},{8,10},{9,11},{10,... | collective-permute-start | bytes 786440 | tf_op jit(solution)/shard_map/ppermute | solution.py:302
  45.4 5.9 %project.1 = (f32[768,512]{1,0:T(8,128)S(1)}, bf16[768,512]{1,0:T(8,128)(2,1)S(1)}) custom-call(s32[8]{0:T(128)S(1)} %stack.116.at_ref, bf16[384,8192]{1,0:T(8,128)(2,1)} %own_ref.5, bf16[384,8192]{1,0:T(8,128)(2,1)} %collective-permute-done.sib_ref, bf16[512,256]{1,0:T(8,128)(2,1)S(1)} %get-tuple-element.93.refs_0_, ...), custom_call_target="tpu_custom_call" | custom-call | flops 84557168640 | bytes 322437120 | tf_op jit(solution)/shard_map/project/pallas_call | solution.py:66
  52.6 1.2 turn.1.turned_ref
  53.8 1.7 %collective-permute-done.16.theirs_ref = f32[768,512]{1,0:T(8,128)S(1)} collective-permute-done((f32[768,512]{1,0:T(8,128)S(1)}, f32[768,512]{1,0:T(8,128)S(1)}, u32[]{:S(2)}, u32[]{:S(2)}) %collective-permute-start.16) | collective-permute-done | bytes 1572896 | tf_op jit(solution)/shard_map/ppermute | solution.py:299
  56.0 1.5 %collective-permute-start.17 = (bf16[256,512]{1,0:T(8,128)(2,1)S(1)}, bf16[256,512]{1,0:T(8,128)(2,1)S(1)}, u32[]{:S(2)}, u32[]{:S(2)}) collective-permute-start(bf16[256,512]{1,0:T(8,128)(2,1)S(1)} %get-tuple-element.62), channel_id=1, source_target_pairs={{0,2},{1,3},{2,0},{3,1},{4,6},{5,7},{6,4},{7,5},{8,10},{9,11},{10,... | collective-permute-start | bytes 786440 | tf_op jit(solution)/shard_map/ppermute | solution.py:302
  57.5 3.3 %outer.2 = (bf16[256,512]{1,0:T(8,128)(2,1)S(1)}, bf16[256,512]{1,0:T(8,128)(2,1)S(1)}, bf16[256,512]{1,0:T(8,128)(2,1)S(1)}, f32[256,512]{1,0:T(8,128)S(1)}) custom-call(s32[4]{0:T(128)S(1)} %pad_add_fusion.1.at_ref, bf16[384,4096]{1,0:T(8,128)(2,1)} %own_ref.7, bf16[384,4096]{1,0:T(8,128)(2,1)} %collective-permute-done.5.sib_ref, ...), custom_call_target="tpu_custom_call" | custom-call | flops 24159191040 | bytes 110100480 | tf_op jit(solution)/shard_map/outer/pallas_call | solution.py:66
  61.4 1.5 %collective-permute-start.21 = (bf16[256,512]{1,0:T(8,128)(2,1)S(1)}, bf16[256,512]{1,0:T(8,128)(2,1)S(1)}, u32[]{:S(2)}, u32[]{:S(2)}) collective-permute-start(bf16[256,512]{1,0:T(8,128)(2,1)S(1)} %get-tuple-element.72), channel_id=1, source_target_pairs={{0,2},{1,3},{2,0},{3,1},{4,6},{5,7},{6,4},{7,5},{8,10},{9,11},{10,... | collective-permute-start | bytes 786440 | tf_op jit(solution)/shard_map/ppermute | solution.py:302
  63.5 1.7 %collective-permute-done.17 = bf16[256,512]{1,0:T(8,128)(2,1)S(1)} collective-permute-done((bf16[256,512]{1,0:T(8,128)(2,1)S(1)}, bf16[256,512]{1,0:T(8,128)(2,1)S(1)}, u32[]{:S(2)}, u32[]{:S(2)}) %collective-permute-start.17) | collective-permute-done | bytes 262176 | tf_op jit(solution)/shard_map/ppermute | solution.py:302
  65.6 2.8 %outer.3 = (f32[256,512]{1,0:T(8,128)S(1)}, f32[256,512]{1,0:T(8,128)S(1)}, f32[256,512]{1,0:T(8,128)S(1)}) custom-call(s32[3]{0:T(128)S(1)} %pad_add_fusion.at_ref, bf16[384,4096]{1,0:T(8,128)(2,1)} %own_ref.7, bf16[384,4096]{1,0:T(8,128)(2,1)} %collective-permute-done.5.sib_ref, bf16[768,512]{1,0:T(8,128)(2,1)S(1)} %get-tuple-element.64.projected_ref), custom_call_target="tpu_custom_call" | custom-call | flops 18119393280 | bytes 82575360 | tf_op jit(solution)/shard_map/outer/pallas_call | solution.py:66
  68.5 2.3 %collective-permute-done.19 = bf16[256,512]{1,0:T(8,128)(2,1)S(1)} collective-permute-done((bf16[256,512]{1,0:T(8,128)(2,1)S(1)}, bf16[256,512]{1,0:T(8,128)(2,1)S(1)}, u32[]{:S(2)}, u32[]{:S(2)}) %collective-permute-start.19) | collective-permute-done | bytes 262176 | tf_op jit(solution)/shard_map/ppermute | solution.py:302
  70.8 2.2 %collective-permute-start.20 = (bf16[256,512]{1,0:T(8,128)(2,1)S(1)}, bf16[256,512]{1,0:T(8,128)(2,1)S(1)}, u32[]{:S(2)}, u32[]{:S(2)}) collective-permute-start(bf16[256,512]{1,0:T(8,128)(2,1)S(1)} %add_convert_fusion.1), channel_id=1, source_target_pairs={{0,12},{1,13},{2,14},{3,15},{4,0},{5,1},{6,2},{7,3},{8,4},{9,5},{1... | collective-permute-start | bytes 786440 | tf_op jit(solution)/shard_map/ppermute | solution.py:305
  73.0 3.4 %collective-permute-done.21 = bf16[256,512]{1,0:T(8,128)(2,1)S(1)} collective-permute-done((bf16[256,512]{1,0:T(8,128)(2,1)S(1)}, bf16[256,512]{1,0:T(8,128)(2,1)S(1)}, u32[]{:S(2)}, u32[]{:S(2)}) %collective-permute-start.21) | collective-permute-done | bytes 262176 | tf_op jit(solution)/shard_map/ppermute | solution.py:302
  76.9 4.5 %collective-permute-done.18 = bf16[256,512]{1,0:T(8,128)(2,1)S(1)} collective-permute-done((bf16[256,512]{1,0:T(8,128)(2,1)S(1)}, bf16[256,512]{1,0:T(8,128)(2,1)S(1)}, u32[]{:S(2)}, u32[]{:S(2)}) %collective-permute-start.18) | collective-permute-done | bytes 262176 | tf_op jit(solution)/shard_map/ppermute | solution.py:302
  81.4 4.1 %collective-permute-done.23 = bf16[256,512]{1,0:T(8,128)(2,1)S(1)} collective-permute-done((bf16[256,512]{1,0:T(8,128)(2,1)S(1)}, bf16[256,512]{1,0:T(8,128)(2,1)S(1)}, u32[]{:S(2)}, u32[]{:S(2)}) %collective-permute-start.23) | collective-permute-done | bytes 262176 | tf_op jit(solution)/shard_map/ppermute | solution.py:305
  85.5 1.4 %divide_convert_fusion = (bf16[256,512]{1,0:T(8,128)(2,1)S(1)}, f32[256,512]{1,0:T(8,128)}, f32[256,512]{1,0:T(8,128)}) fusion(bf16[256,512]{1,0:T(8,128)(2,1)S(1)} %collective-permute-done.23, bf16[256,512]{1,0:T(8,128)(2,1)S(1)} %collective-permute-done.20, f32[256,512]{1,0:T(8,128)S(1)} %get-tuple-element.67, ...), kind=kLoop, calls=%fused_computation.2 | loop fusion | flops 2359296 | bytes 3670016 | tf_op jit(solution)/shard_map/convert_element_type | solution.py:26
  87.0 1.2 %collective-permute-start.27 = (bf16[256,256]{1,0:T(8,128)(2,1)S(1)}, bf16[256,256]{1,0:T(8,128)(2,1)S(1)}, u32[]{:S(2)}, u32[]{:S(2)}) collective-permute-start(bf16[256,256]{1,0:T(8,128)(2,1)S(1)} %get-tuple-element.94), channel_id=1, source_target_pairs={{0,2},{1,3},{2,0},{3,1},{4,6},{5,7},{6,4},{7,5},{8,10},{9,11},{10,... | collective-permute-start | bytes 393224 | tf_op jit(solution)/shard_map/ppermute | solution.py:302
  88.3 1.5 %collective-permute-start.24 = (bf16[256,256]{1,0:T(8,128)(2,1)S(1)}, bf16[256,256]{1,0:T(8,128)(2,1)S(1)}, u32[]{:S(2)}, u32[]{:S(2)}) collective-permute-start(bf16[256,256]{1,0:T(8,128)(2,1)S(1)} %get-tuple-element.95), channel_id=1, source_target_pairs={{0,4},{1,5},{2,6},{3,7},{4,8},{5,9},{6,10},{7,11},{8,12},{9,13},{1... | collective-permute-start | bytes 393224 | tf_op jit(solution)/shard_map/ppermute | solution.py:305
  90.4 3.4 %collective-permute-done.26 = bf16[256,256]{1,0:T(8,128)(2,1)S(1)} collective-permute-done((bf16[256,256]{1,0:T(8,128)(2,1)S(1)}, bf16[256,256]{1,0:T(8,128)(2,1)S(1)}, u32[]{:S(2)}, u32[]{:S(2)}) %collective-permute-start.26) | collective-permute-done | bytes 131104 | tf_op jit(solution)/shard_map/ppermute | solution.py:305
  94.6 0.9 collective-permute-start.31
  95.9 1.6 %collective-permute-start.28 = (bf16[256,256]{1,0:T(8,128)(2,1)S(1)}, bf16[256,256]{1,0:T(8,128)(2,1)S(1)}, u32[]{:S(2)}, u32[]{:S(2)}) collective-permute-start(bf16[256,256]{1,0:T(8,128)(2,1)S(1)} %collective-permute-done.24), channel_id=1, source_target_pairs={{0,4},{1,5},{2,6},{3,7},{4,8},{5,9},{6,10},{7,11},{8,12},{9,13},{1... | collective-permute-start | bytes 393224 | tf_op jit(solution)/shard_map/ppermute | solution.py:305
  97.6 3.2 %collective-permute-done.30 = bf16[256,256]{1,0:T(8,128)(2,1)S(1)} collective-permute-done((bf16[256,256]{1,0:T(8,128)(2,1)S(1)}, bf16[256,256]{1,0:T(8,128)(2,1)S(1)}, u32[]{:S(2)}, u32[]{:S(2)}) %collective-permute-start.30) | collective-permute-done | bytes 131104 | tf_op jit(solution)/shard_map/ppermute | solution.py:305
  100.8 0.9 collective-permute-start.40
  101.7 0.9 collective-permute-done.28
  102.7 2.1 %collective-permute-start.37 = (bf16[256,256]{1,0:T(8,128)(2,1)S(1)}, bf16[256,256]{1,0:T(8,128)(2,1)S(1)}, u32[]{:S(2)}, u32[]{:S(2)}) collective-permute-start(bf16[256,256]{1,0:T(8,128)(2,1)S(1)} %collective-permute-done.28), channel_id=1, source_target_pairs={{0,4},{1,5},{2,6},{3,7},{4,8},{5,9},{6,10},{7,11},{8,12},{9,13},{1... | collective-permute-start | bytes 393224 | tf_op jit(solution)/shard_map/ppermute | solution.py:305
  104.8 4.0 %collective-permute-done.39 = bf16[256,256]{1,0:T(8,128)(2,1)S(1)} collective-permute-done((bf16[256,256]{1,0:T(8,128)(2,1)S(1)}, bf16[256,256]{1,0:T(8,128)(2,1)S(1)}, u32[]{:S(2)}, u32[]{:S(2)}) %collective-permute-start.39) | collective-permute-done | bytes 131104 | tf_op jit(solution)/shard_map/ppermute | solution.py:305
  109.3 0.9 collective-permute-done.37
  111.2 1.3 %collective-permute-start.42 = (bf16[256,256]{1,0:T(8,128)(2,1)S(1)}, bf16[256,256]{1,0:T(8,128)(2,1)S(1)}, u32[]{:S(2)}, u32[]{:S(2)}) collective-permute-start(bf16[256,256]{1,0:T(8,128)(2,1)S(1)} %collective-permute-done.27), channel_id=1, source_target_pairs={{0,12},{1,13},{2,14},{3,15},{4,0},{5,1},{6,2},{7,3},{8,4},{9,5},{1... | collective-permute-start | bytes 393224 | tf_op jit(solution)/shard_map/ppermute | solution.py:305
  113.0 3.0 %back.2.refs_0_ = bf16[4096,512]{1,0:T(8,128)(2,1)} custom-call(s32[10]{0:T(128)S(1)} %stack.107.at_ref, bf16[512,512]{1,0:T(8,128)(2,1)S(1)} %copy-done, bf16[256,512]{1,0:T(8,128)(2,1)S(1)} %get-tuple-element.81.refs_1_, bf16[512,256]{1,0:T(8,128)(2,1)S(1)} %constant_dynamic-update-slice_fusion.refs_2_, ...), custom_call_target="tpu_custom_call" | custom-call | flops 40265318400 | bytes 157286400 | tf_op jit(solution)/shard_map/back/pallas_call | solution.py:66
  117.8 2.4 %back.3 = bf16[4096,512]{1,0:T(8,128)(2,1)} custom-call(s32[6]{0:T(128)S(1)} %stack.96.at_ref, bf16[4096,512]{1,0:T(8,128)(2,1)} %back.2.refs_0_, bf16[512,512]{1,0:T(8,128)(2,1)S(1)} %copy-done, bf16[512,256]{1,0:T(8,128)(2,1)S(1)} %constant_dynamic-update-slice_fusion.8.refs_2_, ...), custom_call_target="tpu_custom_call", output_to_operand_aliasing={{}: (1, {})} | custom-call | flops 24159191040000 | bytes 94371840000 | tf_op jit(solution)/shard_map/back/pallas_call | solution.py:66
  (83 shorter events, 11.0 us)
Async XLA Ops:
  0.6 44.8 %collective-permute-start = (bf16[384,8192]{1,0:T(8,128)(2,1)}, bf16[384,8192]{1,0:T(8,128)(2,1)}, u32[]{:S(2)}, u32[]{:S(2)}) collective-permute-start(bf16[384,8192]{1,0:T(8,128)(2,1)} %own_ref.5), channel_id=1, source_target_pairs={{0,1},{1,0},{2,3},{3,2},{4,5},{5,4},{6,7},{7,6},{8,9},{9,8},{10,11... | collective-permute-start | bytes 18874376 | tf_op jit(solution)/shard_map/ppermute | solution.py:299
  2.2 11.8 %collective-permute-start.1 = (bf16[512,256]{1,0:T(8,128)(2,1)S(1)}, bf16[512,256]{1,0:T(8,128)(2,1)S(1)}, u32[]{:S(2)}, u32[]{:S(2)}) collective-permute-start(bf16[512,256]{1,0:T(8,128)(2,1)S(1)} %get-tuple-element.93.refs_0_), channel_id=1, source_target_pairs={{0,4},{1,5},{2,6},{3,7},{4,8},{5,9},{6,10},{7,11},{8,12},{9,13},{1... | collective-permute-start | bytes 786440 | tf_op jit(solution)/shard_map/ppermute | solution.py:305
  4.9 9.2 %collective-permute-start.2 = (bf16[512,256]{1,0:T(8,128)(2,1)S(1)}, bf16[512,256]{1,0:T(8,128)(2,1)S(1)}, u32[]{:S(2)}, u32[]{:S(2)}) collective-permute-start(bf16[512,256]{1,0:T(8,128)(2,1)S(1)} %get-tuple-element.93.refs_0_), channel_id=1, source_target_pairs={{0,2},{1,3},{2,0},{3,1},{4,6},{5,7},{6,4},{7,5},{8,10},{9,11},{10,... | collective-permute-start | bytes 786440 | tf_op jit(solution)/shard_map/ppermute | solution.py:302
  6.4 13.3 %collective-permute-start.8 = (bf16[512,256]{1,0:T(8,128)(2,1)S(1)}, bf16[512,256]{1,0:T(8,128)(2,1)S(1)}, u32[]{:S(2)}, u32[]{:S(2)}) collective-permute-start(bf16[512,256]{1,0:T(8,128)(2,1)S(1)} %get-tuple-element.92.refs_7_), channel_id=1, source_target_pairs={{0,4},{1,5},{2,6},{3,7},{4,8},{5,9},{6,10},{7,11},{8,12},{9,13},{1... | collective-permute-start | bytes 786440 | tf_op jit(solution)/shard_map/ppermute | solution.py:305
  8.0 11.7 %collective-permute-start.9 = (bf16[512,256]{1,0:T(8,128)(2,1)S(1)}, bf16[512,256]{1,0:T(8,128)(2,1)S(1)}, u32[]{:S(2)}, u32[]{:S(2)}) collective-permute-start(bf16[512,256]{1,0:T(8,128)(2,1)S(1)} %get-tuple-element.92.refs_7_), channel_id=1, source_target_pairs={{0,2},{1,3},{2,0},{3,1},{4,6},{5,7},{6,4},{7,5},{8,10},{9,11},{10,... | collective-permute-start | bytes 786440 | tf_op jit(solution)/shard_map/ppermute | solution.py:302
  14.0 11.2 %collective-permute-start.3 = (bf16[512,256]{1,0:T(8,128)(2,1)S(1)}, bf16[512,256]{1,0:T(8,128)(2,1)S(1)}, u32[]{:S(2)}, u32[]{:S(2)}) collective-permute-start(bf16[512,256]{1,0:T(8,128)(2,1)S(1)} %collective-permute-done.1.refs_2_), channel_id=1, source_target_pairs={{0,4},{1,5},{2,6},{3,7},{4,8},{5,9},{6,10},{7,11},{8,12},{9,13},{1... | collective-permute-start | bytes 786440 | tf_op jit(solution)/shard_map/ppermute | solution.py:305
  15.6 9.7 %collective-permute-start.4 = (bf16[512,256]{1,0:T(8,128)(2,1)S(1)}, bf16[512,256]{1,0:T(8,128)(2,1)S(1)}, u32[]{:S(2)}, u32[]{:S(2)}) collective-permute-start(bf16[512,256]{1,0:T(8,128)(2,1)S(1)} %collective-permute-done.1.refs_2_), channel_id=1, source_target_pairs={{0,2},{1,3},{2,0},{3,1},{4,6},{5,7},{6,4},{7,5},{8,10},{9,11},{10,... | collective-permute-start | bytes 786440 | tf_op jit(solution)/shard_map/ppermute | solution.py:302
  19.7 11.2 %collective-permute-start.10 = (bf16[512,256]{1,0:T(8,128)(2,1)S(1)}, bf16[512,256]{1,0:T(8,128)(2,1)S(1)}, u32[]{:S(2)}, u32[]{:S(2)}) collective-permute-start(bf16[512,256]{1,0:T(8,128)(2,1)S(1)} %collective-permute-done.8.refs_9_), channel_id=1, source_target_pairs={{0,4},{1,5},{2,6},{3,7},{4,8},{5,9},{6,10},{7,11},{8,12},{9,13},{1... | collective-permute-start | bytes 786440 | tf_op jit(solution)/shard_map/ppermute | solution.py:305
  21.2 9.7 %collective-permute-start.11 = (bf16[512,256]{1,0:T(8,128)(2,1)S(1)}, bf16[512,256]{1,0:T(8,128)(2,1)S(1)}, u32[]{:S(2)}, u32[]{:S(2)}) collective-permute-start(bf16[512,256]{1,0:T(8,128)(2,1)S(1)} %collective-permute-done.8.refs_9_), channel_id=1, source_target_pairs={{0,2},{1,3},{2,0},{3,1},{4,6},{5,7},{6,4},{7,5},{8,10},{9,11},{10,... | collective-permute-start | bytes 786440 | tf_op jit(solution)/shard_map/ppermute | solution.py:302
  25.3 11.2 %collective-permute-start.6 = (bf16[512,256]{1,0:T(8,128)(2,1)S(1)}, bf16[512,256]{1,0:T(8,128)(2,1)S(1)}, u32[]{:S(2)}, u32[]{:S(2)}) collective-permute-start(bf16[512,256]{1,0:T(8,128)(2,1)S(1)} %collective-permute-done.3.refs_4_), channel_id=1, source_target_pairs={{0,4},{1,5},{2,6},{3,7},{4,8},{5,9},{6,10},{7,11},{8,12},{9,13},{1... | collective-permute-start | bytes 786440 | tf_op jit(solution)/shard_map/ppermute | solution.py:305
  26.8 9.7 %collective-permute-start.7 = (bf16[512,256]{1,0:T(8,128)(2,1)S(1)}, bf16[512,256]{1,0:T(8,128)(2,1)S(1)}, u32[]{:S(2)}, u32[]{:S(2)}) collective-permute-start(bf16[512,256]{1,0:T(8,128)(2,1)S(1)} %collective-permute-done.3.refs_4_), channel_id=1, source_target_pairs={{0,2},{1,3},{2,0},{3,1},{4,6},{5,7},{6,4},{7,5},{8,10},{9,11},{10,... | collective-permute-start | bytes 786440 | tf_op jit(solution)/shard_map/ppermute | solution.py:302
  30.9 11.0 %collective-permute-start.12 = (bf16[512,256]{1,0:T(8,128)(2,1)S(1)}, bf16[512,256]{1,0:T(8,128)(2,1)S(1)}, u32[]{:S(2)}, u32[]{:S(2)}) collective-permute-start(bf16[512,256]{1,0:T(8,128)(2,1)S(1)} %collective-permute-done.10.refs_11_), channel_id=1, source_target_pairs={{0,4},{1,5},{2,6},{3,7},{4,8},{5,9},{6,10},{7,11},{8,12},{9,13},{1... | collective-permute-start | bytes 786440 | tf_op jit(solution)/shard_map/ppermute | solution.py:305
  32.4 9.5 %collective-permute-start.13 = (bf16[512,256]{1,0:T(8,128)(2,1)S(1)}, bf16[512,256]{1,0:T(8,128)(2,1)}, u32[]{:S(2)}, u32[]{:S(2)}) collective-permute-start(bf16[512,256]{1,0:T(8,128)(2,1)S(1)} %collective-permute-done.10.refs_11_), channel_id=1, source_target_pairs={{0,2},{1,3},{2,0},{3,1},{4,6},{5,7},{6,4},{7,5},{8,10},{9,11},{10,... | collective-permute-start | bytes 786440 | tf_op jit(solution)/shard_map/ppermute | solution.py:302
  41.9 9.3 %collective-permute-start.15 = (bf16[512,256]{1,0:T(8,128)(2,1)S(1)}, bf16[512,256]{1,0:T(8,128)(2,1)S(1)}, u32[]{:S(2)}, u32[]{:S(2)}) collective-permute-start(bf16[512,256]{1,0:T(8,128)(2,1)S(1)} %collective-permute-done.9.refs_8_), channel_id=1, source_target_pairs={{0,12},{1,13},{2,14},{3,15},{4,0},{5,1},{6,2},{7,3},{8,4},{9,5},{1... | collective-permute-start | bytes 786440 | tf_op jit(solution)/shard_map/ppermute | solution.py:305
  43.9 7.6 %collective-permute-start.14 = (bf16[512,256]{1,0:T(8,128)(2,1)S(1)}, bf16[512,256]{1,0:T(8,128)(2,1)S(1)}, u32[]{:S(2)}, u32[]{:S(2)}) collective-permute-start(bf16[512,256]{1,0:T(8,128)(2,1)S(1)} %collective-permute-done.6.refs_6_), channel_id=1, source_target_pairs={{0,2},{1,3},{2,0},{3,1},{4,6},{5,7},{6,4},{7,5},{8,10},{9,11},{10,... | collective-permute-start | bytes 786440 | tf_op jit(solution)/shard_map/ppermute | solution.py:302
  45.4 7.2 %collective-permute-start.5 = (bf16[384,4096]{1,0:T(8,128)(2,1)}, bf16[384,4096]{1,0:T(8,128)(2,1)}, u32[]{:S(2)}, u32[]{:S(2)}) collective-permute-start(bf16[384,4096]{1,0:T(8,128)(2,1)} %own_ref.7), channel_id=1, source_target_pairs={{0,1},{1,0},{2,3},{3,2},{4,5},{5,4},{6,7},{7,6},{8,9},{9,8},{10,11... | collective-permute-start | bytes 9437192 | tf_op jit(solution)/shard_map/ppermute | solution.py:299
  52.1 3.5 %collective-permute-start.16 = (f32[768,512]{1,0:T(8,128)S(1)}, f32[768,512]{1,0:T(8,128)S(1)}, u32[]{:S(2)}, u32[]{:S(2)}) collective-permute-start(f32[768,512]{1,0:T(8,128)S(1)} %project_last.1.mine_ref), channel_id=1, source_target_pairs={{0,1},{1,0},{2,3},{3,2},{4,5},{5,4},{6,7},{7,6},{8,9},{9,8},{10,11... | collective-permute-start | bytes 4718600 | tf_op jit(solution)/shard_map/ppermute | solution.py:299
  56.0 9.2 %collective-permute-start.17 = (bf16[256,512]{1,0:T(8,128)(2,1)S(1)}, bf16[256,512]{1,0:T(8,128)(2,1)S(1)}, u32[]{:S(2)}, u32[]{:S(2)}) collective-permute-start(bf16[256,512]{1,0:T(8,128)(2,1)S(1)} %get-tuple-element.62), channel_id=1, source_target_pairs={{0,2},{1,3},{2,0},{3,1},{4,6},{5,7},{6,4},{7,5},{8,10},{9,11},{10,... | collective-permute-start | bytes 786440 | tf_op jit(solution)/shard_map/ppermute | solution.py:302
  60.8 10.0 %collective-permute-start.19 = (bf16[256,512]{1,0:T(8,128)(2,1)S(1)}, bf16[256,512]{1,0:T(8,128)(2,1)S(1)}, u32[]{:S(2)}, u32[]{:S(2)}) collective-permute-start(bf16[256,512]{1,0:T(8,128)(2,1)S(1)} %get-tuple-element.70), channel_id=1, source_target_pairs={{0,2},{1,3},{2,0},{3,1},{4,6},{5,7},{6,4},{7,5},{8,10},{9,11},{10,... | collective-permute-start | bytes 786440 | tf_op jit(solution)/shard_map/ppermute | solution.py:302
  61.4 14.9 %collective-permute-start.21 = (bf16[256,512]{1,0:T(8,128)(2,1)S(1)}, bf16[256,512]{1,0:T(8,128)(2,1)S(1)}, u32[]{:S(2)}, u32[]{:S(2)}) collective-permute-start(bf16[256,512]{1,0:T(8,128)(2,1)S(1)} %get-tuple-element.72), channel_id=1, source_target_pairs={{0,2},{1,3},{2,0},{3,1},{4,6},{5,7},{6,4},{7,5},{8,10},{9,11},{10,... | collective-permute-start | bytes 786440 | tf_op jit(solution)/shard_map/ppermute | solution.py:302
  62.9 18.5 %collective-permute-start.18 = (bf16[256,512]{1,0:T(8,128)(2,1)S(1)}, bf16[256,512]{1,0:T(8,128)(2,1)S(1)}, u32[]{:S(2)}, u32[]{:S(2)}) collective-permute-start(bf16[256,512]{1,0:T(8,128)(2,1)S(1)} %get-tuple-element.68), channel_id=1, source_target_pairs={{0,2},{1,3},{2,0},{3,1},{4,6},{5,7},{6,4},{7,5},{8,10},{9,11},{10,... | collective-permute-start | bytes 786440 | tf_op jit(solution)/shard_map/ppermute | solution.py:302
  65.2 11.1 %collective-permute-start.22 = (bf16[256,512]{1,0:T(8,128)(2,1)S(1)}, bf16[256,512]{1,0:T(8,128)(2,1)S(1)}, u32[]{:S(2)}, u32[]{:S(2)}) collective-permute-start(bf16[256,512]{1,0:T(8,128)(2,1)S(1)} %convert_add_fusion.1), channel_id=1, source_target_pairs={{0,4},{1,5},{2,6},{3,7},{4,8},{5,9},{6,10},{7,11},{8,12},{9,13},{1... | collective-permute-start | bytes 786440 | tf_op jit(solution)/shard_map/ppermute | solution.py:305
  70.8 10.6 %collective-permute-start.20 = (bf16[256,512]{1,0:T(8,128)(2,1)S(1)}, bf16[256,512]{1,0:T(8,128)(2,1)S(1)}, u32[]{:S(2)}, u32[]{:S(2)}) collective-permute-start(bf16[256,512]{1,0:T(8,128)(2,1)S(1)} %add_convert_fusion.1), channel_id=1, source_target_pairs={{0,12},{1,13},{2,14},{3,15},{4,0},{5,1},{6,2},{7,3},{8,4},{9,5},{1... | collective-permute-start | bytes 786440 | tf_op jit(solution)/shard_map/ppermute | solution.py:305
  76.5 9.0 %collective-permute-start.23 = (bf16[256,512]{1,0:T(8,128)(2,1)S(1)}, bf16[256,512]{1,0:T(8,128)(2,1)S(1)}, u32[]{:S(2)}, u32[]{:S(2)}) collective-permute-start(bf16[256,512]{1,0:T(8,128)(2,1)S(1)} %add_convert_fusion), channel_id=1, source_target_pairs={{0,4},{1,5},{2,6},{3,7},{4,8},{5,9},{6,10},{7,11},{8,12},{9,13},{1... | collective-permute-start | bytes 786440 | tf_op jit(solution)/shard_map/ppermute | solution.py:305
  85.5 27.5 %copy-start = (bf16[512,512]{1,0:T(8,128)(2,1)S(1)}, bf16[512,512]{1,0:T(8,128)(2,1)}, u32[]{:S(2)}) copy-start(bf16[512,512]{1,0:T(8,128)(2,1)} %refs_1_.1) | copy-start | bytes 1572868
  87.0 6.8 %collective-permute-start.26 = (bf16[256,256]{1,0:T(8,128)(2,1)S(1)}, bf16[256,256]{1,0:T(8,128)(2,1)S(1)}, u32[]{:S(2)}, u32[]{:S(2)}) collective-permute-start(bf16[256,256]{1,0:T(8,128)(2,1)S(1)} %get-tuple-element.94), channel_id=1, source_target_pairs={{0,4},{1,5},{2,6},{3,7},{4,8},{5,9},{6,10},{7,11},{8,12},{9,13},{1... | collective-permute-start | bytes 393224 | tf_op jit(solution)/shard_map/ppermute | solution.py:305
  87.0 6.8 %collective-permute-start.27 = (bf16[256,256]{1,0:T(8,128)(2,1)S(1)}, bf16[256,256]{1,0:T(8,128)(2,1)S(1)}, u32[]{:S(2)}, u32[]{:S(2)}) collective-permute-start(bf16[256,256]{1,0:T(8,128)(2,1)S(1)} %get-tuple-element.94), channel_id=1, source_target_pairs={{0,2},{1,3},{2,0},{3,1},{4,6},{5,7},{6,4},{7,5},{8,10},{9,11},{10,... | collective-permute-start | bytes 393224 | tf_op jit(solution)/shard_map/ppermute | solution.py:302
  88.3 7.2 %collective-permute-start.24 = (bf16[256,256]{1,0:T(8,128)(2,1)S(1)}, bf16[256,256]{1,0:T(8,128)(2,1)S(1)}, u32[]{:S(2)}, u32[]{:S(2)}) collective-permute-start(bf16[256,256]{1,0:T(8,128)(2,1)S(1)} %get-tuple-element.95), channel_id=1, source_target_pairs={{0,4},{1,5},{2,6},{3,7},{4,8},{5,9},{6,10},{7,11},{8,12},{9,13},{1... | collective-permute-start | bytes 393224 | tf_op jit(solution)/shard_map/ppermute | solution.py:305
  89.7 6.2 %collective-permute-start.25 = (bf16[256,256]{1,0:T(8,128)(2,1)S(1)}, bf16[256,256]{1,0:T(8,128)(2,1)S(1)}, u32[]{:S(2)}, u32[]{:S(2)}) collective-permute-start(bf16[256,256]{1,0:T(8,128)(2,1)S(1)} %get-tuple-element.95), channel_id=1, source_target_pairs={{0,2},{1,3},{2,0},{3,1},{4,6},{5,7},{6,4},{7,5},{8,10},{9,11},{10,... | collective-permute-start | bytes 393224 | tf_op jit(solution)/shard_map/ppermute | solution.py:302
  93.8 7.0 %collective-permute-start.30 = (bf16[256,256]{1,0:T(8,128)(2,1)S(1)}, bf16[256,256]{1,0:T(8,128)(2,1)S(1)}, u32[]{:S(2)}, u32[]{:S(2)}) collective-permute-start(bf16[256,256]{1,0:T(8,128)(2,1)S(1)} %collective-permute-done.26), channel_id=1, source_target_pairs={{0,4},{1,5},{2,6},{3,7},{4,8},{5,9},{6,10},{7,11},{8,12},{9,13},{1... | collective-permute-start | bytes 393224 | tf_op jit(solution)/shard_map/ppermute | solution.py:305
  94.6 6.3 %collective-permute-start.31 = (bf16[256,256]{1,0:T(8,128)(2,1)S(1)}, bf16[256,256]{1,0:T(8,128)(2,1)S(1)}, u32[]{:S(2)}, u32[]{:S(2)}) collective-permute-start(bf16[256,256]{1,0:T(8,128)(2,1)S(1)} %collective-permute-done.26), channel_id=1, source_target_pairs={{0,2},{1,3},{2,0},{3,1},{4,6},{5,7},{6,4},{7,5},{8,10},{9,11},{10,... | collective-permute-start | bytes 393224 | tf_op jit(solution)/shard_map/ppermute | solution.py:302
  95.9 6.8 %collective-permute-start.28 = (bf16[256,256]{1,0:T(8,128)(2,1)S(1)}, bf16[256,256]{1,0:T(8,128)(2,1)S(1)}, u32[]{:S(2)}, u32[]{:S(2)}) collective-permute-start(bf16[256,256]{1,0:T(8,128)(2,1)S(1)} %collective-permute-done.24), channel_id=1, source_target_pairs={{0,4},{1,5},{2,6},{3,7},{4,8},{5,9},{6,10},{7,11},{8,12},{9,13},{1... | collective-permute-start | bytes 393224 | tf_op jit(solution)/shard_map/ppermute | solution.py:305
  97.5 5.2 %collective-permute-start.29 = (bf16[256,256]{1,0:T(8,128)(2,1)S(1)}, bf16[256,256]{1,0:T(8,128)(2,1)S(1)}, u32[]{:S(2)}, u32[]{:S(2)}) collective-permute-start(bf16[256,256]{1,0:T(8,128)(2,1)S(1)} %collective-permute-done.24), channel_id=1, source_target_pairs={{0,2},{1,3},{2,0},{3,1},{4,6},{5,7},{6,4},{7,5},{8,10},{9,11},{10,... | collective-permute-start | bytes 393224 | tf_op jit(solution)/shard_map/ppermute | solution.py:302
  97.5 13.2 %collective-permute-start.32 = (bf16[256,512]{1,0:T(8,128)(2,1)S(1)}, bf16[256,512]{1,0:T(8,128)(2,1)S(1)}, u32[]{:S(2)}, u32[]{:S(2)}) collective-permute-start(bf16[256,512]{1,0:T(8,128)(2,1)S(1)} %get-tuple-element.81.refs_1_), channel_id=1, source_target_pairs={{0,1},{1,0},{2,3},{3,2},{4,5},{5,4},{6,7},{7,6},{8,9},{9,8},{10,11... | collective-permute-start | bytes 786440 | tf_op jit(solution)/shard_map/ppermute | solution.py:299
  100.8 7.9 %collective-permute-start.39 = (bf16[256,256]{1,0:T(8,128)(2,1)S(1)}, bf16[256,256]{1,0:T(8,128)(2,1)S(1)}, u32[]{:S(2)}, u32[]{:S(2)}) collective-permute-start(bf16[256,256]{1,0:T(8,128)(2,1)S(1)} %collective-permute-done.30), channel_id=1, source_target_pairs={{0,4},{1,5},{2,6},{3,7},{4,8},{5,9},{6,10},{7,11},{8,12},{9,13},{1... | collective-permute-start | bytes 393224 | tf_op jit(solution)/shard_map/ppermute | solution.py:305
  100.8 7.9 %collective-permute-start.40 = (bf16[256,256]{1,0:T(8,128)(2,1)S(1)}, bf16[256,256]{1,0:T(8,128)(2,1)S(1)}, u32[]{:S(2)}, u32[]{:S(2)}) collective-permute-start(bf16[256,256]{1,0:T(8,128)(2,1)S(1)} %collective-permute-done.30), channel_id=1, source_target_pairs={{0,2},{1,3},{2,0},{3,1},{4,6},{5,7},{6,4},{7,5},{8,10},{9,11},{10,... | collective-permute-start | bytes 393224 | tf_op jit(solution)/shard_map/ppermute | solution.py:302
  102.7 7.5 %collective-permute-start.37 = (bf16[256,256]{1,0:T(8,128)(2,1)S(1)}, bf16[256,256]{1,0:T(8,128)(2,1)S(1)}, u32[]{:S(2)}, u32[]{:S(2)}) collective-permute-start(bf16[256,256]{1,0:T(8,128)(2,1)S(1)} %collective-permute-done.28), channel_id=1, source_target_pairs={{0,4},{1,5},{2,6},{3,7},{4,8},{5,9},{6,10},{7,11},{8,12},{9,13},{1... | collective-permute-start | bytes 393224 | tf_op jit(solution)/shard_map/ppermute | solution.py:305
  104.7 5.4 %collective-permute-start.38 = (bf16[256,256]{1,0:T(8,128)(2,1)S(1)}, bf16[256,256]{1,0:T(8,128)(2,1)S(1)}, u32[]{:S(2)}, u32[]{:S(2)}) collective-permute-start(bf16[256,256]{1,0:T(8,128)(2,1)S(1)} %collective-permute-done.28), channel_id=1, source_target_pairs={{0,2},{1,3},{2,0},{3,1},{4,6},{5,7},{6,4},{7,5},{8,10},{9,11},{10,... | collective-permute-start | bytes 393224 | tf_op jit(solution)/shard_map/ppermute | solution.py:302
  108.8 2.4 %collective-permute-start.34 = (bf16[512,256]{1,0:T(8,128)(2,1)S(1)}, bf16[512,256]{1,0:T(8,128)(2,1)S(1)}, u32[]{:S(2)}, u32[]{:S(2)}) collective-permute-start(bf16[512,256]{1,0:T(8,128)(2,1)S(1)} %constant_dynamic-update-slice_fusion.2.refs_3_), channel_id=1, source_target_pairs={{0,1},{1,0},{2,3},{3,2},{4,5},{5,4},{6,7},{7,6},{8,9},{9,8},{10,11... | collective-permute-start | bytes 786440 | tf_op jit(solution)/shard_map/ppermute | solution.py:299
  108.8 3.7 %collective-permute-start.33 = (bf16[512,256]{1,0:T(8,128)(2,1)S(1)}, bf16[512,256]{1,0:T(8,128)(2,1)S(1)}, u32[]{:S(2)}, u32[]{:S(2)}) collective-permute-start(bf16[512,256]{1,0:T(8,128)(2,1)S(1)} %constant_dynamic-update-slice_fusion.refs_2_), channel_id=1, source_target_pairs={{0,1},{1,0},{2,3},{3,2},{4,5},{5,4},{6,7},{7,6},{8,9},{9,8},{10,11... | collective-permute-start | bytes 786440 | tf_op jit(solution)/shard_map/ppermute | solution.py:299
  110.2 2.3 %collective-permute-start.36 = (bf16[512,256]{1,0:T(8,128)(2,1)S(1)}, bf16[512,256]{1,0:T(8,128)(2,1)S(1)}, u32[]{:S(2)}, u32[]{:S(2)}) collective-permute-start(bf16[512,256]{1,0:T(8,128)(2,1)S(1)} %constant_dynamic-update-slice_fusion.6.refs_5_), channel_id=1, source_target_pairs={{0,1},{1,0},{2,3},{3,2},{4,5},{5,4},{6,7},{7,6},{8,9},{9,8},{10,11... | collective-permute-start | bytes 786440 | tf_op jit(solution)/shard_map/ppermute | solution.py:299
  110.2 2.8 %collective-permute-start.35 = (bf16[512,256]{1,0:T(8,128)(2,1)S(1)}, bf16[512,256]{1,0:T(8,128)(2,1)S(1)}, u32[]{:S(2)}, u32[]{:S(2)}) collective-permute-start(bf16[512,256]{1,0:T(8,128)(2,1)S(1)} %constant_dynamic-update-slice_fusion.4.refs_4_), channel_id=1, source_target_pairs={{0,1},{1,0},{2,3},{3,2},{4,5},{5,4},{6,7},{7,6},{8,9},{9,8},{10,11... | collective-permute-start | bytes 786440 | tf_op jit(solution)/shard_map/ppermute | solution.py:299
  110.8 5.6 %collective-permute-start.41 = (bf16[256,256]{1,0:T(8,128)(2,1)S(1)}, bf16[256,256]{1,0:T(8,128)(2,1)S(1)}, u32[]{:S(2)}, u32[]{:S(2)}) collective-permute-start(bf16[256,256]{1,0:T(8,128)(2,1)S(1)} %collective-permute-done.37), channel_id=1, source_target_pairs={{0,2},{1,3},{2,0},{3,1},{4,6},{5,7},{6,4},{7,5},{8,10},{9,11},{10,... | collective-permute-start | bytes 393224 | tf_op jit(solution)/shard_map/ppermute | solution.py:302
  111.2 5.2 %collective-permute-start.42 = (bf16[256,256]{1,0:T(8,128)(2,1)S(1)}, bf16[256,256]{1,0:T(8,128)(2,1)S(1)}, u32[]{:S(2)}, u32[]{:S(2)}) collective-permute-start(bf16[256,256]{1,0:T(8,128)(2,1)S(1)} %collective-permute-done.27), channel_id=1, source_target_pairs={{0,12},{1,13},{2,14},{3,15},{4,0},{5,1},{6,2},{7,3},{8,4},{9,5},{1... | collective-permute-start | bytes 393224 | tf_op jit(solution)/shard_map/ppermute | solution.py:305
  112.5 5.3 %collective-permute-start.44 = (bf16[512,256]{1,0:T(8,128)(2,1)S(1)}, bf16[512,256]{1,0:T(8,128)(2,1)S(1)}, u32[]{:S(2)}, u32[]{:S(2)}) collective-permute-start(bf16[512,256]{1,0:T(8,128)(2,1)S(1)} %constant_dynamic-update-slice_fusion.10.refs_3_), channel_id=1, source_target_pairs={{0,1},{1,0},{2,3},{3,2},{4,5},{5,4},{6,7},{7,6},{8,9},{9,8},{10,11... | collective-permute-start | bytes 786440 | tf_op jit(solution)/shard_map/ppermute | solution.py:299
  112.5 5.3 %collective-permute-start.43 = (bf16[512,256]{1,0:T(8,128)(2,1)S(1)}, bf16[512,256]{1,0:T(8,128)(2,1)S(1)}, u32[]{:S(2)}, u32[]{:S(2)}) collective-permute-start(bf16[512,256]{1,0:T(8,128)(2,1)S(1)} %constant_dynamic-update-slice_fusion.8.refs_2_), channel_id=1, source_target_pairs={{0,1},{1,0},{2,3},{3,2},{4,5},{5,4},{6,7},{7,6},{8,9},{9,8},{10,11... | collective-permute-start | bytes 786440 | tf_op jit(solution)/shard_map/ppermute | solution.py:299
  116.3 1.3 %collective-permute-start.46 = (bf16[256,256]{1,0:T(8,128)(2,1)S(1)}, bf16[256,256]{1,0:T(8,128)(2,1)S(1)}, u32[]{:S(2)}, u32[]{:S(2)}) collective-permute-start(bf16[256,256]{1,0:T(8,128)(2,1)S(1)} %collective-permute-done.42.refs_5_), channel_id=1, source_target_pairs={{0,1},{1,0},{2,3},{3,2},{4,5},{5,4},{6,7},{7,6},{8,9},{9,8},{10,11... | collective-permute-start | bytes 393224 | tf_op jit(solution)/shard_map/ppermute | solution.py:299
  116.3 1.5 %collective-permute-start.45 = (bf16[256,256]{1,0:T(8,128)(2,1)S(1)}, bf16[256,256]{1,0:T(8,128)(2,1)S(1)}, u32[]{:S(2)}, u32[]{:S(2)}) collective-permute-start(bf16[256,256]{1,0:T(8,128)(2,1)S(1)} %collective-permute-done.41.refs_4_), channel_id=1, source_target_pairs={{0,1},{1,0},{2,3},{3,2},{4,5},{5,4},{6,7},{7,6},{8,9},{9,8},{10,11... | collective-permute-start | bytes 393224 | tf_op jit(solution)/shard_map/ppermute | solution.py:299
  (2 other events, 40.6 us)

commit v13 on v12

--- a/solution.py
+++ b/solution.py
@@ -13,7 +13,7 @@
 epsilon = 1e-08
 
 CHUNKS = 2
-W_EARLY, W_LATE, W_OUTER, W_BACK, W_LAST = 30, 30, 30, 30, 30000
+W_EARLY, W_LATE, W_OUTER, W_BACK, W_LAST = 3, 30, 30, 30, 30000
 F32, BF16 = jnp.float32, jnp.bfloat16
 VMEM_LIMIT = 16 * 1024 * 1024
 
@@ -357,9 +357,10 @@
         passed = term + shift_z(passed.astype(BF16), 1).astype(F32)
     back_term = terms[nz - 3].astype(BF16)
     reduced = terms[nz - 2] + shift_z(back_term, nz - 1).astype(F32) + shift_z(passed.astype(BF16), 1).astype(F32)
-    new_first, new_second, direction = adam(reduced, first_moment, second_moment)
+    direction = adam(reduced, first_moment, second_moment)[2]
 
     line, across = gather([direction[:, part] for part in parts])
+    new_first, new_second, _ = adam(after(reduced, line[0][1]), first_moment, second_moment)
     rows_in_all = 4 * nz * width
     steps = range(1, nz)
     mine = [(direction,)] + [tuple(jnp.concatenate([line[i][k], across[i][k - 1]]) for i in range(CHUNKS)) for k in steps]

time: 120 us -> 120 us (level)
  waiting for transfers between devices: 53.1 us -> 51.7 us
  transfers between devices with their start and end apart: 47 -> 47, of which waited for: 22 -> 20; matrix products, arithmetic and copies ran while one was open for 2% -> 3% of each run, Pallas kernels for 14% -> 14%
where the time goes in v13:
time: 120 us
  waiting for transfers between devices  51.7 us (43%)
  starting transfers between devices  43.9 us (37%)
  Pallas kernels  19.6 us (16%)
  other arithmetic  2.03 us (2%)
  local copies, waits for them, and re-layouts  1.47 us (1%)
    ppermute x17, waiting for transfers between devices, shift_z(): return lax.ppermute(x, 'dp', pairs(lambda a, b, c: ((a + k) % nz, b, c)))  37.4 us
    ppermute x17, starting transfers between devices, shift_z(): return lax.ppermute(x, 'dp', pairs(lambda a, b, c: ((a + k) % nz, b, c)))  22.7 us
    pallas_call x6, Pallas kernels, call(): pl.pallas_call(kernel, grid_spec=pltpu.PrefetchScalarGridSpec(num_scalar_...  18.7 us
    ppermute x18, starting transfers between devices, swap_y(): return lax.ppermute(x, 'dp', pairs(lambda a, b, c: (a, 1 - b, c)))  18.2 us
    ppermute x18, waiting for transfers between devices, swap_y(): return lax.ppermute(x, 'dp', pairs(lambda a, b, c: (a, 1 - b, c)))  12.5 us
    ppermute x12, starting transfers between devices, swap_core(): return lax.ppermute(x, 'dp', pairs(lambda a, b, c: (a, b, 1 - c)))  2.98 us
  transfers between devices with their start and end apart: 47, of which 20 were waited for; matrix products, arithmetic and copies ran while one was open for 3% of the time, Pallas kernels for 14%

profile of v13, /device:TPU:0, one launch (start us, length us, event | category | flops | bytes accessed | tf_op | source)
XLA Modules:
  0.0 119.8 jit_solution(15431074398862402510)
XLA Ops:
  1.1 1.1 fusion.7
  2.2 2.6 %collective-permute-start.1 = (bf16[512,256]{1,0:T(8,128)(2,1)S(1)}, bf16[512,256]{1,0:T(8,128)(2,1)S(1)}, u32[]{:S(2)}, u32[]{:S(2)}) collective-permute-start(bf16[512,256]{1,0:T(8,128)(2,1)S(1)} %get-tuple-element.96.refs_0_), channel_id=1, source_target_pairs={{0,4},{1,5},{2,6},{3,7},{4,8},{5,9},{6,10},{7,11},{8,12},{9,13},{1... | collective-permute-start | bytes 786440 | tf_op jit(solution)/shard_map/ppermute | solution.py:305
  4.9 1.5 %collective-permute-start.2 = (bf16[512,256]{1,0:T(8,128)(2,1)S(1)}, bf16[512,256]{1,0:T(8,128)(2,1)S(1)}, u32[]{:S(2)}, u32[]{:S(2)}) collective-permute-start(bf16[512,256]{1,0:T(8,128)(2,1)S(1)} %get-tuple-element.96.refs_0_), channel_id=1, source_target_pairs={{0,2},{1,3},{2,0},{3,1},{4,6},{5,7},{6,4},{7,5},{8,10},{9,11},{10,... | collective-permute-start | bytes 786440 | tf_op jit(solution)/shard_map/ppermute | solution.py:302
  6.4 1.6 %collective-permute-start.8 = (bf16[512,256]{1,0:T(8,128)(2,1)S(1)}, bf16[512,256]{1,0:T(8,128)(2,1)S(1)}, u32[]{:S(2)}, u32[]{:S(2)}) collective-permute-start(bf16[512,256]{1,0:T(8,128)(2,1)S(1)} %get-tuple-element.95.refs_7_), channel_id=1, source_target_pairs={{0,4},{1,5},{2,6},{3,7},{4,8},{5,9},{6,10},{7,11},{8,12},{9,13},{1... | collective-permute-start | bytes 786440 | tf_op jit(solution)/shard_map/ppermute | solution.py:305
  8.5 5.6 %collective-permute-done.1.refs_2_ = bf16[512,256]{1,0:T(8,128)(2,1)S(1)} collective-permute-done((bf16[512,256]{1,0:T(8,128)(2,1)S(1)}, bf16[512,256]{1,0:T(8,128)(2,1)S(1)}, u32[]{:S(2)}, u32[]{:S(2)}) %collective-permute-start.1) | collective-permute-done | bytes 262176 | tf_op jit(solution)/shard_map/ppermute | solution.py:305
  14.0 1.5 %collective-permute-start.3 = (bf16[512,256]{1,0:T(8,128)(2,1)S(1)}, bf16[512,256]{1,0:T(8,128)(2,1)S(1)}, u32[]{:S(2)}, u32[]{:S(2)}) collective-permute-start(bf16[512,256]{1,0:T(8,128)(2,1)S(1)} %collective-permute-done.1.refs_2_), channel_id=1, source_target_pairs={{0,4},{1,5},{2,6},{3,7},{4,8},{5,9},{6,10},{7,11},{8,12},{9,13},{1... | collective-permute-start | bytes 786440 | tf_op jit(solution)/shard_map/ppermute | solution.py:305
  15.6 1.5 %collective-permute-start.4 = (bf16[512,256]{1,0:T(8,128)(2,1)S(1)}, bf16[512,256]{1,0:T(8,128)(2,1)S(1)}, u32[]{:S(2)}, u32[]{:S(2)}) collective-permute-start(bf16[512,256]{1,0:T(8,128)(2,1)S(1)} %collective-permute-done.1.refs_2_), channel_id=1, source_target_pairs={{0,2},{1,3},{2,0},{3,1},{4,6},{5,7},{6,4},{7,5},{8,10},{9,11},{10,... | collective-permute-start | bytes 786440 | tf_op jit(solution)/shard_map/ppermute | solution.py:302
  17.1 2.6 %collective-permute-done.8.refs_9_ = bf16[512,256]{1,0:T(8,128)(2,1)S(1)} collective-permute-done((bf16[512,256]{1,0:T(8,128)(2,1)S(1)}, bf16[512,256]{1,0:T(8,128)(2,1)S(1)}, u32[]{:S(2)}, u32[]{:S(2)}) %collective-permute-start.8) | collective-permute-done | bytes 262176 | tf_op jit(solution)/shard_map/ppermute | solution.py:305
  19.7 1.5 %collective-permute-start.10 = (bf16[512,256]{1,0:T(8,128)(2,1)S(1)}, bf16[512,256]{1,0:T(8,128)(2,1)S(1)}, u32[]{:S(2)}, u32[]{:S(2)}) collective-permute-start(bf16[512,256]{1,0:T(8,128)(2,1)S(1)} %collective-permute-done.8.refs_9_), channel_id=1, source_target_pairs={{0,4},{1,5},{2,6},{3,7},{4,8},{5,9},{6,10},{7,11},{8,12},{9,13},{1... | collective-permute-start | bytes 786440 | tf_op jit(solution)/shard_map/ppermute | solution.py:305
  21.2 1.5 %collective-permute-start.11 = (bf16[512,256]{1,0:T(8,128)(2,1)S(1)}, bf16[512,256]{1,0:T(8,128)(2,1)S(1)}, u32[]{:S(2)}, u32[]{:S(2)}) collective-permute-start(bf16[512,256]{1,0:T(8,128)(2,1)S(1)} %collective-permute-done.8.refs_9_), channel_id=1, source_target_pairs={{0,2},{1,3},{2,0},{3,1},{4,6},{5,7},{6,4},{7,5},{8,10},{9,11},{10,... | collective-permute-start | bytes 786440 | tf_op jit(solution)/shard_map/ppermute | solution.py:302
  22.7 2.6 %collective-permute-done.3.refs_4_ = bf16[512,256]{1,0:T(8,128)(2,1)S(1)} collective-permute-done((bf16[512,256]{1,0:T(8,128)(2,1)S(1)}, bf16[512,256]{1,0:T(8,128)(2,1)S(1)}, u32[]{:S(2)}, u32[]{:S(2)}) %collective-permute-start.3) | collective-permute-done | bytes 262176 | tf_op jit(solution)/shard_map/ppermute | solution.py:305
  25.3 1.5 %collective-permute-start.6 = (bf16[512,256]{1,0:T(8,128)(2,1)S(1)}, bf16[512,256]{1,0:T(8,128)(2,1)S(1)}, u32[]{:S(2)}, u32[]{:S(2)}) collective-permute-start(bf16[512,256]{1,0:T(8,128)(2,1)S(1)} %collective-permute-done.3.refs_4_), channel_id=1, source_target_pairs={{0,4},{1,5},{2,6},{3,7},{4,8},{5,9},{6,10},{7,11},{8,12},{9,13},{1... | collective-permute-start | bytes 786440 | tf_op jit(solution)/shard_map/ppermute | solution.py:305
  26.8 1.5 %collective-permute-start.7 = (bf16[512,256]{1,0:T(8,128)(2,1)S(1)}, bf16[512,256]{1,0:T(8,128)(2,1)S(1)}, u32[]{:S(2)}, u32[]{:S(2)}) collective-permute-start(bf16[512,256]{1,0:T(8,128)(2,1)S(1)} %collective-permute-done.3.refs_4_), channel_id=1, source_target_pairs={{0,2},{1,3},{2,0},{3,1},{4,6},{5,7},{6,4},{7,5},{8,10},{9,11},{10,... | collective-permute-start | bytes 786440 | tf_op jit(solution)/shard_map/ppermute | solution.py:302
  28.3 2.6 %collective-permute-done.10.refs_11_ = bf16[512,256]{1,0:T(8,128)(2,1)S(1)} collective-permute-done((bf16[512,256]{1,0:T(8,128)(2,1)S(1)}, bf16[512,256]{1,0:T(8,128)(2,1)S(1)}, u32[]{:S(2)}, u32[]{:S(2)}) %collective-permute-start.10) | collective-permute-done | bytes 262176 | tf_op jit(solution)/shard_map/ppermute | solution.py:305
  30.9 1.5 %collective-permute-start.12 = (bf16[512,256]{1,0:T(8,128)(2,1)S(1)}, bf16[512,256]{1,0:T(8,128)(2,1)S(1)}, u32[]{:S(2)}, u32[]{:S(2)}) collective-permute-start(bf16[512,256]{1,0:T(8,128)(2,1)S(1)} %collective-permute-done.10.refs_11_), channel_id=1, source_target_pairs={{0,4},{1,5},{2,6},{3,7},{4,8},{5,9},{6,10},{7,11},{8,12},{9,13},{1... | collective-permute-start | bytes 786440 | tf_op jit(solution)/shard_map/ppermute | solution.py:305
  32.4 1.5 %collective-permute-start.13 = (bf16[512,256]{1,0:T(8,128)(2,1)S(1)}, bf16[512,256]{1,0:T(8,128)(2,1)}, u32[]{:S(2)}, u32[]{:S(2)}) collective-permute-start(bf16[512,256]{1,0:T(8,128)(2,1)S(1)} %collective-permute-done.10.refs_11_), channel_id=1, source_target_pairs={{0,2},{1,3},{2,0},{3,1},{4,6},{5,7},{6,4},{7,5},{8,10},{9,11},{10,... | collective-permute-start | bytes 786440 | tf_op jit(solution)/shard_map/ppermute | solution.py:302
  34.0 2.5 %collective-permute-done.6.refs_6_ = bf16[512,256]{1,0:T(8,128)(2,1)S(1)} collective-permute-done((bf16[512,256]{1,0:T(8,128)(2,1)S(1)}, bf16[512,256]{1,0:T(8,128)(2,1)S(1)}, u32[]{:S(2)}, u32[]{:S(2)}) %collective-permute-start.6) | collective-permute-done | bytes 262176 | tf_op jit(solution)/shard_map/ppermute | solution.py:305
  36.5 5.4 %collective-permute-done.12.refs_13_ = bf16[512,256]{1,0:T(8,128)(2,1)S(1)} collective-permute-done((bf16[512,256]{1,0:T(8,128)(2,1)S(1)}, bf16[512,256]{1,0:T(8,128)(2,1)S(1)}, u32[]{:S(2)}, u32[]{:S(2)}) %collective-permute-start.12) | collective-permute-done | bytes 262176 | tf_op jit(solution)/shard_map/ppermute | solution.py:305
  41.9 1.9 %collective-permute-start.15 = (bf16[512,256]{1,0:T(8,128)(2,1)S(1)}, bf16[512,256]{1,0:T(8,128)(2,1)S(1)}, u32[]{:S(2)}, u32[]{:S(2)}) collective-permute-start(bf16[512,256]{1,0:T(8,128)(2,1)S(1)} %collective-permute-done.9.refs_8_), channel_id=1, source_target_pairs={{0,12},{1,13},{2,14},{3,15},{4,0},{5,1},{6,2},{7,3},{8,4},{9,5},{1... | collective-permute-start | bytes 786440 | tf_op jit(solution)/shard_map/ppermute | solution.py:305
  43.9 1.5 %collective-permute-start.14 = (bf16[512,256]{1,0:T(8,128)(2,1)S(1)}, bf16[512,256]{1,0:T(8,128)(2,1)S(1)}, u32[]{:S(2)}, u32[]{:S(2)}) collective-permute-start(bf16[512,256]{1,0:T(8,128)(2,1)S(1)} %collective-permute-done.6.refs_6_), channel_id=1, source_target_pairs={{0,2},{1,3},{2,0},{3,1},{4,6},{5,7},{6,4},{7,5},{8,10},{9,11},{10,... | collective-permute-start | bytes 786440 | tf_op jit(solution)/shard_map/ppermute | solution.py:302
  45.4 5.9 %project.1 = (f32[768,512]{1,0:T(8,128)S(1)}, bf16[768,512]{1,0:T(8,128)(2,1)S(1)}) custom-call(s32[8]{0:T(128)S(1)} %stack.116.at_ref, bf16[384,8192]{1,0:T(8,128)(2,1)} %own_ref.5, bf16[384,8192]{1,0:T(8,128)(2,1)} %collective-permute-done.sib_ref, bf16[512,256]{1,0:T(8,128)(2,1)S(1)} %get-tuple-element.96.refs_0_, ...), custom_call_target="tpu_custom_call" | custom-call | flops 8455716864 | bytes 32243712 | tf_op jit(solution)/shard_map/project/pallas_call | solution.py:66
  52.6 1.2 %turn.1.turned_ref = bf16[256,768]{1,0:T(8,128)(2,1)S(1)} custom-call(s32[1]{0:T(128)} %bitcast.21.at_ref, bf16[384,4096]{1,0:T(8,128)(2,1)} %own_ref.7, bf16[384,4096]{1,0:T(8,128)(2,1)} %collective-permute-done.5.sib_ref), custom_call_target="tpu_custom_call" | custom-call | bytes 23592960 | tf_op jit(solution)/shard_map/turn/pallas_call | solution.py:66
  53.8 1.8 %collective-permute-done.16.theirs_ref = f32[768,512]{1,0:T(8,128)S(1)} collective-permute-done((f32[768,512]{1,0:T(8,128)S(1)}, f32[768,512]{1,0:T(8,128)S(1)}, u32[]{:S(2)}, u32[]{:S(2)}) %collective-permute-start.16) | collective-permute-done | bytes 1572896 | tf_op jit(solution)/shard_map/ppermute | solution.py:299
  56.0 1.5 %collective-permute-start.17 = (bf16[256,512]{1,0:T(8,128)(2,1)S(1)}, bf16[256,512]{1,0:T(8,128)(2,1)S(1)}, u32[]{:S(2)}, u32[]{:S(2)}) collective-permute-start(bf16[256,512]{1,0:T(8,128)(2,1)S(1)} %get-tuple-element.63), channel_id=1, source_target_pairs={{0,2},{1,3},{2,0},{3,1},{4,6},{5,7},{6,4},{7,5},{8,10},{9,11},{10,... | collective-permute-start | bytes 786440 | tf_op jit(solution)/shard_map/ppermute | solution.py:302
  57.5 3.3 %outer.2 = (bf16[256,512]{1,0:T(8,128)(2,1)S(1)}, bf16[256,512]{1,0:T(8,128)(2,1)S(1)}, bf16[256,512]{1,0:T(8,128)(2,1)S(1)}, f32[256,512]{1,0:T(8,128)S(1)}) custom-call(s32[4]{0:T(128)S(1)} %pad_add_fusion.1.at_ref, bf16[384,4096]{1,0:T(8,128)(2,1)} %own_ref.7, bf16[384,4096]{1,0:T(8,128)(2,1)} %collective-permute-done.5.sib_ref, ...), custom_call_target="tpu_custom_call" | custom-call | flops 24159191040 | bytes 110100480 | tf_op jit(solution)/shard_map/outer/pallas_call | solution.py:66
  61.4 1.5 %collective-permute-start.21 = (bf16[256,512]{1,0:T(8,128)(2,1)S(1)}, bf16[256,512]{1,0:T(8,128)(2,1)S(1)}, u32[]{:S(2)}, u32[]{:S(2)}) collective-permute-start(bf16[256,512]{1,0:T(8,128)(2,1)S(1)} %get-tuple-element.73), channel_id=1, source_target_pairs={{0,2},{1,3},{2,0},{3,1},{4,6},{5,7},{6,4},{7,5},{8,10},{9,11},{10,... | collective-permute-start | bytes 786440 | tf_op jit(solution)/shard_map/ppermute | solution.py:302
  63.5 1.7 %collective-permute-done.17 = bf16[256,512]{1,0:T(8,128)(2,1)S(1)} collective-permute-done((bf16[256,512]{1,0:T(8,128)(2,1)S(1)}, bf16[256,512]{1,0:T(8,128)(2,1)S(1)}, u32[]{:S(2)}, u32[]{:S(2)}) %collective-permute-start.17) | collective-permute-done | bytes 262176 | tf_op jit(solution)/shard_map/ppermute | solution.py:302
  65.6 2.8 %outer.3 = (f32[256,512]{1,0:T(8,128)S(1)}, f32[256,512]{1,0:T(8,128)S(1)}, f32[256,512]{1,0:T(8,128)S(1)}) custom-call(s32[3]{0:T(128)S(1)} %pad_add_fusion.at_ref, bf16[384,4096]{1,0:T(8,128)(2,1)} %own_ref.7, bf16[384,4096]{1,0:T(8,128)(2,1)} %collective-permute-done.5.sib_ref, bf16[768,512]{1,0:T(8,128)(2,1)S(1)} %get-tuple-element.65.projected_ref), custom_call_target="tpu_custom_call" | custom-call | flops 18119393280 | bytes 82575360 | tf_op jit(solution)/shard_map/outer/pallas_call | solution.py:66
  68.5 2.3 %collective-permute-done.19 = bf16[256,512]{1,0:T(8,128)(2,1)S(1)} collective-permute-done((bf16[256,512]{1,0:T(8,128)(2,1)S(1)}, bf16[256,512]{1,0:T(8,128)(2,1)S(1)}, u32[]{:S(2)}, u32[]{:S(2)}) %collective-permute-start.19) | collective-permute-done | bytes 262176 | tf_op jit(solution)/shard_map/ppermute | solution.py:302
  70.8 2.2 %collective-permute-start.20 = (bf16[256,512]{1,0:T(8,128)(2,1)S(1)}, bf16[256,512]{1,0:T(8,128)(2,1)S(1)}, u32[]{:S(2)}, u32[]{:S(2)}) collective-permute-start(bf16[256,512]{1,0:T(8,128)(2,1)S(1)} %add_convert_fusion.1), channel_id=1, source_target_pairs={{0,12},{1,13},{2,14},{3,15},{4,0},{5,1},{6,2},{7,3},{8,4},{9,5},{1... | collective-permute-start | bytes 786440 | tf_op jit(solution)/shard_map/ppermute | solution.py:305
  73.0 3.4 %collective-permute-done.21 = bf16[256,512]{1,0:T(8,128)(2,1)S(1)} collective-permute-done((bf16[256,512]{1,0:T(8,128)(2,1)S(1)}, bf16[256,512]{1,0:T(8,128)(2,1)S(1)}, u32[]{:S(2)}, u32[]{:S(2)}) %collective-permute-start.21) | collective-permute-done | bytes 262176 | tf_op jit(solution)/shard_map/ppermute | solution.py:302
  76.9 4.5 %collective-permute-done.18 = bf16[256,512]{1,0:T(8,128)(2,1)S(1)} collective-permute-done((bf16[256,512]{1,0:T(8,128)(2,1)S(1)}, bf16[256,512]{1,0:T(8,128)(2,1)S(1)}, u32[]{:S(2)}, u32[]{:S(2)}) %collective-permute-start.18) | collective-permute-done | bytes 262176 | tf_op jit(solution)/shard_map/ppermute | solution.py:302
  81.4 4.1 %collective-permute-done.23 = bf16[256,512]{1,0:T(8,128)(2,1)S(1)} collective-permute-done((bf16[256,512]{1,0:T(8,128)(2,1)S(1)}, bf16[256,512]{1,0:T(8,128)(2,1)S(1)}, u32[]{:S(2)}, u32[]{:S(2)}) %collective-permute-start.23) | collective-permute-done | bytes 262176 | tf_op jit(solution)/shard_map/ppermute | solution.py:305
  86.0 1.3 %collective-permute-start.27 = (bf16[256,256]{1,0:T(8,128)(2,1)S(1)}, bf16[256,256]{1,0:T(8,128)(2,1)S(1)}, u32[]{:S(2)}, u32[]{:S(2)}) collective-permute-start(bf16[256,256]{1,0:T(8,128)(2,1)S(1)} %get-tuple-element.97), channel_id=1, source_target_pairs={{0,2},{1,3},{2,0},{3,1},{4,6},{5,7},{6,4},{7,5},{8,10},{9,11},{10,... | collective-permute-start | bytes 393224 | tf_op jit(solution)/shard_map/ppermute | solution.py:302
  87.3 1.5 %collective-permute-start.24 = (bf16[256,256]{1,0:T(8,128)(2,1)S(1)}, bf16[256,256]{1,0:T(8,128)(2,1)S(1)}, u32[]{:S(2)}, u32[]{:S(2)}) collective-permute-start(bf16[256,256]{1,0:T(8,128)(2,1)S(1)} %get-tuple-element.98), channel_id=1, source_target_pairs={{0,4},{1,5},{2,6},{3,7},{4,8},{5,9},{6,10},{7,11},{8,12},{9,13},{1... | collective-permute-start | bytes 393224 | tf_op jit(solution)/shard_map/ppermute | solution.py:305
  89.5 3.2 %collective-permute-done.26 = bf16[256,256]{1,0:T(8,128)(2,1)S(1)} collective-permute-done((bf16[256,256]{1,0:T(8,128)(2,1)S(1)}, bf16[256,256]{1,0:T(8,128)(2,1)S(1)}, u32[]{:S(2)}, u32[]{:S(2)}) %collective-permute-start.26) | collective-permute-done | bytes 131104 | tf_op jit(solution)/shard_map/ppermute | solution.py:305
  93.6 0.9 collective-permute-start.31
  95.0 1.6 %collective-permute-start.28 = (bf16[256,256]{1,0:T(8,128)(2,1)S(1)}, bf16[256,256]{1,0:T(8,128)(2,1)S(1)}, u32[]{:S(2)}, u32[]{:S(2)}) collective-permute-start(bf16[256,256]{1,0:T(8,128)(2,1)S(1)} %collective-permute-done.24), channel_id=1, source_target_pairs={{0,4},{1,5},{2,6},{3,7},{4,8},{5,9},{6,10},{7,11},{8,12},{9,13},{1... | collective-permute-start | bytes 393224 | tf_op jit(solution)/shard_map/ppermute | solution.py:305
  96.8 3.0 %collective-permute-done.30 = bf16[256,256]{1,0:T(8,128)(2,1)S(1)} collective-permute-done((bf16[256,256]{1,0:T(8,128)(2,1)S(1)}, bf16[256,256]{1,0:T(8,128)(2,1)S(1)}, u32[]{:S(2)}, u32[]{:S(2)}) %collective-permute-start.30) | collective-permute-done | bytes 131104 | tf_op jit(solution)/shard_map/ppermute | solution.py:305
  99.8 1.0 collective-permute-start.40
  100.8 1.0 collective-permute-done.28
  101.8 2.3 %collective-permute-start.37 = (bf16[256,256]{1,0:T(8,128)(2,1)S(1)}, bf16[256,256]{1,0:T(8,128)(2,1)S(1)}, u32[]{:S(2)}, u32[]{:S(2)}) collective-permute-start(bf16[256,256]{1,0:T(8,128)(2,1)S(1)} %collective-permute-done.28), channel_id=1, source_target_pairs={{0,4},{1,5},{2,6},{3,7},{4,8},{5,9},{6,10},{7,11},{8,12},{9,13},{1... | collective-permute-start | bytes 393224 | tf_op jit(solution)/shard_map/ppermute | solution.py:305
  104.1 3.7 %collective-permute-done.39 = bf16[256,256]{1,0:T(8,128)(2,1)S(1)} collective-permute-done((bf16[256,256]{1,0:T(8,128)(2,1)S(1)}, bf16[256,256]{1,0:T(8,128)(2,1)S(1)}, u32[]{:S(2)}, u32[]{:S(2)}) %collective-permute-start.39) | collective-permute-done | bytes 131104 | tf_op jit(solution)/shard_map/ppermute | solution.py:305
  108.3 0.9 collective-permute-done.37
  110.4 1.2 %collective-permute-start.42 = (bf16[256,256]{1,0:T(8,128)(2,1)S(1)}, bf16[256,256]{1,0:T(8,128)(2,1)S(1)}, u32[]{:S(2)}, u32[]{:S(2)}) collective-permute-start(bf16[256,256]{1,0:T(8,128)(2,1)S(1)} %collective-permute-done.27), channel_id=1, source_target_pairs={{0,12},{1,13},{2,14},{3,15},{4,0},{5,1},{6,2},{7,3},{8,4},{9,5},{1... | collective-permute-start | bytes 393224 | tf_op jit(solution)/shard_map/ppermute | solution.py:305
  112.1 3.0 %back.2.refs_0_ = bf16[4096,512]{1,0:T(8,128)(2,1)} custom-call(s32[10]{0:T(128)S(1)} %stack.107.at_ref, bf16[512,512]{1,0:T(8,128)(2,1)S(1)} %copy-done, bf16[256,512]{1,0:T(8,128)(2,1)S(1)} %get-tuple-element.82.refs_1_, bf16[512,256]{1,0:T(8,128)(2,1)S(1)} %constant_dynamic-update-slice_fusion.refs_2_, ...), custom_call_target="tpu_custom_call" | custom-call | flops 40265318400 | bytes 157286400 | tf_op jit(solution)/shard_map/back/pallas_call | solution.py:66
  116.0 1.2 fusion.5
  117.2 2.4 %back.3 = bf16[4096,512]{1,0:T(8,128)(2,1)} custom-call(s32[6]{0:T(128)S(1)} %stack.96.at_ref, bf16[4096,512]{1,0:T(8,128)(2,1)} %back.2.refs_0_, bf16[512,512]{1,0:T(8,128)(2,1)S(1)} %copy-done, bf16[512,256]{1,0:T(8,128)(2,1)S(1)} %constant_dynamic-update-slice_fusion.8.refs_2_, ...), custom_call_target="tpu_custom_call", output_to_operand_aliasing={{}: (1, {})} | custom-call | flops 24159191040000 | bytes 94371840000 | tf_op jit(solution)/shard_map/back/pallas_call | solution.py:66
  (84 shorter events, 10.8 us)
Async XLA Ops:
  0.6 44.8 %collective-permute-start = (bf16[384,8192]{1,0:T(8,128)(2,1)}, bf16[384,8192]{1,0:T(8,128)(2,1)}, u32[]{:S(2)}, u32[]{:S(2)}) collective-permute-start(bf16[384,8192]{1,0:T(8,128)(2,1)} %own_ref.5), channel_id=1, source_target_pairs={{0,1},{1,0},{2,3},{3,2},{4,5},{5,4},{6,7},{7,6},{8,9},{9,8},{10,11... | collective-permute-start | bytes 18874376 | tf_op jit(solution)/shard_map/ppermute | solution.py:299
  2.2 11.8 %collective-permute-start.1 = (bf16[512,256]{1,0:T(8,128)(2,1)S(1)}, bf16[512,256]{1,0:T(8,128)(2,1)S(1)}, u32[]{:S(2)}, u32[]{:S(2)}) collective-permute-start(bf16[512,256]{1,0:T(8,128)(2,1)S(1)} %get-tuple-element.96.refs_0_), channel_id=1, source_target_pairs={{0,4},{1,5},{2,6},{3,7},{4,8},{5,9},{6,10},{7,11},{8,12},{9,13},{1... | collective-permute-start | bytes 786440 | tf_op jit(solution)/shard_map/ppermute | solution.py:305
  4.9 9.2 %collective-permute-start.2 = (bf16[512,256]{1,0:T(8,128)(2,1)S(1)}, bf16[512,256]{1,0:T(8,128)(2,1)S(1)}, u32[]{:S(2)}, u32[]{:S(2)}) collective-permute-start(bf16[512,256]{1,0:T(8,128)(2,1)S(1)} %get-tuple-element.96.refs_0_), channel_id=1, source_target_pairs={{0,2},{1,3},{2,0},{3,1},{4,6},{5,7},{6,4},{7,5},{8,10},{9,11},{10,... | collective-permute-start | bytes 786440 | tf_op jit(solution)/shard_map/ppermute | solution.py:302
  6.4 13.3 %collective-permute-start.8 = (bf16[512,256]{1,0:T(8,128)(2,1)S(1)}, bf16[512,256]{1,0:T(8,128)(2,1)S(1)}, u32[]{:S(2)}, u32[]{:S(2)}) collective-permute-start(bf16[512,256]{1,0:T(8,128)(2,1)S(1)} %get-tuple-element.95.refs_7_), channel_id=1, source_target_pairs={{0,4},{1,5},{2,6},{3,7},{4,8},{5,9},{6,10},{7,11},{8,12},{9,13},{1... | collective-permute-start | bytes 786440 | tf_op jit(solution)/shard_map/ppermute | solution.py:305
  8.0 11.7 %collective-permute-start.9 = (bf16[512,256]{1,0:T(8,128)(2,1)S(1)}, bf16[512,256]{1,0:T(8,128)(2,1)S(1)}, u32[]{:S(2)}, u32[]{:S(2)}) collective-permute-start(bf16[512,256]{1,0:T(8,128)(2,1)S(1)} %get-tuple-element.95.refs_7_), channel_id=1, source_target_pairs={{0,2},{1,3},{2,0},{3,1},{4,6},{5,7},{6,4},{7,5},{8,10},{9,11},{10,... | collective-permute-start | bytes 786440 | tf_op jit(solution)/shard_map/ppermute | solution.py:302
  14.0 11.2 %collective-permute-start.3 = (bf16[512,256]{1,0:T(8,128)(2,1)S(1)}, bf16[512,256]{1,0:T(8,128)(2,1)S(1)}, u32[]{:S(2)}, u32[]{:S(2)}) collective-permute-start(bf16[512,256]{1,0:T(8,128)(2,1)S(1)} %collective-permute-done.1.refs_2_), channel_id=1, source_target_pairs={{0,4},{1,5},{2,6},{3,7},{4,8},{5,9},{6,10},{7,11},{8,12},{9,13},{1... | collective-permute-start | bytes 786440 | tf_op jit(solution)/shard_map/ppermute | solution.py:305
  15.6 9.7 %collective-permute-start.4 = (bf16[512,256]{1,0:T(8,128)(2,1)S(1)}, bf16[512,256]{1,0:T(8,128)(2,1)S(1)}, u32[]{:S(2)}, u32[]{:S(2)}) collective-permute-start(bf16[512,256]{1,0:T(8,128)(2,1)S(1)} %collective-permute-done.1.refs_2_), channel_id=1, source_target_pairs={{0,2},{1,3},{2,0},{3,1},{4,6},{5,7},{6,4},{7,5},{8,10},{9,11},{10,... | collective-permute-start | bytes 786440 | tf_op jit(solution)/shard_map/ppermute | solution.py:302
  19.7 11.2 %collective-permute-start.10 = (bf16[512,256]{1,0:T(8,128)(2,1)S(1)}, bf16[512,256]{1,0:T(8,128)(2,1)S(1)}, u32[]{:S(2)}, u32[]{:S(2)}) collective-permute-start(bf16[512,256]{1,0:T(8,128)(2,1)S(1)} %collective-permute-done.8.refs_9_), channel_id=1, source_target_pairs={{0,4},{1,5},{2,6},{3,7},{4,8},{5,9},{6,10},{7,11},{8,12},{9,13},{1... | collective-permute-start | bytes 786440 | tf_op jit(solution)/shard_map/ppermute | solution.py:305
  21.2 9.7 %collective-permute-start.11 = (bf16[512,256]{1,0:T(8,128)(2,1)S(1)}, bf16[512,256]{1,0:T(8,128)(2,1)S(1)}, u32[]{:S(2)}, u32[]{:S(2)}) collective-permute-start(bf16[512,256]{1,0:T(8,128)(2,1)S(1)} %collective-permute-done.8.refs_9_), channel_id=1, source_target_pairs={{0,2},{1,3},{2,0},{3,1},{4,6},{5,7},{6,4},{7,5},{8,10},{9,11},{10,... | collective-permute-start | bytes 786440 | tf_op jit(solution)/shard_map/ppermute | solution.py:302
  25.3 11.2 %collective-permute-start.6 = (bf16[512,256]{1,0:T(8,128)(2,1)S(1)}, bf16[512,256]{1,0:T(8,128)(2,1)S(1)}, u32[]{:S(2)}, u32[]{:S(2)}) collective-permute-start(bf16[512,256]{1,0:T(8,128)(2,1)S(1)} %collective-permute-done.3.refs_4_), channel_id=1, source_target_pairs={{0,4},{1,5},{2,6},{3,7},{4,8},{5,9},{6,10},{7,11},{8,12},{9,13},{1... | collective-permute-start | bytes 786440 | tf_op jit(solution)/shard_map/ppermute | solution.py:305
  26.8 9.7 %collective-permute-start.7 = (bf16[512,256]{1,0:T(8,128)(2,1)S(1)}, bf16[512,256]{1,0:T(8,128)(2,1)S(1)}, u32[]{:S(2)}, u32[]{:S(2)}) collective-permute-start(bf16[512,256]{1,0:T(8,128)(2,1)S(1)} %collective-permute-done.3.refs_4_), channel_id=1, source_target_pairs={{0,2},{1,3},{2,0},{3,1},{4,6},{5,7},{6,4},{7,5},{8,10},{9,11},{10,... | collective-permute-start | bytes 786440 | tf_op jit(solution)/shard_map/ppermute | solution.py:302
  30.9 11.0 %collective-permute-start.12 = (bf16[512,256]{1,0:T(8,128)(2,1)S(1)}, bf16[512,256]{1,0:T(8,128)(2,1)S(1)}, u32[]{:S(2)}, u32[]{:S(2)}) collective-permute-start(bf16[512,256]{1,0:T(8,128)(2,1)S(1)} %collective-permute-done.10.refs_11_), channel_id=1, source_target_pairs={{0,4},{1,5},{2,6},{3,7},{4,8},{5,9},{6,10},{7,11},{8,12},{9,13},{1... | collective-permute-start | bytes 786440 | tf_op jit(solution)/shard_map/ppermute | solution.py:305
  32.4 9.5 %collective-permute-start.13 = (bf16[512,256]{1,0:T(8,128)(2,1)S(1)}, bf16[512,256]{1,0:T(8,128)(2,1)}, u32[]{:S(2)}, u32[]{:S(2)}) collective-permute-start(bf16[512,256]{1,0:T(8,128)(2,1)S(1)} %collective-permute-done.10.refs_11_), channel_id=1, source_target_pairs={{0,2},{1,3},{2,0},{3,1},{4,6},{5,7},{6,4},{7,5},{8,10},{9,11},{10,... | collective-permute-start | bytes 786440 | tf_op jit(solution)/shard_map/ppermute | solution.py:302
  41.9 9.3 %collective-permute-start.15 = (bf16[512,256]{1,0:T(8,128)(2,1)S(1)}, bf16[512,256]{1,0:T(8,128)(2,1)S(1)}, u32[]{:S(2)}, u32[]{:S(2)}) collective-permute-start(bf16[512,256]{1,0:T(8,128)(2,1)S(1)} %collective-permute-done.9.refs_8_), channel_id=1, source_target_pairs={{0,12},{1,13},{2,14},{3,15},{4,0},{5,1},{6,2},{7,3},{8,4},{9,5},{1... | collective-permute-start | bytes 786440 | tf_op jit(solution)/shard_map/ppermute | solution.py:305
  43.9 7.6 %collective-permute-start.14 = (bf16[512,256]{1,0:T(8,128)(2,1)S(1)}, bf16[512,256]{1,0:T(8,128)(2,1)S(1)}, u32[]{:S(2)}, u32[]{:S(2)}) collective-permute-start(bf16[512,256]{1,0:T(8,128)(2,1)S(1)} %collective-permute-done.6.refs_6_), channel_id=1, source_target_pairs={{0,2},{1,3},{2,0},{3,1},{4,6},{5,7},{6,4},{7,5},{8,10},{9,11},{10,... | collective-permute-start | bytes 786440 | tf_op jit(solution)/shard_map/ppermute | solution.py:302
  45.4 7.2 %collective-permute-start.5 = (bf16[384,4096]{1,0:T(8,128)(2,1)}, bf16[384,4096]{1,0:T(8,128)(2,1)}, u32[]{:S(2)}, u32[]{:S(2)}) collective-permute-start(bf16[384,4096]{1,0:T(8,128)(2,1)} %own_ref.7), channel_id=1, source_target_pairs={{0,1},{1,0},{2,3},{3,2},{4,5},{5,4},{6,7},{7,6},{8,9},{9,8},{10,11... | collective-permute-start | bytes 9437192 | tf_op jit(solution)/shard_map/ppermute | solution.py:299
  52.1 3.5 %collective-permute-start.16 = (f32[768,512]{1,0:T(8,128)S(1)}, f32[768,512]{1,0:T(8,128)S(1)}, u32[]{:S(2)}, u32[]{:S(2)}) collective-permute-start(f32[768,512]{1,0:T(8,128)S(1)} %project_last.1.mine_ref), channel_id=1, source_target_pairs={{0,1},{1,0},{2,3},{3,2},{4,5},{5,4},{6,7},{7,6},{8,9},{9,8},{10,11... | collective-permute-start | bytes 4718600 | tf_op jit(solution)/shard_map/ppermute | solution.py:299
  56.0 9.2 %collective-permute-start.17 = (bf16[256,512]{1,0:T(8,128)(2,1)S(1)}, bf16[256,512]{1,0:T(8,128)(2,1)S(1)}, u32[]{:S(2)}, u32[]{:S(2)}) collective-permute-start(bf16[256,512]{1,0:T(8,128)(2,1)S(1)} %get-tuple-element.63), channel_id=1, source_target_pairs={{0,2},{1,3},{2,0},{3,1},{4,6},{5,7},{6,4},{7,5},{8,10},{9,11},{10,... | collective-permute-start | bytes 786440 | tf_op jit(solution)/shard_map/ppermute | solution.py:302
  60.8 10.0 %collective-permute-start.19 = (bf16[256,512]{1,0:T(8,128)(2,1)S(1)}, bf16[256,512]{1,0:T(8,128)(2,1)S(1)}, u32[]{:S(2)}, u32[]{:S(2)}) collective-permute-start(bf16[256,512]{1,0:T(8,128)(2,1)S(1)} %get-tuple-element.71), channel_id=1, source_target_pairs={{0,2},{1,3},{2,0},{3,1},{4,6},{5,7},{6,4},{7,5},{8,10},{9,11},{10,... | collective-permute-start | bytes 786440 | tf_op jit(solution)/shard_map/ppermute | solution.py:302
  61.4 15.0 %collective-permute-start.21 = (bf16[256,512]{1,0:T(8,128)(2,1)S(1)}, bf16[256,512]{1,0:T(8,128)(2,1)S(1)}, u32[]{:S(2)}, u32[]{:S(2)}) collective-permute-start(bf16[256,512]{1,0:T(8,128)(2,1)S(1)} %get-tuple-element.73), channel_id=1, source_target_pairs={{0,2},{1,3},{2,0},{3,1},{4,6},{5,7},{6,4},{7,5},{8,10},{9,11},{10,... | collective-permute-start | bytes 786440 | tf_op jit(solution)/shard_map/ppermute | solution.py:302
  62.9 18.5 %collective-permute-start.18 = (bf16[256,512]{1,0:T(8,128)(2,1)S(1)}, bf16[256,512]{1,0:T(8,128)(2,1)S(1)}, u32[]{:S(2)}, u32[]{:S(2)}) collective-permute-start(bf16[256,512]{1,0:T(8,128)(2,1)S(1)} %get-tuple-element.69), channel_id=1, source_target_pairs={{0,2},{1,3},{2,0},{3,1},{4,6},{5,7},{6,4},{7,5},{8,10},{9,11},{10,... | collective-permute-start | bytes 786440 | tf_op jit(solution)/shard_map/ppermute | solution.py:302
  65.3 11.1 %collective-permute-start.22 = (bf16[256,512]{1,0:T(8,128)(2,1)S(1)}, bf16[256,512]{1,0:T(8,128)(2,1)S(1)}, u32[]{:S(2)}, u32[]{:S(2)}) collective-permute-start(bf16[256,512]{1,0:T(8,128)(2,1)S(1)} %convert_add_fusion.1), channel_id=1, source_target_pairs={{0,4},{1,5},{2,6},{3,7},{4,8},{5,9},{6,10},{7,11},{8,12},{9,13},{1... | collective-permute-start | bytes 786440 | tf_op jit(solution)/shard_map/ppermute | solution.py:305
  70.8 10.5 %collective-permute-start.20 = (bf16[256,512]{1,0:T(8,128)(2,1)S(1)}, bf16[256,512]{1,0:T(8,128)(2,1)S(1)}, u32[]{:S(2)}, u32[]{:S(2)}) collective-permute-start(bf16[256,512]{1,0:T(8,128)(2,1)S(1)} %add_convert_fusion.1), channel_id=1, source_target_pairs={{0,12},{1,13},{2,14},{3,15},{4,0},{5,1},{6,2},{7,3},{8,4},{9,5},{1... | collective-permute-start | bytes 786440 | tf_op jit(solution)/shard_map/ppermute | solution.py:305
  76.5 8.9 %collective-permute-start.23 = (bf16[256,512]{1,0:T(8,128)(2,1)S(1)}, bf16[256,512]{1,0:T(8,128)(2,1)S(1)}, u32[]{:S(2)}, u32[]{:S(2)}) collective-permute-start(bf16[256,512]{1,0:T(8,128)(2,1)S(1)} %add_convert_fusion), channel_id=1, source_target_pairs={{0,4},{1,5},{2,6},{3,7},{4,8},{5,9},{6,10},{7,11},{8,12},{9,13},{1... | collective-permute-start | bytes 786440 | tf_op jit(solution)/shard_map/ppermute | solution.py:305
  85.5 26.7 %copy-start = (bf16[512,512]{1,0:T(8,128)(2,1)S(1)}, bf16[512,512]{1,0:T(8,128)(2,1)}, u32[]{:S(2)}) copy-start(bf16[512,512]{1,0:T(8,128)(2,1)} %refs_1_.1) | copy-start | bytes 1572868
  85.9 6.8 %collective-permute-start.26 = (bf16[256,256]{1,0:T(8,128)(2,1)S(1)}, bf16[256,256]{1,0:T(8,128)(2,1)S(1)}, u32[]{:S(2)}, u32[]{:S(2)}) collective-permute-start(bf16[256,256]{1,0:T(8,128)(2,1)S(1)} %get-tuple-element.97), channel_id=1, source_target_pairs={{0,4},{1,5},{2,6},{3,7},{4,8},{5,9},{6,10},{7,11},{8,12},{9,13},{1... | collective-permute-start | bytes 393224 | tf_op jit(solution)/shard_map/ppermute | solution.py:305
  86.0 6.8 %collective-permute-start.27 = (bf16[256,256]{1,0:T(8,128)(2,1)S(1)}, bf16[256,256]{1,0:T(8,128)(2,1)S(1)}, u32[]{:S(2)}, u32[]{:S(2)}) collective-permute-start(bf16[256,256]{1,0:T(8,128)(2,1)S(1)} %get-tuple-element.97), channel_id=1, source_target_pairs={{0,2},{1,3},{2,0},{3,1},{4,6},{5,7},{6,4},{7,5},{8,10},{9,11},{10,... | collective-permute-start | bytes 393224 | tf_op jit(solution)/shard_map/ppermute | solution.py:302
  87.3 7.2 %collective-permute-start.24 = (bf16[256,256]{1,0:T(8,128)(2,1)S(1)}, bf16[256,256]{1,0:T(8,128)(2,1)S(1)}, u32[]{:S(2)}, u32[]{:S(2)}) collective-permute-start(bf16[256,256]{1,0:T(8,128)(2,1)S(1)} %get-tuple-element.98), channel_id=1, source_target_pairs={{0,4},{1,5},{2,6},{3,7},{4,8},{5,9},{6,10},{7,11},{8,12},{9,13},{1... | collective-permute-start | bytes 393224 | tf_op jit(solution)/shard_map/ppermute | solution.py:305
  88.8 6.2 %collective-permute-start.25 = (bf16[256,256]{1,0:T(8,128)(2,1)S(1)}, bf16[256,256]{1,0:T(8,128)(2,1)S(1)}, u32[]{:S(2)}, u32[]{:S(2)}) collective-permute-start(bf16[256,256]{1,0:T(8,128)(2,1)S(1)} %get-tuple-element.98), channel_id=1, source_target_pairs={{0,2},{1,3},{2,0},{3,1},{4,6},{5,7},{6,4},{7,5},{8,10},{9,11},{10,... | collective-permute-start | bytes 393224 | tf_op jit(solution)/shard_map/ppermute | solution.py:302
  92.8 7.0 %collective-permute-start.30 = (bf16[256,256]{1,0:T(8,128)(2,1)S(1)}, bf16[256,256]{1,0:T(8,128)(2,1)S(1)}, u32[]{:S(2)}, u32[]{:S(2)}) collective-permute-start(bf16[256,256]{1,0:T(8,128)(2,1)S(1)} %collective-permute-done.26), channel_id=1, source_target_pairs={{0,4},{1,5},{2,6},{3,7},{4,8},{5,9},{6,10},{7,11},{8,12},{9,13},{1... | collective-permute-start | bytes 393224 | tf_op jit(solution)/shard_map/ppermute | solution.py:305
  93.6 6.2 %collective-permute-start.31 = (bf16[256,256]{1,0:T(8,128)(2,1)S(1)}, bf16[256,256]{1,0:T(8,128)(2,1)S(1)}, u32[]{:S(2)}, u32[]{:S(2)}) collective-permute-start(bf16[256,256]{1,0:T(8,128)(2,1)S(1)} %collective-permute-done.26), channel_id=1, source_target_pairs={{0,2},{1,3},{2,0},{3,1},{4,6},{5,7},{6,4},{7,5},{8,10},{9,11},{10,... | collective-permute-start | bytes 393224 | tf_op jit(solution)/shard_map/ppermute | solution.py:302
  95.0 6.8 %collective-permute-start.28 = (bf16[256,256]{1,0:T(8,128)(2,1)S(1)}, bf16[256,256]{1,0:T(8,128)(2,1)S(1)}, u32[]{:S(2)}, u32[]{:S(2)}) collective-permute-start(bf16[256,256]{1,0:T(8,128)(2,1)S(1)} %collective-permute-done.24), channel_id=1, source_target_pairs={{0,4},{1,5},{2,6},{3,7},{4,8},{5,9},{6,10},{7,11},{8,12},{9,13},{1... | collective-permute-start | bytes 393224 | tf_op jit(solution)/shard_map/ppermute | solution.py:305
  96.6 5.1 %collective-permute-start.29 = (bf16[256,256]{1,0:T(8,128)(2,1)S(1)}, bf16[256,256]{1,0:T(8,128)(2,1)S(1)}, u32[]{:S(2)}, u32[]{:S(2)}) collective-permute-start(bf16[256,256]{1,0:T(8,128)(2,1)S(1)} %collective-permute-done.24), channel_id=1, source_target_pairs={{0,2},{1,3},{2,0},{3,1},{4,6},{5,7},{6,4},{7,5},{8,10},{9,11},{10,... | collective-permute-start | bytes 393224 | tf_op jit(solution)/shard_map/ppermute | solution.py:302
  96.7 13.1 %collective-permute-start.32 = (bf16[256,512]{1,0:T(8,128)(2,1)S(1)}, bf16[256,512]{1,0:T(8,128)(2,1)S(1)}, u32[]{:S(2)}, u32[]{:S(2)}) collective-permute-start(bf16[256,512]{1,0:T(8,128)(2,1)S(1)} %get-tuple-element.82.refs_1_), channel_id=1, source_target_pairs={{0,1},{1,0},{2,3},{3,2},{4,5},{5,4},{6,7},{7,6},{8,9},{9,8},{10,11... | collective-permute-start | bytes 786440 | tf_op jit(solution)/shard_map/ppermute | solution.py:299
  99.8 8.0 %collective-permute-start.39 = (bf16[256,256]{1,0:T(8,128)(2,1)S(1)}, bf16[256,256]{1,0:T(8,128)(2,1)S(1)}, u32[]{:S(2)}, u32[]{:S(2)}) collective-permute-start(bf16[256,256]{1,0:T(8,128)(2,1)S(1)} %collective-permute-done.30), channel_id=1, source_target_pairs={{0,4},{1,5},{2,6},{3,7},{4,8},{5,9},{6,10},{7,11},{8,12},{9,13},{1... | collective-permute-start | bytes 393224 | tf_op jit(solution)/shard_map/ppermute | solution.py:305
  99.8 8.0 %collective-permute-start.40 = (bf16[256,256]{1,0:T(8,128)(2,1)S(1)}, bf16[256,256]{1,0:T(8,128)(2,1)S(1)}, u32[]{:S(2)}, u32[]{:S(2)}) collective-permute-start(bf16[256,256]{1,0:T(8,128)(2,1)S(1)} %collective-permute-done.30), channel_id=1, source_target_pairs={{0,2},{1,3},{2,0},{3,1},{4,6},{5,7},{6,4},{7,5},{8,10},{9,11},{10,... | collective-permute-start | bytes 393224 | tf_op jit(solution)/shard_map/ppermute | solution.py:302
  101.8 7.4 %collective-permute-start.37 = (bf16[256,256]{1,0:T(8,128)(2,1)S(1)}, bf16[256,256]{1,0:T(8,128)(2,1)S(1)}, u32[]{:S(2)}, u32[]{:S(2)}) collective-permute-start(bf16[256,256]{1,0:T(8,128)(2,1)S(1)} %collective-permute-done.28), channel_id=1, source_target_pairs={{0,4},{1,5},{2,6},{3,7},{4,8},{5,9},{6,10},{7,11},{8,12},{9,13},{1... | collective-permute-start | bytes 393224 | tf_op jit(solution)/shard_map/ppermute | solution.py:305
  104.1 5.2 %collective-permute-start.38 = (bf16[256,256]{1,0:T(8,128)(2,1)S(1)}, bf16[256,256]{1,0:T(8,128)(2,1)S(1)}, u32[]{:S(2)}, u32[]{:S(2)}) collective-permute-start(bf16[256,256]{1,0:T(8,128)(2,1)S(1)} %collective-permute-done.28), channel_id=1, source_target_pairs={{0,2},{1,3},{2,0},{3,1},{4,6},{5,7},{6,4},{7,5},{8,10},{9,11},{10,... | collective-permute-start | bytes 393224 | tf_op jit(solution)/shard_map/ppermute | solution.py:302
  107.8 2.6 %collective-permute-start.34 = (bf16[512,256]{1,0:T(8,128)(2,1)S(1)}, bf16[512,256]{1,0:T(8,128)(2,1)S(1)}, u32[]{:S(2)}, u32[]{:S(2)}) collective-permute-start(bf16[512,256]{1,0:T(8,128)(2,1)S(1)} %constant_dynamic-update-slice_fusion.2.refs_3_), channel_id=1, source_target_pairs={{0,1},{1,0},{2,3},{3,2},{4,5},{5,4},{6,7},{7,6},{8,9},{9,8},{10,11... | collective-permute-start | bytes 786440 | tf_op jit(solution)/shard_map/ppermute | solution.py:299
  107.8 3.8 %collective-permute-start.33 = (bf16[512,256]{1,0:T(8,128)(2,1)S(1)}, bf16[512,256]{1,0:T(8,128)(2,1)S(1)}, u32[]{:S(2)}, u32[]{:S(2)}) collective-permute-start(bf16[512,256]{1,0:T(8,128)(2,1)S(1)} %constant_dynamic-update-slice_fusion.refs_2_), channel_id=1, source_target_pairs={{0,1},{1,0},{2,3},{3,2},{4,5},{5,4},{6,7},{7,6},{8,9},{9,8},{10,11... | collective-permute-start | bytes 786440 | tf_op jit(solution)/shard_map/ppermute | solution.py:299
  109.2 2.4 %collective-permute-start.36 = (bf16[512,256]{1,0:T(8,128)(2,1)S(1)}, bf16[512,256]{1,0:T(8,128)(2,1)S(1)}, u32[]{:S(2)}, u32[]{:S(2)}) collective-permute-start(bf16[512,256]{1,0:T(8,128)(2,1)S(1)} %constant_dynamic-update-slice_fusion.6.refs_5_), channel_id=1, source_target_pairs={{0,1},{1,0},{2,3},{3,2},{4,5},{5,4},{6,7},{7,6},{8,9},{9,8},{10,11... | collective-permute-start | bytes 786440 | tf_op jit(solution)/shard_map/ppermute | solution.py:299
  109.2 2.9 %collective-permute-start.35 = (bf16[512,256]{1,0:T(8,128)(2,1)S(1)}, bf16[512,256]{1,0:T(8,128)(2,1)S(1)}, u32[]{:S(2)}, u32[]{:S(2)}) collective-permute-start(bf16[512,256]{1,0:T(8,128)(2,1)S(1)} %constant_dynamic-update-slice_fusion.4.refs_4_), channel_id=1, source_target_pairs={{0,1},{1,0},{2,3},{3,2},{4,5},{5,4},{6,7},{7,6},{8,9},{9,8},{10,11... | collective-permute-start | bytes 786440 | tf_op jit(solution)/shard_map/ppermute | solution.py:299
  109.8 5.7 %collective-permute-start.41 = (bf16[256,256]{1,0:T(8,128)(2,1)S(1)}, bf16[256,256]{1,0:T(8,128)(2,1)S(1)}, u32[]{:S(2)}, u32[]{:S(2)}) collective-permute-start(bf16[256,256]{1,0:T(8,128)(2,1)S(1)} %collective-permute-done.37), channel_id=1, source_target_pairs={{0,2},{1,3},{2,0},{3,1},{4,6},{5,7},{6,4},{7,5},{8,10},{9,11},{10,... | collective-permute-start | bytes 393224 | tf_op jit(solution)/shard_map/ppermute | solution.py:302
  110.4 5.2 %collective-permute-start.42 = (bf16[256,256]{1,0:T(8,128)(2,1)S(1)}, bf16[256,256]{1,0:T(8,128)(2,1)S(1)}, u32[]{:S(2)}, u32[]{:S(2)}) collective-permute-start(bf16[256,256]{1,0:T(8,128)(2,1)S(1)} %collective-permute-done.27), channel_id=1, source_target_pairs={{0,12},{1,13},{2,14},{3,15},{4,0},{5,1},{6,2},{7,3},{8,4},{9,5},{1... | collective-permute-start | bytes 393224 | tf_op jit(solution)/shard_map/ppermute | solution.py:305
  111.6 5.6 %collective-permute-start.44 = (bf16[512,256]{1,0:T(8,128)(2,1)S(1)}, bf16[512,256]{1,0:T(8,128)(2,1)S(1)}, u32[]{:S(2)}, u32[]{:S(2)}) collective-permute-start(bf16[512,256]{1,0:T(8,128)(2,1)S(1)} %constant_dynamic-update-slice_fusion.10.refs_3_), channel_id=1, source_target_pairs={{0,1},{1,0},{2,3},{3,2},{4,5},{5,4},{6,7},{7,6},{8,9},{9,8},{10,11... | collective-permute-start | bytes 786440 | tf_op jit(solution)/shard_map/ppermute | solution.py:299
  111.6 5.6 %collective-permute-start.43 = (bf16[512,256]{1,0:T(8,128)(2,1)S(1)}, bf16[512,256]{1,0:T(8,128)(2,1)S(1)}, u32[]{:S(2)}, u32[]{:S(2)}) collective-permute-start(bf16[512,256]{1,0:T(8,128)(2,1)S(1)} %constant_dynamic-update-slice_fusion.8.refs_2_), channel_id=1, source_target_pairs={{0,1},{1,0},{2,3},{3,2},{4,5},{5,4},{6,7},{7,6},{8,9},{9,8},{10,11... | collective-permute-start | bytes 786440 | tf_op jit(solution)/shard_map/ppermute | solution.py:299
  115.5 1.7 %collective-permute-start.46 = (bf16[256,256]{1,0:T(8,128)(2,1)S(1)}, bf16[256,256]{1,0:T(8,128)(2,1)S(1)}, u32[]{:S(2)}, u32[]{:S(2)}) collective-permute-start(bf16[256,256]{1,0:T(8,128)(2,1)S(1)} %collective-permute-done.42.refs_5_), channel_id=1, source_target_pairs={{0,1},{1,0},{2,3},{3,2},{4,5},{5,4},{6,7},{7,6},{8,9},{9,8},{10,11... | collective-permute-start | bytes 393224 | tf_op jit(solution)/shard_map/ppermute | solution.py:299
  115.5 1.7 %collective-permute-start.45 = (bf16[256,256]{1,0:T(8,128)(2,1)S(1)}, bf16[256,256]{1,0:T(8,128)(2,1)S(1)}, u32[]{:S(2)}, u32[]{:S(2)}) collective-permute-start(bf16[256,256]{1,0:T(8,128)(2,1)S(1)} %collective-permute-done.41.refs_4_), channel_id=1, source_target_pairs={{0,1},{1,0},{2,3},{3,2},{4,5},{5,4},{6,7},{7,6},{8,9},{9,8},{10,11... | collective-permute-start | bytes 393224 | tf_op jit(solution)/shard_map/ppermute | solution.py:299
  (2 other events, 40.4 us)

commit v14 on v13

--- a/solution.py
+++ b/solution.py
@@ -246,11 +246,14 @@
     many, (width, rank) = at.shape[0], projector.shape
     arrays = [x for group in groups for x in group]
     held = [] if before is None else [before]
+    turned = [] if held else [(True, jax.ShapeDtypeStruct((rank, width), BF16))]
 
     def kernel(at_ref, *refs):
         projector_ref, *array_refs = refs[len(held) : len(held) + 1 + len(arrays)]
-        out_ref, pt, o, out_sems = refs[len(held) + 1 + len(arrays) :]
-        pt[...] = projector_ref[...].T
+        out_ref, *refs = refs[len(held) + 1 + len(arrays) :]
+        pt, o, out_sems = [projector_ref, *refs] if held else refs
+        if not held:
+            pt[...] = projector_ref[...].T
         stores, start = [], 0
         for group in groups:
             size, column, total = group[0].shape[0], 0, None
@@ -273,9 +276,8 @@
         at,
         held,
         [projector, *arrays],
-        [(False, jax.ShapeDtypeStruct((rows_in_all, width), BF16))],
+        [(False, jax.ShapeDtypeStruct((rows_in_all, width), BF16))] + turned,
         [
-            pltpu.VMEM((rank, width), BF16),
             pltpu.VMEM((many * rows, width), BF16),
             pltpu.SemaphoreType.DMA((many,)),
         ],
@@ -284,7 +286,7 @@
         moved=2 * many * rows * (width + rank),
         name="back",
         aliases={1: 0} if held else None,
-    )[0]
+    )
 
 
 def levels(activations, out_grads, projector, first_moment, second_moment, *, nz):
@@ -368,12 +370,12 @@
     theirs = [tuple(swap_core(after(x, line[0][1])) for x in mine[0])]
     theirs += [tuple(swap_core(x) for x in group) for group in mine[1:-1]]
     order = [[(0, 0)]] + [[(-k, 0), (1 - k, 1)] for k in steps] + [[(1 - nz, 1)]]
-    update = None
+    update, turned = None, [projector]
     for low, high, weight in ((0, nz - 1, W_BACK), (nz - 1, nz + 1, W_LAST)):
         if low:
             theirs.append(tuple(swap_core(after(x, update)) for x in mine[-1]))
         at = named([(k, dy, dc) for dc in (0, 1) for some in order[low:high] for k, dy in some])
-        update = back(mine[low:high] + theirs[low:high], projector, at, width, rows_in_all, update, weight)
+        update, *turned = back(mine[low:high] + theirs[low:high], *turned, at, width, rows_in_all, update, weight)
     return update, new_first, new_second
 
 

time: 120 us -> 120 us (level)
  no operation moved by 1% of the time
where the time goes in v14:
time: 120 us
  waiting for transfers between devices  51.6 us (43%)
  starting transfers between devices  44 us (37%)
  Pallas kernels  19.5 us (16%)
  other arithmetic  2.03 us (2%)
  local copies, waits for them, and re-layouts  1.47 us (1%)
    ppermute x17, waiting for transfers between devices, shift_z(): return lax.ppermute(x, 'dp', pairs(lambda a, b, c: ((a + k) % nz, b, c)))  37.3 us
    ppermute x17, starting transfers between devices, shift_z(): return lax.ppermute(x, 'dp', pairs(lambda a, b, c: ((a + k) % nz, b, c)))  22.8 us
    pallas_call x6, Pallas kernels, call(): pl.pallas_call(kernel, grid_spec=pltpu.PrefetchScalarGridSpec(num_scalar_...  18.6 us
    ppermute x18, starting transfers between devices, swap_y(): return lax.ppermute(x, 'dp', pairs(lambda a, b, c: (a, 1 - b, c)))  18.2 us
    ppermute x18, waiting for transfers between devices, swap_y(): return lax.ppermute(x, 'dp', pairs(lambda a, b, c: (a, 1 - b, c)))  12.5 us
    ppermute x12, starting transfers between devices, swap_core(): return lax.ppermute(x, 'dp', pairs(lambda a, b, c: (a, b, 1 - c)))  2.98 us
  transfers between devices with their start and end apart: 47, of which 20 were waited for; matrix products, arithmetic and copies ran while one was open for 3% of the time, Pallas kernels for 14%

profile of v14, /device:TPU:0, one launch (start us, length us, event | category | flops | bytes accessed | tf_op | source)
XLA Modules:
  0.0 119.5 jit_solution(9970646761981806380)
XLA Ops:
  1.1 1.1 fusion.7
  2.2 2.6 %collective-permute-start.1 = (bf16[512,256]{1,0:T(8,128)(2,1)S(1)}, bf16[512,256]{1,0:T(8,128)(2,1)S(1)}, u32[]{:S(2)}, u32[]{:S(2)}) collective-permute-start(bf16[512,256]{1,0:T(8,128)(2,1)S(1)} %get-tuple-element.100.refs_0_), channel_id=1, source_target_pairs={{0,4},{1,5},{2,6},{3,7},{4,8},{5,9},{6,10},{7,11},{8,12},{9,13},{1... | collective-permute-start | bytes 786440 | tf_op jit(solution)/shard_map/ppermute | solution.py:307
  4.9 1.5 %collective-permute-start.2 = (bf16[512,256]{1,0:T(8,128)(2,1)S(1)}, bf16[512,256]{1,0:T(8,128)(2,1)S(1)}, u32[]{:S(2)}, u32[]{:S(2)}) collective-permute-start(bf16[512,256]{1,0:T(8,128)(2,1)S(1)} %get-tuple-element.100.refs_0_), channel_id=1, source_target_pairs={{0,2},{1,3},{2,0},{3,1},{4,6},{5,7},{6,4},{7,5},{8,10},{9,11},{10,... | collective-permute-start | bytes 786440 | tf_op jit(solution)/shard_map/ppermute | solution.py:304
  6.4 1.6 %collective-permute-start.8 = (bf16[512,256]{1,0:T(8,128)(2,1)S(1)}, bf16[512,256]{1,0:T(8,128)(2,1)S(1)}, u32[]{:S(2)}, u32[]{:S(2)}) collective-permute-start(bf16[512,256]{1,0:T(8,128)(2,1)S(1)} %get-tuple-element.99.refs_7_), channel_id=1, source_target_pairs={{0,4},{1,5},{2,6},{3,7},{4,8},{5,9},{6,10},{7,11},{8,12},{9,13},{1... | collective-permute-start | bytes 786440 | tf_op jit(solution)/shard_map/ppermute | solution.py:307
  8.5 5.6 %collective-permute-done.1.refs_2_ = bf16[512,256]{1,0:T(8,128)(2,1)S(1)} collective-permute-done((bf16[512,256]{1,0:T(8,128)(2,1)S(1)}, bf16[512,256]{1,0:T(8,128)(2,1)S(1)}, u32[]{:S(2)}, u32[]{:S(2)}) %collective-permute-start.1) | collective-permute-done | bytes 262176 | tf_op jit(solution)/shard_map/ppermute | solution.py:307
  14.0 1.5 %collective-permute-start.3 = (bf16[512,256]{1,0:T(8,128)(2,1)S(1)}, bf16[512,256]{1,0:T(8,128)(2,1)S(1)}, u32[]{:S(2)}, u32[]{:S(2)}) collective-permute-start(bf16[512,256]{1,0:T(8,128)(2,1)S(1)} %collective-permute-done.1.refs_2_), channel_id=1, source_target_pairs={{0,4},{1,5},{2,6},{3,7},{4,8},{5,9},{6,10},{7,11},{8,12},{9,13},{1... | collective-permute-start | bytes 786440 | tf_op jit(solution)/shard_map/ppermute | solution.py:307
  15.6 1.5 %collective-permute-start.4 = (bf16[512,256]{1,0:T(8,128)(2,1)S(1)}, bf16[512,256]{1,0:T(8,128)(2,1)S(1)}, u32[]{:S(2)}, u32[]{:S(2)}) collective-permute-start(bf16[512,256]{1,0:T(8,128)(2,1)S(1)} %collective-permute-done.1.refs_2_), channel_id=1, source_target_pairs={{0,2},{1,3},{2,0},{3,1},{4,6},{5,7},{6,4},{7,5},{8,10},{9,11},{10,... | collective-permute-start | bytes 786440 | tf_op jit(solution)/shard_map/ppermute | solution.py:304
  17.1 2.6 %collective-permute-done.8.refs_9_ = bf16[512,256]{1,0:T(8,128)(2,1)S(1)} collective-permute-done((bf16[512,256]{1,0:T(8,128)(2,1)S(1)}, bf16[512,256]{1,0:T(8,128)(2,1)S(1)}, u32[]{:S(2)}, u32[]{:S(2)}) %collective-permute-start.8) | collective-permute-done | bytes 262176 | tf_op jit(solution)/shard_map/ppermute | solution.py:307
  19.7 1.5 %collective-permute-start.10 = (bf16[512,256]{1,0:T(8,128)(2,1)S(1)}, bf16[512,256]{1,0:T(8,128)(2,1)S(1)}, u32[]{:S(2)}, u32[]{:S(2)}) collective-permute-start(bf16[512,256]{1,0:T(8,128)(2,1)S(1)} %collective-permute-done.8.refs_9_), channel_id=1, source_target_pairs={{0,4},{1,5},{2,6},{3,7},{4,8},{5,9},{6,10},{7,11},{8,12},{9,13},{1... | collective-permute-start | bytes 786440 | tf_op jit(solution)/shard_map/ppermute | solution.py:307
  21.2 1.5 %collective-permute-start.11 = (bf16[512,256]{1,0:T(8,128)(2,1)S(1)}, bf16[512,256]{1,0:T(8,128)(2,1)S(1)}, u32[]{:S(2)}, u32[]{:S(2)}) collective-permute-start(bf16[512,256]{1,0:T(8,128)(2,1)S(1)} %collective-permute-done.8.refs_9_), channel_id=1, source_target_pairs={{0,2},{1,3},{2,0},{3,1},{4,6},{5,7},{6,4},{7,5},{8,10},{9,11},{10,... | collective-permute-start | bytes 786440 | tf_op jit(solution)/shard_map/ppermute | solution.py:304
  22.7 2.6 %collective-permute-done.3.refs_4_ = bf16[512,256]{1,0:T(8,128)(2,1)S(1)} collective-permute-done((bf16[512,256]{1,0:T(8,128)(2,1)S(1)}, bf16[512,256]{1,0:T(8,128)(2,1)S(1)}, u32[]{:S(2)}, u32[]{:S(2)}) %collective-permute-start.3) | collective-permute-done | bytes 262176 | tf_op jit(solution)/shard_map/ppermute | solution.py:307
  25.3 1.5 %collective-permute-start.6 = (bf16[512,256]{1,0:T(8,128)(2,1)S(1)}, bf16[512,256]{1,0:T(8,128)(2,1)S(1)}, u32[]{:S(2)}, u32[]{:S(2)}) collective-permute-start(bf16[512,256]{1,0:T(8,128)(2,1)S(1)} %collective-permute-done.3.refs_4_), channel_id=1, source_target_pairs={{0,4},{1,5},{2,6},{3,7},{4,8},{5,9},{6,10},{7,11},{8,12},{9,13},{1... | collective-permute-start | bytes 786440 | tf_op jit(solution)/shard_map/ppermute | solution.py:307
  26.8 1.5 %collective-permute-start.7 = (bf16[512,256]{1,0:T(8,128)(2,1)S(1)}, bf16[512,256]{1,0:T(8,128)(2,1)S(1)}, u32[]{:S(2)}, u32[]{:S(2)}) collective-permute-start(bf16[512,256]{1,0:T(8,128)(2,1)S(1)} %collective-permute-done.3.refs_4_), channel_id=1, source_target_pairs={{0,2},{1,3},{2,0},{3,1},{4,6},{5,7},{6,4},{7,5},{8,10},{9,11},{10,... | collective-permute-start | bytes 786440 | tf_op jit(solution)/shard_map/ppermute | solution.py:304
  28.3 2.6 %collective-permute-done.10.refs_11_ = bf16[512,256]{1,0:T(8,128)(2,1)S(1)} collective-permute-done((bf16[512,256]{1,0:T(8,128)(2,1)S(1)}, bf16[512,256]{1,0:T(8,128)(2,1)S(1)}, u32[]{:S(2)}, u32[]{:S(2)}) %collective-permute-start.10) | collective-permute-done | bytes 262176 | tf_op jit(solution)/shard_map/ppermute | solution.py:307
  30.9 1.5 %collective-permute-start.12 = (bf16[512,256]{1,0:T(8,128)(2,1)S(1)}, bf16[512,256]{1,0:T(8,128)(2,1)S(1)}, u32[]{:S(2)}, u32[]{:S(2)}) collective-permute-start(bf16[512,256]{1,0:T(8,128)(2,1)S(1)} %collective-permute-done.10.refs_11_), channel_id=1, source_target_pairs={{0,4},{1,5},{2,6},{3,7},{4,8},{5,9},{6,10},{7,11},{8,12},{9,13},{1... | collective-permute-start | bytes 786440 | tf_op jit(solution)/shard_map/ppermute | solution.py:307
  32.4 1.5 %collective-permute-start.13 = (bf16[512,256]{1,0:T(8,128)(2,1)S(1)}, bf16[512,256]{1,0:T(8,128)(2,1)}, u32[]{:S(2)}, u32[]{:S(2)}) collective-permute-start(bf16[512,256]{1,0:T(8,128)(2,1)S(1)} %collective-permute-done.10.refs_11_), channel_id=1, source_target_pairs={{0,2},{1,3},{2,0},{3,1},{4,6},{5,7},{6,4},{7,5},{8,10},{9,11},{10,... | collective-permute-start | bytes 786440 | tf_op jit(solution)/shard_map/ppermute | solution.py:304
  34.0 2.5 %collective-permute-done.6.refs_6_ = bf16[512,256]{1,0:T(8,128)(2,1)S(1)} collective-permute-done((bf16[512,256]{1,0:T(8,128)(2,1)S(1)}, bf16[512,256]{1,0:T(8,128)(2,1)S(1)}, u32[]{:S(2)}, u32[]{:S(2)}) %collective-permute-start.6) | collective-permute-done | bytes 262176 | tf_op jit(solution)/shard_map/ppermute | solution.py:307
  36.5 5.4 %collective-permute-done.12.refs_13_ = bf16[512,256]{1,0:T(8,128)(2,1)S(1)} collective-permute-done((bf16[512,256]{1,0:T(8,128)(2,1)S(1)}, bf16[512,256]{1,0:T(8,128)(2,1)S(1)}, u32[]{:S(2)}, u32[]{:S(2)}) %collective-permute-start.12) | collective-permute-done | bytes 262176 | tf_op jit(solution)/shard_map/ppermute | solution.py:307
  41.9 1.9 %collective-permute-start.15 = (bf16[512,256]{1,0:T(8,128)(2,1)S(1)}, bf16[512,256]{1,0:T(8,128)(2,1)S(1)}, u32[]{:S(2)}, u32[]{:S(2)}) collective-permute-start(bf16[512,256]{1,0:T(8,128)(2,1)S(1)} %collective-permute-done.9.refs_8_), channel_id=1, source_target_pairs={{0,12},{1,13},{2,14},{3,15},{4,0},{5,1},{6,2},{7,3},{8,4},{9,5},{1... | collective-permute-start | bytes 786440 | tf_op jit(solution)/shard_map/ppermute | solution.py:307
  43.9 1.5 %collective-permute-start.14 = (bf16[512,256]{1,0:T(8,128)(2,1)S(1)}, bf16[512,256]{1,0:T(8,128)(2,1)S(1)}, u32[]{:S(2)}, u32[]{:S(2)}) collective-permute-start(bf16[512,256]{1,0:T(8,128)(2,1)S(1)} %collective-permute-done.6.refs_6_), channel_id=1, source_target_pairs={{0,2},{1,3},{2,0},{3,1},{4,6},{5,7},{6,4},{7,5},{8,10},{9,11},{10,... | collective-permute-start | bytes 786440 | tf_op jit(solution)/shard_map/ppermute | solution.py:304
  45.4 5.9 %project.1 = (f32[768,512]{1,0:T(8,128)S(1)}, bf16[768,512]{1,0:T(8,128)(2,1)S(1)}) custom-call(s32[8]{0:T(128)S(1)} %stack.116.at_ref, bf16[384,8192]{1,0:T(8,128)(2,1)} %own_ref.5, bf16[384,8192]{1,0:T(8,128)(2,1)} %collective-permute-done.sib_ref, bf16[512,256]{1,0:T(8,128)(2,1)S(1)} %get-tuple-element.100.refs_0_, ...), custom_call_target="tpu_custom_call" | custom-call | flops 8455716864 | bytes 32243712 | tf_op jit(solution)/shard_map/project/pallas_call | solution.py:66
  52.6 1.2 %turn.1.turned_ref = bf16[256,768]{1,0:T(8,128)(2,1)S(1)} custom-call(s32[1]{0:T(128)} %bitcast.21.at_ref, bf16[384,4096]{1,0:T(8,128)(2,1)} %own_ref.7, bf16[384,4096]{1,0:T(8,128)(2,1)} %collective-permute-done.5.sib_ref), custom_call_target="tpu_custom_call" | custom-call | bytes 23592960 | tf_op jit(solution)/shard_map/turn/pallas_call | solution.py:66
  53.8 1.8 %collective-permute-done.16.theirs_ref = f32[768,512]{1,0:T(8,128)S(1)} collective-permute-done((f32[768,512]{1,0:T(8,128)S(1)}, f32[768,512]{1,0:T(8,128)S(1)}, u32[]{:S(2)}, u32[]{:S(2)}) %collective-permute-start.16) | collective-permute-done | bytes 1572896 | tf_op jit(solution)/shard_map/ppermute | solution.py:301
  56.0 1.5 %collective-permute-start.17 = (bf16[256,512]{1,0:T(8,128)(2,1)S(1)}, bf16[256,512]{1,0:T(8,128)(2,1)S(1)}, u32[]{:S(2)}, u32[]{:S(2)}) collective-permute-start(bf16[256,512]{1,0:T(8,128)(2,1)S(1)} %get-tuple-element.65), channel_id=1, source_target_pairs={{0,2},{1,3},{2,0},{3,1},{4,6},{5,7},{6,4},{7,5},{8,10},{9,11},{10,... | collective-permute-start | bytes 786440 | tf_op jit(solution)/shard_map/ppermute | solution.py:304
  57.5 3.3 %outer.2 = (bf16[256,512]{1,0:T(8,128)(2,1)S(1)}, bf16[256,512]{1,0:T(8,128)(2,1)S(1)}, bf16[256,512]{1,0:T(8,128)(2,1)S(1)}, f32[256,512]{1,0:T(8,128)S(1)}) custom-call(s32[4]{0:T(128)S(1)} %pad_add_fusion.1.at_ref, bf16[384,4096]{1,0:T(8,128)(2,1)} %own_ref.7, bf16[384,4096]{1,0:T(8,128)(2,1)} %collective-permute-done.5.sib_ref, ...), custom_call_target="tpu_custom_call" | custom-call | flops 24159191040 | bytes 110100480 | tf_op jit(solution)/shard_map/outer/pallas_call | solution.py:66
  61.4 1.5 %collective-permute-start.21 = (bf16[256,512]{1,0:T(8,128)(2,1)S(1)}, bf16[256,512]{1,0:T(8,128)(2,1)S(1)}, u32[]{:S(2)}, u32[]{:S(2)}) collective-permute-start(bf16[256,512]{1,0:T(8,128)(2,1)S(1)} %get-tuple-element.75), channel_id=1, source_target_pairs={{0,2},{1,3},{2,0},{3,1},{4,6},{5,7},{6,4},{7,5},{8,10},{9,11},{10,... | collective-permute-start | bytes 786440 | tf_op jit(solution)/shard_map/ppermute | solution.py:304
  63.5 1.7 %collective-permute-done.17 = bf16[256,512]{1,0:T(8,128)(2,1)S(1)} collective-permute-done((bf16[256,512]{1,0:T(8,128)(2,1)S(1)}, bf16[256,512]{1,0:T(8,128)(2,1)S(1)}, u32[]{:S(2)}, u32[]{:S(2)}) %collective-permute-start.17) | collective-permute-done | bytes 262176 | tf_op jit(solution)/shard_map/ppermute | solution.py:304
  65.6 2.8 %outer.3 = (f32[256,512]{1,0:T(8,128)S(1)}, f32[256,512]{1,0:T(8,128)S(1)}, f32[256,512]{1,0:T(8,128)S(1)}) custom-call(s32[3]{0:T(128)S(1)} %pad_add_fusion.at_ref, bf16[384,4096]{1,0:T(8,128)(2,1)} %own_ref.7, bf16[384,4096]{1,0:T(8,128)(2,1)} %collective-permute-done.5.sib_ref, bf16[768,512]{1,0:T(8,128)(2,1)S(1)} %get-tuple-element.67.projected_ref), custom_call_target="tpu_custom_call" | custom-call | flops 18119393280 | bytes 82575360 | tf_op jit(solution)/shard_map/outer/pallas_call | solution.py:66
  68.5 2.3 %collective-permute-done.19 = bf16[256,512]{1,0:T(8,128)(2,1)S(1)} collective-permute-done((bf16[256,512]{1,0:T(8,128)(2,1)S(1)}, bf16[256,512]{1,0:T(8,128)(2,1)S(1)}, u32[]{:S(2)}, u32[]{:S(2)}) %collective-permute-start.19) | collective-permute-done | bytes 262176 | tf_op jit(solution)/shard_map/ppermute | solution.py:304
  70.9 2.1 %collective-permute-start.20 = (bf16[256,512]{1,0:T(8,128)(2,1)S(1)}, bf16[256,512]{1,0:T(8,128)(2,1)S(1)}, u32[]{:S(2)}, u32[]{:S(2)}) collective-permute-start(bf16[256,512]{1,0:T(8,128)(2,1)S(1)} %add_convert_fusion.1), channel_id=1, source_target_pairs={{0,12},{1,13},{2,14},{3,15},{4,0},{5,1},{6,2},{7,3},{8,4},{9,5},{1... | collective-permute-start | bytes 786440 | tf_op jit(solution)/shard_map/ppermute | solution.py:307
  73.0 3.4 %collective-permute-done.21 = bf16[256,512]{1,0:T(8,128)(2,1)S(1)} collective-permute-done((bf16[256,512]{1,0:T(8,128)(2,1)S(1)}, bf16[256,512]{1,0:T(8,128)(2,1)S(1)}, u32[]{:S(2)}, u32[]{:S(2)}) %collective-permute-start.21) | collective-permute-done | bytes 262176 | tf_op jit(solution)/shard_map/ppermute | solution.py:304
  76.9 4.5 %collective-permute-done.18 = bf16[256,512]{1,0:T(8,128)(2,1)S(1)} collective-permute-done((bf16[256,512]{1,0:T(8,128)(2,1)S(1)}, bf16[256,512]{1,0:T(8,128)(2,1)S(1)}, u32[]{:S(2)}, u32[]{:S(2)}) %collective-permute-start.18) | collective-permute-done | bytes 262176 | tf_op jit(solution)/shard_map/ppermute | solution.py:304
  81.4 4.1 %collective-permute-done.23 = bf16[256,512]{1,0:T(8,128)(2,1)S(1)} collective-permute-done((bf16[256,512]{1,0:T(8,128)(2,1)S(1)}, bf16[256,512]{1,0:T(8,128)(2,1)S(1)}, u32[]{:S(2)}, u32[]{:S(2)}) %collective-permute-start.23) | collective-permute-done | bytes 262176 | tf_op jit(solution)/shard_map/ppermute | solution.py:307
  86.0 1.3 %collective-permute-start.27 = (bf16[256,256]{1,0:T(8,128)(2,1)S(1)}, bf16[256,256]{1,0:T(8,128)(2,1)S(1)}, u32[]{:S(2)}, u32[]{:S(2)}) collective-permute-start(bf16[256,256]{1,0:T(8,128)(2,1)S(1)} %get-tuple-element.101), channel_id=1, source_target_pairs={{0,2},{1,3},{2,0},{3,1},{4,6},{5,7},{6,4},{7,5},{8,10},{9,11},{10,... | collective-permute-start | bytes 393224 | tf_op jit(solution)/shard_map/ppermute | solution.py:304
  87.3 1.5 %collective-permute-start.24 = (bf16[256,256]{1,0:T(8,128)(2,1)S(1)}, bf16[256,256]{1,0:T(8,128)(2,1)S(1)}, u32[]{:S(2)}, u32[]{:S(2)}) collective-permute-start(bf16[256,256]{1,0:T(8,128)(2,1)S(1)} %get-tuple-element.102), channel_id=1, source_target_pairs={{0,4},{1,5},{2,6},{3,7},{4,8},{5,9},{6,10},{7,11},{8,12},{9,13},{1... | collective-permute-start | bytes 393224 | tf_op jit(solution)/shard_map/ppermute | solution.py:307
  89.5 3.2 %collective-permute-done.26 = bf16[256,256]{1,0:T(8,128)(2,1)S(1)} collective-permute-done((bf16[256,256]{1,0:T(8,128)(2,1)S(1)}, bf16[256,256]{1,0:T(8,128)(2,1)S(1)}, u32[]{:S(2)}, u32[]{:S(2)}) %collective-permute-start.26) | collective-permute-done | bytes 131104 | tf_op jit(solution)/shard_map/ppermute | solution.py:307
  93.6 0.9 collective-permute-start.31
  94.9 1.7 %collective-permute-start.28 = (bf16[256,256]{1,0:T(8,128)(2,1)S(1)}, bf16[256,256]{1,0:T(8,128)(2,1)S(1)}, u32[]{:S(2)}, u32[]{:S(2)}) collective-permute-start(bf16[256,256]{1,0:T(8,128)(2,1)S(1)} %collective-permute-done.24), channel_id=1, source_target_pairs={{0,4},{1,5},{2,6},{3,7},{4,8},{5,9},{6,10},{7,11},{8,12},{9,13},{1... | collective-permute-start | bytes 393224 | tf_op jit(solution)/shard_map/ppermute | solution.py:307
  96.8 3.0 %collective-permute-done.30 = bf16[256,256]{1,0:T(8,128)(2,1)S(1)} collective-permute-done((bf16[256,256]{1,0:T(8,128)(2,1)S(1)}, bf16[256,256]{1,0:T(8,128)(2,1)S(1)}, u32[]{:S(2)}, u32[]{:S(2)}) %collective-permute-start.30) | collective-permute-done | bytes 131104 | tf_op jit(solution)/shard_map/ppermute | solution.py:307
  99.8 1.0 collective-permute-start.40
  100.8 0.9 collective-permute-done.28
  101.7 2.3 %collective-permute-start.37 = (bf16[256,256]{1,0:T(8,128)(2,1)S(1)}, bf16[256,256]{1,0:T(8,128)(2,1)S(1)}, u32[]{:S(2)}, u32[]{:S(2)}) collective-permute-start(bf16[256,256]{1,0:T(8,128)(2,1)S(1)} %collective-permute-done.28), channel_id=1, source_target_pairs={{0,4},{1,5},{2,6},{3,7},{4,8},{5,9},{6,10},{7,11},{8,12},{9,13},{1... | collective-permute-start | bytes 393224 | tf_op jit(solution)/shard_map/ppermute | solution.py:307
  104.1 3.7 %collective-permute-done.39 = bf16[256,256]{1,0:T(8,128)(2,1)S(1)} collective-permute-done((bf16[256,256]{1,0:T(8,128)(2,1)S(1)}, bf16[256,256]{1,0:T(8,128)(2,1)S(1)}, u32[]{:S(2)}, u32[]{:S(2)}) %collective-permute-start.39) | collective-permute-done | bytes 131104 | tf_op jit(solution)/shard_map/ppermute | solution.py:307
  108.3 0.9 collective-permute-done.37
  110.4 1.2 %collective-permute-start.42 = (bf16[256,256]{1,0:T(8,128)(2,1)S(1)}, bf16[256,256]{1,0:T(8,128)(2,1)S(1)}, u32[]{:S(2)}, u32[]{:S(2)}) collective-permute-start(bf16[256,256]{1,0:T(8,128)(2,1)S(1)} %collective-permute-done.27), channel_id=1, source_target_pairs={{0,12},{1,13},{2,14},{3,15},{4,0},{5,1},{6,2},{7,3},{8,4},{9,5},{1... | collective-permute-start | bytes 393224 | tf_op jit(solution)/shard_map/ppermute | solution.py:307
  112.1 3.0 %back.2 = (bf16[4096,512]{1,0:T(8,128)(2,1)}, bf16[512,512]{1,0:T(8,128)(2,1)S(1)}) custom-call(s32[10]{0:T(128)S(1)} %stack.107.at_ref, bf16[512,512]{1,0:T(8,128)(2,1)S(1)} %copy-done, bf16[256,512]{1,0:T(8,128)(2,1)S(1)} %get-tuple-element.84.refs_1_, bf16[512,256]{1,0:T(8,128)(2,1)S(1)} %constant_dynamic-update-slice_fusion.refs_2_, ...), custom_call_target="tpu_custom_call" | custom-call | flops 40265318400 | bytes 157286400 | tf_op jit(solution)/shard_map/back/pallas_call | solution.py:66
  116.0 1.2 fusion.5
  117.2 2.3 %back.3 = bf16[4096,512]{1,0:T(8,128)(2,1)} custom-call(s32[6]{0:T(128)S(1)} %stack.96.at_ref, bf16[4096,512]{1,0:T(8,128)(2,1)} %get-tuple-element.85.refs_0_, bf16[512,512]{1,0:T(8,128)(2,1)S(1)} %get-tuple-element.86.refs_1_, bf16[512,256]{1,0:T(8,128)(2,1)S(1)} %constant_dynamic-update-slice_fusion.8.refs_2_, ...), custom_call_target="tpu_custom_call", output_to_operand_aliasing={{}: (1, {})} | custom-call | flops 24159191040000 | bytes 94371840000 | tf_op jit(solution)/shard_map/back/pallas_call | solution.py:66
  (84 shorter events, 10.8 us)
Async XLA Ops:
  0.6 44.8 %collective-permute-start = (bf16[384,8192]{1,0:T(8,128)(2,1)}, bf16[384,8192]{1,0:T(8,128)(2,1)}, u32[]{:S(2)}, u32[]{:S(2)}) collective-permute-start(bf16[384,8192]{1,0:T(8,128)(2,1)} %own_ref.5), channel_id=1, source_target_pairs={{0,1},{1,0},{2,3},{3,2},{4,5},{5,4},{6,7},{7,6},{8,9},{9,8},{10,11... | collective-permute-start | bytes 18874376 | tf_op jit(solution)/shard_map/ppermute | solution.py:301
  2.2 11.8 %collective-permute-start.1 = (bf16[512,256]{1,0:T(8,128)(2,1)S(1)}, bf16[512,256]{1,0:T(8,128)(2,1)S(1)}, u32[]{:S(2)}, u32[]{:S(2)}) collective-permute-start(bf16[512,256]{1,0:T(8,128)(2,1)S(1)} %get-tuple-element.100.refs_0_), channel_id=1, source_target_pairs={{0,4},{1,5},{2,6},{3,7},{4,8},{5,9},{6,10},{7,11},{8,12},{9,13},{1... | collective-permute-start | bytes 786440 | tf_op jit(solution)/shard_map/ppermute | solution.py:307
  4.9 9.2 %collective-permute-start.2 = (bf16[512,256]{1,0:T(8,128)(2,1)S(1)}, bf16[512,256]{1,0:T(8,128)(2,1)S(1)}, u32[]{:S(2)}, u32[]{:S(2)}) collective-permute-start(bf16[512,256]{1,0:T(8,128)(2,1)S(1)} %get-tuple-element.100.refs_0_), channel_id=1, source_target_pairs={{0,2},{1,3},{2,0},{3,1},{4,6},{5,7},{6,4},{7,5},{8,10},{9,11},{10,... | collective-permute-start | bytes 786440 | tf_op jit(solution)/shard_map/ppermute | solution.py:304
  6.4 13.3 %collective-permute-start.8 = (bf16[512,256]{1,0:T(8,128)(2,1)S(1)}, bf16[512,256]{1,0:T(8,128)(2,1)S(1)}, u32[]{:S(2)}, u32[]{:S(2)}) collective-permute-start(bf16[512,256]{1,0:T(8,128)(2,1)S(1)} %get-tuple-element.99.refs_7_), channel_id=1, source_target_pairs={{0,4},{1,5},{2,6},{3,7},{4,8},{5,9},{6,10},{7,11},{8,12},{9,13},{1... | collective-permute-start | bytes 786440 | tf_op jit(solution)/shard_map/ppermute | solution.py:307
  8.0 11.7 %collective-permute-start.9 = (bf16[512,256]{1,0:T(8,128)(2,1)S(1)}, bf16[512,256]{1,0:T(8,128)(2,1)S(1)}, u32[]{:S(2)}, u32[]{:S(2)}) collective-permute-start(bf16[512,256]{1,0:T(8,128)(2,1)S(1)} %get-tuple-element.99.refs_7_), channel_id=1, source_target_pairs={{0,2},{1,3},{2,0},{3,1},{4,6},{5,7},{6,4},{7,5},{8,10},{9,11},{10,... | collective-permute-start | bytes 786440 | tf_op jit(solution)/shard_map/ppermute | solution.py:304
  14.0 11.2 %collective-permute-start.3 = (bf16[512,256]{1,0:T(8,128)(2,1)S(1)}, bf16[512,256]{1,0:T(8,128)(2,1)S(1)}, u32[]{:S(2)}, u32[]{:S(2)}) collective-permute-start(bf16[512,256]{1,0:T(8,128)(2,1)S(1)} %collective-permute-done.1.refs_2_), channel_id=1, source_target_pairs={{0,4},{1,5},{2,6},{3,7},{4,8},{5,9},{6,10},{7,11},{8,12},{9,13},{1... | collective-permute-start | bytes 786440 | tf_op jit(solution)/shard_map/ppermute | solution.py:307
  15.6 9.7 %collective-permute-start.4 = (bf16[512,256]{1,0:T(8,128)(2,1)S(1)}, bf16[512,256]{1,0:T(8,128)(2,1)S(1)}, u32[]{:S(2)}, u32[]{:S(2)}) collective-permute-start(bf16[512,256]{1,0:T(8,128)(2,1)S(1)} %collective-permute-done.1.refs_2_), channel_id=1, source_target_pairs={{0,2},{1,3},{2,0},{3,1},{4,6},{5,7},{6,4},{7,5},{8,10},{9,11},{10,... | collective-permute-start | bytes 786440 | tf_op jit(solution)/shard_map/ppermute | solution.py:304
  19.7 11.2 %collective-permute-start.10 = (bf16[512,256]{1,0:T(8,128)(2,1)S(1)}, bf16[512,256]{1,0:T(8,128)(2,1)S(1)}, u32[]{:S(2)}, u32[]{:S(2)}) collective-permute-start(bf16[512,256]{1,0:T(8,128)(2,1)S(1)} %collective-permute-done.8.refs_9_), channel_id=1, source_target_pairs={{0,4},{1,5},{2,6},{3,7},{4,8},{5,9},{6,10},{7,11},{8,12},{9,13},{1... | collective-permute-start | bytes 786440 | tf_op jit(solution)/shard_map/ppermute | solution.py:307
  21.2 9.7 %collective-permute-start.11 = (bf16[512,256]{1,0:T(8,128)(2,1)S(1)}, bf16[512,256]{1,0:T(8,128)(2,1)S(1)}, u32[]{:S(2)}, u32[]{:S(2)}) collective-permute-start(bf16[512,256]{1,0:T(8,128)(2,1)S(1)} %collective-permute-done.8.refs_9_), channel_id=1, source_target_pairs={{0,2},{1,3},{2,0},{3,1},{4,6},{5,7},{6,4},{7,5},{8,10},{9,11},{10,... | collective-permute-start | bytes 786440 | tf_op jit(solution)/shard_map/ppermute | solution.py:304
  25.3 11.2 %collective-permute-start.6 = (bf16[512,256]{1,0:T(8,128)(2,1)S(1)}, bf16[512,256]{1,0:T(8,128)(2,1)S(1)}, u32[]{:S(2)}, u32[]{:S(2)}) collective-permute-start(bf16[512,256]{1,0:T(8,128)(2,1)S(1)} %collective-permute-done.3.refs_4_), channel_id=1, source_target_pairs={{0,4},{1,5},{2,6},{3,7},{4,8},{5,9},{6,10},{7,11},{8,12},{9,13},{1... | collective-permute-start | bytes 786440 | tf_op jit(solution)/shard_map/ppermute | solution.py:307
  26.8 9.7 %collective-permute-start.7 = (bf16[512,256]{1,0:T(8,128)(2,1)S(1)}, bf16[512,256]{1,0:T(8,128)(2,1)S(1)}, u32[]{:S(2)}, u32[]{:S(2)}) collective-permute-start(bf16[512,256]{1,0:T(8,128)(2,1)S(1)} %collective-permute-done.3.refs_4_), channel_id=1, source_target_pairs={{0,2},{1,3},{2,0},{3,1},{4,6},{5,7},{6,4},{7,5},{8,10},{9,11},{10,... | collective-permute-start | bytes 786440 | tf_op jit(solution)/shard_map/ppermute | solution.py:304
  30.9 11.0 %collective-permute-start.12 = (bf16[512,256]{1,0:T(8,128)(2,1)S(1)}, bf16[512,256]{1,0:T(8,128)(2,1)S(1)}, u32[]{:S(2)}, u32[]{:S(2)}) collective-permute-start(bf16[512,256]{1,0:T(8,128)(2,1)S(1)} %collective-permute-done.10.refs_11_), channel_id=1, source_target_pairs={{0,4},{1,5},{2,6},{3,7},{4,8},{5,9},{6,10},{7,11},{8,12},{9,13},{1... | collective-permute-start | bytes 786440 | tf_op jit(solution)/shard_map/ppermute | solution.py:307
  32.4 9.5 %collective-permute-start.13 = (bf16[512,256]{1,0:T(8,128)(2,1)S(1)}, bf16[512,256]{1,0:T(8,128)(2,1)}, u32[]{:S(2)}, u32[]{:S(2)}) collective-permute-start(bf16[512,256]{1,0:T(8,128)(2,1)S(1)} %collective-permute-done.10.refs_11_), channel_id=1, source_target_pairs={{0,2},{1,3},{2,0},{3,1},{4,6},{5,7},{6,4},{7,5},{8,10},{9,11},{10,... | collective-permute-start | bytes 786440 | tf_op jit(solution)/shard_map/ppermute | solution.py:304
  41.9 9.3 %collective-permute-start.15 = (bf16[512,256]{1,0:T(8,128)(2,1)S(1)}, bf16[512,256]{1,0:T(8,128)(2,1)S(1)}, u32[]{:S(2)}, u32[]{:S(2)}) collective-permute-start(bf16[512,256]{1,0:T(8,128)(2,1)S(1)} %collective-permute-done.9.refs_8_), channel_id=1, source_target_pairs={{0,12},{1,13},{2,14},{3,15},{4,0},{5,1},{6,2},{7,3},{8,4},{9,5},{1... | collective-permute-start | bytes 786440 | tf_op jit(solution)/shard_map/ppermute | solution.py:307
  43.9 7.6 %collective-permute-start.14 = (bf16[512,256]{1,0:T(8,128)(2,1)S(1)}, bf16[512,256]{1,0:T(8,128)(2,1)S(1)}, u32[]{:S(2)}, u32[]{:S(2)}) collective-permute-start(bf16[512,256]{1,0:T(8,128)(2,1)S(1)} %collective-permute-done.6.refs_6_), channel_id=1, source_target_pairs={{0,2},{1,3},{2,0},{3,1},{4,6},{5,7},{6,4},{7,5},{8,10},{9,11},{10,... | collective-permute-start | bytes 786440 | tf_op jit(solution)/shard_map/ppermute | solution.py:304
  45.4 7.2 %collective-permute-start.5 = (bf16[384,4096]{1,0:T(8,128)(2,1)}, bf16[384,4096]{1,0:T(8,128)(2,1)}, u32[]{:S(2)}, u32[]{:S(2)}) collective-permute-start(bf16[384,4096]{1,0:T(8,128)(2,1)} %own_ref.7), channel_id=1, source_target_pairs={{0,1},{1,0},{2,3},{3,2},{4,5},{5,4},{6,7},{7,6},{8,9},{9,8},{10,11... | collective-permute-start | bytes 9437192 | tf_op jit(solution)/shard_map/ppermute | solution.py:301
  52.1 3.5 %collective-permute-start.16 = (f32[768,512]{1,0:T(8,128)S(1)}, f32[768,512]{1,0:T(8,128)S(1)}, u32[]{:S(2)}, u32[]{:S(2)}) collective-permute-start(f32[768,512]{1,0:T(8,128)S(1)} %project_last.1.mine_ref), channel_id=1, source_target_pairs={{0,1},{1,0},{2,3},{3,2},{4,5},{5,4},{6,7},{7,6},{8,9},{9,8},{10,11... | collective-permute-start | bytes 4718600 | tf_op jit(solution)/shard_map/ppermute | solution.py:301
  56.0 9.2 %collective-permute-start.17 = (bf16[256,512]{1,0:T(8,128)(2,1)S(1)}, bf16[256,512]{1,0:T(8,128)(2,1)S(1)}, u32[]{:S(2)}, u32[]{:S(2)}) collective-permute-start(bf16[256,512]{1,0:T(8,128)(2,1)S(1)} %get-tuple-element.65), channel_id=1, source_target_pairs={{0,2},{1,3},{2,0},{3,1},{4,6},{5,7},{6,4},{7,5},{8,10},{9,11},{10,... | collective-permute-start | bytes 786440 | tf_op jit(solution)/shard_map/ppermute | solution.py:304
  60.8 10.0 %collective-permute-start.19 = (bf16[256,512]{1,0:T(8,128)(2,1)S(1)}, bf16[256,512]{1,0:T(8,128)(2,1)S(1)}, u32[]{:S(2)}, u32[]{:S(2)}) collective-permute-start(bf16[256,512]{1,0:T(8,128)(2,1)S(1)} %get-tuple-element.73), channel_id=1, source_target_pairs={{0,2},{1,3},{2,0},{3,1},{4,6},{5,7},{6,4},{7,5},{8,10},{9,11},{10,... | collective-permute-start | bytes 786440 | tf_op jit(solution)/shard_map/ppermute | solution.py:304
  61.4 15.0 %collective-permute-start.21 = (bf16[256,512]{1,0:T(8,128)(2,1)S(1)}, bf16[256,512]{1,0:T(8,128)(2,1)S(1)}, u32[]{:S(2)}, u32[]{:S(2)}) collective-permute-start(bf16[256,512]{1,0:T(8,128)(2,1)S(1)} %get-tuple-element.75), channel_id=1, source_target_pairs={{0,2},{1,3},{2,0},{3,1},{4,6},{5,7},{6,4},{7,5},{8,10},{9,11},{10,... | collective-permute-start | bytes 786440 | tf_op jit(solution)/shard_map/ppermute | solution.py:304
  62.9 18.5 %collective-permute-start.18 = (bf16[256,512]{1,0:T(8,128)(2,1)S(1)}, bf16[256,512]{1,0:T(8,128)(2,1)S(1)}, u32[]{:S(2)}, u32[]{:S(2)}) collective-permute-start(bf16[256,512]{1,0:T(8,128)(2,1)S(1)} %get-tuple-element.71), channel_id=1, source_target_pairs={{0,2},{1,3},{2,0},{3,1},{4,6},{5,7},{6,4},{7,5},{8,10},{9,11},{10,... | collective-permute-start | bytes 786440 | tf_op jit(solution)/shard_map/ppermute | solution.py:304
  65.3 11.1 %collective-permute-start.22 = (bf16[256,512]{1,0:T(8,128)(2,1)S(1)}, bf16[256,512]{1,0:T(8,128)(2,1)S(1)}, u32[]{:S(2)}, u32[]{:S(2)}) collective-permute-start(bf16[256,512]{1,0:T(8,128)(2,1)S(1)} %convert_add_fusion.1), channel_id=1, source_target_pairs={{0,4},{1,5},{2,6},{3,7},{4,8},{5,9},{6,10},{7,11},{8,12},{9,13},{1... | collective-permute-start | bytes 786440 | tf_op jit(solution)/shard_map/ppermute | solution.py:307
  70.9 10.5 %collective-permute-start.20 = (bf16[256,512]{1,0:T(8,128)(2,1)S(1)}, bf16[256,512]{1,0:T(8,128)(2,1)S(1)}, u32[]{:S(2)}, u32[]{:S(2)}) collective-permute-start(bf16[256,512]{1,0:T(8,128)(2,1)S(1)} %add_convert_fusion.1), channel_id=1, source_target_pairs={{0,12},{1,13},{2,14},{3,15},{4,0},{5,1},{6,2},{7,3},{8,4},{9,5},{1... | collective-permute-start | bytes 786440 | tf_op jit(solution)/shard_map/ppermute | solution.py:307
  76.5 8.9 %collective-permute-start.23 = (bf16[256,512]{1,0:T(8,128)(2,1)S(1)}, bf16[256,512]{1,0:T(8,128)(2,1)S(1)}, u32[]{:S(2)}, u32[]{:S(2)}) collective-permute-start(bf16[256,512]{1,0:T(8,128)(2,1)S(1)} %add_convert_fusion), channel_id=1, source_target_pairs={{0,4},{1,5},{2,6},{3,7},{4,8},{5,9},{6,10},{7,11},{8,12},{9,13},{1... | collective-permute-start | bytes 786440 | tf_op jit(solution)/shard_map/ppermute | solution.py:307
  85.4 26.7 %copy-start = (bf16[512,512]{1,0:T(8,128)(2,1)S(1)}, bf16[512,512]{1,0:T(8,128)(2,1)}, u32[]{:S(2)}) copy-start(bf16[512,512]{1,0:T(8,128)(2,1)} %refs_0_.1) | copy-start | bytes 1572868
  85.9 6.8 %collective-permute-start.26 = (bf16[256,256]{1,0:T(8,128)(2,1)S(1)}, bf16[256,256]{1,0:T(8,128)(2,1)S(1)}, u32[]{:S(2)}, u32[]{:S(2)}) collective-permute-start(bf16[256,256]{1,0:T(8,128)(2,1)S(1)} %get-tuple-element.101), channel_id=1, source_target_pairs={{0,4},{1,5},{2,6},{3,7},{4,8},{5,9},{6,10},{7,11},{8,12},{9,13},{1... | collective-permute-start | bytes 393224 | tf_op jit(solution)/shard_map/ppermute | solution.py:307
  86.0 6.8 %collective-permute-start.27 = (bf16[256,256]{1,0:T(8,128)(2,1)S(1)}, bf16[256,256]{1,0:T(8,128)(2,1)S(1)}, u32[]{:S(2)}, u32[]{:S(2)}) collective-permute-start(bf16[256,256]{1,0:T(8,128)(2,1)S(1)} %get-tuple-element.101), channel_id=1, source_target_pairs={{0,2},{1,3},{2,0},{3,1},{4,6},{5,7},{6,4},{7,5},{8,10},{9,11},{10,... | collective-permute-start | bytes 393224 | tf_op jit(solution)/shard_map/ppermute | solution.py:304
  87.3 7.2 %collective-permute-start.24 = (bf16[256,256]{1,0:T(8,128)(2,1)S(1)}, bf16[256,256]{1,0:T(8,128)(2,1)S(1)}, u32[]{:S(2)}, u32[]{:S(2)}) collective-permute-start(bf16[256,256]{1,0:T(8,128)(2,1)S(1)} %get-tuple-element.102), channel_id=1, source_target_pairs={{0,4},{1,5},{2,6},{3,7},{4,8},{5,9},{6,10},{7,11},{8,12},{9,13},{1... | collective-permute-start | bytes 393224 | tf_op jit(solution)/shard_map/ppermute | solution.py:307
  88.8 6.1 %collective-permute-start.25 = (bf16[256,256]{1,0:T(8,128)(2,1)S(1)}, bf16[256,256]{1,0:T(8,128)(2,1)S(1)}, u32[]{:S(2)}, u32[]{:S(2)}) collective-permute-start(bf16[256,256]{1,0:T(8,128)(2,1)S(1)} %get-tuple-element.102), channel_id=1, source_target_pairs={{0,2},{1,3},{2,0},{3,1},{4,6},{5,7},{6,4},{7,5},{8,10},{9,11},{10,... | collective-permute-start | bytes 393224 | tf_op jit(solution)/shard_map/ppermute | solution.py:304
  92.8 7.0 %collective-permute-start.30 = (bf16[256,256]{1,0:T(8,128)(2,1)S(1)}, bf16[256,256]{1,0:T(8,128)(2,1)S(1)}, u32[]{:S(2)}, u32[]{:S(2)}) collective-permute-start(bf16[256,256]{1,0:T(8,128)(2,1)S(1)} %collective-permute-done.26), channel_id=1, source_target_pairs={{0,4},{1,5},{2,6},{3,7},{4,8},{5,9},{6,10},{7,11},{8,12},{9,13},{1... | collective-permute-start | bytes 393224 | tf_op jit(solution)/shard_map/ppermute | solution.py:307
  93.6 6.1 %collective-permute-start.31 = (bf16[256,256]{1,0:T(8,128)(2,1)S(1)}, bf16[256,256]{1,0:T(8,128)(2,1)S(1)}, u32[]{:S(2)}, u32[]{:S(2)}) collective-permute-start(bf16[256,256]{1,0:T(8,128)(2,1)S(1)} %collective-permute-done.26), channel_id=1, source_target_pairs={{0,2},{1,3},{2,0},{3,1},{4,6},{5,7},{6,4},{7,5},{8,10},{9,11},{10,... | collective-permute-start | bytes 393224 | tf_op jit(solution)/shard_map/ppermute | solution.py:304
  94.9 6.8 %collective-permute-start.28 = (bf16[256,256]{1,0:T(8,128)(2,1)S(1)}, bf16[256,256]{1,0:T(8,128)(2,1)S(1)}, u32[]{:S(2)}, u32[]{:S(2)}) collective-permute-start(bf16[256,256]{1,0:T(8,128)(2,1)S(1)} %collective-permute-done.24), channel_id=1, source_target_pairs={{0,4},{1,5},{2,6},{3,7},{4,8},{5,9},{6,10},{7,11},{8,12},{9,13},{1... | collective-permute-start | bytes 393224 | tf_op jit(solution)/shard_map/ppermute | solution.py:307
  96.6 5.1 %collective-permute-start.29 = (bf16[256,256]{1,0:T(8,128)(2,1)S(1)}, bf16[256,256]{1,0:T(8,128)(2,1)S(1)}, u32[]{:S(2)}, u32[]{:S(2)}) collective-permute-start(bf16[256,256]{1,0:T(8,128)(2,1)S(1)} %collective-permute-done.24), channel_id=1, source_target_pairs={{0,2},{1,3},{2,0},{3,1},{4,6},{5,7},{6,4},{7,5},{8,10},{9,11},{10,... | collective-permute-start | bytes 393224 | tf_op jit(solution)/shard_map/ppermute | solution.py:304
  96.7 13.1 %collective-permute-start.32 = (bf16[256,512]{1,0:T(8,128)(2,1)S(1)}, bf16[256,512]{1,0:T(8,128)(2,1)S(1)}, u32[]{:S(2)}, u32[]{:S(2)}) collective-permute-start(bf16[256,512]{1,0:T(8,128)(2,1)S(1)} %get-tuple-element.84.refs_1_), channel_id=1, source_target_pairs={{0,1},{1,0},{2,3},{3,2},{4,5},{5,4},{6,7},{7,6},{8,9},{9,8},{10,11... | collective-permute-start | bytes 786440 | tf_op jit(solution)/shard_map/ppermute | solution.py:301
  99.8 8.0 %collective-permute-start.39 = (bf16[256,256]{1,0:T(8,128)(2,1)S(1)}, bf16[256,256]{1,0:T(8,128)(2,1)S(1)}, u32[]{:S(2)}, u32[]{:S(2)}) collective-permute-start(bf16[256,256]{1,0:T(8,128)(2,1)S(1)} %collective-permute-done.30), channel_id=1, source_target_pairs={{0,4},{1,5},{2,6},{3,7},{4,8},{5,9},{6,10},{7,11},{8,12},{9,13},{1... | collective-permute-start | bytes 393224 | tf_op jit(solution)/shard_map/ppermute | solution.py:307
  99.8 8.0 %collective-permute-start.40 = (bf16[256,256]{1,0:T(8,128)(2,1)S(1)}, bf16[256,256]{1,0:T(8,128)(2,1)S(1)}, u32[]{:S(2)}, u32[]{:S(2)}) collective-permute-start(bf16[256,256]{1,0:T(8,128)(2,1)S(1)} %collective-permute-done.30), channel_id=1, source_target_pairs={{0,2},{1,3},{2,0},{3,1},{4,6},{5,7},{6,4},{7,5},{8,10},{9,11},{10,... | collective-permute-start | bytes 393224 | tf_op jit(solution)/shard_map/ppermute | solution.py:304
  101.7 7.5 %collective-permute-start.37 = (bf16[256,256]{1,0:T(8,128)(2,1)S(1)}, bf16[256,256]{1,0:T(8,128)(2,1)S(1)}, u32[]{:S(2)}, u32[]{:S(2)}) collective-permute-start(bf16[256,256]{1,0:T(8,128)(2,1)S(1)} %collective-permute-done.28), channel_id=1, source_target_pairs={{0,4},{1,5},{2,6},{3,7},{4,8},{5,9},{6,10},{7,11},{8,12},{9,13},{1... | collective-permute-start | bytes 393224 | tf_op jit(solution)/shard_map/ppermute | solution.py:307
  104.1 5.1 %collective-permute-start.38 = (bf16[256,256]{1,0:T(8,128)(2,1)S(1)}, bf16[256,256]{1,0:T(8,128)(2,1)S(1)}, u32[]{:S(2)}, u32[]{:S(2)}) collective-permute-start(bf16[256,256]{1,0:T(8,128)(2,1)S(1)} %collective-permute-done.28), channel_id=1, source_target_pairs={{0,2},{1,3},{2,0},{3,1},{4,6},{5,7},{6,4},{7,5},{8,10},{9,11},{10,... | collective-permute-start | bytes 393224 | tf_op jit(solution)/shard_map/ppermute | solution.py:304
  107.8 2.6 %collective-permute-start.34 = (bf16[512,256]{1,0:T(8,128)(2,1)S(1)}, bf16[512,256]{1,0:T(8,128)(2,1)S(1)}, u32[]{:S(2)}, u32[]{:S(2)}) collective-permute-start(bf16[512,256]{1,0:T(8,128)(2,1)S(1)} %constant_dynamic-update-slice_fusion.2.refs_3_), channel_id=1, source_target_pairs={{0,1},{1,0},{2,3},{3,2},{4,5},{5,4},{6,7},{7,6},{8,9},{9,8},{10,11... | collective-permute-start | bytes 786440 | tf_op jit(solution)/shard_map/ppermute | solution.py:301
  107.8 3.8 %collective-permute-start.33 = (bf16[512,256]{1,0:T(8,128)(2,1)S(1)}, bf16[512,256]{1,0:T(8,128)(2,1)S(1)}, u32[]{:S(2)}, u32[]{:S(2)}) collective-permute-start(bf16[512,256]{1,0:T(8,128)(2,1)S(1)} %constant_dynamic-update-slice_fusion.refs_2_), channel_id=1, source_target_pairs={{0,1},{1,0},{2,3},{3,2},{4,5},{5,4},{6,7},{7,6},{8,9},{9,8},{10,11... | collective-permute-start | bytes 786440 | tf_op jit(solution)/shard_map/ppermute | solution.py:301
  109.2 2.4 %collective-permute-start.36 = (bf16[512,256]{1,0:T(8,128)(2,1)S(1)}, bf16[512,256]{1,0:T(8,128)(2,1)S(1)}, u32[]{:S(2)}, u32[]{:S(2)}) collective-permute-start(bf16[512,256]{1,0:T(8,128)(2,1)S(1)} %constant_dynamic-update-slice_fusion.6.refs_5_), channel_id=1, source_target_pairs={{0,1},{1,0},{2,3},{3,2},{4,5},{5,4},{6,7},{7,6},{8,9},{9,8},{10,11... | collective-permute-start | bytes 786440 | tf_op jit(solution)/shard_map/ppermute | solution.py:301
  109.2 2.9 %collective-permute-start.35 = (bf16[512,256]{1,0:T(8,128)(2,1)S(1)}, bf16[512,256]{1,0:T(8,128)(2,1)S(1)}, u32[]{:S(2)}, u32[]{:S(2)}) collective-permute-start(bf16[512,256]{1,0:T(8,128)(2,1)S(1)} %constant_dynamic-update-slice_fusion.4.refs_4_), channel_id=1, source_target_pairs={{0,1},{1,0},{2,3},{3,2},{4,5},{5,4},{6,7},{7,6},{8,9},{9,8},{10,11... | collective-permute-start | bytes 786440 | tf_op jit(solution)/shard_map/ppermute | solution.py:301
  109.8 5.7 %collective-permute-start.41 = (bf16[256,256]{1,0:T(8,128)(2,1)S(1)}, bf16[256,256]{1,0:T(8,128)(2,1)S(1)}, u32[]{:S(2)}, u32[]{:S(2)}) collective-permute-start(bf16[256,256]{1,0:T(8,128)(2,1)S(1)} %collective-permute-done.37), channel_id=1, source_target_pairs={{0,2},{1,3},{2,0},{3,1},{4,6},{5,7},{6,4},{7,5},{8,10},{9,11},{10,... | collective-permute-start | bytes 393224 | tf_op jit(solution)/shard_map/ppermute | solution.py:304
  110.4 5.1 %collective-permute-start.42 = (bf16[256,256]{1,0:T(8,128)(2,1)S(1)}, bf16[256,256]{1,0:T(8,128)(2,1)S(1)}, u32[]{:S(2)}, u32[]{:S(2)}) collective-permute-start(bf16[256,256]{1,0:T(8,128)(2,1)S(1)} %collective-permute-done.27), channel_id=1, source_target_pairs={{0,12},{1,13},{2,14},{3,15},{4,0},{5,1},{6,2},{7,3},{8,4},{9,5},{1... | collective-permute-start | bytes 393224 | tf_op jit(solution)/shard_map/ppermute | solution.py:307
  111.6 5.6 %collective-permute-start.44 = (bf16[512,256]{1,0:T(8,128)(2,1)S(1)}, bf16[512,256]{1,0:T(8,128)(2,1)S(1)}, u32[]{:S(2)}, u32[]{:S(2)}) collective-permute-start(bf16[512,256]{1,0:T(8,128)(2,1)S(1)} %constant_dynamic-update-slice_fusion.10.refs_3_), channel_id=1, source_target_pairs={{0,1},{1,0},{2,3},{3,2},{4,5},{5,4},{6,7},{7,6},{8,9},{9,8},{10,11... | collective-permute-start | bytes 786440 | tf_op jit(solution)/shard_map/ppermute | solution.py:301
  111.6 5.6 %collective-permute-start.43 = (bf16[512,256]{1,0:T(8,128)(2,1)S(1)}, bf16[512,256]{1,0:T(8,128)(2,1)S(1)}, u32[]{:S(2)}, u32[]{:S(2)}) collective-permute-start(bf16[512,256]{1,0:T(8,128)(2,1)S(1)} %constant_dynamic-update-slice_fusion.8.refs_2_), channel_id=1, source_target_pairs={{0,1},{1,0},{2,3},{3,2},{4,5},{5,4},{6,7},{7,6},{8,9},{9,8},{10,11... | collective-permute-start | bytes 786440 | tf_op jit(solution)/shard_map/ppermute | solution.py:301
  115.5 1.7 %collective-permute-start.46 = (bf16[256,256]{1,0:T(8,128)(2,1)S(1)}, bf16[256,256]{1,0:T(8,128)(2,1)S(1)}, u32[]{:S(2)}, u32[]{:S(2)}) collective-permute-start(bf16[256,256]{1,0:T(8,128)(2,1)S(1)} %collective-permute-done.42.refs_5_), channel_id=1, source_target_pairs={{0,1},{1,0},{2,3},{3,2},{4,5},{5,4},{6,7},{7,6},{8,9},{9,8},{10,11... | collective-permute-start | bytes 393224 | tf_op jit(solution)/shard_map/ppermute | solution.py:301
  115.5 1.7 %collective-permute-start.45 = (bf16[256,256]{1,0:T(8,128)(2,1)S(1)}, bf16[256,256]{1,0:T(8,128)(2,1)S(1)}, u32[]{:S(2)}, u32[]{:S(2)}) collective-permute-start(bf16[256,256]{1,0:T(8,128)(2,1)S(1)} %collective-permute-done.41.refs_4_), channel_id=1, source_target_pairs={{0,1},{1,0},{2,3},{3,2},{4,5},{5,4},{6,7},{7,6},{8,9},{9,8},{10,11... | collective-permute-start | bytes 393224 | tf_op jit(solution)/shard_map/ppermute | solution.py:301
  (2 other events, 40.4 us)
